TPU v7x, 32 devices: a whole 2x2x4 slice. The times are simulated.
32 devices in a mesh: dp: 2 (over y), seq: 16 (over z, x, core).
Axes of the slice: x: 2, y: 2, z: 4, core: 2. Of those that a mesh axis runs over, the one named last changes fastest.
Arguments:
- enc_act: bfloat16 [2, 256, 18944], P('dp', None, 'seq'), may hold values from -6 to 6
- down_weight: bfloat16 [18944, 3584], P('seq'), may hold values from -0.046875 to 0.046875
- norm_gain: bfloat16 [3584], replicated, may hold values from 0.099609375 to 1.8984375
- text_in_weight: bfloat16 [3584, 3072], P(None, 'seq'), may hold values from -0.09375 to 0.09375
- modulation_weight: bfloat16 [256, 2, 3072], P(None, None, 'seq'), may hold values from -0.375 to 0.375
- key_value_weight: bfloat16 [3072, 4096], P('seq'), may hold values from -0.109375 to 0.109375
- timesteps: int32 [2], P('dp'), may hold values from 0 to 999
- lengths: int32 [2], P('dp'), may hold values from 32 to 256, as said below
- image_queries: bfloat16 [2, 2048, 2048], P('dp', 'seq'), may hold values from -8 to 8
- image_key_values: bfloat16 [2, 2048, 2, 2048], P('dp', 'seq'), may hold values from -8 to 8
Outputs:
- attended: bfloat16 [2, 2048, 2048], P('dp', 'seq')
- text_kv: bfloat16 [512, 4096], P(('dp', 'seq'))
Inputs may be any that keep to these rules, and one draw needn't show every extreme that they name: `lengths`: some prompt has all 256 tokens valid.
All inputs are finite; a program needn't handle non-finite values.
Results may differ from a plain program's by a relative error of at most 0.022.
Values may be sent and summed in bfloat16 or wider, within the bound.
No kernel may reach another device: no remote copies, remote signals or barrier semaphores. Data moves between devices by JAX's collectives and lax.ppermute only.
A program may use at most 64 MiB of HBM per device.

v0:
```python
import math

import jax
import jax.numpy as jnp
from jax import lax
from jax.sharding import PartitionSpec as P

HEAD_DIM = 128
HEADS = 16
TEMB = 256


epsilon = 1e-06


def normalize(summed, norm_gain):
    scale_rows = lax.rsqrt(jnp.mean(summed * summed, 1, keepdims=True) + epsilon)
    return (summed * scale_rows * norm_gain.astype(jnp.float32)).astype(jnp.bfloat16)


def time_embedding(timesteps, modulation_weight):
    half_width = TEMB // 2
    freqs = jnp.exp(-math.log(10000.0) * jnp.arange(half_width, dtype=jnp.float32) / half_width)
    angles = timesteps.astype(jnp.float32)[:, None] * freqs[None, :]
    embedding = jnp.concatenate([jnp.cos(angles), jnp.sin(angles)], 1)
    embedding = jax.nn.silu(embedding).astype(jnp.bfloat16)
    flat = modulation_weight.reshape(modulation_weight.shape[0], -1)
    product = jnp.dot(embedding, flat, preferred_element_type=jnp.float32)
    return product.reshape(timesteps.shape[0], 2, -1)


def attend(queries, key_rows, value_rows, text_keys, text_values, valid_len):
    factor = 1.0 / math.sqrt(queries.shape[1])
    contract = (((1,), (1,)), ((), ()))
    img_scores = (
        lax.dot_general(queries, key_rows, contract, preferred_element_type=jnp.float32) * factor
    )
    txt_scores = (
        lax.dot_general(queries, text_keys, contract, preferred_element_type=jnp.float32) * factor
    )
    positions = jnp.arange(text_keys.shape[0], dtype=jnp.int32)
    txt_scores = jnp.where(positions[None, :] < valid_len, txt_scores, -jnp.inf)
    row_max = jnp.maximum(jnp.max(img_scores, 1), jnp.max(txt_scores, 1))[:, None]
    img_weights = jnp.exp(img_scores - row_max)
    txt_weights = jnp.exp(txt_scores - row_max)
    denominator = jnp.sum(img_weights, 1) + jnp.sum(txt_weights, 1)
    mixed = jnp.dot(
        img_weights.astype(jnp.bfloat16), value_rows, preferred_element_type=jnp.float32
    )
    mixed = mixed + jnp.dot(
        txt_weights.astype(jnp.bfloat16), text_values, preferred_element_type=jnp.float32
    )
    return (mixed / denominator[:, None]).astype(jnp.bfloat16)


def local(
    enc_act,
    down_weight,
    norm_gain,
    text_in_weight,
    modulation_weight,
    key_value_weight,
    timesteps,
    lengths,
    image_queries,
    image_key_values,
):
    devices = lax.axis_size("seq")
    groups = enc_act.shape[0]
    text_len = enc_act.shape[1]
    ff_share = enc_act.shape[2]
    rows_all = groups * text_len
    share_rows = rows_all // devices
    hidden_act = enc_act.reshape(rows_all, ff_share)
    summed = lax.psum_scatter(
        jnp.dot(hidden_act, down_weight, preferred_element_type=jnp.float32).astype(jnp.bfloat16),
        "seq",
        scatter_dimension=0,
        tiled=True,
    ).astype(jnp.float32)
    text_proj = jnp.dot(
        lax.all_gather(normalize(summed, norm_gain), "seq", axis=0, tiled=True),
        text_in_weight,
        preferred_element_type=jnp.float32,
    )
    model_width = text_proj.shape[1] * devices
    first, second = lax.psum((jnp.sum(text_proj, 1), jnp.sum(text_proj * text_proj, 1)), "seq")
    mean_val = first / model_width
    variance = second / model_width - mean_val * mean_val
    centred = (text_proj - mean_val[:, None]) * lax.rsqrt(variance + epsilon)[:, None]
    modulation = time_embedding(timesteps, modulation_weight)
    shaped = centred.reshape(groups, text_len, -1)
    modulated = (shaped * (1.0 + modulation[:, 1][:, None]) + modulation[:, 0][:, None]).astype(
        jnp.bfloat16
    )
    modulated = modulated.reshape(rows_all, -1)
    text_kv = lax.psum_scatter(
        jnp.dot(modulated, key_value_weight, preferred_element_type=jnp.float32).astype(
            jnp.bfloat16
        ),
        "seq",
        scatter_dimension=0,
        tiled=True,
    )
    copies = devices // HEADS
    spread = text_kv.reshape(share_rows, 2, HEADS, HEAD_DIM).transpose(2, 0, 1, 3)
    spread = jnp.broadcast_to(spread[:, None], (HEADS, copies, share_rows, 2, HEAD_DIM))
    spread = spread.reshape(devices, share_rows, 2, HEAD_DIM)
    text_head = lax.all_to_all(spread, "seq", split_axis=0, concat_axis=0, tiled=True).reshape(
        groups, text_len, 2, HEAD_DIM
    )
    img_dev = image_queries.shape[1]
    part_rows = img_dev // copies
    query_send = image_queries.reshape(groups, copies, part_rows, HEADS, HEAD_DIM).transpose(
        3, 1, 0, 2, 4
    )
    query_send = query_send.reshape(devices, groups, part_rows, HEAD_DIM)
    pair_send = image_key_values.reshape(groups, img_dev, 2, HEADS, HEAD_DIM).transpose(
        3, 0, 1, 2, 4
    )
    pair_send = jnp.broadcast_to(pair_send[:, None], (HEADS, copies, groups, img_dev, 2, HEAD_DIM))
    pair_send = pair_send.reshape(devices, groups, img_dev, 2, HEAD_DIM)
    query_got, pair_got = (
        lax.all_to_all(query_send, "seq", split_axis=0, concat_axis=0, tiled=True),
        lax.all_to_all(pair_send, "seq", split_axis=0, concat_axis=0, tiled=True),
    )
    query_count = devices * part_rows
    block_rows = min(512, query_count)
    head_queries = query_got[:, 0].reshape(query_count // block_rows, block_rows, HEAD_DIM)
    head_pairs = pair_got[:, 0].reshape(devices * img_dev, 2, HEAD_DIM)
    key_rows = head_pairs[:, 0]
    value_rows = head_pairs[:, 1]
    text_keys = text_head[0, :, 0]
    text_values = text_head[0, :, 1]
    valid_len = lengths[0]

    def run_block(
        block,
        key_rows=key_rows,
        value_rows=value_rows,
        text_keys=text_keys,
        text_values=text_values,
        valid_len=valid_len,
    ):
        return attend(block, key_rows, value_rows, text_keys, text_values, valid_len)

    finished = lax.map(run_block, head_queries)
    results = [finished.reshape(devices, part_rows, HEAD_DIM)]
    back_send = jnp.stack(results, 1)
    back_got = lax.all_to_all(back_send, "seq", split_axis=0, concat_axis=0, tiled=True)
    attended = back_got.reshape(HEADS, copies, groups, part_rows, HEAD_DIM).transpose(2, 1, 3, 0, 4)
    attended = attended.reshape(groups, img_dev, HEADS * HEAD_DIM)
    return (attended, text_kv)


def solution(mesh):
    in_specs = (
        P("dp", None, "seq"),
        P("seq", None),
        P(),
        P(None, "seq"),
        P(None, None, "seq"),
        P("seq", None),
        P("dp"),
        P("dp"),
        P("dp", "seq", None),
        P("dp", "seq", None, None),
    )
    out_specs = (P("dp", "seq", None), P(("dp", "seq"), None))
    return jax.shard_map(local, mesh=mesh, in_specs=in_specs, out_specs=out_specs, check_vma=False)
```

profile of v0, /device:TPU:0, one launch (start us, length us, event | category | flops | bytes accessed | tf_op | source)
XLA Modules:
  0.0 293.2 jit_solution(15177917559800373586)
XLA Ops:
  7.2 0.0 copy-start
  7.2 0.0 reduce-scatter.3.cloned.1.call-start
  7.3 7.6 %convolution_convert_fusion = bf16[256,3584]{1,0:T(8,128)(2,1)} fusion(bf16[1184,3584]{1,0:T(8,128)(2,1)} %param.13, bf16[1,256,1184]{1,2,0:T(8,128)(2,1)} %param.12), kind=kOutput, calls=%fused_computation.28 | convolution fusion | flops 2173566976 | bytes 10928128 | tf_op jit(solution)/shard_map/dot_general | solution.py:76
  14.8 0.0 reduce-scatter.3.cloned.1.call-update
  14.8 0.0 all-gather.2.cloned.1.call-start
  14.9 63.3 %reduce-scatter.3.cloned.1.call-done = bf16[16,3584]{1,0:T(8,128)(2,1)} async-done(((bf16[256,3584]{1,0:T(8,128)(2,1)}), bf16[16,3584]{1,0:T(8,128)(2,1)}) %reduce-scatter.3.cloned.1.call-update) | async-done | bytes 114704 | tf_op jit(solution)/shard_map/reduce_scatter | solution.py:75
  78.2 1.0 fusion.36
  79.3 1.6 fusion.38
  80.9 0.0 all-gather.2.cloned.1.call-update
  81.0 0.0 reduce-scatter.5.cloned.1.call-start
  81.8 0.1 fusion.39
  81.9 38.8 %all-gather.2.cloned.1.call-done = bf16[256,3584]{1,0:T(8,128)(2,1)} async-done(((bf16[16,3584]{1,0:T(8,128)(2,1)}), bf16[256,3584]{1,0:T(8,128)(2,1)}) %all-gather.2.cloned.1.call-update) | async-done | bytes 1835024 | tf_op jit(solution)/shard_map/all_gather | solution.py:82
  120.7 2.3 fusion.49
  123.0 31.3 %all-reduce = (f32[256]{0:T(256)S(1)}, f32[256]{0:T(256)S(1)}) all-reduce(f32[256]{0:T(256)S(1)} %get-tuple-element.48, f32[256]{0:T(256)S(1)} %get-tuple-element.47), channel_id=1, replica_groups=mesh['dp'=2,'seq'=16] {'seq'}, use_global_device_ids=true, to_apply=%region_5.0 | all-reduce | flops 512 | bytes 4096 | tf_op jit(solution)/shard_map/psum | solution.py:87
  154.3 2.2 convolution_convert_fusion.1
  156.5 0.0 reduce-scatter.5.cloned.1.call-update
  156.5 2.5 copy.21
  159.1 1.3 copy.22
  160.4 3.7 %all-to-all-start.1 = ((bf16[16,1,128,2,128]{4,2,3,1,0:T(8,128)(2,1)}), bf16[16,1,128,2,128]{4,2,3,1,0:T(8,128)(2,1)S(1)}, u32[]{:S(2)}, u32[]{:S(2)}) async-start(bf16[16,1,128,2,128]{4,2,3,1,0:T(8,128)(2,1)} %copy.22), calls=%async_computation.1 | async-start | bytes 2097152 | tf_op jit(solution)/shard_map/all_to_all | solution.py:125
  164.1 53.2 %reduce-scatter.5.cloned.1.call-done = bf16[16,4096]{1,0:T(8,128)(2,1)} async-done(((bf16[256,4096]{1,0:T(8,128)(2,1)}), bf16[16,4096]{1,0:T(8,128)(2,1)}) %reduce-scatter.5.cloned.1.call-update) | async-done | bytes 131088 | tf_op jit(solution)/shard_map/reduce_scatter | solution.py:97
  217.3 0.9 copy.34
  218.2 0.8 copy.38
  219.0 0.0 all-to-all-done.1
  219.0 3.7 %all-to-all-start.2 = ((bf16[16,16,2,128]{3,2,1,0:T(2,128)(2,1)}), bf16[16,16,2,128]{3,2,1,0:T(2,128)(2,1)S(1)}, u32[]{:S(2)}, u32[]{:S(2)}) async-start(bf16[16,16,2,128]{3,2,1,0:T(2,128)(2,1)} %bitcast.73), calls=%async_computation.4 | async-start | bytes 262144 | tf_op jit(solution)/shard_map/all_to_all | solution.py:109
  222.7 1.3 copy.19
  224.0 1.0 copy.20
  225.0 5.6 %all-to-all-done.2 = bf16[16,16,2,128]{3,2,1,0:T(2,128)(2,1)S(1)} async-done(((bf16[16,16,2,128]{3,2,1,0:T(2,128)(2,1)}), bf16[16,16,2,128]{3,2,1,0:T(2,128)(2,1)S(1)}, u32[]{:S(2)}, u32[]{:S(2)}) %all-to-all-start.2) | async-done | bytes 131104 | tf_op jit(solution)/shard_map/all_to_all | solution.py:109
  230.6 3.6 %all-to-all-start = ((bf16[16,1,128,128]{3,2,1,0:T(8,128)(2,1)}), bf16[16,1,128,128]{3,2,1,0:T(8,128)(2,1)S(1)}, u32[]{:S(2)}, u32[]{:S(2)}) async-start(bf16[16,1,128,128]{3,2,1,0:T(8,128)(2,1)} %copy.20), calls=%async_computation | async-start | bytes 1048576 | tf_op jit(solution)/shard_map/all_to_all | solution.py:124
  234.2 0.1 copy.23
  234.3 0.9 slice_bitcast_fusion
  235.2 0.2 fusion.51
  235.4 13.2 %all-to-all-done = bf16[16,1,128,128]{3,2,1,0:T(8,128)(2,1)S(1)} async-done(((bf16[16,1,128,128]{3,2,1,0:T(8,128)(2,1)}), bf16[16,1,128,128]{3,2,1,0:T(8,128)(2,1)S(1)}, u32[]{:S(2)}, u32[]{:S(2)}) %all-to-all-start) | async-done | bytes 524320 | tf_op jit(solution)/shard_map/all_to_all | solution.py:124
  248.6 18.2 %while.10 = (s32[]{:T(128)}, bf16[4,512,128]{2,1,0:T(8,128)(2,1)}, bf16[4,512,128]{2,1,0:T(8,128)(2,1)S(1)}, bf16[2048,128]{1,0:T(8,128)(2,1)S(1)}, s32[]{:T(128...) while((s32[]{:T(128)}, bf16[4,512,128]{2,1,0:T(8,128)(2,1)}, ...), condition=%wide.region_12.13_spmd, body=%wide.region_7.12_spmd.sunk | while | flops 613481728 | bytes 18382212 | solution.py:147
  248.6 0.6 iota_compare_fusion.2
  249.3 0.3 fusion.78
  249.5 0.8 multiply_reduce_fusion.3
  250.3 0.1 fusion.81
  250.5 0.8 fusion.80
  251.3 0.3 fusion.79
  251.6 1.6 fusion.82
  253.2 0.6 iota_compare_fusion.2
  253.8 0.3 fusion.78
  254.1 0.8 multiply_reduce_fusion.3
  254.9 0.1 fusion.81
  255.0 0.8 fusion.80
  255.9 0.3 fusion.79
  256.1 1.6 fusion.82
  257.8 0.6 iota_compare_fusion.2
  258.4 0.3 fusion.78
  258.7 0.8 multiply_reduce_fusion.3
  259.5 0.1 fusion.81
  259.6 0.8 fusion.80
  260.4 0.3 fusion.79
  260.7 1.6 fusion.82
  262.3 0.6 iota_compare_fusion.2
  263.0 0.2 fusion.78
  263.2 0.8 multiply_reduce_fusion.3
  264.0 0.1 fusion.81
  264.1 0.8 fusion.80
  265.0 0.3 fusion.79
  265.3 1.6 fusion.82
  266.9 18.5 %all_to_all.20 = bf16[16,1,128,128]{3,2,1,0:T(8,128)(2,1)S(1)} all-to-all(bf16[16,1,128,128]{3,2,1,0:T(8,128)(2,1)} %bitcast.98), channel_id=1, replica_groups=mesh['dp'=2,'seq'=16] {'seq'}, dimensions={0} | all-to-all | bytes 1048576 | tf_op jit(solution)/shard_map/all_to_all | solution.py:150
  285.3 0.3 copy.27
  285.6 1.0 copy.28
  (34 shorter events, 0.2 us)
Async XLA Ops:
  7.2 147.2 %copy-start = (bf16[192,4096]{1,0:T(8,128)(2,1)S(1)}, bf16[192,4096]{1,0:T(8,128)(2,1)}, u32[]{:S(2)}) copy-start(bf16[192,4096]{1,0:T(8,128)(2,1)} %param.17) | copy-start | bytes 4718596
  7.2 7.7 %copy-start.4 = (bf16[3584]{0:T(1024)(128)(2,1)S(1)}, bf16[3584]{0:T(1024)(128)(2,1)}, u32[]{:S(2)}) copy-start(bf16[3584]{0:T(1024)(128)(2,1)} %param.14) | copy-start | bytes 21508
  7.2 74.6 %copy-start.3 = (bf16[256,2,192]{0,2,1:T(8,128)(2,1)S(1)}, bf16[256,2,192]{0,2,1:T(8,128)(2,1)}, u32[]{:S(2)}) copy-start(bf16[256,2,192]{0,2,1:T(8,128)(2,1)} %param.16) | copy-start | bytes 589828
  7.2 113.5 %copy-start.1 = (bf16[3584,192]{0,1:T(8,128)(2,1)S(1)}, bf16[3584,192]{0,1:T(8,128)(2,1)}, u32[]{:S(2)}) copy-start(bf16[3584,192]{0,1:T(8,128)(2,1)} %param.15) | copy-start | bytes 4128772
  7.2 71.0 %reduce-scatter.3.cloned.1.call-start = ((), (), s32[]{:S(2)}) async-start(), calls=%async_computation.6 | async-start | bytes 1949696 | tf_op jit(solution)/shard_map/reduce_scatter | solution.py:75
  14.8 105.9 %all-gather.2.cloned.1.call-start = ((), (), s32[]{:S(2)}) async-start(), calls=%async_computation.7 | async-start | bytes 1949696 | tf_op jit(solution)/shard_map/all_gather | solution.py:82
  81.0 136.3 %reduce-scatter.5.cloned.1.call-start = ((), (), s32[]{:S(2)}) async-start(), calls=%async_computation.8 | async-start | bytes 2228224 | tf_op jit(solution)/shard_map/reduce_scatter | solution.py:97
  160.4 58.6 %all-to-all-start.1 = ((bf16[16,1,128,2,128]{4,2,3,1,0:T(8,128)(2,1)}), bf16[16,1,128,2,128]{4,2,3,1,0:T(8,128)(2,1)S(1)}, u32[]{:S(2)}, u32[]{:S(2)}) async-start(bf16[16,1,128,2,128]{4,2,3,1,0:T(8,128)(2,1)} %copy.22), calls=%async_computation.1 | async-start | bytes 2097152 | tf_op jit(solution)/shard_map/all_to_all | solution.py:125
  219.0 11.6 %all-to-all-start.2 = ((bf16[16,16,2,128]{3,2,1,0:T(2,128)(2,1)}), bf16[16,16,2,128]{3,2,1,0:T(2,128)(2,1)S(1)}, u32[]{:S(2)}, u32[]{:S(2)}) async-start(bf16[16,16,2,128]{3,2,1,0:T(2,128)(2,1)} %bitcast.73), calls=%async_computation.4 | async-start | bytes 262144 | tf_op jit(solution)/shard_map/all_to_all | solution.py:109
  230.6 18.0 %all-to-all-start = ((bf16[16,1,128,128]{3,2,1,0:T(8,128)(2,1)}), bf16[16,1,128,128]{3,2,1,0:T(8,128)(2,1)S(1)}, u32[]{:S(2)}, u32[]{:S(2)}) async-start(bf16[16,1,128,128]{3,2,1,0:T(8,128)(2,1)} %copy.20), calls=%async_computation | async-start | bytes 1048576 | tf_op jit(solution)/shard_map/all_to_all | solution.py:124
  249.5 2.0 copy-start.2
  254.1 2.0 copy-start.2
  258.7 2.0 copy-start.2
  263.2 2.0 copy-start.2
Sparse Core Ops, SparseCore 0:
  15.0 63.2 reduce-scatter.2
  81.1 39.5 all-gather.1
  156.7 60.5 reduce-scatter.4
where the time goes:
time: 294 us; the launch traced here: 293 us
  waiting for transfers between devices  174 us (59%)
  blocking collectives  49.8 us (17%)
  matrix products  23.8 us (8%)
  between operations  14.6 us (5%)
  starting transfers between devices  11 us (4%)
  local copies, waits for them, and re-layouts  10.4 us (4%)
  other arithmetic  9.16 us (3%)
    reduce_scatter x1, waiting for transfers between devices, local(): lax.psum_scatter(jnp.dot(hidden_act, down_weight, preferred_element_type=...  63.3 us
    reduce_scatter x1, waiting for transfers between devices, local(): lax.psum_scatter(jnp.dot(modulated, key_value_weight, preferred_element_t...  53.2 us
    all_gather x1, waiting for transfers between devices, local(): lax.all_gather(normalize(summed, norm_gain), 'seq', axis=0, tiled=True)  38.8 us
    psum x1, blocking collectives, local(): lax.psum((jnp.sum(text_proj, 1), jnp.sum(text_proj * text_proj, 1)), 'seq')  31.3 us
    all_to_all x1, blocking collectives, local(): lax.all_to_all(back_send, 'seq', split_axis=0, concat_axis=0, tiled=True)  18.5 us
    all_to_all x1, waiting for transfers between devices, local(): lax.all_to_all(query_send, 'seq', split_axis=0, concat_axis=0, tiled=True)  13.2 us
    dot_general x1, matrix products, local(): jnp.dot(hidden_act, down_weight, preferred_element_type=jnp.float32)  7.56 us
    dot_general x4, matrix products, attend(): jnp.dot(img_weights.astype(jnp.bfloat16), value_rows, preferred_element_t...  6.4 us
  transfers between devices with their start and end apart: 6, of which 5 were waited for; matrix products, arithmetic and copies ran while one was open for 3% of the time, Pallas kernels for 0%

commit v1 on v0

v1 whole, which is shorter than its diff:
```python
import functools
import math

import jax
import jax.numpy as jnp
from jax import lax
from jax.experimental import pallas as pl
from jax.experimental.pallas import tpu as pltpu
from jax.sharding import PartitionSpec as P

HEAD_DIM = 128
HEADS = 16
TEMB = 256
VMEM_LIMIT = 56 * 1024 * 1024

epsilon = 1e-06

SMEM_SPEC = pl.BlockSpec(memory_space=pltpu.SMEM)
VMEM_SPEC = pl.BlockSpec(memory_space=pltpu.VMEM)


def params(**more):
    return pltpu.CompilerParams(vmem_limit_bytes=VMEM_LIMIT, **more)


def swap(value, mask):
    devices = lax.axis_size("seq")
    return lax.ppermute(value, "seq", [(i, i ^ mask) for i in range(devices)])


def reverse_bits(value, chips):
    count = chips.bit_length() - 1
    return sum(((value >> i) & 1) << (count - 1 - i) for i in range(count))


def normalize(summed, norm_gain):
    scale_rows = lax.rsqrt(jnp.mean(summed * summed, 1, keepdims=True) + epsilon)
    return (summed * scale_rows * norm_gain.astype(jnp.float32)).astype(jnp.bfloat16)


def time_embedding(timesteps, modulation_weight):
    half_width = TEMB // 2
    freqs = jnp.exp(-math.log(10000.0) * jnp.arange(half_width, dtype=jnp.float32) / half_width)
    angles = timesteps.astype(jnp.float32)[:, None] * freqs[None, :]
    embedding = jnp.concatenate([jnp.cos(angles), jnp.sin(angles)], 1)
    embedding = jax.nn.silu(embedding).astype(jnp.bfloat16)
    flat = modulation_weight.reshape(modulation_weight.shape[0], -1)
    product = jnp.dot(embedding, flat, preferred_element_type=jnp.float32)
    return product.reshape(timesteps.shape[0], 2, -1)


def encoder_kernel(chips, place_ref, act_ref, weight_ref, own_ref, other_ref, lhs_ref):
    chip_reversed, core = place_ref[0], place_ref[1]

    @pl.when(pl.program_id(0) == 0)
    def _():
        lhs_ref[...] = act_ref[...].T

    result = jnp.dot(lhs_ref[...], weight_ref[...], preferred_element_type=jnp.float32)
    half = result.shape[0] // 2
    share = half // chips
    first = core == 0
    own = jnp.where(first, result[:half], result[half:]).astype(own_ref.dtype)
    other = jnp.where(first, result[half:], result[:half]).astype(own_ref.dtype)
    own = own.reshape(chips, share, -1)
    other = other.reshape(chips, share, -1)
    for block in range(chips):
        at = chip_reversed ^ reverse_bits(block, chips)
        own_ref[at] = own[block]
        other_ref[at] = other[block]


def encoder(place, act, weight, chips):
    depth, rows = act.shape
    width = weight.shape[1]
    tile = 512
    share = rows // 2 // chips
    out = jax.ShapeDtypeStruct((chips, share, width), jnp.bfloat16)
    out_spec = pl.BlockSpec((chips, share, tile), lambda i: (0, 0, i))
    return pl.pallas_call(
        functools.partial(encoder_kernel, chips),
        grid=(width // tile,),
        out_shape=(out, out),
        in_specs=[
            SMEM_SPEC,
            pl.BlockSpec((depth, rows), lambda i: (0, 0)),
            pl.BlockSpec((depth, tile), lambda i: (0, i)),
        ],
        out_specs=(out_spec, out_spec),
        scratch_shapes=[pltpu.VMEM((rows, depth), jnp.bfloat16)],
        compiler_params=params(),
        cost_estimate=pl.CostEstimate(
            flops=2 * rows * depth * width,
            bytes_accessed=2 * (depth * rows + depth * width + rows * width),
            transcendentals=0,
        ),
        name="encoder",
    )(place, act, weight)


def project_kernel(chips, count, place_ref, *refs):
    pieces, refs = refs[:count], refs[count:]
    win0, win1, kv0, kv1, mod0, mod1, out_ref, sums_ref, states, lhs0, lhs1, sums = refs
    chip = place_ref[2]
    row = 0
    for piece in pieces:
        states[row : row + piece.shape[0], :] = piece[...]
        row += piece.shape[0]
    share = row // chips
    contract = (((1,), (1,)), ((), ()))
    proj0 = lax.dot_general(states[...], win0[...], contract, preferred_element_type=jnp.float32)
    proj1 = lax.dot_general(states[...], win1[...], contract, preferred_element_type=jnp.float32)
    first = jnp.sum(proj0, 1, keepdims=True) + jnp.sum(proj1, 1, keepdims=True)
    second = jnp.sum(proj0 * proj0, 1, keepdims=True) + jnp.sum(proj1 * proj1, 1, keepdims=True)
    lane = lax.broadcasted_iota(jnp.int32, sums.shape, 1)
    both = jnp.where(lane == 0, first, second)
    scaled0 = proj0 * (1.0 + mod0[1:2, :])
    scaled1 = proj1 * (1.0 + mod1[1:2, :])
    for at in range(chips):
        rows = pl.ds(pl.multiple_of((chip ^ reverse_bits(at, chips)) * share, share), share)
        lhs0[rows, :] = scaled0[at * share : (at + 1) * share]
        lhs1[rows, :] = scaled1[at * share : (at + 1) * share]
        sums[rows, :] = both[at * share : (at + 1) * share]
    sums_ref[...] = sums[...].T[: sums_ref.shape[0]]
    left0 = lhs0[...].astype(jnp.bfloat16)
    left1 = lhs1[...].astype(jnp.bfloat16)
    width = out_ref.shape[2] // 2
    half = kv0.shape[1] // 2
    for at in range(chips):
        for part in range(2):
            column = part * half + (chip ^ reverse_bits(at, chips)) * width
            columns = pl.ds(pl.multiple_of(column, width), width)
            value = jnp.dot(left0, kv0[:, columns], preferred_element_type=jnp.float32)
            value += jnp.dot(left1, kv1[:, columns], preferred_element_type=jnp.float32)
            out_ref[at, :, part * width : (part + 1) * width] = value.astype(out_ref.dtype)


def project(place, pieces, win0, win1, kv0, kv1, mod0, mod1, chips):
    rows = sum(piece.shape[0] for piece in pieces)
    features, depth = win0.shape
    width = kv0.shape[1]
    return pl.pallas_call(
        functools.partial(project_kernel, chips, len(pieces)),
        out_shape=(
            jax.ShapeDtypeStruct((chips, rows, width // chips), jnp.bfloat16),
            jax.ShapeDtypeStruct((8, rows), jnp.float32),
        ),
        in_specs=[SMEM_SPEC] + [VMEM_SPEC] * (len(pieces) + 6),
        out_specs=(VMEM_SPEC, VMEM_SPEC),
        scratch_shapes=[
            pltpu.VMEM((rows, depth), jnp.bfloat16),
            pltpu.VMEM((rows, features), jnp.float32),
            pltpu.VMEM((rows, features), jnp.float32),
            pltpu.VMEM((rows, 128), jnp.float32),
        ],
        compiler_params=params(),
        cost_estimate=pl.CostEstimate(
            flops=4 * rows * features * (depth + width),
            bytes_accessed=2 * (rows * depth + 2 * features * (depth + width) + rows * width),
            transcendentals=0,
        ),
        name="project",
    )(place, *pieces, win0, win1, kv0, kv1, mod0, mod1)


def image_kernel(factor, queries_ref, keys_ref, values_ref, sum_ref, norm_ref):
    contract = (((1,), (1,)), ((), ()))
    queries = queries_ref[...].reshape(-1, HEAD_DIM)
    keys = keys_ref[...].reshape(-1, HEAD_DIM)
    values = values_ref[...].reshape(-1, HEAD_DIM)
    scores = lax.dot_general(queries, keys, contract, preferred_element_type=jnp.float32) * factor
    top = jnp.max(scores, 1, keepdims=True)
    weights = jnp.exp2(scores - top)
    total = jnp.sum(weights, 1, keepdims=True)
    sum_ref[...] = jnp.dot(weights.astype(jnp.bfloat16), values, preferred_element_type=jnp.float32)
    lane = lax.broadcasted_iota(jnp.int32, norm_ref.shape, 1)
    norm_ref[...] = jnp.where(lane < 64, top, total)


def image_attention(packed, img_dev, part_rows, factor):
    devices = packed.shape[0]
    count = devices * part_rows
    group = max(1, 256 // part_rows)
    block = group * part_rows
    at = 2 * img_dev // part_rows
    out = jax.ShapeDtypeStruct((count, HEAD_DIM), jnp.float32)
    out_spec = pl.BlockSpec((block, HEAD_DIM), lambda i: (i, 0))
    keys = devices * img_dev
    return pl.pallas_call(
        functools.partial(image_kernel, factor),
        grid=(devices // group,),
        out_shape=(out, out),
        in_specs=[
            pl.BlockSpec((group, part_rows, HEAD_DIM), lambda i: (i, at, 0)),
            pl.BlockSpec((devices, img_dev, HEAD_DIM), lambda i: (0, 0, 0)),
            pl.BlockSpec((devices, img_dev, HEAD_DIM), lambda i: (0, 1, 0)),
        ],
        out_specs=(out_spec, out_spec),
        compiler_params=params(),
        cost_estimate=pl.CostEstimate(
            flops=4 * count * keys * HEAD_DIM,
            bytes_accessed=4 * keys * HEAD_DIM + 10 * count * HEAD_DIM,
            transcendentals=count * keys,
        ),
        name="image_attention",
    )(packed, packed, packed)


def finish_kernel(factor, place_ref, queries_ref, sum_ref, norm_ref, mine_ref, got_ref, out_ref):
    core, valid = place_ref[1], place_ref[3]
    devices, part_rows = queries_ref.shape[0], queries_ref.shape[1]
    half = mine_ref.shape[0]
    contract = (((1,), (1,)), ((), ()))
    mine, got = mine_ref[...], got_ref[...]
    keys = jnp.concatenate([mine[:, :HEAD_DIM], got[:, :HEAD_DIM]], 0)
    values = jnp.concatenate([mine[:, HEAD_DIM:], got[:, HEAD_DIM:]], 0)
    lane = lax.broadcasted_iota(jnp.int32, (1, 2 * half), 1)
    position = jnp.where((lane >= half) == (core == 0), half, 0) + lane % half
    group = max(1, 512 // part_rows)
    rows = group * part_rows
    for step in range(devices // group):
        span = slice(step * rows, (step + 1) * rows)
        queries = queries_ref[step * group : (step + 1) * group].reshape(rows, HEAD_DIM)
        scores = lax.dot_general(queries, keys, contract, preferred_element_type=jnp.float32) * factor
        scores = jnp.where(position < valid, scores, -jnp.inf)
        before = norm_ref[span, 0:1]
        top = jnp.maximum(before, jnp.max(scores, 1, keepdims=True))
        rescale = jnp.exp2(before - top)
        weights = jnp.exp2(scores - top)
        total = norm_ref[span, 64:65] * rescale + jnp.sum(weights, 1, keepdims=True)
        mixed = sum_ref[span, :] * rescale + jnp.dot(
            weights.astype(jnp.bfloat16), values, preferred_element_type=jnp.float32
        )
        mixed = (mixed / total).astype(out_ref.dtype)
        out_ref[step * group : (step + 1) * group, :part_rows, :] = mixed.reshape(group, part_rows, HEAD_DIM)
    low = jnp.where(core == 0, mine.astype(jnp.float32), got.astype(jnp.float32))
    high = jnp.where(core == 0, got.astype(jnp.float32), mine.astype(jnp.float32))
    share = 2 * half // devices
    for device in range(devices):
        source = low if device < devices // 2 else high
        start = device * share % half
        block = source[start : start + share]
        block = jnp.concatenate([block[:, :HEAD_DIM], block[:, HEAD_DIM:]], 0)
        out_ref[device, part_rows:, :] = block.astype(out_ref.dtype)


def finish(place, packed, summed, norms, mine, got, img_dev, part_rows, factor):
    devices = packed.shape[0]
    share = 2 * mine.shape[0] // devices
    count = devices * part_rows
    at = 2 * img_dev // part_rows
    return pl.pallas_call(
        functools.partial(finish_kernel, factor),
        grid=(1,),
        out_shape=jax.ShapeDtypeStruct((devices, part_rows + 2 * share, HEAD_DIM), jnp.bfloat16),
        in_specs=[
            SMEM_SPEC,
            pl.BlockSpec((devices, part_rows, HEAD_DIM), lambda i: (0, at, 0)),
            pl.BlockSpec((count, HEAD_DIM), lambda i: (0, 0)),
            pl.BlockSpec((count, HEAD_DIM), lambda i: (0, 0)),
            VMEM_SPEC,
            VMEM_SPEC,
        ],
        out_specs=pl.BlockSpec((devices, part_rows + 2 * share, HEAD_DIM), lambda i: (0, 0, 0)),
        compiler_params=params(),
        cost_estimate=pl.CostEstimate(
            flops=4 * count * 2 * mine.shape[0] * HEAD_DIM,
            bytes_accessed=12 * count * HEAD_DIM,
            transcendentals=count * 2 * mine.shape[0],
        ),
        name="finish",
    )(place, packed, summed, norms, mine, got)


def scatter_chips(blocks, chips):
    step = 2
    while blocks.shape[0] > 1:
        half = blocks.shape[0] // 2
        got = swap(blocks[half:].astype(jnp.bfloat16), step)
        blocks = blocks[:half] + got.astype(jnp.float32)
        step *= 2
    return blocks[0]


def gather_chips(piece, chips):
    pieces = piece
    step = chips
    while step > 1:
        pieces = jnp.concatenate([pieces, swap(pieces, step)], 0)
        step //= 2
    return pieces


def local(
    enc_act,
    down_weight,
    norm_gain,
    text_in_weight,
    modulation_weight,
    key_value_weight,
    timesteps,
    lengths,
    image_queries,
    image_key_values,
):
    devices = lax.axis_size("seq")
    chips = devices // 2
    copies = devices // HEADS
    text_len = enc_act.shape[1]
    share = text_len // devices
    img_dev = image_queries.shape[1]
    part_rows = img_dev // copies
    factor = math.log2(math.e) / math.sqrt(HEAD_DIM)
    index = lax.axis_index("seq")
    chip, core = index // 2, index % 2
    place = jnp.stack([reverse_bits(chip, chips), core, chip, lengths[0]]).astype(jnp.int32)

    pairs = image_key_values.reshape(img_dev, 2, HEADS, HEAD_DIM).transpose(2, 1, 0, 3)
    pairs = pairs.reshape(HEADS, 1, 2 * img_dev, HEAD_DIM)
    pairs = jnp.broadcast_to(pairs, (HEADS, copies, 2 * img_dev, HEAD_DIM))
    queries = image_queries.reshape(copies, part_rows, HEADS, HEAD_DIM).transpose(2, 0, 1, 3)
    packed = jnp.concatenate([pairs, queries], 2).reshape(devices, 2 * img_dev + part_rows, HEAD_DIM)
    packed = lax.all_to_all(packed, "seq", split_axis=0, concat_axis=0, tiled=True)

    win0, kv0 = text_in_weight.T, key_value_weight
    win1, kv1 = swap(win0, 1), swap(kv0, 1)
    mod0 = time_embedding(timesteps, modulation_weight)[0]
    mod1 = swap(mod0, 1)
    lines = jnp.stack([1.0 + mod0[1], mod0[0]])
    lines_high = lines.astype(jnp.bfloat16)
    lines_low = (lines - lines_high.astype(jnp.float32)).astype(jnp.bfloat16)
    lines = jnp.dot(
        jnp.concatenate([lines_high, lines_low]), kv0, preferred_element_type=jnp.float32
    )
    lines = lines[:2] + lines[2:]
    step = 1
    while step < devices:
        lines = lines + swap(lines, step)
        step *= 2
    width = HEADS * HEAD_DIM // chips
    lines = lax.dynamic_index_in_dim(lines.reshape(2, 2, chips, width), chip, 2, keepdims=False)
    lines = lines.reshape(2, 2 * width)

    own, other = encoder(place, enc_act[0].T, down_weight, chips)
    got = swap(other, 1)
    summed = scatter_chips(own.astype(jnp.float32) + got.astype(jnp.float32), chips)
    states = gather_chips(normalize(summed, norm_gain), chips)

    partial, sums = project(place, [states], win0, win1, kv0, kv1, mod0, mod1, chips)
    step = 2
    while step < devices:
        sums = sums + swap(sums, step)
        step *= 2
    total = scatter_chips(partial.astype(jnp.float32), chips)
    model_width = text_in_weight.shape[1] * devices
    mean_val = sums[0] / model_width
    variance = sums[1] / model_width - mean_val * mean_val
    text = (total - mean_val[:, None] * lines[0]) * lax.rsqrt(variance + epsilon)[:, None] + lines[1]
    text = text.astype(jnp.bfloat16).reshape(text_len // 2, 2, 2 // copies, HEAD_DIM)
    if copies == 1:
        mine = lax.dynamic_index_in_dim(text, core, 2, keepdims=False)
        sent = lax.dynamic_index_in_dim(text, 1 - core, 2, keepdims=False)
    else:
        mine = sent = text
    mine = mine.reshape(text_len // 2, 2 * HEAD_DIM)
    got = swap(sent.reshape(text_len // 2, 2 * HEAD_DIM), 1)

    image_sum, norms = image_attention(packed, img_dev, part_rows, factor)
    back = finish(place, packed, image_sum, norms, mine, got, img_dev, part_rows, factor)
    back = lax.all_to_all(back, "seq", split_axis=0, concat_axis=0, tiled=True)
    back = back.reshape(HEADS, copies, part_rows + 2 * share, HEAD_DIM)
    attended = back[:, :, :part_rows].transpose(1, 2, 0, 3).reshape(1, img_dev, HEADS * HEAD_DIM)
    text_kv = back[:, 0, part_rows:].reshape(HEADS, 2, share, HEAD_DIM).transpose(2, 1, 0, 3)
    return (attended, text_kv.reshape(share, 2 * HEADS * HEAD_DIM))


def solution(mesh):
    in_specs = (
        P("dp", None, "seq"),
        P("seq", None),
        P(),
        P(None, "seq"),
        P(None, None, "seq"),
        P("seq", None),
        P("dp"),
        P("dp"),
        P("dp", "seq", None),
        P("dp", "seq", None, None),
    )
    out_specs = (P("dp", "seq", None), P(("dp", "seq"), None))
    return jax.shard_map(local, mesh=mesh, in_specs=in_specs, out_specs=out_specs, check_vma=False)
```

time: 294 us -> 182 us (0.62)
  waiting for transfers between devices: 174 us -> 71.3 us
  Pallas kernels: 0 us -> 31 us
  blocking collectives: 49.8 us -> 22.1 us
  matrix products: 23.8 us -> 0.5 us
  starting transfers between devices: 11 us -> 28.3 us
  between operations: 14.6 us -> 2.35 us
  local copies, waits for them, and re-layouts: 10.4 us -> 13.4 us
    reduce_scatter x2 -> x0, waiting for transfers between devices: 117 us -> none  [the longest x1 63.3 us: local(): lax.psum_scatter(jnp.dot(hidden_act, down_weight, preferred_element_type=...]
    ppermute x0 -> x21, waiting for transfers between devices: none -> 71.3 us  [swap(): return lax.ppermute(value, 'seq', [(i, i ^ mask) for i in range(devices)])]
    all_gather x1 -> x0, waiting for transfers between devices: 38.8 us -> none  [local(): lax.all_gather(normalize(summed, norm_gain), 'seq', axis=0, tiled=True)]
    psum x1 -> x0, blocking collectives: 31.3 us -> none  [local(): lax.psum((jnp.sum(text_proj, 1), jnp.sum(text_proj * text_proj, 1)), 'seq')]
    pallas_call x0 -> x4, Pallas kernels: none -> 31 us  [the longest x1 10.8 us: image_attention(): pl.pallas_call(functools.partial(image_kernel, factor), grid=(devices //...]
    ppermute x0 -> x21, starting transfers between devices: none -> 24.4 us  [swap(): return lax.ppermute(value, 'seq', [(i, i ^ mask) for i in range(devices)])]
    dot_general x19 -> x1, matrix products: 23.7 us -> 0.31 us  [local(): jnp.dot(jnp.concatenate([lines_high, lines_low]), kv0, preferred_element_...]
    all_to_all x3 -> x1, waiting for transfers between devices: 18.8 us -> 0.01 us  [local(): lax.all_to_all(packed, 'seq', split_axis=0, concat_axis=0, tiled=True)]
  transfers between devices with their start and end apart: 6 -> 22, of which waited for: 5 -> 13; matrix products, arithmetic and copies ran while one was open for 3% -> 11% of each run, Pallas kernels for 0% -> 9%
where the time goes in v1:
time: 182 us; the launch traced here: 181 us
  waiting for transfers between devices  71.3 us (39%)
  Pallas kernels  31 us (17%)
  starting transfers between devices  28.3 us (16%)
  blocking collectives  22.1 us (12%)
  local copies, waits for them, and re-layouts  13.4 us (7%)
  other arithmetic  12 us (7%)
  between operations  2.35 us (1%)
    ppermute x21, waiting for transfers between devices, swap(): return lax.ppermute(value, 'seq', [(i, i ^ mask) for i in range(devices)])  71.3 us
    ppermute x21, starting transfers between devices, swap(): return lax.ppermute(value, 'seq', [(i, i ^ mask) for i in range(devices)])  24.4 us
    all_to_all x1, blocking collectives, local(): back = lax.all_to_all(back, 'seq', split_axis=0, concat_axis=0, tiled=True)  22.1 us
    pallas_call x1, Pallas kernels, image_attention(): pl.pallas_call(functools.partial(image_kernel, factor), grid=(devices //...  10.8 us
    pallas_call x1, Pallas kernels, encoder(): pl.pallas_call(functools.partial(encoder_kernel, chips), grid=(width // t...  8.76 us
    pallas_call x1, Pallas kernels, finish(): pl.pallas_call(functools.partial(finish_kernel, factor), grid=(1,), out_s...  5.8 us
    pallas_call x1, Pallas kernels, project(): pl.pallas_call(functools.partial(project_kernel, chips, len(pieces)), out...  5.7 us
    unnamed x22, local copies, waits for them, and re-layouts  5.53 us
  transfers between devices with their start and end apart: 22, of which 13 were waited for; matrix products, arithmetic and copies ran while one was open for 11% of the time, Pallas kernels for 9%

profile of v1, /device:TPU:0, one launch (start us, length us, event | category | flops | bytes accessed | tf_op | source)
XLA Modules:
  0.0 180.9 jit_solution(9352087532762713780)
XLA Ops:
  1.4 0.6 pad_add_fusion.place_ref
  1.9 8.8 %encoder.1 = (bf16[8,16,3584]{2,1,0:T(8,128)(2,1)}, bf16[8,16,3584]{2,1,0:T(8,128)(2,1)}) custom-call(s32[4]{0:T(128)} %pad_add_fusion.place_ref, bf16[1184,256]{1,0:T(8,128)(2,1)} %bitcast.77, bf16[1184,3584]{1,0:T(8,128)(2,1)} %weight_ref.1), custom_call_target="tpu_custom_call" | custom-call | flops 2172649472 | bytes 10928128 | tf_op jit(solution)/shard_map/encoder/pallas_call | solution.py:80
  10.7 0.5 collective-permute-start
  11.1 2.3 %collective-permute-done = bf16[8,16,3584]{2,1,0:T(8,128)(2,1)S(1)} collective-permute-done((bf16[8,16,3584]{2,1,0:T(8,128)(2,1)}, bf16[8,16,3584]{2,1,0:T(8,128)(2,1)S(1)}, u32[]{:S(2)}, u32[]{:S(2)}) %collective-permute-start) | collective-permute-done | bytes 917536 | tf_op jit(solution)/shard_map/ppermute | solution.py:28
  13.5 1.4 convert_add_fusion
  15.0 2.9 %collective-permute-start.1 = (bf16[4,16,3584]{2,1,0:T(8,128)(2,1)S(1)}, bf16[4,16,3584]{2,1,0:T(8,128)(2,1)S(1)}, u32[]{:S(2)}, u32[]{:S(2)}) collective-permute-start(bf16[4,16,3584]{2,1,0:T(8,128)(2,1)S(1)} %slice.145), channel_id=1, source_target_pairs={{0,2},{1,3},{2,0},{3,1},{4,6},{5,7},{6,4},{7,5},{8,10},{9,11},{10,... | collective-permute-start | bytes 1376264 | tf_op jit(solution)/shard_map/ppermute | solution.py:28
  18.6 10.1 %collective-permute-done.1 = bf16[4,16,3584]{2,1,0:T(8,128)(2,1)S(1)} collective-permute-done((bf16[4,16,3584]{2,1,0:T(8,128)(2,1)S(1)}, bf16[4,16,3584]{2,1,0:T(8,128)(2,1)S(1)}, u32[]{:S(2)}, u32[]{:S(2)}) %collective-permute-start.1) | collective-permute-done | bytes 458784 | tf_op jit(solution)/shard_map/ppermute | solution.py:28
  28.7 0.1 slice_add_fusion
  28.9 1.9 %collective-permute-start.2 = (bf16[2,16,3584]{2,1,0:T(8,128)(2,1)S(1)}, bf16[2,16,3584]{2,1,0:T(8,128)(2,1)}, u32[]{:S(2)}, u32[]{:S(2)}) collective-permute-start(bf16[2,16,3584]{2,1,0:T(8,128)(2,1)S(1)} %slice.147), channel_id=1, source_target_pairs={{0,4},{1,5},{2,6},{3,7},{4,0},{5,1},{6,2},{7,3},{8,12},{9,13},{10,... | collective-permute-start | bytes 688136 | tf_op jit(solution)/shard_map/ppermute | solution.py:28
  30.8 0.2 convolution_reduce_fusion
  31.0 0.7 squeeze_reshape.3.refs_5_
  31.6 0.5 collective-permute-start.7
  32.2 4.0 %collective-permute-done.2 = bf16[2,16,3584]{2,1,0:T(8,128)(2,1)} collective-permute-done((bf16[2,16,3584]{2,1,0:T(8,128)(2,1)S(1)}, bf16[2,16,3584]{2,1,0:T(8,128)(2,1)}, u32[]{:S(2)}, u32[]{:S(2)}) %collective-permute-start.2) | collective-permute-done | bytes 229408 | tf_op jit(solution)/shard_map/ppermute | solution.py:28
  36.2 1.0 slice_add_fusion.2
  37.2 2.6 %collective-permute-start.3 = (bf16[1,16,3584]{2,1,0:T(8,128)(2,1)S(1)}, bf16[1,16,3584]{2,1,0:T(8,128)(2,1)S(1)}, u32[]{:S(2)}, u32[]{:S(2)}) collective-permute-start(bf16[1,16,3584]{2,1,0:T(8,128)(2,1)S(1)} %slice.149), channel_id=1, source_target_pairs={{0,8},{1,9},{2,10},{3,11},{4,12},{5,13},{6,14},{7,15},{8,0},{9,1},... | collective-permute-start | bytes 344072 | tf_op jit(solution)/shard_map/ppermute | solution.py:28
  39.8 4.5 %collective-permute-done.3 = bf16[1,16,3584]{2,1,0:T(8,128)(2,1)S(1)} collective-permute-done((bf16[1,16,3584]{2,1,0:T(8,128)(2,1)S(1)}, bf16[1,16,3584]{2,1,0:T(8,128)(2,1)S(1)}, u32[]{:S(2)}, u32[]{:S(2)}) %collective-permute-start.3) | collective-permute-done | bytes 114720 | tf_op jit(solution)/shard_map/ppermute | solution.py:28
  44.4 0.2 multiply_reduce_fusion
  44.5 0.1 multiply_convert_fusion
  44.6 1.2 collective-permute-start.4
  45.9 5.8 %collective-permute-done.4 = bf16[16,3584]{1,0:T(8,128)(2,1)S(1)} collective-permute-done((bf16[16,3584]{1,0:T(8,128)(2,1)S(1)}, bf16[16,3584]{1,0:T(8,128)(2,1)S(1)}, u32[]{:S(2)}, u32[]{:S(2)}) %collective-permute-start.4) | collective-permute-done | bytes 114720 | tf_op jit(solution)/shard_map/ppermute | solution.py:28
  51.8 0.3 fusion.4
  52.1 5.7 %collective-permute-done.5 = bf16[32,3584]{1,0:T(8,128)(2,1)S(1)} collective-permute-done((bf16[32,3584]{1,0:T(8,128)(2,1)S(1)}, bf16[32,3584]{1,0:T(8,128)(2,1)S(1)}, u32[]{:S(2)}, u32[]{:S(2)}) %collective-permute-start.5) | collective-permute-done | bytes 229408 | tf_op jit(solution)/shard_map/ppermute | solution.py:28
  57.8 0.9 pad_maximum_fusion.1
  58.7 1.2 collective-permute-start.6
  60.0 2.5 %reshape.135 = bf16[128,2,16,128]{3,2,1,0:T(8,128)(2,1)} reshape(bf16[1,128,2,2048]{3,2,1,0:T(2,128)(2,1)} %param.19) | data formatting | bytes 2097152 | tf_op jit(solution)/shard_map/reshape | solution.py:318
  62.5 1.6 copy.17
  64.2 1.3 copy.18
  65.5 1.0 copy.19
  66.5 2.3 %maximum_bitcast_fusion = bf16[16,384,128]{2,1,0:T(8,128)(2,1)} fusion(bf16[16,1,128,128]{3,2,0,1:T(8,128)(2,1)} %bitcast.74, bf16[16,1,256,128]{3,2,0,1:T(8,128)(2,1)S(1)} %bitcast.69), kind=kLoop, calls=%fused_computation.1 | loop fusion | flops 3145728 | bytes 3145728 | tf_op jit(solution)/shard_map/reshape | solution.py:322
  68.8 3.9 %all-to-all-start = ((bf16[16,384,128]{2,1,0:T(8,128)(2,1)}), bf16[16,384,128]{2,1,0:T(8,128)(2,1)S(1)}, u32[]{:S(2)}, u32[]{:S(2)}) async-start(bf16[16,384,128]{2,1,0:T(8,128)(2,1)} %maximum_bitcast_fusion), calls=%async_computation | async-start | bytes 3145728 | tf_op jit(solution)/shard_map/all_to_all | solution.py:323
  72.8 2.1 %pad_maximum_fusion.refs_0_ = bf16[128,3584]{1,0:T(8,128)(2,1)} fusion(bf16[64,3584]{1,0:T(8,128)(2,1)} %collective-permute-done.6, bf16[32,3584]{1,0:T(8,128)(2,1)} %copy-done.5, bf16[16,3584]{1,0:T(8,128)(2,1)} %copy-done.4, bf16[16,3584]{1,0:T(8,128)(2,1)S(1)} %multiply_convert_fusion), kind=kLoop, calls=%fused_computation.6 | loop fusion | flops 3670016 | bytes 1835008 | tf_op jit(solution)/shard_map/concatenate | solution.py:289
  74.9 5.7 %project.1 = (bf16[8,128,512]{2,1,0:T(8,128)(2,1)}, f32[8,128]{1,0:T(8,128)}) custom-call(s32[4]{0:T(128)} %pad_add_fusion.place_ref, bf16[128,3584]{1,0:T(8,128)(2,1)} %pad_maximum_fusion.refs_0_, bf16[192,3584]{1,0:T(8,128)(2,1)} %bitcast.76, bf16[192,3584]{1,0:T(8,128)(2,1)} %collective-permute-done.7.refs_2_, bf16[192,4096]{1,0:T(8,128)(2,1)} %refs_3_.1, ...), custom_call_target="tpu_custom_call" | custom-call | flops 754974720 | bytes 7864320 | tf_op jit(solution)/shard_map/project/pallas_call | solution.py:142
  80.6 1.2 slice.89
  81.8 2.0 %collective-permute-start.10 = (bf16[4,128,512]{2,1,0:T(8,128)(2,1)S(1)}, bf16[4,128,512]{2,1,0:T(8,128)(2,1)}, u32[]{:S(2)}, u32[]{:S(2)}) collective-permute-start(bf16[4,128,512]{2,1,0:T(8,128)(2,1)S(1)} %slice.89), channel_id=1, source_target_pairs={{0,2},{1,3},{2,0},{3,1},{4,6},{5,7},{6,4},{7,5},{8,10},{9,11},{10,... | collective-permute-start | bytes 1572872 | tf_op jit(solution)/shard_map/ppermute | solution.py:28
  83.8 0.8 fusion.18
  84.6 0.2 collective-permute-start.17
  84.7 20.7 %collective-permute-done.17 = f32[2,4096]{1,0:T(2,128)S(1)} collective-permute-done((f32[2,4096]{1,0:T(2,128)S(1)}, f32[2,4096]{1,0:T(2,128)S(1)}, u32[]{:S(2)}, u32[]{:S(2)}) %collective-permute-start.17) | collective-permute-done | bytes 32800 | tf_op jit(solution)/shard_map/ppermute | solution.py:28
  105.5 1.5 collective-permute-start.18
  107.0 2.5 %collective-permute-done.18 = f32[2,4096]{1,0:T(2,128)S(1)} collective-permute-done((f32[2,4096]{1,0:T(2,128)S(1)}, f32[2,4096]{1,0:T(2,128)S(1)}, u32[]{:S(2)}, u32[]{:S(2)}) %collective-permute-start.18) | collective-permute-done | bytes 32800 | tf_op jit(solution)/shard_map/ppermute | solution.py:28
  109.5 1.7 collective-permute-start.19
  111.2 2.5 %collective-permute-start.13 = (f32[8,128]{1,0:T(8,128)}, f32[8,128]{1,0:T(8,128)S(1)}, u32[]{:S(2)}, u32[]{:S(2)}) collective-permute-start(f32[8,128]{1,0:T(8,128)} %get-tuple-element.13), channel_id=1, source_target_pairs={{0,2},{1,3},{2,0},{3,1},{4,6},{5,7},{6,4},{7,5},{8,10},{9,11},{10,... | collective-permute-start | bytes 12296 | tf_op jit(solution)/shard_map/ppermute | solution.py:28
  113.7 1.8 collective-permute-done.13
  115.5 0.7 add.126
  116.2 1.8 collective-permute-start.14
  118.0 1.8 collective-permute-done.14
  119.8 0.8 collective-permute-start.15
  120.6 1.2 convert_add_fusion.1
  121.9 1.5 collective-permute-start.11
  123.4 0.9 collective-permute-done.15
  124.3 5.4 %collective-permute-done.11 = bf16[2,128,512]{2,1,0:T(8,128)(2,1)S(1)} collective-permute-done((bf16[2,128,512]{2,1,0:T(8,128)(2,1)S(1)}, bf16[2,128,512]{2,1,0:T(8,128)(2,1)S(1)}, u32[]{:S(2)}, u32[]{:S(2)}) %collective-permute-start.11) | collective-permute-done | bytes 262176 | tf_op jit(solution)/shard_map/ppermute | solution.py:28
  129.8 1.4 collective-permute-start.12
  131.3 5.6 %collective-permute-done.12 = bf16[1,128,512]{2,1,0:T(8,128)(2,1)S(1)} collective-permute-done((bf16[1,128,512]{2,1,0:T(8,128)(2,1)S(1)}, bf16[1,128,512]{2,1,0:T(8,128)(2,1)S(1)}, u32[]{:S(2)}, u32[]{:S(2)}) %collective-permute-start.12) | collective-permute-done | bytes 131104 | tf_op jit(solution)/shard_map/ppermute | solution.py:28
  136.9 0.2 squeeze.19
  137.1 0.3 fusion.2
  137.5 0.1 constant_dynamic-slice_fusion.1
  137.7 1.2 copy-done.1
  138.9 10.8 %image_attention.1 = (f32[2048,128]{1,0:T(8,128)}, f32[2048,128]{1,0:T(8,128)}) custom-call(bf16[16,384,128]{2,1,0:T(8,128)(2,1)} %copy-done.1, bf16[16,384,128]{2,1,0:T(8,128)(2,1)} %copy-done.1, bf16[16,384,128]{2,1,0:T(8,128)(2,1)} %copy-done.1), custom_call_target="tpu_custom_call" | custom-call | flops 2147483648 | bytes 3670016 | tf_op jit(solution)/shard_map/image_attention/pallas_call | solution.py:189
  149.6 0.6 copy.43
  150.3 0.6 copy-done.6
  150.9 5.8 %finish.1 = bf16[16,160,128]{2,1,0:T(8,128)(2,1)} custom-call(s32[4]{0:T(128)} %pad_add_fusion.place_ref, bf16[16,384,128]{2,1,0:T(8,128)(2,1)} %copy-done.1, f32[2048,128]{1,0:T(8,128)} %get-tuple-element.8.sum_ref, f32[2048,128]{1,0:T(8,128)} %get-tuple-element.9.norm_ref, bf16[128,256]{1,0:T(8,128)(2,1)} %bitcast.80, bf16[128,256]{1,0:T(8,128)(2,1)} %copy-done.6), custom_call_target="tpu_custom_call" | custom-call | flops 268435456 | bytes 3145728 | tf_op jit(solution)/shard_map/finish/pallas_call | solution.py:252
  156.7 22.1 %all_to_all.10 = bf16[16,160,128]{2,1,0:T(8,128)(2,1)S(1)} all-to-all(bf16[16,160,128]{2,1,0:T(8,128)(2,1)} %finish.1), channel_id=1, replica_groups=mesh['dp'=2,'seq'=16] {'seq'}, dimensions={0} | all-to-all | bytes 1310720 | tf_op jit(solution)/shard_map/all_to_all | solution.py:370
  178.9 0.3 copy.23
  179.1 1.0 copy.25
  180.2 0.7 copy.41
  (60 shorter events, 1.0 us)
Async XLA Ops:
  0.6 30.1 %copy-start = (bf16[256,2,192]{0,2,1:T(8,128)(2,1)S(1)}, bf16[256,2,192]{0,2,1:T(8,128)(2,1)}, u32[]{:S(2)}) copy-start(bf16[256,2,192]{0,2,1:T(8,128)(2,1)} %param.14) | copy-start | bytes 589828
  10.7 2.8 %collective-permute-start = (bf16[8,16,3584]{2,1,0:T(8,128)(2,1)}, bf16[8,16,3584]{2,1,0:T(8,128)(2,1)S(1)}, u32[]{:S(2)}, u32[]{:S(2)}) collective-permute-start(bf16[8,16,3584]{2,1,0:T(8,128)(2,1)} %get-tuple-element.11), channel_id=1, source_target_pairs={{0,1},{1,0},{2,3},{3,2},{4,5},{5,4},{6,7},{7,6},{8,9},{9,8},{10,11... | collective-permute-start | bytes 2752520 | tf_op jit(solution)/shard_map/ppermute | solution.py:28
  14.9 17.3 %copy-start.2 = (bf16[192,4096]{1,0:T(8,128)(2,1)S(1)}, bf16[192,4096]{1,0:T(8,128)(2,1)}, u32[]{:S(2)}) copy-start(bf16[192,4096]{1,0:T(8,128)(2,1)} %refs_3_.1) | copy-start | bytes 4718596
  14.9 17.3 %copy-start.7 = (bf16[3584]{0:T(1024)(128)(2,1)S(1)}, bf16[3584]{0:T(1024)(128)(2,1)}, u32[]{:S(2)}) copy-start(bf16[3584]{0:T(1024)(128)(2,1)} %param.12) | copy-start | bytes 21508
  15.0 13.7 %collective-permute-start.1 = (bf16[4,16,3584]{2,1,0:T(8,128)(2,1)S(1)}, bf16[4,16,3584]{2,1,0:T(8,128)(2,1)S(1)}, u32[]{:S(2)}, u32[]{:S(2)}) collective-permute-start(bf16[4,16,3584]{2,1,0:T(8,128)(2,1)S(1)} %slice.145), channel_id=1, source_target_pairs={{0,2},{1,3},{2,0},{3,1},{4,6},{5,7},{6,4},{7,5},{8,10},{9,11},{10,... | collective-permute-start | bytes 1376264 | tf_op jit(solution)/shard_map/ppermute | solution.py:28
  28.9 7.3 %collective-permute-start.2 = (bf16[2,16,3584]{2,1,0:T(8,128)(2,1)S(1)}, bf16[2,16,3584]{2,1,0:T(8,128)(2,1)}, u32[]{:S(2)}, u32[]{:S(2)}) collective-permute-start(bf16[2,16,3584]{2,1,0:T(8,128)(2,1)S(1)} %slice.147), channel_id=1, source_target_pairs={{0,4},{1,5},{2,6},{3,7},{4,0},{5,1},{6,2},{7,3},{8,12},{9,13},{10,... | collective-permute-start | bytes 688136 | tf_op jit(solution)/shard_map/ppermute | solution.py:28
  31.6 43.3 %collective-permute-start.9 = (f32[2,192]{1,0:T(2,128)}, f32[2,192]{1,0:T(2,128)}, u32[]{:S(2)}, u32[]{:S(2)}) collective-permute-start(f32[2,192]{1,0:T(2,128)} %squeeze_reshape.3.refs_5_), channel_id=1, source_target_pairs={{0,1},{1,0},{2,3},{3,2},{4,5},{5,4},{6,7},{7,6},{8,9},{9,8},{10,11... | collective-permute-start | bytes 4616 | tf_op jit(solution)/shard_map/ppermute | solution.py:28
  31.6 43.3 %collective-permute-start.7 = (bf16[192,3584]{1,0:T(8,128)(2,1)}, bf16[192,3584]{1,0:T(8,128)(2,1)}, u32[]{:S(2)}, u32[]{:S(2)}) collective-permute-start(bf16[192,3584]{1,0:T(8,128)(2,1)} %bitcast.75), channel_id=1, source_target_pairs={{0,1},{1,0},{2,3},{3,2},{4,5},{5,4},{6,7},{7,6},{8,9},{9,8},{10,11... | collective-permute-start | bytes 4128776 | tf_op jit(solution)/shard_map/ppermute | solution.py:28
  32.1 42.8 %collective-permute-start.8 = (bf16[192,4096]{1,0:T(8,128)(2,1)S(1)}, bf16[192,4096]{1,0:T(8,128)(2,1)}, u32[]{:S(2)}, u32[]{:S(2)}) collective-permute-start(bf16[192,4096]{1,0:T(8,128)(2,1)S(1)} %copy-done.2), channel_id=1, source_target_pairs={{0,1},{1,0},{2,3},{3,2},{4,5},{5,4},{6,7},{7,6},{8,9},{9,8},{10,11... | collective-permute-start | bytes 4718600 | tf_op jit(solution)/shard_map/ppermute | solution.py:28
  37.2 7.2 %collective-permute-start.3 = (bf16[1,16,3584]{2,1,0:T(8,128)(2,1)S(1)}, bf16[1,16,3584]{2,1,0:T(8,128)(2,1)S(1)}, u32[]{:S(2)}, u32[]{:S(2)}) collective-permute-start(bf16[1,16,3584]{2,1,0:T(8,128)(2,1)S(1)} %slice.149), channel_id=1, source_target_pairs={{0,8},{1,9},{2,10},{3,11},{4,12},{5,13},{6,14},{7,15},{8,0},{9,1},... | collective-permute-start | bytes 344072 | tf_op jit(solution)/shard_map/ppermute | solution.py:28
  44.6 7.1 %collective-permute-start.4 = (bf16[16,3584]{1,0:T(8,128)(2,1)S(1)}, bf16[16,3584]{1,0:T(8,128)(2,1)S(1)}, u32[]{:S(2)}, u32[]{:S(2)}) collective-permute-start(bf16[16,3584]{1,0:T(8,128)(2,1)S(1)} %multiply_convert_fusion), channel_id=1, source_target_pairs={{0,8},{1,9},{2,10},{3,11},{4,12},{5,13},{6,14},{7,15},{8,0},{9,1},... | collective-permute-start | bytes 344072 | tf_op jit(solution)/shard_map/ppermute | solution.py:28
  51.7 6.1 %copy-start.4 = (bf16[16,3584]{1,0:T(8,128)(2,1)}, bf16[16,3584]{1,0:T(8,128)(2,1)S(1)}, u32[]{:S(2)}) copy-start(bf16[16,3584]{1,0:T(8,128)(2,1)S(1)} %collective-permute-done.4) | copy-start | bytes 344068
  51.7 6.1 %collective-permute-start.5 = (bf16[32,3584]{1,0:T(8,128)(2,1)S(1)}, bf16[32,3584]{1,0:T(8,128)(2,1)S(1)}, u32[]{:S(2)}, u32[]{:S(2)}) collective-permute-start(bf16[32,3584]{1,0:T(8,128)(2,1)S(1)} %pad_maximum_fusion.2), channel_id=1, source_target_pairs={{0,4},{1,5},{2,6},{3,7},{4,0},{5,1},{6,2},{7,3},{8,12},{9,13},{10,... | collective-permute-start | bytes 688136 | tf_op jit(solution)/shard_map/ppermute | solution.py:28
  57.8 0.9 copy-start.5
  58.7 14.1 %collective-permute-start.6 = (bf16[64,3584]{1,0:T(8,128)(2,1)}, bf16[64,3584]{1,0:T(8,128)(2,1)}, u32[]{:S(2)}, u32[]{:S(2)}) collective-permute-start(bf16[64,3584]{1,0:T(8,128)(2,1)} %pad_maximum_fusion.1), channel_id=1, source_target_pairs={{0,2},{1,3},{2,0},{3,1},{4,6},{5,7},{6,4},{7,5},{8,10},{9,11},{10,... | collective-permute-start | bytes 1376264 | tf_op jit(solution)/shard_map/ppermute | solution.py:28
  59.9 23.9 %collective-permute-start.16 = (f32[2,4096]{1,0:T(2,128)S(1)}, f32[2,4096]{1,0:T(2,128)}, u32[]{:S(2)}, u32[]{:S(2)}) collective-permute-start(f32[2,4096]{1,0:T(2,128)S(1)} %slice_add_fusion.5), channel_id=1, source_target_pairs={{0,1},{1,0},{2,3},{3,2},{4,5},{5,4},{6,7},{7,6},{8,9},{9,8},{10,11... | collective-permute-start | bytes 98312 | tf_op jit(solution)/shard_map/ppermute | solution.py:28
  68.8 68.8 %all-to-all-start = ((bf16[16,384,128]{2,1,0:T(8,128)(2,1)}), bf16[16,384,128]{2,1,0:T(8,128)(2,1)S(1)}, u32[]{:S(2)}, u32[]{:S(2)}) async-start(bf16[16,384,128]{2,1,0:T(8,128)(2,1)} %maximum_bitcast_fusion), calls=%async_computation | async-start | bytes 3145728 | tf_op jit(solution)/shard_map/all_to_all | solution.py:323
  80.6 40.0 %copy-start.3 = (bf16[8,128,512]{2,1,0:T(8,128)(2,1)S(1)}, bf16[8,128,512]{2,1,0:T(8,128)(2,1)}, u32[]{:S(2)}) copy-start(bf16[8,128,512]{2,1,0:T(8,128)(2,1)} %get-tuple-element.12) | copy-start | bytes 3145732
  81.8 38.8 %collective-permute-start.10 = (bf16[4,128,512]{2,1,0:T(8,128)(2,1)S(1)}, bf16[4,128,512]{2,1,0:T(8,128)(2,1)}, u32[]{:S(2)}, u32[]{:S(2)}) collective-permute-start(bf16[4,128,512]{2,1,0:T(8,128)(2,1)S(1)} %slice.89), channel_id=1, source_target_pairs={{0,2},{1,3},{2,0},{3,1},{4,6},{5,7},{6,4},{7,5},{8,10},{9,11},{10,... | collective-permute-start | bytes 1572872 | tf_op jit(solution)/shard_map/ppermute | solution.py:28
  84.6 20.9 %collective-permute-start.17 = (f32[2,4096]{1,0:T(2,128)S(1)}, f32[2,4096]{1,0:T(2,128)S(1)}, u32[]{:S(2)}, u32[]{:S(2)}) collective-permute-start(f32[2,4096]{1,0:T(2,128)S(1)} %fusion.18), channel_id=1, source_target_pairs={{0,2},{1,3},{2,0},{3,1},{4,6},{5,7},{6,4},{7,5},{8,10},{9,11},{10,... | collective-permute-start | bytes 98312 | tf_op jit(solution)/shard_map/ppermute | solution.py:28
  105.5 4.0 %collective-permute-start.18 = (f32[2,4096]{1,0:T(2,128)S(1)}, f32[2,4096]{1,0:T(2,128)S(1)}, u32[]{:S(2)}, u32[]{:S(2)}) collective-permute-start(f32[2,4096]{1,0:T(2,128)S(1)} %add.134), channel_id=1, source_target_pairs={{0,4},{1,5},{2,6},{3,7},{4,0},{5,1},{6,2},{7,3},{8,12},{9,13},{10,... | collective-permute-start | bytes 98312 | tf_op jit(solution)/shard_map/ppermute | solution.py:28
  109.5 8.4 %collective-permute-start.19 = (f32[2,4096]{1,0:T(2,128)S(1)}, f32[2,4096]{1,0:T(2,128)S(1)}, u32[]{:S(2)}, u32[]{:S(2)}) collective-permute-start(f32[2,4096]{1,0:T(2,128)S(1)} %add.135), channel_id=1, source_target_pairs={{0,8},{1,9},{2,10},{3,11},{4,12},{5,13},{6,14},{7,15},{8,0},{9,1},... | collective-permute-start | bytes 98312 | tf_op jit(solution)/shard_map/ppermute | solution.py:28
  111.2 4.3 %collective-permute-start.13 = (f32[8,128]{1,0:T(8,128)}, f32[8,128]{1,0:T(8,128)S(1)}, u32[]{:S(2)}, u32[]{:S(2)}) collective-permute-start(f32[8,128]{1,0:T(8,128)} %get-tuple-element.13), channel_id=1, source_target_pairs={{0,2},{1,3},{2,0},{3,1},{4,6},{5,7},{6,4},{7,5},{8,10},{9,11},{10,... | collective-permute-start | bytes 12296 | tf_op jit(solution)/shard_map/ppermute | solution.py:28
  116.2 3.6 %collective-permute-start.14 = (f32[8,128]{1,0:T(8,128)S(1)}, f32[8,128]{1,0:T(8,128)S(1)}, u32[]{:S(2)}, u32[]{:S(2)}) collective-permute-start(f32[8,128]{1,0:T(8,128)S(1)} %add.126), channel_id=1, source_target_pairs={{0,4},{1,5},{2,6},{3,7},{4,0},{5,1},{6,2},{7,3},{8,12},{9,13},{10,... | collective-permute-start | bytes 12296 | tf_op jit(solution)/shard_map/ppermute | solution.py:28
  119.8 4.5 %collective-permute-start.15 = (f32[8,128]{1,0:T(8,128)S(1)}, f32[8,128]{1,0:T(8,128)S(1)}, u32[]{:S(2)}, u32[]{:S(2)}) collective-permute-start(f32[8,128]{1,0:T(8,128)S(1)} %add.127), channel_id=1, source_target_pairs={{0,8},{1,9},{2,10},{3,11},{4,12},{5,13},{6,14},{7,15},{8,0},{9,1},... | collective-permute-start | bytes 12296 | tf_op jit(solution)/shard_map/ppermute | solution.py:28
  121.9 7.8 %collective-permute-start.11 = (bf16[2,128,512]{2,1,0:T(8,128)(2,1)S(1)}, bf16[2,128,512]{2,1,0:T(8,128)(2,1)S(1)}, u32[]{:S(2)}, u32[]{:S(2)}) collective-permute-start(bf16[2,128,512]{2,1,0:T(8,128)(2,1)S(1)} %slice.146), channel_id=1, source_target_pairs={{0,4},{1,5},{2,6},{3,7},{4,0},{5,1},{6,2},{7,3},{8,12},{9,13},{10,... | collective-permute-start | bytes 786440 | tf_op jit(solution)/shard_map/ppermute | solution.py:28
  129.8 7.1 %collective-permute-start.12 = (bf16[1,128,512]{2,1,0:T(8,128)(2,1)S(1)}, bf16[1,128,512]{2,1,0:T(8,128)(2,1)S(1)}, u32[]{:S(2)}, u32[]{:S(2)}) collective-permute-start(bf16[1,128,512]{2,1,0:T(8,128)(2,1)S(1)} %slice.148), channel_id=1, source_target_pairs={{0,8},{1,9},{2,10},{3,11},{4,12},{5,13},{6,14},{7,15},{8,0},{9,1},... | collective-permute-start | bytes 393224 | tf_op jit(solution)/shard_map/ppermute | solution.py:28
  137.6 12.7 %collective-permute-start.20 = (bf16[128,256]{1,0:T(8,128)(2,1)S(1)}, bf16[128,256]{1,0:T(8,128)(2,1)S(1)}, u32[]{:S(2)}, u32[]{:S(2)}) collective-permute-start(bf16[128,256]{1,0:T(8,128)(2,1)S(1)} %bitcast.85), channel_id=1, source_target_pairs={{0,1},{1,0},{2,3},{3,2},{4,5},{5,4},{6,7},{7,6},{8,9},{9,8},{10,11... | collective-permute-start | bytes 196616 | tf_op jit(solution)/shard_map/ppermute | solution.py:28
  137.7 1.2 copy-start.1
  150.3 0.6 copy-start.6

commit v2 on v1

v2 whole, which is shorter than its diff:
```python
import functools
import math

import jax
import jax.numpy as jnp
from jax import lax
from jax.experimental import pallas as pl
from jax.experimental.pallas import tpu as pltpu
from jax.sharding import PartitionSpec as P

HEAD_DIM = 128
HEADS = 16
TEMB = 256
MIB = 1024 * 1024

epsilon = 1e-06

SMEM_SPEC = pl.BlockSpec(memory_space=pltpu.SMEM)
VMEM_SPEC = pl.BlockSpec(memory_space=pltpu.VMEM)


def params(mib):
    return pltpu.CompilerParams(vmem_limit_bytes=mib * MIB)


def swap(value, mask):
    devices = lax.axis_size("seq")
    return lax.ppermute(value, "seq", [(i, i ^ mask) for i in range(devices)])


def orders(chips):
    bits = [1 << i for i in range(chips.bit_length() - 1)]
    turn = len(bits) // 2
    return (bits, bits[turn:] + bits[:turn])


def position(chip, order):
    last = len(order) - 1
    return sum(((chip >> (bit.bit_length() - 1)) & 1) << (last - i) for i, bit in enumerate(order))


def member(at, order):
    last = len(order) - 1
    return sum(bit for i, bit in enumerate(order) if (at >> (last - i)) & 1)


def normalize(summed, norm_gain):
    scale_rows = lax.rsqrt(jnp.mean(summed * summed, 1, keepdims=True) + epsilon)
    return (summed * scale_rows * norm_gain.astype(jnp.float32)).astype(jnp.bfloat16)


def time_embedding(timesteps, modulation_weight):
    half_width = TEMB // 2
    freqs = jnp.exp(-math.log(10000.0) * jnp.arange(half_width, dtype=jnp.float32) / half_width)
    angles = timesteps.astype(jnp.float32)[:, None] * freqs[None, :]
    embedding = jnp.concatenate([jnp.cos(angles), jnp.sin(angles)], 1)
    embedding = jax.nn.silu(embedding).astype(jnp.bfloat16)
    flat = modulation_weight.reshape(modulation_weight.shape[0], -1)
    product = jnp.dot(embedding, flat, preferred_element_type=jnp.float32)
    return product.reshape(timesteps.shape[0], 2, -1)


def encoder_kernel(lane, order, place_ref, act_ref, weight_ref, own_ref, other_ref, lhs_ref):
    chips = own_ref.shape[0]
    at, core = place_ref[lane], place_ref[2]

    @pl.when(pl.program_id(0) == 0)
    def _():
        lhs_ref[...] = act_ref[...].T

    result = jnp.dot(lhs_ref[...], weight_ref[...], preferred_element_type=jnp.float32)
    half = result.shape[0] // 2
    share = half // chips
    first = core == 0
    own = jnp.where(first, result[:half], result[half:]).astype(own_ref.dtype)
    other = jnp.where(first, result[half:], result[:half]).astype(own_ref.dtype)
    own = own.reshape(chips, share, -1)
    other = other.reshape(chips, share, -1)
    for block in range(chips):
        own_ref[at ^ position(block, order)] = own[block]
        other_ref[at ^ position(block, order)] = other[block]


def encoder(lane, order, place, act, weight):
    chips = 1 << len(order)
    depth, rows = act.shape
    width = weight.shape[1] // 2
    steps = 2
    tile = width // steps
    share = rows // 2 // chips
    out = jax.ShapeDtypeStruct((chips, share, width), jnp.bfloat16)
    out_spec = pl.BlockSpec((chips, share, tile), lambda i: (0, 0, i))
    return pl.pallas_call(
        functools.partial(encoder_kernel, lane, order),
        grid=(steps,),
        out_shape=(out, out),
        in_specs=[
            SMEM_SPEC,
            pl.BlockSpec((depth, rows), lambda i: (0, 0)),
            pl.BlockSpec((depth, tile), lambda i: (0, lane * steps + i)),
        ],
        out_specs=(out_spec, out_spec),
        scratch_shapes=[pltpu.VMEM((rows, depth), jnp.bfloat16)],
        compiler_params=params(24),
        cost_estimate=pl.CostEstimate(
            flops=2 * rows * depth * width,
            bytes_accessed=2 * (depth * rows + depth * width + rows * width),
            transcendentals=0,
        ),
        name="encoder",
    )(place, act, weight)


def slot_rows(chips, width):
    per_slot = 2 * 128 // width
    return chips * per_slot, -(-(chips * per_slot + 2) // 16) * 16


def project_kernel(lanes, place_ref, *refs):
    pieces, refs = (refs[:2], refs[2:4]), refs[4:]
    win0, win1, kv0, kv1, mod0, mod1, keys_ref, values_ref, states, proj0, proj1, sums = refs
    chip = place_ref[3]
    chips = keys_ref.shape[0]
    rows = proj0.shape[0]
    share = rows // chips
    depth = states.shape[1]
    contract = (((1,), (1,)), ((), ()))
    for lane, order in enumerate(lanes):
        top, low = pieces[lane]
        states[: rows // 2, :] = top[...]
        states[rows // 2 :, :] = low[...]
        span = slice(lane * depth, (lane + 1) * depth)
        for win, proj in ((win0, proj0), (win1, proj1)):
            part = lax.dot_general(
                states[...], win[:, span], contract, preferred_element_type=jnp.float32
            )
            for at in range(chips):
                start = pl.multiple_of((chip ^ member(at, order)) * share, share)
                block = part[at * share : (at + 1) * share]
                if lane == 0:
                    proj[pl.ds(start, share), :] = block
                else:
                    proj[pl.ds(start, share), :] += block
    value0, value1 = proj0[...], proj1[...]
    first = jnp.sum(value0, 1, keepdims=True) + jnp.sum(value1, 1, keepdims=True)
    second = jnp.sum(value0 * value0, 1, keepdims=True) + jnp.sum(value1 * value1, 1, keepdims=True)
    lane = lax.broadcasted_iota(jnp.int32, sums.shape, 1)
    sums[...] = jnp.where(lane == 0, first, second).T
    left = []
    for value, mod in ((value0, mod0), (value1, mod1)):
        scale, shift = 1.0 + mod[1:2, :], mod[0:1, :]
        row = lax.broadcasted_iota(jnp.int32, (16, value.shape[1]), 0)
        lines = jnp.where(row < 2, scale, shift)
        high = lines.astype(jnp.bfloat16).astype(jnp.float32)
        lines = jnp.where(row % 2 == 0, high, lines - high)
        lines = jnp.where(row < 4, lines, 0.0)
        left.append(jnp.concatenate([value * scale, lines], 0).astype(jnp.bfloat16))
    width = keys_ref.shape[2]
    slots, extra = slot_rows(chips, width)
    per_slot = slots // chips
    row = lax.broadcasted_iota(jnp.int32, (extra, width), 0)
    column = lax.broadcasted_iota(jnp.int32, (extra, width), 1)
    half = kv0.shape[1] // 2
    for lane, (out_ref, order) in enumerate(zip((keys_ref, values_ref), lanes)):
        line = sums[lane : lane + 1, :]
        high = line.astype(jnp.bfloat16).astype(jnp.float32)
        low = line - high
        if per_slot == 1:
            line = jnp.concatenate([high, low], 1)
        else:
            line = jnp.where(row % 2 == 0, high, low)
        line = jnp.where(row // per_slot == chip, line, 0.0)
        for at in range(chips):
            start = lane * half + (chip ^ member(at, order)) * width
            columns = pl.ds(pl.multiple_of(start, width), width)
            value = jnp.dot(left[0], kv0[:, columns], preferred_element_type=jnp.float32)
            value += jnp.dot(left[1], kv1[:, columns], preferred_element_type=jnp.float32)
            out_ref[at, :rows, :] = value[:rows].astype(out_ref.dtype)
            below = jnp.where(row == slots, value[rows : rows + 1] + value[rows + 1 : rows + 2], line)
            below = jnp.where(
                row == slots + 1, value[rows + 2 : rows + 3] + value[rows + 3 : rows + 4], below
            )
            out_ref[at, rows:, :] = below.astype(out_ref.dtype)


def project(lanes, place, pieces, win0, win1, kv0, kv1, mod0, mod1):
    chips = 1 << len(lanes[0])
    rows = 2 * pieces[0].shape[0]
    features, depth = win0.shape
    total = kv0.shape[1]
    width = total // 2 // chips
    extra = slot_rows(chips, width)[1]
    out = jax.ShapeDtypeStruct((chips, rows + extra, width), jnp.bfloat16)
    return pl.pallas_call(
        functools.partial(project_kernel, lanes),
        out_shape=(out, out),
        in_specs=[SMEM_SPEC] + [VMEM_SPEC] * 10,
        out_specs=(VMEM_SPEC, VMEM_SPEC),
        scratch_shapes=[
            pltpu.VMEM((rows, depth // 2), jnp.bfloat16),
            pltpu.VMEM((rows, features), jnp.float32),
            pltpu.VMEM((rows, features), jnp.float32),
            pltpu.VMEM((rows, 128), jnp.float32),
        ],
        compiler_params=params(20),
        cost_estimate=pl.CostEstimate(
            flops=4 * rows * features * (depth + total),
            bytes_accessed=2 * (rows * depth + 2 * features * (depth + total) + rows * total),
            transcendentals=0,
        ),
        name="project",
    )(place, *pieces, win0, win1, kv0, kv1, mod0, mod1)


def combine_kernel(chips, model_width, place_ref, *refs):
    refs, mine_ref, sent_ref = refs[:4], refs[4], refs[5]
    core = place_ref[2]
    rows = mine_ref.shape[0]
    width = refs[0].shape[1]
    slots = slot_rows(chips, width)[0]
    totals = [
        refs[2 * lane][...].astype(jnp.float32) + refs[2 * lane + 1][...].astype(jnp.float32)
        for lane in range(2)
    ]
    sums = []
    for total in totals:
        line = jnp.sum(total[rows : rows + slots], 0, keepdims=True)
        if width > 128:
            line = line[:, :128] + line[:, 128:]
        sums.append(line)
    mean_val = sums[0] / model_width
    scale = lax.rsqrt(sums[1] / model_width - mean_val * mean_val + epsilon)
    mean_val = jnp.broadcast_to(mean_val, (rows, rows)).T[:, 0:1]
    scale = jnp.broadcast_to(scale, (rows, rows)).T[:, 0:1]
    texts = []
    for total in totals:
        text = (total[:rows] - mean_val * total[rows + slots : rows + slots + 1]) * scale
        texts.append(text + total[rows + slots + 1 : rows + slots + 2])
    for part, text in enumerate(texts):
        span = slice(part * HEAD_DIM, (part + 1) * HEAD_DIM)
        if width > HEAD_DIM:
            low, high = text[:, :HEAD_DIM], text[:, HEAD_DIM:]
            mine_ref[:, span] = jnp.where(core == 0, low, high).astype(mine_ref.dtype)
            sent_ref[:, span] = jnp.where(core == 0, high, low).astype(mine_ref.dtype)
        else:
            mine_ref[:, span] = text.astype(mine_ref.dtype)
            sent_ref[:, span] = text.astype(mine_ref.dtype)


def combine(place, parts, chips, rows, model_width):
    out = jax.ShapeDtypeStruct((rows, 2 * HEAD_DIM), jnp.bfloat16)
    return pl.pallas_call(
        functools.partial(combine_kernel, chips, model_width),
        out_shape=(out, out),
        in_specs=[SMEM_SPEC] + [VMEM_SPEC] * 4,
        out_specs=(VMEM_SPEC, VMEM_SPEC),
        compiler_params=params(8),
        cost_estimate=pl.CostEstimate(
            flops=8 * rows * 512, bytes_accessed=12 * rows * 512, transcendentals=0
        ),
        name="combine",
    )(place, *parts)


def pack_kernel(copies, queries_ref, keys_ref, values_ref, out_ref):
    img_dev = keys_ref.shape[0]
    part_rows = img_dev // copies
    for device in range(out_ref.shape[0]):
        head, copy = device // copies, device % copies
        span = slice(head * HEAD_DIM, (head + 1) * HEAD_DIM)
        out_ref[device, :img_dev, :] = keys_ref[:, span]
        out_ref[device, img_dev : 2 * img_dev, :] = values_ref[:, span]
        out_ref[device, 2 * img_dev :, :] = queries_ref[copy * part_rows : (copy + 1) * part_rows, span]


def pack(copies, queries, keys, values):
    img_dev = keys.shape[0]
    rows = 2 * img_dev + img_dev // copies
    return pl.pallas_call(
        functools.partial(pack_kernel, copies),
        out_shape=jax.ShapeDtypeStruct((HEADS * copies, rows, HEAD_DIM), jnp.bfloat16),
        in_specs=[VMEM_SPEC] * 3,
        out_specs=VMEM_SPEC,
        compiler_params=params(8),
        cost_estimate=pl.CostEstimate(
            flops=0, bytes_accessed=4 * HEADS * copies * rows * HEAD_DIM, transcendentals=0
        ),
        name="pack",
    )(queries, keys, values)


def unpack_kernel(copies, part_rows, blocks_ref, attended_ref, text_ref):
    share = text_ref.shape[0]
    half = text_ref.shape[1] // 2
    for device in range(blocks_ref.shape[0]):
        head, copy = device // copies, device % copies
        start = head * HEAD_DIM
        rows = slice(copy * part_rows, (copy + 1) * part_rows)
        attended_ref[rows, start : start + HEAD_DIM] = blocks_ref[device, :part_rows, :]
        if copy == 0:
            block = blocks_ref[device, part_rows:, :].astype(jnp.float32)
            text_ref[:, start : start + HEAD_DIM] = block[:share].astype(text_ref.dtype)
            start += half
            text_ref[:, start : start + HEAD_DIM] = block[share:].astype(text_ref.dtype)


def unpack(copies, part_rows, blocks):
    share = (blocks.shape[1] - part_rows) // 2
    return pl.pallas_call(
        functools.partial(unpack_kernel, copies, part_rows),
        out_shape=(
            jax.ShapeDtypeStruct((part_rows * copies, HEADS * HEAD_DIM), jnp.bfloat16),
            jax.ShapeDtypeStruct((share, 2 * HEADS * HEAD_DIM), jnp.bfloat16),
        ),
        in_specs=[VMEM_SPEC],
        out_specs=(VMEM_SPEC, VMEM_SPEC),
        compiler_params=params(8),
        name="unpack",
    )(blocks)


def image_kernel(factor, queries_ref, keys_ref, values_ref, sum_ref, norm_ref):
    contract = (((1,), (1,)), ((), ()))
    queries = queries_ref[...].reshape(-1, HEAD_DIM)
    keys = keys_ref[...].reshape(-1, HEAD_DIM)
    values = values_ref[...].reshape(-1, HEAD_DIM)
    scores = lax.dot_general(queries, keys, contract, preferred_element_type=jnp.float32) * factor
    top = jnp.max(scores, 1, keepdims=True)
    weights = jnp.exp2(scores - top)
    total = jnp.sum(weights, 1, keepdims=True)
    sum_ref[...] = jnp.dot(weights.astype(jnp.bfloat16), values, preferred_element_type=jnp.float32)
    lane = lax.broadcasted_iota(jnp.int32, norm_ref.shape, 1)
    norm_ref[...] = jnp.where(lane < 64, top, total)


def image_attention(packed, img_dev, part_rows, factor, call, calls):
    devices = packed.shape[0]
    count = devices * part_rows // calls
    group = max(1, 256 // part_rows)
    block = group * part_rows
    at = 2 * img_dev // part_rows
    steps = devices // group // calls
    out = jax.ShapeDtypeStruct((count, HEAD_DIM), jnp.float32)
    out_spec = pl.BlockSpec((block, HEAD_DIM), lambda i: (i, 0))
    keys = devices * img_dev
    return pl.pallas_call(
        functools.partial(image_kernel, factor),
        grid=(steps,),
        out_shape=(out, out),
        in_specs=[
            pl.BlockSpec((group, part_rows, HEAD_DIM), lambda i: (call * steps + i, at, 0)),
            pl.BlockSpec((devices, img_dev, HEAD_DIM), lambda i: (0, 0, 0)),
            pl.BlockSpec((devices, img_dev, HEAD_DIM), lambda i: (0, 1, 0)),
        ],
        out_specs=(out_spec, out_spec),
        compiler_params=params(20),
        cost_estimate=pl.CostEstimate(
            flops=4 * count * keys * HEAD_DIM,
            bytes_accessed=4 * keys * HEAD_DIM + 10 * count * HEAD_DIM,
            transcendentals=count * keys,
        ),
        name="image_attention",
    )(packed, packed, packed)


def finish_kernel(factor, calls, place_ref, queries_ref, *refs):
    images, (mine_ref, got_ref, out_ref) = refs[: 2 * calls], refs[2 * calls :]
    core, valid = place_ref[2], place_ref[4]
    devices, part_rows = queries_ref.shape[0], queries_ref.shape[1]
    half = mine_ref.shape[0]
    contract = (((1,), (1,)), ((), ()))
    mine, got = mine_ref[...], got_ref[...]
    keys = jnp.concatenate([mine[:, :HEAD_DIM], got[:, :HEAD_DIM]], 0)
    values = jnp.concatenate([mine[:, HEAD_DIM:], got[:, HEAD_DIM:]], 0)
    lane = lax.broadcasted_iota(jnp.int32, (1, 2 * half), 1)
    text_position = jnp.where((lane >= half) == (core == 0), half, 0) + lane % half
    group = max(1, 512 // part_rows)
    rows = group * part_rows
    each = devices // group // calls
    for step in range(devices // group):
        sum_ref, norm_ref = images[2 * (step // each)], images[2 * (step // each) + 1]
        span = slice(step % each * rows, (step % each + 1) * rows)
        queries = queries_ref[step * group : (step + 1) * group].reshape(rows, HEAD_DIM)
        scores = lax.dot_general(queries, keys, contract, preferred_element_type=jnp.float32) * factor
        scores = jnp.where(text_position < valid, scores, -jnp.inf)
        before = norm_ref[span, 0:1]
        top = jnp.maximum(before, jnp.max(scores, 1, keepdims=True))
        rescale = jnp.exp2(before - top)
        weights = jnp.exp2(scores - top)
        total = norm_ref[span, 64:65] * rescale + jnp.sum(weights, 1, keepdims=True)
        mixed = sum_ref[span, :] * rescale + jnp.dot(
            weights.astype(jnp.bfloat16), values, preferred_element_type=jnp.float32
        )
        mixed = (mixed / total).astype(out_ref.dtype)
        out_ref[step * group : (step + 1) * group, :part_rows, :] = mixed.reshape(group, part_rows, HEAD_DIM)
    low = jnp.where(core == 0, mine.astype(jnp.float32), got.astype(jnp.float32))
    high = jnp.where(core == 0, got.astype(jnp.float32), mine.astype(jnp.float32))
    share = 2 * half // devices
    for device in range(devices):
        source = low if device < devices // 2 else high
        start = device * share % half
        block = source[start : start + share]
        block = jnp.concatenate([block[:, :HEAD_DIM], block[:, HEAD_DIM:]], 0)
        out_ref[device, part_rows:, :] = block.astype(out_ref.dtype)


def finish(place, packed, images, mine, got, img_dev, part_rows, factor):
    devices = packed.shape[0]
    share = 2 * mine.shape[0] // devices
    count = devices * part_rows
    at = 2 * img_dev // part_rows
    return pl.pallas_call(
        functools.partial(finish_kernel, factor, len(images) // 2),
        grid=(1,),
        out_shape=jax.ShapeDtypeStruct((devices, part_rows + 2 * share, HEAD_DIM), jnp.bfloat16),
        in_specs=[SMEM_SPEC, pl.BlockSpec((devices, part_rows, HEAD_DIM), lambda i: (0, at, 0))]
        + [VMEM_SPEC] * (len(images) + 2),
        out_specs=pl.BlockSpec((devices, part_rows + 2 * share, HEAD_DIM), lambda i: (0, 0, 0)),
        compiler_params=params(20),
        cost_estimate=pl.CostEstimate(
            flops=4 * count * 2 * mine.shape[0] * HEAD_DIM,
            bytes_accessed=12 * count * HEAD_DIM,
            transcendentals=count * 2 * mine.shape[0],
        ),
        name="finish",
    )(place, packed, *images, mine, got)


def halves(blocks):
    half = blocks.shape[0] // 2
    return blocks[:half], blocks[half:].astype(jnp.bfloat16)


def local(
    enc_act,
    down_weight,
    norm_gain,
    text_in_weight,
    modulation_weight,
    key_value_weight,
    timesteps,
    lengths,
    image_queries,
    image_key_values,
):
    devices = lax.axis_size("seq")
    chips = devices // 2
    copies = devices // HEADS
    text_len = enc_act.shape[1]
    img_dev = image_queries.shape[1]
    part_rows = img_dev // copies
    factor = math.log2(math.e) / math.sqrt(HEAD_DIM)
    lanes = orders(chips)
    index = lax.axis_index("seq")
    chip, core = index // 2, index % 2
    place = jnp.stack([position(chip, lanes[0]), position(chip, lanes[1]), core, chip, lengths[0]])
    place = place.astype(jnp.int32)

    win0, kv0 = text_in_weight.T, key_value_weight
    win1, kv1 = swap(win0, 1), swap(kv0, 1)
    mod0 = time_embedding(timesteps, modulation_weight)[0]
    mod1 = swap(mod0, 1)

    act = enc_act[0].T
    blocks = []
    for lane, order in enumerate(lanes):
        own, other = encoder(lane, order, place, act, down_weight)
        blocks.append(own.astype(jnp.float32) + swap(other, 1).astype(jnp.float32))
    for step in range(len(lanes[0])):
        keep, sent = zip(*[halves(block) for block in blocks])
        if step == 0:
            sent, image_queries, image_key_values = lax.optimization_barrier(
                (sent, image_queries, image_key_values)
            )
            packed = pack(
                copies, image_queries[0], image_key_values[0, :, 0], image_key_values[0, :, 1]
            )
        got = [swap(part, 2 * order[step]) for part, order in zip(sent, lanes)]
        if step == 0:
            got, packed = lax.optimization_barrier((got, packed))
            packed = lax.all_to_all(packed, "seq", split_axis=0, concat_axis=0, tiled=True)
        blocks = [mine + part.astype(jnp.float32) for mine, part in zip(keep, got)]

    summed = jnp.concatenate([block[0] for block in blocks], 1)
    states = normalize(summed, norm_gain)
    pieces = jnp.split(states, 2, axis=1)
    for step in reversed(range(len(lanes[0]))):
        got = [swap(piece, 2 * order[step]) for piece, order in zip(pieces, lanes)]
        if step > 0:
            pieces = [jnp.concatenate(pair, 0) for pair in zip(pieces, got)]
    pieces = [piece for pair in zip(pieces, got) for piece in pair]

    blocks = project(lanes, place, pieces, win0, win1, kv0, kv1, mod0, mod1)
    calls = 2
    images = []
    for step in range(len(lanes[0])):
        keep, sent = zip(*[halves(block) for block in blocks])
        if step < calls:
            sent, packed = lax.optimization_barrier((sent, packed))
            image = image_attention(packed, img_dev, part_rows, factor, step, calls)
        got = [swap(part, 2 * order[step]) for part, order in zip(sent, lanes)]
        if step < calls:
            got, image = lax.optimization_barrier((got, image))
            images += image
        if step < len(lanes[0]) - 1:
            blocks = [
                mine.astype(jnp.float32) + part.astype(jnp.float32) for mine, part in zip(keep, got)
            ]
    parts = [part[0] for pair in zip(keep, got) for part in pair]
    model_width = text_in_weight.shape[1] * devices
    mine, sent = combine(place, parts, chips, text_len // 2, model_width)
    got = swap(sent, 1)

    back = finish(place, packed, images, mine, got, img_dev, part_rows, factor)
    back = lax.all_to_all(back, "seq", split_axis=0, concat_axis=0, tiled=True)
    attended, text_kv = unpack(copies, part_rows, back)
    return (attended[None], text_kv)


def solution(mesh):
    in_specs = (
        P("dp", None, "seq"),
        P("seq", None),
        P(),
        P(None, "seq"),
        P(None, None, "seq"),
        P("seq", None),
        P("dp"),
        P("dp"),
        P("dp", "seq", None),
        P("dp", "seq", None, None),
    )
    out_specs = (P("dp", "seq", None), P(("dp", "seq"), None))
    return jax.shard_map(local, mesh=mesh, in_specs=in_specs, out_specs=out_specs, check_vma=False)
```

time: 182 us -> 153 us (0.84)
  waiting for transfers between devices: 71.3 us -> 59.2 us
  other arithmetic: 12 us -> 3.61 us
  Pallas kernels: 31 us -> 25.6 us
  local copies, waits for them, and re-layouts: 13.4 us -> 8.89 us
  starting transfers between devices: 28.3 us -> 30.8 us
    ppermute x21 -> x24, waiting for transfers between devices: 71.3 us -> 59.2 us  [swap(): return lax.ppermute(value, 'seq', [(i, i ^ mask) for i in range(devices)])]
    pallas_call x4 -> x9, Pallas kernels: 31 us -> 25.6 us  [the longest x2 8.94 us: image_attention(): pl.pallas_call(functools.partial(image_kernel, factor), grid=(steps,), ou...]
    reshape x3 -> x0, local copies, waits for them, and re-layouts: 5.17 us -> none  [the longest x2 4.16 us: local(): image_key_values.reshape(img_dev, 2, HEADS, HEAD_DIM).transpose(2, 1, 0, 3)]
    concatenate x3 -> x4, other arithmetic: 2.99 us -> 0.05 us  [local(): pieces = [jnp.concatenate(pair, 0) for pair in zip(pieces, got)]]
    ppermute x21 -> x24, starting transfers between devices: 24.4 us -> 27 us  [swap(): return lax.ppermute(value, 'seq', [(i, i ^ mask) for i in range(devices)])]
    reshape x1 -> x0, other arithmetic: 2.34 us -> none  [local(): jnp.concatenate([pairs, queries], 2)]
    add x15 -> x10, other arithmetic: 5.42 us -> 3.22 us  [the longest x4 2.85 us: local(): blocks = [mine + part.astype(jnp.float32) for mine, part in zip(keep, got)]]
    unnamed x22 -> x24, local copies, waits for them, and re-layouts: 5.53 us -> 7.18 us
  transfers between devices with their start and end apart: 22 -> 25, of which waited for: 13 -> 18; matrix products, arithmetic and copies ran while one was open for 11% -> 3% of each run, Pallas kernels for 9% -> 11%
where the time goes in v2:
time: 153 us; the launch traced here: 152 us
  waiting for transfers between devices  59.2 us (39%)
  starting transfers between devices  30.8 us (20%)
  Pallas kernels  25.6 us (17%)
  blocking collectives  21.8 us (14%)
  local copies, waits for them, and re-layouts  8.89 us (6%)
  other arithmetic  3.61 us (2%)
  between operations  2.46 us (2%)
    ppermute x24, waiting for transfers between devices, swap(): return lax.ppermute(value, 'seq', [(i, i ^ mask) for i in range(devices)])  59.2 us
    ppermute x24, starting transfers between devices, swap(): return lax.ppermute(value, 'seq', [(i, i ^ mask) for i in range(devices)])  27 us
    all_to_all x1, blocking collectives, local(): back = lax.all_to_all(back, 'seq', split_axis=0, concat_axis=0, tiled=True)  21.8 us
    pallas_call x2, Pallas kernels, image_attention(): pl.pallas_call(functools.partial(image_kernel, factor), grid=(steps,), ou...  8.94 us
    unnamed x24, local copies, waits for them, and re-layouts  7.18 us
    pallas_call x2, Pallas kernels, encoder(): pl.pallas_call(functools.partial(encoder_kernel, lane, order), grid=(step...  5.55 us
    pallas_call x1, Pallas kernels, project(): pl.pallas_call(functools.partial(project_kernel, lanes), out_shape=(out,...  4.04 us
    all_to_all x1, starting transfers between devices, local(): lax.all_to_all(packed, 'seq', split_axis=0, concat_axis=0, tiled=True)  3.89 us
  transfers between devices with their start and end apart: 25, of which 18 were waited for; matrix products, arithmetic and copies ran while one was open for 3% of the time, Pallas kernels for 11%

profile of v2, /device:TPU:0, one launch (start us, length us, event | category | flops | bytes accessed | tf_op | source)
XLA Modules:
  0.0 152.5 jit_solution(9029502724769107843)
XLA Ops:
  1.4 0.1 stack.19.place_ref
  1.4 3.4 %copy-done.1 = bf16[1184,3584]{1,0:T(8,128)(2,1)S(1)} copy-done((bf16[1184,3584]{1,0:T(8,128)(2,1)S(1)}, bf16[1184,3584]{1,0:T(8,128)(2,1)}, u32[]{:S(2)}) %copy-start.1) | copy-done | bytes 8486936
  4.8 1.1 copy-done.2
  5.9 2.8 %encoder.3 = (bf16[8,16,1792]{2,1,0:T(8,128)(2,1)S(1)}, bf16[8,16,1792]{2,1,0:T(8,128)(2,1)S(1)}) custom-call(s32[5]{0:T(128)S(1)} %stack.19.place_ref, bf16[1184,256]{1,0:T(8,128)(2,1)S(1)} %bitcast.36, bf16[1184,3584]{1,0:T(8,128)(2,1)S(1)} %copy-done.1), custom_call_target="tpu_custom_call" | custom-call | flops 1086324736 | bytes 5767168 | tf_op jit(solution)/shard_map/encoder/pallas_call | solution.py:93
  8.7 0.5 collective-permute-start.1
  9.2 2.8 %encoder.2 = (bf16[8,16,1792]{2,1,0:T(8,128)(2,1)S(1)}, bf16[8,16,1792]{2,1,0:T(8,128)(2,1)S(1)}) custom-call(s32[5]{0:T(128)S(1)} %stack.19.place_ref, bf16[1184,256]{1,0:T(8,128)(2,1)S(1)} %bitcast.37, bf16[1184,3584]{1,0:T(8,128)(2,1)S(1)} %copy-done.1), custom_call_target="tpu_custom_call" | custom-call | flops 1086324736 | bytes 5767168 | tf_op jit(solution)/shard_map/encoder/pallas_call | solution.py:93
  12.0 0.1 collective-permute-start
  12.1 0.5 collective-permute-start.14
  12.6 0.1 collective-permute-start.15
  13.4 0.1 convert_add_fusion
  13.6 0.3 collective-permute-done
  13.9 0.1 convert_add_fusion.1
  14.0 2.7 %collective-permute-start.2 = (bf16[4,16,1792]{2,1,0:T(8,128)(2,1)S(1)}, bf16[4,16,1792]{2,1,0:T(8,128)(2,1)S(1)}, u32[]{:S(2)}, u32[]{:S(2)}) collective-permute-start(bf16[4,16,1792]{2,1,0:T(8,128)(2,1)S(1)} %slice.165), channel_id=1, source_target_pairs={{0,2},{1,3},{2,0},{3,1},{4,6},{5,7},{6,4},{7,5},{8,10},{9,11},{10,... | collective-permute-start | bytes 688136 | tf_op jit(solution)/shard_map/ppermute | solution.py:28
  16.7 1.6 %collective-permute-start.3 = (bf16[4,16,1792]{2,1,0:T(8,128)(2,1)S(1)}, bf16[4,16,1792]{2,1,0:T(8,128)(2,1)S(1)}, u32[]{:S(2)}, u32[]{:S(2)}) collective-permute-start(bf16[4,16,1792]{2,1,0:T(8,128)(2,1)S(1)} %slice.164), channel_id=1, source_target_pairs={{0,4},{1,5},{2,6},{3,7},{4,0},{5,1},{6,2},{7,3},{8,12},{9,13},{10,... | collective-permute-start | bytes 688136 | tf_op jit(solution)/shard_map/ppermute | solution.py:28
  18.3 0.3 copy.12
  18.7 0.1 slice_bitcast_fusion
  18.8 0.9 copy-done.8
  19.7 1.4 pack.1
  21.2 1.7 %collective-permute-done.2 = bf16[4,16,1792]{2,1,0:T(8,128)(2,1)S(1)} collective-permute-done((bf16[4,16,1792]{2,1,0:T(8,128)(2,1)S(1)}, bf16[4,16,1792]{2,1,0:T(8,128)(2,1)S(1)}, u32[]{:S(2)}, u32[]{:S(2)}) %collective-permute-start.2) | collective-permute-done | bytes 229408 | tf_op jit(solution)/shard_map/ppermute | solution.py:28
  22.9 1.5 collective-permute-done.3
  24.4 0.8 copy-done.9
  25.2 2.7 %collective-permute-start.6 = (bf16[2,16,1792]{2,1,0:T(8,128)(2,1)S(1)}, bf16[2,16,1792]{2,1,0:T(8,128)(2,1)}, u32[]{:S(2)}, u32[]{:S(2)}) collective-permute-start(bf16[2,16,1792]{2,1,0:T(8,128)(2,1)S(1)} %slice.168), channel_id=1, source_target_pairs={{0,8},{1,9},{2,10},{3,11},{4,12},{5,13},{6,14},{7,15},{8,0},{9,1},... | collective-permute-start | bytes 344072 | tf_op jit(solution)/shard_map/ppermute | solution.py:28
  27.8 0.8 slice_add_fusion.1
  28.6 3.9 %all-to-all-start = ((bf16[16,384,128]{2,1,0:T(8,128)(2,1)}), bf16[16,384,128]{2,1,0:T(8,128)(2,1)S(1)}, u32[]{:S(2)}, u32[]{:S(2)}) async-start(bf16[16,384,128]{2,1,0:T(8,128)(2,1)} %pack.1), calls=%async_computation | async-start | bytes 3145728 | tf_op jit(solution)/shard_map/all_to_all | solution.py:481
  32.5 1.0 slice.169
  33.5 1.7 %collective-permute-start.4 = (bf16[2,16,1792]{2,1,0:T(8,128)(2,1)S(1)}, bf16[2,16,1792]{2,1,0:T(8,128)(2,1)S(1)}, u32[]{:S(2)}, u32[]{:S(2)}) collective-permute-start(bf16[2,16,1792]{2,1,0:T(8,128)(2,1)S(1)} %slice.169), channel_id=1, source_target_pairs={{0,4},{1,5},{2,6},{3,7},{4,0},{5,1},{6,2},{7,3},{8,12},{9,13},{10,... | collective-permute-start | bytes 344072 | tf_op jit(solution)/shard_map/ppermute | solution.py:28
  35.2 1.0 slice_add_fusion.4
  36.2 1.5 %collective-permute-start.7 = (bf16[1,16,1792]{2,1,0:T(8,128)(2,1)S(1)}, bf16[1,16,1792]{2,1,0:T(8,128)(2,1)S(1)}, u32[]{:S(2)}, u32[]{:S(2)}) collective-permute-start(bf16[1,16,1792]{2,1,0:T(8,128)(2,1)S(1)} %slice.172), channel_id=1, source_target_pairs={{0,2},{1,3},{2,0},{3,1},{4,6},{5,7},{6,4},{7,5},{8,10},{9,11},{10,... | collective-permute-start | bytes 172040 | tf_op jit(solution)/shard_map/ppermute | solution.py:28
  37.8 23.4 %collective-permute-done.4 = bf16[2,16,1792]{2,1,0:T(8,128)(2,1)S(1)} collective-permute-done((bf16[2,16,1792]{2,1,0:T(8,128)(2,1)S(1)}, bf16[2,16,1792]{2,1,0:T(8,128)(2,1)S(1)}, u32[]{:S(2)}, u32[]{:S(2)}) %collective-permute-start.4) | collective-permute-done | bytes 114720 | tf_op jit(solution)/shard_map/ppermute | solution.py:28
  61.1 1.0 slice_add_fusion.5
  62.1 4.6 %collective-permute-start.5 = (bf16[1,16,1792]{2,1,0:T(8,128)(2,1)S(1)}, bf16[1,16,1792]{2,1,0:T(8,128)(2,1)S(1)}, u32[]{:S(2)}, u32[]{:S(2)}) collective-permute-start(bf16[1,16,1792]{2,1,0:T(8,128)(2,1)S(1)} %slice.173), channel_id=1, source_target_pairs={{0,8},{1,9},{2,10},{3,11},{4,12},{5,13},{6,14},{7,15},{8,0},{9,1},... | collective-permute-start | bytes 172040 | tf_op jit(solution)/shard_map/ppermute | solution.py:28
  66.7 5.8 %collective-permute-done.5 = bf16[1,16,1792]{2,1,0:T(8,128)(2,1)S(1)} collective-permute-done((bf16[1,16,1792]{2,1,0:T(8,128)(2,1)S(1)}, bf16[1,16,1792]{2,1,0:T(8,128)(2,1)S(1)}, u32[]{:S(2)}, u32[]{:S(2)}) %collective-permute-start.5) | collective-permute-done | bytes 57376 | tf_op jit(solution)/shard_map/ppermute | solution.py:28
  72.6 0.1 multiply_reduce_fusion
  72.7 0.1 multiply_convert_fusion
  72.8 0.1 collective-permute-start.8
  73.0 1.6 %collective-permute-start.11 = (bf16[16,1792]{1,0:T(8,128)(2,1)S(1)}, bf16[16,1792]{1,0:T(8,128)(2,1)S(1)}, u32[]{:S(2)}, u32[]{:S(2)}) collective-permute-start(bf16[16,1792]{1,0:T(8,128)(2,1)S(1)} %get-tuple-element.74), channel_id=1, source_target_pairs={{0,2},{1,3},{2,0},{3,1},{4,6},{5,7},{6,4},{7,5},{8,10},{9,11},{10,... | collective-permute-start | bytes 172040 | tf_op jit(solution)/shard_map/ppermute | solution.py:28
  74.6 3.4 %collective-permute-done.8 = bf16[16,1792]{1,0:T(8,128)(2,1)S(1)} collective-permute-done((bf16[16,1792]{1,0:T(8,128)(2,1)S(1)}, bf16[16,1792]{1,0:T(8,128)(2,1)S(1)}, u32[]{:S(2)}, u32[]{:S(2)}) %collective-permute-start.8) | collective-permute-done | bytes 57376 | tf_op jit(solution)/shard_map/ppermute | solution.py:28
  78.1 2.3 %collective-permute-start.12 = (bf16[32,1792]{1,0:T(8,128)(2,1)S(1)}, bf16[32,1792]{1,0:T(8,128)(2,1)S(1)}, u32[]{:S(2)}, u32[]{:S(2)}) collective-permute-start(bf16[32,1792]{1,0:T(8,128)(2,1)S(1)} %pad_maximum_fusion.4), channel_id=1, source_target_pairs={{0,8},{1,9},{2,10},{3,11},{4,12},{5,13},{6,14},{7,15},{8,0},{9,1},... | collective-permute-start | bytes 344072 | tf_op jit(solution)/shard_map/ppermute | solution.py:28
  80.4 3.5 %collective-permute-done.9 = bf16[32,1792]{1,0:T(8,128)(2,1)S(1)} collective-permute-done((bf16[32,1792]{1,0:T(8,128)(2,1)S(1)}, bf16[32,1792]{1,0:T(8,128)(2,1)S(1)}, u32[]{:S(2)}, u32[]{:S(2)}) %collective-permute-start.9) | collective-permute-done | bytes 114720 | tf_op jit(solution)/shard_map/ppermute | solution.py:28
  83.9 1.4 collective-permute-start.10
  85.3 0.6 collective-permute-done.12
  86.0 0.1 fusion
  86.2 1.2 collective-permute-done.16.refs_9_
  87.4 2.6 %collective-permute-done.10.refs_1_ = bf16[64,1792]{1,0:T(8,128)(2,1)S(1)} collective-permute-done((bf16[64,1792]{1,0:T(8,128)(2,1)S(1)}, bf16[64,1792]{1,0:T(8,128)(2,1)S(1)}, u32[]{:S(2)}, u32[]{:S(2)}) %collective-permute-start.10) | collective-permute-done | bytes 229408 | tf_op jit(solution)/shard_map/ppermute | solution.py:28
  90.0 2.0 %collective-permute-done.13.refs_3_ = bf16[64,1792]{1,0:T(8,128)(2,1)S(1)} collective-permute-done((bf16[64,1792]{1,0:T(8,128)(2,1)S(1)}, bf16[64,1792]{1,0:T(8,128)(2,1)S(1)}, u32[]{:S(2)}, u32[]{:S(2)}) %collective-permute-start.13) | collective-permute-done | bytes 229408 | tf_op jit(solution)/shard_map/ppermute | solution.py:28
  92.1 4.0 %project.1 = (bf16[8,144,256]{2,1,0:T(8,128)(2,1)S(1)}, bf16[8,144,256]{2,1,0:T(8,128)(2,1)S(1)}) custom-call(s32[5]{0:T(128)S(1)} %stack.19.place_ref, bf16[64,1792]{1,0:T(8,128)(2,1)S(1)} %pad_maximum_fusion.1.refs_0_, bf16[64,1792]{1,0:T(8,128)(2,1)S(1)} %collective-permute-done.10.refs_1_, bf16[64,1792]{1,0:T(8,128)(2,1)S(1)} %pad_maximum_fusion.2.refs_2_, ...), custom_call_target="tpu_custom_call" | custom-call | flops 754974720 | bytes 7864320 | tf_op jit(solution)/shard_map/project/pallas_call | solution.py:194
  96.1 0.8 copy-done.4
  96.9 0.2 copy-done.6
  97.2 1.6 %collective-permute-start.17 = (bf16[4,144,256]{2,1,0:T(8,128)(2,1)S(1)}, bf16[4,144,256]{2,1,0:T(8,128)(2,1)S(1)}, u32[]{:S(2)}, u32[]{:S(2)}) collective-permute-start(bf16[4,144,256]{2,1,0:T(8,128)(2,1)S(1)} %slice.103), channel_id=1, source_target_pairs={{0,2},{1,3},{2,0},{3,1},{4,6},{5,7},{6,4},{7,5},{8,10},{9,11},{10,... | collective-permute-start | bytes 884744 | tf_op jit(solution)/shard_map/ppermute | solution.py:28
  98.8 4.5 %image_attention.2 = (f32[1024,128]{1,0:T(8,128)S(1)}, f32[1024,128]{1,0:T(8,128)S(1)}) custom-call(bf16[16,384,128]{2,1,0:T(8,128)(2,1)S(1)} %all-to-all-done.queries_ref.keys_ref.values_ref, bf16[16,384,128]{2,1,0:T(8,128)(2,1)S(1)} %all-to-all-done.queries_ref.keys_ref.values_ref, bf16[16,384,128]{2,1,0:T(8,128)(2,1)S(1)} %all-to-all-done.queries_ref.keys_ref.values_ref), custom_call_target="tpu_custom_call" | custom-call | flops 1073741824 | bytes 2359296 | tf_op jit(solution)/shard_map/image_attention/pallas_call | solution.py:346
  103.2 0.7 collective-permute-done.17
  104.0 4.7 %collective-permute-done.18 = bf16[4,144,256]{2,1,0:T(8,128)(2,1)S(1)} collective-permute-done((bf16[4,144,256]{2,1,0:T(8,128)(2,1)S(1)}, bf16[4,144,256]{2,1,0:T(8,128)(2,1)S(1)}, u32[]{:S(2)}, u32[]{:S(2)}) %collective-permute-start.18) | collective-permute-done | bytes 294944 | tf_op jit(solution)/shard_map/ppermute | solution.py:28
  108.8 0.1 collective-permute-start.19
  108.9 2.2 %collective-permute-start.20 = (bf16[2,144,256]{2,1,0:T(8,128)(2,1)S(1)}, bf16[2,144,256]{2,1,0:T(8,128)(2,1)S(1)}, u32[]{:S(2)}, u32[]{:S(2)}) collective-permute-start(bf16[2,144,256]{2,1,0:T(8,128)(2,1)S(1)} %slice.166), channel_id=1, source_target_pairs={{0,8},{1,9},{2,10},{3,11},{4,12},{5,13},{6,14},{7,15},{8,0},{9,1},... | collective-permute-start | bytes 442376 | tf_op jit(solution)/shard_map/ppermute | solution.py:28
  111.1 4.5 %image_attention.3 = (f32[1024,128]{1,0:T(8,128)S(1)}, f32[1024,128]{1,0:T(8,128)S(1)}) custom-call(bf16[16,384,128]{2,1,0:T(8,128)(2,1)S(1)} %all-to-all-done.queries_ref.keys_ref.values_ref, bf16[16,384,128]{2,1,0:T(8,128)(2,1)S(1)} %all-to-all-done.queries_ref.keys_ref.values_ref, bf16[16,384,128]{2,1,0:T(8,128)(2,1)S(1)} %all-to-all-done.queries_ref.keys_ref.values_ref), custom_call_target="tpu_custom_call" | custom-call | flops 1073741824 | bytes 2359296 | tf_op jit(solution)/shard_map/image_attention/pallas_call | solution.py:346
  115.6 1.2 collective-permute-done.20
  117.0 1.5 collective-permute-start.22
  118.5 2.9 %collective-permute-done.22 = bf16[1,144,256]{2,1,0:T(8,128)(2,1)S(1)} collective-permute-done((bf16[1,144,256]{2,1,0:T(8,128)(2,1)S(1)}, bf16[1,144,256]{2,1,0:T(8,128)(2,1)S(1)}, u32[]{:S(2)}, u32[]{:S(2)}) %collective-permute-start.22) | collective-permute-done | bytes 73760 | tf_op jit(solution)/shard_map/ppermute | solution.py:28
  121.4 2.4 %collective-permute-done.21 = bf16[1,144,256]{2,1,0:T(8,128)(2,1)S(1)} collective-permute-done((bf16[1,144,256]{2,1,0:T(8,128)(2,1)S(1)}, bf16[1,144,256]{2,1,0:T(8,128)(2,1)S(1)}, u32[]{:S(2)}, u32[]{:S(2)}) %collective-permute-start.21) | collective-permute-done | bytes 73760 | tf_op jit(solution)/shard_map/ppermute | solution.py:28
  123.8 0.7 combine.1
  124.6 1.2 collective-permute-done.23.refs_5_
  125.8 3.9 %finish.1 = bf16[16,160,128]{2,1,0:T(8,128)(2,1)S(1)} custom-call(s32[5]{0:T(128)S(1)} %stack.19.place_ref, bf16[16,384,128]{2,1,0:T(8,128)(2,1)S(1)} %all-to-all-done.queries_ref.keys_ref.values_ref, f32[1024,128]{1,0:T(8,128)S(1)} %get-tuple-element.58.refs_0_, f32[1024,128]{1,0:T(8,128)S(1)} %get-tuple-element.59.refs_1_, ...), custom_call_target="tpu_custom_call" | custom-call | flops 268435456 | bytes 3145728 | tf_op jit(solution)/shard_map/finish/pallas_call | solution.py:412
  129.7 21.8 %all_to_all.10.blocks_ref = bf16[16,160,128]{2,1,0:T(8,128)(2,1)S(1)} all-to-all(bf16[16,160,128]{2,1,0:T(8,128)(2,1)S(1)} %finish.1), channel_id=1, replica_groups=mesh['dp'=2,'seq'=16] {'seq'}, dimensions={0} | all-to-all | bytes 1310720 | tf_op jit(solution)/shard_map/all_to_all | solution.py:515
  151.5 1.0 unpack.1
  (63 shorter events, 0.9 us)
Async XLA Ops:
  0.6 85.4 %copy-start = (bf16[256,2,192]{0,2,1:T(8,128)(2,1)S(1)}, bf16[256,2,192]{0,2,1:T(8,128)(2,1)}, u32[]{:S(2)}) copy-start(bf16[256,2,192]{0,2,1:T(8,128)(2,1)} %param.14) | copy-start | bytes 589828
  1.4 3.4 %copy-start.1 = (bf16[1184,3584]{1,0:T(8,128)(2,1)S(1)}, bf16[1184,3584]{1,0:T(8,128)(2,1)}, u32[]{:S(2)}) copy-start(bf16[1184,3584]{1,0:T(8,128)(2,1)} %weight_ref.3) | copy-start | bytes 25460740
  4.8 1.1 copy-start.2
  8.7 3.9 %copy-start.3 = (bf16[192,4096]{1,0:T(8,128)(2,1)S(1)}, bf16[192,4096]{1,0:T(8,128)(2,1)}, u32[]{:S(2)}) copy-start(bf16[192,4096]{1,0:T(8,128)(2,1)} %refs_6_.1) | copy-start | bytes 4718596
  8.7 4.6 %copy-start.11 = (bf16[3584]{0:T(1024)(128)(2,1)S(1)}, bf16[3584]{0:T(1024)(128)(2,1)}, u32[]{:S(2)}) copy-start(bf16[3584]{0:T(1024)(128)(2,1)} %param.12) | copy-start | bytes 21508
  8.7 4.7 %collective-permute-start.1 = (bf16[8,16,1792]{2,1,0:T(8,128)(2,1)S(1)}, bf16[8,16,1792]{2,1,0:T(8,128)(2,1)S(1)}, u32[]{:S(2)}, u32[]{:S(2)}) collective-permute-start(bf16[8,16,1792]{2,1,0:T(8,128)(2,1)S(1)} %get-tuple-element.40), channel_id=1, source_target_pairs={{0,1},{1,0},{2,3},{3,2},{4,5},{5,4},{6,7},{7,6},{8,9},{9,8},{10,11... | collective-permute-start | bytes 1376264 | tf_op jit(solution)/shard_map/ppermute | solution.py:28
  12.0 1.9 %collective-permute-start = (bf16[8,16,1792]{2,1,0:T(8,128)(2,1)S(1)}, bf16[8,16,1792]{2,1,0:T(8,128)(2,1)S(1)}, u32[]{:S(2)}, u32[]{:S(2)}) collective-permute-start(bf16[8,16,1792]{2,1,0:T(8,128)(2,1)S(1)} %get-tuple-element.38), channel_id=1, source_target_pairs={{0,1},{1,0},{2,3},{3,2},{4,5},{5,4},{6,7},{7,6},{8,9},{9,8},{10,11... | collective-permute-start | bytes 1376264 | tf_op jit(solution)/shard_map/ppermute | solution.py:28
  12.1 79.9 %collective-permute-start.14 = (bf16[192,3584]{1,0:T(8,128)(2,1)}, bf16[192,3584]{1,0:T(8,128)(2,1)}, u32[]{:S(2)}, u32[]{:S(2)}) collective-permute-start(bf16[192,3584]{1,0:T(8,128)(2,1)} %bitcast.12.refs_4_), channel_id=1, source_target_pairs={{0,1},{1,0},{2,3},{3,2},{4,5},{5,4},{6,7},{7,6},{8,9},{9,8},{10,11... | collective-permute-start | bytes 4128776 | tf_op jit(solution)/shard_map/ppermute | solution.py:28
  12.6 79.5 %collective-permute-start.15 = (bf16[192,4096]{1,0:T(8,128)(2,1)S(1)}, bf16[192,4096]{1,0:T(8,128)(2,1)}, u32[]{:S(2)}, u32[]{:S(2)}) collective-permute-start(bf16[192,4096]{1,0:T(8,128)(2,1)S(1)} %copy-done.3), channel_id=1, source_target_pairs={{0,1},{1,0},{2,3},{3,2},{4,5},{5,4},{6,7},{7,6},{8,9},{9,8},{10,11... | collective-permute-start | bytes 4718600 | tf_op jit(solution)/shard_map/ppermute | solution.py:28
  13.5 4.8 %copy-start.10 = (bf16[1,128,2,2048]{3,2,1,0:T(2,128)(2,1)S(1)}, bf16[1,128,2,2048]{3,2,1,0:T(2,128)(2,1)}, u32[]{:S(2)}) copy-start(bf16[1,128,2,2048]{3,2,1,0:T(2,128)(2,1)} %param.19) | copy-start | bytes 3145732
  14.0 8.8 %collective-permute-start.2 = (bf16[4,16,1792]{2,1,0:T(8,128)(2,1)S(1)}, bf16[4,16,1792]{2,1,0:T(8,128)(2,1)S(1)}, u32[]{:S(2)}, u32[]{:S(2)}) collective-permute-start(bf16[4,16,1792]{2,1,0:T(8,128)(2,1)S(1)} %slice.165), channel_id=1, source_target_pairs={{0,2},{1,3},{2,0},{3,1},{4,6},{5,7},{6,4},{7,5},{8,10},{9,11},{10,... | collective-permute-start | bytes 688136 | tf_op jit(solution)/shard_map/ppermute | solution.py:28
  16.7 7.6 %collective-permute-start.3 = (bf16[4,16,1792]{2,1,0:T(8,128)(2,1)S(1)}, bf16[4,16,1792]{2,1,0:T(8,128)(2,1)S(1)}, u32[]{:S(2)}, u32[]{:S(2)}) collective-permute-start(bf16[4,16,1792]{2,1,0:T(8,128)(2,1)S(1)} %slice.164), channel_id=1, source_target_pairs={{0,4},{1,5},{2,6},{3,7},{4,0},{5,1},{6,2},{7,3},{8,12},{9,13},{10,... | collective-permute-start | bytes 688136 | tf_op jit(solution)/shard_map/ppermute | solution.py:28
  18.7 1.0 copy-start.8
  24.4 0.8 copy-start.9
  25.2 10.0 %collective-permute-start.6 = (bf16[2,16,1792]{2,1,0:T(8,128)(2,1)S(1)}, bf16[2,16,1792]{2,1,0:T(8,128)(2,1)}, u32[]{:S(2)}, u32[]{:S(2)}) collective-permute-start(bf16[2,16,1792]{2,1,0:T(8,128)(2,1)S(1)} %slice.168), channel_id=1, source_target_pairs={{0,8},{1,9},{2,10},{3,11},{4,12},{5,13},{6,14},{7,15},{8,0},{9,1},... | collective-permute-start | bytes 344072 | tf_op jit(solution)/shard_map/ppermute | solution.py:28
  28.6 68.5 %all-to-all-start = ((bf16[16,384,128]{2,1,0:T(8,128)(2,1)}), bf16[16,384,128]{2,1,0:T(8,128)(2,1)S(1)}, u32[]{:S(2)}, u32[]{:S(2)}) async-start(bf16[16,384,128]{2,1,0:T(8,128)(2,1)} %pack.1), calls=%async_computation | async-start | bytes 3145728 | tf_op jit(solution)/shard_map/all_to_all | solution.py:481
  33.5 27.7 %collective-permute-start.4 = (bf16[2,16,1792]{2,1,0:T(8,128)(2,1)S(1)}, bf16[2,16,1792]{2,1,0:T(8,128)(2,1)S(1)}, u32[]{:S(2)}, u32[]{:S(2)}) collective-permute-start(bf16[2,16,1792]{2,1,0:T(8,128)(2,1)S(1)} %slice.169), channel_id=1, source_target_pairs={{0,4},{1,5},{2,6},{3,7},{4,0},{5,1},{6,2},{7,3},{8,12},{9,13},{10,... | collective-permute-start | bytes 344072 | tf_op jit(solution)/shard_map/ppermute | solution.py:28
  36.2 30.5 %collective-permute-start.7 = (bf16[1,16,1792]{2,1,0:T(8,128)(2,1)S(1)}, bf16[1,16,1792]{2,1,0:T(8,128)(2,1)S(1)}, u32[]{:S(2)}, u32[]{:S(2)}) collective-permute-start(bf16[1,16,1792]{2,1,0:T(8,128)(2,1)S(1)} %slice.172), channel_id=1, source_target_pairs={{0,2},{1,3},{2,0},{3,1},{4,6},{5,7},{6,4},{7,5},{8,10},{9,11},{10,... | collective-permute-start | bytes 172040 | tf_op jit(solution)/shard_map/ppermute | solution.py:28
  62.1 10.4 %collective-permute-start.5 = (bf16[1,16,1792]{2,1,0:T(8,128)(2,1)S(1)}, bf16[1,16,1792]{2,1,0:T(8,128)(2,1)S(1)}, u32[]{:S(2)}, u32[]{:S(2)}) collective-permute-start(bf16[1,16,1792]{2,1,0:T(8,128)(2,1)S(1)} %slice.173), channel_id=1, source_target_pairs={{0,8},{1,9},{2,10},{3,11},{4,12},{5,13},{6,14},{7,15},{8,0},{9,1},... | collective-permute-start | bytes 172040 | tf_op jit(solution)/shard_map/ppermute | solution.py:28
  72.8 5.1 %collective-permute-start.8 = (bf16[16,1792]{1,0:T(8,128)(2,1)S(1)}, bf16[16,1792]{1,0:T(8,128)(2,1)S(1)}, u32[]{:S(2)}, u32[]{:S(2)}) collective-permute-start(bf16[16,1792]{1,0:T(8,128)(2,1)S(1)} %get-tuple-element.75), channel_id=1, source_target_pairs={{0,8},{1,9},{2,10},{3,11},{4,12},{5,13},{6,14},{7,15},{8,0},{9,1},... | collective-permute-start | bytes 172040 | tf_op jit(solution)/shard_map/ppermute | solution.py:28
  73.0 5.1 %collective-permute-start.11 = (bf16[16,1792]{1,0:T(8,128)(2,1)S(1)}, bf16[16,1792]{1,0:T(8,128)(2,1)S(1)}, u32[]{:S(2)}, u32[]{:S(2)}) collective-permute-start(bf16[16,1792]{1,0:T(8,128)(2,1)S(1)} %get-tuple-element.74), channel_id=1, source_target_pairs={{0,2},{1,3},{2,0},{3,1},{4,6},{5,7},{6,4},{7,5},{8,10},{9,11},{10,... | collective-permute-start | bytes 172040 | tf_op jit(solution)/shard_map/ppermute | solution.py:28
  78.0 5.9 %collective-permute-start.9 = (bf16[32,1792]{1,0:T(8,128)(2,1)S(1)}, bf16[32,1792]{1,0:T(8,128)(2,1)S(1)}, u32[]{:S(2)}, u32[]{:S(2)}) collective-permute-start(bf16[32,1792]{1,0:T(8,128)(2,1)S(1)} %pad_maximum_fusion.3), channel_id=1, source_target_pairs={{0,4},{1,5},{2,6},{3,7},{4,0},{5,1},{6,2},{7,3},{8,12},{9,13},{10,... | collective-permute-start | bytes 344072 | tf_op jit(solution)/shard_map/ppermute | solution.py:28
  78.1 7.8 %collective-permute-start.12 = (bf16[32,1792]{1,0:T(8,128)(2,1)S(1)}, bf16[32,1792]{1,0:T(8,128)(2,1)S(1)}, u32[]{:S(2)}, u32[]{:S(2)}) collective-permute-start(bf16[32,1792]{1,0:T(8,128)(2,1)S(1)} %pad_maximum_fusion.4), channel_id=1, source_target_pairs={{0,8},{1,9},{2,10},{3,11},{4,12},{5,13},{6,14},{7,15},{8,0},{9,1},... | collective-permute-start | bytes 344072 | tf_op jit(solution)/shard_map/ppermute | solution.py:28
  83.9 6.1 %collective-permute-start.10 = (bf16[64,1792]{1,0:T(8,128)(2,1)S(1)}, bf16[64,1792]{1,0:T(8,128)(2,1)S(1)}, u32[]{:S(2)}, u32[]{:S(2)}) collective-permute-start(bf16[64,1792]{1,0:T(8,128)(2,1)S(1)} %pad_maximum_fusion.1.refs_0_), channel_id=1, source_target_pairs={{0,2},{1,3},{2,0},{3,1},{4,6},{5,7},{6,4},{7,5},{8,10},{9,11},{10,... | collective-permute-start | bytes 688136 | tf_op jit(solution)/shard_map/ppermute | solution.py:28
  86.0 6.1 %collective-permute-start.13 = (bf16[64,1792]{1,0:T(8,128)(2,1)S(1)}, bf16[64,1792]{1,0:T(8,128)(2,1)S(1)}, u32[]{:S(2)}, u32[]{:S(2)}) collective-permute-start(bf16[64,1792]{1,0:T(8,128)(2,1)S(1)} %pad_maximum_fusion.2.refs_2_), channel_id=1, source_target_pairs={{0,4},{1,5},{2,6},{3,7},{4,0},{5,1},{6,2},{7,3},{8,12},{9,13},{10,... | collective-permute-start | bytes 688136 | tf_op jit(solution)/shard_map/ppermute | solution.py:28
  86.2 1.2 collective-permute-start.16
  96.1 0.8 copy-start.4
  96.1 1.0 copy-start.6
  97.1 11.5 %copy-start.7 = (bf16[8,144,256]{2,1,0:T(8,128)(2,1)S(1)}, bf16[8,144,256]{2,1,0:T(8,128)(2,1)}, u32[]{:S(2)}) copy-start(bf16[8,144,256]{2,1,0:T(8,128)(2,1)} %copy-done.6) | copy-start | bytes 1769476
  97.1 11.5 %copy-start.5 = (bf16[8,144,256]{2,1,0:T(8,128)(2,1)S(1)}, bf16[8,144,256]{2,1,0:T(8,128)(2,1)}, u32[]{:S(2)}) copy-start(bf16[8,144,256]{2,1,0:T(8,128)(2,1)} %copy-done.4) | copy-start | bytes 1769476
  97.2 6.8 %collective-permute-start.17 = (bf16[4,144,256]{2,1,0:T(8,128)(2,1)S(1)}, bf16[4,144,256]{2,1,0:T(8,128)(2,1)S(1)}, u32[]{:S(2)}, u32[]{:S(2)}) collective-permute-start(bf16[4,144,256]{2,1,0:T(8,128)(2,1)S(1)} %slice.103), channel_id=1, source_target_pairs={{0,2},{1,3},{2,0},{3,1},{4,6},{5,7},{6,4},{7,5},{8,10},{9,11},{10,... | collective-permute-start | bytes 884744 | tf_op jit(solution)/shard_map/ppermute | solution.py:28
  98.7 9.9 %collective-permute-start.18 = (bf16[4,144,256]{2,1,0:T(8,128)(2,1)S(1)}, bf16[4,144,256]{2,1,0:T(8,128)(2,1)S(1)}, u32[]{:S(2)}, u32[]{:S(2)}) collective-permute-start(bf16[4,144,256]{2,1,0:T(8,128)(2,1)S(1)} %slice.104), channel_id=1, source_target_pairs={{0,4},{1,5},{2,6},{3,7},{4,0},{5,1},{6,2},{7,3},{8,12},{9,13},{10,... | collective-permute-start | bytes 884744 | tf_op jit(solution)/shard_map/ppermute | solution.py:28
  108.8 6.8 %collective-permute-start.19 = (bf16[2,144,256]{2,1,0:T(8,128)(2,1)S(1)}, bf16[2,144,256]{2,1,0:T(8,128)(2,1)S(1)}, u32[]{:S(2)}, u32[]{:S(2)}) collective-permute-start(bf16[2,144,256]{2,1,0:T(8,128)(2,1)S(1)} %slice.167), channel_id=1, source_target_pairs={{0,4},{1,5},{2,6},{3,7},{4,0},{5,1},{6,2},{7,3},{8,12},{9,13},{10,... | collective-permute-start | bytes 442376 | tf_op jit(solution)/shard_map/ppermute | solution.py:28
  108.9 8.0 %collective-permute-start.20 = (bf16[2,144,256]{2,1,0:T(8,128)(2,1)S(1)}, bf16[2,144,256]{2,1,0:T(8,128)(2,1)S(1)}, u32[]{:S(2)}, u32[]{:S(2)}) collective-permute-start(bf16[2,144,256]{2,1,0:T(8,128)(2,1)S(1)} %slice.166), channel_id=1, source_target_pairs={{0,8},{1,9},{2,10},{3,11},{4,12},{5,13},{6,14},{7,15},{8,0},{9,1},... | collective-permute-start | bytes 442376 | tf_op jit(solution)/shard_map/ppermute | solution.py:28
  117.0 4.4 %collective-permute-start.22 = (bf16[1,144,256]{2,1,0:T(8,128)(2,1)S(1)}, bf16[1,144,256]{2,1,0:T(8,128)(2,1)S(1)}, u32[]{:S(2)}, u32[]{:S(2)}) collective-permute-start(bf16[1,144,256]{2,1,0:T(8,128)(2,1)S(1)} %slice.170), channel_id=1, source_target_pairs={{0,2},{1,3},{2,0},{3,1},{4,6},{5,7},{6,4},{7,5},{8,10},{9,11},{10,... | collective-permute-start | bytes 221192 | tf_op jit(solution)/shard_map/ppermute | solution.py:28
  118.5 5.3 %collective-permute-start.21 = (bf16[1,144,256]{2,1,0:T(8,128)(2,1)S(1)}, bf16[1,144,256]{2,1,0:T(8,128)(2,1)S(1)}, u32[]{:S(2)}, u32[]{:S(2)}) collective-permute-start(bf16[1,144,256]{2,1,0:T(8,128)(2,1)S(1)} %slice.171), channel_id=1, source_target_pairs={{0,8},{1,9},{2,10},{3,11},{4,12},{5,13},{6,14},{7,15},{8,0},{9,1},... | collective-permute-start | bytes 221192 | tf_op jit(solution)/shard_map/ppermute | solution.py:28
  124.5 1.3 collective-permute-start.23

commit v3 on v2

v3 whole, which is shorter than its diff:
```python
import functools
import math

import jax
import jax.numpy as jnp
from jax import lax
from jax.experimental import pallas as pl
from jax.experimental.pallas import tpu as pltpu
from jax.sharding import PartitionSpec as P

HEAD_DIM = 128
HEADS = 16
TEMB = 256
MIB = 1024 * 1024

epsilon = 1e-06

SMEM_SPEC = pl.BlockSpec(memory_space=pltpu.SMEM)
VMEM_SPEC = pl.BlockSpec(memory_space=pltpu.VMEM)


def params(mib):
    return pltpu.CompilerParams(vmem_limit_bytes=mib * MIB)


def swap(value, mask):
    devices = lax.axis_size("seq")
    return lax.ppermute(value, "seq", [(i, i ^ mask) for i in range(devices)])


def orders(chips):
    bits = [1 << i for i in range(chips.bit_length() - 1)]
    turn = len(bits) // 2
    return (bits, bits[turn:] + bits[:turn])


def position(chip, order):
    last = len(order) - 1
    return sum(((chip >> (bit.bit_length() - 1)) & 1) << (last - i) for i, bit in enumerate(order))


def member(at, order):
    last = len(order) - 1
    return sum(bit for i, bit in enumerate(order) if (at >> (last - i)) & 1)


def normalize(summed, norm_gain):
    scale_rows = lax.rsqrt(jnp.mean(summed * summed, 1, keepdims=True) + epsilon)
    return (summed * scale_rows * norm_gain.astype(jnp.float32)).astype(jnp.bfloat16)


def time_embedding(timesteps, modulation_weight):
    half_width = TEMB // 2
    freqs = jnp.exp(-math.log(10000.0) * jnp.arange(half_width, dtype=jnp.float32) / half_width)
    angles = timesteps.astype(jnp.float32)[:, None] * freqs[None, :]
    embedding = jnp.concatenate([jnp.cos(angles), jnp.sin(angles)], 1)
    embedding = jax.nn.silu(embedding).astype(jnp.bfloat16)
    flat = modulation_weight.reshape(modulation_weight.shape[0], -1)
    product = jnp.dot(embedding, flat, preferred_element_type=jnp.float32)
    return product.reshape(timesteps.shape[0], 2, -1)


def encoder_kernel(lane, order, place_ref, act_ref, weight_ref, own_ref, other_ref, *refs):
    chips = own_ref.shape[0]
    at, core = place_ref[lane], place_ref[2]
    lhs_ref = refs[0] if refs else act_ref

    if refs:

        @pl.when(pl.program_id(0) == 0)
        def _():
            lhs_ref[...] = act_ref[...].T

    result = jnp.dot(lhs_ref[...], weight_ref[...], preferred_element_type=jnp.float32)
    half = result.shape[0] // 2
    share = half // chips
    first = core == 0
    own = jnp.where(first, result[:half], result[half:]).astype(own_ref.dtype)
    other = jnp.where(first, result[half:], result[:half]).astype(own_ref.dtype)
    own = own.reshape(chips, share, -1)
    other = other.reshape(chips, share, -1)
    for block in range(chips):
        own_ref[at ^ position(block, order)] = own[block]
        other_ref[at ^ position(block, order)] = other[block]


def encoder(lane, order, place, act, weight):
    chips = 1 << len(order)
    depth = weight.shape[0]
    rows = act.size // depth
    width = weight.shape[1] // 2
    steps = 2
    turn = act.shape[0] == depth
    tile = width // steps
    share = rows // 2 // chips
    out = jax.ShapeDtypeStruct((chips, share, width), jnp.bfloat16)
    out_spec = pl.BlockSpec((chips, share, tile), lambda i: (0, 0, i))
    return pl.pallas_call(
        functools.partial(encoder_kernel, lane, order),
        grid=(steps,),
        out_shape=(out, out) + (jax.ShapeDtypeStruct((rows, depth), act.dtype),) * turn,
        in_specs=[
            SMEM_SPEC,
            pl.BlockSpec(act.shape, lambda i: (0, 0)),
            pl.BlockSpec((depth, tile), lambda i: (0, lane * steps + i)),
        ],
        out_specs=(out_spec, out_spec) + (pl.BlockSpec((rows, depth), lambda i: (0, 0)),) * turn,
        compiler_params=params(24),
        cost_estimate=pl.CostEstimate(
            flops=2 * rows * depth * width,
            bytes_accessed=2 * (depth * rows + depth * width + rows * width),
            transcendentals=0,
        ),
        name="encoder",
    )(place, act, weight)


def slot_rows(chips, width):
    per_slot = 2 * 128 // width
    return chips * per_slot, -(-(chips * per_slot + 2) // 16) * 16


def project_kernel(lanes, place_ref, *refs):
    pieces, refs = (refs[:2], refs[2:4]), refs[4:]
    win0, win1, kv0, kv1, mod0, mod1, *outs, states, proj0, proj1, sums = refs
    chip = place_ref[3]
    half_chips = outs[0].shape[0]
    chips = 2 * half_chips
    rows = proj0.shape[0]
    share = rows // chips
    depth = states.shape[1]
    contract = (((1,), (1,)), ((), ()))
    for lane, order in enumerate(lanes):
        top, low = pieces[lane]
        states[: rows // 2, :] = top[...]
        states[rows // 2 :, :] = low[...]
        span = slice(lane * depth, (lane + 1) * depth)
        for win, proj in ((win0, proj0), (win1, proj1)):
            part = lax.dot_general(
                states[...], win[:, span], contract, preferred_element_type=jnp.float32
            )
            for at in range(chips):
                start = pl.multiple_of((chip ^ member(at, order)) * share, share)
                block = part[at * share : (at + 1) * share]
                if lane == 0:
                    proj[pl.ds(start, share), :] = block
                else:
                    proj[pl.ds(start, share), :] += block
    value0, value1 = proj0[...], proj1[...]
    first = jnp.sum(value0, 1, keepdims=True) + jnp.sum(value1, 1, keepdims=True)
    second = jnp.sum(value0 * value0, 1, keepdims=True) + jnp.sum(value1 * value1, 1, keepdims=True)
    lane = lax.broadcasted_iota(jnp.int32, sums.shape, 1)
    sums[...] = jnp.where(lane == 0, first, second).T
    left = []
    for value, mod in ((value0, mod0), (value1, mod1)):
        scale, shift = 1.0 + mod[1:2, :], mod[0:1, :]
        row = lax.broadcasted_iota(jnp.int32, (16, value.shape[1]), 0)
        lines = jnp.where(row < 2, scale, shift)
        high = lines.astype(jnp.bfloat16).astype(jnp.float32)
        lines = jnp.where(row % 2 == 0, high, lines - high)
        lines = jnp.where(row < 4, lines, 0.0)
        left.append(jnp.concatenate([value * scale, lines], 0).astype(jnp.bfloat16))
    width = outs[0].shape[2]
    slots, extra = slot_rows(chips, width)
    per_slot = slots // chips
    row = lax.broadcasted_iota(jnp.int32, (extra, width), 0)
    column = lax.broadcasted_iota(jnp.int32, (extra, width), 1)
    half = kv0.shape[1] // 2
    for lane, order in enumerate(lanes):
        line = sums[lane : lane + 1, :]
        high = line.astype(jnp.bfloat16).astype(jnp.float32)
        low = line - high
        if per_slot == 1:
            line = jnp.concatenate([high, low], 1)
        else:
            line = jnp.where(row % 2 == 0, high, low)
        line = jnp.where(row // per_slot == chip, line, 0.0)
        for at in reversed(range(chips)):
            out_ref, to = outs[2 * lane + at // half_chips], at % half_chips
            start = lane * half + (chip ^ member(at, order)) * width
            columns = pl.ds(pl.multiple_of(start, width), width)
            value = jnp.dot(left[0], kv0[:, columns], preferred_element_type=jnp.float32)
            value += jnp.dot(left[1], kv1[:, columns], preferred_element_type=jnp.float32)
            out_ref[to, :rows, :] = value[:rows].astype(out_ref.dtype)
            below = jnp.where(row == slots, value[rows : rows + 1] + value[rows + 1 : rows + 2], line)
            below = jnp.where(
                row == slots + 1, value[rows + 2 : rows + 3] + value[rows + 3 : rows + 4], below
            )
            out_ref[to, rows:, :] = below.astype(out_ref.dtype)


def project(lanes, place, pieces, win0, win1, kv0, kv1, mod0, mod1):
    chips = 1 << len(lanes[0])
    rows = 2 * pieces[0].shape[0]
    features, depth = win0.shape
    total = kv0.shape[1]
    width = total // 2 // chips
    extra = slot_rows(chips, width)[1]
    out = jax.ShapeDtypeStruct((chips // 2, rows + extra, width), jnp.bfloat16)
    return pl.pallas_call(
        functools.partial(project_kernel, lanes),
        out_shape=(out,) * 4,
        in_specs=[SMEM_SPEC] + [VMEM_SPEC] * 10,
        out_specs=(VMEM_SPEC,) * 4,
        scratch_shapes=[
            pltpu.VMEM((rows, depth // 2), jnp.bfloat16),
            pltpu.VMEM((rows, features), jnp.float32),
            pltpu.VMEM((rows, features), jnp.float32),
            pltpu.VMEM((rows, 128), jnp.float32),
        ],
        compiler_params=params(20),
        cost_estimate=pl.CostEstimate(
            flops=4 * rows * features * (depth + total),
            bytes_accessed=2 * (rows * depth + 2 * features * (depth + total) + rows * total),
            transcendentals=0,
        ),
        name="project",
    )(place, *pieces, win0, win1, kv0, kv1, mod0, mod1)


def combine_kernel(chips, model_width, place_ref, *refs):
    refs, mine_ref, sent_ref = refs[:4], refs[4], refs[5]
    core = place_ref[2]
    rows = mine_ref.shape[0]
    width = refs[0].shape[1]
    slots = slot_rows(chips, width)[0]
    totals = [
        refs[2 * lane][...].astype(jnp.float32) + refs[2 * lane + 1][...].astype(jnp.float32)
        for lane in range(2)
    ]
    sums = []
    for total in totals:
        line = jnp.sum(total[rows : rows + slots], 0, keepdims=True)
        if width > 128:
            line = line[:, :128] + line[:, 128:]
        sums.append(line)
    mean_val = sums[0] / model_width
    scale = lax.rsqrt(sums[1] / model_width - mean_val * mean_val + epsilon)
    mean_val = jnp.broadcast_to(mean_val, (rows, rows)).T[:, 0:1]
    scale = jnp.broadcast_to(scale, (rows, rows)).T[:, 0:1]
    texts = []
    for total in totals:
        text = (total[:rows] - mean_val * total[rows + slots : rows + slots + 1]) * scale
        texts.append(text + total[rows + slots + 1 : rows + slots + 2])
    for part, text in enumerate(texts):
        span = slice(part * HEAD_DIM, (part + 1) * HEAD_DIM)
        if width > HEAD_DIM:
            low, high = text[:, :HEAD_DIM], text[:, HEAD_DIM:]
            mine_ref[:, span] = jnp.where(core == 0, low, high).astype(mine_ref.dtype)
            sent_ref[:, span] = jnp.where(core == 0, high, low).astype(mine_ref.dtype)
        else:
            mine_ref[:, span] = text.astype(mine_ref.dtype)
            sent_ref[:, span] = text.astype(mine_ref.dtype)


def combine(place, parts, chips, rows, model_width):
    out = jax.ShapeDtypeStruct((rows, 2 * HEAD_DIM), jnp.bfloat16)
    return pl.pallas_call(
        functools.partial(combine_kernel, chips, model_width),
        out_shape=(out, out),
        in_specs=[SMEM_SPEC] + [VMEM_SPEC] * 4,
        out_specs=(VMEM_SPEC, VMEM_SPEC),
        compiler_params=params(8),
        cost_estimate=pl.CostEstimate(
            flops=8 * rows * 512, bytes_accessed=12 * rows * 512, transcendentals=0
        ),
        name="combine",
    )(place, *parts)


def pack_kernel(copies, place_ref, queries_ref, keys_ref, values_ref, *outs):
    img_dev = keys_ref.shape[0]
    part_rows = img_dev // copies
    for mask, out_ref in enumerate(outs):
        device = (2 * place_ref[3] + place_ref[2]) ^ mask
        head, copy = device // copies, device % copies
        span = pl.ds(pl.multiple_of(head * HEAD_DIM, HEAD_DIM), HEAD_DIM)
        rows = pl.ds(pl.multiple_of(copy * part_rows, part_rows), part_rows)
        out_ref[:img_dev, :] = keys_ref[:, span]
        out_ref[img_dev : 2 * img_dev, :] = values_ref[:, span]
        out_ref[2 * img_dev :, :] = queries_ref[rows, span]


def pack(devices, copies, place, queries, keys, values):
    img_dev = keys.shape[0]
    rows = 2 * img_dev + img_dev // copies
    out = jax.ShapeDtypeStruct((rows, HEAD_DIM), jnp.bfloat16)
    return pl.pallas_call(
        functools.partial(pack_kernel, copies),
        out_shape=(out,) * devices,
        in_specs=[SMEM_SPEC] + [VMEM_SPEC] * 3,
        out_specs=(VMEM_SPEC,) * devices,
        compiler_params=params(8),
        cost_estimate=pl.CostEstimate(
            flops=0, bytes_accessed=4 * devices * rows * HEAD_DIM, transcendentals=0
        ),
        name="pack",
    )(place, queries, keys, values)


def unpack_kernel(copies, part_rows, place_ref, *refs):
    blocks, (attended_ref, text_ref) = refs[:-2], refs[-2:]
    device = 2 * place_ref[3] + place_ref[2]
    share = text_ref.shape[0]
    half = text_ref.shape[1] // 2
    for mask, block_ref in enumerate(blocks):
        head, copy = (device ^ mask) // copies, (device ^ mask) % copies
        start = pl.multiple_of(head * HEAD_DIM, HEAD_DIM)
        rows = pl.ds(pl.multiple_of(copy * part_rows, part_rows), part_rows)
        attended_ref[rows, pl.ds(start, HEAD_DIM)] = block_ref[:part_rows, :]
        block = block_ref[part_rows:, :].astype(jnp.float32)
        text_ref[:, pl.ds(start, HEAD_DIM)] = block[:share].astype(text_ref.dtype)
        start = pl.multiple_of(half + head * HEAD_DIM, HEAD_DIM)
        text_ref[:, pl.ds(start, HEAD_DIM)] = block[share:].astype(text_ref.dtype)


def unpack(copies, part_rows, place, blocks):
    share = (blocks[0].shape[0] - part_rows) // 2
    return pl.pallas_call(
        functools.partial(unpack_kernel, copies, part_rows),
        out_shape=(
            jax.ShapeDtypeStruct((part_rows * copies, HEADS * HEAD_DIM), jnp.bfloat16),
            jax.ShapeDtypeStruct((share, 2 * HEADS * HEAD_DIM), jnp.bfloat16),
        ),
        in_specs=[SMEM_SPEC] + [VMEM_SPEC] * len(blocks),
        out_specs=(VMEM_SPEC, VMEM_SPEC),
        compiler_params=params(8),
        name="unpack",
    )(place, *blocks)


def image_kernel(factor, call, calls, img_dev, *refs):
    pieces, (sum_ref, norm_ref, keys_ref, values_ref) = refs[:-4], refs[-4:]
    contract = (((1,), (1,)), ((), ()))
    for at, piece in enumerate(pieces):
        rows = slice(at * img_dev, (at + 1) * img_dev)
        keys_ref[rows, :] = piece[:img_dev, :]
        values_ref[rows, :] = piece[img_dev : 2 * img_dev, :]
    blocks = pieces[call * len(pieces) // calls : (call + 1) * len(pieces) // calls]
    part_rows = sum_ref.shape[0] // len(blocks)
    group = max(1, 256 // part_rows)
    for step in range(len(blocks) // group):
        span = slice(step * group * part_rows, (step + 1) * group * part_rows)
        queries = [piece[2 * img_dev :, :] for piece in blocks[step * group : (step + 1) * group]]
        queries = jnp.concatenate(queries, 0)
        scores = lax.dot_general(queries, keys_ref[...], contract, preferred_element_type=jnp.float32)
        scores = scores * factor
        top = jnp.max(scores, 1, keepdims=True)
        weights = jnp.exp2(scores - top)
        total = jnp.sum(weights, 1, keepdims=True)
        sum_ref[span, :] = jnp.dot(
            weights.astype(jnp.bfloat16), values_ref[...], preferred_element_type=jnp.float32
        )
        lane = lax.broadcasted_iota(jnp.int32, (queries.shape[0], 128), 1)
        norm_ref[span, :] = jnp.where(lane < 64, top, total)


def image_attention(pieces, img_dev, factor, call, calls):
    part_rows = pieces[0].shape[0] - 2 * img_dev
    keys = len(pieces) * img_dev
    count = len(pieces) * part_rows // calls
    out = jax.ShapeDtypeStruct((count, HEAD_DIM), jnp.float32)
    return pl.pallas_call(
        functools.partial(image_kernel, factor, call, calls, img_dev),
        out_shape=(out, out),
        in_specs=[VMEM_SPEC] * len(pieces),
        out_specs=(VMEM_SPEC, VMEM_SPEC),
        scratch_shapes=[pltpu.VMEM((keys, HEAD_DIM), jnp.bfloat16)] * 2,
        compiler_params=params(24),
        cost_estimate=pl.CostEstimate(
            flops=4 * count * keys * HEAD_DIM,
            bytes_accessed=4 * keys * HEAD_DIM + 10 * count * HEAD_DIM,
            transcendentals=count * keys,
        ),
        name="image_attention",
    )(*pieces)


def finish_kernel(factor, masks, img_dev, place_ref, *refs):
    pieces, refs = refs[: len(masks)], refs[len(masks) :]
    sum_ref, norm_ref, mine_ref, got_ref, *outs, text_ref = refs
    chip, core, valid = place_ref[3], place_ref[2], place_ref[4]
    half = mine_ref.shape[0]
    contract = (((1,), (1,)), ((), ()))
    mine, got = mine_ref[...], got_ref[...]
    keys = jnp.concatenate([mine[:, :HEAD_DIM], got[:, :HEAD_DIM]], 0)
    values = jnp.concatenate([mine[:, HEAD_DIM:], got[:, HEAD_DIM:]], 0)
    lane = lax.broadcasted_iota(jnp.int32, (1, 2 * half), 1)
    text_position = jnp.where((lane >= half) == (core == 0), half, 0) + lane % half
    part_rows = sum_ref.shape[0] // len(pieces)
    group = max(1, 512 // part_rows)
    for step in range(len(pieces) // group):
        span = slice(step * group * part_rows, (step + 1) * group * part_rows)
        queries = [piece[2 * img_dev :, :] for piece in pieces[step * group : (step + 1) * group]]
        queries = jnp.concatenate(queries, 0)
        scores = lax.dot_general(queries, keys, contract, preferred_element_type=jnp.float32) * factor
        scores = jnp.where(text_position < valid, scores, -jnp.inf)
        before = norm_ref[span, 0:1]
        top = jnp.maximum(before, jnp.max(scores, 1, keepdims=True))
        rescale = jnp.exp2(before - top)
        weights = jnp.exp2(scores - top)
        total = norm_ref[span, 64:65] * rescale + jnp.sum(weights, 1, keepdims=True)
        mixed = sum_ref[span, :] * rescale + jnp.dot(
            weights.astype(jnp.bfloat16), values, preferred_element_type=jnp.float32
        )
        mixed = (mixed / total).astype(jnp.bfloat16)
        for at in range(group):
            outs[step * group + at][:part_rows, :] = mixed[at * part_rows : (at + 1) * part_rows]
    low, high = mine.astype(jnp.float32), got.astype(jnp.float32)
    text_ref[:half, :] = jnp.where(core == 0, low, high)
    text_ref[half:, :] = jnp.where(core == 0, high, low)
    share = (outs[0].shape[0] - part_rows) // 2
    for at, out_ref in enumerate(outs):
        device = (2 * chip + core) ^ masks[at]
        block = text_ref[pl.ds(pl.multiple_of(device * share, share), share), :]
        block = jnp.concatenate([block[:, :HEAD_DIM], block[:, HEAD_DIM:]], 0)
        out_ref[part_rows:, :] = block.astype(out_ref.dtype)


def finish(place, masks, pieces, image, mine, got, img_dev, factor):
    devices = len(pieces)
    part_rows = pieces[0].shape[0] - 2 * img_dev
    half = mine.shape[0]
    share = 2 * half // devices
    count = len(masks) * part_rows
    out = jax.ShapeDtypeStruct((part_rows + 2 * share, HEAD_DIM), jnp.bfloat16)
    return pl.pallas_call(
        functools.partial(finish_kernel, factor, masks, img_dev),
        out_shape=(out,) * len(masks),
        in_specs=[SMEM_SPEC] + [VMEM_SPEC] * (len(masks) + 4),
        out_specs=(VMEM_SPEC,) * len(masks),
        scratch_shapes=[pltpu.VMEM((2 * half, 2 * HEAD_DIM), jnp.float32)],
        compiler_params=params(16),
        cost_estimate=pl.CostEstimate(
            flops=8 * count * half * HEAD_DIM,
            bytes_accessed=12 * count * HEAD_DIM,
            transcendentals=2 * count * half,
        ),
        name="finish",
    )(place, *[pieces[mask] for mask in masks], *image, mine, got)


def add(one, other, dtype):
    return (one.astype(jnp.float32) + other.astype(jnp.float32)).astype(dtype)


ROUND = {12: 1, 3: 2, 4: 2, 13: 3, 1: 3, 10: 4, 5: 4, 6: 5, 7: 5, 14: 6, 11: 7, 15: 7}


def local(
    enc_act,
    down_weight,
    norm_gain,
    text_in_weight,
    modulation_weight,
    key_value_weight,
    timesteps,
    lengths,
    image_queries,
    image_key_values,
):
    devices = lax.axis_size("seq")
    chips = devices // 2
    copies = devices // HEADS
    text_len = enc_act.shape[1]
    img_dev = image_queries.shape[1]
    part_rows = img_dev // copies
    factor = math.log2(math.e) / math.sqrt(HEAD_DIM)
    lanes = orders(chips)
    index = lax.axis_index("seq")
    chip, core = index // 2, index % 2
    place = jnp.stack([position(chip, lanes[0]), position(chip, lanes[1]), core, chip, lengths[0]])
    place = place.astype(jnp.int32)

    win0, kv0 = text_in_weight.T, key_value_weight
    win1, kv1 = swap(win0, 1), swap(kv0, 1)
    mod0 = time_embedding(timesteps, modulation_weight)[0]
    mod1 = swap(mod0, 1)

    rounds = len(lanes[0])
    tie = lax.optimization_barrier

    pieces = pack(
        devices, copies, place, image_queries[0], image_key_values[0, :, 0], image_key_values[0, :, 1]
    )
    pieces = list(pieces)
    masks = [[m for m in range(1, devices) if ROUND.get(m, 0) == at] for at in range(8)]

    def send_pieces(at, chain):
        chain, held = tie((chain, [pieces[mask] for mask in masks[at]]))
        for mask, piece in zip(masks[at], held):
            pieces[mask] = swap(piece, mask)
        return chain

    def take_pieces(at, chain):
        chain, held = tie((chain, [pieces[mask] for mask in masks[at]]))
        for mask, piece in zip(masks[at], held):
            pieces[mask] = piece
        return chain

    act = send_pieces(0, enc_act[0].T)
    keep, sent = [], []
    for lane, order in enumerate(lanes):
        own, other, *turned = encoder(lane, order, place, act, down_weight)
        if lane == 0:
            act = turned[0]
        else:
            other = take_pieces(0, other)
        got = swap(other, 1)
        sent.append(add(own[chips // 2 :], got[chips // 2 :], jnp.bfloat16))
        keep.append(add(own[: chips // 2], got[: chips // 2], jnp.float32))
    for step in range(rounds):
        if step < 3:
            sent = send_pieces(1 + step, sent)
        got = [swap(part, 2 * order[step]) for part, order in zip(sent, lanes)]
        if step == 0:
            got, win1, kv1 = tie((got, win1, kv1))
        elif step < 3:
            got = take_pieces(step, got)
        half = keep[0].shape[0] // 2
        if half:
            sent = [add(mine[half:], part[half:], jnp.bfloat16) for mine, part in zip(keep, got)]
            keep = [add(mine[:half], part[:half], jnp.float32) for mine, part in zip(keep, got)]
    summed = [add(mine[0], part[0], jnp.float32) for mine, part in zip(keep, got)]

    width = summed[0].shape[1]
    square = sum(jnp.sum(part * part, 1, keepdims=True) for part in summed)
    scale_rows = lax.rsqrt(square / (2 * width) + epsilon)
    gains = norm_gain.astype(jnp.float32)
    states = [
        (part * scale_rows * gains[lane * width : (lane + 1) * width]).astype(jnp.bfloat16)
        for lane, part in enumerate(summed)
    ]
    for step in range(rounds):
        if step < 3:
            states = send_pieces(4 + step, states)
        bit = rounds - 1 - step
        got = [swap(state, 2 * order[bit]) for state, order in zip(states, lanes)]
        if step < 3:
            got = take_pieces(3 + step, got)
        if bit:
            states = [jnp.concatenate(pair, 0) for pair in zip(states, got)]
    got = send_pieces(7, got)
    states = [state for pair in zip(states, got) for state in pair]

    blocks = project(lanes, place, states, win0, win1, kv0, kv1, mod0, mod1)
    keep, sent = [blocks[0], blocks[2]], [blocks[1], blocks[3]]
    images = []
    for step in range(rounds):
        got = [swap(part, 2 * order[step]) for part, order in zip(sent, lanes)]
        if step == 0:
            got = take_pieces(6, got)
            got = take_pieces(7, got)
        elif step <= 2:
            sent, pieces = tie((sent, pieces))
            image = image_attention(pieces, img_dev, factor, step - 1, 2)
            got, image = tie((got, image))
            images.append(image)
        half = keep[0].shape[0] // 2
        if half:
            sent = [add(mine[half:], part[half:], jnp.bfloat16) for mine, part in zip(keep, got)]
            keep = [add(mine[:half], part[:half], jnp.float32) for mine, part in zip(keep, got)]
    parts = [part[0] for pair in zip(keep, got) for part in pair]
    model_width = text_in_weight.shape[1] * devices
    mine, sent = combine(place, parts, chips, text_len // 2, model_width)
    got = swap(sent, 1)

    back = [None] * devices
    for call in (1, 0):
        masks = range(call * devices // 2, (call + 1) * devices // 2)
        blocks = finish(place, masks, pieces, images[call], mine, got, img_dev, factor)
        for mask, block in zip(masks, blocks):
            back[mask] = swap(block, mask) if mask else block
    attended, text_kv = unpack(copies, part_rows, place, back)
    return (attended[None], text_kv)


def solution(mesh):
    in_specs = (
        P("dp", None, "seq"),
        P("seq", None),
        P(),
        P(None, "seq"),
        P(None, None, "seq"),
        P("seq", None),
        P("dp"),
        P("dp"),
        P("dp", "seq", None),
        P("dp", "seq", None, None),
    )
    out_specs = (P("dp", "seq", None), P(("dp", "seq"), None))
    return jax.shard_map(local, mesh=mesh, in_specs=in_specs, out_specs=out_specs, check_vma=False)
```

time: 153 us -> 162 us (1.059)
  starting transfers between devices: 30.8 us -> 67.4 us
  blocking collectives: 21.8 us -> 0 us
  waiting for transfers between devices: 59.2 us -> 55 us
  local copies, waits for them, and re-layouts: 8.89 us -> 11.5 us
  other arithmetic: 3.61 us -> 1.03 us
    ppermute x24 -> x54, starting transfers between devices: 27 us -> 67.4 us  [swap(): return lax.ppermute(value, 'seq', [(i, i ^ mask) for i in range(devices)])]
    all_to_all x1 -> x0, blocking collectives: 21.8 us -> none  [local(): back = lax.all_to_all(back, 'seq', split_axis=0, concat_axis=0, tiled=True)]
    ppermute x24 -> x54, waiting for transfers between devices: 59.2 us -> 55 us  [swap(): return lax.ppermute(value, 'seq', [(i, i ^ mask) for i in range(devices)])]
    all_to_all x1 -> x0, starting transfers between devices: 3.89 us -> none  [local(): lax.all_to_all(packed, 'seq', split_axis=0, concat_axis=0, tiled=True)]
    slice x12 -> x2, local copies, waits for them, and re-layouts: 1.13 us -> 4.51 us  [the longest x1 4.5 us: local(): image_key_values[0, :, 1]]
    add x10 -> x3, other arithmetic: 3.22 us -> 0.22 us  [add(): return (one.astype(jnp.float32) + other.astype(jnp.float32)).astype(dtype)]
    unnamed x24 -> x16, local copies, waits for them, and re-layouts: 7.18 us -> 4.58 us
    pallas_call x5 -> x6, Pallas kernels: 18.3 us -> 16 us  [the longest x2 7.34 us: image_attention(): pl.pallas_call(functools.partial(image_kernel, factor, call, calls, img_d...]
  transfers between devices with their start and end apart: 25 -> 54, of which waited for: 18 -> 23; matrix products, arithmetic and copies ran while one was open for 3% -> 1% of each run, Pallas kernels for 11% -> 8%
where the time goes in v3:
time: 162 us; the launch traced here: 161 us
  starting transfers between devices  67.4 us (42%)
  waiting for transfers between devices  55 us (34%)
  Pallas kernels  24 us (15%)
  local copies, waits for them, and re-layouts  11.5 us (7%)
  between operations  2.33 us (1%)
    ppermute x54, starting transfers between devices, swap(): return lax.ppermute(value, 'seq', [(i, i ^ mask) for i in range(devices)])  67.4 us
    ppermute x54, waiting for transfers between devices, swap(): return lax.ppermute(value, 'seq', [(i, i ^ mask) for i in range(devices)])  55 us
    pallas_call x2, Pallas kernels, image_attention(): pl.pallas_call(functools.partial(image_kernel, factor, call, calls, img_d...  7.34 us
    pallas_call x2, Pallas kernels, encoder(): pl.pallas_call(functools.partial(encoder_kernel, lane, order), grid=(step...  5.51 us
    pallas_call x2, Pallas kernels, finish(): pl.pallas_call(functools.partial(finish_kernel, factor, masks, img_dev),...  5.38 us
    unnamed x16, local copies, waits for them, and re-layouts  4.58 us
    slice x1, local copies, waits for them, and re-layouts, local(): image_key_values[0, :, 1]  4.5 us
  transfers between devices with their start and end apart: 54, of which 23 were waited for; matrix products, arithmetic and copies ran while one was open for 1% of the time, Pallas kernels for 8%

profile of v3, /device:TPU:0, one launch (start us, length us, event | category | flops | bytes accessed | tf_op | source)
XLA Modules:
  0.0 161.4 jit_solution(13035058076387946356)
XLA Ops:
  1.4 4.5 %fusion.17 = (bf16[1,128,1,2048]{3,2,1,0:T(2,128)(2,1)}, bf16[1,128,1,2048]{3,2,1,0:T(2,128)(2,1)}) fusion(bf16[1,128,2,2048]{3,2,1,0:T(2,128)(2,1)} %param.19), kind=kLoop, calls=%fused_computation.52 | loop fusion | bytes 2097152 | tf_op jit(solution)/shard_map/slice | solution.py:484
  5.9 2.3 %copy_bitcast_fusion = (bf16[128,2048]{1,0:T(8,128)(2,1)S(1)}, bf16[128,2048]{1,0:T(8,128)(2,1)S(1)}) fusion(bf16[1,128,1,2048]{3,2,1,0:T(2,128)(2,1)} %get-tuple-element.308, bf16[1,128,1,2048]{3,2,1,0:T(2,128)(2,1)} %get-tuple-element.309), kind=kLoop, calls=%fused_computation | loop fusion | bytes 2097152 | tf_op jit(solution)/shard_map/squeeze | solution.py:484
  8.2 1.0 copy-done.6
  9.3 1.0 pack.1
  10.3 3.5 %copy-done.1 = bf16[1184,3584]{1,0:T(8,128)(2,1)S(1)} copy-done((bf16[1184,3584]{1,0:T(8,128)(2,1)S(1)}, bf16[1184,3584]{1,0:T(8,128)(2,1)}, u32[]{:S(2)}) %copy-start.1) | copy-done | bytes 8486936
  13.8 2.8 %encoder.2 = (bf16[8,16,1792]{2,1,0:T(8,128)(2,1)S(1)}, bf16[8,16,1792]{2,1,0:T(8,128)(2,1)S(1)}, bf16[256,1184]{1,0:T(8,128)(2,1)S(1)}) custom-call(s32[5]{0:T(128)S(1)} %stack.19.place_ref, bf16[1184,256]{1,0:T(8,128)(2,1)S(1)} %bitcast.46, bf16[1184,3584]{1,0:T(8,128)(2,1)S(1)} %copy-done.1), custom_call_target="tpu_custom_call" | custom-call | flops 1086324736 | bytes 5767168 | tf_op jit(solution)/shard_map/encoder/pallas_call | solution.py:98
  17.2 2.9 %collective-permute-start.1 = (bf16[384,128]{1,0:T(8,128)(2,1)S(1)}, bf16[384,128]{1,0:T(8,128)(2,1)S(1)}, u32[]{:S(2)}, u32[]{:S(2)}) collective-permute-start(bf16[384,128]{1,0:T(8,128)(2,1)S(1)} %get-tuple-element.164), channel_id=1, source_target_pairs={{0,2},{1,3},{2,0},{3,1},{4,6},{5,7},{6,4},{7,5},{8,10},{9,11},{10,... | collective-permute-start | bytes 294920 | tf_op jit(solution)/shard_map/ppermute | solution.py:28
  20.1 2.6 %collective-permute-start.2 = (bf16[384,128]{1,0:T(8,128)(2,1)S(1)}, bf16[384,128]{1,0:T(8,128)(2,1)S(1)}, u32[]{:S(2)}, u32[]{:S(2)}) collective-permute-start(bf16[384,128]{1,0:T(8,128)(2,1)S(1)} %get-tuple-element.165), channel_id=1, source_target_pairs={{0,8},{1,9},{2,10},{3,11},{4,12},{5,13},{6,14},{7,15},{8,0},{9,1},... | collective-permute-start | bytes 294920 | tf_op jit(solution)/shard_map/ppermute | solution.py:28
  23.1 1.7 %collective-permute-start.3 = (bf16[384,128]{1,0:T(8,128)(2,1)S(1)}, bf16[384,128]{1,0:T(8,128)(2,1)S(1)}, u32[]{:S(2)}, u32[]{:S(2)}) collective-permute-start(bf16[384,128]{1,0:T(8,128)(2,1)S(1)} %get-tuple-element.166), channel_id=1, source_target_pairs={{0,9},{1,8},{2,11},{3,10},{4,13},{5,12},{6,15},{7,14},{8,1},{9,0},... | collective-permute-start | bytes 294920 | tf_op jit(solution)/shard_map/ppermute | solution.py:28
  24.8 2.7 %encoder.3 = (bf16[8,16,1792]{2,1,0:T(8,128)(2,1)S(1)}, bf16[8,16,1792]{2,1,0:T(8,128)(2,1)S(1)}) custom-call(s32[5]{0:T(128)S(1)} %stack.19.place_ref, bf16[256,1184]{1,0:T(8,128)(2,1)S(1)} %get-tuple-element.161.act_ref, bf16[1184,3584]{1,0:T(8,128)(2,1)S(1)} %copy-done.2), custom_call_target="tpu_custom_call" | custom-call | flops 1086324736 | bytes 5767168 | tf_op jit(solution)/shard_map/encoder/pallas_call | solution.py:98
  27.6 3.2 %collective-permute-done.2.refs_8_.refs_0_ = bf16[384,128]{1,0:T(8,128)(2,1)S(1)} collective-permute-done((bf16[384,128]{1,0:T(8,128)(2,1)S(1)}, bf16[384,128]{1,0:T(8,128)(2,1)S(1)}, u32[]{:S(2)}, u32[]{:S(2)}) %collective-permute-start.2) | collective-permute-done | bytes 98336 | tf_op jit(solution)/shard_map/ppermute | solution.py:28
  30.8 1.3 collective-permute-done.3.refs_9_.refs_1_
  32.4 1.5 collective-permute-done.4
  34.0 0.7 collective-permute-start.5
  34.8 1.0 collective-permute-start.6
  35.7 6.1 %collective-permute-done.5 = bf16[4,16,1792]{2,1,0:T(8,128)(2,1)S(1)} collective-permute-done((bf16[4,16,1792]{2,1,0:T(8,128)(2,1)S(1)}, bf16[4,16,1792]{2,1,0:T(8,128)(2,1)S(1)}, u32[]{:S(2)}, u32[]{:S(2)}) %collective-permute-start.5) | collective-permute-done | bytes 229408 | tf_op jit(solution)/shard_map/ppermute | solution.py:28
  42.2 2.6 %collective-permute-start.10 = (bf16[2,16,1792]{2,1,0:T(8,128)(2,1)S(1)}, bf16[2,16,1792]{2,1,0:T(8,128)(2,1)S(1)}, u32[]{:S(2)}, u32[]{:S(2)}) collective-permute-start(bf16[2,16,1792]{2,1,0:T(8,128)(2,1)S(1)} %get-tuple-element.176), channel_id=1, source_target_pairs={{0,8},{1,9},{2,10},{3,11},{4,12},{5,13},{6,14},{7,15},{8,0},{9,1},... | collective-permute-start | bytes 344072 | tf_op jit(solution)/shard_map/ppermute | solution.py:28
  44.8 1.7 %collective-permute-start.9 = (bf16[2,16,1792]{2,1,0:T(8,128)(2,1)S(1)}, bf16[2,16,1792]{2,1,0:T(8,128)(2,1)S(1)}, u32[]{:S(2)}, u32[]{:S(2)}) collective-permute-start(bf16[2,16,1792]{2,1,0:T(8,128)(2,1)S(1)} %get-tuple-element.175), channel_id=1, source_target_pairs={{0,4},{1,5},{2,6},{3,7},{4,0},{5,1},{6,2},{7,3},{8,12},{9,13},{10,... | collective-permute-start | bytes 344072 | tf_op jit(solution)/shard_map/ppermute | solution.py:28
  47.2 5.9 %collective-permute-done.11.refs_12_.refs_4_ = bf16[384,128]{1,0:T(8,128)(2,1)S(1)} collective-permute-done((bf16[384,128]{1,0:T(8,128)(2,1)S(1)}, bf16[384,128]{1,0:T(8,128)(2,1)S(1)}, u32[]{:S(2)}, u32[]{:S(2)}) %collective-permute-start.11) | collective-permute-done | bytes 98336 | tf_op jit(solution)/shard_map/ppermute | solution.py:28
  53.2 3.8 %collective-permute-start.12 = (bf16[1,16,1792]{2,1,0:T(8,128)(2,1)S(1)}, bf16[1,16,1792]{2,1,0:T(8,128)(2,1)S(1)}, u32[]{:S(2)}, u32[]{:S(2)}) collective-permute-start(bf16[1,16,1792]{2,1,0:T(8,128)(2,1)S(1)} %fusion.11), channel_id=1, source_target_pairs={{0,8},{1,9},{2,10},{3,11},{4,12},{5,13},{6,14},{7,15},{8,0},{9,1},... | collective-permute-start | bytes 172040 | tf_op jit(solution)/shard_map/ppermute | solution.py:28
  56.9 1.6 collective-permute-start.13
  59.7 1.4 collective-permute-done.13
  61.5 1.0 collective-permute-start.16
  62.5 2.0 %collective-permute-start.17 = (bf16[16,1792]{1,0:T(8,128)(2,1)S(1)}, bf16[16,1792]{1,0:T(8,128)(2,1)S(1)}, u32[]{:S(2)}, u32[]{:S(2)}) collective-permute-start(bf16[16,1792]{1,0:T(8,128)(2,1)S(1)} %get-tuple-element.191), channel_id=1, source_target_pairs={{0,2},{1,3},{2,0},{3,1},{4,6},{5,7},{6,4},{7,5},{8,10},{9,11},{10,... | collective-permute-start | bytes 172040 | tf_op jit(solution)/shard_map/ppermute | solution.py:28
  65.1 3.0 %collective-permute-done.16 = bf16[16,1792]{1,0:T(8,128)(2,1)S(1)} collective-permute-done((bf16[16,1792]{1,0:T(8,128)(2,1)S(1)}, bf16[16,1792]{1,0:T(8,128)(2,1)S(1)}, u32[]{:S(2)}, u32[]{:S(2)}) %collective-permute-start.16) | collective-permute-done | bytes 57376 | tf_op jit(solution)/shard_map/ppermute | solution.py:28
  68.3 1.9 %collective-permute-start.21 = (bf16[32,1792]{1,0:T(8,128)(2,1)S(1)}, bf16[32,1792]{1,0:T(8,128)(2,1)S(1)}, u32[]{:S(2)}, u32[]{:S(2)}) collective-permute-start(bf16[32,1792]{1,0:T(8,128)(2,1)S(1)} %pad_maximum_fusion.3), channel_id=1, source_target_pairs={{0,8},{1,9},{2,10},{3,11},{4,12},{5,13},{6,14},{7,15},{8,0},{9,1},... | collective-permute-start | bytes 344072 | tf_op jit(solution)/shard_map/ppermute | solution.py:28
  70.4 1.3 collective-permute-start.23
  71.7 2.7 %collective-permute-start.26 = (bf16[384,128]{1,0:T(8,128)(2,1)S(1)}, bf16[384,128]{1,0:T(8,128)(2,1)S(1)}, u32[]{:S(2)}, u32[]{:S(2)}) collective-permute-start(bf16[384,128]{1,0:T(8,128)(2,1)S(1)} %get-tuple-element.207), channel_id=1, source_target_pairs={{0,6},{1,7},{2,4},{3,5},{4,2},{5,3},{6,0},{7,1},{8,14},{9,15},{10,... | collective-permute-start | bytes 294920 | tf_op jit(solution)/shard_map/ppermute | solution.py:28
  74.4 2.1 %collective-permute-done.22.refs_5_ = bf16[384,128]{1,0:T(8,128)(2,1)S(1)} collective-permute-done((bf16[384,128]{1,0:T(8,128)(2,1)S(1)}, bf16[384,128]{1,0:T(8,128)(2,1)S(1)}, u32[]{:S(2)}, u32[]{:S(2)}) %collective-permute-start.22) | collective-permute-done | bytes 98336 | tf_op jit(solution)/shard_map/ppermute | solution.py:28
  76.6 1.7 %collective-permute-start.27 = (bf16[384,128]{1,0:T(8,128)(2,1)S(1)}, bf16[384,128]{1,0:T(8,128)(2,1)S(1)}, u32[]{:S(2)}, u32[]{:S(2)}) collective-permute-start(bf16[384,128]{1,0:T(8,128)(2,1)S(1)} %get-tuple-element.208), channel_id=1, source_target_pairs={{0,7},{1,6},{2,5},{3,4},{4,3},{5,2},{6,1},{7,0},{8,15},{9,14},{10,... | collective-permute-start | bytes 294920 | tf_op jit(solution)/shard_map/ppermute | solution.py:28
  78.2 1.7 %collective-permute-done.23.refs_10_.refs_2_ = bf16[384,128]{1,0:T(8,128)(2,1)S(1)} collective-permute-done((bf16[384,128]{1,0:T(8,128)(2,1)S(1)}, bf16[384,128]{1,0:T(8,128)(2,1)S(1)}, u32[]{:S(2)}, u32[]{:S(2)}) %collective-permute-start.23) | collective-permute-done | bytes 98336 | tf_op jit(solution)/shard_map/ppermute | solution.py:28
  80.0 2.5 %collective-permute-start.24 = (bf16[64,1792]{1,0:T(8,128)(2,1)S(1)}, bf16[64,1792]{1,0:T(8,128)(2,1)S(1)}, u32[]{:S(2)}, u32[]{:S(2)}) collective-permute-start(bf16[64,1792]{1,0:T(8,128)(2,1)S(1)} %pad_maximum_fusion.refs_0_), channel_id=1, source_target_pairs={{0,2},{1,3},{2,0},{3,1},{4,6},{5,7},{6,4},{7,5},{8,10},{9,11},{10,... | collective-permute-start | bytes 688136 | tf_op jit(solution)/shard_map/ppermute | solution.py:28
  82.5 1.4 collective-permute-start.25
  84.1 5.3 %collective-permute-done.24.refs_1_ = bf16[64,1792]{1,0:T(8,128)(2,1)S(1)} collective-permute-done((bf16[64,1792]{1,0:T(8,128)(2,1)S(1)}, bf16[64,1792]{1,0:T(8,128)(2,1)S(1)}, u32[]{:S(2)}, u32[]{:S(2)}) %collective-permute-start.24) | collective-permute-done | bytes 229408 | tf_op jit(solution)/shard_map/ppermute | solution.py:28
  89.4 2.3 %project.1 = (bf16[4,144,256]{2,1,0:T(8,128)(2,1)S(1)}, bf16[4,144,256]{2,1,0:T(8,128)(2,1)S(1)}, bf16[4,144,256]{2,1,0:T(8,128)(2,1)S(1)}, bf16[4,144,256]{2,1,0:T(8,128)(2,1)S(1)}) custom-call(s32[5]{0:T(128)S(1)} %stack.19.place_ref, bf16[64,1792]{1,0:T(8,128)(2,1)S(1)} %pad_maximum_fusion.refs_0_, bf16[64,1792]{1,0:T(8,128)(2,1)S(1)} %collective-permute-done.24.refs_1_, ...), custom_call_target="tpu_custom_call" | custom-call | flops 754974720 | bytes 7864320 | tf_op jit(solution)/shard_map/project/pallas_call | solution.py:200
  91.7 1.8 %collective-permute-start.29 = (bf16[4,144,256]{2,1,0:T(8,128)(2,1)S(1)}, bf16[4,144,256]{2,1,0:T(8,128)(2,1)S(1)}, u32[]{:S(2)}, u32[]{:S(2)}) collective-permute-start(bf16[4,144,256]{2,1,0:T(8,128)(2,1)S(1)} %get-tuple-element.218), channel_id=1, source_target_pairs={{0,2},{1,3},{2,0},{3,1},{4,6},{5,7},{6,4},{7,5},{8,10},{9,11},{10,... | collective-permute-start | bytes 884744 | tf_op jit(solution)/shard_map/ppermute | solution.py:28
  93.5 1.9 %collective-permute-start.31 = (bf16[384,128]{1,0:T(8,128)(2,1)S(1)}, bf16[384,128]{1,0:T(8,128)(2,1)S(1)}, u32[]{:S(2)}, u32[]{:S(2)}) collective-permute-start(bf16[384,128]{1,0:T(8,128)(2,1)S(1)} %get-tuple-element.220), channel_id=1, source_target_pairs={{0,14},{1,15},{2,12},{3,13},{4,10},{5,11},{6,8},{7,9},{8,6},{9,7},... | collective-permute-start | bytes 294920 | tf_op jit(solution)/shard_map/ppermute | solution.py:28
  95.6 3.1 %collective-permute-start.33 = (bf16[384,128]{1,0:T(8,128)(2,1)S(1)}, bf16[384,128]{1,0:T(8,128)(2,1)S(1)}, u32[]{:S(2)}, u32[]{:S(2)}) collective-permute-start(bf16[384,128]{1,0:T(8,128)(2,1)S(1)} %get-tuple-element.224), channel_id=1, source_target_pairs={{0,15},{1,14},{2,13},{3,12},{4,11},{5,10},{6,9},{7,8},{8,7},{9,6},... | collective-permute-start | bytes 294920 | tf_op jit(solution)/shard_map/ppermute | solution.py:28
  98.7 6.9 %collective-permute-done.31.refs_14_.refs_6_ = bf16[384,128]{1,0:T(8,128)(2,1)S(1)} collective-permute-done((bf16[384,128]{1,0:T(8,128)(2,1)S(1)}, bf16[384,128]{1,0:T(8,128)(2,1)S(1)}, u32[]{:S(2)}, u32[]{:S(2)}) %collective-permute-start.31) | collective-permute-done | bytes 98336 | tf_op jit(solution)/shard_map/ppermute | solution.py:28
  105.9 2.2 %collective-permute-done.32.refs_11_.refs_3_ = bf16[384,128]{1,0:T(8,128)(2,1)S(1)} collective-permute-done((bf16[384,128]{1,0:T(8,128)(2,1)S(1)}, bf16[384,128]{1,0:T(8,128)(2,1)S(1)}, u32[]{:S(2)}, u32[]{:S(2)}) %collective-permute-start.32) | collective-permute-done | bytes 98336 | tf_op jit(solution)/shard_map/ppermute | solution.py:28
  108.1 3.0 %collective-permute-start.35 = (bf16[2,144,256]{2,1,0:T(8,128)(2,1)S(1)}, bf16[2,144,256]{2,1,0:T(8,128)(2,1)S(1)}, u32[]{:S(2)}, u32[]{:S(2)}) collective-permute-start(bf16[2,144,256]{2,1,0:T(8,128)(2,1)S(1)} %get-tuple-element.319), channel_id=1, source_target_pairs={{0,8},{1,9},{2,10},{3,11},{4,12},{5,13},{6,14},{7,15},{8,0},{9,1},... | collective-permute-start | bytes 442376 | tf_op jit(solution)/shard_map/ppermute | solution.py:28
  111.3 3.7 %image_attention.2 = (f32[1024,128]{1,0:T(8,128)S(1)}, f32[1024,128]{1,0:T(8,128)S(1)}) custom-call(bf16[384,128]{1,0:T(8,128)(2,1)S(1)} %get-tuple-element.264.refs_0_, bf16[384,128]{1,0:T(8,128)(2,1)S(1)} %collective-permute-done.18.refs_1_, bf16[384,128]{1,0:T(8,128)(2,1)S(1)} %collective-permute-done.1.refs_2_, ...), custom_call_target="tpu_custom_call" | custom-call | flops 1073741824 | bytes 2359296 | tf_op jit(solution)/shard_map/image_attention/pallas_call | solution.py:363
  115.0 3.8 %collective-permute-done.35 = bf16[2,144,256]{2,1,0:T(8,128)(2,1)S(1)} collective-permute-done((bf16[2,144,256]{2,1,0:T(8,128)(2,1)S(1)}, bf16[2,144,256]{2,1,0:T(8,128)(2,1)S(1)}, u32[]{:S(2)}, u32[]{:S(2)}) %collective-permute-start.35) | collective-permute-done | bytes 147488 | tf_op jit(solution)/shard_map/ppermute | solution.py:28
  119.4 2.8 %collective-permute-start.36 = (bf16[1,144,256]{2,1,0:T(8,128)(2,1)S(1)}, bf16[1,144,256]{2,1,0:T(8,128)(2,1)S(1)}, u32[]{:S(2)}, u32[]{:S(2)}) collective-permute-start(bf16[1,144,256]{2,1,0:T(8,128)(2,1)S(1)} %get-tuple-element.325), channel_id=1, source_target_pairs={{0,8},{1,9},{2,10},{3,11},{4,12},{5,13},{6,14},{7,15},{8,0},{9,1},... | collective-permute-start | bytes 221192 | tf_op jit(solution)/shard_map/ppermute | solution.py:28
  122.1 3.7 %image_attention.3 = (f32[1024,128]{1,0:T(8,128)S(1)}, f32[1024,128]{1,0:T(8,128)S(1)}) custom-call(bf16[384,128]{1,0:T(8,128)(2,1)S(1)} %get-tuple-element.264.refs_0_, bf16[384,128]{1,0:T(8,128)(2,1)S(1)} %collective-permute-done.18.refs_1_, bf16[384,128]{1,0:T(8,128)(2,1)S(1)} %collective-permute-done.1.refs_2_, ...), custom_call_target="tpu_custom_call" | custom-call | flops 1073741824 | bytes 2359296 | tf_op jit(solution)/shard_map/image_attention/pallas_call | solution.py:363
  125.8 1.0 combine.1
  126.9 1.2 collective-permute-done.38.refs_11_
  128.1 2.7 %finish.3 = (bf16[160,128]{1,0:T(8,128)(2,1)S(1)}, bf16[160,128]{1,0:T(8,128)(2,1)S(1)}, bf16[160,128]{1,0:T(8,128)(2,1)S(1)}, bf16[160,128]{1,0:T(8,128)(2,1)S(...) custom-call(s32[5]{0:T(128)S(1)} %stack.19.place_ref, ...), custom_call_target="tpu_custom_call" | custom-call | flops 134217728 | bytes 1572864 | tf_op jit(solution)/shard_map/finish/pallas_call | solution.py:427
  130.8 1.7 %collective-permute-start.46 = (bf16[160,128]{1,0:T(8,128)(2,1)S(1)}, bf16[160,128]{1,0:T(8,128)(2,1)S(1)}, u32[]{:S(2)}, u32[]{:S(2)}) collective-permute-start(bf16[160,128]{1,0:T(8,128)(2,1)S(1)} %get-tuple-element.298), channel_id=1, source_target_pairs={{0,8},{1,9},{2,10},{3,11},{4,12},{5,13},{6,14},{7,15},{8,0},{9,1},... | collective-permute-start | bytes 122888 | tf_op jit(solution)/shard_map/ppermute | solution.py:28
  132.5 0.8 collective-permute-start.47
  133.3 2.4 %collective-permute-start.48 = (bf16[160,128]{1,0:T(8,128)(2,1)S(1)}, bf16[160,128]{1,0:T(8,128)(2,1)S(1)}, u32[]{:S(2)}, u32[]{:S(2)}) collective-permute-start(bf16[160,128]{1,0:T(8,128)(2,1)S(1)} %get-tuple-element.300), channel_id=1, source_target_pairs={{0,10},{1,11},{2,8},{3,9},{4,14},{5,15},{6,12},{7,13},{8,2},{9,3},... | collective-permute-start | bytes 122888 | tf_op jit(solution)/shard_map/ppermute | solution.py:28
  135.7 1.3 collective-permute-start.49
  137.1 2.9 %collective-permute-start.50 = (bf16[160,128]{1,0:T(8,128)(2,1)S(1)}, bf16[160,128]{1,0:T(8,128)(2,1)S(1)}, u32[]{:S(2)}, u32[]{:S(2)}) collective-permute-start(bf16[160,128]{1,0:T(8,128)(2,1)S(1)} %get-tuple-element.302), channel_id=1, source_target_pairs={{0,12},{1,13},{2,14},{3,15},{4,8},{5,9},{6,10},{7,11},{8,4},{9,5},... | collective-permute-start | bytes 122888 | tf_op jit(solution)/shard_map/ppermute | solution.py:28
  140.0 2.7 %finish.2 = (bf16[160,128]{1,0:T(8,128)(2,1)S(1)}, bf16[160,128]{1,0:T(8,128)(2,1)S(1)}, bf16[160,128]{1,0:T(8,128)(2,1)S(1)}, bf16[160,128]{1,0:T(8,128)(2,1)S(...) custom-call(s32[5]{0:T(128)S(1)} %stack.19.place_ref, ...), custom_call_target="tpu_custom_call" | custom-call | flops 134217728 | bytes 1572864 | tf_op jit(solution)/shard_map/finish/pallas_call | solution.py:427
  143.2 3.9 %collective-permute-start.52 = (bf16[160,128]{1,0:T(8,128)(2,1)S(1)}, bf16[160,128]{1,0:T(8,128)(2,1)S(1)}, u32[]{:S(2)}, u32[]{:S(2)}) collective-permute-start(bf16[160,128]{1,0:T(8,128)(2,1)S(1)} %get-tuple-element.304), channel_id=1, source_target_pairs={{0,14},{1,15},{2,12},{3,13},{4,10},{5,11},{6,8},{7,9},{8,6},{9,7},... | collective-permute-start | bytes 122888 | tf_op jit(solution)/shard_map/ppermute | solution.py:28
  147.0 0.8 collective-permute-start.53
  148.0 1.6 collective-permute-start.40
  150.4 2.9 %collective-permute-done.53.refs_15_ = bf16[160,128]{1,0:T(8,128)(2,1)S(1)} collective-permute-done((bf16[160,128]{1,0:T(8,128)(2,1)S(1)}, bf16[160,128]{1,0:T(8,128)(2,1)S(1)}, u32[]{:S(2)}, u32[]{:S(2)}) %collective-permute-start.53) | collective-permute-done | bytes 40992 | tf_op jit(solution)/shard_map/ppermute | solution.py:28
  153.3 1.9 %collective-permute-start.44 = (bf16[160,128]{1,0:T(8,128)(2,1)S(1)}, bf16[160,128]{1,0:T(8,128)(2,1)S(1)}, u32[]{:S(2)}, u32[]{:S(2)}) collective-permute-start(bf16[160,128]{1,0:T(8,128)(2,1)S(1)} %get-tuple-element.294), channel_id=1, source_target_pairs={{0,6},{1,7},{2,4},{3,5},{4,2},{5,3},{6,0},{7,1},{8,14},{9,15},{10,... | collective-permute-start | bytes 122888 | tf_op jit(solution)/shard_map/ppermute | solution.py:28
  155.2 0.7 collective-permute-start.45
  155.8 0.9 collective-permute-done.43.refs_5_
  156.7 1.5 collective-permute-done.44.refs_6_
  158.2 1.7 %collective-permute-done.45.refs_7_ = bf16[160,128]{1,0:T(8,128)(2,1)S(1)} collective-permute-done((bf16[160,128]{1,0:T(8,128)(2,1)S(1)}, bf16[160,128]{1,0:T(8,128)(2,1)S(1)}, u32[]{:S(2)}, u32[]{:S(2)}) %collective-permute-start.45) | collective-permute-done | bytes 40992 | tf_op jit(solution)/shard_map/ppermute | solution.py:28
  159.8 1.5 unpack.1
  (97 shorter events, 7.4 us)
Async XLA Ops:
  0.6 83.3 %copy-start = (bf16[256,2,192]{0,2,1:T(8,128)(2,1)S(1)}, bf16[256,2,192]{0,2,1:T(8,128)(2,1)}, u32[]{:S(2)}) copy-start(bf16[256,2,192]{0,2,1:T(8,128)(2,1)} %param.14) | copy-start | bytes 589828
  5.9 4.4 %copy-start.5 = (bf16[1,256,1184]{1,2,0:T(8,128)(2,1)S(1)}, bf16[1,256,1184]{1,2,0:T(8,128)(2,1)}, u32[]{:S(2)}) copy-start(bf16[1,256,1184]{1,2,0:T(8,128)(2,1)} %param.10) | copy-start | bytes 1818628
  5.9 14.2 %copy-start.4 = (bf16[3584,192]{0,1:T(8,128)(2,1)S(1)}, bf16[3584,192]{0,1:T(8,128)(2,1)}, u32[]{:S(2)}) copy-start(bf16[3584,192]{0,1:T(8,128)(2,1)} %param.13) | copy-start | bytes 4128772
  8.2 1.0 copy-start.6
  9.3 7.8 %copy-start.3 = (bf16[192,4096]{1,0:T(8,128)(2,1)S(1)}, bf16[192,4096]{1,0:T(8,128)(2,1)}, u32[]{:S(2)}) copy-start(bf16[192,4096]{1,0:T(8,128)(2,1)} %refs_6_.1) | copy-start | bytes 4718596
  10.3 3.5 %copy-start.1 = (bf16[1184,3584]{1,0:T(8,128)(2,1)S(1)}, bf16[1184,3584]{1,0:T(8,128)(2,1)}, u32[]{:S(2)}) copy-start(bf16[1184,3584]{1,0:T(8,128)(2,1)} %weight_ref.3) | copy-start | bytes 25460740
  13.8 11.0 %copy-start.2 = (bf16[1184,3584]{1,0:T(8,128)(2,1)S(1)}, bf16[1184,3584]{1,0:T(8,128)(2,1)}, u32[]{:S(2)}) copy-start(bf16[1184,3584]{1,0:T(8,128)(2,1)} %weight_ref.3) | copy-start | bytes 25460740
  16.6 15.8 %collective-permute-start = (bf16[8,16,1792]{2,1,0:T(8,128)(2,1)S(1)}, bf16[8,16,1792]{2,1,0:T(8,128)(2,1)S(1)}, u32[]{:S(2)}, u32[]{:S(2)}) collective-permute-start(bf16[8,16,1792]{2,1,0:T(8,128)(2,1)S(1)} %get-tuple-element.160), channel_id=1, source_target_pairs={{0,1},{1,0},{2,3},{3,2},{4,5},{5,4},{6,7},{7,6},{8,9},{9,8},{10,11... | collective-permute-start | bytes 1376264 | tf_op jit(solution)/shard_map/ppermute | solution.py:28
  17.1 25.1 %collective-permute-start.8 = (bf16[192,4096]{1,0:T(8,128)(2,1)S(1)}, bf16[192,4096]{1,0:T(8,128)(2,1)S(1)}, u32[]{:S(2)}, u32[]{:S(2)}) collective-permute-start(bf16[192,4096]{1,0:T(8,128)(2,1)S(1)} %copy-done.3), channel_id=1, source_target_pairs={{0,1},{1,0},{2,3},{3,2},{4,5},{5,4},{6,7},{7,6},{8,9},{9,8},{10,11... | collective-permute-start | bytes 4718600 | tf_op jit(solution)/shard_map/ppermute | solution.py:28
  17.2 6.0 %collective-permute-start.1 = (bf16[384,128]{1,0:T(8,128)(2,1)S(1)}, bf16[384,128]{1,0:T(8,128)(2,1)S(1)}, u32[]{:S(2)}, u32[]{:S(2)}) collective-permute-start(bf16[384,128]{1,0:T(8,128)(2,1)S(1)} %get-tuple-element.164), channel_id=1, source_target_pairs={{0,2},{1,3},{2,0},{3,1},{4,6},{5,7},{6,4},{7,5},{8,10},{9,11},{10,... | collective-permute-start | bytes 294920 | tf_op jit(solution)/shard_map/ppermute | solution.py:28
  20.1 22.1 %collective-permute-start.7 = (bf16[192,3584]{1,0:T(8,128)(2,1)S(1)}, bf16[192,3584]{1,0:T(8,128)(2,1)S(1)}, u32[]{:S(2)}, u32[]{:S(2)}) collective-permute-start(bf16[192,3584]{1,0:T(8,128)(2,1)S(1)} %bitcast.44), channel_id=1, source_target_pairs={{0,1},{1,0},{2,3},{3,2},{4,5},{5,4},{6,7},{7,6},{8,9},{9,8},{10,11... | collective-permute-start | bytes 4128776 | tf_op jit(solution)/shard_map/ppermute | solution.py:28
  20.1 10.7 %collective-permute-start.2 = (bf16[384,128]{1,0:T(8,128)(2,1)S(1)}, bf16[384,128]{1,0:T(8,128)(2,1)S(1)}, u32[]{:S(2)}, u32[]{:S(2)}) collective-permute-start(bf16[384,128]{1,0:T(8,128)(2,1)S(1)} %get-tuple-element.165), channel_id=1, source_target_pairs={{0,8},{1,9},{2,10},{3,11},{4,12},{5,13},{6,14},{7,15},{8,0},{9,1},... | collective-permute-start | bytes 294920 | tf_op jit(solution)/shard_map/ppermute | solution.py:28
  23.1 9.0 %collective-permute-start.3 = (bf16[384,128]{1,0:T(8,128)(2,1)S(1)}, bf16[384,128]{1,0:T(8,128)(2,1)S(1)}, u32[]{:S(2)}, u32[]{:S(2)}) collective-permute-start(bf16[384,128]{1,0:T(8,128)(2,1)S(1)} %get-tuple-element.166), channel_id=1, source_target_pairs={{0,9},{1,8},{2,11},{3,10},{4,13},{5,12},{6,15},{7,14},{8,1},{9,0},... | collective-permute-start | bytes 294920 | tf_op jit(solution)/shard_map/ppermute | solution.py:28
  32.1 1.8 %collective-permute-start.4 = (bf16[8,16,1792]{2,1,0:T(8,128)(2,1)S(1)}, bf16[8,16,1792]{2,1,0:T(8,128)(2,1)S(1)}, u32[]{:S(2)}, u32[]{:S(2)}) collective-permute-start(bf16[8,16,1792]{2,1,0:T(8,128)(2,1)S(1)} %get-tuple-element.167), channel_id=1, source_target_pairs={{0,1},{1,0},{2,3},{3,2},{4,5},{5,4},{6,7},{7,6},{8,9},{9,8},{10,11... | collective-permute-start | bytes 1376264 | tf_op jit(solution)/shard_map/ppermute | solution.py:28
  34.0 24.5 %copy-start.7 = (bf16[3584]{0:T(1024)(128)(2,1)S(1)}, bf16[3584]{0:T(1024)(128)(2,1)}, u32[]{:S(2)}) copy-start(bf16[3584]{0:T(1024)(128)(2,1)} %param.12) | copy-start | bytes 21508
  34.0 7.8 %collective-permute-start.5 = (bf16[4,16,1792]{2,1,0:T(8,128)(2,1)S(1)}, bf16[4,16,1792]{2,1,0:T(8,128)(2,1)S(1)}, u32[]{:S(2)}, u32[]{:S(2)}) collective-permute-start(bf16[4,16,1792]{2,1,0:T(8,128)(2,1)S(1)} %get-tuple-element.169), channel_id=1, source_target_pairs={{0,2},{1,3},{2,0},{3,1},{4,6},{5,7},{6,4},{7,5},{8,10},{9,11},{10,... | collective-permute-start | bytes 688136 | tf_op jit(solution)/shard_map/ppermute | solution.py:28
  34.8 7.4 %collective-permute-start.6 = (bf16[4,16,1792]{2,1,0:T(8,128)(2,1)S(1)}, bf16[4,16,1792]{2,1,0:T(8,128)(2,1)S(1)}, u32[]{:S(2)}, u32[]{:S(2)}) collective-permute-start(bf16[4,16,1792]{2,1,0:T(8,128)(2,1)S(1)} %get-tuple-element.170), channel_id=1, source_target_pairs={{0,4},{1,5},{2,6},{3,7},{4,0},{5,1},{6,2},{7,3},{8,12},{9,13},{10,... | collective-permute-start | bytes 688136 | tf_op jit(solution)/shard_map/ppermute | solution.py:28
  42.2 10.9 %collective-permute-start.10 = (bf16[2,16,1792]{2,1,0:T(8,128)(2,1)S(1)}, bf16[2,16,1792]{2,1,0:T(8,128)(2,1)S(1)}, u32[]{:S(2)}, u32[]{:S(2)}) collective-permute-start(bf16[2,16,1792]{2,1,0:T(8,128)(2,1)S(1)} %get-tuple-element.176), channel_id=1, source_target_pairs={{0,8},{1,9},{2,10},{3,11},{4,12},{5,13},{6,14},{7,15},{8,0},{9,1},... | collective-permute-start | bytes 344072 | tf_op jit(solution)/shard_map/ppermute | solution.py:28
  44.8 8.3 %collective-permute-start.9 = (bf16[2,16,1792]{2,1,0:T(8,128)(2,1)S(1)}, bf16[2,16,1792]{2,1,0:T(8,128)(2,1)S(1)}, u32[]{:S(2)}, u32[]{:S(2)}) collective-permute-start(bf16[2,16,1792]{2,1,0:T(8,128)(2,1)S(1)} %get-tuple-element.175), channel_id=1, source_target_pairs={{0,4},{1,5},{2,6},{3,7},{4,0},{5,1},{6,2},{7,3},{8,12},{9,13},{10,... | collective-permute-start | bytes 344072 | tf_op jit(solution)/shard_map/ppermute | solution.py:28
  46.6 6.5 %collective-permute-start.11 = (bf16[384,128]{1,0:T(8,128)(2,1)S(1)}, bf16[384,128]{1,0:T(8,128)(2,1)S(1)}, u32[]{:S(2)}, u32[]{:S(2)}) collective-permute-start(bf16[384,128]{1,0:T(8,128)(2,1)S(1)} %get-tuple-element.177), channel_id=1, source_target_pairs={{0,12},{1,13},{2,14},{3,15},{4,8},{5,9},{6,10},{7,11},{8,4},{9,5},... | collective-permute-start | bytes 294920 | tf_op jit(solution)/shard_map/ppermute | solution.py:28
  46.7 11.9 %collective-permute-start.14 = (bf16[384,128]{1,0:T(8,128)(2,1)S(1)}, bf16[384,128]{1,0:T(8,128)(2,1)S(1)}, u32[]{:S(2)}, u32[]{:S(2)}) collective-permute-start(bf16[384,128]{1,0:T(8,128)(2,1)S(1)} %get-tuple-element.184), channel_id=1, source_target_pairs={{0,3},{1,2},{2,1},{3,0},{4,7},{5,6},{6,5},{7,4},{8,11},{9,10},{10,... | collective-permute-start | bytes 294920 | tf_op jit(solution)/shard_map/ppermute | solution.py:28
  46.7 12.4 %collective-permute-start.15 = (bf16[384,128]{1,0:T(8,128)(2,1)S(1)}, bf16[384,128]{1,0:T(8,128)(2,1)S(1)}, u32[]{:S(2)}, u32[]{:S(2)}) collective-permute-start(bf16[384,128]{1,0:T(8,128)(2,1)S(1)} %get-tuple-element.185), channel_id=1, source_target_pairs={{0,4},{1,5},{2,6},{3,7},{4,0},{5,1},{6,2},{7,3},{8,12},{9,13},{10,... | collective-permute-start | bytes 294920 | tf_op jit(solution)/shard_map/ppermute | solution.py:28
  53.2 6.5 %collective-permute-start.12 = (bf16[1,16,1792]{2,1,0:T(8,128)(2,1)S(1)}, bf16[1,16,1792]{2,1,0:T(8,128)(2,1)S(1)}, u32[]{:S(2)}, u32[]{:S(2)}) collective-permute-start(bf16[1,16,1792]{2,1,0:T(8,128)(2,1)S(1)} %fusion.11), channel_id=1, source_target_pairs={{0,8},{1,9},{2,10},{3,11},{4,12},{5,13},{6,14},{7,15},{8,0},{9,1},... | collective-permute-start | bytes 172040 | tf_op jit(solution)/shard_map/ppermute | solution.py:28
  56.9 4.2 %collective-permute-start.13 = (bf16[1,16,1792]{2,1,0:T(8,128)(2,1)S(1)}, bf16[1,16,1792]{2,1,0:T(8,128)(2,1)S(1)}, u32[]{:S(2)}, u32[]{:S(2)}) collective-permute-start(bf16[1,16,1792]{2,1,0:T(8,128)(2,1)S(1)} %fusion.10), channel_id=1, source_target_pairs={{0,2},{1,3},{2,0},{3,1},{4,6},{5,7},{6,4},{7,5},{8,10},{9,11},{10,... | collective-permute-start | bytes 172040 | tf_op jit(solution)/shard_map/ppermute | solution.py:28
  58.6 6.6 %collective-permute-start.18 = (bf16[384,128]{1,0:T(8,128)(2,1)S(1)}, bf16[384,128]{1,0:T(8,128)(2,1)S(1)}, u32[]{:S(2)}, u32[]{:S(2)}) collective-permute-start(bf16[384,128]{1,0:T(8,128)(2,1)S(1)} %get-tuple-element.192), channel_id=1, source_target_pairs={{0,1},{1,0},{2,3},{3,2},{4,5},{5,4},{6,7},{7,6},{8,9},{9,8},{10,11... | collective-permute-start | bytes 294920 | tf_op jit(solution)/shard_map/ppermute | solution.py:28
  58.6 6.6 %collective-permute-start.19 = (bf16[384,128]{1,0:T(8,128)(2,1)S(1)}, bf16[384,128]{1,0:T(8,128)(2,1)S(1)}, u32[]{:S(2)}, u32[]{:S(2)}) collective-permute-start(bf16[384,128]{1,0:T(8,128)(2,1)S(1)} %get-tuple-element.193), channel_id=1, source_target_pairs={{0,13},{1,12},{2,15},{3,14},{4,9},{5,8},{6,11},{7,10},{8,5},{9,4},... | collective-permute-start | bytes 294920 | tf_op jit(solution)/shard_map/ppermute | solution.py:28
  61.5 6.7 %collective-permute-start.16 = (bf16[16,1792]{1,0:T(8,128)(2,1)S(1)}, bf16[16,1792]{1,0:T(8,128)(2,1)S(1)}, u32[]{:S(2)}, u32[]{:S(2)}) collective-permute-start(bf16[16,1792]{1,0:T(8,128)(2,1)S(1)} %get-tuple-element.190), channel_id=1, source_target_pairs={{0,8},{1,9},{2,10},{3,11},{4,12},{5,13},{6,14},{7,15},{8,0},{9,1},... | collective-permute-start | bytes 172040 | tf_op jit(solution)/shard_map/ppermute | solution.py:28
  62.5 5.7 %collective-permute-start.17 = (bf16[16,1792]{1,0:T(8,128)(2,1)S(1)}, bf16[16,1792]{1,0:T(8,128)(2,1)S(1)}, u32[]{:S(2)}, u32[]{:S(2)}) collective-permute-start(bf16[16,1792]{1,0:T(8,128)(2,1)S(1)} %get-tuple-element.191), channel_id=1, source_target_pairs={{0,2},{1,3},{2,0},{3,1},{4,6},{5,7},{6,4},{7,5},{8,10},{9,11},{10,... | collective-permute-start | bytes 172040 | tf_op jit(solution)/shard_map/ppermute | solution.py:28
  68.2 11.7 %collective-permute-start.20 = (bf16[32,1792]{1,0:T(8,128)(2,1)S(1)}, bf16[32,1792]{1,0:T(8,128)(2,1)S(1)}, u32[]{:S(2)}, u32[]{:S(2)}) collective-permute-start(bf16[32,1792]{1,0:T(8,128)(2,1)S(1)} %pad_maximum_fusion.2), channel_id=1, source_target_pairs={{0,4},{1,5},{2,6},{3,7},{4,0},{5,1},{6,2},{7,3},{8,12},{9,13},{10,... | collective-permute-start | bytes 344072 | tf_op jit(solution)/shard_map/ppermute | solution.py:28
  68.3 11.6 %collective-permute-start.21 = (bf16[32,1792]{1,0:T(8,128)(2,1)S(1)}, bf16[32,1792]{1,0:T(8,128)(2,1)S(1)}, u32[]{:S(2)}, u32[]{:S(2)}) collective-permute-start(bf16[32,1792]{1,0:T(8,128)(2,1)S(1)} %pad_maximum_fusion.3), channel_id=1, source_target_pairs={{0,8},{1,9},{2,10},{3,11},{4,12},{5,13},{6,14},{7,15},{8,0},{9,1},... | collective-permute-start | bytes 344072 | tf_op jit(solution)/shard_map/ppermute | solution.py:28
  70.3 6.3 %collective-permute-start.22 = (bf16[384,128]{1,0:T(8,128)(2,1)S(1)}, bf16[384,128]{1,0:T(8,128)(2,1)S(1)}, u32[]{:S(2)}, u32[]{:S(2)}) collective-permute-start(bf16[384,128]{1,0:T(8,128)(2,1)S(1)} %get-tuple-element.200), channel_id=1, source_target_pairs={{0,5},{1,4},{2,7},{3,6},{4,1},{5,0},{6,3},{7,2},{8,13},{9,12},{10,... | collective-permute-start | bytes 294920 | tf_op jit(solution)/shard_map/ppermute | solution.py:28
  70.4 9.5 %collective-permute-start.23 = (bf16[384,128]{1,0:T(8,128)(2,1)S(1)}, bf16[384,128]{1,0:T(8,128)(2,1)S(1)}, u32[]{:S(2)}, u32[]{:S(2)}) collective-permute-start(bf16[384,128]{1,0:T(8,128)(2,1)S(1)} %get-tuple-element.201), channel_id=1, source_target_pairs={{0,10},{1,11},{2,8},{3,9},{4,14},{5,15},{6,12},{7,13},{8,2},{9,3},... | collective-permute-start | bytes 294920 | tf_op jit(solution)/shard_map/ppermute | solution.py:28
  71.7 12.4 %collective-permute-start.26 = (bf16[384,128]{1,0:T(8,128)(2,1)S(1)}, bf16[384,128]{1,0:T(8,128)(2,1)S(1)}, u32[]{:S(2)}, u32[]{:S(2)}) collective-permute-start(bf16[384,128]{1,0:T(8,128)(2,1)S(1)} %get-tuple-element.207), channel_id=1, source_target_pairs={{0,6},{1,7},{2,4},{3,5},{4,2},{5,3},{6,0},{7,1},{8,14},{9,15},{10,... | collective-permute-start | bytes 294920 | tf_op jit(solution)/shard_map/ppermute | solution.py:28
  76.6 7.5 %collective-permute-start.27 = (bf16[384,128]{1,0:T(8,128)(2,1)S(1)}, bf16[384,128]{1,0:T(8,128)(2,1)S(1)}, u32[]{:S(2)}, u32[]{:S(2)}) collective-permute-start(bf16[384,128]{1,0:T(8,128)(2,1)S(1)} %get-tuple-element.208), channel_id=1, source_target_pairs={{0,7},{1,6},{2,5},{3,4},{4,3},{5,2},{6,1},{7,0},{8,15},{9,14},{10,... | collective-permute-start | bytes 294920 | tf_op jit(solution)/shard_map/ppermute | solution.py:28
  80.0 9.4 %collective-permute-start.24 = (bf16[64,1792]{1,0:T(8,128)(2,1)S(1)}, bf16[64,1792]{1,0:T(8,128)(2,1)S(1)}, u32[]{:S(2)}, u32[]{:S(2)}) collective-permute-start(bf16[64,1792]{1,0:T(8,128)(2,1)S(1)} %pad_maximum_fusion.refs_0_), channel_id=1, source_target_pairs={{0,2},{1,3},{2,0},{3,1},{4,6},{5,7},{6,4},{7,5},{8,10},{9,11},{10,... | collective-permute-start | bytes 688136 | tf_op jit(solution)/shard_map/ppermute | solution.py:28
  82.5 6.9 %collective-permute-start.25 = (bf16[64,1792]{1,0:T(8,128)(2,1)S(1)}, bf16[64,1792]{1,0:T(8,128)(2,1)S(1)}, u32[]{:S(2)}, u32[]{:S(2)}) collective-permute-start(bf16[64,1792]{1,0:T(8,128)(2,1)S(1)} %pad_maximum_fusion.1.refs_2_), channel_id=1, source_target_pairs={{0,4},{1,5},{2,6},{3,7},{4,0},{5,1},{6,2},{7,3},{8,12},{9,13},{10,... | collective-permute-start | bytes 688136 | tf_op jit(solution)/shard_map/ppermute | solution.py:28
  84.0 5.3 %collective-permute-start.28 = (f32[2,192]{1,0:T(2,128)S(1)}, f32[2,192]{1,0:T(2,128)S(1)}, u32[]{:S(2)}, u32[]{:S(2)}) collective-permute-start(f32[2,192]{1,0:T(2,128)S(1)} %bitcast.50), channel_id=1, source_target_pairs={{0,1},{1,0},{2,3},{3,2},{4,5},{5,4},{6,7},{7,6},{8,9},{9,8},{10,11... | collective-permute-start | bytes 4616 | tf_op jit(solution)/shard_map/ppermute | solution.py:28
  91.7 13.8 %collective-permute-start.29 = (bf16[4,144,256]{2,1,0:T(8,128)(2,1)S(1)}, bf16[4,144,256]{2,1,0:T(8,128)(2,1)S(1)}, u32[]{:S(2)}, u32[]{:S(2)}) collective-permute-start(bf16[4,144,256]{2,1,0:T(8,128)(2,1)S(1)} %get-tuple-element.218), channel_id=1, source_target_pairs={{0,2},{1,3},{2,0},{3,1},{4,6},{5,7},{6,4},{7,5},{8,10},{9,11},{10,... | collective-permute-start | bytes 884744 | tf_op jit(solution)/shard_map/ppermute | solution.py:28
  93.5 12.3 %collective-permute-start.30 = (bf16[4,144,256]{2,1,0:T(8,128)(2,1)S(1)}, bf16[4,144,256]{2,1,0:T(8,128)(2,1)S(1)}, u32[]{:S(2)}, u32[]{:S(2)}) collective-permute-start(bf16[4,144,256]{2,1,0:T(8,128)(2,1)S(1)} %get-tuple-element.219), channel_id=1, source_target_pairs={{0,4},{1,5},{2,6},{3,7},{4,0},{5,1},{6,2},{7,3},{8,12},{9,13},{10,... | collective-permute-start | bytes 884744 | tf_op jit(solution)/shard_map/ppermute | solution.py:28
  93.5 12.0 %collective-permute-start.31 = (bf16[384,128]{1,0:T(8,128)(2,1)S(1)}, bf16[384,128]{1,0:T(8,128)(2,1)S(1)}, u32[]{:S(2)}, u32[]{:S(2)}) collective-permute-start(bf16[384,128]{1,0:T(8,128)(2,1)S(1)} %get-tuple-element.220), channel_id=1, source_target_pairs={{0,14},{1,15},{2,12},{3,13},{4,10},{5,11},{6,8},{7,9},{8,6},{9,7},... | collective-permute-start | bytes 294920 | tf_op jit(solution)/shard_map/ppermute | solution.py:28
  95.4 12.7 %collective-permute-start.32 = (bf16[384,128]{1,0:T(8,128)(2,1)S(1)}, bf16[384,128]{1,0:T(8,128)(2,1)S(1)}, u32[]{:S(2)}, u32[]{:S(2)}) collective-permute-start(bf16[384,128]{1,0:T(8,128)(2,1)S(1)} %get-tuple-element.223), channel_id=1, source_target_pairs={{0,11},{1,10},{2,9},{3,8},{4,15},{5,14},{6,13},{7,12},{8,3},{9,2},... | collective-permute-start | bytes 294920 | tf_op jit(solution)/shard_map/ppermute | solution.py:28
  95.6 12.5 %collective-permute-start.33 = (bf16[384,128]{1,0:T(8,128)(2,1)S(1)}, bf16[384,128]{1,0:T(8,128)(2,1)S(1)}, u32[]{:S(2)}, u32[]{:S(2)}) collective-permute-start(bf16[384,128]{1,0:T(8,128)(2,1)S(1)} %get-tuple-element.224), channel_id=1, source_target_pairs={{0,15},{1,14},{2,13},{3,12},{4,11},{5,10},{6,9},{7,8},{8,7},{9,6},... | collective-permute-start | bytes 294920 | tf_op jit(solution)/shard_map/ppermute | solution.py:28
  108.1 10.7 %collective-permute-start.35 = (bf16[2,144,256]{2,1,0:T(8,128)(2,1)S(1)}, bf16[2,144,256]{2,1,0:T(8,128)(2,1)S(1)}, u32[]{:S(2)}, u32[]{:S(2)}) collective-permute-start(bf16[2,144,256]{2,1,0:T(8,128)(2,1)S(1)} %get-tuple-element.319), channel_id=1, source_target_pairs={{0,8},{1,9},{2,10},{3,11},{4,12},{5,13},{6,14},{7,15},{8,0},{9,1},... | collective-permute-start | bytes 442376 | tf_op jit(solution)/shard_map/ppermute | solution.py:28
  111.3 7.5 %collective-permute-start.34 = (bf16[2,144,256]{2,1,0:T(8,128)(2,1)S(1)}, bf16[2,144,256]{2,1,0:T(8,128)(2,1)S(1)}, u32[]{:S(2)}, u32[]{:S(2)}) collective-permute-start(bf16[2,144,256]{2,1,0:T(8,128)(2,1)S(1)} %get-tuple-element.320), channel_id=1, source_target_pairs={{0,4},{1,5},{2,6},{3,7},{4,0},{5,1},{6,2},{7,3},{8,12},{9,13},{10,... | collective-permute-start | bytes 442376 | tf_op jit(solution)/shard_map/ppermute | solution.py:28
  118.8 7.0 %collective-permute-start.37 = (bf16[1,144,256]{2,1,0:T(8,128)(2,1)S(1)}, bf16[1,144,256]{2,1,0:T(8,128)(2,1)S(1)}, u32[]{:S(2)}, u32[]{:S(2)}) collective-permute-start(bf16[1,144,256]{2,1,0:T(8,128)(2,1)S(1)} %get-tuple-element.323), channel_id=1, source_target_pairs={{0,2},{1,3},{2,0},{3,1},{4,6},{5,7},{6,4},{7,5},{8,10},{9,11},{10,... | collective-permute-start | bytes 221192 | tf_op jit(solution)/shard_map/ppermute | solution.py:28
  119.4 6.5 %collective-permute-start.36 = (bf16[1,144,256]{2,1,0:T(8,128)(2,1)S(1)}, bf16[1,144,256]{2,1,0:T(8,128)(2,1)S(1)}, u32[]{:S(2)}, u32[]{:S(2)}) collective-permute-start(bf16[1,144,256]{2,1,0:T(8,128)(2,1)S(1)} %get-tuple-element.325), channel_id=1, source_target_pairs={{0,8},{1,9},{2,10},{3,11},{4,12},{5,13},{6,14},{7,15},{8,0},{9,1},... | collective-permute-start | bytes 221192 | tf_op jit(solution)/shard_map/ppermute | solution.py:28
  126.8 1.3 collective-permute-start.38
  130.8 11.9 %collective-permute-start.46 = (bf16[160,128]{1,0:T(8,128)(2,1)S(1)}, bf16[160,128]{1,0:T(8,128)(2,1)S(1)}, u32[]{:S(2)}, u32[]{:S(2)}) collective-permute-start(bf16[160,128]{1,0:T(8,128)(2,1)S(1)} %get-tuple-element.298), channel_id=1, source_target_pairs={{0,8},{1,9},{2,10},{3,11},{4,12},{5,13},{6,14},{7,15},{8,0},{9,1},... | collective-permute-start | bytes 122888 | tf_op jit(solution)/shard_map/ppermute | solution.py:28
  132.5 10.6 %collective-permute-start.47 = (bf16[160,128]{1,0:T(8,128)(2,1)S(1)}, bf16[160,128]{1,0:T(8,128)(2,1)S(1)}, u32[]{:S(2)}, u32[]{:S(2)}) collective-permute-start(bf16[160,128]{1,0:T(8,128)(2,1)S(1)} %get-tuple-element.299), channel_id=1, source_target_pairs={{0,9},{1,8},{2,11},{3,10},{4,13},{5,12},{6,15},{7,14},{8,1},{9,0},... | collective-permute-start | bytes 122888 | tf_op jit(solution)/shard_map/ppermute | solution.py:28
  133.3 13.7 %collective-permute-start.48 = (bf16[160,128]{1,0:T(8,128)(2,1)S(1)}, bf16[160,128]{1,0:T(8,128)(2,1)S(1)}, u32[]{:S(2)}, u32[]{:S(2)}) collective-permute-start(bf16[160,128]{1,0:T(8,128)(2,1)S(1)} %get-tuple-element.300), channel_id=1, source_target_pairs={{0,10},{1,11},{2,8},{3,9},{4,14},{5,15},{6,12},{7,13},{8,2},{9,3},... | collective-permute-start | bytes 122888 | tf_op jit(solution)/shard_map/ppermute | solution.py:28
  135.7 12.1 %collective-permute-start.49 = (bf16[160,128]{1,0:T(8,128)(2,1)S(1)}, bf16[160,128]{1,0:T(8,128)(2,1)S(1)}, u32[]{:S(2)}, u32[]{:S(2)}) collective-permute-start(bf16[160,128]{1,0:T(8,128)(2,1)S(1)} %get-tuple-element.301), channel_id=1, source_target_pairs={{0,11},{1,10},{2,9},{3,8},{4,15},{5,14},{6,13},{7,12},{8,3},{9,2},... | collective-permute-start | bytes 122888 | tf_op jit(solution)/shard_map/ppermute | solution.py:28
  137.1 10.9 %collective-permute-start.50 = (bf16[160,128]{1,0:T(8,128)(2,1)S(1)}, bf16[160,128]{1,0:T(8,128)(2,1)S(1)}, u32[]{:S(2)}, u32[]{:S(2)}) collective-permute-start(bf16[160,128]{1,0:T(8,128)(2,1)S(1)} %get-tuple-element.302), channel_id=1, source_target_pairs={{0,12},{1,13},{2,14},{3,15},{4,8},{5,9},{6,10},{7,11},{8,4},{9,5},... | collective-permute-start | bytes 122888 | tf_op jit(solution)/shard_map/ppermute | solution.py:28
  142.7 6.9 %collective-permute-start.51 = (bf16[160,128]{1,0:T(8,128)(2,1)S(1)}, bf16[160,128]{1,0:T(8,128)(2,1)S(1)}, u32[]{:S(2)}, u32[]{:S(2)}) collective-permute-start(bf16[160,128]{1,0:T(8,128)(2,1)S(1)} %get-tuple-element.303), channel_id=1, source_target_pairs={{0,13},{1,12},{2,15},{3,14},{4,9},{5,8},{6,11},{7,10},{8,5},{9,4},... | collective-permute-start | bytes 122888 | tf_op jit(solution)/shard_map/ppermute | solution.py:28
  143.2 7.2 %collective-permute-start.52 = (bf16[160,128]{1,0:T(8,128)(2,1)S(1)}, bf16[160,128]{1,0:T(8,128)(2,1)S(1)}, u32[]{:S(2)}, u32[]{:S(2)}) collective-permute-start(bf16[160,128]{1,0:T(8,128)(2,1)S(1)} %get-tuple-element.304), channel_id=1, source_target_pairs={{0,14},{1,15},{2,12},{3,13},{4,10},{5,11},{6,8},{7,9},{8,6},{9,7},... | collective-permute-start | bytes 122888 | tf_op jit(solution)/shard_map/ppermute | solution.py:28
  147.0 6.2 %collective-permute-start.53 = (bf16[160,128]{1,0:T(8,128)(2,1)S(1)}, bf16[160,128]{1,0:T(8,128)(2,1)S(1)}, u32[]{:S(2)}, u32[]{:S(2)}) collective-permute-start(bf16[160,128]{1,0:T(8,128)(2,1)S(1)} %get-tuple-element.305), channel_id=1, source_target_pairs={{0,15},{1,14},{2,13},{3,12},{4,11},{5,10},{6,9},{7,8},{8,7},{9,6},... | collective-permute-start | bytes 122888 | tf_op jit(solution)/shard_map/ppermute | solution.py:28
  147.8 5.4 %collective-permute-start.39 = (bf16[160,128]{1,0:T(8,128)(2,1)S(1)}, bf16[160,128]{1,0:T(8,128)(2,1)S(1)}, u32[]{:S(2)}, u32[]{:S(2)}) collective-permute-start(bf16[160,128]{1,0:T(8,128)(2,1)S(1)} %get-tuple-element.289), channel_id=1, source_target_pairs={{0,1},{1,0},{2,3},{3,2},{4,5},{5,4},{6,7},{7,6},{8,9},{9,8},{10,11... | collective-permute-start | bytes 122888 | tf_op jit(solution)/shard_map/ppermute | solution.py:28
  148.0 7.2 %collective-permute-start.40 = (bf16[160,128]{1,0:T(8,128)(2,1)S(1)}, bf16[160,128]{1,0:T(8,128)(2,1)S(1)}, u32[]{:S(2)}, u32[]{:S(2)}) collective-permute-start(bf16[160,128]{1,0:T(8,128)(2,1)S(1)} %get-tuple-element.290), channel_id=1, source_target_pairs={{0,2},{1,3},{2,0},{3,1},{4,6},{5,7},{6,4},{7,5},{8,10},{9,11},{10,... | collective-permute-start | bytes 122888 | tf_op jit(solution)/shard_map/ppermute | solution.py:28
  149.6 6.2 %collective-permute-start.41 = (bf16[160,128]{1,0:T(8,128)(2,1)S(1)}, bf16[160,128]{1,0:T(8,128)(2,1)S(1)}, u32[]{:S(2)}, u32[]{:S(2)}) collective-permute-start(bf16[160,128]{1,0:T(8,128)(2,1)S(1)} %get-tuple-element.291), channel_id=1, source_target_pairs={{0,3},{1,2},{2,1},{3,0},{4,7},{5,6},{6,5},{7,4},{8,11},{9,10},{10,... | collective-permute-start | bytes 122888 | tf_op jit(solution)/shard_map/ppermute | solution.py:28
  150.4 5.5 %collective-permute-start.42 = (bf16[160,128]{1,0:T(8,128)(2,1)S(1)}, bf16[160,128]{1,0:T(8,128)(2,1)S(1)}, u32[]{:S(2)}, u32[]{:S(2)}) collective-permute-start(bf16[160,128]{1,0:T(8,128)(2,1)S(1)} %get-tuple-element.292), channel_id=1, source_target_pairs={{0,4},{1,5},{2,6},{3,7},{4,0},{5,1},{6,2},{7,3},{8,12},{9,13},{10,... | collective-permute-start | bytes 122888 | tf_op jit(solution)/shard_map/ppermute | solution.py:28
  153.3 3.4 %collective-permute-start.43 = (bf16[160,128]{1,0:T(8,128)(2,1)S(1)}, bf16[160,128]{1,0:T(8,128)(2,1)S(1)}, u32[]{:S(2)}, u32[]{:S(2)}) collective-permute-start(bf16[160,128]{1,0:T(8,128)(2,1)S(1)} %get-tuple-element.293), channel_id=1, source_target_pairs={{0,5},{1,4},{2,7},{3,6},{4,1},{5,0},{6,3},{7,2},{8,13},{9,12},{10,... | collective-permute-start | bytes 122888 | tf_op jit(solution)/shard_map/ppermute | solution.py:28
  153.3 4.9 %collective-permute-start.44 = (bf16[160,128]{1,0:T(8,128)(2,1)S(1)}, bf16[160,128]{1,0:T(8,128)(2,1)S(1)}, u32[]{:S(2)}, u32[]{:S(2)}) collective-permute-start(bf16[160,128]{1,0:T(8,128)(2,1)S(1)} %get-tuple-element.294), channel_id=1, source_target_pairs={{0,6},{1,7},{2,4},{3,5},{4,2},{5,3},{6,0},{7,1},{8,14},{9,15},{10,... | collective-permute-start | bytes 122888 | tf_op jit(solution)/shard_map/ppermute | solution.py:28
  155.2 4.7 %collective-permute-start.45 = (bf16[160,128]{1,0:T(8,128)(2,1)S(1)}, bf16[160,128]{1,0:T(8,128)(2,1)S(1)}, u32[]{:S(2)}, u32[]{:S(2)}) collective-permute-start(bf16[160,128]{1,0:T(8,128)(2,1)S(1)} %get-tuple-element.295), channel_id=1, source_target_pairs={{0,7},{1,6},{2,5},{3,4},{4,3},{5,2},{6,1},{7,0},{8,15},{9,14},{10,... | collective-permute-start | bytes 122888 | tf_op jit(solution)/shard_map/ppermute | solution.py:28

commit v4 on v2

--- a/solution.py
+++ b/solution.py
@@ -49,59 +49,73 @@
     return (summed * scale_rows * norm_gain.astype(jnp.float32)).astype(jnp.bfloat16)
 
 
-def time_embedding(timesteps, modulation_weight):
+def time_embedding(timesteps):
     half_width = TEMB // 2
     freqs = jnp.exp(-math.log(10000.0) * jnp.arange(half_width, dtype=jnp.float32) / half_width)
     angles = timesteps.astype(jnp.float32)[:, None] * freqs[None, :]
     embedding = jnp.concatenate([jnp.cos(angles), jnp.sin(angles)], 1)
-    embedding = jax.nn.silu(embedding).astype(jnp.bfloat16)
-    flat = modulation_weight.reshape(modulation_weight.shape[0], -1)
-    product = jnp.dot(embedding, flat, preferred_element_type=jnp.float32)
-    return product.reshape(timesteps.shape[0], 2, -1)
-
-
-def encoder_kernel(lane, order, place_ref, act_ref, weight_ref, own_ref, other_ref, lhs_ref):
-    chips = own_ref.shape[0]
+    return jax.nn.silu(embedding).astype(jnp.bfloat16)
+
+
+def encoder_kernel(lane, order, place_ref, act_ref, weight_ref, own_ref, other_ref, *refs):
+    *turned, held_ref, arrived = refs
+    chips, share, width = own_ref.shape
     at, core = place_ref[lane], place_ref[2]
-
-    @pl.when(pl.program_id(0) == 0)
-    def _():
+    depth = weight_ref.shape[0]
+    tile = 256
+    loads = []
+    for start in range(0, width, tile):
+        load = pltpu.make_async_copy(
+            weight_ref.at[:, pl.ds(lane * width + start, tile)],
+            held_ref.at[:, pl.ds(start, tile)],
+            arrived.at[start // tile],
+        )
+        load.start()
+        loads.append(load)
+    lhs_ref = act_ref
+    if turned:
+        (lhs_ref,) = turned
         lhs_ref[...] = act_ref[...].T
-
-    result = jnp.dot(lhs_ref[...], weight_ref[...], preferred_element_type=jnp.float32)
-    half = result.shape[0] // 2
-    share = half // chips
+    cut = depth // 256 * 256
+    half = chips * share
     first = core == 0
-    own = jnp.where(first, result[:half], result[half:]).astype(own_ref.dtype)
-    other = jnp.where(first, result[half:], result[:half]).astype(own_ref.dtype)
-    own = own.reshape(chips, share, -1)
-    other = other.reshape(chips, share, -1)
-    for block in range(chips):
-        own_ref[at ^ position(block, order)] = own[block]
-        other_ref[at ^ position(block, order)] = other[block]
+    for start in range(0, width, tile):
+        columns = slice(start, start + tile)
+        loads[start // tile].wait()
+        result = jnp.dot(
+            lhs_ref[:, :cut], held_ref[:cut, columns], preferred_element_type=jnp.float32
+        )
+        if cut < depth:
+            result += jnp.dot(
+                lhs_ref[:, cut:], held_ref[cut:, columns], preferred_element_type=jnp.float32
+            )
+        own = jnp.where(first, result[:half], result[half:]).astype(own_ref.dtype)
+        other = jnp.where(first, result[half:], result[:half]).astype(own_ref.dtype)
+        own = own.reshape(chips, share, tile)
+        other = other.reshape(chips, share, tile)
+        for block in range(chips):
+            to = at ^ position(block, order)
+            own_ref[to, :, start : start + tile] = own[block]
+            other_ref[to, :, start : start + tile] = other[block]
 
 
 def encoder(lane, order, place, act, weight):
     chips = 1 << len(order)
-    depth, rows = act.shape
+    depth = weight.shape[0]
+    rows = act.size // depth
     width = weight.shape[1] // 2
-    steps = 2
-    tile = width // steps
-    share = rows // 2 // chips
-    out = jax.ShapeDtypeStruct((chips, share, width), jnp.bfloat16)
-    out_spec = pl.BlockSpec((chips, share, tile), lambda i: (0, 0, i))
+    turn = act.shape[0] == depth
+    out = jax.ShapeDtypeStruct((chips, rows // 2 // chips, width), jnp.bfloat16)
     return pl.pallas_call(
         functools.partial(encoder_kernel, lane, order),
-        grid=(steps,),
-        out_shape=(out, out),
-        in_specs=[
-            SMEM_SPEC,
-            pl.BlockSpec((depth, rows), lambda i: (0, 0)),
-            pl.BlockSpec((depth, tile), lambda i: (0, lane * steps + i)),
+        out_shape=(out, out) + (jax.ShapeDtypeStruct((rows, depth), act.dtype),) * turn,
+        in_specs=[SMEM_SPEC, VMEM_SPEC, pl.BlockSpec(memory_space=pl.ANY)],
+        out_specs=(VMEM_SPEC,) * (2 + turn),
+        scratch_shapes=[
+            pltpu.VMEM((depth, width), weight.dtype),
+            pltpu.SemaphoreType.DMA((width // 256,)),
         ],
-        out_specs=(out_spec, out_spec),
-        scratch_shapes=[pltpu.VMEM((rows, depth), jnp.bfloat16)],
-        compiler_params=params(24),
+        compiler_params=params(60),
         cost_estimate=pl.CostEstimate(
             flops=2 * rows * depth * width,
             bytes_accessed=2 * (depth * rows + depth * width + rows * width),
@@ -118,9 +132,10 @@
 
 def project_kernel(lanes, place_ref, *refs):
     pieces, refs = (refs[:2], refs[2:4]), refs[4:]
-    win0, win1, kv0, kv1, mod0, mod1, keys_ref, values_ref, states, proj0, proj1, sums = refs
+    time, win0, win1, kv0, kv1, mod0, mod1, *outs, states, proj0, proj1, sums = refs
     chip = place_ref[3]
-    chips = keys_ref.shape[0]
+    half_chips = outs[0].shape[0]
+    chips = 2 * half_chips
     rows = proj0.shape[0]
     share = rows // chips
     depth = states.shape[1]
@@ -147,21 +162,27 @@
     lane = lax.broadcasted_iota(jnp.int32, sums.shape, 1)
     sums[...] = jnp.where(lane == 0, first, second).T
     left = []
+    embedding = jnp.broadcast_to(time[...].astype(jnp.float32), (16, time.shape[1]))
+    embedding = embedding.astype(jnp.bfloat16)
     for value, mod in ((value0, mod0), (value1, mod1)):
-        scale, shift = 1.0 + mod[1:2, :], mod[0:1, :]
+        shift, scale = [
+            lax.dot_general(embedding, mod[at], contract, preferred_element_type=jnp.float32)[:1]
+            for at in range(2)
+        ]
+        scale = 1.0 + scale
         row = lax.broadcasted_iota(jnp.int32, (16, value.shape[1]), 0)
         lines = jnp.where(row < 2, scale, shift)
         high = lines.astype(jnp.bfloat16).astype(jnp.float32)
         lines = jnp.where(row % 2 == 0, high, lines - high)
         lines = jnp.where(row < 4, lines, 0.0)
         left.append(jnp.concatenate([value * scale, lines], 0).astype(jnp.bfloat16))
-    width = keys_ref.shape[2]
+    width = outs[0].shape[2]
     slots, extra = slot_rows(chips, width)
     per_slot = slots // chips
     row = lax.broadcasted_iota(jnp.int32, (extra, width), 0)
     column = lax.broadcasted_iota(jnp.int32, (extra, width), 1)
     half = kv0.shape[1] // 2
-    for lane, (out_ref, order) in enumerate(zip((keys_ref, values_ref), lanes)):
+    for lane, order in enumerate(lanes):
         line = sums[lane : lane + 1, :]
         high = line.astype(jnp.bfloat16).astype(jnp.float32)
         low = line - high
@@ -170,32 +191,33 @@
         else:
             line = jnp.where(row % 2 == 0, high, low)
         line = jnp.where(row // per_slot == chip, line, 0.0)
-        for at in range(chips):
+        for at in reversed(range(chips)):
+            out_ref, to = outs[2 * lane + at // half_chips], at % half_chips
             start = lane * half + (chip ^ member(at, order)) * width
             columns = pl.ds(pl.multiple_of(start, width), width)
             value = jnp.dot(left[0], kv0[:, columns], preferred_element_type=jnp.float32)
             value += jnp.dot(left[1], kv1[:, columns], preferred_element_type=jnp.float32)
-            out_ref[at, :rows, :] = value[:rows].astype(out_ref.dtype)
+            out_ref[to, :rows, :] = value[:rows].astype(out_ref.dtype)
             below = jnp.where(row == slots, value[rows : rows + 1] + value[rows + 1 : rows + 2], line)
             below = jnp.where(
                 row == slots + 1, value[rows + 2 : rows + 3] + value[rows + 3 : rows + 4], below
             )
-            out_ref[at, rows:, :] = below.astype(out_ref.dtype)
-
-
-def project(lanes, place, pieces, win0, win1, kv0, kv1, mod0, mod1):
+            out_ref[to, rows:, :] = below.astype(out_ref.dtype)
+
+
+def project(lanes, place, pieces, time, win0, win1, kv0, kv1, mod0, mod1):
     chips = 1 << len(lanes[0])
     rows = 2 * pieces[0].shape[0]
     features, depth = win0.shape
     total = kv0.shape[1]
     width = total // 2 // chips
     extra = slot_rows(chips, width)[1]
-    out = jax.ShapeDtypeStruct((chips, rows + extra, width), jnp.bfloat16)
+    out = jax.ShapeDtypeStruct((chips // 2, rows + extra, width), jnp.bfloat16)
     return pl.pallas_call(
         functools.partial(project_kernel, lanes),
-        out_shape=(out, out),
-        in_specs=[SMEM_SPEC] + [VMEM_SPEC] * 10,
-        out_specs=(VMEM_SPEC, VMEM_SPEC),
+        out_shape=(out,) * 4,
+        in_specs=[SMEM_SPEC] + [VMEM_SPEC] * 11,
+        out_specs=(VMEM_SPEC,) * 4,
         scratch_shapes=[
             pltpu.VMEM((rows, depth // 2), jnp.bfloat16),
             pltpu.VMEM((rows, features), jnp.float32),
@@ -209,7 +231,7 @@
             transcendentals=0,
         ),
         name="project",
-    )(place, *pieces, win0, win1, kv0, kv1, mod0, mod1)
+    )(place, *pieces, time, win0, win1, kv0, kv1, mod0, mod1)
 
 
 def combine_kernel(chips, model_width, place_ref, *refs):
@@ -262,31 +284,25 @@
     )(place, *parts)
 
 
-def pack_kernel(copies, queries_ref, keys_ref, values_ref, out_ref):
-    img_dev = keys_ref.shape[0]
-    part_rows = img_dev // copies
+def pack_kernel(copies, rows_ref, out_ref):
+    count = out_ref.shape[1]
     for device in range(out_ref.shape[0]):
         head, copy = device // copies, device % copies
         span = slice(head * HEAD_DIM, (head + 1) * HEAD_DIM)
-        out_ref[device, :img_dev, :] = keys_ref[:, span]
-        out_ref[device, img_dev : 2 * img_dev, :] = values_ref[:, span]
-        out_ref[device, 2 * img_dev :, :] = queries_ref[copy * part_rows : (copy + 1) * part_rows, span]
-
-
-def pack(copies, queries, keys, values):
-    img_dev = keys.shape[0]
-    rows = 2 * img_dev + img_dev // copies
+        start = copy * count if count < rows_ref.shape[0] else 0
+        out_ref[device] = rows_ref[start : start + count, span]
+
+
+def pack(copies, rows, count):
     return pl.pallas_call(
         functools.partial(pack_kernel, copies),
-        out_shape=jax.ShapeDtypeStruct((HEADS * copies, rows, HEAD_DIM), jnp.bfloat16),
-        in_specs=[VMEM_SPEC] * 3,
+        out_shape=jax.ShapeDtypeStruct((HEADS * copies, count, HEAD_DIM), jnp.bfloat16),
+        in_specs=[VMEM_SPEC],
         out_specs=VMEM_SPEC,
         compiler_params=params(8),
-        cost_estimate=pl.CostEstimate(
-            flops=0, bytes_accessed=4 * HEADS * copies * rows * HEAD_DIM, transcendentals=0
-        ),
+        cost_estimate=pl.CostEstimate(flops=0, bytes_accessed=4 * rows.size, transcendentals=0),
         name="pack",
-    )(queries, keys, values)
+    )(rows)
 
 
 def unpack_kernel(copies, part_rows, blocks_ref, attended_ref, text_ref):
@@ -319,48 +335,46 @@
     )(blocks)
 
 
-def image_kernel(factor, queries_ref, keys_ref, values_ref, sum_ref, norm_ref):
+def image_kernel(factor, call, queries_ref, keys_ref, values_ref, sum_ref, norm_ref):
+    part_rows = queries_ref.shape[1]
+    group = max(1, 256 // part_rows)
+    rows = group * part_rows
     contract = (((1,), (1,)), ((), ()))
-    queries = queries_ref[...].reshape(-1, HEAD_DIM)
     keys = keys_ref[...].reshape(-1, HEAD_DIM)
     values = values_ref[...].reshape(-1, HEAD_DIM)
-    scores = lax.dot_general(queries, keys, contract, preferred_element_type=jnp.float32) * factor
-    top = jnp.max(scores, 1, keepdims=True)
-    weights = jnp.exp2(scores - top)
-    total = jnp.sum(weights, 1, keepdims=True)
-    sum_ref[...] = jnp.dot(weights.astype(jnp.bfloat16), values, preferred_element_type=jnp.float32)
-    lane = lax.broadcasted_iota(jnp.int32, norm_ref.shape, 1)
-    norm_ref[...] = jnp.where(lane < 64, top, total)
-
-
-def image_attention(packed, img_dev, part_rows, factor, call, calls):
-    devices = packed.shape[0]
-    count = devices * part_rows // calls
-    group = max(1, 256 // part_rows)
-    block = group * part_rows
-    at = 2 * img_dev // part_rows
-    steps = devices // group // calls
+    steps = sum_ref.shape[0] // rows
+    for step in range(steps):
+        at = (call * steps + step) * group
+        span = slice(step * rows, (step + 1) * rows)
+        queries = queries_ref[at : at + group].reshape(rows, HEAD_DIM)
+        scores = lax.dot_general(queries, keys, contract, preferred_element_type=jnp.float32) * factor
+        top = jnp.max(scores, 1, keepdims=True)
+        weights = jnp.exp2(scores - top)
+        total = jnp.sum(weights, 1, keepdims=True)
+        sum_ref[span, :] = jnp.dot(
+            weights.astype(jnp.bfloat16), values, preferred_element_type=jnp.float32
+        )
+        lane = lax.broadcasted_iota(jnp.int32, (rows, 128), 1)
+        norm_ref[span, :] = jnp.where(lane < 64, top, total)
+
+
+def image_attention(queries, keys, values, factor, call, calls):
+    count = queries.shape[0] * queries.shape[1] // calls
+    total = keys.shape[0] * keys.shape[1]
     out = jax.ShapeDtypeStruct((count, HEAD_DIM), jnp.float32)
-    out_spec = pl.BlockSpec((block, HEAD_DIM), lambda i: (i, 0))
-    keys = devices * img_dev
-    return pl.pallas_call(
-        functools.partial(image_kernel, factor),
-        grid=(steps,),
+    return pl.pallas_call(
+        functools.partial(image_kernel, factor, call),
         out_shape=(out, out),
-        in_specs=[
-            pl.BlockSpec((group, part_rows, HEAD_DIM), lambda i: (call * steps + i, at, 0)),
-            pl.BlockSpec((devices, img_dev, HEAD_DIM), lambda i: (0, 0, 0)),
-            pl.BlockSpec((devices, img_dev, HEAD_DIM), lambda i: (0, 1, 0)),
-        ],
-        out_specs=(out_spec, out_spec),
-        compiler_params=params(20),
+        in_specs=[VMEM_SPEC] * 3,
+        out_specs=(VMEM_SPEC, VMEM_SPEC),
+        compiler_params=params(24),
         cost_estimate=pl.CostEstimate(
-            flops=4 * count * keys * HEAD_DIM,
-            bytes_accessed=4 * keys * HEAD_DIM + 10 * count * HEAD_DIM,
-            transcendentals=count * keys,
+            flops=4 * count * total * HEAD_DIM,
+            bytes_accessed=4 * total * HEAD_DIM + 10 * count * HEAD_DIM,
+            transcendentals=count * total,
         ),
         name="image_attention",
-    )(packed, packed, packed)
+    )(queries, keys, values)
 
 
 def finish_kernel(factor, calls, place_ref, queries_ref, *refs):
@@ -404,31 +418,27 @@
         out_ref[device, part_rows:, :] = block.astype(out_ref.dtype)
 
 
-def finish(place, packed, images, mine, got, img_dev, part_rows, factor):
-    devices = packed.shape[0]
+def finish(place, queries, images, mine, got, factor):
+    devices, part_rows = queries.shape[0], queries.shape[1]
     share = 2 * mine.shape[0] // devices
     count = devices * part_rows
-    at = 2 * img_dev // part_rows
     return pl.pallas_call(
         functools.partial(finish_kernel, factor, len(images) // 2),
-        grid=(1,),
         out_shape=jax.ShapeDtypeStruct((devices, part_rows + 2 * share, HEAD_DIM), jnp.bfloat16),
-        in_specs=[SMEM_SPEC, pl.BlockSpec((devices, part_rows, HEAD_DIM), lambda i: (0, at, 0))]
-        + [VMEM_SPEC] * (len(images) + 2),
-        out_specs=pl.BlockSpec((devices, part_rows + 2 * share, HEAD_DIM), lambda i: (0, 0, 0)),
-        compiler_params=params(20),
+        in_specs=[SMEM_SPEC] + [VMEM_SPEC] * (len(images) + 3),
+        out_specs=VMEM_SPEC,
+        compiler_params=params(16),
         cost_estimate=pl.CostEstimate(
             flops=4 * count * 2 * mine.shape[0] * HEAD_DIM,
             bytes_accessed=12 * count * HEAD_DIM,
             transcendentals=count * 2 * mine.shape[0],
         ),
         name="finish",
-    )(place, packed, *images, mine, got)
-
-
-def halves(blocks):
-    half = blocks.shape[0] // 2
-    return blocks[:half], blocks[half:].astype(jnp.bfloat16)
+    )(place, queries, *images, mine, got)
+
+
+def add(one, other, dtype):
+    return (one.astype(jnp.float32) + other.astype(jnp.float32)).astype(dtype)
 
 
 def local(
@@ -457,62 +467,84 @@
     place = place.astype(jnp.int32)
 
     win0, kv0 = text_in_weight.T, key_value_weight
-    win1, kv1 = swap(win0, 1), swap(kv0, 1)
-    mod0 = time_embedding(timesteps, modulation_weight)[0]
-    mod1 = swap(mod0, 1)
+    mod0 = modulation_weight.transpose(1, 2, 0)
+    win1, kv1, mod1 = swap(win0, 1), swap(kv0, 1), swap(mod0, 1)
+    time = time_embedding(timesteps)
+
+    rounds = len(lanes[0])
+    tie = lax.optimization_barrier
+
+    def exchange(rows):
+        return lax.all_to_all(rows, "seq", split_axis=0, concat_axis=0, tiled=True)
 
     act = enc_act[0].T
-    blocks = []
+    act, queries = tie((act, pack(copies, image_queries[0], part_rows)))
+    queries = exchange(queries)
+    keep, sent = [], []
     for lane, order in enumerate(lanes):
-        own, other = encoder(lane, order, place, act, down_weight)
-        blocks.append(own.astype(jnp.float32) + swap(other, 1).astype(jnp.float32))
-    for step in range(len(lanes[0])):
-        keep, sent = zip(*[halves(block) for block in blocks])
+        own, other, *turned = encoder(lane, order, place, act, down_weight)
+        if lane == 0:
+            act = turned[0]
+        got = swap(other, 1)
+        sent.append(add(own[chips // 2 :], got[chips // 2 :], jnp.bfloat16))
+        keep.append(add(own[: chips // 2], got[: chips // 2], jnp.float32))
+    for step in range(rounds):
         if step == 0:
-            sent, image_queries, image_key_values = lax.optimization_barrier(
-                (sent, image_queries, image_key_values)
-            )
-            packed = pack(
-                copies, image_queries[0], image_key_values[0, :, 0], image_key_values[0, :, 1]
-            )
+            sent, image_key_values = tie((sent, image_key_values))
+            keys = exchange(pack(copies, image_key_values[0, :, 0], img_dev))
         got = [swap(part, 2 * order[step]) for part, order in zip(sent, lanes)]
         if step == 0:
-            got, packed = lax.optimization_barrier((got, packed))
-            packed = lax.all_to_all(packed, "seq", split_axis=0, concat_axis=0, tiled=True)
-        blocks = [mine + part.astype(jnp.float32) for mine, part in zip(keep, got)]
-
-    summed = jnp.concatenate([block[0] for block in blocks], 1)
-    states = normalize(summed, norm_gain)
-    pieces = jnp.split(states, 2, axis=1)
-    for step in reversed(range(len(lanes[0]))):
-        got = [swap(piece, 2 * order[step]) for piece, order in zip(pieces, lanes)]
-        if step > 0:
-            pieces = [jnp.concatenate(pair, 0) for pair in zip(pieces, got)]
-    pieces = [piece for pair in zip(pieces, got) for piece in pair]
-
-    blocks = project(lanes, place, pieces, win0, win1, kv0, kv1, mod0, mod1)
-    calls = 2
+            got, win1, kv1, mod1, queries = tie((got, win1, kv1, mod1, queries))
+        if step == 2:
+            got, keys = tie((got, keys))
+        half = keep[0].shape[0] // 2
+        if half:
+            sent = [add(mine[half:], part[half:], jnp.bfloat16) for mine, part in zip(keep, got)]
+            keep = [add(mine[:half], part[:half], jnp.float32) for mine, part in zip(keep, got)]
+    summed = [add(mine[0], part[0], jnp.float32) for mine, part in zip(keep, got)]
+
+    width = summed[0].shape[1]
+    square = sum(jnp.sum(part * part, 1, keepdims=True) for part in summed)
+    scale_rows = lax.rsqrt(square / (2 * width) + epsilon)
+    gains = norm_gain.astype(jnp.float32)
+    states = [
+        (part * scale_rows * gains[lane * width : (lane + 1) * width]).astype(jnp.bfloat16)
+        for lane, part in enumerate(summed)
+    ]
+    for step in reversed(range(rounds)):
+        if step == 1:
+            states, image_key_values = tie((states, image_key_values))
+            values = pack(copies, image_key_values[0, :, 1], img_dev)
+        if step == 0:
+            states, values = tie((states, values))
+            values = exchange(values)
+        got = [swap(state, 2 * order[step]) for state, order in zip(states, lanes)]
+        if step:
+            states = [jnp.concatenate(pair, 0) for pair in zip(states, got)]
+    states = [state for pair in zip(states, got) for state in pair]
+
+    blocks = project(lanes, place, states, time, win0, win1, kv0, kv1, mod0, mod1)
+    keep, sent = [blocks[0], blocks[2]], [blocks[1], blocks[3]]
     images = []
-    for step in range(len(lanes[0])):
-        keep, sent = zip(*[halves(block) for block in blocks])
-        if step < calls:
-            sent, packed = lax.optimization_barrier((sent, packed))
-            image = image_attention(packed, img_dev, part_rows, factor, step, calls)
+    for step in range(rounds):
         got = [swap(part, 2 * order[step]) for part, order in zip(sent, lanes)]
-        if step < calls:
-            got, image = lax.optimization_barrier((got, image))
+        if step == 0:
+            got, values = tie((got, values))
+        elif step <= 2:
+            sent, queries = tie((sent, queries))
+            image = image_attention(queries, keys, values, factor, step - 1, 2)
+            got, image = tie((got, image))
             images += image
-        if step < len(lanes[0]) - 1:
-            blocks = [
-                mine.astype(jnp.float32) + part.astype(jnp.float32) for mine, part in zip(keep, got)
-            ]
+        half = keep[0].shape[0] // 2
+        if half:
+            sent = [add(mine[half:], part[half:], jnp.bfloat16) for mine, part in zip(keep, got)]
+            keep = [add(mine[:half], part[:half], jnp.float32) for mine, part in zip(keep, got)]
     parts = [part[0] for pair in zip(keep, got) for part in pair]
     model_width = text_in_weight.shape[1] * devices
     mine, sent = combine(place, parts, chips, text_len // 2, model_width)
     got = swap(sent, 1)
 
-    back = finish(place, packed, images, mine, got, img_dev, part_rows, factor)
-    back = lax.all_to_all(back, "seq", split_axis=0, concat_axis=0, tiled=True)
+    back = exchange(finish(place, queries, images, mine, got, factor))
     attended, text_kv = unpack(copies, part_rows, back)
     return (attended[None], text_kv)
 

time: 153 us -> 167 us (1.092)
  waiting for transfers between devices: 59.2 us -> 49.3 us
  other arithmetic: 3.61 us -> 12.9 us
  Pallas kernels: 25.6 us -> 34.6 us
  starting transfers between devices: 30.8 us -> 38.1 us
  local copies, waits for them, and re-layouts: 8.89 us -> 6.62 us
    all_to_all x1 -> x3, starting transfers between devices: 3.89 us -> 15.7 us  [exchange(): return lax.all_to_all(rows, 'seq', split_axis=0, concat_axis=0, tiled=True)]
    ppermute x24, waiting for transfers between devices: 59.2 us -> 49.3 us  [swap(): return lax.ppermute(value, 'seq', [(i, i ^ mask) for i in range(devices)])]
    convert_element_type x3 -> x8, other arithmetic: 0.12 us -> 8.11 us  [the longest x6 6.96 us: add(): return (one.astype(jnp.float32) + other.astype(jnp.float32)).astype(dtype)]
    pallas_call x5, Pallas kernels: 18.5 us -> 26.4 us  [the longest x2 13.1 us: encoder(): pl.pallas_call(functools.partial(encoder_kernel, lane, order), out_shape=...]
    ppermute x24, starting transfers between devices: 27 us -> 22.4 us  [swap(): return lax.ppermute(value, 'seq', [(i, i ^ mask) for i in range(devices)])]
    unnamed x24 -> x32, local copies, waits for them, and re-layouts: 7.18 us -> 4.4 us
  transfers between devices with their start and end apart: 25 -> 27, of which waited for: 18 -> 15; matrix products, arithmetic and copies ran while one was open for 3% -> 6% of each run, Pallas kernels for 11% -> 13%
where the time goes in v4:
time: 167 us; the launch traced here: 166 us
  waiting for transfers between devices  49.3 us (30%)
  starting transfers between devices  38.1 us (23%)
  Pallas kernels  34.6 us (21%)
  blocking collectives  22 us (13%)
  other arithmetic  12.9 us (8%)
  local copies, waits for them, and re-layouts  6.62 us (4%)
  between operations  2.25 us (1%)
    ppermute x24, waiting for transfers between devices, swap(): return lax.ppermute(value, 'seq', [(i, i ^ mask) for i in range(devices)])  49.3 us
    ppermute x24, starting transfers between devices, swap(): return lax.ppermute(value, 'seq', [(i, i ^ mask) for i in range(devices)])  22.4 us
    all_to_all x1, blocking collectives, exchange(): return lax.all_to_all(rows, 'seq', split_axis=0, concat_axis=0, tiled=True)  22 us
    all_to_all x3, starting transfers between devices, exchange(): return lax.all_to_all(rows, 'seq', split_axis=0, concat_axis=0, tiled=True)  15.7 us
    pallas_call x2, Pallas kernels, encoder(): pl.pallas_call(functools.partial(encoder_kernel, lane, order), out_shape=...  13.1 us
    pallas_call x2, Pallas kernels, image_attention(): pl.pallas_call(functools.partial(image_kernel, factor, call), out_shape=(...  9.54 us
    convert_element_type x6, other arithmetic, add(): return (one.astype(jnp.float32) + other.astype(jnp.float32)).astype(dtype)  6.96 us
    unnamed x32, local copies, waits for them, and re-layouts  4.4 us
  transfers between devices with their start and end apart: 27, of which 15 were waited for; matrix products, arithmetic and copies ran while one was open for 6% of the time, Pallas kernels for 13%

profile of v4, /device:TPU:0, one launch (start us, length us, event | category | flops | bytes accessed | tf_op | source)
XLA Modules:
  0.0 165.8 jit_solution(15444667488737732059)
XLA Ops:
  1.3 1.0 copy-done.4
  2.3 0.9 pack.3
  3.2 0.7 stack.19.place_ref
  3.9 6.7 %encoder.2 = (bf16[8,16,1792]{2,1,0:T(8,128)(2,1)}, bf16[8,16,1792]{2,1,0:T(8,128)(2,1)}, bf16[256,1184]{1,0:T(8,128)(2,1)}) custom-call(s32[5]{0:T(128)} %stack.19.place_ref, bf16[1184,256]{1,0:T(8,128)(2,1)} %bitcast.43, bf16[1184,3584]{1,0:T(8,128)(2,1)} %weight_ref.3), custom_call_target="tpu_custom_call" | custom-call | flops 1086324736 | bytes 5767168 | tf_op jit(solution)/shard_map/encoder/pallas_call | solution.py:109
  10.6 0.5 collective-permute-start
  11.7 7.0 %all-to-all-start = ((bf16[16,128,128]{2,1,0:T(8,128)(2,1)}), bf16[16,128,128]{2,1,0:T(8,128)(2,1)S(1)}, u32[]{:S(2)}, u32[]{:S(2)}) async-start(bf16[16,128,128]{2,1,0:T(8,128)(2,1)} %pack.3), calls=%async_computation | async-start | bytes 1048576 | tf_op jit(solution)/shard_map/all_to_all | solution.py:478
  18.7 0.5 collective-permute-start.4
  19.2 6.4 %encoder.3 = (bf16[8,16,1792]{2,1,0:T(8,128)(2,1)}, bf16[8,16,1792]{2,1,0:T(8,128)(2,1)}) custom-call(s32[5]{0:T(128)} %stack.19.place_ref, bf16[256,1184]{1,0:T(8,128)(2,1)} %get-tuple-element.55.act_ref, bf16[1184,3584]{1,0:T(8,128)(2,1)} %weight_ref.3), custom_call_target="tpu_custom_call" | custom-call | flops 1086324736 | bytes 5767168 | tf_op jit(solution)/shard_map/encoder/pallas_call | solution.py:109
  25.8 2.2 %add_convert_fusion.1 = (bf16[4,16,1792]{2,1,0:T(8,128)(2,1)}, f32[4,16,1792]{2,1,0:T(8,128)}) fusion(bf16[8,16,1792]{2,1,0:T(8,128)(2,1)} %collective-permute-done, bf16[8,16,1792]{2,1,0:T(8,128)(2,1)S(1)} %copy-done.12), kind=kLoop, calls=%fused_computation.4 | loop fusion | flops 802816 | bytes 1605632 | tf_op jit(solution)/shard_map/convert_element_type | solution.py:441
  27.9 1.0 convert_add_fusion
  28.9 1.9 %collective-permute-start.2 = (bf16[4,16,1792]{2,1,0:T(8,128)(2,1)}, bf16[4,16,1792]{2,1,0:T(8,128)(2,1)}, u32[]{:S(2)}, u32[]{:S(2)}) collective-permute-start(bf16[4,16,1792]{2,1,0:T(8,128)(2,1)} %get-tuple-element.58), channel_id=1, source_target_pairs={{0,2},{1,3},{2,0},{3,1},{4,6},{5,7},{6,4},{7,5},{8,10},{9,11},{10,... | collective-permute-start | bytes 688136 | tf_op jit(solution)/shard_map/ppermute | solution.py:28
  30.8 1.5 collective-permute-start.3
  32.7 0.9 pack.4
  33.6 4.2 %all-to-all-start.1 = ((bf16[16,128,128]{2,1,0:T(8,128)(2,1)}), bf16[16,128,128]{2,1,0:T(8,128)(2,1)}, u32[]{:S(2)}, u32[]{:S(2)}) async-start(bf16[16,128,128]{2,1,0:T(8,128)(2,1)} %pack.4), calls=%async_computation.1 | async-start | bytes 1048576 | tf_op jit(solution)/shard_map/all_to_all | solution.py:478
  38.0 0.5 collective-permute-done.3
  38.5 1.2 fusion
  39.8 2.4 %collective-permute-start.9 = (bf16[2,16,1792]{2,1,0:T(8,128)(2,1)S(1)}, bf16[2,16,1792]{2,1,0:T(8,128)(2,1)S(1)}, u32[]{:S(2)}, u32[]{:S(2)}) collective-permute-start(bf16[2,16,1792]{2,1,0:T(8,128)(2,1)S(1)} %get-tuple-element.106), channel_id=1, source_target_pairs={{0,8},{1,9},{2,10},{3,11},{4,12},{5,13},{6,14},{7,15},{8,0},{9,1},... | collective-permute-start | bytes 344072 | tf_op jit(solution)/shard_map/ppermute | solution.py:28
  42.2 1.2 fusion.1
  43.4 1.5 collective-permute-start.7
  45.0 13.0 %collective-permute-done.9 = bf16[2,16,1792]{2,1,0:T(8,128)(2,1)S(1)} collective-permute-done((bf16[2,16,1792]{2,1,0:T(8,128)(2,1)S(1)}, bf16[2,16,1792]{2,1,0:T(8,128)(2,1)S(1)}, u32[]{:S(2)}, u32[]{:S(2)}) %collective-permute-start.9) | collective-permute-done | bytes 114720 | tf_op jit(solution)/shard_map/ppermute | solution.py:28
  57.9 0.7 fusion.8
  58.6 1.5 collective-permute-start.10
  60.1 0.7 fusion.9
  60.7 0.8 fusion.13
  61.5 1.4 collective-permute-done.10
  63.0 3.2 %collective-permute-done.8 = bf16[1,16,1792]{2,1,0:T(8,128)(2,1)} collective-permute-done((bf16[1,16,1792]{2,1,0:T(8,128)(2,1)}, bf16[1,16,1792]{2,1,0:T(8,128)(2,1)}, u32[]{:S(2)}, u32[]{:S(2)}) %collective-permute-start.8) | collective-permute-done | bytes 57376 | tf_op jit(solution)/shard_map/ppermute | solution.py:28
  66.1 1.2 multiply_reduce_fusion
  67.3 1.1 multiply_convert_fusion
  68.5 0.6 collective-permute-start.12
  69.1 3.6 %collective-permute-done.12 = bf16[16,1792]{1,0:T(8,128)(2,1)S(1)} collective-permute-done((bf16[16,1792]{1,0:T(8,128)(2,1)S(1)}, bf16[16,1792]{1,0:T(8,128)(2,1)S(1)}, u32[]{:S(2)}, u32[]{:S(2)}) %collective-permute-start.12) | collective-permute-done | bytes 57376 | tf_op jit(solution)/shard_map/ppermute | solution.py:28
  72.7 1.4 collective-permute-done.11
  74.3 2.1 %collective-permute-start.14 = (bf16[32,1792]{1,0:T(8,128)(2,1)S(1)}, bf16[32,1792]{1,0:T(8,128)(2,1)S(1)}, u32[]{:S(2)}, u32[]{:S(2)}) collective-permute-start(bf16[32,1792]{1,0:T(8,128)(2,1)S(1)} %pad_maximum_fusion.3), channel_id=1, source_target_pairs={{0,8},{1,9},{2,10},{3,11},{4,12},{5,13},{6,14},{7,15},{8,0},{9,1},... | collective-permute-start | bytes 344072 | tf_op jit(solution)/shard_map/ppermute | solution.py:28
  76.8 0.9 pack.5
  77.6 2.6 %collective-permute-done.13 = bf16[32,1792]{1,0:T(8,128)(2,1)S(1)} collective-permute-done((bf16[32,1792]{1,0:T(8,128)(2,1)S(1)}, bf16[32,1792]{1,0:T(8,128)(2,1)S(1)}, u32[]{:S(2)}, u32[]{:S(2)}) %collective-permute-start.13) | collective-permute-done | bytes 114720 | tf_op jit(solution)/shard_map/ppermute | solution.py:28
  80.3 0.7 pad_maximum_fusion.refs_0_
  81.0 0.7 pad_maximum_fusion.1.refs_2_
  81.7 4.4 %all-to-all-start.2 = ((bf16[16,128,128]{2,1,0:T(8,128)(2,1)}), bf16[16,128,128]{2,1,0:T(8,128)(2,1)}, u32[]{:S(2)}, u32[]{:S(2)}) async-start(bf16[16,128,128]{2,1,0:T(8,128)(2,1)} %pack.5), calls=%async_computation.2 | async-start | bytes 1048576 | tf_op jit(solution)/shard_map/all_to_all | solution.py:478
  86.2 1.6 collective-permute-start.15
  87.8 1.5 collective-permute-start.16
  90.0 8.2 %collective-permute-done.15.refs_1_ = bf16[64,1792]{1,0:T(8,128)(2,1)S(1)} collective-permute-done((bf16[64,1792]{1,0:T(8,128)(2,1)}, bf16[64,1792]{1,0:T(8,128)(2,1)S(1)}, u32[]{:S(2)}, u32[]{:S(2)}) %collective-permute-start.15) | collective-permute-done | bytes 229408 | tf_op jit(solution)/shard_map/ppermute | solution.py:28
  98.3 4.0 %collective-permute-done.16.refs_3_ = bf16[64,1792]{1,0:T(8,128)(2,1)S(1)} collective-permute-done((bf16[64,1792]{1,0:T(8,128)(2,1)}, bf16[64,1792]{1,0:T(8,128)(2,1)S(1)}, u32[]{:S(2)}, u32[]{:S(2)}) %collective-permute-start.16) | collective-permute-done | bytes 229408 | tf_op jit(solution)/shard_map/ppermute | solution.py:28
  102.3 0.9 copy-done.2
  103.2 0.9 copy-done.3
  104.2 3.7 %project.1 = (bf16[4,144,256]{2,1,0:T(8,128)(2,1)S(1)}, bf16[4,144,256]{2,1,0:T(8,128)(2,1)S(1)}, bf16[4,144,256]{2,1,0:T(8,128)(2,1)S(1)}, bf16[4,144,256]{2,1,0:T(8,128)(2,1)S(1)}) custom-call(s32[5]{0:T(128)S(1)} %copy-done.7, bf16[64,1792]{1,0:T(8,128)(2,1)S(1)} %copy-done.2, bf16[64,1792]{1,0:T(8,128)(2,1)S(1)} %collective-permute-done.15.refs_1_, ...), custom_call_target="tpu_custom_call" | custom-call | flops 754974720 | bytes 7864320 | tf_op jit(solution)/shard_map/project/pallas_call | solution.py:216
  107.9 0.7 copy-done.5
  108.6 0.7 copy-done.6
  109.3 1.5 collective-permute-start.17
  110.8 0.6 collective-permute-start.18
  111.4 6.5 %collective-permute-done.17 = bf16[4,144,256]{2,1,0:T(8,128)(2,1)S(1)} collective-permute-done((bf16[4,144,256]{2,1,0:T(8,128)(2,1)S(1)}, bf16[4,144,256]{2,1,0:T(8,128)(2,1)S(1)}, u32[]{:S(2)}, u32[]{:S(2)}) %collective-permute-start.17) | collective-permute-done | bytes 294944 | tf_op jit(solution)/shard_map/ppermute | solution.py:28
  117.9 1.2 collective-permute-done.18
  119.1 1.0 convert_add_fusion.2
  120.2 2.6 %collective-permute-start.20 = (bf16[2,144,256]{2,1,0:T(8,128)(2,1)S(1)}, bf16[2,144,256]{2,1,0:T(8,128)(2,1)S(1)}, u32[]{:S(2)}, u32[]{:S(2)}) collective-permute-start(bf16[2,144,256]{2,1,0:T(8,128)(2,1)S(1)} %get-tuple-element.111), channel_id=1, source_target_pairs={{0,8},{1,9},{2,10},{3,11},{4,12},{5,13},{6,14},{7,15},{8,0},{9,1},... | collective-permute-start | bytes 442376 | tf_op jit(solution)/shard_map/ppermute | solution.py:28
  122.7 1.0 add_convert_fusion.3
  123.8 0.6 collective-permute-start.19
  124.3 4.8 %image_attention.2 = (f32[1024,128]{1,0:T(8,128)S(1)}, f32[1024,128]{1,0:T(8,128)S(1)}) custom-call(bf16[16,128,128]{2,1,0:T(8,128)(2,1)S(1)} %all-to-all-done.queries_ref, bf16[16,128,128]{2,1,0:T(8,128)(2,1)} %all-to-all-done.1.keys_ref, bf16[16,128,128]{2,1,0:T(8,128)(2,1)} %all-to-all-done.2.values_ref), custom_call_target="tpu_custom_call" | custom-call | flops 1073741824 | bytes 2359296 | tf_op jit(solution)/shard_map/image_attention/pallas_call | solution.py:365
  129.1 0.9 collective-permute-done.19
  130.1 0.7 collective-permute-start.22
  130.9 4.8 %image_attention.3 = (f32[1024,128]{1,0:T(8,128)S(1)}, f32[1024,128]{1,0:T(8,128)S(1)}) custom-call(bf16[16,128,128]{2,1,0:T(8,128)(2,1)S(1)} %all-to-all-done.queries_ref, bf16[16,128,128]{2,1,0:T(8,128)(2,1)} %all-to-all-done.1.keys_ref, bf16[16,128,128]{2,1,0:T(8,128)(2,1)} %all-to-all-done.2.values_ref), custom_call_target="tpu_custom_call" | custom-call | flops 1073741824 | bytes 2359296 | tf_op jit(solution)/shard_map/image_attention/pallas_call | solution.py:365
  135.7 1.2 collective-permute-done.21
  136.9 0.7 combine.1
  137.7 1.2 collective-permute-done.23.refs_5_
  139.0 3.8 %finish.1 = bf16[16,160,128]{2,1,0:T(8,128)(2,1)S(1)} custom-call(s32[5]{0:T(128)S(1)} %copy-done.7, bf16[16,128,128]{2,1,0:T(8,128)(2,1)S(1)} %all-to-all-done.queries_ref, f32[1024,128]{1,0:T(8,128)S(1)} %get-tuple-element.90.refs_0_, f32[1024,128]{1,0:T(8,128)S(1)} %get-tuple-element.91.refs_1_, f32[1024,128]{1,0:T(8,128)S(1)} %get-tuple-element.94.refs_2_, ...), custom_call_target="tpu_custom_call" | custom-call | flops 268435456 | bytes 3145728 | tf_op jit(solution)/shard_map/finish/pallas_call | solution.py:425
  142.7 22.0 %all_to_all.20.blocks_ref = bf16[16,160,128]{2,1,0:T(8,128)(2,1)S(1)} all-to-all(bf16[16,160,128]{2,1,0:T(8,128)(2,1)S(1)} %finish.1), channel_id=1, replica_groups=mesh['dp'=2,'seq'=16] {'seq'}, dimensions={0} | all-to-all | bytes 1310720 | tf_op jit(solution)/shard_map/all_to_all | solution.py:478
  164.8 1.0 unpack.1
  (59 shorter events, 2.1 us)
Async XLA Ops:
  1.3 1.0 copy-start.4
  3.9 7.3 %copy-start = (bf16[192,4096]{1,0:T(8,128)(2,1)S(1)}, bf16[192,4096]{1,0:T(8,128)(2,1)}, u32[]{:S(2)}) copy-start(bf16[192,4096]{1,0:T(8,128)(2,1)} %refs_7_.1) | copy-start | bytes 4718596
  3.9 14.8 %copy-start.1 = (bf16[3584,192]{0,1:T(8,128)(2,1)S(1)}, bf16[3584,192]{0,1:T(8,128)(2,1)}, u32[]{:S(2)}) copy-start(bf16[3584,192]{0,1:T(8,128)(2,1)} %param.13) | copy-start | bytes 4128772
  10.6 15.1 %collective-permute-start = (bf16[8,16,1792]{2,1,0:T(8,128)(2,1)}, bf16[8,16,1792]{2,1,0:T(8,128)(2,1)}, u32[]{:S(2)}, u32[]{:S(2)}) collective-permute-start(bf16[8,16,1792]{2,1,0:T(8,128)(2,1)} %get-tuple-element.54), channel_id=1, source_target_pairs={{0,1},{1,0},{2,3},{3,2},{4,5},{5,4},{6,7},{7,6},{8,9},{9,8},{10,11... | collective-permute-start | bytes 1376264 | tf_op jit(solution)/shard_map/ppermute | solution.py:28
  11.2 27.4 %collective-permute-start.5 = (bf16[192,4096]{1,0:T(8,128)(2,1)S(1)}, bf16[192,4096]{1,0:T(8,128)(2,1)}, u32[]{:S(2)}, u32[]{:S(2)}) collective-permute-start(bf16[192,4096]{1,0:T(8,128)(2,1)S(1)} %copy-done), channel_id=1, source_target_pairs={{0,1},{1,0},{2,3},{3,2},{4,5},{5,4},{6,7},{7,6},{8,9},{9,8},{10,11... | collective-permute-start | bytes 4718600 | tf_op jit(solution)/shard_map/ppermute | solution.py:28
  11.2 26.6 %collective-permute-start.6 = (bf16[2,192,256]{2,1,0:T(8,128)(2,1)}, bf16[2,192,256]{2,1,0:T(8,128)(2,1)}, u32[]{:S(2)}, u32[]{:S(2)}) collective-permute-start(bf16[2,192,256]{2,1,0:T(8,128)(2,1)} %bitcast.8.refs_9_), channel_id=1, source_target_pairs={{0,1},{1,0},{2,3},{3,2},{4,5},{5,4},{6,7},{7,6},{8,9},{9,8},{10,11... | collective-permute-start | bytes 589832 | tf_op jit(solution)/shard_map/ppermute | solution.py:28
  11.7 21.9 %all-to-all-start = ((bf16[16,128,128]{2,1,0:T(8,128)(2,1)}), bf16[16,128,128]{2,1,0:T(8,128)(2,1)S(1)}, u32[]{:S(2)}, u32[]{:S(2)}) async-start(bf16[16,128,128]{2,1,0:T(8,128)(2,1)} %pack.3), calls=%async_computation | async-start | bytes 1048576 | tf_op jit(solution)/shard_map/all_to_all | solution.py:478
  18.7 19.8 %collective-permute-start.4 = (bf16[192,3584]{1,0:T(8,128)(2,1)S(1)}, bf16[192,3584]{1,0:T(8,128)(2,1)}, u32[]{:S(2)}, u32[]{:S(2)}) collective-permute-start(bf16[192,3584]{1,0:T(8,128)(2,1)S(1)} %bitcast.38), channel_id=1, source_target_pairs={{0,1},{1,0},{2,3},{3,2},{4,5},{5,4},{6,7},{7,6},{8,9},{9,8},{10,11... | collective-permute-start | bytes 4128776 | tf_op jit(solution)/shard_map/ppermute | solution.py:28
  19.2 6.6 %copy-start.12 = (bf16[8,16,1792]{2,1,0:T(8,128)(2,1)S(1)}, bf16[8,16,1792]{2,1,0:T(8,128)(2,1)}, u32[]{:S(2)}) copy-start(bf16[8,16,1792]{2,1,0:T(8,128)(2,1)} %get-tuple-element.53) | copy-start | bytes 1376260
  25.6 2.3 %copy-start.13 = (bf16[8,16,1792]{2,1,0:T(8,128)(2,1)S(1)}, bf16[8,16,1792]{2,1,0:T(8,128)(2,1)}, u32[]{:S(2)}) copy-start(bf16[8,16,1792]{2,1,0:T(8,128)(2,1)} %get-tuple-element.56) | copy-start | bytes 1376260
  25.6 2.3 %collective-permute-start.1 = (bf16[8,16,1792]{2,1,0:T(8,128)(2,1)}, bf16[8,16,1792]{2,1,0:T(8,128)(2,1)S(1)}, u32[]{:S(2)}, u32[]{:S(2)}) collective-permute-start(bf16[8,16,1792]{2,1,0:T(8,128)(2,1)} %get-tuple-element.57), channel_id=1, source_target_pairs={{0,1},{1,0},{2,3},{3,2},{4,5},{5,4},{6,7},{7,6},{8,9},{9,8},{10,11... | collective-permute-start | bytes 1376264 | tf_op jit(solution)/shard_map/ppermute | solution.py:28
  25.8 6.5 %copy-start.8 = (bf16[1,128,2,2048]{3,2,1,0:T(2,128)(2,1)S(1)}, bf16[1,128,2,2048]{3,2,1,0:T(2,128)(2,1)}, u32[]{:S(2)}) copy-start(bf16[1,128,2,2048]{3,2,1,0:T(2,128)(2,1)} %param.19) | copy-start | bytes 3145732
  28.9 9.1 %collective-permute-start.2 = (bf16[4,16,1792]{2,1,0:T(8,128)(2,1)}, bf16[4,16,1792]{2,1,0:T(8,128)(2,1)}, u32[]{:S(2)}, u32[]{:S(2)}) collective-permute-start(bf16[4,16,1792]{2,1,0:T(8,128)(2,1)} %get-tuple-element.58), channel_id=1, source_target_pairs={{0,2},{1,3},{2,0},{3,1},{4,6},{5,7},{6,4},{7,5},{8,10},{9,11},{10,... | collective-permute-start | bytes 688136 | tf_op jit(solution)/shard_map/ppermute | solution.py:28
  30.8 7.7 %collective-permute-start.3 = (bf16[4,16,1792]{2,1,0:T(8,128)(2,1)}, bf16[4,16,1792]{2,1,0:T(8,128)(2,1)}, u32[]{:S(2)}, u32[]{:S(2)}) collective-permute-start(bf16[4,16,1792]{2,1,0:T(8,128)(2,1)} %get-tuple-element.59), channel_id=1, source_target_pairs={{0,4},{1,5},{2,6},{3,7},{4,0},{5,1},{6,2},{7,3},{8,12},{9,13},{10,... | collective-permute-start | bytes 688136 | tf_op jit(solution)/shard_map/ppermute | solution.py:28
  33.6 27.9 %all-to-all-start.1 = ((bf16[16,128,128]{2,1,0:T(8,128)(2,1)}), bf16[16,128,128]{2,1,0:T(8,128)(2,1)}, u32[]{:S(2)}, u32[]{:S(2)}) async-start(bf16[16,128,128]{2,1,0:T(8,128)(2,1)} %pack.4), calls=%async_computation.1 | async-start | bytes 1048576 | tf_op jit(solution)/shard_map/all_to_all | solution.py:478
  39.8 18.2 %copy-start.10 = (f32[2,16,1792]{2,1,0:T(8,128)}, f32[2,16,1792]{2,1,0:T(8,128)S(1)}, u32[]{:S(2)}) copy-start(f32[2,16,1792]{2,1,0:T(8,128)S(1)} %get-tuple-element.107) | copy-start | bytes 688132
  39.8 18.2 %collective-permute-start.9 = (bf16[2,16,1792]{2,1,0:T(8,128)(2,1)S(1)}, bf16[2,16,1792]{2,1,0:T(8,128)(2,1)S(1)}, u32[]{:S(2)}, u32[]{:S(2)}) collective-permute-start(bf16[2,16,1792]{2,1,0:T(8,128)(2,1)S(1)} %get-tuple-element.106), channel_id=1, source_target_pairs={{0,8},{1,9},{2,10},{3,11},{4,12},{5,13},{6,14},{7,15},{8,0},{9,1},... | collective-permute-start | bytes 344072 | tf_op jit(solution)/shard_map/ppermute | solution.py:28
  43.4 16.6 %copy-start.11 = (f32[2,16,1792]{2,1,0:T(8,128)}, f32[2,16,1792]{2,1,0:T(8,128)S(1)}, u32[]{:S(2)}) copy-start(f32[2,16,1792]{2,1,0:T(8,128)S(1)} %get-tuple-element.109) | copy-start | bytes 688132
  43.4 16.6 %collective-permute-start.7 = (bf16[2,16,1792]{2,1,0:T(8,128)(2,1)S(1)}, bf16[2,16,1792]{2,1,0:T(8,128)(2,1)S(1)}, u32[]{:S(2)}, u32[]{:S(2)}) collective-permute-start(bf16[2,16,1792]{2,1,0:T(8,128)(2,1)S(1)} %get-tuple-element.108), channel_id=1, source_target_pairs={{0,4},{1,5},{2,6},{3,7},{4,0},{5,1},{6,2},{7,3},{8,12},{9,13},{10,... | collective-permute-start | bytes 344072 | tf_op jit(solution)/shard_map/ppermute | solution.py:28
  57.9 2.8 %copy-start.14 = (bf16[2,16,1792]{2,1,0:T(8,128)(2,1)}, bf16[2,16,1792]{2,1,0:T(8,128)(2,1)S(1)}, u32[]{:S(2)}) copy-start(bf16[2,16,1792]{2,1,0:T(8,128)(2,1)S(1)} %collective-permute-done.9) | copy-start | bytes 344068
  58.6 4.4 %collective-permute-start.10 = (bf16[1,16,1792]{2,1,0:T(8,128)(2,1)}, bf16[1,16,1792]{2,1,0:T(8,128)(2,1)S(1)}, u32[]{:S(2)}, u32[]{:S(2)}) collective-permute-start(bf16[1,16,1792]{2,1,0:T(8,128)(2,1)} %fusion.8), channel_id=1, source_target_pairs={{0,2},{1,3},{2,0},{3,1},{4,6},{5,7},{6,4},{7,5},{8,10},{9,11},{10,... | collective-permute-start | bytes 172040 | tf_op jit(solution)/shard_map/ppermute | solution.py:28
  60.1 0.7 copy-start.15
  60.7 5.4 %collective-permute-start.8 = (bf16[1,16,1792]{2,1,0:T(8,128)(2,1)}, bf16[1,16,1792]{2,1,0:T(8,128)(2,1)}, u32[]{:S(2)}, u32[]{:S(2)}) collective-permute-start(bf16[1,16,1792]{2,1,0:T(8,128)(2,1)} %fusion.9), channel_id=1, source_target_pairs={{0,8},{1,9},{2,10},{3,11},{4,12},{5,13},{6,14},{7,15},{8,0},{9,1},... | collective-permute-start | bytes 172040 | tf_op jit(solution)/shard_map/ppermute | solution.py:28
  61.5 14.8 %copy-start.9 = (bf16[1,128,2,2048]{3,2,1,0:T(2,128)(2,1)S(1)}, bf16[1,128,2,2048]{3,2,1,0:T(2,128)(2,1)}, u32[]{:S(2)}) copy-start(bf16[1,128,2,2048]{3,2,1,0:T(2,128)(2,1)} %param.19) | copy-start | bytes 3145732
  68.5 4.2 %collective-permute-start.12 = (bf16[16,1792]{1,0:T(8,128)(2,1)S(1)}, bf16[16,1792]{1,0:T(8,128)(2,1)S(1)}, u32[]{:S(2)}, u32[]{:S(2)}) collective-permute-start(bf16[16,1792]{1,0:T(8,128)(2,1)S(1)} %get-tuple-element.120), channel_id=1, source_target_pairs={{0,2},{1,3},{2,0},{3,1},{4,6},{5,7},{6,4},{7,5},{8,10},{9,11},{10,... | collective-permute-start | bytes 172040 | tf_op jit(solution)/shard_map/ppermute | solution.py:28
  69.1 5.1 %collective-permute-start.11 = (bf16[16,1792]{1,0:T(8,128)(2,1)S(1)}, bf16[16,1792]{1,0:T(8,128)(2,1)S(1)}, u32[]{:S(2)}, u32[]{:S(2)}) collective-permute-start(bf16[16,1792]{1,0:T(8,128)(2,1)S(1)} %get-tuple-element.121), channel_id=1, source_target_pairs={{0,8},{1,9},{2,10},{3,11},{4,12},{5,13},{6,14},{7,15},{8,0},{9,1},... | collective-permute-start | bytes 172040 | tf_op jit(solution)/shard_map/ppermute | solution.py:28
  74.2 6.1 %collective-permute-start.13 = (bf16[32,1792]{1,0:T(8,128)(2,1)S(1)}, bf16[32,1792]{1,0:T(8,128)(2,1)S(1)}, u32[]{:S(2)}, u32[]{:S(2)}) collective-permute-start(bf16[32,1792]{1,0:T(8,128)(2,1)S(1)} %pad_maximum_fusion.2), channel_id=1, source_target_pairs={{0,4},{1,5},{2,6},{3,7},{4,0},{5,1},{6,2},{7,3},{8,12},{9,13},{10,... | collective-permute-start | bytes 344072 | tf_op jit(solution)/shard_map/ppermute | solution.py:28
  74.3 6.7 %collective-permute-start.14 = (bf16[32,1792]{1,0:T(8,128)(2,1)S(1)}, bf16[32,1792]{1,0:T(8,128)(2,1)S(1)}, u32[]{:S(2)}, u32[]{:S(2)}) collective-permute-start(bf16[32,1792]{1,0:T(8,128)(2,1)S(1)} %pad_maximum_fusion.3), channel_id=1, source_target_pairs={{0,8},{1,9},{2,10},{3,11},{4,12},{5,13},{6,14},{7,15},{8,0},{9,1},... | collective-permute-start | bytes 344072 | tf_op jit(solution)/shard_map/ppermute | solution.py:28
  76.7 25.6 %copy-start.7 = (s32[5]{0:T(128)S(1)}, s32[5]{0:T(128)}, u32[]{:S(2)}) copy-start(s32[5]{0:T(128)} %stack.19.place_ref) | copy-start | bytes 64
  81.7 37.4 %all-to-all-start.2 = ((bf16[16,128,128]{2,1,0:T(8,128)(2,1)}), bf16[16,128,128]{2,1,0:T(8,128)(2,1)}, u32[]{:S(2)}, u32[]{:S(2)}) async-start(bf16[16,128,128]{2,1,0:T(8,128)(2,1)} %pack.5), calls=%async_computation.2 | async-start | bytes 1048576 | tf_op jit(solution)/shard_map/all_to_all | solution.py:478
  86.2 12.1 %collective-permute-start.15 = (bf16[64,1792]{1,0:T(8,128)(2,1)}, bf16[64,1792]{1,0:T(8,128)(2,1)S(1)}, u32[]{:S(2)}, u32[]{:S(2)}) collective-permute-start(bf16[64,1792]{1,0:T(8,128)(2,1)} %pad_maximum_fusion.refs_0_), channel_id=1, source_target_pairs={{0,2},{1,3},{2,0},{3,1},{4,6},{5,7},{6,4},{7,5},{8,10},{9,11},{10,... | collective-permute-start | bytes 688136 | tf_op jit(solution)/shard_map/ppermute | solution.py:28
  87.8 14.5 %collective-permute-start.16 = (bf16[64,1792]{1,0:T(8,128)(2,1)}, bf16[64,1792]{1,0:T(8,128)(2,1)S(1)}, u32[]{:S(2)}, u32[]{:S(2)}) collective-permute-start(bf16[64,1792]{1,0:T(8,128)(2,1)} %pad_maximum_fusion.1.refs_2_), channel_id=1, source_target_pairs={{0,4},{1,5},{2,6},{3,7},{4,0},{5,1},{6,2},{7,3},{8,12},{9,13},{10,... | collective-permute-start | bytes 688136 | tf_op jit(solution)/shard_map/ppermute | solution.py:28
  102.3 0.9 copy-start.2
  103.2 0.9 copy-start.3
  107.9 0.7 copy-start.5
  108.6 0.7 copy-start.6
  109.3 8.5 %collective-permute-start.17 = (bf16[4,144,256]{2,1,0:T(8,128)(2,1)S(1)}, bf16[4,144,256]{2,1,0:T(8,128)(2,1)S(1)}, u32[]{:S(2)}, u32[]{:S(2)}) collective-permute-start(bf16[4,144,256]{2,1,0:T(8,128)(2,1)S(1)} %get-tuple-element.75), channel_id=1, source_target_pairs={{0,2},{1,3},{2,0},{3,1},{4,6},{5,7},{6,4},{7,5},{8,10},{9,11},{10,... | collective-permute-start | bytes 884744 | tf_op jit(solution)/shard_map/ppermute | solution.py:28
  110.8 8.3 %collective-permute-start.18 = (bf16[4,144,256]{2,1,0:T(8,128)(2,1)S(1)}, bf16[4,144,256]{2,1,0:T(8,128)(2,1)S(1)}, u32[]{:S(2)}, u32[]{:S(2)}) collective-permute-start(bf16[4,144,256]{2,1,0:T(8,128)(2,1)S(1)} %get-tuple-element.76), channel_id=1, source_target_pairs={{0,4},{1,5},{2,6},{3,7},{4,0},{5,1},{6,2},{7,3},{8,12},{9,13},{10,... | collective-permute-start | bytes 884744 | tf_op jit(solution)/shard_map/ppermute | solution.py:28
  120.2 9.0 %collective-permute-start.20 = (bf16[2,144,256]{2,1,0:T(8,128)(2,1)S(1)}, bf16[2,144,256]{2,1,0:T(8,128)(2,1)S(1)}, u32[]{:S(2)}, u32[]{:S(2)}) collective-permute-start(bf16[2,144,256]{2,1,0:T(8,128)(2,1)S(1)} %get-tuple-element.111), channel_id=1, source_target_pairs={{0,8},{1,9},{2,10},{3,11},{4,12},{5,13},{6,14},{7,15},{8,0},{9,1},... | collective-permute-start | bytes 442376 | tf_op jit(solution)/shard_map/ppermute | solution.py:28
  123.8 6.3 %collective-permute-start.19 = (bf16[2,144,256]{2,1,0:T(8,128)(2,1)S(1)}, bf16[2,144,256]{2,1,0:T(8,128)(2,1)S(1)}, u32[]{:S(2)}, u32[]{:S(2)}) collective-permute-start(bf16[2,144,256]{2,1,0:T(8,128)(2,1)S(1)} %get-tuple-element.112), channel_id=1, source_target_pairs={{0,4},{1,5},{2,6},{3,7},{4,0},{5,1},{6,2},{7,3},{8,12},{9,13},{10,... | collective-permute-start | bytes 442376 | tf_op jit(solution)/shard_map/ppermute | solution.py:28
  130.1 5.6 %collective-permute-start.22 = (bf16[1,144,256]{2,1,0:T(8,128)(2,1)S(1)}, bf16[1,144,256]{2,1,0:T(8,128)(2,1)S(1)}, u32[]{:S(2)}, u32[]{:S(2)}) collective-permute-start(bf16[1,144,256]{2,1,0:T(8,128)(2,1)S(1)} %get-tuple-element.115), channel_id=1, source_target_pairs={{0,2},{1,3},{2,0},{3,1},{4,6},{5,7},{6,4},{7,5},{8,10},{9,11},{10,... | collective-permute-start | bytes 221192 | tf_op jit(solution)/shard_map/ppermute | solution.py:28
  130.8 6.1 %collective-permute-start.21 = (bf16[1,144,256]{2,1,0:T(8,128)(2,1)S(1)}, bf16[1,144,256]{2,1,0:T(8,128)(2,1)S(1)}, u32[]{:S(2)}, u32[]{:S(2)}) collective-permute-start(bf16[1,144,256]{2,1,0:T(8,128)(2,1)S(1)} %get-tuple-element.117), channel_id=1, source_target_pairs={{0,8},{1,9},{2,10},{3,11},{4,12},{5,13},{6,14},{7,15},{8,0},{9,1},... | collective-permute-start | bytes 221192 | tf_op jit(solution)/shard_map/ppermute | solution.py:28
  137.7 1.3 collective-permute-start.23

commit v5 on v4

--- a/solution.py
+++ b/solution.py
@@ -12,6 +12,7 @@
 HEADS = 16
 TEMB = 256
 MIB = 1024 * 1024
+DEPTH_BLOCK = 512
 
 epsilon = 1e-06
 
@@ -30,8 +31,7 @@
 
 def orders(chips):
     bits = [1 << i for i in range(chips.bit_length() - 1)]
-    turn = len(bits) // 2
-    return (bits, bits[turn:] + bits[:turn])
+    return (bits, [bits[1], bits[0]] + bits[2:])
 
 
 def position(chip, order):
@@ -58,17 +58,16 @@
 
 
 def encoder_kernel(lane, order, place_ref, act_ref, weight_ref, own_ref, other_ref, *refs):
-    *turned, held_ref, arrived = refs
+    *turned, held_ref, total_ref, arrived = refs
     chips, share, width = own_ref.shape
     at, core = place_ref[lane], place_ref[2]
     depth = weight_ref.shape[0]
-    tile = 256
+    starts = range(0, depth, DEPTH_BLOCK)
     loads = []
-    for start in range(0, width, tile):
+    for step, start in enumerate(starts):
+        rows = pl.ds(start, min(DEPTH_BLOCK, depth - start))
         load = pltpu.make_async_copy(
-            weight_ref.at[:, pl.ds(lane * width + start, tile)],
-            held_ref.at[:, pl.ds(start, tile)],
-            arrived.at[start // tile],
+            weight_ref.at[rows, pl.ds(lane * width, width)], held_ref.at[rows, :], arrived.at[step]
         )
         load.start()
         loads.append(load)
@@ -76,27 +75,30 @@
     if turned:
         (lhs_ref,) = turned
         lhs_ref[...] = act_ref[...].T
-    cut = depth // 256 * 256
     half = chips * share
     first = core == 0
-    for start in range(0, width, tile):
-        columns = slice(start, start + tile)
-        loads[start // tile].wait()
-        result = jnp.dot(
-            lhs_ref[:, :cut], held_ref[:cut, columns], preferred_element_type=jnp.float32
-        )
-        if cut < depth:
-            result += jnp.dot(
-                lhs_ref[:, cut:], held_ref[cut:, columns], preferred_element_type=jnp.float32
+    tile = 256
+    for step, start in enumerate(starts):
+        rows = slice(start, min(start + DEPTH_BLOCK, depth))
+        loads[step].wait()
+        for column in range(0, width, tile):
+            columns = slice(column, column + tile)
+            result = jnp.dot(
+                lhs_ref[:, rows], held_ref[rows, columns], preferred_element_type=jnp.float32
             )
-        own = jnp.where(first, result[:half], result[half:]).astype(own_ref.dtype)
-        other = jnp.where(first, result[half:], result[:half]).astype(own_ref.dtype)
-        own = own.reshape(chips, share, tile)
-        other = other.reshape(chips, share, tile)
-        for block in range(chips):
-            to = at ^ position(block, order)
-            own_ref[to, :, start : start + tile] = own[block]
-            other_ref[to, :, start : start + tile] = other[block]
+            if step > 0:
+                result += total_ref[:, columns]
+            if rows.stop < depth:
+                total_ref[:, columns] = result
+                continue
+            own = jnp.where(first, result[:half], result[half:]).astype(own_ref.dtype)
+            other = jnp.where(first, result[half:], result[:half]).astype(own_ref.dtype)
+            own = own.reshape(chips, share, tile)
+            other = other.reshape(chips, share, tile)
+            for block in range(chips):
+                to = at ^ position(block, order)
+                own_ref[to, :, columns] = own[block]
+                other_ref[to, :, columns] = other[block]
 
 
 def encoder(lane, order, place, act, weight):
@@ -113,7 +115,8 @@
         out_specs=(VMEM_SPEC,) * (2 + turn),
         scratch_shapes=[
             pltpu.VMEM((depth, width), weight.dtype),
-            pltpu.SemaphoreType.DMA((width // 256,)),
+            pltpu.VMEM((rows, width), jnp.float32),
+            pltpu.SemaphoreType.DMA((-(-depth // DEPTH_BLOCK),)),
         ],
         compiler_params=params(60),
         cost_estimate=pl.CostEstimate(
@@ -284,25 +287,31 @@
     )(place, *parts)
 
 
-def pack_kernel(copies, rows_ref, out_ref):
-    count = out_ref.shape[1]
+def pack_kernel(copies, queries_ref, keys_ref, values_ref, out_ref):
+    img_dev = keys_ref.shape[0]
+    part_rows = img_dev // copies
     for device in range(out_ref.shape[0]):
         head, copy = device // copies, device % copies
         span = slice(head * HEAD_DIM, (head + 1) * HEAD_DIM)
-        start = copy * count if count < rows_ref.shape[0] else 0
-        out_ref[device] = rows_ref[start : start + count, span]
-
-
-def pack(copies, rows, count):
+        out_ref[device, :img_dev, :] = keys_ref[:, span]
+        out_ref[device, img_dev : 2 * img_dev, :] = values_ref[:, span]
+        out_ref[device, 2 * img_dev :, :] = queries_ref[copy * part_rows : (copy + 1) * part_rows, span]
+
+
+def pack(copies, queries, keys, values):
+    img_dev = keys.shape[0]
+    rows = 2 * img_dev + img_dev // copies
     return pl.pallas_call(
         functools.partial(pack_kernel, copies),
-        out_shape=jax.ShapeDtypeStruct((HEADS * copies, count, HEAD_DIM), jnp.bfloat16),
-        in_specs=[VMEM_SPEC],
+        out_shape=jax.ShapeDtypeStruct((HEADS * copies, rows, HEAD_DIM), jnp.bfloat16),
+        in_specs=[VMEM_SPEC] * 3,
         out_specs=VMEM_SPEC,
         compiler_params=params(8),
-        cost_estimate=pl.CostEstimate(flops=0, bytes_accessed=4 * rows.size, transcendentals=0),
+        cost_estimate=pl.CostEstimate(
+            flops=0, bytes_accessed=4 * HEADS * copies * rows * HEAD_DIM, transcendentals=0
+        ),
         name="pack",
-    )(rows)
+    )(queries, keys, values)
 
 
 def unpack_kernel(copies, part_rows, blocks_ref, attended_ref, text_ref):
@@ -335,52 +344,58 @@
     )(blocks)
 
 
-def image_kernel(factor, call, queries_ref, keys_ref, values_ref, sum_ref, norm_ref):
-    part_rows = queries_ref.shape[1]
+def image_kernel(factor, call, img_dev, packed_ref, sum_ref, norm_ref, keys_ref, values_ref):
+    devices = packed_ref.shape[0]
+    part_rows = packed_ref.shape[1] - 2 * img_dev
+    for device in range(devices):
+        rows = slice(device * img_dev, (device + 1) * img_dev)
+        keys_ref[rows, :] = packed_ref[device, :img_dev, :]
+        values_ref[rows, :] = packed_ref[device, img_dev : 2 * img_dev, :]
     group = max(1, 256 // part_rows)
     rows = group * part_rows
     contract = (((1,), (1,)), ((), ()))
-    keys = keys_ref[...].reshape(-1, HEAD_DIM)
-    values = values_ref[...].reshape(-1, HEAD_DIM)
     steps = sum_ref.shape[0] // rows
     for step in range(steps):
         at = (call * steps + step) * group
         span = slice(step * rows, (step + 1) * rows)
-        queries = queries_ref[at : at + group].reshape(rows, HEAD_DIM)
-        scores = lax.dot_general(queries, keys, contract, preferred_element_type=jnp.float32) * factor
+        queries = packed_ref[at : at + group, 2 * img_dev :, :].reshape(rows, HEAD_DIM)
+        scores = lax.dot_general(queries, keys_ref[...], contract, preferred_element_type=jnp.float32)
+        scores = scores * factor
         top = jnp.max(scores, 1, keepdims=True)
         weights = jnp.exp2(scores - top)
         total = jnp.sum(weights, 1, keepdims=True)
         sum_ref[span, :] = jnp.dot(
-            weights.astype(jnp.bfloat16), values, preferred_element_type=jnp.float32
+            weights.astype(jnp.bfloat16), values_ref[...], preferred_element_type=jnp.float32
         )
         lane = lax.broadcasted_iota(jnp.int32, (rows, 128), 1)
         norm_ref[span, :] = jnp.where(lane < 64, top, total)
 
 
-def image_attention(queries, keys, values, factor, call, calls):
-    count = queries.shape[0] * queries.shape[1] // calls
-    total = keys.shape[0] * keys.shape[1]
+def image_attention(packed, img_dev, factor, call, calls):
+    devices = packed.shape[0]
+    keys = devices * img_dev
+    count = devices * (packed.shape[1] - 2 * img_dev) // calls
     out = jax.ShapeDtypeStruct((count, HEAD_DIM), jnp.float32)
     return pl.pallas_call(
-        functools.partial(image_kernel, factor, call),
+        functools.partial(image_kernel, factor, call, img_dev),
         out_shape=(out, out),
-        in_specs=[VMEM_SPEC] * 3,
+        in_specs=[VMEM_SPEC],
         out_specs=(VMEM_SPEC, VMEM_SPEC),
+        scratch_shapes=[pltpu.VMEM((keys, HEAD_DIM), jnp.bfloat16)] * 2,
         compiler_params=params(24),
         cost_estimate=pl.CostEstimate(
-            flops=4 * count * total * HEAD_DIM,
-            bytes_accessed=4 * total * HEAD_DIM + 10 * count * HEAD_DIM,
-            transcendentals=count * total,
+            flops=4 * count * keys * HEAD_DIM,
+            bytes_accessed=4 * keys * HEAD_DIM + 10 * count * HEAD_DIM,
+            transcendentals=count * keys,
         ),
         name="image_attention",
-    )(queries, keys, values)
-
-
-def finish_kernel(factor, calls, place_ref, queries_ref, *refs):
+    )(packed)
+
+
+def finish_kernel(factor, calls, img_dev, place_ref, packed_ref, *refs):
     images, (mine_ref, got_ref, out_ref) = refs[: 2 * calls], refs[2 * calls :]
     core, valid = place_ref[2], place_ref[4]
-    devices, part_rows = queries_ref.shape[0], queries_ref.shape[1]
+    devices, part_rows = packed_ref.shape[0], packed_ref.shape[1] - 2 * img_dev
     half = mine_ref.shape[0]
     contract = (((1,), (1,)), ((), ()))
     mine, got = mine_ref[...], got_ref[...]
@@ -394,7 +409,8 @@
     for step in range(devices // group):
         sum_ref, norm_ref = images[2 * (step // each)], images[2 * (step // each) + 1]
         span = slice(step % each * rows, (step % each + 1) * rows)
-        queries = queries_ref[step * group : (step + 1) * group].reshape(rows, HEAD_DIM)
+        queries = packed_ref[step * group : (step + 1) * group, 2 * img_dev :, :]
+        queries = queries.reshape(rows, HEAD_DIM)
         scores = lax.dot_general(queries, keys, contract, preferred_element_type=jnp.float32) * factor
         scores = jnp.where(text_position < valid, scores, -jnp.inf)
         before = norm_ref[span, 0:1]
@@ -418,12 +434,12 @@
         out_ref[device, part_rows:, :] = block.astype(out_ref.dtype)
 
 
-def finish(place, queries, images, mine, got, factor):
-    devices, part_rows = queries.shape[0], queries.shape[1]
+def finish(place, packed, images, mine, got, img_dev, factor):
+    devices, part_rows = packed.shape[0], packed.shape[1] - 2 * img_dev
     share = 2 * mine.shape[0] // devices
     count = devices * part_rows
     return pl.pallas_call(
-        functools.partial(finish_kernel, factor, len(images) // 2),
+        functools.partial(finish_kernel, factor, len(images) // 2, img_dev),
         out_shape=jax.ShapeDtypeStruct((devices, part_rows + 2 * share, HEAD_DIM), jnp.bfloat16),
         in_specs=[SMEM_SPEC] + [VMEM_SPEC] * (len(images) + 3),
         out_specs=VMEM_SPEC,
@@ -434,7 +450,7 @@
             transcendentals=count * 2 * mine.shape[0],
         ),
         name="finish",
-    )(place, queries, *images, mine, got)
+    )(place, packed, *images, mine, got)
 
 
 def add(one, other, dtype):
@@ -478,8 +494,6 @@
         return lax.all_to_all(rows, "seq", split_axis=0, concat_axis=0, tiled=True)
 
     act = enc_act[0].T
-    act, queries = tie((act, pack(copies, image_queries[0], part_rows)))
-    queries = exchange(queries)
     keep, sent = [], []
     for lane, order in enumerate(lanes):
         own, other, *turned = encoder(lane, order, place, act, down_weight)
@@ -490,13 +504,14 @@
         keep.append(add(own[: chips // 2], got[: chips // 2], jnp.float32))
     for step in range(rounds):
         if step == 0:
-            sent, image_key_values = tie((sent, image_key_values))
-            keys = exchange(pack(copies, image_key_values[0, :, 0], img_dev))
+            sent, image_key_values, image_queries = tie((sent, image_key_values, image_queries))
+            packed = pack(
+                copies, image_queries[0], image_key_values[0, :, 0], image_key_values[0, :, 1]
+            )
+            packed = exchange(packed)
         got = [swap(part, 2 * order[step]) for part, order in zip(sent, lanes)]
         if step == 0:
-            got, win1, kv1, mod1, queries = tie((got, win1, kv1, mod1, queries))
-        if step == 2:
-            got, keys = tie((got, keys))
+            got, win1, kv1, mod1 = tie((got, win1, kv1, mod1))
         half = keep[0].shape[0] // 2
         if half:
             sent = [add(mine[half:], part[half:], jnp.bfloat16) for mine, part in zip(keep, got)]
@@ -511,28 +526,27 @@
         (part * scale_rows * gains[lane * width : (lane + 1) * width]).astype(jnp.bfloat16)
         for lane, part in enumerate(summed)
     ]
+    images = []
+
     for step in reversed(range(rounds)):
-        if step == 1:
-            states, image_key_values = tie((states, image_key_values))
-            values = pack(copies, image_key_values[0, :, 1], img_dev)
         if step == 0:
-            states, values = tie((states, values))
-            values = exchange(values)
+            states, packed = tie((states, packed))
+            image = image_attention(packed, img_dev, factor, 0, 2)
         got = [swap(state, 2 * order[step]) for state, order in zip(states, lanes)]
         if step:
             states = [jnp.concatenate(pair, 0) for pair in zip(states, got)]
+    got, image = tie((got, image))
+    images += image
     states = [state for pair in zip(states, got) for state in pair]
 
     blocks = project(lanes, place, states, time, win0, win1, kv0, kv1, mod0, mod1)
     keep, sent = [blocks[0], blocks[2]], [blocks[1], blocks[3]]
-    images = []
     for step in range(rounds):
+        if step == 0:
+            sent, packed = tie((sent, packed))
+            image = image_attention(packed, img_dev, factor, 1, 2)
         got = [swap(part, 2 * order[step]) for part, order in zip(sent, lanes)]
         if step == 0:
-            got, values = tie((got, values))
-        elif step <= 2:
-            sent, queries = tie((sent, queries))
-            image = image_attention(queries, keys, values, factor, step - 1, 2)
             got, image = tie((got, image))
             images += image
         half = keep[0].shape[0] // 2
@@ -544,7 +558,7 @@
     mine, sent = combine(place, parts, chips, text_len // 2, model_width)
     got = swap(sent, 1)
 
-    back = exchange(finish(place, queries, images, mine, got, factor))
+    back = exchange(finish(place, packed, images, mine, got, img_dev, factor))
     attended, text_kv = unpack(copies, part_rows, back)
     return (attended[None], text_kv)
 

time: 167 us -> 146 us (0.87)
  other arithmetic: 12.9 us -> 5.82 us
  starting transfers between devices: 38.1 us -> 32.3 us
  Pallas kernels: 34.6 us -> 29.1 us
  local copies, waits for them, and re-layouts: 6.62 us -> 2.05 us
  waiting for transfers between devices: 49.3 us -> 52.7 us
    all_to_all x3 -> x1, starting transfers between devices: 15.7 us -> 4.15 us  [exchange(): return lax.all_to_all(rows, 'seq', split_axis=0, concat_axis=0, tiled=True)]
    ppermute x24, starting transfers between devices: 22.4 us -> 28.1 us  [swap(): return lax.ppermute(value, 'seq', [(i, i ^ mask) for i in range(devices)])]
    ppermute x24, waiting for transfers between devices: 49.3 us -> 52.7 us  [swap(): return lax.ppermute(value, 'seq', [(i, i ^ mask) for i in range(devices)])]
    unnamed x32 -> x24, local copies, waits for them, and re-layouts: 4.4 us -> 1.01 us
    convert_element_type x6 -> x9, other arithmetic: 6.96 us -> 3.64 us  [add(): return (one.astype(jnp.float32) + other.astype(jnp.float32)).astype(dtype)]
    pallas_call x2, Pallas kernels: 13.1 us -> 10.7 us  [encoder(): pl.pallas_call(functools.partial(encoder_kernel, lane, order), out_shape=...]
    pallas_call x3, Pallas kernels: 13.3 us -> 11.1 us  [the longest x2 7.31 us: image_attention(): pl.pallas_call(functools.partial(image_kernel, factor, call, img_dev), ou...]
  transfers between devices with their start and end apart: 27 -> 25, of which waited for: 15 -> 17; matrix products, arithmetic and copies ran while one was open for 6% -> 4% of each run, Pallas kernels for 13% -> 10%
where the time goes in v5:
time: 146 us
  waiting for transfers between devices  52.7 us (36%)
  starting transfers between devices  32.3 us (22%)
  Pallas kernels  29.1 us (20%)
  blocking collectives  21.8 us (15%)
  other arithmetic  5.82 us (4%)
  between operations  2.25 us (2%)
  local copies, waits for them, and re-layouts  2.05 us (1%)
    ppermute x24, waiting for transfers between devices, swap(): return lax.ppermute(value, 'seq', [(i, i ^ mask) for i in range(devices)])  52.7 us
    ppermute x24, starting transfers between devices, swap(): return lax.ppermute(value, 'seq', [(i, i ^ mask) for i in range(devices)])  28.1 us
    all_to_all x1, blocking collectives, exchange(): return lax.all_to_all(rows, 'seq', split_axis=0, concat_axis=0, tiled=True)  21.8 us
    pallas_call x2, Pallas kernels, encoder(): pl.pallas_call(functools.partial(encoder_kernel, lane, order), out_shape=...  10.7 us
    pallas_call x2, Pallas kernels, image_attention(): pl.pallas_call(functools.partial(image_kernel, factor, call, img_dev), ou...  7.31 us
    all_to_all x1, starting transfers between devices, exchange(): return lax.all_to_all(rows, 'seq', split_axis=0, concat_axis=0, tiled=True)  4.15 us
    pallas_call x1, Pallas kernels, project(): pl.pallas_call(functools.partial(project_kernel, lanes), out_shape=(out,)...  4.1 us
    pallas_call x1, Pallas kernels, finish(): pl.pallas_call(functools.partial(finish_kernel, factor, len(images) // 2,...  3.82 us
  transfers between devices with their start and end apart: 25, of which 17 were waited for; matrix products, arithmetic and copies ran while one was open for 4% of the time, Pallas kernels for 10%

profile of v5, /device:TPU:0, one launch (start us, length us, event | category | flops | bytes accessed | tf_op | source)
XLA Modules:
  0.0 146.1 jit_solution(2798574430020170301)
XLA Ops:
  1.3 0.6 stack.19.place_ref
  1.9 5.4 %encoder.2 = (bf16[8,16,1792]{2,1,0:T(8,128)(2,1)}, bf16[8,16,1792]{2,1,0:T(8,128)(2,1)}, bf16[256,1184]{1,0:T(8,128)(2,1)}) custom-call(s32[5]{0:T(128)} %stack.19.place_ref, bf16[1184,256]{1,0:T(8,128)(2,1)} %bitcast.43, bf16[1184,3584]{1,0:T(8,128)(2,1)} %weight_ref.3), custom_call_target="tpu_custom_call" | custom-call | flops 1086324736 | bytes 5767168 | tf_op jit(solution)/shard_map/encoder/pallas_call | solution.py:111
  7.3 0.5 collective-permute-start
  7.9 0.1 collective-permute-start.6
  7.9 0.4 collective-permute-start.4
  8.4 5.3 %encoder.3 = (bf16[8,16,1792]{2,1,0:T(8,128)(2,1)}, bf16[8,16,1792]{2,1,0:T(8,128)(2,1)}) custom-call(s32[5]{0:T(128)} %stack.19.place_ref, bf16[256,1184]{1,0:T(8,128)(2,1)} %get-tuple-element.44.act_ref, bf16[1184,3584]{1,0:T(8,128)(2,1)} %weight_ref.3), custom_call_target="tpu_custom_call" | custom-call | flops 1086324736 | bytes 5767168 | tf_op jit(solution)/shard_map/encoder/pallas_call | solution.py:111
  13.7 0.2 collective-permute-start.1
  13.8 0.4 collective-permute-start.5
  14.3 1.0 add_convert_fusion.1
  15.3 0.5 collective-permute-done.1
  15.8 1.0 convert_add_fusion
  16.8 2.6 %collective-permute-start.2 = (bf16[4,16,1792]{2,1,0:T(8,128)(2,1)}, bf16[4,16,1792]{2,1,0:T(8,128)(2,1)}, u32[]{:S(2)}, u32[]{:S(2)}) collective-permute-start(bf16[4,16,1792]{2,1,0:T(8,128)(2,1)} %get-tuple-element.47), channel_id=1, source_target_pairs={{0,2},{1,3},{2,0},{3,1},{4,6},{5,7},{6,4},{7,5},{8,10},{9,11},{10,... | collective-permute-start | bytes 688136 | tf_op jit(solution)/shard_map/ppermute | solution.py:29
  19.4 1.6 %collective-permute-start.3 = (bf16[4,16,1792]{2,1,0:T(8,128)(2,1)}, bf16[4,16,1792]{2,1,0:T(8,128)(2,1)}, u32[]{:S(2)}, u32[]{:S(2)}) collective-permute-start(bf16[4,16,1792]{2,1,0:T(8,128)(2,1)} %get-tuple-element.48), channel_id=1, source_target_pairs={{0,4},{1,5},{2,6},{3,7},{4,0},{5,1},{6,2},{7,3},{8,12},{9,13},{10,... | collective-permute-start | bytes 688136 | tf_op jit(solution)/shard_map/ppermute | solution.py:29
  21.0 0.3 copy.12
  21.4 0.1 slice_bitcast_fusion
  21.4 1.0 copy-done.2
  22.4 1.4 pack.1
  23.8 4.2 %all-to-all-start = ((bf16[16,384,128]{2,1,0:T(8,128)(2,1)}), bf16[16,384,128]{2,1,0:T(8,128)(2,1)S(1)}, u32[]{:S(2)}, u32[]{:S(2)}) async-start(bf16[16,384,128]{2,1,0:T(8,128)(2,1)} %pack.1), calls=%async_computation | async-start | bytes 3145728 | tf_op jit(solution)/shard_map/all_to_all | solution.py:494
  28.0 1.2 fusion
  29.3 1.8 %collective-permute-start.9 = (bf16[2,16,1792]{2,1,0:T(8,128)(2,1)S(1)}, bf16[2,16,1792]{2,1,0:T(8,128)(2,1)S(1)}, u32[]{:S(2)}, u32[]{:S(2)}) collective-permute-start(bf16[2,16,1792]{2,1,0:T(8,128)(2,1)S(1)} %get-tuple-element.88), channel_id=1, source_target_pairs={{0,2},{1,3},{2,0},{3,1},{4,6},{5,7},{6,4},{7,5},{8,10},{9,11},{10,... | collective-permute-start | bytes 344072 | tf_op jit(solution)/shard_map/ppermute | solution.py:29
  31.1 1.2 fusion.1
  32.3 1.5 %collective-permute-start.7 = (bf16[2,16,1792]{2,1,0:T(8,128)(2,1)S(1)}, bf16[2,16,1792]{2,1,0:T(8,128)(2,1)S(1)}, u32[]{:S(2)}, u32[]{:S(2)}) collective-permute-start(bf16[2,16,1792]{2,1,0:T(8,128)(2,1)S(1)} %get-tuple-element.90), channel_id=1, source_target_pairs={{0,4},{1,5},{2,6},{3,7},{4,0},{5,1},{6,2},{7,3},{8,12},{9,13},{10,... | collective-permute-start | bytes 344072 | tf_op jit(solution)/shard_map/ppermute | solution.py:29
  33.9 9.0 %collective-permute-done.9 = bf16[2,16,1792]{2,1,0:T(8,128)(2,1)S(1)} collective-permute-done((bf16[2,16,1792]{2,1,0:T(8,128)(2,1)S(1)}, bf16[2,16,1792]{2,1,0:T(8,128)(2,1)S(1)}, u32[]{:S(2)}, u32[]{:S(2)}) %collective-permute-start.9) | collective-permute-done | bytes 114720 | tf_op jit(solution)/shard_map/ppermute | solution.py:29
  42.9 1.4 collective-permute-start.10
  44.3 12.7 %collective-permute-done.7 = bf16[2,16,1792]{2,1,0:T(8,128)(2,1)S(1)} collective-permute-done((bf16[2,16,1792]{2,1,0:T(8,128)(2,1)S(1)}, bf16[2,16,1792]{2,1,0:T(8,128)(2,1)S(1)}, u32[]{:S(2)}, u32[]{:S(2)}) %collective-permute-start.7) | collective-permute-done | bytes 114720 | tf_op jit(solution)/shard_map/ppermute | solution.py:29
  57.0 4.8 %collective-permute-start.8 = (bf16[1,16,1792]{2,1,0:T(8,128)(2,1)S(1)}, bf16[1,16,1792]{2,1,0:T(8,128)(2,1)S(1)}, u32[]{:S(2)}, u32[]{:S(2)}) collective-permute-start(bf16[1,16,1792]{2,1,0:T(8,128)(2,1)S(1)} %fusion.9), channel_id=1, source_target_pairs={{0,8},{1,9},{2,10},{3,11},{4,12},{5,13},{6,14},{7,15},{8,0},{9,1},... | collective-permute-start | bytes 172040 | tf_op jit(solution)/shard_map/ppermute | solution.py:29
  61.7 8.0 %collective-permute-done.10 = bf16[1,16,1792]{2,1,0:T(8,128)(2,1)S(1)} collective-permute-done((bf16[1,16,1792]{2,1,0:T(8,128)(2,1)S(1)}, bf16[1,16,1792]{2,1,0:T(8,128)(2,1)S(1)}, u32[]{:S(2)}, u32[]{:S(2)}) %collective-permute-start.10) | collective-permute-done | bytes 57376 | tf_op jit(solution)/shard_map/ppermute | solution.py:29
  69.7 0.1 multiply_reduce_fusion
  69.9 0.6 collective-permute-done.8
  70.5 0.1 multiply_reduce_fusion.1
  70.6 0.1 multiply_convert_fusion
  70.8 0.1 collective-permute-start.13
  71.5 3.0 %collective-permute-start.11 = (bf16[16,1792]{1,0:T(8,128)(2,1)S(1)}, bf16[16,1792]{1,0:T(8,128)(2,1)S(1)}, u32[]{:S(2)}, u32[]{:S(2)}) collective-permute-start(bf16[16,1792]{1,0:T(8,128)(2,1)S(1)} %get-tuple-element.103), channel_id=1, source_target_pairs={{0,8},{1,9},{2,10},{3,11},{4,12},{5,13},{6,14},{7,15},{8,0},{9,1},... | collective-permute-start | bytes 172040 | tf_op jit(solution)/shard_map/ppermute | solution.py:29
  74.5 2.5 %collective-permute-done.13 = bf16[16,1792]{1,0:T(8,128)(2,1)S(1)} collective-permute-done((bf16[16,1792]{1,0:T(8,128)(2,1)S(1)}, bf16[16,1792]{1,0:T(8,128)(2,1)S(1)}, u32[]{:S(2)}, u32[]{:S(2)}) %collective-permute-start.13) | collective-permute-done | bytes 57376 | tf_op jit(solution)/shard_map/ppermute | solution.py:29
  77.0 1.4 collective-permute-start.14
  78.5 0.4 collective-permute-start.12
  78.9 3.0 %collective-permute-done.14 = bf16[32,1792]{1,0:T(8,128)(2,1)S(1)} collective-permute-done((bf16[32,1792]{1,0:T(8,128)(2,1)S(1)}, bf16[32,1792]{1,0:T(8,128)(2,1)S(1)}, u32[]{:S(2)}, u32[]{:S(2)}) %collective-permute-start.14) | collective-permute-done | bytes 114720 | tf_op jit(solution)/shard_map/ppermute | solution.py:29
  81.9 1.4 collective-permute-done.12
  83.3 0.7 pad_maximum_fusion.refs_0_
  84.0 0.6 collective-permute-start.15
  84.7 1.1 collective-permute-start.16
  85.9 3.6 %image_attention.2 = (f32[1024,128]{1,0:T(8,128)S(1)}, f32[1024,128]{1,0:T(8,128)S(1)}) custom-call(bf16[16,384,128]{2,1,0:T(8,128)(2,1)S(1)} %all-to-all-done.packed_ref), custom_call_target="tpu_custom_call" | custom-call | flops 1073741824 | bytes 2359296 | tf_op jit(solution)/shard_map/image_attention/pallas_call | solution.py:379
  89.5 0.7 collective-permute-done.15.refs_1_
  90.3 0.4 collective-permute-done.16.refs_3_
  90.7 4.1 %project.1 = (bf16[4,144,256]{2,1,0:T(8,128)(2,1)S(1)}, bf16[4,144,256]{2,1,0:T(8,128)(2,1)S(1)}, bf16[4,144,256]{2,1,0:T(8,128)(2,1)S(1)}, bf16[4,144,256]{2,1,0:T(8,128)(2,1)S(1)}) custom-call(s32[5]{0:T(128)S(1)} %copy-done.7, bf16[64,1792]{1,0:T(8,128)(2,1)S(1)} %copy-done.1, bf16[64,1792]{1,0:T(8,128)(2,1)S(1)} %collective-permute-done.15.refs_1_, ...), custom_call_target="tpu_custom_call" | custom-call | flops 754974720 | bytes 7864320 | tf_op jit(solution)/shard_map/project/pallas_call | solution.py:219
  94.8 1.4 collective-permute-start.17
  96.2 0.3 collective-permute-start.18
  96.6 3.7 %image_attention.3 = (f32[1024,128]{1,0:T(8,128)S(1)}, f32[1024,128]{1,0:T(8,128)S(1)}) custom-call(bf16[16,384,128]{2,1,0:T(8,128)(2,1)S(1)} %all-to-all-done.packed_ref), custom_call_target="tpu_custom_call" | custom-call | flops 1073741824 | bytes 2359296 | tf_op jit(solution)/shard_map/image_attention/pallas_call | solution.py:379
  100.3 2.5 %collective-permute-done.17 = bf16[4,144,256]{2,1,0:T(8,128)(2,1)S(1)} collective-permute-done((bf16[4,144,256]{2,1,0:T(8,128)(2,1)S(1)}, bf16[4,144,256]{2,1,0:T(8,128)(2,1)S(1)}, u32[]{:S(2)}, u32[]{:S(2)}) %collective-permute-start.17) | collective-permute-done | bytes 294944 | tf_op jit(solution)/shard_map/ppermute | solution.py:29
  102.7 1.8 %collective-permute-done.18 = bf16[4,144,256]{2,1,0:T(8,128)(2,1)S(1)} collective-permute-done((bf16[4,144,256]{2,1,0:T(8,128)(2,1)S(1)}, bf16[4,144,256]{2,1,0:T(8,128)(2,1)S(1)}, u32[]{:S(2)}, u32[]{:S(2)}) %collective-permute-start.18) | collective-permute-done | bytes 294944 | tf_op jit(solution)/shard_map/ppermute | solution.py:29
  104.6 0.4 collective-permute-start.21
  105.1 1.5 collective-permute-start.19
  106.5 3.3 %collective-permute-done.21 = bf16[2,144,256]{2,1,0:T(8,128)(2,1)S(1)} collective-permute-done((bf16[2,144,256]{2,1,0:T(8,128)(2,1)S(1)}, bf16[2,144,256]{2,1,0:T(8,128)(2,1)S(1)}, u32[]{:S(2)}, u32[]{:S(2)}) %collective-permute-start.21) | collective-permute-done | bytes 147488 | tf_op jit(solution)/shard_map/ppermute | solution.py:29
  109.9 0.8 collective-permute-start.22
  110.6 0.5 collective-permute-done.19
  111.2 1.7 %collective-permute-start.20 = (bf16[1,144,256]{2,1,0:T(8,128)(2,1)S(1)}, bf16[1,144,256]{2,1,0:T(8,128)(2,1)S(1)}, u32[]{:S(2)}, u32[]{:S(2)}) collective-permute-start(bf16[1,144,256]{2,1,0:T(8,128)(2,1)S(1)} %get-tuple-element.98), channel_id=1, source_target_pairs={{0,8},{1,9},{2,10},{3,11},{4,12},{5,13},{6,14},{7,15},{8,0},{9,1},... | collective-permute-start | bytes 221192 | tf_op jit(solution)/shard_map/ppermute | solution.py:29
  113.0 2.8 %collective-permute-done.22 = bf16[1,144,256]{2,1,0:T(8,128)(2,1)S(1)} collective-permute-done((bf16[1,144,256]{2,1,0:T(8,128)(2,1)S(1)}, bf16[1,144,256]{2,1,0:T(8,128)(2,1)S(1)}, u32[]{:S(2)}, u32[]{:S(2)}) %collective-permute-start.22) | collective-permute-done | bytes 73760 | tf_op jit(solution)/shard_map/ppermute | solution.py:29
  115.8 1.6 %collective-permute-done.20 = bf16[1,144,256]{2,1,0:T(8,128)(2,1)S(1)} collective-permute-done((bf16[1,144,256]{2,1,0:T(8,128)(2,1)S(1)}, bf16[1,144,256]{2,1,0:T(8,128)(2,1)S(1)}, u32[]{:S(2)}, u32[]{:S(2)}) %collective-permute-start.20) | collective-permute-done | bytes 73760 | tf_op jit(solution)/shard_map/ppermute | solution.py:29
  117.3 0.7 combine.1
  118.1 0.1 collective-permute-start.23
  118.2 1.2 collective-permute-done.23.refs_5_
  119.4 3.8 %finish.1 = bf16[16,160,128]{2,1,0:T(8,128)(2,1)S(1)} custom-call(s32[5]{0:T(128)S(1)} %copy-done.7, bf16[16,384,128]{2,1,0:T(8,128)(2,1)S(1)} %all-to-all-done.packed_ref, f32[1024,128]{1,0:T(8,128)S(1)} %get-tuple-element.66.refs_0_, f32[1024,128]{1,0:T(8,128)S(1)} %get-tuple-element.67.refs_1_, f32[1024,128]{1,0:T(8,128)S(1)} %get-tuple-element.72.refs_2_, ...), custom_call_target="tpu_custom_call" | custom-call | flops 268435456 | bytes 3145728 | tf_op jit(solution)/shard_map/finish/pallas_call | solution.py:441
  123.2 21.8 %all_to_all.10.blocks_ref = bf16[16,160,128]{2,1,0:T(8,128)(2,1)S(1)} all-to-all(bf16[16,160,128]{2,1,0:T(8,128)(2,1)S(1)} %finish.1), channel_id=1, replica_groups=mesh['dp'=2,'seq'=16] {'seq'}, dimensions={0} | all-to-all | bytes 1310720 | tf_op jit(solution)/shard_map/all_to_all | solution.py:494
  145.1 1.0 unpack.1
  (44 shorter events, 0.4 us)
Async XLA Ops:
  1.9 5.9 %copy-start.3 = (bf16[256,2,192]{0,2,1:T(8,128)(2,1)S(1)}, bf16[256,2,192]{0,2,1:T(8,128)(2,1)}, u32[]{:S(2)}) copy-start(bf16[256,2,192]{0,2,1:T(8,128)(2,1)} %param.14) | copy-start | bytes 589828
  7.3 6.9 %collective-permute-start = (bf16[8,16,1792]{2,1,0:T(8,128)(2,1)}, bf16[8,16,1792]{2,1,0:T(8,128)(2,1)S(1)}, u32[]{:S(2)}, u32[]{:S(2)}) collective-permute-start(bf16[8,16,1792]{2,1,0:T(8,128)(2,1)} %get-tuple-element.43), channel_id=1, source_target_pairs={{0,1},{1,0},{2,3},{3,2},{4,5},{5,4},{6,7},{7,6},{8,9},{9,8},{10,11... | collective-permute-start | bytes 1376264 | tf_op jit(solution)/shard_map/ppermute | solution.py:29
  7.9 20.1 %collective-permute-start.6 = (bf16[2,192,256]{2,1,0:T(8,128)(2,1)S(1)}, bf16[2,192,256]{2,1,0:T(8,128)(2,1)S(1)}, u32[]{:S(2)}, u32[]{:S(2)}) collective-permute-start(bf16[2,192,256]{2,1,0:T(8,128)(2,1)S(1)} %bitcast.39), channel_id=1, source_target_pairs={{0,1},{1,0},{2,3},{3,2},{4,5},{5,4},{6,7},{7,6},{8,9},{9,8},{10,11... | collective-permute-start | bytes 589832 | tf_op jit(solution)/shard_map/ppermute | solution.py:29
  7.9 20.1 %collective-permute-start.4 = (bf16[192,3584]{1,0:T(8,128)(2,1)}, bf16[192,3584]{1,0:T(8,128)(2,1)}, u32[]{:S(2)}, u32[]{:S(2)}) collective-permute-start(bf16[192,3584]{1,0:T(8,128)(2,1)} %bitcast.6.refs_5_), channel_id=1, source_target_pairs={{0,1},{1,0},{2,3},{3,2},{4,5},{5,4},{6,7},{7,6},{8,9},{9,8},{10,11... | collective-permute-start | bytes 4128776 | tf_op jit(solution)/shard_map/ppermute | solution.py:29
  8.4 5.5 %copy-start = (bf16[192,4096]{1,0:T(8,128)(2,1)S(1)}, bf16[192,4096]{1,0:T(8,128)(2,1)}, u32[]{:S(2)}) copy-start(bf16[192,4096]{1,0:T(8,128)(2,1)} %refs_7_.1) | copy-start | bytes 4718596
  8.4 5.9 %copy-start.11 = (bf16[3584]{0:T(1024)(128)(2,1)S(1)}, bf16[3584]{0:T(1024)(128)(2,1)}, u32[]{:S(2)}) copy-start(bf16[3584]{0:T(1024)(128)(2,1)} %param.12) | copy-start | bytes 21508
  8.4 5.9 %copy-start.9 = (bf16[8,16,1792]{2,1,0:T(8,128)(2,1)S(1)}, bf16[8,16,1792]{2,1,0:T(8,128)(2,1)}, u32[]{:S(2)}) copy-start(bf16[8,16,1792]{2,1,0:T(8,128)(2,1)} %get-tuple-element.42) | copy-start | bytes 1376260
  13.7 2.1 %copy-start.10 = (bf16[8,16,1792]{2,1,0:T(8,128)(2,1)S(1)}, bf16[8,16,1792]{2,1,0:T(8,128)(2,1)}, u32[]{:S(2)}) copy-start(bf16[8,16,1792]{2,1,0:T(8,128)(2,1)} %get-tuple-element.45) | copy-start | bytes 1376260
  13.7 2.1 %collective-permute-start.1 = (bf16[8,16,1792]{2,1,0:T(8,128)(2,1)}, bf16[8,16,1792]{2,1,0:T(8,128)(2,1)S(1)}, u32[]{:S(2)}, u32[]{:S(2)}) collective-permute-start(bf16[8,16,1792]{2,1,0:T(8,128)(2,1)} %get-tuple-element.46), channel_id=1, source_target_pairs={{0,1},{1,0},{2,3},{3,2},{4,5},{5,4},{6,7},{7,6},{8,9},{9,8},{10,11... | collective-permute-start | bytes 1376264 | tf_op jit(solution)/shard_map/ppermute | solution.py:29
  13.8 14.2 %collective-permute-start.5 = (bf16[192,4096]{1,0:T(8,128)(2,1)S(1)}, bf16[192,4096]{1,0:T(8,128)(2,1)}, u32[]{:S(2)}, u32[]{:S(2)}) collective-permute-start(bf16[192,4096]{1,0:T(8,128)(2,1)S(1)} %copy-done), channel_id=1, source_target_pairs={{0,1},{1,0},{2,3},{3,2},{4,5},{5,4},{6,7},{7,6},{8,9},{9,8},{10,11... | collective-permute-start | bytes 4718600 | tf_op jit(solution)/shard_map/ppermute | solution.py:29
  14.3 6.7 %copy-start.8 = (bf16[1,128,2,2048]{3,2,1,0:T(2,128)(2,1)S(1)}, bf16[1,128,2,2048]{3,2,1,0:T(2,128)(2,1)}, u32[]{:S(2)}) copy-start(bf16[1,128,2,2048]{3,2,1,0:T(2,128)(2,1)} %param.19) | copy-start | bytes 3145732
  16.8 11.2 %collective-permute-start.2 = (bf16[4,16,1792]{2,1,0:T(8,128)(2,1)}, bf16[4,16,1792]{2,1,0:T(8,128)(2,1)}, u32[]{:S(2)}, u32[]{:S(2)}) collective-permute-start(bf16[4,16,1792]{2,1,0:T(8,128)(2,1)} %get-tuple-element.47), channel_id=1, source_target_pairs={{0,2},{1,3},{2,0},{3,1},{4,6},{5,7},{6,4},{7,5},{8,10},{9,11},{10,... | collective-permute-start | bytes 688136 | tf_op jit(solution)/shard_map/ppermute | solution.py:29
  19.4 8.6 %collective-permute-start.3 = (bf16[4,16,1792]{2,1,0:T(8,128)(2,1)}, bf16[4,16,1792]{2,1,0:T(8,128)(2,1)}, u32[]{:S(2)}, u32[]{:S(2)}) collective-permute-start(bf16[4,16,1792]{2,1,0:T(8,128)(2,1)} %get-tuple-element.48), channel_id=1, source_target_pairs={{0,4},{1,5},{2,6},{3,7},{4,0},{5,1},{6,2},{7,3},{8,12},{9,13},{10,... | collective-permute-start | bytes 688136 | tf_op jit(solution)/shard_map/ppermute | solution.py:29
  21.4 1.0 copy-start.2
  23.8 60.2 %all-to-all-start = ((bf16[16,384,128]{2,1,0:T(8,128)(2,1)}), bf16[16,384,128]{2,1,0:T(8,128)(2,1)S(1)}, u32[]{:S(2)}, u32[]{:S(2)}) async-start(bf16[16,384,128]{2,1,0:T(8,128)(2,1)} %pack.1), calls=%async_computation | async-start | bytes 3145728 | tf_op jit(solution)/shard_map/all_to_all | solution.py:494
  28.0 42.8 %copy-start.5 = (bf16[2,192,256]{2,1,0:T(8,128)(2,1)}, bf16[2,192,256]{2,1,0:T(8,128)(2,1)S(1)}, u32[]{:S(2)}) copy-start(bf16[2,192,256]{2,1,0:T(8,128)(2,1)S(1)} %collective-permute-done.6.refs_10_) | copy-start | bytes 589828
  29.3 13.6 %collective-permute-start.9 = (bf16[2,16,1792]{2,1,0:T(8,128)(2,1)S(1)}, bf16[2,16,1792]{2,1,0:T(8,128)(2,1)S(1)}, u32[]{:S(2)}, u32[]{:S(2)}) collective-permute-start(bf16[2,16,1792]{2,1,0:T(8,128)(2,1)S(1)} %get-tuple-element.88), channel_id=1, source_target_pairs={{0,2},{1,3},{2,0},{3,1},{4,6},{5,7},{6,4},{7,5},{8,10},{9,11},{10,... | collective-permute-start | bytes 344072 | tf_op jit(solution)/shard_map/ppermute | solution.py:29
  32.3 24.6 %collective-permute-start.7 = (bf16[2,16,1792]{2,1,0:T(8,128)(2,1)S(1)}, bf16[2,16,1792]{2,1,0:T(8,128)(2,1)S(1)}, u32[]{:S(2)}, u32[]{:S(2)}) collective-permute-start(bf16[2,16,1792]{2,1,0:T(8,128)(2,1)S(1)} %get-tuple-element.90), channel_id=1, source_target_pairs={{0,4},{1,5},{2,6},{3,7},{4,0},{5,1},{6,2},{7,3},{8,12},{9,13},{10,... | collective-permute-start | bytes 344072 | tf_op jit(solution)/shard_map/ppermute | solution.py:29
  42.9 26.9 %collective-permute-start.10 = (bf16[1,16,1792]{2,1,0:T(8,128)(2,1)S(1)}, bf16[1,16,1792]{2,1,0:T(8,128)(2,1)S(1)}, u32[]{:S(2)}, u32[]{:S(2)}) collective-permute-start(bf16[1,16,1792]{2,1,0:T(8,128)(2,1)S(1)} %fusion.6), channel_id=1, source_target_pairs={{0,8},{1,9},{2,10},{3,11},{4,12},{5,13},{6,14},{7,15},{8,0},{9,1},... | collective-permute-start | bytes 172040 | tf_op jit(solution)/shard_map/ppermute | solution.py:29
  57.0 13.5 %collective-permute-start.8 = (bf16[1,16,1792]{2,1,0:T(8,128)(2,1)S(1)}, bf16[1,16,1792]{2,1,0:T(8,128)(2,1)S(1)}, u32[]{:S(2)}, u32[]{:S(2)}) collective-permute-start(bf16[1,16,1792]{2,1,0:T(8,128)(2,1)S(1)} %fusion.9), channel_id=1, source_target_pairs={{0,8},{1,9},{2,10},{3,11},{4,12},{5,13},{6,14},{7,15},{8,0},{9,1},... | collective-permute-start | bytes 172040 | tf_op jit(solution)/shard_map/ppermute | solution.py:29
  70.8 6.2 %collective-permute-start.13 = (bf16[16,1792]{1,0:T(8,128)(2,1)S(1)}, bf16[16,1792]{1,0:T(8,128)(2,1)S(1)}, u32[]{:S(2)}, u32[]{:S(2)}) collective-permute-start(bf16[16,1792]{1,0:T(8,128)(2,1)S(1)} %get-tuple-element.102), channel_id=1, source_target_pairs={{0,8},{1,9},{2,10},{3,11},{4,12},{5,13},{6,14},{7,15},{8,0},{9,1},... | collective-permute-start | bytes 172040 | tf_op jit(solution)/shard_map/ppermute | solution.py:29
  71.5 7.0 %collective-permute-start.11 = (bf16[16,1792]{1,0:T(8,128)(2,1)S(1)}, bf16[16,1792]{1,0:T(8,128)(2,1)S(1)}, u32[]{:S(2)}, u32[]{:S(2)}) collective-permute-start(bf16[16,1792]{1,0:T(8,128)(2,1)S(1)} %get-tuple-element.103), channel_id=1, source_target_pairs={{0,8},{1,9},{2,10},{3,11},{4,12},{5,13},{6,14},{7,15},{8,0},{9,1},... | collective-permute-start | bytes 172040 | tf_op jit(solution)/shard_map/ppermute | solution.py:29
  77.0 4.9 %collective-permute-start.14 = (bf16[32,1792]{1,0:T(8,128)(2,1)S(1)}, bf16[32,1792]{1,0:T(8,128)(2,1)S(1)}, u32[]{:S(2)}, u32[]{:S(2)}) collective-permute-start(bf16[32,1792]{1,0:T(8,128)(2,1)S(1)} %pad_maximum_fusion.3), channel_id=1, source_target_pairs={{0,2},{1,3},{2,0},{3,1},{4,6},{5,7},{6,4},{7,5},{8,10},{9,11},{10,... | collective-permute-start | bytes 344072 | tf_op jit(solution)/shard_map/ppermute | solution.py:29
  78.5 4.9 %collective-permute-start.12 = (bf16[32,1792]{1,0:T(8,128)(2,1)S(1)}, bf16[32,1792]{1,0:T(8,128)(2,1)S(1)}, u32[]{:S(2)}, u32[]{:S(2)}) collective-permute-start(bf16[32,1792]{1,0:T(8,128)(2,1)S(1)} %pad_maximum_fusion.2), channel_id=1, source_target_pairs={{0,4},{1,5},{2,6},{3,7},{4,0},{5,1},{6,2},{7,3},{8,12},{9,13},{10,... | collective-permute-start | bytes 344072 | tf_op jit(solution)/shard_map/ppermute | solution.py:29
  84.0 6.2 %collective-permute-start.15 = (bf16[64,1792]{1,0:T(8,128)(2,1)}, bf16[64,1792]{1,0:T(8,128)(2,1)S(1)}, u32[]{:S(2)}, u32[]{:S(2)}) collective-permute-start(bf16[64,1792]{1,0:T(8,128)(2,1)} %pad_maximum_fusion.refs_0_), channel_id=1, source_target_pairs={{0,2},{1,3},{2,0},{3,1},{4,6},{5,7},{6,4},{7,5},{8,10},{9,11},{10,... | collective-permute-start | bytes 688136 | tf_op jit(solution)/shard_map/ppermute | solution.py:29
  84.7 6.0 %collective-permute-start.16 = (bf16[64,1792]{1,0:T(8,128)(2,1)S(1)}, bf16[64,1792]{1,0:T(8,128)(2,1)S(1)}, u32[]{:S(2)}, u32[]{:S(2)}) collective-permute-start(bf16[64,1792]{1,0:T(8,128)(2,1)S(1)} %pad_maximum_fusion.1.refs_2_), channel_id=1, source_target_pairs={{0,4},{1,5},{2,6},{3,7},{4,0},{5,1},{6,2},{7,3},{8,12},{9,13},{10,... | collective-permute-start | bytes 688136 | tf_op jit(solution)/shard_map/ppermute | solution.py:29
  85.8 4.9 %copy-start.1 = (bf16[64,1792]{1,0:T(8,128)(2,1)S(1)}, bf16[64,1792]{1,0:T(8,128)(2,1)}, u32[]{:S(2)}) copy-start(bf16[64,1792]{1,0:T(8,128)(2,1)} %pad_maximum_fusion.refs_0_) | copy-start | bytes 688132
  85.8 4.9 %copy-start.4 = (bf16[256,2,192]{0,2,1:T(8,128)(2,1)S(1)}, bf16[256,2,192]{0,2,1:T(8,128)(2,1)}, u32[]{:S(2)}) copy-start(bf16[256,2,192]{0,2,1:T(8,128)(2,1)} %param.14) | copy-start | bytes 589828
  85.8 4.9 %copy-start.6 = (bf16[2,192,256]{2,1,0:T(8,128)(2,1)S(1)}, bf16[2,192,256]{2,1,0:T(8,128)(2,1)}, u32[]{:S(2)}) copy-start(bf16[2,192,256]{2,1,0:T(8,128)(2,1)} %copy-done.5) | copy-start | bytes 589828
  85.8 4.9 %copy-start.7 = (s32[5]{0:T(128)S(1)}, s32[5]{0:T(128)}, u32[]{:S(2)}) copy-start(s32[5]{0:T(128)} %stack.19.place_ref) | copy-start | bytes 64
  94.8 7.9 %collective-permute-start.17 = (bf16[4,144,256]{2,1,0:T(8,128)(2,1)S(1)}, bf16[4,144,256]{2,1,0:T(8,128)(2,1)S(1)}, u32[]{:S(2)}, u32[]{:S(2)}) collective-permute-start(bf16[4,144,256]{2,1,0:T(8,128)(2,1)S(1)} %get-tuple-element.68), channel_id=1, source_target_pairs={{0,2},{1,3},{2,0},{3,1},{4,6},{5,7},{6,4},{7,5},{8,10},{9,11},{10,... | collective-permute-start | bytes 884744 | tf_op jit(solution)/shard_map/ppermute | solution.py:29
  96.2 8.3 %collective-permute-start.18 = (bf16[4,144,256]{2,1,0:T(8,128)(2,1)S(1)}, bf16[4,144,256]{2,1,0:T(8,128)(2,1)S(1)}, u32[]{:S(2)}, u32[]{:S(2)}) collective-permute-start(bf16[4,144,256]{2,1,0:T(8,128)(2,1)S(1)} %get-tuple-element.69), channel_id=1, source_target_pairs={{0,4},{1,5},{2,6},{3,7},{4,0},{5,1},{6,2},{7,3},{8,12},{9,13},{10,... | collective-permute-start | bytes 884744 | tf_op jit(solution)/shard_map/ppermute | solution.py:29
  104.6 5.2 %collective-permute-start.21 = (bf16[2,144,256]{2,1,0:T(8,128)(2,1)S(1)}, bf16[2,144,256]{2,1,0:T(8,128)(2,1)S(1)}, u32[]{:S(2)}, u32[]{:S(2)}) collective-permute-start(bf16[2,144,256]{2,1,0:T(8,128)(2,1)S(1)} %get-tuple-element.92), channel_id=1, source_target_pairs={{0,2},{1,3},{2,0},{3,1},{4,6},{5,7},{6,4},{7,5},{8,10},{9,11},{10,... | collective-permute-start | bytes 442376 | tf_op jit(solution)/shard_map/ppermute | solution.py:29
  105.1 6.1 %collective-permute-start.19 = (bf16[2,144,256]{2,1,0:T(8,128)(2,1)S(1)}, bf16[2,144,256]{2,1,0:T(8,128)(2,1)S(1)}, u32[]{:S(2)}, u32[]{:S(2)}) collective-permute-start(bf16[2,144,256]{2,1,0:T(8,128)(2,1)S(1)} %get-tuple-element.94), channel_id=1, source_target_pairs={{0,4},{1,5},{2,6},{3,7},{4,0},{5,1},{6,2},{7,3},{8,12},{9,13},{10,... | collective-permute-start | bytes 442376 | tf_op jit(solution)/shard_map/ppermute | solution.py:29
  109.9 5.9 %collective-permute-start.22 = (bf16[1,144,256]{2,1,0:T(8,128)(2,1)S(1)}, bf16[1,144,256]{2,1,0:T(8,128)(2,1)S(1)}, u32[]{:S(2)}, u32[]{:S(2)}) collective-permute-start(bf16[1,144,256]{2,1,0:T(8,128)(2,1)S(1)} %get-tuple-element.96), channel_id=1, source_target_pairs={{0,8},{1,9},{2,10},{3,11},{4,12},{5,13},{6,14},{7,15},{8,0},{9,1},... | collective-permute-start | bytes 221192 | tf_op jit(solution)/shard_map/ppermute | solution.py:29
  111.2 6.1 %collective-permute-start.20 = (bf16[1,144,256]{2,1,0:T(8,128)(2,1)S(1)}, bf16[1,144,256]{2,1,0:T(8,128)(2,1)S(1)}, u32[]{:S(2)}, u32[]{:S(2)}) collective-permute-start(bf16[1,144,256]{2,1,0:T(8,128)(2,1)S(1)} %get-tuple-element.98), channel_id=1, source_target_pairs={{0,8},{1,9},{2,10},{3,11},{4,12},{5,13},{6,14},{7,15},{8,0},{9,1},... | collective-permute-start | bytes 221192 | tf_op jit(solution)/shard_map/ppermute | solution.py:29
  118.1 1.3 collective-permute-start.23

commit v6 on v5

--- a/solution.py
+++ b/solution.py
@@ -77,7 +77,7 @@
         lhs_ref[...] = act_ref[...].T
     half = chips * share
     first = core == 0
-    tile = 256
+    tile = width // 2
     for step, start in enumerate(starts):
         rows = slice(start, min(start + DEPTH_BLOCK, depth))
         loads[step].wait()
@@ -128,6 +128,33 @@
     )(place, act, weight)
 
 
+def modulation_kernel(time_ref, mod0_ref, mod1_ref, out_ref):
+    contract = (((1,), (1,)), ((), ()))
+    embedding = jnp.broadcast_to(time_ref[...].astype(jnp.float32), (16, time_ref.shape[1]))
+    embedding = embedding.astype(jnp.bfloat16)
+    row = lax.broadcasted_iota(jnp.int32, (16, mod0_ref.shape[1]), 0)
+    for side, mod in enumerate((mod0_ref, mod1_ref)):
+        shift, scale = [
+            lax.dot_general(embedding, mod[at], contract, preferred_element_type=jnp.float32)
+            for at in range(2)
+        ]
+        lines = jnp.where(row < 2, 1.0 + scale, shift)
+        high = lines.astype(jnp.bfloat16).astype(jnp.float32)
+        low = jnp.where(row % 2 == 0, high, lines - high)
+        out_ref[side] = jnp.where(row < 4, low, 1.0 + scale)
+
+
+def modulation(time, mod0, mod1):
+    return pl.pallas_call(
+        modulation_kernel,
+        out_shape=jax.ShapeDtypeStruct((2, 16, mod0.shape[1]), jnp.float32),
+        in_specs=[VMEM_SPEC] * 3,
+        out_specs=VMEM_SPEC,
+        compiler_params=params(8),
+        name="modulation",
+    )(time, mod0, mod1)
+
+
 def slot_rows(chips, width):
     per_slot = 2 * 128 // width
     return chips * per_slot, -(-(chips * per_slot + 2) // 16) * 16
@@ -135,7 +162,7 @@
 
 def project_kernel(lanes, place_ref, *refs):
     pieces, refs = (refs[:2], refs[2:4]), refs[4:]
-    time, win0, win1, kv0, kv1, mod0, mod1, *outs, states, proj0, proj1, sums = refs
+    lines_ref, win0, win1, kv0, kv1, *outs, states, proj0, proj1, sums = refs
     chip = place_ref[3]
     half_chips = outs[0].shape[0]
     chips = 2 * half_chips
@@ -165,19 +192,10 @@
     lane = lax.broadcasted_iota(jnp.int32, sums.shape, 1)
     sums[...] = jnp.where(lane == 0, first, second).T
     left = []
-    embedding = jnp.broadcast_to(time[...].astype(jnp.float32), (16, time.shape[1]))
-    embedding = embedding.astype(jnp.bfloat16)
-    for value, mod in ((value0, mod0), (value1, mod1)):
-        shift, scale = [
-            lax.dot_general(embedding, mod[at], contract, preferred_element_type=jnp.float32)[:1]
-            for at in range(2)
-        ]
-        scale = 1.0 + scale
-        row = lax.broadcasted_iota(jnp.int32, (16, value.shape[1]), 0)
-        lines = jnp.where(row < 2, scale, shift)
-        high = lines.astype(jnp.bfloat16).astype(jnp.float32)
-        lines = jnp.where(row % 2 == 0, high, lines - high)
-        lines = jnp.where(row < 4, lines, 0.0)
+    for side, value in enumerate((value0, value1)):
+        lines = lines_ref[side]
+        row = lax.broadcasted_iota(jnp.int32, lines.shape, 0)
+        lines, scale = jnp.where(row < 4, lines, 0.0), lines[4:5]
         left.append(jnp.concatenate([value * scale, lines], 0).astype(jnp.bfloat16))
     width = outs[0].shape[2]
     slots, extra = slot_rows(chips, width)
@@ -208,7 +226,7 @@
             out_ref[to, rows:, :] = below.astype(out_ref.dtype)
 
 
-def project(lanes, place, pieces, time, win0, win1, kv0, kv1, mod0, mod1):
+def project(lanes, place, pieces, lines, win0, win1, kv0, kv1):
     chips = 1 << len(lanes[0])
     rows = 2 * pieces[0].shape[0]
     features, depth = win0.shape
@@ -219,7 +237,7 @@
     return pl.pallas_call(
         functools.partial(project_kernel, lanes),
         out_shape=(out,) * 4,
-        in_specs=[SMEM_SPEC] + [VMEM_SPEC] * 11,
+        in_specs=[SMEM_SPEC] + [VMEM_SPEC] * 9,
         out_specs=(VMEM_SPEC,) * 4,
         scratch_shapes=[
             pltpu.VMEM((rows, depth // 2), jnp.bfloat16),
@@ -234,7 +252,7 @@
             transcendentals=0,
         ),
         name="project",
-    )(place, *pieces, time, win0, win1, kv0, kv1, mod0, mod1)
+    )(place, *pieces, lines, win0, win1, kv0, kv1)
 
 
 def combine_kernel(chips, model_width, place_ref, *refs):
@@ -493,7 +511,10 @@
     def exchange(rows):
         return lax.all_to_all(rows, "seq", split_axis=0, concat_axis=0, tiled=True)
 
-    act = enc_act[0].T
+    image_key_values, image_queries = tie((image_key_values, image_queries))
+    packed = pack(copies, image_queries[0], image_key_values[0, :, 0], image_key_values[0, :, 1])
+    act, packed = tie((enc_act[0].T, packed))
+    packed = exchange(packed)
     keep, sent = [], []
     for lane, order in enumerate(lanes):
         own, other, *turned = encoder(lane, order, place, act, down_weight)
@@ -503,15 +524,12 @@
         sent.append(add(own[chips // 2 :], got[chips // 2 :], jnp.bfloat16))
         keep.append(add(own[: chips // 2], got[: chips // 2], jnp.float32))
     for step in range(rounds):
-        if step == 0:
-            sent, image_key_values, image_queries = tie((sent, image_key_values, image_queries))
-            packed = pack(
-                copies, image_queries[0], image_key_values[0, :, 0], image_key_values[0, :, 1]
-            )
-            packed = exchange(packed)
         got = [swap(part, 2 * order[step]) for part, order in zip(sent, lanes)]
         if step == 0:
             got, win1, kv1, mod1 = tie((got, win1, kv1, mod1))
+            lines = modulation(time, mod0, mod1)
+        if step == 1:
+            got, lines = tie((got, lines))
         half = keep[0].shape[0] // 2
         if half:
             sent = [add(mine[half:], part[half:], jnp.bfloat16) for mine, part in zip(keep, got)]
@@ -539,7 +557,7 @@
     images += image
     states = [state for pair in zip(states, got) for state in pair]
 
-    blocks = project(lanes, place, states, time, win0, win1, kv0, kv1, mod0, mod1)
+    blocks = project(lanes, place, states, lines, win0, win1, kv0, kv1)
     keep, sent = [blocks[0], blocks[2]], [blocks[1], blocks[3]]
     for step in range(rounds):
         if step == 0:

time: 146 us -> 147 us (level)
  starting transfers between devices: 32.3 us -> 27.3 us
  waiting for transfers between devices: 52.7 us -> 56.9 us
  local copies, waits for them, and re-layouts: 2.05 us -> 3.91 us
    ppermute x24, starting transfers between devices: 28.1 us -> 22.9 us  [swap(): return lax.ppermute(value, 'seq', [(i, i ^ mask) for i in range(devices)])]
    ppermute x24, waiting for transfers between devices: 52.7 us -> 56.9 us  [swap(): return lax.ppermute(value, 'seq', [(i, i ^ mask) for i in range(devices)])]
    convert_element_type x9 -> x8, other arithmetic: 3.64 us -> 2.4 us  [add(): return (one.astype(jnp.float32) + other.astype(jnp.float32)).astype(dtype)]
  transfers between devices with their start and end apart: 25 -> 25, of which waited for: 17 -> 17; matrix products, arithmetic and copies ran while one was open for 4% -> 4% of each run, Pallas kernels for 10% -> 9%
where the time goes in v6:
time: 147 us
  waiting for transfers between devices  56.9 us (39%)
  Pallas kernels  29.8 us (20%)
  starting transfers between devices  27.3 us (19%)
  blocking collectives  20.8 us (14%)
  other arithmetic  5.76 us (4%)
  local copies, waits for them, and re-layouts  3.91 us (3%)
  between operations  2.22 us (2%)
    ppermute x24, waiting for transfers between devices, swap(): return lax.ppermute(value, 'seq', [(i, i ^ mask) for i in range(devices)])  56.9 us
    ppermute x24, starting transfers between devices, swap(): return lax.ppermute(value, 'seq', [(i, i ^ mask) for i in range(devices)])  22.9 us
    all_to_all x1, blocking collectives, exchange(): return lax.all_to_all(rows, 'seq', split_axis=0, concat_axis=0, tiled=True)  20.8 us
    pallas_call x2, Pallas kernels, encoder(): pl.pallas_call(functools.partial(encoder_kernel, lane, order), out_shape=...  11.2 us
    pallas_call x2, Pallas kernels, image_attention(): pl.pallas_call(functools.partial(image_kernel, factor, call, img_dev), ou...  7.31 us
    all_to_all x1, starting transfers between devices, exchange(): return lax.all_to_all(rows, 'seq', split_axis=0, concat_axis=0, tiled=True)  4.41 us
    pallas_call x1, Pallas kernels, project(): pl.pallas_call(functools.partial(project_kernel, lanes), out_shape=(out,)...  4.06 us
    pallas_call x1, Pallas kernels, finish(): pl.pallas_call(functools.partial(finish_kernel, factor, len(images) // 2,...  3.76 us
  transfers between devices with their start and end apart: 25, of which 17 were waited for; matrix products, arithmetic and copies ran while one was open for 4% of the time, Pallas kernels for 9%

profile of v6, /device:TPU:0, one launch (start us, length us, event | category | flops | bytes accessed | tf_op | source)
XLA Modules:
  0.0 146.6 jit_solution(11761214209627852830)
XLA Ops:
  1.3 1.6 %copy.12 = bf16[1,128,2,2048]{3,1,2,0:T(8,128)(2,1)S(1)} copy(bf16[1,128,2,2048]{3,2,1,0:T(2,128)(2,1)} %param.19) | data formatting | bytes 2097152 | tf_op jit(solution)/shard_map/optimization_barrier | solution.py:514
  2.9 0.1 slice_bitcast_fusion
  3.0 0.9 copy-done.2
  3.9 1.5 pack.1
  5.4 0.6 stack.19.place_ref
  6.0 5.7 %encoder.2 = (bf16[8,16,1792]{2,1,0:T(8,128)(2,1)}, bf16[8,16,1792]{2,1,0:T(8,128)(2,1)}, bf16[256,1184]{1,0:T(8,128)(2,1)}) custom-call(s32[5]{0:T(128)} %stack.19.place_ref, bf16[1184,256]{1,0:T(8,128)(2,1)} %bitcast.43, bf16[1184,3584]{1,0:T(8,128)(2,1)} %weight_ref.3), custom_call_target="tpu_custom_call" | custom-call | flops 1086324736 | bytes 5767168 | tf_op jit(solution)/shard_map/encoder/pallas_call | solution.py:111
  11.8 0.5 collective-permute-start
  12.3 0.1 collective-permute-start.5
  12.4 0.4 collective-permute-start.4
  12.8 5.5 %encoder.3 = (bf16[8,16,1792]{2,1,0:T(8,128)(2,1)}, bf16[8,16,1792]{2,1,0:T(8,128)(2,1)}) custom-call(s32[5]{0:T(128)} %stack.19.place_ref, bf16[256,1184]{1,0:T(8,128)(2,1)} %get-tuple-element.50.act_ref, bf16[1184,3584]{1,0:T(8,128)(2,1)} %weight_ref.3), custom_call_target="tpu_custom_call" | custom-call | flops 1086324736 | bytes 5767168 | tf_op jit(solution)/shard_map/encoder/pallas_call | solution.py:111
  18.3 0.1 collective-permute-start.2
  18.5 1.0 add_convert_fusion.1
  19.4 2.9 %collective-permute-start.1 = (bf16[4,16,1792]{2,1,0:T(8,128)(2,1)}, bf16[4,16,1792]{2,1,0:T(8,128)(2,1)}, u32[]{:S(2)}, u32[]{:S(2)}) collective-permute-start(bf16[4,16,1792]{2,1,0:T(8,128)(2,1)} %get-tuple-element.92), channel_id=1, source_target_pairs={{0,2},{1,3},{2,0},{3,1},{4,6},{5,7},{6,4},{7,5},{8,10},{9,11},{10,... | collective-permute-start | bytes 688136 | tf_op jit(solution)/shard_map/ppermute | solution.py:29
  22.3 1.0 convert_add_fusion
  23.3 1.6 %collective-permute-start.3 = (bf16[4,16,1792]{2,1,0:T(8,128)(2,1)}, bf16[4,16,1792]{2,1,0:T(8,128)(2,1)}, u32[]{:S(2)}, u32[]{:S(2)}) collective-permute-start(bf16[4,16,1792]{2,1,0:T(8,128)(2,1)} %get-tuple-element.91), channel_id=1, source_target_pairs={{0,4},{1,5},{2,6},{3,7},{4,0},{5,1},{6,2},{7,3},{8,12},{9,13},{10,... | collective-permute-start | bytes 688136 | tf_op jit(solution)/shard_map/ppermute | solution.py:29
  24.9 4.4 %all-to-all-start = ((bf16[16,384,128]{2,1,0:T(8,128)(2,1)}), bf16[16,384,128]{2,1,0:T(8,128)(2,1)S(1)}, u32[]{:S(2)}, u32[]{:S(2)}) async-start(bf16[16,384,128]{2,1,0:T(8,128)(2,1)} %pack.1), calls=%async_computation | async-start | bytes 3145728 | tf_op jit(solution)/shard_map/all_to_all | solution.py:512
  30.0 0.9 collective-permute-done.3
  30.9 1.2 slice_add_fusion
  32.2 1.3 collective-permute-start.8
  33.5 1.2 fusion.1
  34.7 1.6 %collective-permute-start.7 = (bf16[2,16,1792]{2,1,0:T(8,128)(2,1)S(1)}, bf16[2,16,1792]{2,1,0:T(8,128)(2,1)S(1)}, u32[]{:S(2)}, u32[]{:S(2)}) collective-permute-start(bf16[2,16,1792]{2,1,0:T(8,128)(2,1)S(1)} %get-tuple-element.96), channel_id=1, source_target_pairs={{0,4},{1,5},{2,6},{3,7},{4,0},{5,1},{6,2},{7,3},{8,12},{9,13},{10,... | collective-permute-start | bytes 344072 | tf_op jit(solution)/shard_map/ppermute | solution.py:29
  36.4 0.2 modulation.1.refs_4_
  36.6 0.6 copy-done.4
  37.3 6.9 %collective-permute-done.8 = bf16[2,16,1792]{2,1,0:T(8,128)(2,1)S(1)} collective-permute-done((bf16[2,16,1792]{2,1,0:T(8,128)(2,1)S(1)}, bf16[2,16,1792]{2,1,0:T(8,128)(2,1)S(1)}, u32[]{:S(2)}, u32[]{:S(2)}) %collective-permute-start.8) | collective-permute-done | bytes 114720 | tf_op jit(solution)/shard_map/ppermute | solution.py:29
  44.2 13.9 %collective-permute-done.7 = bf16[2,16,1792]{2,1,0:T(8,128)(2,1)S(1)} collective-permute-done((bf16[2,16,1792]{2,1,0:T(8,128)(2,1)S(1)}, bf16[2,16,1792]{2,1,0:T(8,128)(2,1)S(1)}, u32[]{:S(2)}, u32[]{:S(2)}) %collective-permute-start.7) | collective-permute-done | bytes 114720 | tf_op jit(solution)/shard_map/ppermute | solution.py:29
  58.1 4.5 %collective-permute-start.10 = (bf16[1,16,1792]{2,1,0:T(8,128)(2,1)S(1)}, bf16[1,16,1792]{2,1,0:T(8,128)(2,1)S(1)}, u32[]{:S(2)}, u32[]{:S(2)}) collective-permute-start(bf16[1,16,1792]{2,1,0:T(8,128)(2,1)S(1)} %fusion.6), channel_id=1, source_target_pairs={{0,8},{1,9},{2,10},{3,11},{4,12},{5,13},{6,14},{7,15},{8,0},{9,1},... | collective-permute-start | bytes 172040 | tf_op jit(solution)/shard_map/ppermute | solution.py:29
  62.6 0.1 collective-permute-start.9
  62.7 8.4 %collective-permute-done.10 = bf16[1,16,1792]{2,1,0:T(8,128)(2,1)S(1)} collective-permute-done((bf16[1,16,1792]{2,1,0:T(8,128)(2,1)S(1)}, bf16[1,16,1792]{2,1,0:T(8,128)(2,1)S(1)}, u32[]{:S(2)}, u32[]{:S(2)}) %collective-permute-start.10) | collective-permute-done | bytes 57376 | tf_op jit(solution)/shard_map/ppermute | solution.py:29
  71.1 0.1 multiply_reduce_fusion
  71.2 0.6 collective-permute-done.9
  71.8 0.1 multiply_reduce_fusion.1
  72.0 0.1 multiply_convert_fusion
  72.1 0.1 collective-permute-start.13
  72.2 2.9 %collective-permute-start.11 = (bf16[16,1792]{1,0:T(8,128)(2,1)S(1)}, bf16[16,1792]{1,0:T(8,128)(2,1)S(1)}, u32[]{:S(2)}, u32[]{:S(2)}) collective-permute-start(bf16[16,1792]{1,0:T(8,128)(2,1)S(1)} %get-tuple-element.109), channel_id=1, source_target_pairs={{0,8},{1,9},{2,10},{3,11},{4,12},{5,13},{6,14},{7,15},{8,0},{9,1},... | collective-permute-start | bytes 172040 | tf_op jit(solution)/shard_map/ppermute | solution.py:29
  75.1 3.8 %collective-permute-done.13 = bf16[16,1792]{1,0:T(8,128)(2,1)S(1)} collective-permute-done((bf16[16,1792]{1,0:T(8,128)(2,1)S(1)}, bf16[16,1792]{1,0:T(8,128)(2,1)S(1)}, u32[]{:S(2)}, u32[]{:S(2)}) %collective-permute-start.13) | collective-permute-done | bytes 57376 | tf_op jit(solution)/shard_map/ppermute | solution.py:29
  78.9 1.4 collective-permute-start.14
  80.4 0.1 collective-permute-start.12
  80.5 3.3 %collective-permute-done.14 = bf16[32,1792]{1,0:T(8,128)(2,1)S(1)} collective-permute-done((bf16[32,1792]{1,0:T(8,128)(2,1)S(1)}, bf16[32,1792]{1,0:T(8,128)(2,1)S(1)}, u32[]{:S(2)}, u32[]{:S(2)}) %collective-permute-start.14) | collective-permute-done | bytes 114720 | tf_op jit(solution)/shard_map/ppermute | solution.py:29
  83.8 1.4 collective-permute-done.12
  85.2 0.7 pad_maximum_fusion.refs_0_
  86.0 0.7 collective-permute-start.15
  86.7 3.7 %image_attention.2 = (f32[1024,128]{1,0:T(8,128)S(1)}, f32[1024,128]{1,0:T(8,128)S(1)}) custom-call(bf16[16,384,128]{2,1,0:T(8,128)(2,1)S(1)} %all-to-all-done.packed_ref), custom_call_target="tpu_custom_call" | custom-call | flops 1073741824 | bytes 2359296 | tf_op jit(solution)/shard_map/image_attention/pallas_call | solution.py:397
  90.3 1.9 %collective-permute-done.15.refs_1_ = bf16[64,1792]{1,0:T(8,128)(2,1)S(1)} collective-permute-done((bf16[64,1792]{1,0:T(8,128)(2,1)}, bf16[64,1792]{1,0:T(8,128)(2,1)S(1)}, u32[]{:S(2)}, u32[]{:S(2)}) %collective-permute-start.15) | collective-permute-done | bytes 229408 | tf_op jit(solution)/shard_map/ppermute | solution.py:29
  92.3 0.4 collective-permute-done.16.refs_3_
  92.7 4.1 %project.1 = (bf16[4,144,256]{2,1,0:T(8,128)(2,1)S(1)}, bf16[4,144,256]{2,1,0:T(8,128)(2,1)S(1)}, bf16[4,144,256]{2,1,0:T(8,128)(2,1)S(1)}, bf16[4,144,256]{2,1,0:T(8,128)(2,1)S(1)}) custom-call(s32[5]{0:T(128)S(1)} %copy-done.6, bf16[64,1792]{1,0:T(8,128)(2,1)S(1)} %copy-done.1, bf16[64,1792]{1,0:T(8,128)(2,1)S(1)} %collective-permute-done.15.refs_1_, ...), custom_call_target="tpu_custom_call" | custom-call | flops 754974720 | bytes 7864320 | tf_op jit(solution)/shard_map/project/pallas_call | solution.py:237
  96.8 1.4 collective-permute-start.17
  98.2 3.7 %image_attention.3 = (f32[1024,128]{1,0:T(8,128)S(1)}, f32[1024,128]{1,0:T(8,128)S(1)}) custom-call(bf16[16,384,128]{2,1,0:T(8,128)(2,1)S(1)} %all-to-all-done.packed_ref), custom_call_target="tpu_custom_call" | custom-call | flops 1073741824 | bytes 2359296 | tf_op jit(solution)/shard_map/image_attention/pallas_call | solution.py:397
  101.9 3.3 %collective-permute-done.17 = bf16[4,144,256]{2,1,0:T(8,128)(2,1)S(1)} collective-permute-done((bf16[4,144,256]{2,1,0:T(8,128)(2,1)S(1)}, bf16[4,144,256]{2,1,0:T(8,128)(2,1)S(1)}, u32[]{:S(2)}, u32[]{:S(2)}) %collective-permute-start.17) | collective-permute-done | bytes 294944 | tf_op jit(solution)/shard_map/ppermute | solution.py:29
  105.2 1.4 collective-permute-done.18
  106.5 0.1 add_convert_fusion.2
  106.6 0.7 collective-permute-start.21
  107.4 0.1 collective-permute-start.19
  107.5 4.3 %collective-permute-done.21 = bf16[2,144,256]{2,1,0:T(8,128)(2,1)S(1)} collective-permute-done((bf16[2,144,256]{2,1,0:T(8,128)(2,1)S(1)}, bf16[2,144,256]{2,1,0:T(8,128)(2,1)S(1)}, u32[]{:S(2)}, u32[]{:S(2)}) %collective-permute-start.21) | collective-permute-done | bytes 147488 | tf_op jit(solution)/shard_map/ppermute | solution.py:29
  111.8 0.1 collective-permute-start.22
  111.9 0.9 collective-permute-done.19
  112.8 2.1 %collective-permute-start.20 = (bf16[1,144,256]{2,1,0:T(8,128)(2,1)S(1)}, bf16[1,144,256]{2,1,0:T(8,128)(2,1)S(1)}, u32[]{:S(2)}, u32[]{:S(2)}) collective-permute-start(bf16[1,144,256]{2,1,0:T(8,128)(2,1)S(1)} %get-tuple-element.104), channel_id=1, source_target_pairs={{0,8},{1,9},{2,10},{3,11},{4,12},{5,13},{6,14},{7,15},{8,0},{9,1},... | collective-permute-start | bytes 221192 | tf_op jit(solution)/shard_map/ppermute | solution.py:29
  114.9 3.2 %collective-permute-done.22 = bf16[1,144,256]{2,1,0:T(8,128)(2,1)S(1)} collective-permute-done((bf16[1,144,256]{2,1,0:T(8,128)(2,1)S(1)}, bf16[1,144,256]{2,1,0:T(8,128)(2,1)S(1)}, u32[]{:S(2)}, u32[]{:S(2)}) %collective-permute-start.22) | collective-permute-done | bytes 73760 | tf_op jit(solution)/shard_map/ppermute | solution.py:29
  118.2 0.8 collective-permute-done.20
  118.9 0.7 combine.1
  119.7 0.1 collective-permute-start.23
  119.8 1.2 collective-permute-done.23.refs_5_
  121.0 3.8 %finish.1 = bf16[16,160,128]{2,1,0:T(8,128)(2,1)S(1)} custom-call(s32[5]{0:T(128)S(1)} %copy-done.6, bf16[16,384,128]{2,1,0:T(8,128)(2,1)S(1)} %all-to-all-done.packed_ref, f32[1024,128]{1,0:T(8,128)S(1)} %get-tuple-element.72.refs_0_, f32[1024,128]{1,0:T(8,128)S(1)} %get-tuple-element.73.refs_1_, f32[1024,128]{1,0:T(8,128)S(1)} %get-tuple-element.78.refs_2_, ...), custom_call_target="tpu_custom_call" | custom-call | flops 268435456 | bytes 3145728 | tf_op jit(solution)/shard_map/finish/pallas_call | solution.py:459
  124.8 20.8 %all_to_all.10.blocks_ref = bf16[16,160,128]{2,1,0:T(8,128)(2,1)S(1)} all-to-all(bf16[16,160,128]{2,1,0:T(8,128)(2,1)S(1)} %finish.1), channel_id=1, replica_groups=mesh['dp'=2,'seq'=16] {'seq'}, dimensions={0} | all-to-all | bytes 1310720 | tf_op jit(solution)/shard_map/all_to_all | solution.py:512
  145.6 1.0 unpack.1
  (41 shorter events, 0.4 us)
Async XLA Ops:
  2.9 1.0 copy-start.2
  6.0 6.3 %copy-start = (bf16[192,4096]{1,0:T(8,128)(2,1)S(1)}, bf16[192,4096]{1,0:T(8,128)(2,1)}, u32[]{:S(2)}) copy-start(bf16[192,4096]{1,0:T(8,128)(2,1)} %refs_7_.1) | copy-start | bytes 4718596
  11.8 6.7 %collective-permute-start = (bf16[8,16,1792]{2,1,0:T(8,128)(2,1)}, bf16[8,16,1792]{2,1,0:T(8,128)(2,1)S(1)}, u32[]{:S(2)}, u32[]{:S(2)}) collective-permute-start(bf16[8,16,1792]{2,1,0:T(8,128)(2,1)} %get-tuple-element.49), channel_id=1, source_target_pairs={{0,1},{1,0},{2,3},{3,2},{4,5},{5,4},{6,7},{7,6},{8,9},{9,8},{10,11... | collective-permute-start | bytes 1376264 | tf_op jit(solution)/shard_map/ppermute | solution.py:29
  12.3 18.6 %collective-permute-start.5 = (bf16[192,4096]{1,0:T(8,128)(2,1)S(1)}, bf16[192,4096]{1,0:T(8,128)(2,1)}, u32[]{:S(2)}, u32[]{:S(2)}) collective-permute-start(bf16[192,4096]{1,0:T(8,128)(2,1)S(1)} %copy-done), channel_id=1, source_target_pairs={{0,1},{1,0},{2,3},{3,2},{4,5},{5,4},{6,7},{7,6},{8,9},{9,8},{10,11... | collective-permute-start | bytes 4718600 | tf_op jit(solution)/shard_map/ppermute | solution.py:29
  12.4 18.5 %collective-permute-start.4 = (bf16[192,3584]{1,0:T(8,128)(2,1)}, bf16[192,3584]{1,0:T(8,128)(2,1)}, u32[]{:S(2)}, u32[]{:S(2)}) collective-permute-start(bf16[192,3584]{1,0:T(8,128)(2,1)} %bitcast.9.refs_5_), channel_id=1, source_target_pairs={{0,1},{1,0},{2,3},{3,2},{4,5},{5,4},{6,7},{7,6},{8,9},{9,8},{10,11... | collective-permute-start | bytes 4128776 | tf_op jit(solution)/shard_map/ppermute | solution.py:29
  12.8 5.6 %copy-start.7 = (bf16[8,16,1792]{2,1,0:T(8,128)(2,1)S(1)}, bf16[8,16,1792]{2,1,0:T(8,128)(2,1)}, u32[]{:S(2)}) copy-start(bf16[8,16,1792]{2,1,0:T(8,128)(2,1)} %get-tuple-element.48) | copy-start | bytes 1376260
  18.3 4.0 %copy-start.8 = (bf16[8,16,1792]{2,1,0:T(8,128)(2,1)S(1)}, bf16[8,16,1792]{2,1,0:T(8,128)(2,1)}, u32[]{:S(2)}) copy-start(bf16[8,16,1792]{2,1,0:T(8,128)(2,1)} %get-tuple-element.51) | copy-start | bytes 1376260
  18.3 4.0 %collective-permute-start.2 = (bf16[8,16,1792]{2,1,0:T(8,128)(2,1)}, bf16[8,16,1792]{2,1,0:T(8,128)(2,1)S(1)}, u32[]{:S(2)}, u32[]{:S(2)}) collective-permute-start(bf16[8,16,1792]{2,1,0:T(8,128)(2,1)} %get-tuple-element.52), channel_id=1, source_target_pairs={{0,1},{1,0},{2,3},{3,2},{4,5},{5,4},{6,7},{7,6},{8,9},{9,8},{10,11... | collective-permute-start | bytes 1376264 | tf_op jit(solution)/shard_map/ppermute | solution.py:29
  18.5 6.4 %copy-start.3 = (bf16[256,2,192]{0,2,1:T(8,128)(2,1)S(1)}, bf16[256,2,192]{0,2,1:T(8,128)(2,1)}, u32[]{:S(2)}) copy-start(bf16[256,2,192]{0,2,1:T(8,128)(2,1)} %param.14) | copy-start | bytes 589828
  19.4 10.6 %collective-permute-start.1 = (bf16[4,16,1792]{2,1,0:T(8,128)(2,1)}, bf16[4,16,1792]{2,1,0:T(8,128)(2,1)}, u32[]{:S(2)}, u32[]{:S(2)}) collective-permute-start(bf16[4,16,1792]{2,1,0:T(8,128)(2,1)} %get-tuple-element.92), channel_id=1, source_target_pairs={{0,2},{1,3},{2,0},{3,1},{4,6},{5,7},{6,4},{7,5},{8,10},{9,11},{10,... | collective-permute-start | bytes 688136 | tf_op jit(solution)/shard_map/ppermute | solution.py:29
  23.3 7.6 %collective-permute-start.3 = (bf16[4,16,1792]{2,1,0:T(8,128)(2,1)}, bf16[4,16,1792]{2,1,0:T(8,128)(2,1)}, u32[]{:S(2)}, u32[]{:S(2)}) collective-permute-start(bf16[4,16,1792]{2,1,0:T(8,128)(2,1)} %get-tuple-element.91), channel_id=1, source_target_pairs={{0,4},{1,5},{2,6},{3,7},{4,0},{5,1},{6,2},{7,3},{8,12},{9,13},{10,... | collective-permute-start | bytes 688136 | tf_op jit(solution)/shard_map/ppermute | solution.py:29
  24.9 5.1 %copy-start.9 = (bf16[3584]{0:T(1024)(128)(2,1)S(1)}, bf16[3584]{0:T(1024)(128)(2,1)}, u32[]{:S(2)}) copy-start(bf16[3584]{0:T(1024)(128)(2,1)} %param.12) | copy-start | bytes 21508
  24.9 5.1 %collective-permute-start.6 = (bf16[2,192,256]{2,1,0:T(8,128)(2,1)S(1)}, bf16[2,192,256]{2,1,0:T(8,128)(2,1)S(1)}, u32[]{:S(2)}, u32[]{:S(2)}) collective-permute-start(bf16[2,192,256]{2,1,0:T(8,128)(2,1)S(1)} %bitcast.39), channel_id=1, source_target_pairs={{0,1},{1,0},{2,3},{3,2},{4,5},{5,4},{6,7},{7,6},{8,9},{9,8},{10,11... | collective-permute-start | bytes 589832 | tf_op jit(solution)/shard_map/ppermute | solution.py:29
  24.9 61.1 %all-to-all-start = ((bf16[16,384,128]{2,1,0:T(8,128)(2,1)}), bf16[16,384,128]{2,1,0:T(8,128)(2,1)S(1)}, u32[]{:S(2)}, u32[]{:S(2)}) async-start(bf16[16,384,128]{2,1,0:T(8,128)(2,1)} %pack.1), calls=%async_computation | async-start | bytes 3145728 | tf_op jit(solution)/shard_map/all_to_all | solution.py:512
  32.2 12.0 %collective-permute-start.8 = (bf16[2,16,1792]{2,1,0:T(8,128)(2,1)S(1)}, bf16[2,16,1792]{2,1,0:T(8,128)(2,1)S(1)}, u32[]{:S(2)}, u32[]{:S(2)}) collective-permute-start(bf16[2,16,1792]{2,1,0:T(8,128)(2,1)S(1)} %get-tuple-element.95), channel_id=1, source_target_pairs={{0,2},{1,3},{2,0},{3,1},{4,6},{5,7},{6,4},{7,5},{8,10},{9,11},{10,... | collective-permute-start | bytes 344072 | tf_op jit(solution)/shard_map/ppermute | solution.py:29
  34.7 23.4 %collective-permute-start.7 = (bf16[2,16,1792]{2,1,0:T(8,128)(2,1)S(1)}, bf16[2,16,1792]{2,1,0:T(8,128)(2,1)S(1)}, u32[]{:S(2)}, u32[]{:S(2)}) collective-permute-start(bf16[2,16,1792]{2,1,0:T(8,128)(2,1)S(1)} %get-tuple-element.96), channel_id=1, source_target_pairs={{0,4},{1,5},{2,6},{3,7},{4,0},{5,1},{6,2},{7,3},{8,12},{9,13},{10,... | collective-permute-start | bytes 344072 | tf_op jit(solution)/shard_map/ppermute | solution.py:29
  36.6 0.6 copy-start.4
  58.1 13.0 %collective-permute-start.10 = (bf16[1,16,1792]{2,1,0:T(8,128)(2,1)S(1)}, bf16[1,16,1792]{2,1,0:T(8,128)(2,1)S(1)}, u32[]{:S(2)}, u32[]{:S(2)}) collective-permute-start(bf16[1,16,1792]{2,1,0:T(8,128)(2,1)S(1)} %fusion.6), channel_id=1, source_target_pairs={{0,8},{1,9},{2,10},{3,11},{4,12},{5,13},{6,14},{7,15},{8,0},{9,1},... | collective-permute-start | bytes 172040 | tf_op jit(solution)/shard_map/ppermute | solution.py:29
  62.6 9.2 %collective-permute-start.9 = (bf16[1,16,1792]{2,1,0:T(8,128)(2,1)S(1)}, bf16[1,16,1792]{2,1,0:T(8,128)(2,1)S(1)}, u32[]{:S(2)}, u32[]{:S(2)}) collective-permute-start(bf16[1,16,1792]{2,1,0:T(8,128)(2,1)S(1)} %fusion.9), channel_id=1, source_target_pairs={{0,8},{1,9},{2,10},{3,11},{4,12},{5,13},{6,14},{7,15},{8,0},{9,1},... | collective-permute-start | bytes 172040 | tf_op jit(solution)/shard_map/ppermute | solution.py:29
  72.1 6.8 %collective-permute-start.13 = (bf16[16,1792]{1,0:T(8,128)(2,1)S(1)}, bf16[16,1792]{1,0:T(8,128)(2,1)S(1)}, u32[]{:S(2)}, u32[]{:S(2)}) collective-permute-start(bf16[16,1792]{1,0:T(8,128)(2,1)S(1)} %get-tuple-element.108), channel_id=1, source_target_pairs={{0,8},{1,9},{2,10},{3,11},{4,12},{5,13},{6,14},{7,15},{8,0},{9,1},... | collective-permute-start | bytes 172040 | tf_op jit(solution)/shard_map/ppermute | solution.py:29
  72.2 8.2 %collective-permute-start.11 = (bf16[16,1792]{1,0:T(8,128)(2,1)S(1)}, bf16[16,1792]{1,0:T(8,128)(2,1)S(1)}, u32[]{:S(2)}, u32[]{:S(2)}) collective-permute-start(bf16[16,1792]{1,0:T(8,128)(2,1)S(1)} %get-tuple-element.109), channel_id=1, source_target_pairs={{0,8},{1,9},{2,10},{3,11},{4,12},{5,13},{6,14},{7,15},{8,0},{9,1},... | collective-permute-start | bytes 172040 | tf_op jit(solution)/shard_map/ppermute | solution.py:29
  78.9 4.9 %collective-permute-start.14 = (bf16[32,1792]{1,0:T(8,128)(2,1)S(1)}, bf16[32,1792]{1,0:T(8,128)(2,1)S(1)}, u32[]{:S(2)}, u32[]{:S(2)}) collective-permute-start(bf16[32,1792]{1,0:T(8,128)(2,1)S(1)} %pad_maximum_fusion.3), channel_id=1, source_target_pairs={{0,2},{1,3},{2,0},{3,1},{4,6},{5,7},{6,4},{7,5},{8,10},{9,11},{10,... | collective-permute-start | bytes 344072 | tf_op jit(solution)/shard_map/ppermute | solution.py:29
  80.4 4.9 %collective-permute-start.12 = (bf16[32,1792]{1,0:T(8,128)(2,1)S(1)}, bf16[32,1792]{1,0:T(8,128)(2,1)S(1)}, u32[]{:S(2)}, u32[]{:S(2)}) collective-permute-start(bf16[32,1792]{1,0:T(8,128)(2,1)S(1)} %pad_maximum_fusion.2), channel_id=1, source_target_pairs={{0,4},{1,5},{2,6},{3,7},{4,0},{5,1},{6,2},{7,3},{8,12},{9,13},{10,... | collective-permute-start | bytes 344072 | tf_op jit(solution)/shard_map/ppermute | solution.py:29
  85.9 6.8 %copy-start.5 = (f32[2,16,192]{2,1,0:T(8,128)S(1)}, f32[2,16,192]{2,1,0:T(8,128)}, u32[]{:S(2)}) copy-start(f32[2,16,192]{2,1,0:T(8,128)} %copy-done.4) | copy-start | bytes 73732
  85.9 6.8 %copy-start.6 = (s32[5]{0:T(128)S(1)}, s32[5]{0:T(128)}, u32[]{:S(2)}) copy-start(s32[5]{0:T(128)} %stack.19.place_ref) | copy-start | bytes 64
  86.0 6.8 %copy-start.1 = (bf16[64,1792]{1,0:T(8,128)(2,1)S(1)}, bf16[64,1792]{1,0:T(8,128)(2,1)}, u32[]{:S(2)}) copy-start(bf16[64,1792]{1,0:T(8,128)(2,1)} %pad_maximum_fusion.refs_0_) | copy-start | bytes 688132
  86.0 6.3 %collective-permute-start.15 = (bf16[64,1792]{1,0:T(8,128)(2,1)}, bf16[64,1792]{1,0:T(8,128)(2,1)S(1)}, u32[]{:S(2)}, u32[]{:S(2)}) collective-permute-start(bf16[64,1792]{1,0:T(8,128)(2,1)} %pad_maximum_fusion.refs_0_), channel_id=1, source_target_pairs={{0,2},{1,3},{2,0},{3,1},{4,6},{5,7},{6,4},{7,5},{8,10},{9,11},{10,... | collective-permute-start | bytes 688136 | tf_op jit(solution)/shard_map/ppermute | solution.py:29
  86.7 6.0 %collective-permute-start.16 = (bf16[64,1792]{1,0:T(8,128)(2,1)S(1)}, bf16[64,1792]{1,0:T(8,128)(2,1)S(1)}, u32[]{:S(2)}, u32[]{:S(2)}) collective-permute-start(bf16[64,1792]{1,0:T(8,128)(2,1)S(1)} %pad_maximum_fusion.1.refs_2_), channel_id=1, source_target_pairs={{0,4},{1,5},{2,6},{3,7},{4,0},{5,1},{6,2},{7,3},{8,12},{9,13},{10,... | collective-permute-start | bytes 688136 | tf_op jit(solution)/shard_map/ppermute | solution.py:29
  96.8 8.4 %collective-permute-start.17 = (bf16[4,144,256]{2,1,0:T(8,128)(2,1)S(1)}, bf16[4,144,256]{2,1,0:T(8,128)(2,1)S(1)}, u32[]{:S(2)}, u32[]{:S(2)}) collective-permute-start(bf16[4,144,256]{2,1,0:T(8,128)(2,1)S(1)} %get-tuple-element.74), channel_id=1, source_target_pairs={{0,2},{1,3},{2,0},{3,1},{4,6},{5,7},{6,4},{7,5},{8,10},{9,11},{10,... | collective-permute-start | bytes 884744 | tf_op jit(solution)/shard_map/ppermute | solution.py:29
  98.2 8.3 %collective-permute-start.18 = (bf16[4,144,256]{2,1,0:T(8,128)(2,1)S(1)}, bf16[4,144,256]{2,1,0:T(8,128)(2,1)S(1)}, u32[]{:S(2)}, u32[]{:S(2)}) collective-permute-start(bf16[4,144,256]{2,1,0:T(8,128)(2,1)S(1)} %get-tuple-element.75), channel_id=1, source_target_pairs={{0,4},{1,5},{2,6},{3,7},{4,0},{5,1},{6,2},{7,3},{8,12},{9,13},{10,... | collective-permute-start | bytes 884744 | tf_op jit(solution)/shard_map/ppermute | solution.py:29
  106.6 5.2 %collective-permute-start.21 = (bf16[2,144,256]{2,1,0:T(8,128)(2,1)S(1)}, bf16[2,144,256]{2,1,0:T(8,128)(2,1)S(1)}, u32[]{:S(2)}, u32[]{:S(2)}) collective-permute-start(bf16[2,144,256]{2,1,0:T(8,128)(2,1)S(1)} %get-tuple-element.98), channel_id=1, source_target_pairs={{0,2},{1,3},{2,0},{3,1},{4,6},{5,7},{6,4},{7,5},{8,10},{9,11},{10,... | collective-permute-start | bytes 442376 | tf_op jit(solution)/shard_map/ppermute | solution.py:29
  107.4 5.4 %collective-permute-start.19 = (bf16[2,144,256]{2,1,0:T(8,128)(2,1)S(1)}, bf16[2,144,256]{2,1,0:T(8,128)(2,1)S(1)}, u32[]{:S(2)}, u32[]{:S(2)}) collective-permute-start(bf16[2,144,256]{2,1,0:T(8,128)(2,1)S(1)} %get-tuple-element.100), channel_id=1, source_target_pairs={{0,4},{1,5},{2,6},{3,7},{4,0},{5,1},{6,2},{7,3},{8,12},{9,13},{10,... | collective-permute-start | bytes 442376 | tf_op jit(solution)/shard_map/ppermute | solution.py:29
  111.8 6.3 %collective-permute-start.22 = (bf16[1,144,256]{2,1,0:T(8,128)(2,1)S(1)}, bf16[1,144,256]{2,1,0:T(8,128)(2,1)S(1)}, u32[]{:S(2)}, u32[]{:S(2)}) collective-permute-start(bf16[1,144,256]{2,1,0:T(8,128)(2,1)S(1)} %get-tuple-element.102), channel_id=1, source_target_pairs={{0,8},{1,9},{2,10},{3,11},{4,12},{5,13},{6,14},{7,15},{8,0},{9,1},... | collective-permute-start | bytes 221192 | tf_op jit(solution)/shard_map/ppermute | solution.py:29
  112.8 6.1 %collective-permute-start.20 = (bf16[1,144,256]{2,1,0:T(8,128)(2,1)S(1)}, bf16[1,144,256]{2,1,0:T(8,128)(2,1)S(1)}, u32[]{:S(2)}, u32[]{:S(2)}) collective-permute-start(bf16[1,144,256]{2,1,0:T(8,128)(2,1)S(1)} %get-tuple-element.104), channel_id=1, source_target_pairs={{0,8},{1,9},{2,10},{3,11},{4,12},{5,13},{6,14},{7,15},{8,0},{9,1},... | collective-permute-start | bytes 221192 | tf_op jit(solution)/shard_map/ppermute | solution.py:29
  119.7 1.3 collective-permute-start.23

commit v7 on v6

--- a/solution.py
+++ b/solution.py
@@ -12,7 +12,6 @@
 HEADS = 16
 TEMB = 256
 MIB = 1024 * 1024
-DEPTH_BLOCK = 512
 
 epsilon = 1e-06
 
@@ -57,68 +56,43 @@
     return jax.nn.silu(embedding).astype(jnp.bfloat16)
 
 
-def encoder_kernel(lane, order, place_ref, act_ref, weight_ref, own_ref, other_ref, *refs):
-    *turned, held_ref, total_ref, arrived = refs
-    chips, share, width = own_ref.shape
-    at, core = place_ref[lane], place_ref[2]
-    depth = weight_ref.shape[0]
-    starts = range(0, depth, DEPTH_BLOCK)
-    loads = []
-    for step, start in enumerate(starts):
-        rows = pl.ds(start, min(DEPTH_BLOCK, depth - start))
-        load = pltpu.make_async_copy(
-            weight_ref.at[rows, pl.ds(lane * width, width)], held_ref.at[rows, :], arrived.at[step]
-        )
-        load.start()
-        loads.append(load)
-    lhs_ref = act_ref
-    if turned:
-        (lhs_ref,) = turned
-        lhs_ref[...] = act_ref[...].T
+def encoder_kernel(lanes, place_ref, act_ref, weight_ref, *refs):
+    outs, lhs_ref = refs[:-1], refs[-1]
+    chips, share, width = outs[0].shape
+    core = place_ref[2]
     half = chips * share
     first = core == 0
     tile = width // 2
-    for step, start in enumerate(starts):
-        rows = slice(start, min(start + DEPTH_BLOCK, depth))
-        loads[step].wait()
+    lhs_ref[...] = act_ref[...].T
+    for lane, order in enumerate(lanes):
+        own_ref, other_ref = outs[2 * lane], outs[2 * lane + 1]
         for column in range(0, width, tile):
-            columns = slice(column, column + tile)
+            start = lane * width + column
             result = jnp.dot(
-                lhs_ref[:, rows], held_ref[rows, columns], preferred_element_type=jnp.float32
+                lhs_ref[...], weight_ref[:, start : start + tile], preferred_element_type=jnp.float32
             )
-            if step > 0:
-                result += total_ref[:, columns]
-            if rows.stop < depth:
-                total_ref[:, columns] = result
-                continue
             own = jnp.where(first, result[:half], result[half:]).astype(own_ref.dtype)
             other = jnp.where(first, result[half:], result[:half]).astype(own_ref.dtype)
             own = own.reshape(chips, share, tile)
             other = other.reshape(chips, share, tile)
             for block in range(chips):
-                to = at ^ position(block, order)
-                own_ref[to, :, columns] = own[block]
-                other_ref[to, :, columns] = other[block]
-
-
-def encoder(lane, order, place, act, weight):
-    chips = 1 << len(order)
-    depth = weight.shape[0]
-    rows = act.size // depth
-    width = weight.shape[1] // 2
-    turn = act.shape[0] == depth
-    out = jax.ShapeDtypeStruct((chips, rows // 2 // chips, width), jnp.bfloat16)
-    return pl.pallas_call(
-        functools.partial(encoder_kernel, lane, order),
-        out_shape=(out, out) + (jax.ShapeDtypeStruct((rows, depth), act.dtype),) * turn,
-        in_specs=[SMEM_SPEC, VMEM_SPEC, pl.BlockSpec(memory_space=pl.ANY)],
-        out_specs=(VMEM_SPEC,) * (2 + turn),
-        scratch_shapes=[
-            pltpu.VMEM((depth, width), weight.dtype),
-            pltpu.VMEM((rows, width), jnp.float32),
-            pltpu.SemaphoreType.DMA((-(-depth // DEPTH_BLOCK),)),
-        ],
-        compiler_params=params(60),
+                to = place_ref[lane] ^ position(block, order)
+                own_ref[to, :, column : column + tile] = own[block]
+                other_ref[to, :, column : column + tile] = other[block]
+
+
+def encoder(lanes, place, act, weight):
+    chips = 1 << len(lanes[0])
+    depth, rows = act.shape
+    width = weight.shape[1]
+    out = jax.ShapeDtypeStruct((chips, rows // 2 // chips, width // 2), jnp.bfloat16)
+    return pl.pallas_call(
+        functools.partial(encoder_kernel, lanes),
+        out_shape=(out,) * 4,
+        in_specs=[SMEM_SPEC, VMEM_SPEC, VMEM_SPEC],
+        out_specs=(VMEM_SPEC,) * 4,
+        scratch_shapes=[pltpu.VMEM((rows, depth), jnp.bfloat16)],
+        compiler_params=params(24),
         cost_estimate=pl.CostEstimate(
             flops=2 * rows * depth * width,
             bytes_accessed=2 * (depth * rows + depth * width + rows * width),
@@ -516,17 +490,15 @@
     act, packed = tie((enc_act[0].T, packed))
     packed = exchange(packed)
     keep, sent = [], []
-    for lane, order in enumerate(lanes):
-        own, other, *turned = encoder(lane, order, place, act, down_weight)
-        if lane == 0:
-            act = turned[0]
+    encoded = encoder(lanes, place, act, down_weight)
+    for own, other in (encoded[:2], encoded[2:]):
         got = swap(other, 1)
         sent.append(add(own[chips // 2 :], got[chips // 2 :], jnp.bfloat16))
         keep.append(add(own[: chips // 2], got[: chips // 2], jnp.float32))
     for step in range(rounds):
         got = [swap(part, 2 * order[step]) for part, order in zip(sent, lanes)]
         if step == 0:
-            got, win1, kv1, mod1 = tie((got, win1, kv1, mod1))
+            got, win1, kv1, mod1, packed = tie((got, win1, kv1, mod1, packed))
             lines = modulation(time, mod0, mod1)
         if step == 1:
             got, lines = tie((got, lines))

time: 147 us -> 139 us (0.946)
  waiting for transfers between devices: 56.9 us -> 45.1 us
  Pallas kernels: 29.8 us -> 20.5 us
  local copies, waits for them, and re-layouts: 3.91 us -> 10.7 us
  starting transfers between devices: 27.3 us -> 33.1 us
    ppermute x24, waiting for transfers between devices: 56.9 us -> 45.1 us  [swap(): return lax.ppermute(value, 'seq', [(i, i ^ mask) for i in range(devices)])]
    pallas_call x2 -> x1, Pallas kernels: 11.2 us -> 3.47 us  [encoder(): pl.pallas_call(functools.partial(encoder_kernel, lanes), out_shape=(out,)...]
    unnamed x20 -> x30, local copies, waits for them, and re-layouts: 1.59 us -> 8.36 us
    all_to_all x1, starting transfers between devices: 4.41 us -> 7.36 us  [exchange(): return lax.all_to_all(rows, 'seq', split_axis=0, concat_axis=0, tiled=True)]
    ppermute x24, starting transfers between devices: 22.9 us -> 25.8 us  [swap(): return lax.ppermute(value, 'seq', [(i, i ^ mask) for i in range(devices)])]
    pallas_call x1, Pallas kernels: 4.06 us -> 2.33 us  [project(): pl.pallas_call(functools.partial(project_kernel, lanes), out_shape=(out,)...]
  transfers between devices with their start and end apart: 25 -> 25, of which waited for: 17 -> 20; matrix products, arithmetic and copies ran while one was open for 4% -> 3% of each run, Pallas kernels for 9% -> 8%
where the time goes in v7:
time: 139 us
  waiting for transfers between devices  45.1 us (32%)
  starting transfers between devices  33.1 us (24%)
  blocking collectives  22.2 us (16%)
  Pallas kernels  20.5 us (15%)
  local copies, waits for them, and re-layouts  10.7 us (8%)
  other arithmetic  4.91 us (4%)
  between operations  2.18 us (2%)
    ppermute x24, waiting for transfers between devices, swap(): return lax.ppermute(value, 'seq', [(i, i ^ mask) for i in range(devices)])  45.1 us
    ppermute x24, starting transfers between devices, swap(): return lax.ppermute(value, 'seq', [(i, i ^ mask) for i in range(devices)])  25.8 us
    all_to_all x1, blocking collectives, exchange(): return lax.all_to_all(rows, 'seq', split_axis=0, concat_axis=0, tiled=True)  22.2 us
    unnamed x30, local copies, waits for them, and re-layouts  8.36 us
    pallas_call x2, Pallas kernels, image_attention(): pl.pallas_call(functools.partial(image_kernel, factor, call, img_dev), ou...  7.51 us
    all_to_all x1, starting transfers between devices, exchange(): return lax.all_to_all(rows, 'seq', split_axis=0, concat_axis=0, tiled=True)  7.36 us
    pallas_call x1, Pallas kernels, finish(): pl.pallas_call(functools.partial(finish_kernel, factor, len(images) // 2,...  3.76 us
    pallas_call x1, Pallas kernels, encoder(): pl.pallas_call(functools.partial(encoder_kernel, lanes), out_shape=(out,)...  3.47 us
  transfers between devices with their start and end apart: 25, of which 20 were waited for; matrix products, arithmetic and copies ran while one was open for 3% of the time, Pallas kernels for 8%

profile of v7, /device:TPU:0, one launch (start us, length us, event | category | flops | bytes accessed | tf_op | source)
XLA Modules:
  0.0 138.7 jit_solution(1383189168470683764)
XLA Ops:
  0.6 1.6 %copy.12 = bf16[1,128,2,2048]{3,1,2,0:T(8,128)(2,1)S(1)} copy(bf16[1,128,2,2048]{3,2,1,0:T(2,128)(2,1)} %param.19) | data formatting | bytes 2097152 | tf_op jit(solution)/shard_map/optimization_barrier | solution.py:488
  2.3 1.0 copy-done.9
  3.3 1.4 %pack.1 = bf16[16,384,128]{2,1,0:T(8,128)(2,1)} custom-call(bf16[128,2048]{1,0:T(8,128)(2,1)S(1)} %bitcast.41, bf16[128,2048]{1,0:T(8,128)(2,1)S(1)} %get-tuple-element.89.keys_ref, bf16[128,2048]{1,0:T(8,128)(2,1)S(1)} %get-tuple-element.88.values_ref), custom_call_target="tpu_custom_call" | custom-call | bytes 3145728 | tf_op jit(solution)/shard_map/pack/pallas_call | solution.py:296
  4.7 7.4 %all-to-all-start = ((bf16[16,384,128]{2,1,0:T(8,128)(2,1)}), bf16[16,384,128]{2,1,0:T(8,128)(2,1)S(1)}, u32[]{:S(2)}, u32[]{:S(2)}) async-start(bf16[16,384,128]{2,1,0:T(8,128)(2,1)} %pack.1), calls=%async_computation | async-start | bytes 3145728 | tf_op jit(solution)/shard_map/all_to_all | solution.py:486
  12.8 3.4 %copy-done = bf16[1184,3584]{1,0:T(8,128)(2,1)S(1)} copy-done((bf16[1184,3584]{1,0:T(8,128)(2,1)S(1)}, bf16[1184,3584]{1,0:T(8,128)(2,1)}, u32[]{:S(2)}) %copy-start) | copy-done | bytes 8486936
  16.2 1.1 copy-done.8
  17.3 3.5 %encoder.1 = (bf16[8,16,1792]{2,1,0:T(8,128)(2,1)S(1)}, bf16[8,16,1792]{2,1,0:T(8,128)(2,1)S(1)}, bf16[8,16,1792]{2,1,0:T(8,128)(2,1)S(1)}, bf16[8,16,1792]{2,1,0:T(8,128)(2,1)S(1)}) custom-call(s32[5]{0:T(128)S(1)} %stack.19.place_ref, bf16[1184,256]{1,0:T(8,128)(2,1)S(1)} %bitcast.40, bf16[1184,3584]{1,0:T(8,128)(2,1)S(1)} %copy-done), custom_call_target="tpu_custom_call" | custom-call | flops 2172649472 | bytes 10928128 | tf_op jit(solution)/shard_map/encoder/pallas_call | solution.py:89
  20.8 0.4 collective-permute-start
  21.2 0.1 collective-permute-start.5
  21.4 0.4 collective-permute-start.4
  21.9 0.8 collective-permute-done
  22.7 0.9 add_convert_fusion.1
  23.5 1.9 %collective-permute-start.1 = (bf16[4,16,1792]{2,1,0:T(8,128)(2,1)S(1)}, bf16[4,16,1792]{2,1,0:T(8,128)(2,1)S(1)}, u32[]{:S(2)}, u32[]{:S(2)}) collective-permute-start(bf16[4,16,1792]{2,1,0:T(8,128)(2,1)S(1)} %get-tuple-element.92), channel_id=1, source_target_pairs={{0,2},{1,3},{2,0},{3,1},{4,6},{5,7},{6,4},{7,5},{8,10},{9,11},{10,... | collective-permute-start | bytes 688136 | tf_op jit(solution)/shard_map/ppermute | solution.py:28
  25.4 2.1 %collective-permute-done.2 = bf16[8,16,1792]{2,1,0:T(8,128)(2,1)S(1)} collective-permute-done((bf16[8,16,1792]{2,1,0:T(8,128)(2,1)S(1)}, bf16[8,16,1792]{2,1,0:T(8,128)(2,1)S(1)}, u32[]{:S(2)}, u32[]{:S(2)}) %collective-permute-start.2) | collective-permute-done | bytes 458784 | tf_op jit(solution)/shard_map/ppermute | solution.py:28
  27.6 0.9 convert_add_fusion
  28.4 1.9 %collective-permute-start.3 = (bf16[4,16,1792]{2,1,0:T(8,128)(2,1)S(1)}, bf16[4,16,1792]{2,1,0:T(8,128)(2,1)S(1)}, u32[]{:S(2)}, u32[]{:S(2)}) collective-permute-start(bf16[4,16,1792]{2,1,0:T(8,128)(2,1)S(1)} %get-tuple-element.91), channel_id=1, source_target_pairs={{0,4},{1,5},{2,6},{3,7},{4,0},{5,1},{6,2},{7,3},{8,12},{9,13},{10,... | collective-permute-start | bytes 688136 | tf_op jit(solution)/shard_map/ppermute | solution.py:28
  31.0 0.6 fusion.13
  31.6 0.2 collective-permute-done.6.mod1_ref
  31.8 4.9 %collective-permute-done.1 = bf16[4,16,1792]{2,1,0:T(8,128)(2,1)S(1)} collective-permute-done((bf16[4,16,1792]{2,1,0:T(8,128)(2,1)S(1)}, bf16[4,16,1792]{2,1,0:T(8,128)(2,1)S(1)}, u32[]{:S(2)}, u32[]{:S(2)}) %collective-permute-start.1) | collective-permute-done | bytes 229408 | tf_op jit(solution)/shard_map/ppermute | solution.py:28
  36.7 6.8 %collective-permute-done.3 = bf16[4,16,1792]{2,1,0:T(8,128)(2,1)S(1)} collective-permute-done((bf16[4,16,1792]{2,1,0:T(8,128)(2,1)S(1)}, bf16[4,16,1792]{2,1,0:T(8,128)(2,1)S(1)}, u32[]{:S(2)}, u32[]{:S(2)}) %collective-permute-start.3) | collective-permute-done | bytes 229408 | tf_op jit(solution)/shard_map/ppermute | solution.py:28
  43.5 0.7 copy-done.12
  44.2 1.1 copy-done.6
  45.3 1.1 copy-done.2
  46.4 1.2 slice_add_fusion
  47.7 1.7 %collective-permute-start.8 = (bf16[2,16,1792]{2,1,0:T(8,128)(2,1)S(1)}, bf16[2,16,1792]{2,1,0:T(8,128)(2,1)S(1)}, u32[]{:S(2)}, u32[]{:S(2)}) collective-permute-start(bf16[2,16,1792]{2,1,0:T(8,128)(2,1)S(1)} %get-tuple-element.95), channel_id=1, source_target_pairs={{0,2},{1,3},{2,0},{3,1},{4,6},{5,7},{6,4},{7,5},{8,10},{9,11},{10,... | collective-permute-start | bytes 344072 | tf_op jit(solution)/shard_map/ppermute | solution.py:28
  49.4 1.2 fusion.1
  50.6 3.5 %collective-permute-start.7 = (bf16[2,16,1792]{2,1,0:T(8,128)(2,1)S(1)}, bf16[2,16,1792]{2,1,0:T(8,128)(2,1)S(1)}, u32[]{:S(2)}, u32[]{:S(2)}) collective-permute-start(bf16[2,16,1792]{2,1,0:T(8,128)(2,1)S(1)} %get-tuple-element.96), channel_id=1, source_target_pairs={{0,4},{1,5},{2,6},{3,7},{4,0},{5,1},{6,2},{7,3},{8,12},{9,13},{10,... | collective-permute-start | bytes 344072 | tf_op jit(solution)/shard_map/ppermute | solution.py:28
  54.2 0.2 modulation.1.refs_4_
  54.4 3.0 %collective-permute-done.7 = bf16[2,16,1792]{2,1,0:T(8,128)(2,1)S(1)} collective-permute-done((bf16[2,16,1792]{2,1,0:T(8,128)(2,1)S(1)}, bf16[2,16,1792]{2,1,0:T(8,128)(2,1)S(1)}, u32[]{:S(2)}, u32[]{:S(2)}) %collective-permute-start.7) | collective-permute-done | bytes 114720 | tf_op jit(solution)/shard_map/ppermute | solution.py:28
  57.5 2.4 %collective-permute-start.10 = (bf16[1,16,1792]{2,1,0:T(8,128)(2,1)S(1)}, bf16[1,16,1792]{2,1,0:T(8,128)(2,1)S(1)}, u32[]{:S(2)}, u32[]{:S(2)}) collective-permute-start(bf16[1,16,1792]{2,1,0:T(8,128)(2,1)S(1)} %fusion.6), channel_id=1, source_target_pairs={{0,8},{1,9},{2,10},{3,11},{4,12},{5,13},{6,14},{7,15},{8,0},{9,1},... | collective-permute-start | bytes 172040 | tf_op jit(solution)/shard_map/ppermute | solution.py:28
  59.9 0.6 collective-permute-start.9
  60.6 3.9 %collective-permute-done.10 = bf16[1,16,1792]{2,1,0:T(8,128)(2,1)S(1)} collective-permute-done((bf16[1,16,1792]{2,1,0:T(8,128)(2,1)S(1)}, bf16[1,16,1792]{2,1,0:T(8,128)(2,1)S(1)}, u32[]{:S(2)}, u32[]{:S(2)}) %collective-permute-start.10) | collective-permute-done | bytes 57376 | tf_op jit(solution)/shard_map/ppermute | solution.py:28
  64.4 0.1 multiply_reduce_fusion
  64.6 1.1 collective-permute-done.9
  65.7 0.1 multiply_reduce_fusion.1
  66.0 2.9 %collective-permute-start.11 = (bf16[16,1792]{1,0:T(8,128)(2,1)S(1)}, bf16[16,1792]{1,0:T(8,128)(2,1)S(1)}, u32[]{:S(2)}, u32[]{:S(2)}) collective-permute-start(bf16[16,1792]{1,0:T(8,128)(2,1)S(1)} %get-tuple-element.109), channel_id=1, source_target_pairs={{0,8},{1,9},{2,10},{3,11},{4,12},{5,13},{6,14},{7,15},{8,0},{9,1},... | collective-permute-start | bytes 172040 | tf_op jit(solution)/shard_map/ppermute | solution.py:28
  68.9 3.1 %collective-permute-done.13 = bf16[16,1792]{1,0:T(8,128)(2,1)S(1)} collective-permute-done((bf16[16,1792]{1,0:T(8,128)(2,1)S(1)}, bf16[16,1792]{1,0:T(8,128)(2,1)S(1)}, u32[]{:S(2)}, u32[]{:S(2)}) %collective-permute-start.13) | collective-permute-done | bytes 57376 | tf_op jit(solution)/shard_map/ppermute | solution.py:28
  72.0 0.7 collective-permute-start.14
  72.7 1.2 collective-permute-start.12
  73.9 3.0 %collective-permute-done.14 = bf16[32,1792]{1,0:T(8,128)(2,1)S(1)} collective-permute-done((bf16[32,1792]{1,0:T(8,128)(2,1)S(1)}, bf16[32,1792]{1,0:T(8,128)(2,1)S(1)}, u32[]{:S(2)}, u32[]{:S(2)}) %collective-permute-start.14) | collective-permute-done | bytes 114720 | tf_op jit(solution)/shard_map/ppermute | solution.py:28
  76.9 0.7 collective-permute-done.12
  77.6 1.7 %collective-permute-start.15 = (bf16[64,1792]{1,0:T(8,128)(2,1)S(1)}, bf16[64,1792]{1,0:T(8,128)(2,1)S(1)}, u32[]{:S(2)}, u32[]{:S(2)}) collective-permute-start(bf16[64,1792]{1,0:T(8,128)(2,1)S(1)} %pad_maximum_fusion.refs_0_), channel_id=1, source_target_pairs={{0,2},{1,3},{2,0},{3,1},{4,6},{5,7},{6,4},{7,5},{8,10},{9,11},{10,... | collective-permute-start | bytes 688136 | tf_op jit(solution)/shard_map/ppermute | solution.py:28
  79.4 3.7 %image_attention.2 = (f32[1024,128]{1,0:T(8,128)S(1)}, f32[1024,128]{1,0:T(8,128)S(1)}) custom-call(bf16[16,384,128]{2,1,0:T(8,128)(2,1)S(1)} %all-to-all-done.packed_ref), custom_call_target="tpu_custom_call" | custom-call | flops 1073741824 | bytes 2359296 | tf_op jit(solution)/shard_map/image_attention/pallas_call | solution.py:371
  83.1 0.6 collective-permute-done.15.refs_1_
  83.7 1.6 %collective-permute-done.16.refs_3_ = bf16[64,1792]{1,0:T(8,128)(2,1)S(1)} collective-permute-done((bf16[64,1792]{1,0:T(8,128)(2,1)S(1)}, bf16[64,1792]{1,0:T(8,128)(2,1)S(1)}, u32[]{:S(2)}, u32[]{:S(2)}) %collective-permute-start.16) | collective-permute-done | bytes 229408 | tf_op jit(solution)/shard_map/ppermute | solution.py:28
  85.3 2.3 %project.1 = (bf16[4,144,256]{2,1,0:T(8,128)(2,1)S(1)}, bf16[4,144,256]{2,1,0:T(8,128)(2,1)S(1)}, bf16[4,144,256]{2,1,0:T(8,128)(2,1)S(1)}, bf16[4,144,256]{2,1,0:T(8,128)(2,1)S(1)}) custom-call(s32[5]{0:T(128)S(1)} %stack.19.place_ref, bf16[64,1792]{1,0:T(8,128)(2,1)S(1)} %pad_maximum_fusion.refs_0_, bf16[64,1792]{1,0:T(8,128)(2,1)S(1)} %collective-permute-done.15.refs_1_, ...), custom_call_target="tpu_custom_call" | custom-call | flops 754974720 | bytes 7864320 | tf_op jit(solution)/shard_map/project/pallas_call | solution.py:211
  87.7 0.5 collective-permute-start.17
  88.2 1.1 collective-permute-start.18
  89.2 3.8 %image_attention.3 = (f32[1024,128]{1,0:T(8,128)S(1)}, f32[1024,128]{1,0:T(8,128)S(1)}) custom-call(bf16[16,384,128]{2,1,0:T(8,128)(2,1)S(1)} %all-to-all-done.packed_ref), custom_call_target="tpu_custom_call" | custom-call | flops 1073741824 | bytes 2359296 | tf_op jit(solution)/shard_map/image_attention/pallas_call | solution.py:371
  93.1 2.9 %collective-permute-done.17 = bf16[4,144,256]{2,1,0:T(8,128)(2,1)S(1)} collective-permute-done((bf16[4,144,256]{2,1,0:T(8,128)(2,1)S(1)}, bf16[4,144,256]{2,1,0:T(8,128)(2,1)S(1)}, u32[]{:S(2)}, u32[]{:S(2)}) %collective-permute-start.17) | collective-permute-done | bytes 294944 | tf_op jit(solution)/shard_map/ppermute | solution.py:28
  96.0 0.4 collective-permute-done.18
  96.5 1.7 %collective-permute-start.21 = (bf16[2,144,256]{2,1,0:T(8,128)(2,1)S(1)}, bf16[2,144,256]{2,1,0:T(8,128)(2,1)S(1)}, u32[]{:S(2)}, u32[]{:S(2)}) collective-permute-start(bf16[2,144,256]{2,1,0:T(8,128)(2,1)S(1)} %get-tuple-element.98), channel_id=1, source_target_pairs={{0,2},{1,3},{2,0},{3,1},{4,6},{5,7},{6,4},{7,5},{8,10},{9,11},{10,... | collective-permute-start | bytes 442376 | tf_op jit(solution)/shard_map/ppermute | solution.py:28
  98.3 0.2 collective-permute-start.19
  98.4 3.3 %collective-permute-done.21 = bf16[2,144,256]{2,1,0:T(8,128)(2,1)S(1)} collective-permute-done((bf16[2,144,256]{2,1,0:T(8,128)(2,1)S(1)}, bf16[2,144,256]{2,1,0:T(8,128)(2,1)S(1)}, u32[]{:S(2)}, u32[]{:S(2)}) %collective-permute-start.21) | collective-permute-done | bytes 147488 | tf_op jit(solution)/shard_map/ppermute | solution.py:28
  101.8 1.1 collective-permute-start.22
  102.9 0.6 collective-permute-done.19
  103.5 1.4 collective-permute-start.20
  104.9 3.0 %collective-permute-done.22 = bf16[1,144,256]{2,1,0:T(8,128)(2,1)S(1)} collective-permute-done((bf16[1,144,256]{2,1,0:T(8,128)(2,1)S(1)}, bf16[1,144,256]{2,1,0:T(8,128)(2,1)S(1)}, u32[]{:S(2)}, u32[]{:S(2)}) %collective-permute-start.22) | collective-permute-done | bytes 73760 | tf_op jit(solution)/shard_map/ppermute | solution.py:28
  107.9 1.7 %collective-permute-done.20 = bf16[1,144,256]{2,1,0:T(8,128)(2,1)S(1)} collective-permute-done((bf16[1,144,256]{2,1,0:T(8,128)(2,1)S(1)}, bf16[1,144,256]{2,1,0:T(8,128)(2,1)S(1)}, u32[]{:S(2)}, u32[]{:S(2)}) %collective-permute-start.20) | collective-permute-done | bytes 73760 | tf_op jit(solution)/shard_map/ppermute | solution.py:28
  109.6 0.7 combine.1
  110.5 1.2 collective-permute-done.23.refs_5_
  111.7 3.8 %finish.1 = bf16[16,160,128]{2,1,0:T(8,128)(2,1)S(1)} custom-call(s32[5]{0:T(128)S(1)} %stack.19.place_ref, bf16[16,384,128]{2,1,0:T(8,128)(2,1)S(1)} %all-to-all-done.packed_ref, f32[1024,128]{1,0:T(8,128)S(1)} %get-tuple-element.72.refs_0_, f32[1024,128]{1,0:T(8,128)S(1)} %get-tuple-element.73.refs_1_, f32[1024,128]{1,0:T(8,128)S(1)} %get-tuple-element.78.refs_2_, ...), custom_call_target="tpu_custom_call" | custom-call | flops 268435456 | bytes 3145728 | tf_op jit(solution)/shard_map/finish/pallas_call | solution.py:433
  115.5 22.2 %all_to_all.10.blocks_ref = bf16[16,160,128]{2,1,0:T(8,128)(2,1)S(1)} all-to-all(bf16[16,160,128]{2,1,0:T(8,128)(2,1)S(1)} %finish.1), channel_id=1, replica_groups=mesh['dp'=2,'seq'=16] {'seq'}, dimensions={0} | all-to-all | bytes 1310720 | tf_op jit(solution)/shard_map/all_to_all | solution.py:486
  137.7 1.0 unpack.1
  (50 shorter events, 1.0 us)
Async XLA Ops:
  2.2 1.0 copy-start.9
  4.7 41.7 %all-to-all-start = ((bf16[16,384,128]{2,1,0:T(8,128)(2,1)}), bf16[16,384,128]{2,1,0:T(8,128)(2,1)S(1)}, u32[]{:S(2)}, u32[]{:S(2)}) async-start(bf16[16,384,128]{2,1,0:T(8,128)(2,1)} %pack.1), calls=%async_computation | async-start | bytes 3145728 | tf_op jit(solution)/shard_map/all_to_all | solution.py:486
  12.8 3.4 %copy-start = (bf16[1184,3584]{1,0:T(8,128)(2,1)S(1)}, bf16[1184,3584]{1,0:T(8,128)(2,1)}, u32[]{:S(2)}) copy-start(bf16[1184,3584]{1,0:T(8,128)(2,1)} %weight_ref.1) | copy-start | bytes 25460740
  16.2 1.1 copy-start.8
  17.3 3.9 %copy-start.1 = (bf16[192,4096]{1,0:T(8,128)(2,1)S(1)}, bf16[192,4096]{1,0:T(8,128)(2,1)}, u32[]{:S(2)}) copy-start(bf16[192,4096]{1,0:T(8,128)(2,1)} %refs_7_.1) | copy-start | bytes 4718596
  17.3 4.1 %copy-start.4 = (bf16[3584,192]{0,1:T(8,128)(2,1)S(1)}, bf16[3584,192]{0,1:T(8,128)(2,1)}, u32[]{:S(2)}) copy-start(bf16[3584,192]{0,1:T(8,128)(2,1)} %param.13) | copy-start | bytes 4128772
  20.8 1.9 %collective-permute-start = (bf16[8,16,1792]{2,1,0:T(8,128)(2,1)S(1)}, bf16[8,16,1792]{2,1,0:T(8,128)(2,1)S(1)}, u32[]{:S(2)}, u32[]{:S(2)}) collective-permute-start(bf16[8,16,1792]{2,1,0:T(8,128)(2,1)S(1)} %get-tuple-element.49), channel_id=1, source_target_pairs={{0,1},{1,0},{2,3},{3,2},{4,5},{5,4},{6,7},{7,6},{8,9},{9,8},{10,11... | collective-permute-start | bytes 1376264 | tf_op jit(solution)/shard_map/ppermute | solution.py:28
  21.2 24.1 %collective-permute-start.5 = (bf16[192,4096]{1,0:T(8,128)(2,1)S(1)}, bf16[192,4096]{1,0:T(8,128)(2,1)S(1)}, u32[]{:S(2)}, u32[]{:S(2)}) collective-permute-start(bf16[192,4096]{1,0:T(8,128)(2,1)S(1)} %copy-done.1), channel_id=1, source_target_pairs={{0,1},{1,0},{2,3},{3,2},{4,5},{5,4},{6,7},{7,6},{8,9},{9,8},{10,11... | collective-permute-start | bytes 4718600 | tf_op jit(solution)/shard_map/ppermute | solution.py:28
  21.4 22.2 %collective-permute-start.4 = (bf16[192,3584]{1,0:T(8,128)(2,1)S(1)}, bf16[192,3584]{1,0:T(8,128)(2,1)S(1)}, u32[]{:S(2)}, u32[]{:S(2)}) collective-permute-start(bf16[192,3584]{1,0:T(8,128)(2,1)S(1)} %bitcast.38), channel_id=1, source_target_pairs={{0,1},{1,0},{2,3},{3,2},{4,5},{5,4},{6,7},{7,6},{8,9},{9,8},{10,11... | collective-permute-start | bytes 4128776 | tf_op jit(solution)/shard_map/ppermute | solution.py:28
  21.8 5.8 %collective-permute-start.2 = (bf16[8,16,1792]{2,1,0:T(8,128)(2,1)S(1)}, bf16[8,16,1792]{2,1,0:T(8,128)(2,1)S(1)}, u32[]{:S(2)}, u32[]{:S(2)}) collective-permute-start(bf16[8,16,1792]{2,1,0:T(8,128)(2,1)S(1)} %get-tuple-element.51), channel_id=1, source_target_pairs={{0,1},{1,0},{2,3},{3,2},{4,5},{5,4},{6,7},{7,6},{8,9},{9,8},{10,11... | collective-permute-start | bytes 1376264 | tf_op jit(solution)/shard_map/ppermute | solution.py:28
  22.7 7.7 %copy-start.10 = (bf16[256,2,192]{0,2,1:T(8,128)(2,1)S(1)}, bf16[256,2,192]{0,2,1:T(8,128)(2,1)}, u32[]{:S(2)}) copy-start(bf16[256,2,192]{0,2,1:T(8,128)(2,1)} %param.14) | copy-start | bytes 589828
  22.7 8.3 %copy-start.14 = (bf16[3584]{0:T(1024)(128)(2,1)S(1)}, bf16[3584]{0:T(1024)(128)(2,1)}, u32[]{:S(2)}) copy-start(bf16[3584]{0:T(1024)(128)(2,1)} %param.12) | copy-start | bytes 21508
  23.5 13.2 %collective-permute-start.1 = (bf16[4,16,1792]{2,1,0:T(8,128)(2,1)S(1)}, bf16[4,16,1792]{2,1,0:T(8,128)(2,1)S(1)}, u32[]{:S(2)}, u32[]{:S(2)}) collective-permute-start(bf16[4,16,1792]{2,1,0:T(8,128)(2,1)S(1)} %get-tuple-element.92), channel_id=1, source_target_pairs={{0,2},{1,3},{2,0},{3,1},{4,6},{5,7},{6,4},{7,5},{8,10},{9,11},{10,... | collective-permute-start | bytes 688136 | tf_op jit(solution)/shard_map/ppermute | solution.py:28
  28.4 15.1 %collective-permute-start.3 = (bf16[4,16,1792]{2,1,0:T(8,128)(2,1)S(1)}, bf16[4,16,1792]{2,1,0:T(8,128)(2,1)S(1)}, u32[]{:S(2)}, u32[]{:S(2)}) collective-permute-start(bf16[4,16,1792]{2,1,0:T(8,128)(2,1)S(1)} %get-tuple-element.91), channel_id=1, source_target_pairs={{0,4},{1,5},{2,6},{3,7},{4,0},{5,1},{6,2},{7,3},{8,12},{9,13},{10,... | collective-permute-start | bytes 688136 | tf_op jit(solution)/shard_map/ppermute | solution.py:28
  30.3 1.4 %collective-permute-start.6 = (bf16[2,192,256]{2,1,0:T(8,128)(2,1)S(1)}, bf16[2,192,256]{2,1,0:T(8,128)(2,1)S(1)}, u32[]{:S(2)}, u32[]{:S(2)}) collective-permute-start(bf16[2,192,256]{2,1,0:T(8,128)(2,1)S(1)} %bitcast.42), channel_id=1, source_target_pairs={{0,1},{1,0},{2,3},{3,2},{4,5},{5,4},{6,7},{7,6},{8,9},{9,8},{10,11... | collective-permute-start | bytes 589832 | tf_op jit(solution)/shard_map/ppermute | solution.py:28
  36.7 6.8 %copy-start.11 = (bf16[4,16,1792]{2,1,0:T(8,128)(2,1)}, bf16[4,16,1792]{2,1,0:T(8,128)(2,1)S(1)}, u32[]{:S(2)}) copy-start(bf16[4,16,1792]{2,1,0:T(8,128)(2,1)S(1)} %collective-permute-done.1) | copy-start | bytes 688132
  43.5 0.7 copy-start.12
  44.2 1.1 copy-start.6
  45.3 1.1 copy-start.2
  46.4 19.4 %copy-start.13 = (f32[1792]{0:T(1024)S(1)}, f32[1792]{0:T(1024)}, u32[]{:S(2)}) copy-start(f32[1792]{0:T(1024)} %get-tuple-element.107) | copy-start | bytes 21508
  47.7 6.7 %collective-permute-start.8 = (bf16[2,16,1792]{2,1,0:T(8,128)(2,1)S(1)}, bf16[2,16,1792]{2,1,0:T(8,128)(2,1)S(1)}, u32[]{:S(2)}, u32[]{:S(2)}) collective-permute-start(bf16[2,16,1792]{2,1,0:T(8,128)(2,1)S(1)} %get-tuple-element.95), channel_id=1, source_target_pairs={{0,2},{1,3},{2,0},{3,1},{4,6},{5,7},{6,4},{7,5},{8,10},{9,11},{10,... | collective-permute-start | bytes 344072 | tf_op jit(solution)/shard_map/ppermute | solution.py:28
  50.6 6.9 %collective-permute-start.7 = (bf16[2,16,1792]{2,1,0:T(8,128)(2,1)S(1)}, bf16[2,16,1792]{2,1,0:T(8,128)(2,1)S(1)}, u32[]{:S(2)}, u32[]{:S(2)}) collective-permute-start(bf16[2,16,1792]{2,1,0:T(8,128)(2,1)S(1)} %get-tuple-element.96), channel_id=1, source_target_pairs={{0,4},{1,5},{2,6},{3,7},{4,0},{5,1},{6,2},{7,3},{8,12},{9,13},{10,... | collective-permute-start | bytes 344072 | tf_op jit(solution)/shard_map/ppermute | solution.py:28
  57.5 7.0 %collective-permute-start.10 = (bf16[1,16,1792]{2,1,0:T(8,128)(2,1)S(1)}, bf16[1,16,1792]{2,1,0:T(8,128)(2,1)S(1)}, u32[]{:S(2)}, u32[]{:S(2)}) collective-permute-start(bf16[1,16,1792]{2,1,0:T(8,128)(2,1)S(1)} %fusion.6), channel_id=1, source_target_pairs={{0,8},{1,9},{2,10},{3,11},{4,12},{5,13},{6,14},{7,15},{8,0},{9,1},... | collective-permute-start | bytes 172040 | tf_op jit(solution)/shard_map/ppermute | solution.py:28
  59.9 5.8 %collective-permute-start.9 = (bf16[1,16,1792]{2,1,0:T(8,128)(2,1)S(1)}, bf16[1,16,1792]{2,1,0:T(8,128)(2,1)S(1)}, u32[]{:S(2)}, u32[]{:S(2)}) collective-permute-start(bf16[1,16,1792]{2,1,0:T(8,128)(2,1)S(1)} %fusion.9), channel_id=1, source_target_pairs={{0,8},{1,9},{2,10},{3,11},{4,12},{5,13},{6,14},{7,15},{8,0},{9,1},... | collective-permute-start | bytes 172040 | tf_op jit(solution)/shard_map/ppermute | solution.py:28
  65.9 6.1 %collective-permute-start.13 = (bf16[16,1792]{1,0:T(8,128)(2,1)S(1)}, bf16[16,1792]{1,0:T(8,128)(2,1)S(1)}, u32[]{:S(2)}, u32[]{:S(2)}) collective-permute-start(bf16[16,1792]{1,0:T(8,128)(2,1)S(1)} %get-tuple-element.108), channel_id=1, source_target_pairs={{0,8},{1,9},{2,10},{3,11},{4,12},{5,13},{6,14},{7,15},{8,0},{9,1},... | collective-permute-start | bytes 172040 | tf_op jit(solution)/shard_map/ppermute | solution.py:28
  66.0 6.7 %collective-permute-start.11 = (bf16[16,1792]{1,0:T(8,128)(2,1)S(1)}, bf16[16,1792]{1,0:T(8,128)(2,1)S(1)}, u32[]{:S(2)}, u32[]{:S(2)}) collective-permute-start(bf16[16,1792]{1,0:T(8,128)(2,1)S(1)} %get-tuple-element.109), channel_id=1, source_target_pairs={{0,8},{1,9},{2,10},{3,11},{4,12},{5,13},{6,14},{7,15},{8,0},{9,1},... | collective-permute-start | bytes 172040 | tf_op jit(solution)/shard_map/ppermute | solution.py:28
  72.0 4.9 %collective-permute-start.14 = (bf16[32,1792]{1,0:T(8,128)(2,1)S(1)}, bf16[32,1792]{1,0:T(8,128)(2,1)S(1)}, u32[]{:S(2)}, u32[]{:S(2)}) collective-permute-start(bf16[32,1792]{1,0:T(8,128)(2,1)S(1)} %pad_maximum_fusion.3), channel_id=1, source_target_pairs={{0,2},{1,3},{2,0},{3,1},{4,6},{5,7},{6,4},{7,5},{8,10},{9,11},{10,... | collective-permute-start | bytes 344072 | tf_op jit(solution)/shard_map/ppermute | solution.py:28
  72.7 4.9 %collective-permute-start.12 = (bf16[32,1792]{1,0:T(8,128)(2,1)S(1)}, bf16[32,1792]{1,0:T(8,128)(2,1)S(1)}, u32[]{:S(2)}, u32[]{:S(2)}) collective-permute-start(bf16[32,1792]{1,0:T(8,128)(2,1)S(1)} %pad_maximum_fusion.2), channel_id=1, source_target_pairs={{0,4},{1,5},{2,6},{3,7},{4,0},{5,1},{6,2},{7,3},{8,12},{9,13},{10,... | collective-permute-start | bytes 344072 | tf_op jit(solution)/shard_map/ppermute | solution.py:28
  77.6 7.7 %copy-start.7 = (bf16[192,3584]{1,0:T(8,128)(2,1)S(1)}, bf16[192,3584]{1,0:T(8,128)(2,1)}, u32[]{:S(2)}) copy-start(bf16[192,3584]{1,0:T(8,128)(2,1)} %copy-done.6) | copy-start | bytes 4128772
  77.6 7.7 %copy-start.3 = (bf16[192,4096]{1,0:T(8,128)(2,1)S(1)}, bf16[192,4096]{1,0:T(8,128)(2,1)}, u32[]{:S(2)}) copy-start(bf16[192,4096]{1,0:T(8,128)(2,1)} %copy-done.2) | copy-start | bytes 4718596
  77.6 7.7 %copy-start.5 = (bf16[3584,192]{0,1:T(8,128)(2,1)S(1)}, bf16[3584,192]{0,1:T(8,128)(2,1)}, u32[]{:S(2)}) copy-start(bf16[3584,192]{0,1:T(8,128)(2,1)} %param.13) | copy-start | bytes 4128772
  77.6 6.1 %collective-permute-start.15 = (bf16[64,1792]{1,0:T(8,128)(2,1)S(1)}, bf16[64,1792]{1,0:T(8,128)(2,1)S(1)}, u32[]{:S(2)}, u32[]{:S(2)}) collective-permute-start(bf16[64,1792]{1,0:T(8,128)(2,1)S(1)} %pad_maximum_fusion.refs_0_), channel_id=1, source_target_pairs={{0,2},{1,3},{2,0},{3,1},{4,6},{5,7},{6,4},{7,5},{8,10},{9,11},{10,... | collective-permute-start | bytes 688136 | tf_op jit(solution)/shard_map/ppermute | solution.py:28
  79.3 6.0 %collective-permute-start.16 = (bf16[64,1792]{1,0:T(8,128)(2,1)S(1)}, bf16[64,1792]{1,0:T(8,128)(2,1)S(1)}, u32[]{:S(2)}, u32[]{:S(2)}) collective-permute-start(bf16[64,1792]{1,0:T(8,128)(2,1)S(1)} %pad_maximum_fusion.1.refs_2_), channel_id=1, source_target_pairs={{0,4},{1,5},{2,6},{3,7},{4,0},{5,1},{6,2},{7,3},{8,12},{9,13},{10,... | collective-permute-start | bytes 688136 | tf_op jit(solution)/shard_map/ppermute | solution.py:28
  87.7 8.4 %collective-permute-start.17 = (bf16[4,144,256]{2,1,0:T(8,128)(2,1)S(1)}, bf16[4,144,256]{2,1,0:T(8,128)(2,1)S(1)}, u32[]{:S(2)}, u32[]{:S(2)}) collective-permute-start(bf16[4,144,256]{2,1,0:T(8,128)(2,1)S(1)} %get-tuple-element.74), channel_id=1, source_target_pairs={{0,2},{1,3},{2,0},{3,1},{4,6},{5,7},{6,4},{7,5},{8,10},{9,11},{10,... | collective-permute-start | bytes 884744 | tf_op jit(solution)/shard_map/ppermute | solution.py:28
  88.2 8.3 %collective-permute-start.18 = (bf16[4,144,256]{2,1,0:T(8,128)(2,1)S(1)}, bf16[4,144,256]{2,1,0:T(8,128)(2,1)S(1)}, u32[]{:S(2)}, u32[]{:S(2)}) collective-permute-start(bf16[4,144,256]{2,1,0:T(8,128)(2,1)S(1)} %get-tuple-element.75), channel_id=1, source_target_pairs={{0,4},{1,5},{2,6},{3,7},{4,0},{5,1},{6,2},{7,3},{8,12},{9,13},{10,... | collective-permute-start | bytes 884744 | tf_op jit(solution)/shard_map/ppermute | solution.py:28
  96.5 5.2 %collective-permute-start.21 = (bf16[2,144,256]{2,1,0:T(8,128)(2,1)S(1)}, bf16[2,144,256]{2,1,0:T(8,128)(2,1)S(1)}, u32[]{:S(2)}, u32[]{:S(2)}) collective-permute-start(bf16[2,144,256]{2,1,0:T(8,128)(2,1)S(1)} %get-tuple-element.98), channel_id=1, source_target_pairs={{0,2},{1,3},{2,0},{3,1},{4,6},{5,7},{6,4},{7,5},{8,10},{9,11},{10,... | collective-permute-start | bytes 442376 | tf_op jit(solution)/shard_map/ppermute | solution.py:28
  98.3 5.2 %collective-permute-start.19 = (bf16[2,144,256]{2,1,0:T(8,128)(2,1)S(1)}, bf16[2,144,256]{2,1,0:T(8,128)(2,1)S(1)}, u32[]{:S(2)}, u32[]{:S(2)}) collective-permute-start(bf16[2,144,256]{2,1,0:T(8,128)(2,1)S(1)} %get-tuple-element.100), channel_id=1, source_target_pairs={{0,4},{1,5},{2,6},{3,7},{4,0},{5,1},{6,2},{7,3},{8,12},{9,13},{10,... | collective-permute-start | bytes 442376 | tf_op jit(solution)/shard_map/ppermute | solution.py:28
  101.8 6.1 %collective-permute-start.22 = (bf16[1,144,256]{2,1,0:T(8,128)(2,1)S(1)}, bf16[1,144,256]{2,1,0:T(8,128)(2,1)S(1)}, u32[]{:S(2)}, u32[]{:S(2)}) collective-permute-start(bf16[1,144,256]{2,1,0:T(8,128)(2,1)S(1)} %get-tuple-element.102), channel_id=1, source_target_pairs={{0,8},{1,9},{2,10},{3,11},{4,12},{5,13},{6,14},{7,15},{8,0},{9,1},... | collective-permute-start | bytes 221192 | tf_op jit(solution)/shard_map/ppermute | solution.py:28
  103.5 6.1 %collective-permute-start.20 = (bf16[1,144,256]{2,1,0:T(8,128)(2,1)S(1)}, bf16[1,144,256]{2,1,0:T(8,128)(2,1)S(1)}, u32[]{:S(2)}, u32[]{:S(2)}) collective-permute-start(bf16[1,144,256]{2,1,0:T(8,128)(2,1)S(1)} %get-tuple-element.104), channel_id=1, source_target_pairs={{0,8},{1,9},{2,10},{3,11},{4,12},{5,13},{6,14},{7,15},{8,0},{9,1},... | collective-permute-start | bytes 221192 | tf_op jit(solution)/shard_map/ppermute | solution.py:28
  110.4 1.3 collective-permute-start.23

commit v8 on v7

--- a/solution.py
+++ b/solution.py
@@ -279,31 +279,62 @@
     )(place, *parts)
 
 
-def pack_kernel(copies, queries_ref, keys_ref, values_ref, out_ref):
+def pack_kernel(copies, place_ref, queries_ref, keys_ref, values_ref, *outs):
+    chip, core = place_ref[3], place_ref[2]
     img_dev = keys_ref.shape[0]
     part_rows = img_dev // copies
-    for device in range(out_ref.shape[0]):
-        head, copy = device // copies, device % copies
-        span = slice(head * HEAD_DIM, (head + 1) * HEAD_DIM)
-        out_ref[device, :img_dev, :] = keys_ref[:, span]
-        out_ref[device, img_dev : 2 * img_dev, :] = values_ref[:, span]
-        out_ref[device, 2 * img_dev :, :] = queries_ref[copy * part_rows : (copy + 1) * part_rows, span]
-
-
-def pack(copies, queries, keys, values):
+    for mask, out_ref in enumerate(outs):
+        for side in range(2):
+            device = 2 * (chip ^ mask) + (core ^ side)
+            head, copy = device // copies, device % copies
+            span = pl.ds(pl.multiple_of(head * HEAD_DIM, HEAD_DIM), HEAD_DIM)
+            rows = pl.ds(pl.multiple_of(copy * part_rows, part_rows), part_rows)
+            out_ref[side, :img_dev, :] = keys_ref[:, span]
+            out_ref[side, img_dev : 2 * img_dev, :] = values_ref[:, span]
+            out_ref[side, 2 * img_dev :, :] = queries_ref[rows, span]
+
+
+def pack(chips, copies, place, queries, keys, values):
     img_dev = keys.shape[0]
     rows = 2 * img_dev + img_dev // copies
+    out = jax.ShapeDtypeStruct((2, rows, HEAD_DIM), jnp.bfloat16)
     return pl.pallas_call(
         functools.partial(pack_kernel, copies),
-        out_shape=jax.ShapeDtypeStruct((HEADS * copies, rows, HEAD_DIM), jnp.bfloat16),
-        in_specs=[VMEM_SPEC] * 3,
+        out_shape=(out,) * chips,
+        in_specs=[SMEM_SPEC] + [VMEM_SPEC] * 3,
+        out_specs=(VMEM_SPEC,) * chips,
+        compiler_params=params(8),
+        cost_estimate=pl.CostEstimate(
+            flops=0, bytes_accessed=8 * chips * rows * HEAD_DIM, transcendentals=0
+        ),
+        name="pack",
+    )(place, queries, keys, values)
+
+
+def gather_kernel(*refs):
+    for at, piece in enumerate(refs[:-1]):
+        refs[-1][at] = piece[1]
+
+
+def gather_other(pieces):
+    shape = (len(pieces),) + pieces[0].shape[1:]
+    return pl.pallas_call(
+        gather_kernel,
+        out_shape=jax.ShapeDtypeStruct(shape, pieces[0].dtype),
+        in_specs=[VMEM_SPEC] * len(pieces),
         out_specs=VMEM_SPEC,
         compiler_params=params(8),
         cost_estimate=pl.CostEstimate(
-            flops=0, bytes_accessed=4 * HEADS * copies * rows * HEAD_DIM, transcendentals=0
-        ),
-        name="pack",
-    )(queries, keys, values)
+            flops=0, bytes_accessed=4 * len(pieces) * pieces[0].size // 2, transcendentals=0
+        ),
+        name="gather_other",
+    )(*pieces)
+
+
+def by_distance(pieces, early, late, early_ref, late_ref):
+    passed = {mask: (early_ref, at) for at, mask in enumerate(early)}
+    passed.update({mask: (late_ref, at) for at, mask in enumerate(late)})
+    return [block for mask, piece in enumerate(pieces) for block in ((piece, 0), passed[mask])]
 
 
 def unpack_kernel(copies, part_rows, blocks_ref, attended_ref, text_ref):
@@ -336,13 +367,15 @@
     )(blocks)
 
 
-def image_kernel(factor, call, img_dev, packed_ref, sum_ref, norm_ref, keys_ref, values_ref):
-    devices = packed_ref.shape[0]
-    part_rows = packed_ref.shape[1] - 2 * img_dev
-    for device in range(devices):
-        rows = slice(device * img_dev, (device + 1) * img_dev)
-        keys_ref[rows, :] = packed_ref[device, :img_dev, :]
-        values_ref[rows, :] = packed_ref[device, img_dev : 2 * img_dev, :]
+def image_kernel(factor, call, early, late, img_dev, *refs):
+    *pieces, early_ref, late_ref, sum_ref, top_ref, keys_ref, values_ref = refs
+    blocks = by_distance(pieces, early, late, early_ref, late_ref)
+    values_ref[:, HEAD_DIM:] = jnp.ones((values_ref.shape[0], HEAD_DIM), values_ref.dtype)
+    for at, (piece, side) in enumerate(blocks):
+        rows = slice(at * img_dev, (at + 1) * img_dev)
+        keys_ref[rows, :] = piece[side, :img_dev, :]
+        values_ref[rows, :HEAD_DIM] = piece[side, img_dev : 2 * img_dev, :]
+    part_rows = pieces[0].shape[1] - 2 * img_dev
     group = max(1, 256 // part_rows)
     rows = group * part_rows
     contract = (((1,), (1,)), ((), ()))
@@ -350,30 +383,32 @@
     for step in range(steps):
         at = (call * steps + step) * group
         span = slice(step * rows, (step + 1) * rows)
-        queries = packed_ref[at : at + group, 2 * img_dev :, :].reshape(rows, HEAD_DIM)
+        queries = [piece[side, 2 * img_dev :, :] for piece, side in blocks[at : at + group]]
+        queries = jnp.concatenate(queries, 0)
         scores = lax.dot_general(queries, keys_ref[...], contract, preferred_element_type=jnp.float32)
         scores = scores * factor
         top = jnp.max(scores, 1, keepdims=True)
-        weights = jnp.exp2(scores - top)
-        total = jnp.sum(weights, 1, keepdims=True)
-        sum_ref[span, :] = jnp.dot(
-            weights.astype(jnp.bfloat16), values_ref[...], preferred_element_type=jnp.float32
-        )
-        lane = lax.broadcasted_iota(jnp.int32, (rows, 128), 1)
-        norm_ref[span, :] = jnp.where(lane < 64, top, total)
-
-
-def image_attention(packed, img_dev, factor, call, calls):
-    devices = packed.shape[0]
+        weights = jnp.exp2(scores - top).astype(jnp.bfloat16)
+        sum_ref[span, :] = jnp.dot(weights, values_ref[...], preferred_element_type=jnp.float32)
+        top_ref[span, :] = jnp.broadcast_to(top, (rows, HEAD_DIM))
+
+
+def image_attention(pieces, passed, early, late, img_dev, factor, call, calls):
+    devices = 2 * len(pieces)
     keys = devices * img_dev
-    count = devices * (packed.shape[1] - 2 * img_dev) // calls
-    out = jax.ShapeDtypeStruct((count, HEAD_DIM), jnp.float32)
-    return pl.pallas_call(
-        functools.partial(image_kernel, factor, call, img_dev),
-        out_shape=(out, out),
-        in_specs=[VMEM_SPEC],
+    count = devices * (pieces[0].shape[1] - 2 * img_dev) // calls
+    return pl.pallas_call(
+        functools.partial(image_kernel, factor, call, early, late, img_dev),
+        out_shape=(
+            jax.ShapeDtypeStruct((count, 2 * HEAD_DIM), jnp.float32),
+            jax.ShapeDtypeStruct((count, HEAD_DIM), jnp.float32),
+        ),
+        in_specs=[VMEM_SPEC] * (len(pieces) + 2),
         out_specs=(VMEM_SPEC, VMEM_SPEC),
-        scratch_shapes=[pltpu.VMEM((keys, HEAD_DIM), jnp.bfloat16)] * 2,
+        scratch_shapes=[
+            pltpu.VMEM((keys, HEAD_DIM), jnp.bfloat16),
+            pltpu.VMEM((keys, 2 * HEAD_DIM), jnp.bfloat16),
+        ],
         compiler_params=params(24),
         cost_estimate=pl.CostEstimate(
             flops=4 * count * keys * HEAD_DIM,
@@ -381,40 +416,46 @@
             transcendentals=count * keys,
         ),
         name="image_attention",
-    )(packed)
-
-
-def finish_kernel(factor, calls, img_dev, place_ref, packed_ref, *refs):
-    images, (mine_ref, got_ref, out_ref) = refs[: 2 * calls], refs[2 * calls :]
+    )(*pieces, *passed)
+
+
+def finish_kernel(factor, calls, early, late, img_dev, place_ref, *refs):
+    *pieces, early_ref, late_ref = refs[: -3 - 2 * calls]
+    images, (mine_ref, got_ref, out_ref) = refs[-3 - 2 * calls : -3], refs[-3:]
+    blocks = by_distance(pieces, early, late, early_ref, late_ref)
     core, valid = place_ref[2], place_ref[4]
-    devices, part_rows = packed_ref.shape[0], packed_ref.shape[1] - 2 * img_dev
+    me = 2 * place_ref[3] + core
+    devices, part_rows = len(blocks), pieces[0].shape[1] - 2 * img_dev
     half = mine_ref.shape[0]
     contract = (((1,), (1,)), ((), ()))
     mine, got = mine_ref[...], got_ref[...]
     keys = jnp.concatenate([mine[:, :HEAD_DIM], got[:, :HEAD_DIM]], 0)
     values = jnp.concatenate([mine[:, HEAD_DIM:], got[:, HEAD_DIM:]], 0)
+    values = jnp.concatenate([values, jnp.ones(values.shape, values.dtype)], 1)
     lane = lax.broadcasted_iota(jnp.int32, (1, 2 * half), 1)
     text_position = jnp.where((lane >= half) == (core == 0), half, 0) + lane % half
+    bias = jnp.where(text_position < valid, 0.0, -jnp.inf)
     group = max(1, 512 // part_rows)
     rows = group * part_rows
     each = devices // group // calls
     for step in range(devices // group):
-        sum_ref, norm_ref = images[2 * (step // each)], images[2 * (step // each) + 1]
+        sum_ref, top_ref = images[2 * (step // each)], images[2 * (step // each) + 1]
         span = slice(step % each * rows, (step % each + 1) * rows)
-        queries = packed_ref[step * group : (step + 1) * group, 2 * img_dev :, :]
-        queries = queries.reshape(rows, HEAD_DIM)
-        scores = lax.dot_general(queries, keys, contract, preferred_element_type=jnp.float32) * factor
-        scores = jnp.where(text_position < valid, scores, -jnp.inf)
-        before = norm_ref[span, 0:1]
+        queries = blocks[step * group : (step + 1) * group]
+        queries = jnp.concatenate([piece[side, 2 * img_dev :, :] for piece, side in queries], 0)
+        scores = lax.dot_general(queries, keys, contract, preferred_element_type=jnp.float32)
+        scores = scores * factor + bias
+        before = top_ref[span, :]
         top = jnp.maximum(before, jnp.max(scores, 1, keepdims=True))
         rescale = jnp.exp2(before - top)
-        weights = jnp.exp2(scores - top)
-        total = norm_ref[span, 64:65] * rescale + jnp.sum(weights, 1, keepdims=True)
-        mixed = sum_ref[span, :] * rescale + jnp.dot(
-            weights.astype(jnp.bfloat16), values, preferred_element_type=jnp.float32
-        )
+        weights = jnp.exp2(scores - jnp.concatenate([top] * (2 * half // HEAD_DIM), 1))
+        total = jnp.dot(weights.astype(jnp.bfloat16), values, preferred_element_type=jnp.float32)
+        mixed = sum_ref[span, :HEAD_DIM] * rescale + total[:, :HEAD_DIM]
+        total = sum_ref[span, HEAD_DIM:] * rescale + total[:, HEAD_DIM:]
         mixed = (mixed / total).astype(out_ref.dtype)
-        out_ref[step * group : (step + 1) * group, :part_rows, :] = mixed.reshape(group, part_rows, HEAD_DIM)
+        for at in range(group):
+            to = me ^ (step * group + at)
+            out_ref[to, :part_rows, :] = mixed[at * part_rows : (at + 1) * part_rows]
     low = jnp.where(core == 0, mine.astype(jnp.float32), got.astype(jnp.float32))
     high = jnp.where(core == 0, got.astype(jnp.float32), mine.astype(jnp.float32))
     share = 2 * half // devices
@@ -426,14 +467,14 @@
         out_ref[device, part_rows:, :] = block.astype(out_ref.dtype)
 
 
-def finish(place, packed, images, mine, got, img_dev, factor):
-    devices, part_rows = packed.shape[0], packed.shape[1] - 2 * img_dev
+def finish(place, pieces, passed, early, late, images, mine, got, img_dev, factor):
+    devices, part_rows = 2 * len(pieces), pieces[0].shape[1] - 2 * img_dev
     share = 2 * mine.shape[0] // devices
     count = devices * part_rows
     return pl.pallas_call(
-        functools.partial(finish_kernel, factor, len(images) // 2, img_dev),
+        functools.partial(finish_kernel, factor, len(images) // 2, early, late, img_dev),
         out_shape=jax.ShapeDtypeStruct((devices, part_rows + 2 * share, HEAD_DIM), jnp.bfloat16),
-        in_specs=[SMEM_SPEC] + [VMEM_SPEC] * (len(images) + 3),
+        in_specs=[SMEM_SPEC] + [VMEM_SPEC] * (len(pieces) + len(images) + 4),
         out_specs=VMEM_SPEC,
         compiler_params=params(16),
         cost_estimate=pl.CostEstimate(
@@ -442,7 +483,7 @@
             transcendentals=count * 2 * mine.shape[0],
         ),
         name="finish",
-    )(place, packed, *images, mine, got)
+    )(place, *pieces, *passed, *images, mine, got)
 
 
 def add(one, other, dtype):
@@ -486,22 +527,47 @@
         return lax.all_to_all(rows, "seq", split_axis=0, concat_axis=0, tiled=True)
 
     image_key_values, image_queries = tie((image_key_values, image_queries))
-    packed = pack(copies, image_queries[0], image_key_values[0, :, 0], image_key_values[0, :, 1])
-    act, packed = tie((enc_act[0].T, packed))
-    packed = exchange(packed)
+    pieces = pack(
+        chips, copies, place, image_queries[0], image_key_values[0, :, 0], image_key_values[0, :, 1]
+    )
+    pieces = list(pieces)
+    act, pieces = tie((enc_act[0].T, pieces))
+    late = [6, 7]
+    early = [mask for mask in range(chips) if mask not in late]
+
+    def send_piece(mask, chain):
+        chain, piece = tie((chain, pieces[mask]))
+        pieces[mask] = swap(piece, 2 * mask)
+        return chain
+
+    def take_pieces(masks, chain):
+        chain, taken = tie((chain, [pieces[mask] for mask in masks]))
+        for mask, piece in zip(masks, taken):
+            pieces[mask] = piece
+        return chain
+
+    first, second = [4, 1, 2], [mask for mask in early if mask in (3, 5) or mask > 7]
+    for mask in first:
+        act = send_piece(mask, act)
     keep, sent = [], []
-    encoded = encoder(lanes, place, act, down_weight)
+    encoded = list(encoder(lanes, place, act, down_weight))
+    encoded[1::2] = take_pieces(first[:2], encoded[1::2])
+    for mask in second:
+        encoded = send_piece(mask, encoded)
     for own, other in (encoded[:2], encoded[2:]):
         got = swap(other, 1)
         sent.append(add(own[chips // 2 :], got[chips // 2 :], jnp.bfloat16))
         keep.append(add(own[: chips // 2], got[: chips // 2], jnp.float32))
+    sent = take_pieces(first[2:], sent)
     for step in range(rounds):
         got = [swap(part, 2 * order[step]) for part, order in zip(sent, lanes)]
         if step == 0:
-            got, win1, kv1, mod1, packed = tie((got, win1, kv1, mod1, packed))
+            got = take_pieces(second, got)
+        if step == 1:
+            passed_early = gather_other([pieces[mask] for mask in early])
+        if step == 2:
+            got, win1, kv1, mod1 = tie((got, win1, kv1, mod1))
             lines = modulation(time, mod0, mod1)
-        if step == 1:
-            got, lines = tie((got, lines))
         half = keep[0].shape[0] // 2
         if half:
             sent = [add(mine[half:], part[half:], jnp.bfloat16) for mine, part in zip(keep, got)]
@@ -519,24 +585,30 @@
     images = []
 
     for step in reversed(range(rounds)):
-        if step == 0:
-            states, packed = tie((states, packed))
-            image = image_attention(packed, img_dev, factor, 0, 2)
+        if step < 2:
+            states = send_piece(late[1 - step], states)
         got = [swap(state, 2 * order[step]) for state, order in zip(states, lanes)]
+        if step == rounds - 1:
+            passed_early = swap(passed_early, 1)
+            got, lines = tie((got, lines))
+        if step == rounds - 2:
+            got, passed_early = tie((got, passed_early))
         if step:
             states = [jnp.concatenate(pair, 0) for pair in zip(states, got)]
-    got, image = tie((got, image))
-    images += image
+    got = take_pieces(late[:1], got)
     states = [state for pair in zip(states, got) for state in pair]
 
     blocks = project(lanes, place, states, lines, win0, win1, kv0, kv1)
     keep, sent = [blocks[0], blocks[2]], [blocks[1], blocks[3]]
     for step in range(rounds):
-        if step == 0:
-            sent, packed = tie((sent, packed))
-            image = image_attention(packed, img_dev, factor, 1, 2)
         got = [swap(part, 2 * order[step]) for part, order in zip(sent, lanes)]
         if step == 0:
+            passed_late = swap(gather_other([pieces[mask] for mask in late]), 1)
+            got, passed_late = tie((got, passed_late))
+            passed = (passed_early, passed_late)
+        elif step <= 2:
+            sent, passed = tie((sent, passed))
+            image = image_attention(pieces, passed, early, late, img_dev, factor, step - 1, 2)
             got, image = tie((got, image))
             images += image
         half = keep[0].shape[0] // 2
@@ -548,7 +620,7 @@
     mine, sent = combine(place, parts, chips, text_len // 2, model_width)
     got = swap(sent, 1)
 
-    back = exchange(finish(place, packed, images, mine, got, img_dev, factor))
+    back = exchange(finish(place, pieces, passed, early, late, images, mine, got, img_dev, factor))
     attended, text_kv = unpack(copies, part_rows, back)
     return (attended[None], text_kv)
 

time: 139 us -> 141 us (1.014)
  starting transfers between devices: 33.1 us -> 42.6 us
  local copies, waits for them, and re-layouts: 10.7 us -> 6.02 us
  other arithmetic: 4.91 us -> 0.89 us
  waiting for transfers between devices: 45.1 us -> 48.3 us
  Pallas kernels: 20.5 us -> 17.4 us
    ppermute x24 -> x33, starting transfers between devices: 25.8 us -> 42.6 us  [swap(): return lax.ppermute(value, 'seq', [(i, i ^ mask) for i in range(devices)])]
    all_to_all x1 -> x0, starting transfers between devices: 7.36 us -> none  [exchange(): return lax.all_to_all(rows, 'seq', split_axis=0, concat_axis=0, tiled=True)]
    unnamed x30 -> x14, local copies, waits for them, and re-layouts: 8.36 us -> 4.25 us
    ppermute x24 -> x33, waiting for transfers between devices: 45.1 us -> 48.3 us  [swap(): return lax.ppermute(value, 'seq', [(i, i ^ mask) for i in range(devices)])]
    pallas_call x1, Pallas kernels: 3.76 us -> 1.54 us  [finish(): pl.pallas_call(functools.partial(finish_kernel, factor, len(images) // 2,...]
    convert_element_type x8 -> x5, other arithmetic: 2.3 us -> 0.17 us  [add(): return (one.astype(jnp.float32) + other.astype(jnp.float32)).astype(dtype)]
    add x2 -> x3, other arithmetic: 2.12 us -> 0.27 us  [add(): return (one.astype(jnp.float32) + other.astype(jnp.float32)).astype(dtype)]
    pallas_call x3 -> x5, Pallas kernels: 8.95 us -> 8.09 us  [the longest x2 7.08 us: image_attention(): pl.pallas_call(functools.partial(image_kernel, factor, call, early, late,...]
  transfers between devices with their start and end apart: 25 -> 33, of which waited for: 20 -> 19; matrix products, arithmetic and copies ran while one was open for 3% -> 1% of each run, Pallas kernels for 8% -> 9%
where the time goes in v8:
time: 141 us; the launch traced here: 140 us
  waiting for transfers between devices  48.3 us (34%)
  starting transfers between devices  42.6 us (30%)
  blocking collectives  23.1 us (16%)
  Pallas kernels  17.4 us (12%)
  local copies, waits for them, and re-layouts  6.02 us (4%)
  between operations  2.25 us (2%)
    ppermute x33, waiting for transfers between devices, swap(): return lax.ppermute(value, 'seq', [(i, i ^ mask) for i in range(devices)])  48.3 us
    ppermute x33, starting transfers between devices, swap(): return lax.ppermute(value, 'seq', [(i, i ^ mask) for i in range(devices)])  42.6 us
    all_to_all x1, blocking collectives, exchange(): return lax.all_to_all(rows, 'seq', split_axis=0, concat_axis=0, tiled=True)  23.1 us
    pallas_call x2, Pallas kernels, image_attention(): pl.pallas_call(functools.partial(image_kernel, factor, call, early, late,...  7.08 us
    unnamed x14, local copies, waits for them, and re-layouts  4.25 us
    pallas_call x1, Pallas kernels, encoder(): pl.pallas_call(functools.partial(encoder_kernel, lanes), out_shape=(out,)...  3.49 us
  transfers between devices with their start and end apart: 33, of which 19 were waited for; matrix products, arithmetic and copies ran while one was open for 1% of the time, Pallas kernels for 9%

profile of v8, /device:TPU:0, one launch (start us, length us, event | category | flops | bytes accessed | tf_op | source)
XLA Modules:
  0.0 140.5 jit_solution(4996304465878572782)
XLA Ops:
  1.3 1.6 %copy.12 = bf16[1,128,2,2048]{3,1,2,0:T(8,128)(2,1)S(1)} copy(bf16[1,128,2,2048]{3,2,1,0:T(2,128)(2,1)} %param.19) | data formatting | bytes 2097152 | tf_op jit(solution)/shard_map/optimization_barrier | solution.py:529
  2.9 0.1 slice_bitcast_fusion
  3.0 0.1 stack.19.place_ref
  3.1 0.8 copy-done.4
  3.9 1.0 pack.1
  4.9 4.1 %collective-permute-start = (bf16[2,384,128]{2,1,0:T(8,128)(2,1)S(1)}, bf16[2,384,128]{2,1,0:T(8,128)(2,1)S(1)}, u32[]{:S(2)}, u32[]{:S(2)}) collective-permute-start(bf16[2,384,128]{2,1,0:T(8,128)(2,1)S(1)} %get-tuple-element.119), channel_id=1, source_target_pairs={{0,8},{1,9},{2,10},{3,11},{4,12},{5,13},{6,14},{7,15},{8,0},{9,1},... | collective-permute-start | bytes 589832 | tf_op jit(solution)/shard_map/ppermute | solution.py:28
  9.0 1.5 %collective-permute-start.1 = (bf16[2,384,128]{2,1,0:T(8,128)(2,1)S(1)}, bf16[2,384,128]{2,1,0:T(8,128)(2,1)S(1)}, u32[]{:S(2)}, u32[]{:S(2)}) collective-permute-start(bf16[2,384,128]{2,1,0:T(8,128)(2,1)S(1)} %get-tuple-element.120), channel_id=1, source_target_pairs={{0,2},{1,3},{2,0},{3,1},{4,6},{5,7},{6,4},{7,5},{8,10},{9,11},{10,... | collective-permute-start | bytes 589832 | tf_op jit(solution)/shard_map/ppermute | solution.py:28
  10.5 3.4 %copy-done = bf16[1184,3584]{1,0:T(8,128)(2,1)S(1)} copy-done((bf16[1184,3584]{1,0:T(8,128)(2,1)S(1)}, bf16[1184,3584]{1,0:T(8,128)(2,1)}, u32[]{:S(2)}) %copy-start) | copy-done | bytes 8486936
  13.9 3.5 %encoder.1 = (bf16[8,16,1792]{2,1,0:T(8,128)(2,1)S(1)}, bf16[8,16,1792]{2,1,0:T(8,128)(2,1)S(1)}, bf16[8,16,1792]{2,1,0:T(8,128)(2,1)S(1)}, bf16[8,16,1792]{2,1,0:T(8,128)(2,1)S(1)}) custom-call(s32[5]{0:T(128)S(1)} %stack.19.place_ref, bf16[1184,256]{1,0:T(8,128)(2,1)S(1)} %bitcast.40, bf16[1184,3584]{1,0:T(8,128)(2,1)S(1)} %copy-done), custom_call_target="tpu_custom_call" | custom-call | flops 2172649472 | bytes 10928128 | tf_op jit(solution)/shard_map/encoder/pallas_call | solution.py:89
  17.4 0.7 collective-permute-done.refs_4_
  18.2 1.0 collective-permute-start.4
  19.2 0.2 collective-permute-start.3
  19.3 0.7 collective-permute-done.2
  20.0 0.1 convert_add_fusion.1
  20.1 0.9 collective-permute-done.3
  21.0 0.1 convert_add_fusion
  21.1 4.4 %collective-permute-done.4.refs_2_ = bf16[2,384,128]{2,1,0:T(8,128)(2,1)S(1)} collective-permute-done((bf16[2,384,128]{2,1,0:T(8,128)(2,1)S(1)}, bf16[2,384,128]{2,1,0:T(8,128)(2,1)S(1)}, u32[]{:S(2)}, u32[]{:S(2)}) %collective-permute-start.4) | collective-permute-done | bytes 196640 | tf_op jit(solution)/shard_map/ppermute | solution.py:28
  25.5 1.5 %collective-permute-start.5 = (bf16[4,16,1792]{2,1,0:T(8,128)(2,1)S(1)}, bf16[4,16,1792]{2,1,0:T(8,128)(2,1)S(1)}, u32[]{:S(2)}, u32[]{:S(2)}) collective-permute-start(bf16[4,16,1792]{2,1,0:T(8,128)(2,1)S(1)} %get-tuple-element.138), channel_id=1, source_target_pairs={{0,2},{1,3},{2,0},{3,1},{4,6},{5,7},{6,4},{7,5},{8,10},{9,11},{10,... | collective-permute-start | bytes 688136 | tf_op jit(solution)/shard_map/ppermute | solution.py:28
  27.1 0.7 collective-permute-start.6
  28.4 1.3 collective-permute-start.7
  29.7 3.3 %collective-permute-start.8 = (bf16[2,384,128]{2,1,0:T(8,128)(2,1)S(1)}, bf16[2,384,128]{2,1,0:T(8,128)(2,1)S(1)}, u32[]{:S(2)}, u32[]{:S(2)}) collective-permute-start(bf16[2,384,128]{2,1,0:T(8,128)(2,1)S(1)} %get-tuple-element.141), channel_id=1, source_target_pairs={{0,10},{1,11},{2,8},{3,9},{4,14},{5,15},{6,12},{7,13},{8,2},{9,3},... | collective-permute-start | bytes 589832 | tf_op jit(solution)/shard_map/ppermute | solution.py:28
  33.0 9.3 %collective-permute-done.7.refs_3_ = bf16[2,384,128]{2,1,0:T(8,128)(2,1)S(1)} collective-permute-done((bf16[2,384,128]{2,1,0:T(8,128)(2,1)S(1)}, bf16[2,384,128]{2,1,0:T(8,128)(2,1)S(1)}, u32[]{:S(2)}, u32[]{:S(2)}) %collective-permute-start.7) | collective-permute-done | bytes 196640 | tf_op jit(solution)/shard_map/ppermute | solution.py:28
  42.3 0.5 collective-permute-start.15
  42.9 2.1 %collective-permute-start.9 = (bf16[2,16,1792]{2,1,0:T(8,128)(2,1)S(1)}, bf16[2,16,1792]{2,1,0:T(8,128)(2,1)S(1)}, u32[]{:S(2)}, u32[]{:S(2)}) collective-permute-start(bf16[2,16,1792]{2,1,0:T(8,128)(2,1)S(1)} %get-tuple-element.204), channel_id=1, source_target_pairs={{0,4},{1,5},{2,6},{3,7},{4,0},{5,1},{6,2},{7,3},{8,12},{9,13},{10,... | collective-permute-start | bytes 344072 | tf_op jit(solution)/shard_map/ppermute | solution.py:28
  45.0 1.6 %collective-permute-start.11 = (bf16[2,16,1792]{2,1,0:T(8,128)(2,1)S(1)}, bf16[2,16,1792]{2,1,0:T(8,128)(2,1)S(1)}, u32[]{:S(2)}, u32[]{:S(2)}) collective-permute-start(bf16[2,16,1792]{2,1,0:T(8,128)(2,1)S(1)} %get-tuple-element.202), channel_id=1, source_target_pairs={{0,2},{1,3},{2,0},{3,1},{4,6},{5,7},{6,4},{7,5},{8,10},{9,11},{10,... | collective-permute-start | bytes 344072 | tf_op jit(solution)/shard_map/ppermute | solution.py:28
  46.6 2.2 %collective-permute-done.9 = bf16[2,16,1792]{2,1,0:T(8,128)(2,1)S(1)} collective-permute-done((bf16[2,16,1792]{2,1,0:T(8,128)(2,1)S(1)}, bf16[2,16,1792]{2,1,0:T(8,128)(2,1)S(1)}, u32[]{:S(2)}, u32[]{:S(2)}) %collective-permute-start.9) | collective-permute-done | bytes 114720 | tf_op jit(solution)/shard_map/ppermute | solution.py:28
  48.8 2.1 %collective-permute-start.10 = (bf16[1,16,1792]{2,1,0:T(8,128)(2,1)S(1)}, bf16[1,16,1792]{2,1,0:T(8,128)(2,1)S(1)}, u32[]{:S(2)}, u32[]{:S(2)}) collective-permute-start(bf16[1,16,1792]{2,1,0:T(8,128)(2,1)S(1)} %fusion.9), channel_id=1, source_target_pairs={{0,8},{1,9},{2,10},{3,11},{4,12},{5,13},{6,14},{7,15},{8,0},{9,1},... | collective-permute-start | bytes 172040 | tf_op jit(solution)/shard_map/ppermute | solution.py:28
  51.0 1.5 %collective-permute-start.12 = (bf16[1,16,1792]{2,1,0:T(8,128)(2,1)S(1)}, bf16[1,16,1792]{2,1,0:T(8,128)(2,1)S(1)}, u32[]{:S(2)}, u32[]{:S(2)}) collective-permute-start(bf16[1,16,1792]{2,1,0:T(8,128)(2,1)S(1)} %fusion.8), channel_id=1, source_target_pairs={{0,8},{1,9},{2,10},{3,11},{4,12},{5,13},{6,14},{7,15},{8,0},{9,1},... | collective-permute-start | bytes 172040 | tf_op jit(solution)/shard_map/ppermute | solution.py:28
  52.7 3.3 %collective-permute-done.10 = bf16[1,16,1792]{2,1,0:T(8,128)(2,1)S(1)} collective-permute-done((bf16[1,16,1792]{2,1,0:T(8,128)(2,1)S(1)}, bf16[1,16,1792]{2,1,0:T(8,128)(2,1)S(1)}, u32[]{:S(2)}, u32[]{:S(2)}) %collective-permute-start.10) | collective-permute-done | bytes 57376 | tf_op jit(solution)/shard_map/ppermute | solution.py:28
  56.1 1.5 %collective-permute-done.12 = bf16[1,16,1792]{2,1,0:T(8,128)(2,1)S(1)} collective-permute-done((bf16[1,16,1792]{2,1,0:T(8,128)(2,1)S(1)}, bf16[1,16,1792]{2,1,0:T(8,128)(2,1)S(1)}, u32[]{:S(2)}, u32[]{:S(2)}) %collective-permute-start.12) | collective-permute-done | bytes 57376 | tf_op jit(solution)/shard_map/ppermute | solution.py:28
  57.6 0.2 multiply_reduce_fusion
  57.8 0.1 multiply_convert_fusion
  57.9 0.1 collective-permute-start.16
  58.0 2.9 %collective-permute-start.17 = (bf16[16,1792]{1,0:T(8,128)(2,1)S(1)}, bf16[16,1792]{1,0:T(8,128)(2,1)S(1)}, u32[]{:S(2)}, u32[]{:S(2)}) collective-permute-start(bf16[16,1792]{1,0:T(8,128)(2,1)S(1)} %get-tuple-element.216), channel_id=1, source_target_pairs={{0,8},{1,9},{2,10},{3,11},{4,12},{5,13},{6,14},{7,15},{8,0},{9,1},... | collective-permute-start | bytes 172040 | tf_op jit(solution)/shard_map/ppermute | solution.py:28
  60.9 0.2 modulation.1.refs_4_
  61.1 3.2 %collective-permute-done.16 = bf16[16,1792]{1,0:T(8,128)(2,1)S(1)} collective-permute-done((bf16[16,1792]{1,0:T(8,128)(2,1)S(1)}, bf16[16,1792]{1,0:T(8,128)(2,1)S(1)}, u32[]{:S(2)}, u32[]{:S(2)}) %collective-permute-start.16) | collective-permute-done | bytes 57376 | tf_op jit(solution)/shard_map/ppermute | solution.py:28
  64.3 0.6 collective-permute-done.17
  64.9 1.4 collective-permute-start.18
  66.3 1.5 %collective-permute-start.19 = (bf16[32,1792]{1,0:T(8,128)(2,1)S(1)}, bf16[32,1792]{1,0:T(8,128)(2,1)S(1)}, u32[]{:S(2)}, u32[]{:S(2)}) collective-permute-start(bf16[32,1792]{1,0:T(8,128)(2,1)S(1)} %pad_maximum_fusion.3), channel_id=1, source_target_pairs={{0,2},{1,3},{2,0},{3,1},{4,6},{5,7},{6,4},{7,5},{8,10},{9,11},{10,... | collective-permute-start | bytes 344072 | tf_op jit(solution)/shard_map/ppermute | solution.py:28
  67.8 2.0 %collective-permute-done.18 = bf16[32,1792]{1,0:T(8,128)(2,1)S(1)} collective-permute-done((bf16[32,1792]{1,0:T(8,128)(2,1)S(1)}, bf16[32,1792]{1,0:T(8,128)(2,1)S(1)}, u32[]{:S(2)}, u32[]{:S(2)}) %collective-permute-start.18) | collective-permute-done | bytes 114720 | tf_op jit(solution)/shard_map/ppermute | solution.py:28
  69.8 1.7 %collective-permute-done.19 = bf16[32,1792]{1,0:T(8,128)(2,1)S(1)} collective-permute-done((bf16[32,1792]{1,0:T(8,128)(2,1)S(1)}, bf16[32,1792]{1,0:T(8,128)(2,1)S(1)}, u32[]{:S(2)}, u32[]{:S(2)}) %collective-permute-start.19) | collective-permute-done | bytes 114720 | tf_op jit(solution)/shard_map/ppermute | solution.py:28
  71.5 1.6 %collective-permute-start.21 = (bf16[64,1792]{1,0:T(8,128)(2,1)S(1)}, bf16[64,1792]{1,0:T(8,128)(2,1)S(1)}, u32[]{:S(2)}, u32[]{:S(2)}) collective-permute-start(bf16[64,1792]{1,0:T(8,128)(2,1)S(1)} %pad_maximum_fusion.refs_0_), channel_id=1, source_target_pairs={{0,2},{1,3},{2,0},{3,1},{4,6},{5,7},{6,4},{7,5},{8,10},{9,11},{10,... | collective-permute-start | bytes 688136 | tf_op jit(solution)/shard_map/ppermute | solution.py:28
  73.1 0.7 collective-permute-start.22
  73.8 2.3 %collective-permute-start.23 = (bf16[2,384,128]{2,1,0:T(8,128)(2,1)S(1)}, bf16[2,384,128]{2,1,0:T(8,128)(2,1)S(1)}, u32[]{:S(2)}, u32[]{:S(2)}) collective-permute-start(bf16[2,384,128]{2,1,0:T(8,128)(2,1)S(1)} %get-tuple-element.160), channel_id=1, source_target_pairs={{0,12},{1,13},{2,14},{3,15},{4,8},{5,9},{6,10},{7,11},{8,4},{9,5},... | collective-permute-start | bytes 589832 | tf_op jit(solution)/shard_map/ppermute | solution.py:28
  76.1 1.5 %collective-permute-start.24 = (bf16[2,384,128]{2,1,0:T(8,128)(2,1)S(1)}, bf16[2,384,128]{2,1,0:T(8,128)(2,1)S(1)}, u32[]{:S(2)}, u32[]{:S(2)}) collective-permute-start(bf16[2,384,128]{2,1,0:T(8,128)(2,1)S(1)} %get-tuple-element.162), channel_id=1, source_target_pairs={{0,14},{1,15},{2,12},{3,13},{4,10},{5,11},{6,8},{7,9},{8,6},{9,7},... | collective-permute-start | bytes 589832 | tf_op jit(solution)/shard_map/ppermute | solution.py:28
  77.6 9.2 %collective-permute-done.23.refs_0_.refs_6_ = bf16[2,384,128]{2,1,0:T(8,128)(2,1)S(1)} collective-permute-done((bf16[2,384,128]{2,1,0:T(8,128)(2,1)S(1)}, bf16[2,384,128]{2,1,0:T(8,128)(2,1)S(1)}, u32[]{:S(2)}, u32[]{:S(2)}) %collective-permute-start.23) | collective-permute-done | bytes 196640 | tf_op jit(solution)/shard_map/ppermute | solution.py:28
  86.9 2.3 %project.1 = (bf16[4,144,256]{2,1,0:T(8,128)(2,1)S(1)}, bf16[4,144,256]{2,1,0:T(8,128)(2,1)S(1)}, bf16[4,144,256]{2,1,0:T(8,128)(2,1)S(1)}, bf16[4,144,256]{2,1,0:T(8,128)(2,1)S(1)}) custom-call(s32[5]{0:T(128)S(1)} %stack.19.place_ref, bf16[64,1792]{1,0:T(8,128)(2,1)S(1)} %pad_maximum_fusion.refs_0_, bf16[64,1792]{1,0:T(8,128)(2,1)S(1)} %collective-permute-done.21.refs_1_, ...), custom_call_target="tpu_custom_call" | custom-call | flops 754974720 | bytes 7864320 | tf_op jit(solution)/shard_map/project/pallas_call | solution.py:211
  89.3 1.8 %collective-permute-start.26 = (bf16[4,144,256]{2,1,0:T(8,128)(2,1)S(1)}, bf16[4,144,256]{2,1,0:T(8,128)(2,1)S(1)}, u32[]{:S(2)}, u32[]{:S(2)}) collective-permute-start(bf16[4,144,256]{2,1,0:T(8,128)(2,1)S(1)} %get-tuple-element.170), channel_id=1, source_target_pairs={{0,4},{1,5},{2,6},{3,7},{4,0},{5,1},{6,2},{7,3},{8,12},{9,13},{10,... | collective-permute-start | bytes 884744 | tf_op jit(solution)/shard_map/ppermute | solution.py:28
  91.1 1.4 %collective-permute-done.27.refs_9_ = bf16[2,384,128]{2,1,0:T(8,128)(2,1)S(1)} collective-permute-done((bf16[2,384,128]{2,1,0:T(8,128)(2,1)S(1)}, bf16[2,384,128]{2,1,0:T(8,128)(2,1)S(1)}, u32[]{:S(2)}, u32[]{:S(2)}) %collective-permute-start.27) | collective-permute-done | bytes 196640 | tf_op jit(solution)/shard_map/ppermute | solution.py:28
  92.6 3.5 %collective-permute-done.25 = bf16[4,144,256]{2,1,0:T(8,128)(2,1)S(1)} collective-permute-done((bf16[4,144,256]{2,1,0:T(8,128)(2,1)S(1)}, bf16[4,144,256]{2,1,0:T(8,128)(2,1)S(1)}, u32[]{:S(2)}, u32[]{:S(2)}) %collective-permute-start.25) | collective-permute-done | bytes 294944 | tf_op jit(solution)/shard_map/ppermute | solution.py:28
  96.1 0.8 collective-permute-done.26
  96.9 2.5 %collective-permute-start.28 = (bf16[2,144,256]{2,1,0:T(8,128)(2,1)S(1)}, bf16[2,144,256]{2,1,0:T(8,128)(2,1)S(1)}, u32[]{:S(2)}, u32[]{:S(2)}) collective-permute-start(bf16[2,144,256]{2,1,0:T(8,128)(2,1)S(1)} %get-tuple-element.208), channel_id=1, source_target_pairs={{0,4},{1,5},{2,6},{3,7},{4,0},{5,1},{6,2},{7,3},{8,12},{9,13},{10,... | collective-permute-start | bytes 442376 | tf_op jit(solution)/shard_map/ppermute | solution.py:28
  99.6 1.5 %collective-permute-start.29 = (bf16[2,144,256]{2,1,0:T(8,128)(2,1)S(1)}, bf16[2,144,256]{2,1,0:T(8,128)(2,1)S(1)}, u32[]{:S(2)}, u32[]{:S(2)}) collective-permute-start(bf16[2,144,256]{2,1,0:T(8,128)(2,1)S(1)} %get-tuple-element.207), channel_id=1, source_target_pairs={{0,2},{1,3},{2,0},{3,1},{4,6},{5,7},{6,4},{7,5},{8,10},{9,11},{10,... | collective-permute-start | bytes 442376 | tf_op jit(solution)/shard_map/ppermute | solution.py:28
  101.1 3.5 %image_attention.2 = (f32[1024,256]{1,0:T(8,128)S(1)}, f32[1024,128]{1,0:T(8,128)S(1)}) custom-call(bf16[2,384,128]{2,1,0:T(8,128)(2,1)S(1)} %get-tuple-element.109.refs_0_, bf16[2,384,128]{2,1,0:T(8,128)(2,1)S(1)} %collective-permute-done.1.refs_1_, bf16[2,384,128]{2,1,0:T(8,128)(2,1)S(1)} %collective-permute-done.4.refs_2_, ...), custom_call_target="tpu_custom_call" | custom-call | flops 1073741824 | bytes 2359296 | tf_op jit(solution)/shard_map/image_attention/pallas_call | solution.py:400
  104.5 0.2 collective-permute-done.29
  104.8 2.6 %collective-permute-start.30 = (bf16[1,144,256]{2,1,0:T(8,128)(2,1)S(1)}, bf16[1,144,256]{2,1,0:T(8,128)(2,1)S(1)}, u32[]{:S(2)}, u32[]{:S(2)}) collective-permute-start(bf16[1,144,256]{2,1,0:T(8,128)(2,1)S(1)} %get-tuple-element.213), channel_id=1, source_target_pairs={{0,8},{1,9},{2,10},{3,11},{4,12},{5,13},{6,14},{7,15},{8,0},{9,1},... | collective-permute-start | bytes 221192 | tf_op jit(solution)/shard_map/ppermute | solution.py:28
  107.5 0.4 collective-permute-start.31
  107.9 3.6 %image_attention.3 = (f32[1024,256]{1,0:T(8,128)S(1)}, f32[1024,128]{1,0:T(8,128)S(1)}) custom-call(bf16[2,384,128]{2,1,0:T(8,128)(2,1)S(1)} %get-tuple-element.109.refs_0_, bf16[2,384,128]{2,1,0:T(8,128)(2,1)S(1)} %collective-permute-done.1.refs_1_, bf16[2,384,128]{2,1,0:T(8,128)(2,1)S(1)} %collective-permute-done.4.refs_2_, ...), custom_call_target="tpu_custom_call" | custom-call | flops 1073741824 | bytes 2359296 | tf_op jit(solution)/shard_map/image_attention/pallas_call | solution.py:400
  111.5 1.2 collective-permute-done.31
  112.8 0.7 combine.1
  113.6 1.2 collective-permute-done.32.refs_15_
  114.8 1.5 %finish.1 = bf16[16,160,128]{2,1,0:T(8,128)(2,1)S(1)} custom-call(s32[5]{0:T(128)S(1)} %stack.19.place_ref, bf16[2,384,128]{2,1,0:T(8,128)(2,1)S(1)} %get-tuple-element.109.refs_0_, bf16[2,384,128]{2,1,0:T(8,128)(2,1)S(1)} %collective-permute-done.1.refs_1_, bf16[2,384,128]{2,1,0:T(8,128)(2,1)S(1)} %collective-permute-done.4.refs_2_, ...), custom_call_target="tpu_custom_call" | custom-call | flops 268435456 | bytes 3145728 | tf_op jit(solution)/shard_map/finish/pallas_call | solution.py:474
  116.4 23.1 %all_to_all.5.blocks_ref = bf16[16,160,128]{2,1,0:T(8,128)(2,1)S(1)} all-to-all(bf16[16,160,128]{2,1,0:T(8,128)(2,1)S(1)} %finish.1), channel_id=1, replica_groups=mesh['dp'=2,'seq'=16] {'seq'}, dimensions={0} | all-to-all | bytes 1310720 | tf_op jit(solution)/shard_map/all_to_all | solution.py:527
  139.5 1.0 unpack.1
  (51 shorter events, 0.9 us)
Async XLA Ops:
  2.9 1.0 copy-start.4
  2.9 7.6 %copy-start.3 = (bf16[1,256,1184]{1,2,0:T(8,128)(2,1)S(1)}, bf16[1,256,1184]{1,2,0:T(8,128)(2,1)}, u32[]{:S(2)}) copy-start(bf16[1,256,1184]{1,2,0:T(8,128)(2,1)} %param.10) | copy-start | bytes 1818628
  4.9 13.2 %collective-permute-start = (bf16[2,384,128]{2,1,0:T(8,128)(2,1)S(1)}, bf16[2,384,128]{2,1,0:T(8,128)(2,1)S(1)}, u32[]{:S(2)}, u32[]{:S(2)}) collective-permute-start(bf16[2,384,128]{2,1,0:T(8,128)(2,1)S(1)} %get-tuple-element.119), channel_id=1, source_target_pairs={{0,8},{1,9},{2,10},{3,11},{4,12},{5,13},{6,14},{7,15},{8,0},{9,1},... | collective-permute-start | bytes 589832 | tf_op jit(solution)/shard_map/ppermute | solution.py:28
  9.0 9.1 %collective-permute-start.1 = (bf16[2,384,128]{2,1,0:T(8,128)(2,1)S(1)}, bf16[2,384,128]{2,1,0:T(8,128)(2,1)S(1)}, u32[]{:S(2)}, u32[]{:S(2)}) collective-permute-start(bf16[2,384,128]{2,1,0:T(8,128)(2,1)S(1)} %get-tuple-element.120), channel_id=1, source_target_pairs={{0,2},{1,3},{2,0},{3,1},{4,6},{5,7},{6,4},{7,5},{8,10},{9,11},{10,... | collective-permute-start | bytes 589832 | tf_op jit(solution)/shard_map/ppermute | solution.py:28
  10.5 3.4 %copy-start = (bf16[1184,3584]{1,0:T(8,128)(2,1)S(1)}, bf16[1184,3584]{1,0:T(8,128)(2,1)}, u32[]{:S(2)}) copy-start(bf16[1184,3584]{1,0:T(8,128)(2,1)} %weight_ref.1) | copy-start | bytes 25460740
  18.1 9.6 %copy-start.2 = (bf16[3584,192]{0,1:T(8,128)(2,1)S(1)}, bf16[3584,192]{0,1:T(8,128)(2,1)}, u32[]{:S(2)}) copy-start(bf16[3584,192]{0,1:T(8,128)(2,1)} %param.13) | copy-start | bytes 4128772
  18.1 14.9 %copy-start.6 = (bf16[3584]{0:T(1024)(128)(2,1)S(1)}, bf16[3584]{0:T(1024)(128)(2,1)}, u32[]{:S(2)}) copy-start(bf16[3584]{0:T(1024)(128)(2,1)} %param.12) | copy-start | bytes 21508
  18.1 24.2 %copy-start.1 = (bf16[192,4096]{1,0:T(8,128)(2,1)S(1)}, bf16[192,4096]{1,0:T(8,128)(2,1)}, u32[]{:S(2)}) copy-start(bf16[192,4096]{1,0:T(8,128)(2,1)} %refs_7_.1) | copy-start | bytes 4718596
  18.1 24.2 %copy-start.5 = (bf16[256,2,192]{0,2,1:T(8,128)(2,1)S(1)}, bf16[256,2,192]{0,2,1:T(8,128)(2,1)}, u32[]{:S(2)}) copy-start(bf16[256,2,192]{0,2,1:T(8,128)(2,1)} %param.14) | copy-start | bytes 589828
  18.1 1.9 %collective-permute-start.2 = (bf16[8,16,1792]{2,1,0:T(8,128)(2,1)S(1)}, bf16[8,16,1792]{2,1,0:T(8,128)(2,1)S(1)}, u32[]{:S(2)}, u32[]{:S(2)}) collective-permute-start(bf16[8,16,1792]{2,1,0:T(8,128)(2,1)S(1)} %get-tuple-element.133), channel_id=1, source_target_pairs={{0,1},{1,0},{2,3},{3,2},{4,5},{5,4},{6,7},{7,6},{8,9},{9,8},{10,11... | collective-permute-start | bytes 1376264 | tf_op jit(solution)/shard_map/ppermute | solution.py:28
  18.2 7.3 %collective-permute-start.4 = (bf16[2,384,128]{2,1,0:T(8,128)(2,1)S(1)}, bf16[2,384,128]{2,1,0:T(8,128)(2,1)S(1)}, u32[]{:S(2)}, u32[]{:S(2)}) collective-permute-start(bf16[2,384,128]{2,1,0:T(8,128)(2,1)S(1)} %get-tuple-element.136), channel_id=1, source_target_pairs={{0,4},{1,5},{2,6},{3,7},{4,0},{5,1},{6,2},{7,3},{8,12},{9,13},{10,... | collective-permute-start | bytes 589832 | tf_op jit(solution)/shard_map/ppermute | solution.py:28
  19.2 1.8 %collective-permute-start.3 = (bf16[8,16,1792]{2,1,0:T(8,128)(2,1)S(1)}, bf16[8,16,1792]{2,1,0:T(8,128)(2,1)S(1)}, u32[]{:S(2)}, u32[]{:S(2)}) collective-permute-start(bf16[8,16,1792]{2,1,0:T(8,128)(2,1)S(1)} %get-tuple-element.135), channel_id=1, source_target_pairs={{0,1},{1,0},{2,3},{3,2},{4,5},{5,4},{6,7},{7,6},{8,9},{9,8},{10,11... | collective-permute-start | bytes 1376264 | tf_op jit(solution)/shard_map/ppermute | solution.py:28
  25.5 17.3 %collective-permute-start.5 = (bf16[4,16,1792]{2,1,0:T(8,128)(2,1)S(1)}, bf16[4,16,1792]{2,1,0:T(8,128)(2,1)S(1)}, u32[]{:S(2)}, u32[]{:S(2)}) collective-permute-start(bf16[4,16,1792]{2,1,0:T(8,128)(2,1)S(1)} %get-tuple-element.138), channel_id=1, source_target_pairs={{0,2},{1,3},{2,0},{3,1},{4,6},{5,7},{6,4},{7,5},{8,10},{9,11},{10,... | collective-permute-start | bytes 688136 | tf_op jit(solution)/shard_map/ppermute | solution.py:28
  27.1 15.8 %collective-permute-start.6 = (bf16[4,16,1792]{2,1,0:T(8,128)(2,1)S(1)}, bf16[4,16,1792]{2,1,0:T(8,128)(2,1)S(1)}, u32[]{:S(2)}, u32[]{:S(2)}) collective-permute-start(bf16[4,16,1792]{2,1,0:T(8,128)(2,1)S(1)} %get-tuple-element.139), channel_id=1, source_target_pairs={{0,4},{1,5},{2,6},{3,7},{4,0},{5,1},{6,2},{7,3},{8,12},{9,13},{10,... | collective-permute-start | bytes 688136 | tf_op jit(solution)/shard_map/ppermute | solution.py:28
  27.7 29.8 %collective-permute-start.13 = (bf16[192,3584]{1,0:T(8,128)(2,1)S(1)}, bf16[192,3584]{1,0:T(8,128)(2,1)S(1)}, u32[]{:S(2)}, u32[]{:S(2)}) collective-permute-start(bf16[192,3584]{1,0:T(8,128)(2,1)S(1)} %bitcast.38), channel_id=1, source_target_pairs={{0,1},{1,0},{2,3},{3,2},{4,5},{5,4},{6,7},{7,6},{8,9},{9,8},{10,11... | collective-permute-start | bytes 4128776 | tf_op jit(solution)/shard_map/ppermute | solution.py:28
  28.4 13.9 %collective-permute-start.7 = (bf16[2,384,128]{2,1,0:T(8,128)(2,1)S(1)}, bf16[2,384,128]{2,1,0:T(8,128)(2,1)S(1)}, u32[]{:S(2)}, u32[]{:S(2)}) collective-permute-start(bf16[2,384,128]{2,1,0:T(8,128)(2,1)S(1)} %get-tuple-element.140), channel_id=1, source_target_pairs={{0,6},{1,7},{2,4},{3,5},{4,2},{5,3},{6,0},{7,1},{8,14},{9,15},{10,... | collective-permute-start | bytes 589832 | tf_op jit(solution)/shard_map/ppermute | solution.py:28
  29.7 12.6 %collective-permute-start.8 = (bf16[2,384,128]{2,1,0:T(8,128)(2,1)S(1)}, bf16[2,384,128]{2,1,0:T(8,128)(2,1)S(1)}, u32[]{:S(2)}, u32[]{:S(2)}) collective-permute-start(bf16[2,384,128]{2,1,0:T(8,128)(2,1)S(1)} %get-tuple-element.141), channel_id=1, source_target_pairs={{0,10},{1,11},{2,8},{3,9},{4,14},{5,15},{6,12},{7,13},{8,2},{9,3},... | collective-permute-start | bytes 589832 | tf_op jit(solution)/shard_map/ppermute | solution.py:28
  42.3 15.3 %collective-permute-start.14 = (bf16[192,4096]{1,0:T(8,128)(2,1)S(1)}, bf16[192,4096]{1,0:T(8,128)(2,1)S(1)}, u32[]{:S(2)}, u32[]{:S(2)}) collective-permute-start(bf16[192,4096]{1,0:T(8,128)(2,1)S(1)} %copy-done.1), channel_id=1, source_target_pairs={{0,1},{1,0},{2,3},{3,2},{4,5},{5,4},{6,7},{7,6},{8,9},{9,8},{10,11... | collective-permute-start | bytes 4718600 | tf_op jit(solution)/shard_map/ppermute | solution.py:28
  42.3 10.3 %collective-permute-start.15 = (bf16[2,192,256]{2,1,0:T(8,128)(2,1)S(1)}, bf16[2,192,256]{2,1,0:T(8,128)(2,1)S(1)}, u32[]{:S(2)}, u32[]{:S(2)}) collective-permute-start(bf16[2,192,256]{2,1,0:T(8,128)(2,1)S(1)} %bitcast.42), channel_id=1, source_target_pairs={{0,1},{1,0},{2,3},{3,2},{4,5},{5,4},{6,7},{7,6},{8,9},{9,8},{10,11... | collective-permute-start | bytes 589832 | tf_op jit(solution)/shard_map/ppermute | solution.py:28
  42.9 5.9 %collective-permute-start.9 = (bf16[2,16,1792]{2,1,0:T(8,128)(2,1)S(1)}, bf16[2,16,1792]{2,1,0:T(8,128)(2,1)S(1)}, u32[]{:S(2)}, u32[]{:S(2)}) collective-permute-start(bf16[2,16,1792]{2,1,0:T(8,128)(2,1)S(1)} %get-tuple-element.204), channel_id=1, source_target_pairs={{0,4},{1,5},{2,6},{3,7},{4,0},{5,1},{6,2},{7,3},{8,12},{9,13},{10,... | collective-permute-start | bytes 344072 | tf_op jit(solution)/shard_map/ppermute | solution.py:28
  45.0 5.9 %collective-permute-start.11 = (bf16[2,16,1792]{2,1,0:T(8,128)(2,1)S(1)}, bf16[2,16,1792]{2,1,0:T(8,128)(2,1)S(1)}, u32[]{:S(2)}, u32[]{:S(2)}) collective-permute-start(bf16[2,16,1792]{2,1,0:T(8,128)(2,1)S(1)} %get-tuple-element.202), channel_id=1, source_target_pairs={{0,2},{1,3},{2,0},{3,1},{4,6},{5,7},{6,4},{7,5},{8,10},{9,11},{10,... | collective-permute-start | bytes 344072 | tf_op jit(solution)/shard_map/ppermute | solution.py:28
  48.8 7.2 %collective-permute-start.10 = (bf16[1,16,1792]{2,1,0:T(8,128)(2,1)S(1)}, bf16[1,16,1792]{2,1,0:T(8,128)(2,1)S(1)}, u32[]{:S(2)}, u32[]{:S(2)}) collective-permute-start(bf16[1,16,1792]{2,1,0:T(8,128)(2,1)S(1)} %fusion.9), channel_id=1, source_target_pairs={{0,8},{1,9},{2,10},{3,11},{4,12},{5,13},{6,14},{7,15},{8,0},{9,1},... | collective-permute-start | bytes 172040 | tf_op jit(solution)/shard_map/ppermute | solution.py:28
  51.0 6.6 %collective-permute-start.12 = (bf16[1,16,1792]{2,1,0:T(8,128)(2,1)S(1)}, bf16[1,16,1792]{2,1,0:T(8,128)(2,1)S(1)}, u32[]{:S(2)}, u32[]{:S(2)}) collective-permute-start(bf16[1,16,1792]{2,1,0:T(8,128)(2,1)S(1)} %fusion.8), channel_id=1, source_target_pairs={{0,8},{1,9},{2,10},{3,11},{4,12},{5,13},{6,14},{7,15},{8,0},{9,1},... | collective-permute-start | bytes 172040 | tf_op jit(solution)/shard_map/ppermute | solution.py:28
  52.6 15.1 %collective-permute-start.20 = (bf16[6,384,128]{2,1,0:T(8,128)(2,1)S(1)}, bf16[6,384,128]{2,1,0:T(8,128)(2,1)S(1)}, u32[]{:S(2)}, u32[]{:S(2)}) collective-permute-start(bf16[6,384,128]{2,1,0:T(8,128)(2,1)S(1)} %gather_other.2), channel_id=1, source_target_pairs={{0,1},{1,0},{2,3},{3,2},{4,5},{5,4},{6,7},{7,6},{8,9},{9,8},{10,11... | collective-permute-start | bytes 1769480 | tf_op jit(solution)/shard_map/ppermute | solution.py:28
  57.9 6.4 %collective-permute-start.16 = (bf16[16,1792]{1,0:T(8,128)(2,1)S(1)}, bf16[16,1792]{1,0:T(8,128)(2,1)S(1)}, u32[]{:S(2)}, u32[]{:S(2)}) collective-permute-start(bf16[16,1792]{1,0:T(8,128)(2,1)S(1)} %get-tuple-element.217), channel_id=1, source_target_pairs={{0,8},{1,9},{2,10},{3,11},{4,12},{5,13},{6,14},{7,15},{8,0},{9,1},... | collective-permute-start | bytes 172040 | tf_op jit(solution)/shard_map/ppermute | solution.py:28
  58.0 6.9 %collective-permute-start.17 = (bf16[16,1792]{1,0:T(8,128)(2,1)S(1)}, bf16[16,1792]{1,0:T(8,128)(2,1)S(1)}, u32[]{:S(2)}, u32[]{:S(2)}) collective-permute-start(bf16[16,1792]{1,0:T(8,128)(2,1)S(1)} %get-tuple-element.216), channel_id=1, source_target_pairs={{0,8},{1,9},{2,10},{3,11},{4,12},{5,13},{6,14},{7,15},{8,0},{9,1},... | collective-permute-start | bytes 172040 | tf_op jit(solution)/shard_map/ppermute | solution.py:28
  64.9 4.9 %collective-permute-start.18 = (bf16[32,1792]{1,0:T(8,128)(2,1)S(1)}, bf16[32,1792]{1,0:T(8,128)(2,1)S(1)}, u32[]{:S(2)}, u32[]{:S(2)}) collective-permute-start(bf16[32,1792]{1,0:T(8,128)(2,1)S(1)} %pad_maximum_fusion.2), channel_id=1, source_target_pairs={{0,4},{1,5},{2,6},{3,7},{4,0},{5,1},{6,2},{7,3},{8,12},{9,13},{10,... | collective-permute-start | bytes 344072 | tf_op jit(solution)/shard_map/ppermute | solution.py:28
  66.3 5.2 %collective-permute-start.19 = (bf16[32,1792]{1,0:T(8,128)(2,1)S(1)}, bf16[32,1792]{1,0:T(8,128)(2,1)S(1)}, u32[]{:S(2)}, u32[]{:S(2)}) collective-permute-start(bf16[32,1792]{1,0:T(8,128)(2,1)S(1)} %pad_maximum_fusion.3), channel_id=1, source_target_pairs={{0,2},{1,3},{2,0},{3,1},{4,6},{5,7},{6,4},{7,5},{8,10},{9,11},{10,... | collective-permute-start | bytes 344072 | tf_op jit(solution)/shard_map/ppermute | solution.py:28
  71.5 15.3 %collective-permute-start.21 = (bf16[64,1792]{1,0:T(8,128)(2,1)S(1)}, bf16[64,1792]{1,0:T(8,128)(2,1)S(1)}, u32[]{:S(2)}, u32[]{:S(2)}) collective-permute-start(bf16[64,1792]{1,0:T(8,128)(2,1)S(1)} %pad_maximum_fusion.refs_0_), channel_id=1, source_target_pairs={{0,2},{1,3},{2,0},{3,1},{4,6},{5,7},{6,4},{7,5},{8,10},{9,11},{10,... | collective-permute-start | bytes 688136 | tf_op jit(solution)/shard_map/ppermute | solution.py:28
  73.1 13.8 %collective-permute-start.22 = (bf16[64,1792]{1,0:T(8,128)(2,1)S(1)}, bf16[64,1792]{1,0:T(8,128)(2,1)S(1)}, u32[]{:S(2)}, u32[]{:S(2)}) collective-permute-start(bf16[64,1792]{1,0:T(8,128)(2,1)S(1)} %pad_maximum_fusion.1.refs_2_), channel_id=1, source_target_pairs={{0,4},{1,5},{2,6},{3,7},{4,0},{5,1},{6,2},{7,3},{8,12},{9,13},{10,... | collective-permute-start | bytes 688136 | tf_op jit(solution)/shard_map/ppermute | solution.py:28
  73.8 13.0 %collective-permute-start.23 = (bf16[2,384,128]{2,1,0:T(8,128)(2,1)S(1)}, bf16[2,384,128]{2,1,0:T(8,128)(2,1)S(1)}, u32[]{:S(2)}, u32[]{:S(2)}) collective-permute-start(bf16[2,384,128]{2,1,0:T(8,128)(2,1)S(1)} %get-tuple-element.160), channel_id=1, source_target_pairs={{0,12},{1,13},{2,14},{3,15},{4,8},{5,9},{6,10},{7,11},{8,4},{9,5},... | collective-permute-start | bytes 589832 | tf_op jit(solution)/shard_map/ppermute | solution.py:28
  76.1 14.9 %collective-permute-start.24 = (bf16[2,384,128]{2,1,0:T(8,128)(2,1)S(1)}, bf16[2,384,128]{2,1,0:T(8,128)(2,1)S(1)}, u32[]{:S(2)}, u32[]{:S(2)}) collective-permute-start(bf16[2,384,128]{2,1,0:T(8,128)(2,1)S(1)} %get-tuple-element.162), channel_id=1, source_target_pairs={{0,14},{1,15},{2,12},{3,13},{4,10},{5,11},{6,8},{7,9},{8,6},{9,7},... | collective-permute-start | bytes 589832 | tf_op jit(solution)/shard_map/ppermute | solution.py:28
  89.2 6.9 %collective-permute-start.25 = (bf16[4,144,256]{2,1,0:T(8,128)(2,1)S(1)}, bf16[4,144,256]{2,1,0:T(8,128)(2,1)S(1)}, u32[]{:S(2)}, u32[]{:S(2)}) collective-permute-start(bf16[4,144,256]{2,1,0:T(8,128)(2,1)S(1)} %get-tuple-element.169), channel_id=1, source_target_pairs={{0,2},{1,3},{2,0},{3,1},{4,6},{5,7},{6,4},{7,5},{8,10},{9,11},{10,... | collective-permute-start | bytes 884744 | tf_op jit(solution)/shard_map/ppermute | solution.py:28
  89.3 7.6 %collective-permute-start.26 = (bf16[4,144,256]{2,1,0:T(8,128)(2,1)S(1)}, bf16[4,144,256]{2,1,0:T(8,128)(2,1)S(1)}, u32[]{:S(2)}, u32[]{:S(2)}) collective-permute-start(bf16[4,144,256]{2,1,0:T(8,128)(2,1)S(1)} %get-tuple-element.170), channel_id=1, source_target_pairs={{0,4},{1,5},{2,6},{3,7},{4,0},{5,1},{6,2},{7,3},{8,12},{9,13},{10,... | collective-permute-start | bytes 884744 | tf_op jit(solution)/shard_map/ppermute | solution.py:28
  91.1 1.5 %collective-permute-start.27 = (bf16[2,384,128]{2,1,0:T(8,128)(2,1)S(1)}, bf16[2,384,128]{2,1,0:T(8,128)(2,1)S(1)}, u32[]{:S(2)}, u32[]{:S(2)}) collective-permute-start(bf16[2,384,128]{2,1,0:T(8,128)(2,1)S(1)} %gather_other.3), channel_id=1, source_target_pairs={{0,1},{1,0},{2,3},{3,2},{4,5},{5,4},{6,7},{7,6},{8,9},{9,8},{10,11... | collective-permute-start | bytes 589832 | tf_op jit(solution)/shard_map/ppermute | solution.py:28
  96.9 7.6 %collective-permute-start.28 = (bf16[2,144,256]{2,1,0:T(8,128)(2,1)S(1)}, bf16[2,144,256]{2,1,0:T(8,128)(2,1)S(1)}, u32[]{:S(2)}, u32[]{:S(2)}) collective-permute-start(bf16[2,144,256]{2,1,0:T(8,128)(2,1)S(1)} %get-tuple-element.208), channel_id=1, source_target_pairs={{0,4},{1,5},{2,6},{3,7},{4,0},{5,1},{6,2},{7,3},{8,12},{9,13},{10,... | collective-permute-start | bytes 442376 | tf_op jit(solution)/shard_map/ppermute | solution.py:28
  99.6 5.2 %collective-permute-start.29 = (bf16[2,144,256]{2,1,0:T(8,128)(2,1)S(1)}, bf16[2,144,256]{2,1,0:T(8,128)(2,1)S(1)}, u32[]{:S(2)}, u32[]{:S(2)}) collective-permute-start(bf16[2,144,256]{2,1,0:T(8,128)(2,1)S(1)} %get-tuple-element.207), channel_id=1, source_target_pairs={{0,2},{1,3},{2,0},{3,1},{4,6},{5,7},{6,4},{7,5},{8,10},{9,11},{10,... | collective-permute-start | bytes 442376 | tf_op jit(solution)/shard_map/ppermute | solution.py:28
  104.8 6.7 %collective-permute-start.30 = (bf16[1,144,256]{2,1,0:T(8,128)(2,1)S(1)}, bf16[1,144,256]{2,1,0:T(8,128)(2,1)S(1)}, u32[]{:S(2)}, u32[]{:S(2)}) collective-permute-start(bf16[1,144,256]{2,1,0:T(8,128)(2,1)S(1)} %get-tuple-element.213), channel_id=1, source_target_pairs={{0,8},{1,9},{2,10},{3,11},{4,12},{5,13},{6,14},{7,15},{8,0},{9,1},... | collective-permute-start | bytes 221192 | tf_op jit(solution)/shard_map/ppermute | solution.py:28
  107.5 5.3 %collective-permute-start.31 = (bf16[1,144,256]{2,1,0:T(8,128)(2,1)S(1)}, bf16[1,144,256]{2,1,0:T(8,128)(2,1)S(1)}, u32[]{:S(2)}, u32[]{:S(2)}) collective-permute-start(bf16[1,144,256]{2,1,0:T(8,128)(2,1)S(1)} %get-tuple-element.211), channel_id=1, source_target_pairs={{0,8},{1,9},{2,10},{3,11},{4,12},{5,13},{6,14},{7,15},{8,0},{9,1},... | collective-permute-start | bytes 221192 | tf_op jit(solution)/shard_map/ppermute | solution.py:28
  113.5 1.3 collective-permute-start.32

commit v9 on v8

--- a/solution.py
+++ b/solution.py
@@ -279,33 +279,34 @@
     )(place, *parts)
 
 
-def pack_kernel(copies, place_ref, queries_ref, keys_ref, values_ref, *outs):
+def pack_kernel(copies, place_ref, queries_ref, keys_ref, values_ref, out_ref):
     chip, core = place_ref[3], place_ref[2]
     img_dev = keys_ref.shape[0]
     part_rows = img_dev // copies
-    for mask, out_ref in enumerate(outs):
-        for side in range(2):
-            device = 2 * (chip ^ mask) + (core ^ side)
-            head, copy = device // copies, device % copies
-            span = pl.ds(pl.multiple_of(head * HEAD_DIM, HEAD_DIM), HEAD_DIM)
-            rows = pl.ds(pl.multiple_of(copy * part_rows, part_rows), part_rows)
-            out_ref[side, :img_dev, :] = keys_ref[:, span]
-            out_ref[side, img_dev : 2 * img_dev, :] = values_ref[:, span]
-            out_ref[side, 2 * img_dev :, :] = queries_ref[rows, span]
+    half_chips = out_ref.shape[1]
+    for top in range(2):
+        for mask in range(half_chips):
+            for side in range(2):
+                device = 2 * (top * half_chips + (chip % half_chips) ^ mask) + (core ^ side)
+                head, copy = device // copies, device % copies
+                span = pl.ds(pl.multiple_of(head * HEAD_DIM, HEAD_DIM), HEAD_DIM)
+                rows = pl.ds(pl.multiple_of(copy * part_rows, part_rows), part_rows)
+                out_ref[top, mask, side, :img_dev, :] = keys_ref[:, span]
+                out_ref[top, mask, side, img_dev : 2 * img_dev, :] = values_ref[:, span]
+                out_ref[top, mask, side, 2 * img_dev :, :] = queries_ref[rows, span]
 
 
 def pack(chips, copies, place, queries, keys, values):
     img_dev = keys.shape[0]
-    rows = 2 * img_dev + img_dev // copies
-    out = jax.ShapeDtypeStruct((2, rows, HEAD_DIM), jnp.bfloat16)
+    shape = (2, chips // 2, 2, 2 * img_dev + img_dev // copies, HEAD_DIM)
     return pl.pallas_call(
         functools.partial(pack_kernel, copies),
-        out_shape=(out,) * chips,
+        out_shape=jax.ShapeDtypeStruct(shape, jnp.bfloat16),
         in_specs=[SMEM_SPEC] + [VMEM_SPEC] * 3,
-        out_specs=(VMEM_SPEC,) * chips,
+        out_specs=VMEM_SPEC,
         compiler_params=params(8),
         cost_estimate=pl.CostEstimate(
-            flops=0, bytes_accessed=8 * chips * rows * HEAD_DIM, transcendentals=0
+            flops=0, bytes_accessed=4 * math.prod(shape), transcendentals=0
         ),
         name="pack",
     )(place, queries, keys, values)
@@ -331,10 +332,15 @@
     )(*pieces)
 
 
-def by_distance(pieces, early, late, early_ref, late_ref):
-    passed = {mask: (early_ref, at) for at, mask in enumerate(early)}
-    passed.update({mask: (late_ref, at) for at, mask in enumerate(late)})
-    return [block for mask, piece in enumerate(pieces) for block in ((piece, 0), passed[mask])]
+def all_blocks(pieces, passed_ref):
+    views = [(piece.at[0], passed_ref.at[at]) for at, piece in enumerate(pieces)]
+    return [view for pair in views for view in pair]
+
+
+def origin(at, count, chip, core):
+    half_chips = count // 4
+    mask, top, side = at // 4, at // 2 % 2, at % 2
+    return 2 * (top * half_chips + (chip % half_chips) ^ mask) + (core ^ side)
 
 
 def unpack_kernel(copies, part_rows, blocks_ref, attended_ref, text_ref):
@@ -367,14 +373,14 @@
     )(blocks)
 
 
-def image_kernel(factor, call, early, late, img_dev, *refs):
-    *pieces, early_ref, late_ref, sum_ref, top_ref, keys_ref, values_ref = refs
-    blocks = by_distance(pieces, early, late, early_ref, late_ref)
+def image_kernel(factor, call, img_dev, *refs):
+    *pieces, passed_ref, sum_ref, top_ref, keys_ref, values_ref = refs
+    blocks = all_blocks(pieces, passed_ref)
     values_ref[:, HEAD_DIM:] = jnp.ones((values_ref.shape[0], HEAD_DIM), values_ref.dtype)
-    for at, (piece, side) in enumerate(blocks):
+    for at, block in enumerate(blocks):
         rows = slice(at * img_dev, (at + 1) * img_dev)
-        keys_ref[rows, :] = piece[side, :img_dev, :]
-        values_ref[rows, :HEAD_DIM] = piece[side, img_dev : 2 * img_dev, :]
+        keys_ref[rows, :] = block[:img_dev, :]
+        values_ref[rows, :HEAD_DIM] = block[img_dev : 2 * img_dev, :]
     part_rows = pieces[0].shape[1] - 2 * img_dev
     group = max(1, 256 // part_rows)
     rows = group * part_rows
@@ -383,7 +389,7 @@
     for step in range(steps):
         at = (call * steps + step) * group
         span = slice(step * rows, (step + 1) * rows)
-        queries = [piece[side, 2 * img_dev :, :] for piece, side in blocks[at : at + group]]
+        queries = [block[2 * img_dev :, :] for block in blocks[at : at + group]]
         queries = jnp.concatenate(queries, 0)
         scores = lax.dot_general(queries, keys_ref[...], contract, preferred_element_type=jnp.float32)
         scores = scores * factor
@@ -393,17 +399,17 @@
         top_ref[span, :] = jnp.broadcast_to(top, (rows, HEAD_DIM))
 
 
-def image_attention(pieces, passed, early, late, img_dev, factor, call, calls):
+def image_attention(pieces, passed, img_dev, factor, call, calls):
     devices = 2 * len(pieces)
     keys = devices * img_dev
     count = devices * (pieces[0].shape[1] - 2 * img_dev) // calls
     return pl.pallas_call(
-        functools.partial(image_kernel, factor, call, early, late, img_dev),
+        functools.partial(image_kernel, factor, call, img_dev),
         out_shape=(
             jax.ShapeDtypeStruct((count, 2 * HEAD_DIM), jnp.float32),
             jax.ShapeDtypeStruct((count, HEAD_DIM), jnp.float32),
         ),
-        in_specs=[VMEM_SPEC] * (len(pieces) + 2),
+        in_specs=[VMEM_SPEC] * (len(pieces) + 1),
         out_specs=(VMEM_SPEC, VMEM_SPEC),
         scratch_shapes=[
             pltpu.VMEM((keys, HEAD_DIM), jnp.bfloat16),
@@ -416,15 +422,14 @@
             transcendentals=count * keys,
         ),
         name="image_attention",
-    )(*pieces, *passed)
-
-
-def finish_kernel(factor, calls, early, late, img_dev, place_ref, *refs):
-    *pieces, early_ref, late_ref = refs[: -3 - 2 * calls]
+    )(*pieces, passed)
+
+
+def finish_kernel(factor, calls, img_dev, place_ref, *refs):
+    *pieces, passed_ref = refs[: -3 - 2 * calls]
     images, (mine_ref, got_ref, out_ref) = refs[-3 - 2 * calls : -3], refs[-3:]
-    blocks = by_distance(pieces, early, late, early_ref, late_ref)
+    blocks = all_blocks(pieces, passed_ref)
     core, valid = place_ref[2], place_ref[4]
-    me = 2 * place_ref[3] + core
     devices, part_rows = len(blocks), pieces[0].shape[1] - 2 * img_dev
     half = mine_ref.shape[0]
     contract = (((1,), (1,)), ((), ()))
@@ -442,7 +447,7 @@
         sum_ref, top_ref = images[2 * (step // each)], images[2 * (step // each) + 1]
         span = slice(step % each * rows, (step % each + 1) * rows)
         queries = blocks[step * group : (step + 1) * group]
-        queries = jnp.concatenate([piece[side, 2 * img_dev :, :] for piece, side in queries], 0)
+        queries = jnp.concatenate([block[2 * img_dev :, :] for block in queries], 0)
         scores = lax.dot_general(queries, keys, contract, preferred_element_type=jnp.float32)
         scores = scores * factor + bias
         before = top_ref[span, :]
@@ -454,7 +459,7 @@
         total = sum_ref[span, HEAD_DIM:] * rescale + total[:, HEAD_DIM:]
         mixed = (mixed / total).astype(out_ref.dtype)
         for at in range(group):
-            to = me ^ (step * group + at)
+            to = origin(step * group + at, devices, place_ref[3], core)
             out_ref[to, :part_rows, :] = mixed[at * part_rows : (at + 1) * part_rows]
     low = jnp.where(core == 0, mine.astype(jnp.float32), got.astype(jnp.float32))
     high = jnp.where(core == 0, got.astype(jnp.float32), mine.astype(jnp.float32))
@@ -467,14 +472,14 @@
         out_ref[device, part_rows:, :] = block.astype(out_ref.dtype)
 
 
-def finish(place, pieces, passed, early, late, images, mine, got, img_dev, factor):
+def finish(place, pieces, passed, images, mine, got, img_dev, factor):
     devices, part_rows = 2 * len(pieces), pieces[0].shape[1] - 2 * img_dev
     share = 2 * mine.shape[0] // devices
     count = devices * part_rows
     return pl.pallas_call(
-        functools.partial(finish_kernel, factor, len(images) // 2, early, late, img_dev),
+        functools.partial(finish_kernel, factor, len(images) // 2, img_dev),
         out_shape=jax.ShapeDtypeStruct((devices, part_rows + 2 * share, HEAD_DIM), jnp.bfloat16),
-        in_specs=[SMEM_SPEC] + [VMEM_SPEC] * (len(pieces) + len(images) + 4),
+        in_specs=[SMEM_SPEC] + [VMEM_SPEC] * (len(pieces) + len(images) + 3),
         out_specs=VMEM_SPEC,
         compiler_params=params(16),
         cost_estimate=pl.CostEstimate(
@@ -483,7 +488,7 @@
             transcendentals=count * 2 * mine.shape[0],
         ),
         name="finish",
-    )(place, *pieces, *passed, *images, mine, got)
+    )(place, *pieces, passed, *images, mine, got)
 
 
 def add(one, other, dtype):
@@ -527,52 +532,41 @@
         return lax.all_to_all(rows, "seq", split_axis=0, concat_axis=0, tiled=True)
 
     image_key_values, image_queries = tie((image_key_values, image_queries))
-    pieces = pack(
+    packed = pack(
         chips, copies, place, image_queries[0], image_key_values[0, :, 0], image_key_values[0, :, 1]
     )
-    pieces = list(pieces)
-    act, pieces = tie((enc_act[0].T, pieces))
-    late = [6, 7]
-    early = [mask for mask in range(chips) if mask not in late]
-
-    def send_piece(mask, chain):
-        chain, piece = tie((chain, pieces[mask]))
-        pieces[mask] = swap(piece, 2 * mask)
-        return chain
-
-    def take_pieces(masks, chain):
-        chain, taken = tie((chain, [pieces[mask] for mask in masks]))
-        for mask, piece in zip(masks, taken):
-            pieces[mask] = piece
-        return chain
-
-    first, second = [4, 1, 2], [mask for mask in early if mask in (3, 5) or mask > 7]
-    for mask in first:
-        act = send_piece(mask, act)
+    half_chips = chips // 2
+    pairs = [[i, i + half_chips * 2] for i in range(half_chips * 2)]
+    act, packed = tie((enc_act[0].T, packed))
+    packed = lax.all_to_all(
+        packed, "seq", split_axis=0, concat_axis=0, axis_index_groups=pairs, tiled=True
+    )
+
+    def move(chain, array, mask):
+        chain, array = tie((chain, array))
+        return chain, swap(array, 2 * mask)
+
+    encoded = list(encoder(lanes, place, act, down_weight))
     keep, sent = [], []
-    encoded = list(encoder(lanes, place, act, down_weight))
-    encoded[1::2] = take_pieces(first[:2], encoded[1::2])
-    for mask in second:
-        encoded = send_piece(mask, encoded)
     for own, other in (encoded[:2], encoded[2:]):
         got = swap(other, 1)
         sent.append(add(own[chips // 2 :], got[chips // 2 :], jnp.bfloat16))
         keep.append(add(own[: chips // 2], got[: chips // 2], jnp.float32))
-    sent = take_pieces(first[2:], sent)
     for step in range(rounds):
         got = [swap(part, 2 * order[step]) for part, order in zip(sent, lanes)]
         if step == 0:
-            got = take_pieces(second, got)
+            got, win1 = tie((got, win1))
         if step == 1:
-            passed_early = gather_other([pieces[mask] for mask in early])
+            got, kv1, mod1 = tie((got, kv1, mod1))
+            lines = modulation(time, mod0, mod1)
         if step == 2:
-            got, win1, kv1, mod1 = tie((got, win1, kv1, mod1))
-            lines = modulation(time, mod0, mod1)
+            got, packed = tie((got, packed))
         half = keep[0].shape[0] // 2
         if half:
             sent = [add(mine[half:], part[half:], jnp.bfloat16) for mine, part in zip(keep, got)]
             keep = [add(mine[:half], part[:half], jnp.float32) for mine, part in zip(keep, got)]
     summed = [add(mine[0], part[0], jnp.float32) for mine, part in zip(keep, got)]
+    pieces = {(mask, top): packed[top, mask] for mask in range(half_chips) for top in range(2)}
 
     width = summed[0].shape[1]
     square = sum(jnp.sum(part * part, 1, keepdims=True) for part in summed)
@@ -585,30 +579,39 @@
     images = []
 
     for step in reversed(range(rounds)):
-        if step < 2:
-            states = send_piece(late[1 - step], states)
+        if step > 0:
+            top = step % 2
+            for mask in (1, 2):
+                if step > rounds - 3:
+                    states, pieces[mask, top] = move(states, pieces[mask, top], mask)
+        if step == 0:
+            for mask in range(3, half_chips):
+                for top in range(2):
+                    states, pieces[mask, top] = move(states, pieces[mask, top], mask)
         got = [swap(state, 2 * order[step]) for state, order in zip(states, lanes)]
+        if step > rounds - 3 and step > 0:
+            got, pieces[1, top], pieces[2, top] = tie((got, pieces[1, top], pieces[2, top]))
         if step == rounds - 1:
-            passed_early = swap(passed_early, 1)
             got, lines = tie((got, lines))
-        if step == rounds - 2:
-            got, passed_early = tie((got, passed_early))
+        if step == 0:
+            for mask in range(3, half_chips):
+                got, pieces[mask, 0] = tie((got, pieces[mask, 0]))
         if step:
             states = [jnp.concatenate(pair, 0) for pair in zip(states, got)]
-    got = take_pieces(late[:1], got)
+    pieces = [pieces[mask, top] for mask in range(half_chips) for top in range(2)]
     states = [state for pair in zip(states, got) for state in pair]
 
     blocks = project(lanes, place, states, lines, win0, win1, kv0, kv1)
+    blocks, pieces = tie((blocks, pieces))
     keep, sent = [blocks[0], blocks[2]], [blocks[1], blocks[3]]
     for step in range(rounds):
         got = [swap(part, 2 * order[step]) for part, order in zip(sent, lanes)]
         if step == 0:
-            passed_late = swap(gather_other([pieces[mask] for mask in late]), 1)
-            got, passed_late = tie((got, passed_late))
-            passed = (passed_early, passed_late)
+            passed = swap(gather_other(pieces), 1)
+            got, passed = tie((got, passed))
         elif step <= 2:
             sent, passed = tie((sent, passed))
-            image = image_attention(pieces, passed, early, late, img_dev, factor, step - 1, 2)
+            image = image_attention(pieces, passed, img_dev, factor, step - 1, 2)
             got, image = tie((got, image))
             images += image
         half = keep[0].shape[0] // 2
@@ -620,7 +623,7 @@
     mine, sent = combine(place, parts, chips, text_len // 2, model_width)
     got = swap(sent, 1)
 
-    back = exchange(finish(place, pieces, passed, early, late, images, mine, got, img_dev, factor))
+    back = exchange(finish(place, pieces, passed, images, mine, got, img_dev, factor))
     attended, text_kv = unpack(copies, part_rows, back)
     return (attended[None], text_kv)
 

time: 141 us -> 161 us (1.14)
  waiting for transfers between devices: 48.3 us -> 62.1 us
  other arithmetic: 0.89 us -> 7.94 us
  starting transfers between devices: 42.6 us -> 37.5 us
  Pallas kernels: 17.4 us -> 19.9 us
  local copies, waits for them, and re-layouts: 6.02 us -> 8.23 us
    all_to_all x0 -> x1, waiting for transfers between devices: none -> 13.8 us  [local(): lax.all_to_all(packed, 'seq', split_axis=0, concat_axis=0, axis_index_gro...]
    ppermute x33 -> x31, starting transfers between devices: 42.6 us -> 32.7 us  [swap(): return lax.ppermute(value, 'seq', [(i, i ^ mask) for i in range(devices)])]
    all_to_all x0 -> x1, starting transfers between devices: none -> 4.79 us  [local(): lax.all_to_all(packed, 'seq', split_axis=0, concat_axis=0, axis_index_gro...]
    convert_element_type x5, other arithmetic: 0.17 us -> 3.59 us  [add(): return (one.astype(jnp.float32) + other.astype(jnp.float32)).astype(dtype)]
    add x3, other arithmetic: 0.27 us -> 2.22 us  [add(): return (one.astype(jnp.float32) + other.astype(jnp.float32)).astype(dtype)]
    unnamed x14 -> x30, local copies, waits for them, and re-layouts: 4.25 us -> 4.3 us
    ppermute x33 -> x31, waiting for transfers between devices: 48.3 us -> 48.3 us  [swap(): return lax.ppermute(value, 'seq', [(i, i ^ mask) for i in range(devices)])]
  transfers between devices with their start and end apart: 33 -> 32, of which waited for: 19 -> 19; matrix products, arithmetic and copies ran while one was open for 1% -> 4% of each run, Pallas kernels for 9% -> 7%
where the time goes in v9:
time: 161 us; the launch traced here: 160 us
  waiting for transfers between devices  62.1 us (39%)
  starting transfers between devices  37.5 us (23%)
  blocking collectives  22.6 us (14%)
  Pallas kernels  19.9 us (12%)
  local copies, waits for them, and re-layouts  8.23 us (5%)
  other arithmetic  7.94 us (5%)
  between operations  2.29 us (1%)
    ppermute x31, waiting for transfers between devices, swap(): return lax.ppermute(value, 'seq', [(i, i ^ mask) for i in range(devices)])  48.3 us
    ppermute x31, starting transfers between devices, swap(): return lax.ppermute(value, 'seq', [(i, i ^ mask) for i in range(devices)])  32.7 us
    all_to_all x1, blocking collectives, exchange(): return lax.all_to_all(rows, 'seq', split_axis=0, concat_axis=0, tiled=True)  22.6 us
    all_to_all x1, waiting for transfers between devices, local(): lax.all_to_all(packed, 'seq', split_axis=0, concat_axis=0, axis_index_gro...  13.8 us
    pallas_call x2, Pallas kernels, image_attention(): pl.pallas_call(functools.partial(image_kernel, factor, call, img_dev), ou...  7.07 us
    all_to_all x1, starting transfers between devices, local(): lax.all_to_all(packed, 'seq', split_axis=0, concat_axis=0, axis_index_gro...  4.79 us
    unnamed x30, local copies, waits for them, and re-layouts  4.3 us
    convert_element_type x5, other arithmetic, add(): return (one.astype(jnp.float32) + other.astype(jnp.float32)).astype(dtype)  3.59 us
  transfers between devices with their start and end apart: 32, of which 19 were waited for; matrix products, arithmetic and copies ran while one was open for 4% of the time, Pallas kernels for 7%

profile of v9, /device:TPU:0, one launch (start us, length us, event | category | flops | bytes accessed | tf_op | source)
XLA Modules:
  0.0 160.5 jit_solution(5354277956332724069)
XLA Ops:
  1.3 1.6 copy.12
  3.1 0.8 copy-done.3
  3.9 2.1 %pack.1 = bf16[2,4,2,384,128]{4,3,2,1,0:T(8,128)(2,1)} custom-call(s32[5]{0:T(128)S(1)} %stack.19.place_ref, bf16[128,2048]{1,0:T(8,128)(2,1)S(1)} %bitcast.55, bf16[128,2048]{1,0:T(8,128)(2,1)S(1)} %get-tuple-element.185.keys_ref, bf16[128,2048]{1,0:T(8,128)(2,1)S(1)} %get-tuple-element.184.values_ref), custom_call_target="tpu_custom_call" | custom-call | bytes 3145728 | tf_op jit(solution)/shard_map/pack/pallas_call | solution.py:302
  6.1 3.4 %copy-done = bf16[1184,3584]{1,0:T(8,128)(2,1)S(1)} copy-done((bf16[1184,3584]{1,0:T(8,128)(2,1)S(1)}, bf16[1184,3584]{1,0:T(8,128)(2,1)}, u32[]{:S(2)}) %copy-start) | copy-done | bytes 8486936
  9.5 3.5 %encoder.1 = (bf16[8,16,1792]{2,1,0:T(8,128)(2,1)S(1)}, bf16[8,16,1792]{2,1,0:T(8,128)(2,1)S(1)}, bf16[8,16,1792]{2,1,0:T(8,128)(2,1)S(1)}, bf16[8,16,1792]{2,1,0:T(8,128)(2,1)S(1)}) custom-call(s32[5]{0:T(128)S(1)} %stack.19.place_ref, bf16[1184,256]{1,0:T(8,128)(2,1)S(1)} %bitcast.54, bf16[1184,3584]{1,0:T(8,128)(2,1)S(1)} %copy-done), custom_call_target="tpu_custom_call" | custom-call | flops 2172649472 | bytes 10928128 | tf_op jit(solution)/shard_map/encoder/pallas_call | solution.py:89
  13.0 0.5 collective-permute-start.2
  13.6 0.4 collective-permute-start
  14.1 0.9 collective-permute-done.2
  14.9 0.9 convert_add_fusion
  15.9 2.9 %collective-permute-start.3 = (bf16[4,16,1792]{2,1,0:T(8,128)(2,1)}, bf16[4,16,1792]{2,1,0:T(8,128)(2,1)}, u32[]{:S(2)}, u32[]{:S(2)}) collective-permute-start(bf16[4,16,1792]{2,1,0:T(8,128)(2,1)} %get-tuple-element.187), channel_id=1, source_target_pairs={{0,4},{1,5},{2,6},{3,7},{4,0},{5,1},{6,2},{7,3},{8,12},{9,13},{10,... | collective-permute-start | bytes 688136 | tf_op jit(solution)/shard_map/ppermute | solution.py:28
  18.8 1.0 add_convert_fusion.1
  19.9 1.5 collective-permute-start.1
  21.4 4.8 %all-to-all-start = ((bf16[2,4,2,384,128]{4,3,2,1,0:T(8,128)(2,1)}), bf16[2,4,2,384,128]{4,3,2,1,0:T(8,128)(2,1)}, u32[]{:S(2)}, u32[]{:S(2)}) async-start(bf16[2,4,2,384,128]{4,3,2,1,0:T(8,128)(2,1)} %pack.1), calls=%async_computation | async-start | bytes 3145728 | tf_op jit(solution)/shard_map/all_to_all | solution.py:541
  26.2 1.4 collective-permute-done.1
  27.5 1.2 slice_add_fusion
  28.8 1.6 collective-permute-start.6
  30.3 1.2 fusion.1
  31.6 0.7 collective-permute-start.5
  32.3 1.4 collective-permute-done.6
  33.6 13.0 %collective-permute-done.5 = bf16[2,16,1792]{2,1,0:T(8,128)(2,1)S(1)} collective-permute-done((bf16[2,16,1792]{2,1,0:T(8,128)(2,1)S(1)}, bf16[2,16,1792]{2,1,0:T(8,128)(2,1)S(1)}, u32[]{:S(2)}, u32[]{:S(2)}) %collective-permute-start.5) | collective-permute-done | bytes 114720 | tf_op jit(solution)/shard_map/ppermute | solution.py:28
  46.6 0.7 fusion.8
  47.3 3.5 %collective-permute-start.10 = (bf16[1,16,1792]{2,1,0:T(8,128)(2,1)}, bf16[1,16,1792]{2,1,0:T(8,128)(2,1)}, u32[]{:S(2)}, u32[]{:S(2)}) collective-permute-start(bf16[1,16,1792]{2,1,0:T(8,128)(2,1)} %fusion.8), channel_id=1, source_target_pairs={{0,8},{1,9},{2,10},{3,11},{4,12},{5,13},{6,14},{7,15},{8,0},{9,1},... | collective-permute-start | bytes 172040 | tf_op jit(solution)/shard_map/ppermute | solution.py:28
  50.8 0.6 fusion.9
  51.4 0.6 fusion.13
  52.7 13.8 %all-to-all-done = bf16[2,4,2,384,128]{4,3,2,1,0:T(8,128)(2,1)} async-done(((bf16[2,4,2,384,128]{4,3,2,1,0:T(8,128)(2,1)}), bf16[2,4,2,384,128]{4,3,2,1,0:T(8,128)(2,1)}, u32[]{:S(2)}, u32[]{:S(2)}) %all-to-all-start) | async-done | bytes 1572896 | tf_op jit(solution)/shard_map/all_to_all | solution.py:541
  66.5 1.2 collective-permute-done.10
  67.7 1.2 collective-permute-done.9
  68.9 1.6 slice_bitcast_fusion.2
  70.5 1.0 multiply_reduce_fusion
  71.6 0.9 multiply_convert_fusion
  72.6 0.6 collective-permute-start.13
  73.2 0.8 collective-permute-start.11
  74.0 2.2 %collective-permute-start.12 = (bf16[16,1792]{1,0:T(8,128)(2,1)S(1)}, bf16[16,1792]{1,0:T(8,128)(2,1)S(1)}, u32[]{:S(2)}, u32[]{:S(2)}) collective-permute-start(bf16[16,1792]{1,0:T(8,128)(2,1)S(1)} %get-tuple-element.107), channel_id=1, source_target_pairs={{0,8},{1,9},{2,10},{3,11},{4,12},{5,13},{6,14},{7,15},{8,0},{9,1},... | collective-permute-start | bytes 172040 | tf_op jit(solution)/shard_map/ppermute | solution.py:28
  76.4 2.7 %collective-permute-done.11 = bf16[16,1792]{1,0:T(8,128)(2,1)S(1)} collective-permute-done((bf16[16,1792]{1,0:T(8,128)(2,1)S(1)}, bf16[16,1792]{1,0:T(8,128)(2,1)S(1)}, u32[]{:S(2)}, u32[]{:S(2)}) %collective-permute-start.11) | collective-permute-done | bytes 57376 | tf_op jit(solution)/shard_map/ppermute | solution.py:28
  79.2 2.5 %collective-permute-done.12 = bf16[16,1792]{1,0:T(8,128)(2,1)S(1)} collective-permute-done((bf16[16,1792]{1,0:T(8,128)(2,1)S(1)}, bf16[16,1792]{1,0:T(8,128)(2,1)S(1)}, u32[]{:S(2)}, u32[]{:S(2)}) %collective-permute-start.12) | collective-permute-done | bytes 57376 | tf_op jit(solution)/shard_map/ppermute | solution.py:28
  81.7 0.3 collective-permute-done.14.refs_4_
  82.0 1.2 collective-permute-start.17
  83.2 1.9 %collective-permute-start.15 = (bf16[32,1792]{1,0:T(8,128)(2,1)S(1)}, bf16[32,1792]{1,0:T(8,128)(2,1)S(1)}, u32[]{:S(2)}, u32[]{:S(2)}) collective-permute-start(bf16[32,1792]{1,0:T(8,128)(2,1)S(1)} %pad_maximum_fusion.2), channel_id=1, source_target_pairs={{0,4},{1,5},{2,6},{3,7},{4,0},{5,1},{6,2},{7,3},{8,12},{9,13},{10,... | collective-permute-start | bytes 344072 | tf_op jit(solution)/shard_map/ppermute | solution.py:28
  85.2 0.9 collective-permute-start.16
  86.1 3.9 %collective-permute-done.15 = bf16[32,1792]{1,0:T(8,128)(2,1)S(1)} collective-permute-done((bf16[32,1792]{1,0:T(8,128)(2,1)S(1)}, bf16[32,1792]{1,0:T(8,128)(2,1)S(1)}, u32[]{:S(2)}, u32[]{:S(2)}) %collective-permute-start.15) | collective-permute-done | bytes 114720 | tf_op jit(solution)/shard_map/ppermute | solution.py:28
  90.0 0.3 collective-permute-done.16
  90.3 1.3 collective-permute-start.19
  91.6 1.7 %collective-permute-start.20 = (bf16[64,1792]{1,0:T(8,128)(2,1)S(1)}, bf16[64,1792]{1,0:T(8,128)(2,1)S(1)}, u32[]{:S(2)}, u32[]{:S(2)}) collective-permute-start(bf16[64,1792]{1,0:T(8,128)(2,1)S(1)} %pad_maximum_fusion.1.refs_2_), channel_id=1, source_target_pairs={{0,4},{1,5},{2,6},{3,7},{4,0},{5,1},{6,2},{7,3},{8,12},{9,13},{10,... | collective-permute-start | bytes 688136 | tf_op jit(solution)/shard_map/ppermute | solution.py:28
  93.3 0.6 collective-permute-start.21
  93.8 2.4 %collective-permute-start.22 = (bf16[2,384,128]{2,1,0:T(8,128)(2,1)S(1)}, bf16[2,384,128]{2,1,0:T(8,128)(2,1)S(1)}, u32[]{:S(2)}, u32[]{:S(2)}) collective-permute-start(bf16[2,384,128]{2,1,0:T(8,128)(2,1)S(1)} %get-tuple-element.142), channel_id=1, source_target_pairs={{0,6},{1,7},{2,4},{3,5},{4,2},{5,3},{6,0},{7,1},{8,14},{9,15},{10,... | collective-permute-start | bytes 589832 | tf_op jit(solution)/shard_map/ppermute | solution.py:28
  96.2 7.4 %collective-permute-done.21.refs_6_ = bf16[2,384,128]{2,1,0:T(8,128)(2,1)S(1)} collective-permute-done((bf16[2,384,128]{2,1,0:T(8,128)(2,1)S(1)}, bf16[2,384,128]{2,1,0:T(8,128)(2,1)S(1)}, u32[]{:S(2)}, u32[]{:S(2)}) %collective-permute-start.21) | collective-permute-done | bytes 196640 | tf_op jit(solution)/shard_map/ppermute | solution.py:28
  103.6 3.5 %project.1 = (bf16[4,144,256]{2,1,0:T(8,128)(2,1)S(1)}, bf16[4,144,256]{2,1,0:T(8,128)(2,1)S(1)}, bf16[4,144,256]{2,1,0:T(8,128)(2,1)S(1)}, bf16[4,144,256]{2,1,0:T(8,128)(2,1)S(1)}) custom-call(s32[5]{0:T(128)S(1)} %stack.19.place_ref, bf16[64,1792]{1,0:T(8,128)(2,1)S(1)} %pad_maximum_fusion.refs_0_, bf16[64,1792]{1,0:T(8,128)(2,1)S(1)} %collective-permute-done.19.refs_1_, ...), custom_call_target="tpu_custom_call" | custom-call | flops 754974720 | bytes 7864320 | tf_op jit(solution)/shard_map/project/pallas_call | solution.py:211
  107.3 1.1 collective-permute-start.23
  108.5 1.4 collective-permute-start.24
  109.9 6.9 %collective-permute-done.23 = bf16[4,144,256]{2,1,0:T(8,128)(2,1)S(1)} collective-permute-done((bf16[4,144,256]{2,1,0:T(8,128)(2,1)S(1)}, bf16[4,144,256]{2,1,0:T(8,128)(2,1)S(1)}, u32[]{:S(2)}, u32[]{:S(2)}) %collective-permute-start.23) | collective-permute-done | bytes 294944 | tf_op jit(solution)/shard_map/ppermute | solution.py:28
  116.8 0.8 collective-permute-done.24
  117.6 1.0 collective-permute-start.27
  118.7 0.9 collective-permute-start.26
  119.6 3.5 %image_attention.2 = (f32[1024,256]{1,0:T(8,128)S(1)}, f32[1024,128]{1,0:T(8,128)S(1)}) custom-call(bf16[2,384,128]{2,1,0:T(8,128)(2,1)S(1)} %get-tuple-element.143.refs_0_, bf16[2,384,128]{2,1,0:T(8,128)(2,1)S(1)} %get-tuple-element.144.refs_1_, bf16[2,384,128]{2,1,0:T(8,128)(2,1)S(1)} %collective-permute-done.13.refs_2_, ...), custom_call_target="tpu_custom_call" | custom-call | flops 1073741824 | bytes 2359296 | tf_op jit(solution)/shard_map/image_attention/pallas_call | solution.py:406
  123.2 0.8 collective-permute-done.26
  124.0 2.8 %collective-permute-start.29 = (bf16[1,144,256]{2,1,0:T(8,128)(2,1)S(1)}, bf16[1,144,256]{2,1,0:T(8,128)(2,1)S(1)}, u32[]{:S(2)}, u32[]{:S(2)}) collective-permute-start(bf16[1,144,256]{2,1,0:T(8,128)(2,1)S(1)} %get-tuple-element.199), channel_id=1, source_target_pairs={{0,8},{1,9},{2,10},{3,11},{4,12},{5,13},{6,14},{7,15},{8,0},{9,1},... | collective-permute-start | bytes 221192 | tf_op jit(solution)/shard_map/ppermute | solution.py:28
  127.0 3.5 %image_attention.3 = (f32[1024,256]{1,0:T(8,128)S(1)}, f32[1024,128]{1,0:T(8,128)S(1)}) custom-call(bf16[2,384,128]{2,1,0:T(8,128)(2,1)S(1)} %get-tuple-element.143.refs_0_, bf16[2,384,128]{2,1,0:T(8,128)(2,1)S(1)} %get-tuple-element.144.refs_1_, bf16[2,384,128]{2,1,0:T(8,128)(2,1)S(1)} %collective-permute-done.13.refs_2_, ...), custom_call_target="tpu_custom_call" | custom-call | flops 1073741824 | bytes 2359296 | tf_op jit(solution)/shard_map/image_attention/pallas_call | solution.py:406
  130.6 1.0 collective-permute-done.29
  131.6 1.7 %collective-permute-done.28 = bf16[1,144,256]{2,1,0:T(8,128)(2,1)S(1)} collective-permute-done((bf16[1,144,256]{2,1,0:T(8,128)(2,1)S(1)}, bf16[1,144,256]{2,1,0:T(8,128)(2,1)S(1)}, u32[]{:S(2)}, u32[]{:S(2)}) %collective-permute-start.28) | collective-permute-done | bytes 73760 | tf_op jit(solution)/shard_map/ppermute | solution.py:28
  133.2 0.7 combine.1
  134.1 1.2 collective-permute-done.30.refs_14_
  135.3 1.6 finish.1
  136.9 22.6 %all_to_all.10.blocks_ref = bf16[16,160,128]{2,1,0:T(8,128)(2,1)S(1)} all-to-all(bf16[16,160,128]{2,1,0:T(8,128)(2,1)S(1)} %finish.1), channel_id=1, replica_groups=mesh['dp'=2,'seq'=16] {'seq'}, dimensions={0} | all-to-all | bytes 1310720 | tf_op jit(solution)/shard_map/all_to_all | solution.py:532
  159.5 1.0 unpack.1
  (65 shorter events, 1.5 us)
Async XLA Ops:
  2.9 1.0 copy-start.3
  3.9 2.1 %copy-start.2 = (bf16[1,256,1184]{1,2,0:T(8,128)(2,1)S(1)}, bf16[1,256,1184]{1,2,0:T(8,128)(2,1)}, u32[]{:S(2)}) copy-start(bf16[1,256,1184]{1,2,0:T(8,128)(2,1)} %param.10) | copy-start | bytes 1818628
  6.1 3.4 %copy-start = (bf16[1184,3584]{1,0:T(8,128)(2,1)S(1)}, bf16[1184,3584]{1,0:T(8,128)(2,1)}, u32[]{:S(2)}) copy-start(bf16[1184,3584]{1,0:T(8,128)(2,1)} %weight_ref.1) | copy-start | bytes 25460740
  9.5 4.5 %copy-start.1 = (bf16[192,4096]{1,0:T(8,128)(2,1)S(1)}, bf16[192,4096]{1,0:T(8,128)(2,1)}, u32[]{:S(2)}) copy-start(bf16[192,4096]{1,0:T(8,128)(2,1)} %refs_7_.1) | copy-start | bytes 4718596
  13.0 2.0 %collective-permute-start.2 = (bf16[8,16,1792]{2,1,0:T(8,128)(2,1)S(1)}, bf16[8,16,1792]{2,1,0:T(8,128)(2,1)S(1)}, u32[]{:S(2)}, u32[]{:S(2)}) collective-permute-start(bf16[8,16,1792]{2,1,0:T(8,128)(2,1)S(1)} %get-tuple-element.95), channel_id=1, source_target_pairs={{0,1},{1,0},{2,3},{3,2},{4,5},{5,4},{6,7},{7,6},{8,9},{9,8},{10,11... | collective-permute-start | bytes 1376264 | tf_op jit(solution)/shard_map/ppermute | solution.py:28
  13.5 14.0 %collective-permute-start.4 = (bf16[192,3584]{1,0:T(8,128)(2,1)}, bf16[192,3584]{1,0:T(8,128)(2,1)}, u32[]{:S(2)}, u32[]{:S(2)}) collective-permute-start(bf16[192,3584]{1,0:T(8,128)(2,1)} %bitcast.9.refs_5_), channel_id=1, source_target_pairs={{0,1},{1,0},{2,3},{3,2},{4,5},{5,4},{6,7},{7,6},{8,9},{9,8},{10,11... | collective-permute-start | bytes 4128776 | tf_op jit(solution)/shard_map/ppermute | solution.py:28
  13.6 5.3 %collective-permute-start = (bf16[8,16,1792]{2,1,0:T(8,128)(2,1)S(1)}, bf16[8,16,1792]{2,1,0:T(8,128)(2,1)S(1)}, u32[]{:S(2)}, u32[]{:S(2)}) collective-permute-start(bf16[8,16,1792]{2,1,0:T(8,128)(2,1)S(1)} %get-tuple-element.93), channel_id=1, source_target_pairs={{0,1},{1,0},{2,3},{3,2},{4,5},{5,4},{6,7},{7,6},{8,9},{9,8},{10,11... | collective-permute-start | bytes 1376264 | tf_op jit(solution)/shard_map/ppermute | solution.py:28
  14.0 32.6 %collective-permute-start.7 = (bf16[192,4096]{1,0:T(8,128)(2,1)S(1)}, bf16[192,4096]{1,0:T(8,128)(2,1)S(1)}, u32[]{:S(2)}, u32[]{:S(2)}) collective-permute-start(bf16[192,4096]{1,0:T(8,128)(2,1)S(1)} %copy-done.1), channel_id=1, source_target_pairs={{0,1},{1,0},{2,3},{3,2},{4,5},{5,4},{6,7},{7,6},{8,9},{9,8},{10,11... | collective-permute-start | bytes 4718600 | tf_op jit(solution)/shard_map/ppermute | solution.py:28
  14.9 6.4 %copy-start.4 = (bf16[256,2,192]{0,2,1:T(8,128)(2,1)S(1)}, bf16[256,2,192]{0,2,1:T(8,128)(2,1)}, u32[]{:S(2)}) copy-start(bf16[256,2,192]{0,2,1:T(8,128)(2,1)} %param.14) | copy-start | bytes 589828
  15.9 10.3 %collective-permute-start.3 = (bf16[4,16,1792]{2,1,0:T(8,128)(2,1)}, bf16[4,16,1792]{2,1,0:T(8,128)(2,1)}, u32[]{:S(2)}, u32[]{:S(2)}) collective-permute-start(bf16[4,16,1792]{2,1,0:T(8,128)(2,1)} %get-tuple-element.187), channel_id=1, source_target_pairs={{0,4},{1,5},{2,6},{3,7},{4,0},{5,1},{6,2},{7,3},{8,12},{9,13},{10,... | collective-permute-start | bytes 688136 | tf_op jit(solution)/shard_map/ppermute | solution.py:28
  19.9 7.7 %collective-permute-start.1 = (bf16[4,16,1792]{2,1,0:T(8,128)(2,1)}, bf16[4,16,1792]{2,1,0:T(8,128)(2,1)}, u32[]{:S(2)}, u32[]{:S(2)}) collective-permute-start(bf16[4,16,1792]{2,1,0:T(8,128)(2,1)} %get-tuple-element.188), channel_id=1, source_target_pairs={{0,2},{1,3},{2,0},{3,1},{4,6},{5,7},{6,4},{7,5},{8,10},{9,11},{10,... | collective-permute-start | bytes 688136 | tf_op jit(solution)/shard_map/ppermute | solution.py:28
  21.3 10.9 %collective-permute-start.8 = (bf16[2,192,256]{2,1,0:T(8,128)(2,1)S(1)}, bf16[2,192,256]{2,1,0:T(8,128)(2,1)S(1)}, u32[]{:S(2)}, u32[]{:S(2)}) collective-permute-start(bf16[2,192,256]{2,1,0:T(8,128)(2,1)S(1)} %bitcast.56), channel_id=1, source_target_pairs={{0,1},{1,0},{2,3},{3,2},{4,5},{5,4},{6,7},{7,6},{8,9},{9,8},{10,11... | collective-permute-start | bytes 589832 | tf_op jit(solution)/shard_map/ppermute | solution.py:28
  21.4 45.1 %all-to-all-start = ((bf16[2,4,2,384,128]{4,3,2,1,0:T(8,128)(2,1)}), bf16[2,4,2,384,128]{4,3,2,1,0:T(8,128)(2,1)}, u32[]{:S(2)}, u32[]{:S(2)}) async-start(bf16[2,4,2,384,128]{4,3,2,1,0:T(8,128)(2,1)} %pack.1), calls=%async_computation | async-start | bytes 3145728 | tf_op jit(solution)/shard_map/all_to_all | solution.py:541
  26.2 25.3 %copy-start.14 = (bf16[3584]{0:T(1024)(128)(2,1)S(1)}, bf16[3584]{0:T(1024)(128)(2,1)}, u32[]{:S(2)}) copy-start(bf16[3584]{0:T(1024)(128)(2,1)} %param.12) | copy-start | bytes 21508
  28.8 17.9 %copy-start.5 = (f32[2,16,1792]{2,1,0:T(8,128)}, f32[2,16,1792]{2,1,0:T(8,128)S(1)}, u32[]{:S(2)}) copy-start(f32[2,16,1792]{2,1,0:T(8,128)S(1)} %get-tuple-element.190) | copy-start | bytes 688132
  28.8 4.9 %collective-permute-start.6 = (bf16[2,16,1792]{2,1,0:T(8,128)(2,1)S(1)}, bf16[2,16,1792]{2,1,0:T(8,128)(2,1)S(1)}, u32[]{:S(2)}, u32[]{:S(2)}) collective-permute-start(bf16[2,16,1792]{2,1,0:T(8,128)(2,1)S(1)} %get-tuple-element.191), channel_id=1, source_target_pairs={{0,2},{1,3},{2,0},{3,1},{4,6},{5,7},{6,4},{7,5},{8,10},{9,11},{10,... | collective-permute-start | bytes 344072 | tf_op jit(solution)/shard_map/ppermute | solution.py:28
  31.6 19.2 %copy-start.7 = (f32[2,16,1792]{2,1,0:T(8,128)}, f32[2,16,1792]{2,1,0:T(8,128)S(1)}, u32[]{:S(2)}) copy-start(f32[2,16,1792]{2,1,0:T(8,128)S(1)} %get-tuple-element.193) | copy-start | bytes 688132
  31.6 15.0 %collective-permute-start.5 = (bf16[2,16,1792]{2,1,0:T(8,128)(2,1)S(1)}, bf16[2,16,1792]{2,1,0:T(8,128)(2,1)S(1)}, u32[]{:S(2)}, u32[]{:S(2)}) collective-permute-start(bf16[2,16,1792]{2,1,0:T(8,128)(2,1)S(1)} %get-tuple-element.192), channel_id=1, source_target_pairs={{0,4},{1,5},{2,6},{3,7},{4,0},{5,1},{6,2},{7,3},{8,12},{9,13},{10,... | collective-permute-start | bytes 344072 | tf_op jit(solution)/shard_map/ppermute | solution.py:28
  33.6 17.8 %copy-start.9 = (bf16[2,16,1792]{2,1,0:T(8,128)(2,1)}, bf16[2,16,1792]{2,1,0:T(8,128)(2,1)S(1)}, u32[]{:S(2)}) copy-start(bf16[2,16,1792]{2,1,0:T(8,128)(2,1)S(1)} %collective-permute-done.6) | copy-start | bytes 344068
  46.6 4.8 %copy-start.11 = (bf16[2,16,1792]{2,1,0:T(8,128)(2,1)}, bf16[2,16,1792]{2,1,0:T(8,128)(2,1)S(1)}, u32[]{:S(2)}) copy-start(bf16[2,16,1792]{2,1,0:T(8,128)(2,1)S(1)} %collective-permute-done.5) | copy-start | bytes 344068
  47.3 20.4 %collective-permute-start.10 = (bf16[1,16,1792]{2,1,0:T(8,128)(2,1)}, bf16[1,16,1792]{2,1,0:T(8,128)(2,1)}, u32[]{:S(2)}, u32[]{:S(2)}) collective-permute-start(bf16[1,16,1792]{2,1,0:T(8,128)(2,1)} %fusion.8), channel_id=1, source_target_pairs={{0,8},{1,9},{2,10},{3,11},{4,12},{5,13},{6,14},{7,15},{8,0},{9,1},... | collective-permute-start | bytes 172040 | tf_op jit(solution)/shard_map/ppermute | solution.py:28
  51.4 17.5 %collective-permute-start.9 = (bf16[1,16,1792]{2,1,0:T(8,128)(2,1)}, bf16[1,16,1792]{2,1,0:T(8,128)(2,1)}, u32[]{:S(2)}, u32[]{:S(2)}) collective-permute-start(bf16[1,16,1792]{2,1,0:T(8,128)(2,1)} %fusion.9), channel_id=1, source_target_pairs={{0,8},{1,9},{2,10},{3,11},{4,12},{5,13},{6,14},{7,15},{8,0},{9,1},... | collective-permute-start | bytes 172040 | tf_op jit(solution)/shard_map/ppermute | solution.py:28
  66.5 4.0 %copy-start.6 = (f32[2,16,1792]{2,1,0:T(8,128)S(1)}, f32[2,16,1792]{2,1,0:T(8,128)}, u32[]{:S(2)}) copy-start(f32[2,16,1792]{2,1,0:T(8,128)} %copy-done.5) | copy-start | bytes 688132
  66.5 4.0 %copy-start.8 = (f32[2,16,1792]{2,1,0:T(8,128)S(1)}, f32[2,16,1792]{2,1,0:T(8,128)}, u32[]{:S(2)}) copy-start(f32[2,16,1792]{2,1,0:T(8,128)} %copy-done.7) | copy-start | bytes 688132
  66.5 4.0 %copy-start.10 = (bf16[2,16,1792]{2,1,0:T(8,128)(2,1)S(1)}, bf16[2,16,1792]{2,1,0:T(8,128)(2,1)}, u32[]{:S(2)}) copy-start(bf16[2,16,1792]{2,1,0:T(8,128)(2,1)} %copy-done.9) | copy-start | bytes 344068
  66.5 4.0 %copy-start.12 = (bf16[2,16,1792]{2,1,0:T(8,128)(2,1)S(1)}, bf16[2,16,1792]{2,1,0:T(8,128)(2,1)}, u32[]{:S(2)}) copy-start(bf16[2,16,1792]{2,1,0:T(8,128)(2,1)} %copy-done.11) | copy-start | bytes 344068
  66.5 5.1 %copy-start.13 = (f32[1792]{0:T(1024)S(1)}, f32[1792]{0:T(1024)}, u32[]{:S(2)}) copy-start(f32[1792]{0:T(1024)} %get-tuple-element.203) | copy-start | bytes 21508
  72.5 9.4 %collective-permute-start.14 = (bf16[2,384,128]{2,1,0:T(8,128)(2,1)S(1)}, bf16[2,384,128]{2,1,0:T(8,128)(2,1)S(1)}, u32[]{:S(2)}, u32[]{:S(2)}) collective-permute-start(bf16[2,384,128]{2,1,0:T(8,128)(2,1)S(1)} %get-tuple-element.109), channel_id=1, source_target_pairs={{0,4},{1,5},{2,6},{3,7},{4,0},{5,1},{6,2},{7,3},{8,12},{9,13},{10,... | collective-permute-start | bytes 589832 | tf_op jit(solution)/shard_map/ppermute | solution.py:28
  72.6 9.3 %collective-permute-start.13 = (bf16[2,384,128]{2,1,0:T(8,128)(2,1)S(1)}, bf16[2,384,128]{2,1,0:T(8,128)(2,1)S(1)}, u32[]{:S(2)}, u32[]{:S(2)}) collective-permute-start(bf16[2,384,128]{2,1,0:T(8,128)(2,1)S(1)} %get-tuple-element.108), channel_id=1, source_target_pairs={{0,2},{1,3},{2,0},{3,1},{4,6},{5,7},{6,4},{7,5},{8,10},{9,11},{10,... | collective-permute-start | bytes 589832 | tf_op jit(solution)/shard_map/ppermute | solution.py:28
  73.2 5.9 %collective-permute-start.11 = (bf16[16,1792]{1,0:T(8,128)(2,1)S(1)}, bf16[16,1792]{1,0:T(8,128)(2,1)S(1)}, u32[]{:S(2)}, u32[]{:S(2)}) collective-permute-start(bf16[16,1792]{1,0:T(8,128)(2,1)S(1)} %get-tuple-element.106), channel_id=1, source_target_pairs={{0,8},{1,9},{2,10},{3,11},{4,12},{5,13},{6,14},{7,15},{8,0},{9,1},... | collective-permute-start | bytes 172040 | tf_op jit(solution)/shard_map/ppermute | solution.py:28
  74.0 7.6 %collective-permute-start.12 = (bf16[16,1792]{1,0:T(8,128)(2,1)S(1)}, bf16[16,1792]{1,0:T(8,128)(2,1)S(1)}, u32[]{:S(2)}, u32[]{:S(2)}) collective-permute-start(bf16[16,1792]{1,0:T(8,128)(2,1)S(1)} %get-tuple-element.107), channel_id=1, source_target_pairs={{0,8},{1,9},{2,10},{3,11},{4,12},{5,13},{6,14},{7,15},{8,0},{9,1},... | collective-permute-start | bytes 172040 | tf_op jit(solution)/shard_map/ppermute | solution.py:28
  82.0 8.3 %collective-permute-start.18 = (bf16[2,384,128]{2,1,0:T(8,128)(2,1)S(1)}, bf16[2,384,128]{2,1,0:T(8,128)(2,1)S(1)}, u32[]{:S(2)}, u32[]{:S(2)}) collective-permute-start(bf16[2,384,128]{2,1,0:T(8,128)(2,1)S(1)} %get-tuple-element.120), channel_id=1, source_target_pairs={{0,4},{1,5},{2,6},{3,7},{4,0},{5,1},{6,2},{7,3},{8,12},{9,13},{10,... | collective-permute-start | bytes 589832 | tf_op jit(solution)/shard_map/ppermute | solution.py:28
  82.0 8.2 %collective-permute-start.17 = (bf16[2,384,128]{2,1,0:T(8,128)(2,1)S(1)}, bf16[2,384,128]{2,1,0:T(8,128)(2,1)S(1)}, u32[]{:S(2)}, u32[]{:S(2)}) collective-permute-start(bf16[2,384,128]{2,1,0:T(8,128)(2,1)S(1)} %get-tuple-element.119), channel_id=1, source_target_pairs={{0,2},{1,3},{2,0},{3,1},{4,6},{5,7},{6,4},{7,5},{8,10},{9,11},{10,... | collective-permute-start | bytes 589832 | tf_op jit(solution)/shard_map/ppermute | solution.py:28
  83.2 6.7 %collective-permute-start.15 = (bf16[32,1792]{1,0:T(8,128)(2,1)S(1)}, bf16[32,1792]{1,0:T(8,128)(2,1)S(1)}, u32[]{:S(2)}, u32[]{:S(2)}) collective-permute-start(bf16[32,1792]{1,0:T(8,128)(2,1)S(1)} %pad_maximum_fusion.2), channel_id=1, source_target_pairs={{0,4},{1,5},{2,6},{3,7},{4,0},{5,1},{6,2},{7,3},{8,12},{9,13},{10,... | collective-permute-start | bytes 344072 | tf_op jit(solution)/shard_map/ppermute | solution.py:28
  85.2 5.0 %collective-permute-start.16 = (bf16[32,1792]{1,0:T(8,128)(2,1)S(1)}, bf16[32,1792]{1,0:T(8,128)(2,1)S(1)}, u32[]{:S(2)}, u32[]{:S(2)}) collective-permute-start(bf16[32,1792]{1,0:T(8,128)(2,1)S(1)} %pad_maximum_fusion.3), channel_id=1, source_target_pairs={{0,2},{1,3},{2,0},{3,1},{4,6},{5,7},{6,4},{7,5},{8,10},{9,11},{10,... | collective-permute-start | bytes 344072 | tf_op jit(solution)/shard_map/ppermute | solution.py:28
  90.3 13.3 %collective-permute-start.19 = (bf16[64,1792]{1,0:T(8,128)(2,1)S(1)}, bf16[64,1792]{1,0:T(8,128)(2,1)S(1)}, u32[]{:S(2)}, u32[]{:S(2)}) collective-permute-start(bf16[64,1792]{1,0:T(8,128)(2,1)S(1)} %pad_maximum_fusion.refs_0_), channel_id=1, source_target_pairs={{0,2},{1,3},{2,0},{3,1},{4,6},{5,7},{6,4},{7,5},{8,10},{9,11},{10,... | collective-permute-start | bytes 688136 | tf_op jit(solution)/shard_map/ppermute | solution.py:28
  91.6 12.0 %collective-permute-start.20 = (bf16[64,1792]{1,0:T(8,128)(2,1)S(1)}, bf16[64,1792]{1,0:T(8,128)(2,1)S(1)}, u32[]{:S(2)}, u32[]{:S(2)}) collective-permute-start(bf16[64,1792]{1,0:T(8,128)(2,1)S(1)} %pad_maximum_fusion.1.refs_2_), channel_id=1, source_target_pairs={{0,4},{1,5},{2,6},{3,7},{4,0},{5,1},{6,2},{7,3},{8,12},{9,13},{10,... | collective-permute-start | bytes 688136 | tf_op jit(solution)/shard_map/ppermute | solution.py:28
  93.3 10.3 %collective-permute-start.21 = (bf16[2,384,128]{2,1,0:T(8,128)(2,1)S(1)}, bf16[2,384,128]{2,1,0:T(8,128)(2,1)S(1)}, u32[]{:S(2)}, u32[]{:S(2)}) collective-permute-start(bf16[2,384,128]{2,1,0:T(8,128)(2,1)S(1)} %get-tuple-element.127), channel_id=1, source_target_pairs={{0,6},{1,7},{2,4},{3,5},{4,2},{5,3},{6,0},{7,1},{8,14},{9,15},{10,... | collective-permute-start | bytes 589832 | tf_op jit(solution)/shard_map/ppermute | solution.py:28
  93.8 13.4 %collective-permute-start.22 = (bf16[2,384,128]{2,1,0:T(8,128)(2,1)S(1)}, bf16[2,384,128]{2,1,0:T(8,128)(2,1)S(1)}, u32[]{:S(2)}, u32[]{:S(2)}) collective-permute-start(bf16[2,384,128]{2,1,0:T(8,128)(2,1)S(1)} %get-tuple-element.142), channel_id=1, source_target_pairs={{0,6},{1,7},{2,4},{3,5},{4,2},{5,3},{6,0},{7,1},{8,14},{9,15},{10,... | collective-permute-start | bytes 589832 | tf_op jit(solution)/shard_map/ppermute | solution.py:28
  107.3 10.3 %collective-permute-start.25 = (bf16[8,384,128]{2,1,0:T(8,128)(2,1)S(1)}, bf16[8,384,128]{2,1,0:T(8,128)(2,1)S(1)}, u32[]{:S(2)}, u32[]{:S(2)}) collective-permute-start(bf16[8,384,128]{2,1,0:T(8,128)(2,1)S(1)} %gather_other.1), channel_id=1, source_target_pairs={{0,1},{1,0},{2,3},{3,2},{4,5},{5,4},{6,7},{7,6},{8,9},{9,8},{10,11... | collective-permute-start | bytes 2359304 | tf_op jit(solution)/shard_map/ppermute | solution.py:28
  107.3 9.4 %collective-permute-start.23 = (bf16[4,144,256]{2,1,0:T(8,128)(2,1)S(1)}, bf16[4,144,256]{2,1,0:T(8,128)(2,1)S(1)}, u32[]{:S(2)}, u32[]{:S(2)}) collective-permute-start(bf16[4,144,256]{2,1,0:T(8,128)(2,1)S(1)} %get-tuple-element.152), channel_id=1, source_target_pairs={{0,2},{1,3},{2,0},{3,1},{4,6},{5,7},{6,4},{7,5},{8,10},{9,11},{10,... | collective-permute-start | bytes 884744 | tf_op jit(solution)/shard_map/ppermute | solution.py:28
  108.5 9.1 %collective-permute-start.24 = (bf16[4,144,256]{2,1,0:T(8,128)(2,1)S(1)}, bf16[4,144,256]{2,1,0:T(8,128)(2,1)S(1)}, u32[]{:S(2)}, u32[]{:S(2)}) collective-permute-start(bf16[4,144,256]{2,1,0:T(8,128)(2,1)S(1)} %get-tuple-element.153), channel_id=1, source_target_pairs={{0,4},{1,5},{2,6},{3,7},{4,0},{5,1},{6,2},{7,3},{8,12},{9,13},{10,... | collective-permute-start | bytes 884744 | tf_op jit(solution)/shard_map/ppermute | solution.py:28
  117.6 5.5 %collective-permute-start.27 = (bf16[2,144,256]{2,1,0:T(8,128)(2,1)S(1)}, bf16[2,144,256]{2,1,0:T(8,128)(2,1)S(1)}, u32[]{:S(2)}, u32[]{:S(2)}) collective-permute-start(bf16[2,144,256]{2,1,0:T(8,128)(2,1)S(1)} %get-tuple-element.195), channel_id=1, source_target_pairs={{0,2},{1,3},{2,0},{3,1},{4,6},{5,7},{6,4},{7,5},{8,10},{9,11},{10,... | collective-permute-start | bytes 442376 | tf_op jit(solution)/shard_map/ppermute | solution.py:28
  118.7 5.2 %collective-permute-start.26 = (bf16[2,144,256]{2,1,0:T(8,128)(2,1)S(1)}, bf16[2,144,256]{2,1,0:T(8,128)(2,1)S(1)}, u32[]{:S(2)}, u32[]{:S(2)}) collective-permute-start(bf16[2,144,256]{2,1,0:T(8,128)(2,1)S(1)} %get-tuple-element.196), channel_id=1, source_target_pairs={{0,4},{1,5},{2,6},{3,7},{4,0},{5,1},{6,2},{7,3},{8,12},{9,13},{10,... | collective-permute-start | bytes 442376 | tf_op jit(solution)/shard_map/ppermute | solution.py:28
  124.0 7.6 %collective-permute-start.29 = (bf16[1,144,256]{2,1,0:T(8,128)(2,1)S(1)}, bf16[1,144,256]{2,1,0:T(8,128)(2,1)S(1)}, u32[]{:S(2)}, u32[]{:S(2)}) collective-permute-start(bf16[1,144,256]{2,1,0:T(8,128)(2,1)S(1)} %get-tuple-element.199), channel_id=1, source_target_pairs={{0,8},{1,9},{2,10},{3,11},{4,12},{5,13},{6,14},{7,15},{8,0},{9,1},... | collective-permute-start | bytes 221192 | tf_op jit(solution)/shard_map/ppermute | solution.py:28
  126.8 6.4 %collective-permute-start.28 = (bf16[1,144,256]{2,1,0:T(8,128)(2,1)S(1)}, bf16[1,144,256]{2,1,0:T(8,128)(2,1)S(1)}, u32[]{:S(2)}, u32[]{:S(2)}) collective-permute-start(bf16[1,144,256]{2,1,0:T(8,128)(2,1)S(1)} %get-tuple-element.201), channel_id=1, source_target_pairs={{0,8},{1,9},{2,10},{3,11},{4,12},{5,13},{6,14},{7,15},{8,0},{9,1},... | collective-permute-start | bytes 221192 | tf_op jit(solution)/shard_map/ppermute | solution.py:28
  134.0 1.3 collective-permute-start.30

commit v10 on v7

--- a/solution.py
+++ b/solution.py
@@ -279,31 +279,25 @@
     )(place, *parts)
 
 
-def pack_kernel(copies, queries_ref, keys_ref, values_ref, out_ref):
-    img_dev = keys_ref.shape[0]
-    part_rows = img_dev // copies
+def pack_kernel(copies, rows_ref, out_ref):
+    count = out_ref.shape[1]
     for device in range(out_ref.shape[0]):
         head, copy = device // copies, device % copies
         span = slice(head * HEAD_DIM, (head + 1) * HEAD_DIM)
-        out_ref[device, :img_dev, :] = keys_ref[:, span]
-        out_ref[device, img_dev : 2 * img_dev, :] = values_ref[:, span]
-        out_ref[device, 2 * img_dev :, :] = queries_ref[copy * part_rows : (copy + 1) * part_rows, span]
-
-
-def pack(copies, queries, keys, values):
-    img_dev = keys.shape[0]
-    rows = 2 * img_dev + img_dev // copies
+        start = copy * count if count < rows_ref.shape[0] else 0
+        out_ref[device] = rows_ref[start : start + count, span]
+
+
+def pack(copies, rows, count):
     return pl.pallas_call(
         functools.partial(pack_kernel, copies),
-        out_shape=jax.ShapeDtypeStruct((HEADS * copies, rows, HEAD_DIM), jnp.bfloat16),
-        in_specs=[VMEM_SPEC] * 3,
+        out_shape=jax.ShapeDtypeStruct((HEADS * copies, count, HEAD_DIM), jnp.bfloat16),
+        in_specs=[VMEM_SPEC],
         out_specs=VMEM_SPEC,
         compiler_params=params(8),
-        cost_estimate=pl.CostEstimate(
-            flops=0, bytes_accessed=4 * HEADS * copies * rows * HEAD_DIM, transcendentals=0
-        ),
+        cost_estimate=pl.CostEstimate(flops=0, bytes_accessed=4 * rows.size, transcendentals=0),
         name="pack",
-    )(queries, keys, values)
+    )(rows)
 
 
 def unpack_kernel(copies, part_rows, blocks_ref, attended_ref, text_ref):
@@ -336,83 +330,75 @@
     )(blocks)
 
 
-def image_kernel(factor, call, img_dev, packed_ref, sum_ref, norm_ref, keys_ref, values_ref):
-    devices = packed_ref.shape[0]
-    part_rows = packed_ref.shape[1] - 2 * img_dev
-    for device in range(devices):
-        rows = slice(device * img_dev, (device + 1) * img_dev)
-        keys_ref[rows, :] = packed_ref[device, :img_dev, :]
-        values_ref[rows, :] = packed_ref[device, img_dev : 2 * img_dev, :]
-    group = max(1, 256 // part_rows)
-    rows = group * part_rows
+def image_kernel(factor, call, queries_ref, keys_ref, values_ref, sum_ref, top_ref, wide_ref):
+    wide_ref[:, :HEAD_DIM] = values_ref[...]
+    wide_ref[:, HEAD_DIM:] = jnp.ones(values_ref.shape, values_ref.dtype)
+    rows = 256
     contract = (((1,), (1,)), ((), ()))
-    steps = sum_ref.shape[0] // rows
-    for step in range(steps):
-        at = (call * steps + step) * group
-        span = slice(step * rows, (step + 1) * rows)
-        queries = packed_ref[at : at + group, 2 * img_dev :, :].reshape(rows, HEAD_DIM)
+    count = sum_ref.shape[0]
+    for start in range(0, count, rows):
+        span = slice(start, start + rows)
+        queries = queries_ref[call * count + start : call * count + start + rows, :]
         scores = lax.dot_general(queries, keys_ref[...], contract, preferred_element_type=jnp.float32)
         scores = scores * factor
         top = jnp.max(scores, 1, keepdims=True)
-        weights = jnp.exp2(scores - top)
-        total = jnp.sum(weights, 1, keepdims=True)
-        sum_ref[span, :] = jnp.dot(
-            weights.astype(jnp.bfloat16), values_ref[...], preferred_element_type=jnp.float32
-        )
-        lane = lax.broadcasted_iota(jnp.int32, (rows, 128), 1)
-        norm_ref[span, :] = jnp.where(lane < 64, top, total)
-
-
-def image_attention(packed, img_dev, factor, call, calls):
-    devices = packed.shape[0]
-    keys = devices * img_dev
-    count = devices * (packed.shape[1] - 2 * img_dev) // calls
-    out = jax.ShapeDtypeStruct((count, HEAD_DIM), jnp.float32)
-    return pl.pallas_call(
-        functools.partial(image_kernel, factor, call, img_dev),
-        out_shape=(out, out),
-        in_specs=[VMEM_SPEC],
+        weights = jnp.exp2(scores - top).astype(jnp.bfloat16)
+        sum_ref[span, :] = jnp.dot(weights, wide_ref[...], preferred_element_type=jnp.float32)
+        top_ref[span, :] = jnp.broadcast_to(top, (rows, HEAD_DIM))
+
+
+def image_attention(queries, keys, values, factor, call, calls):
+    count = queries.shape[0] // calls
+    total = keys.shape[0]
+    return pl.pallas_call(
+        functools.partial(image_kernel, factor, call),
+        out_shape=(
+            jax.ShapeDtypeStruct((count, 2 * HEAD_DIM), jnp.float32),
+            jax.ShapeDtypeStruct((count, HEAD_DIM), jnp.float32),
+        ),
+        in_specs=[VMEM_SPEC] * 3,
         out_specs=(VMEM_SPEC, VMEM_SPEC),
-        scratch_shapes=[pltpu.VMEM((keys, HEAD_DIM), jnp.bfloat16)] * 2,
+        scratch_shapes=[pltpu.VMEM((total, 2 * HEAD_DIM), jnp.bfloat16)],
         compiler_params=params(24),
         cost_estimate=pl.CostEstimate(
-            flops=4 * count * keys * HEAD_DIM,
-            bytes_accessed=4 * keys * HEAD_DIM + 10 * count * HEAD_DIM,
-            transcendentals=count * keys,
+            flops=4 * count * total * HEAD_DIM,
+            bytes_accessed=4 * total * HEAD_DIM + 10 * count * HEAD_DIM,
+            transcendentals=count * total,
         ),
         name="image_attention",
-    )(packed)
-
-
-def finish_kernel(factor, calls, img_dev, place_ref, packed_ref, *refs):
+    )(queries, keys, values)
+
+
+def finish_kernel(factor, calls, place_ref, queries_ref, *refs):
     images, (mine_ref, got_ref, out_ref) = refs[: 2 * calls], refs[2 * calls :]
     core, valid = place_ref[2], place_ref[4]
-    devices, part_rows = packed_ref.shape[0], packed_ref.shape[1] - 2 * img_dev
+    devices = out_ref.shape[0]
+    part_rows = queries_ref.shape[0] // devices
     half = mine_ref.shape[0]
     contract = (((1,), (1,)), ((), ()))
     mine, got = mine_ref[...], got_ref[...]
     keys = jnp.concatenate([mine[:, :HEAD_DIM], got[:, :HEAD_DIM]], 0)
     values = jnp.concatenate([mine[:, HEAD_DIM:], got[:, HEAD_DIM:]], 0)
+    values = jnp.concatenate([values, jnp.ones(values.shape, values.dtype)], 1)
     lane = lax.broadcasted_iota(jnp.int32, (1, 2 * half), 1)
     text_position = jnp.where((lane >= half) == (core == 0), half, 0) + lane % half
+    bias = jnp.where(text_position < valid, 0.0, -jnp.inf)
     group = max(1, 512 // part_rows)
     rows = group * part_rows
     each = devices // group // calls
     for step in range(devices // group):
-        sum_ref, norm_ref = images[2 * (step // each)], images[2 * (step // each) + 1]
+        sum_ref, top_ref = images[2 * (step // each)], images[2 * (step // each) + 1]
         span = slice(step % each * rows, (step % each + 1) * rows)
-        queries = packed_ref[step * group : (step + 1) * group, 2 * img_dev :, :]
-        queries = queries.reshape(rows, HEAD_DIM)
-        scores = lax.dot_general(queries, keys, contract, preferred_element_type=jnp.float32) * factor
-        scores = jnp.where(text_position < valid, scores, -jnp.inf)
-        before = norm_ref[span, 0:1]
+        queries = queries_ref[step * rows : (step + 1) * rows, :]
+        scores = lax.dot_general(queries, keys, contract, preferred_element_type=jnp.float32)
+        scores = scores * factor + bias
+        before = top_ref[span, :]
         top = jnp.maximum(before, jnp.max(scores, 1, keepdims=True))
         rescale = jnp.exp2(before - top)
-        weights = jnp.exp2(scores - top)
-        total = norm_ref[span, 64:65] * rescale + jnp.sum(weights, 1, keepdims=True)
-        mixed = sum_ref[span, :] * rescale + jnp.dot(
-            weights.astype(jnp.bfloat16), values, preferred_element_type=jnp.float32
-        )
+        weights = jnp.exp2(scores - jnp.concatenate([top] * (2 * half // HEAD_DIM), 1))
+        total = jnp.dot(weights.astype(jnp.bfloat16), values, preferred_element_type=jnp.float32)
+        mixed = sum_ref[span, :HEAD_DIM] * rescale + total[:, :HEAD_DIM]
+        total = sum_ref[span, HEAD_DIM:] * rescale + total[:, HEAD_DIM:]
         mixed = (mixed / total).astype(out_ref.dtype)
         out_ref[step * group : (step + 1) * group, :part_rows, :] = mixed.reshape(group, part_rows, HEAD_DIM)
     low = jnp.where(core == 0, mine.astype(jnp.float32), got.astype(jnp.float32))
@@ -426,12 +412,12 @@
         out_ref[device, part_rows:, :] = block.astype(out_ref.dtype)
 
 
-def finish(place, packed, images, mine, got, img_dev, factor):
-    devices, part_rows = packed.shape[0], packed.shape[1] - 2 * img_dev
+def finish(place, devices, queries, images, mine, got, factor):
+    count = queries.shape[0]
+    part_rows = count // devices
     share = 2 * mine.shape[0] // devices
-    count = devices * part_rows
-    return pl.pallas_call(
-        functools.partial(finish_kernel, factor, len(images) // 2, img_dev),
+    return pl.pallas_call(
+        functools.partial(finish_kernel, factor, len(images) // 2),
         out_shape=jax.ShapeDtypeStruct((devices, part_rows + 2 * share, HEAD_DIM), jnp.bfloat16),
         in_specs=[SMEM_SPEC] + [VMEM_SPEC] * (len(images) + 3),
         out_specs=VMEM_SPEC,
@@ -442,7 +428,7 @@
             transcendentals=count * 2 * mine.shape[0],
         ),
         name="finish",
-    )(place, packed, *images, mine, got)
+    )(place, queries, *images, mine, got)
 
 
 def add(one, other, dtype):
@@ -485,23 +471,23 @@
     def exchange(rows):
         return lax.all_to_all(rows, "seq", split_axis=0, concat_axis=0, tiled=True)
 
-    image_key_values, image_queries = tie((image_key_values, image_queries))
-    packed = pack(copies, image_queries[0], image_key_values[0, :, 0], image_key_values[0, :, 1])
-    act, packed = tie((enc_act[0].T, packed))
-    packed = exchange(packed)
+    act, queries = tie((enc_act[0].T, pack(copies, image_queries[0], part_rows)))
+    queries = exchange(queries)
     keep, sent = [], []
     encoded = encoder(lanes, place, act, down_weight)
     for own, other in (encoded[:2], encoded[2:]):
         got = swap(other, 1)
         sent.append(add(own[chips // 2 :], got[chips // 2 :], jnp.bfloat16))
         keep.append(add(own[: chips // 2], got[: chips // 2], jnp.float32))
+    sent, queries, image_key_values = tie((sent, queries, image_key_values))
+    keys = exchange(pack(copies, image_key_values[0, :, 0], img_dev))
     for step in range(rounds):
         got = [swap(part, 2 * order[step]) for part, order in zip(sent, lanes)]
         if step == 0:
-            got, win1, kv1, mod1, packed = tie((got, win1, kv1, mod1, packed))
+            got, win1, kv1, mod1 = tie((got, win1, kv1, mod1))
             lines = modulation(time, mod0, mod1)
         if step == 1:
-            got, lines = tie((got, lines))
+            got, lines, keys = tie((got, lines, keys))
         half = keep[0].shape[0] // 2
         if half:
             sent = [add(mine[half:], part[half:], jnp.bfloat16) for mine, part in zip(keep, got)]
@@ -520,23 +506,23 @@
 
     for step in reversed(range(rounds)):
         if step == 0:
-            states, packed = tie((states, packed))
-            image = image_attention(packed, img_dev, factor, 0, 2)
+            states, image_key_values = tie((states, image_key_values))
+            values = exchange(pack(copies, image_key_values[0, :, 1], img_dev))
         got = [swap(state, 2 * order[step]) for state, order in zip(states, lanes)]
         if step:
             states = [jnp.concatenate(pair, 0) for pair in zip(states, got)]
-    got, image = tie((got, image))
-    images += image
     states = [state for pair in zip(states, got) for state in pair]
 
     blocks = project(lanes, place, states, lines, win0, win1, kv0, kv1)
     keep, sent = [blocks[0], blocks[2]], [blocks[1], blocks[3]]
     for step in range(rounds):
-        if step == 0:
-            sent, packed = tie((sent, packed))
-            image = image_attention(packed, img_dev, factor, 1, 2)
         got = [swap(part, 2 * order[step]) for part, order in zip(sent, lanes)]
         if step == 0:
+            got, values = tie((got, values))
+            queries, keys, values = [part.reshape(-1, HEAD_DIM) for part in (queries, keys, values)]
+        elif step <= 2:
+            sent, queries = tie((sent, queries))
+            image = image_attention(queries, keys, values, factor, step - 1, 2)
             got, image = tie((got, image))
             images += image
         half = keep[0].shape[0] // 2
@@ -548,7 +534,7 @@
     mine, sent = combine(place, parts, chips, text_len // 2, model_width)
     got = swap(sent, 1)
 
-    back = exchange(finish(place, packed, images, mine, got, img_dev, factor))
+    back = exchange(finish(place, devices, queries, images, mine, got, factor))
     attended, text_kv = unpack(copies, part_rows, back)
     return (attended[None], text_kv)
 

time: 139 us -> 169 us (1.22)
  other arithmetic: 4.91 us -> 17 us
  starting transfers between devices: 33.1 us -> 39.8 us
  Pallas kernels: 20.5 us -> 24.1 us
  waiting for transfers between devices: 45.1 us -> 48.6 us
  local copies, waits for them, and re-layouts: 10.7 us -> 12.5 us
    all_to_all x1 -> x3, waiting for transfers between devices: 0.01 us -> 9.69 us  [exchange(): return lax.all_to_all(rows, 'seq', split_axis=0, concat_axis=0, tiled=True)]
    all_to_all x1 -> x3, starting transfers between devices: 7.36 us -> 16 us  [exchange(): return lax.all_to_all(rows, 'seq', split_axis=0, concat_axis=0, tiled=True)]
    ppermute x24, waiting for transfers between devices: 45.1 us -> 38.9 us  [swap(): return lax.ppermute(value, 'seq', [(i, i ^ mask) for i in range(devices)])]
    convert_element_type x8 -> x5, other arithmetic: 2.3 us -> 7.15 us  [add(): return (one.astype(jnp.float32) + other.astype(jnp.float32)).astype(dtype)]
    add x2 -> x3, other arithmetic: 2.12 us -> 4.99 us  [add(): return (one.astype(jnp.float32) + other.astype(jnp.float32)).astype(dtype)]
    unnamed x30, local copies, waits for them, and re-layouts: 8.36 us -> 10.4 us
    ppermute x24, starting transfers between devices: 25.8 us -> 23.8 us  [swap(): return lax.ppermute(value, 'seq', [(i, i ^ mask) for i in range(devices)])]
    reduce_sum x2, other arithmetic: 0.28 us -> 2.15 us  [local(): square = sum((jnp.sum(part * part, 1, keepdims=True) for part in summed))]
  transfers between devices with their start and end apart: 25 -> 27, of which waited for: 20 -> 13; matrix products, arithmetic and copies ran while one was open for 3% -> 8% of each run, Pallas kernels for 8% -> 9%
where the time goes in v10:
time: 169 us; the launch traced here: 168 us
  waiting for transfers between devices  48.6 us (29%)
  starting transfers between devices  39.8 us (24%)
  Pallas kernels  24.1 us (14%)
  blocking collectives  23.6 us (14%)
  other arithmetic  17 us (10%)
  local copies, waits for them, and re-layouts  12.5 us (7%)
  between operations  2.27 us (1%)
    ppermute x24, waiting for transfers between devices, swap(): return lax.ppermute(value, 'seq', [(i, i ^ mask) for i in range(devices)])  38.9 us
    ppermute x24, starting transfers between devices, swap(): return lax.ppermute(value, 'seq', [(i, i ^ mask) for i in range(devices)])  23.8 us
    all_to_all x1, blocking collectives, exchange(): return lax.all_to_all(rows, 'seq', split_axis=0, concat_axis=0, tiled=True)  23.6 us
    all_to_all x3, starting transfers between devices, exchange(): return lax.all_to_all(rows, 'seq', split_axis=0, concat_axis=0, tiled=True)  16 us
    unnamed x30, local copies, waits for them, and re-layouts  10.4 us
    all_to_all x3, waiting for transfers between devices, exchange(): return lax.all_to_all(rows, 'seq', split_axis=0, concat_axis=0, tiled=True)  9.69 us
    pallas_call x2, Pallas kernels, image_attention(): pl.pallas_call(functools.partial(image_kernel, factor, call), out_shape=(...  9.15 us
    convert_element_type x5, other arithmetic, add(): return (one.astype(jnp.float32) + other.astype(jnp.float32)).astype(dtype)  7.15 us
  transfers between devices with their start and end apart: 27, of which 13 were waited for; matrix products, arithmetic and copies ran while one was open for 8% of the time, Pallas kernels for 9%

profile of v10, /device:TPU:0, one launch (start us, length us, event | category | flops | bytes accessed | tf_op | source)
XLA Modules:
  0.0 167.8 jit_solution(2525712931425608484)
XLA Ops:
  1.3 1.0 copy-done.6
  2.3 0.9 pack.3
  3.3 3.4 %copy-done = bf16[1184,3584]{1,0:T(8,128)(2,1)S(1)} copy-done((bf16[1184,3584]{1,0:T(8,128)(2,1)S(1)}, bf16[1184,3584]{1,0:T(8,128)(2,1)}, u32[]{:S(2)}) %copy-start) | copy-done | bytes 8486936
  6.7 1.1 copy-done.5
  7.8 4.2 %encoder.1 = (bf16[8,16,1792]{2,1,0:T(8,128)(2,1)S(1)}, bf16[8,16,1792]{2,1,0:T(8,128)(2,1)}, bf16[8,16,1792]{2,1,0:T(8,128)(2,1)S(1)}, bf16[8,16,1792]{2,1,0:T(8,128)(2,1)}) custom-call(s32[5]{0:T(128)S(1)} %stack.19.place_ref, bf16[1184,256]{1,0:T(8,128)(2,1)S(1)} %bitcast.46, bf16[1184,3584]{1,0:T(8,128)(2,1)S(1)} %copy-done), custom_call_target="tpu_custom_call" | custom-call | flops 2172649472 | bytes 10928128 | tf_op jit(solution)/shard_map/encoder/pallas_call | solution.py:89
  12.0 0.8 copy-done.7
  12.8 0.8 copy-done.9
  14.1 7.3 %all-to-all-start = ((bf16[16,128,128]{2,1,0:T(8,128)(2,1)}), bf16[16,128,128]{2,1,0:T(8,128)(2,1)S(1)}, u32[]{:S(2)}, u32[]{:S(2)}) async-start(bf16[16,128,128]{2,1,0:T(8,128)(2,1)} %pack.3), calls=%async_computation | async-start | bytes 1048576 | tf_op jit(solution)/shard_map/all_to_all | solution.py:472
  23.2 2.2 %add_convert_fusion.1 = (bf16[4,16,1792]{2,1,0:T(8,128)(2,1)}, f32[4,16,1792]{2,1,0:T(8,128)}) fusion(bf16[8,16,1792]{2,1,0:T(8,128)(2,1)} %collective-permute-done, bf16[8,16,1792]{2,1,0:T(8,128)(2,1)} %copy-done.9), kind=kLoop, calls=%fused_computation.4 | loop fusion | flops 802816 | bytes 1605632 | tf_op jit(solution)/shard_map/convert_element_type | solution.py:435
  25.4 2.0 %convert_add_fusion = (f32[4,16,1792]{2,1,0:T(8,128)}, bf16[4,16,1792]{2,1,0:T(8,128)(2,1)}) fusion(bf16[8,16,1792]{2,1,0:T(8,128)(2,1)} %collective-permute-done.1, bf16[8,16,1792]{2,1,0:T(8,128)(2,1)S(1)} %copy-done.8), kind=kLoop, calls=%fused_computation.2 | loop fusion | flops 802816 | bytes 1605632 | tf_op jit(solution)/shard_map/add | solution.py:435
  27.4 8.5 %all-to-all-done = bf16[16,128,128]{2,1,0:T(8,128)(2,1)S(1)} async-done(((bf16[16,128,128]{2,1,0:T(8,128)(2,1)}), bf16[16,128,128]{2,1,0:T(8,128)(2,1)S(1)}, u32[]{:S(2)}, u32[]{:S(2)}) %all-to-all-start) | async-done | bytes 524320 | tf_op jit(solution)/shard_map/all_to_all | solution.py:472
  36.3 2.0 %collective-permute-start.3 = (bf16[4,16,1792]{2,1,0:T(8,128)(2,1)}, bf16[4,16,1792]{2,1,0:T(8,128)(2,1)}, u32[]{:S(2)}, u32[]{:S(2)}) collective-permute-start(bf16[4,16,1792]{2,1,0:T(8,128)(2,1)} %get-tuple-element.56), channel_id=1, source_target_pairs={{0,4},{1,5},{2,6},{3,7},{4,0},{5,1},{6,2},{7,3},{8,12},{9,13},{10,... | collective-permute-start | bytes 688136 | tf_op jit(solution)/shard_map/ppermute | solution.py:28
  38.3 1.6 copy.12
  39.9 0.9 pack.4
  40.8 4.3 %all-to-all-start.1 = ((bf16[16,128,128]{2,1,0:T(8,128)(2,1)}), bf16[16,128,128]{2,1,0:T(8,128)(2,1)}, u32[]{:S(2)}, u32[]{:S(2)}) async-start(bf16[16,128,128]{2,1,0:T(8,128)(2,1)} %pack.4), calls=%async_computation.1 | async-start | bytes 1048576 | tf_op jit(solution)/shard_map/all_to_all | solution.py:472
  45.2 2.0 %fusion.1 = (bf16[2,16,1792]{2,1,0:T(8,128)(2,1)S(1)}, f32[2,16,1792]{2,1,0:T(8,128)}) fusion(f32[4,16,1792]{2,1,0:T(8,128)} %get-tuple-element.99, bf16[4,16,1792]{2,1,0:T(8,128)(2,1)} %collective-permute-done.2), kind=kLoop, calls=%fused_computation.14 | loop fusion | flops 286720 | bytes 1032192 | tf_op jit(solution)/shard_map/convert_element_type | solution.py:435
  47.1 1.9 %collective-permute-start.7 = (bf16[2,16,1792]{2,1,0:T(8,128)(2,1)S(1)}, bf16[2,16,1792]{2,1,0:T(8,128)(2,1)}, u32[]{:S(2)}, u32[]{:S(2)}) collective-permute-start(bf16[2,16,1792]{2,1,0:T(8,128)(2,1)S(1)} %get-tuple-element.102), channel_id=1, source_target_pairs={{0,4},{1,5},{2,6},{3,7},{4,0},{5,1},{6,2},{7,3},{8,12},{9,13},{10,... | collective-permute-start | bytes 344072 | tf_op jit(solution)/shard_map/ppermute | solution.py:28
  49.0 1.9 %slice_add_fusion = (f32[2,16,1792]{2,1,0:T(8,128)}, bf16[2,16,1792]{2,1,0:T(8,128)(2,1)S(1)}) fusion(f32[4,16,1792]{2,1,0:T(8,128)} %get-tuple-element.96, bf16[4,16,1792]{2,1,0:T(8,128)(2,1)} %collective-permute-done.3), kind=kLoop, calls=%fused_computation.10 | loop fusion | flops 286720 | bytes 1032192 | tf_op jit(solution)/shard_map/add | solution.py:435
  50.9 1.5 collective-permute-start.8
  52.4 1.1 modulation.1.refs_4_
  53.6 5.2 %collective-permute-done.7 = bf16[2,16,1792]{2,1,0:T(8,128)(2,1)} collective-permute-done((bf16[2,16,1792]{2,1,0:T(8,128)(2,1)S(1)}, bf16[2,16,1792]{2,1,0:T(8,128)(2,1)}, u32[]{:S(2)}, u32[]{:S(2)}) %collective-permute-start.7) | collective-permute-done | bytes 114720 | tf_op jit(solution)/shard_map/ppermute | solution.py:28
  58.8 1.2 all-to-all-done.1
  60.0 1.0 fusion.9
  61.0 1.9 %collective-permute-start.9 = (bf16[1,16,1792]{2,1,0:T(8,128)(2,1)S(1)}, bf16[1,16,1792]{2,1,0:T(8,128)(2,1)S(1)}, u32[]{:S(2)}, u32[]{:S(2)}) collective-permute-start(bf16[1,16,1792]{2,1,0:T(8,128)(2,1)S(1)} %fusion.9), channel_id=1, source_target_pairs={{0,8},{1,9},{2,10},{3,11},{4,12},{5,13},{6,14},{7,15},{8,0},{9,1},... | collective-permute-start | bytes 172040 | tf_op jit(solution)/shard_map/ppermute | solution.py:28
  62.9 0.9 fusion.6
  63.9 1.1 collective-permute-start.10
  65.0 4.0 %collective-permute-done.9 = bf16[1,16,1792]{2,1,0:T(8,128)(2,1)S(1)} collective-permute-done((bf16[1,16,1792]{2,1,0:T(8,128)(2,1)S(1)}, bf16[1,16,1792]{2,1,0:T(8,128)(2,1)S(1)}, u32[]{:S(2)}, u32[]{:S(2)}) %collective-permute-start.9) | collective-permute-done | bytes 57376 | tf_op jit(solution)/shard_map/ppermute | solution.py:28
  68.9 1.1 multiply_reduce_fusion.1
  70.0 1.1 multiply_reduce_fusion
  71.1 1.1 multiply_convert_fusion
  72.4 2.8 %collective-permute-start.13 = (bf16[16,1792]{1,0:T(8,128)(2,1)S(1)}, bf16[16,1792]{1,0:T(8,128)(2,1)S(1)}, u32[]{:S(2)}, u32[]{:S(2)}) collective-permute-start(bf16[16,1792]{1,0:T(8,128)(2,1)S(1)} %get-tuple-element.114), channel_id=1, source_target_pairs={{0,8},{1,9},{2,10},{3,11},{4,12},{5,13},{6,14},{7,15},{8,0},{9,1},... | collective-permute-start | bytes 172040 | tf_op jit(solution)/shard_map/ppermute | solution.py:28
  75.2 3.5 %collective-permute-done.11 = bf16[16,1792]{1,0:T(8,128)(2,1)S(1)} collective-permute-done((bf16[16,1792]{1,0:T(8,128)(2,1)S(1)}, bf16[16,1792]{1,0:T(8,128)(2,1)S(1)}, u32[]{:S(2)}, u32[]{:S(2)}) %collective-permute-start.11) | collective-permute-done | bytes 57376 | tf_op jit(solution)/shard_map/ppermute | solution.py:28
  78.8 0.8 collective-permute-done.13
  79.6 0.7 collective-permute-start.14
  80.3 3.3 %collective-permute-done.12 = bf16[32,1792]{1,0:T(8,128)(2,1)S(1)} collective-permute-done((bf16[32,1792]{1,0:T(8,128)(2,1)S(1)}, bf16[32,1792]{1,0:T(8,128)(2,1)S(1)}, u32[]{:S(2)}, u32[]{:S(2)}) %collective-permute-start.12) | collective-permute-done | bytes 114720 | tf_op jit(solution)/shard_map/ppermute | solution.py:28
  83.6 0.7 pad_maximum_fusion.refs_0_
  84.4 0.7 pad_maximum_fusion.1.refs_2_
  85.5 0.9 pack.5
  86.4 4.4 %all-to-all-start.2 = ((bf16[16,128,128]{2,1,0:T(8,128)(2,1)}), bf16[16,128,128]{2,1,0:T(8,128)(2,1)}, u32[]{:S(2)}, u32[]{:S(2)}) async-start(bf16[16,128,128]{2,1,0:T(8,128)(2,1)} %pack.5), calls=%async_computation.2 | async-start | bytes 1048576 | tf_op jit(solution)/shard_map/all_to_all | solution.py:472
  90.9 1.8 %collective-permute-start.15 = (bf16[64,1792]{1,0:T(8,128)(2,1)}, bf16[64,1792]{1,0:T(8,128)(2,1)S(1)}, u32[]{:S(2)}, u32[]{:S(2)}) collective-permute-start(bf16[64,1792]{1,0:T(8,128)(2,1)} %pad_maximum_fusion.refs_0_), channel_id=1, source_target_pairs={{0,2},{1,3},{2,0},{3,1},{4,6},{5,7},{6,4},{7,5},{8,10},{9,11},{10,... | collective-permute-start | bytes 688136 | tf_op jit(solution)/shard_map/ppermute | solution.py:28
  92.6 1.5 collective-permute-start.16
  94.1 9.0 %collective-permute-done.15.refs_1_ = bf16[64,1792]{1,0:T(8,128)(2,1)S(1)} collective-permute-done((bf16[64,1792]{1,0:T(8,128)(2,1)}, bf16[64,1792]{1,0:T(8,128)(2,1)S(1)}, u32[]{:S(2)}, u32[]{:S(2)}) %collective-permute-start.15) | collective-permute-done | bytes 229408 | tf_op jit(solution)/shard_map/ppermute | solution.py:28
  103.1 4.0 %collective-permute-done.16.refs_3_ = bf16[64,1792]{1,0:T(8,128)(2,1)S(1)} collective-permute-done((bf16[64,1792]{1,0:T(8,128)(2,1)}, bf16[64,1792]{1,0:T(8,128)(2,1)S(1)}, u32[]{:S(2)}, u32[]{:S(2)}) %collective-permute-start.16) | collective-permute-done | bytes 229408 | tf_op jit(solution)/shard_map/ppermute | solution.py:28
  107.1 0.9 copy-done.3
  108.0 0.9 copy-done.4
  109.0 3.7 %project.1 = (bf16[4,144,256]{2,1,0:T(8,128)(2,1)S(1)}, bf16[4,144,256]{2,1,0:T(8,128)(2,1)S(1)}, bf16[4,144,256]{2,1,0:T(8,128)(2,1)S(1)}, bf16[4,144,256]{2,1,0:T(8,128)(2,1)S(1)}) custom-call(s32[5]{0:T(128)S(1)} %stack.19.place_ref, bf16[64,1792]{1,0:T(8,128)(2,1)S(1)} %copy-done.3, bf16[64,1792]{1,0:T(8,128)(2,1)S(1)} %collective-permute-done.15.refs_1_, ...), custom_call_target="tpu_custom_call" | custom-call | flops 754974720 | bytes 7864320 | tf_op jit(solution)/shard_map/project/pallas_call | solution.py:211
  112.6 0.7 copy-done.10
  113.3 0.7 copy-done.11
  114.1 1.4 collective-permute-start.17
  116.1 6.5 %collective-permute-done.17 = bf16[4,144,256]{2,1,0:T(8,128)(2,1)S(1)} collective-permute-done((bf16[4,144,256]{2,1,0:T(8,128)(2,1)S(1)}, bf16[4,144,256]{2,1,0:T(8,128)(2,1)S(1)}, u32[]{:S(2)}, u32[]{:S(2)}) %collective-permute-start.17) | collective-permute-done | bytes 294944 | tf_op jit(solution)/shard_map/ppermute | solution.py:28
  122.6 1.2 collective-permute-done.18
  123.8 1.0 add_convert_fusion.3
  124.8 0.6 collective-permute-start.19
  125.5 1.0 convert_add_fusion.2
  126.5 0.7 collective-permute-start.20
  127.3 4.6 %image_attention.2 = (f32[1024,256]{1,0:T(8,128)S(1)}, f32[1024,128]{1,0:T(8,128)S(1)}) custom-call(bf16[2048,128]{1,0:T(8,128)(2,1)S(1)} %bitcast.41, bf16[2048,128]{1,0:T(8,128)(2,1)} %bitcast.17.keys_ref, bf16[2048,128]{1,0:T(8,128)(2,1)} %bitcast.18.values_ref), custom_call_target="tpu_custom_call" | custom-call | flops 1073741824 | bytes 2359296 | tf_op jit(solution)/shard_map/image_attention/pallas_call | solution.py:353
  131.9 2.4 %collective-permute-start.21 = (bf16[1,144,256]{2,1,0:T(8,128)(2,1)S(1)}, bf16[1,144,256]{2,1,0:T(8,128)(2,1)S(1)}, u32[]{:S(2)}, u32[]{:S(2)}) collective-permute-start(bf16[1,144,256]{2,1,0:T(8,128)(2,1)S(1)} %get-tuple-element.111), channel_id=1, source_target_pairs={{0,8},{1,9},{2,10},{3,11},{4,12},{5,13},{6,14},{7,15},{8,0},{9,1},... | collective-permute-start | bytes 221192 | tf_op jit(solution)/shard_map/ppermute | solution.py:28
  134.3 0.7 collective-permute-start.22
  135.0 4.6 %image_attention.3 = (f32[1024,256]{1,0:T(8,128)S(1)}, f32[1024,128]{1,0:T(8,128)S(1)}) custom-call(bf16[2048,128]{1,0:T(8,128)(2,1)S(1)} %bitcast.42, bf16[2048,128]{1,0:T(8,128)(2,1)} %bitcast.17.keys_ref, bf16[2048,128]{1,0:T(8,128)(2,1)} %bitcast.18.values_ref), custom_call_target="tpu_custom_call" | custom-call | flops 1073741824 | bytes 2359296 | tf_op jit(solution)/shard_map/image_attention/pallas_call | solution.py:353
  139.6 0.7 combine.1
  140.4 1.2 collective-permute-done.23.refs_5_
  141.7 1.5 finish.1
  143.2 23.6 %all_to_all.20.blocks_ref = bf16[16,160,128]{2,1,0:T(8,128)(2,1)S(1)} all-to-all(bf16[16,160,128]{2,1,0:T(8,128)(2,1)S(1)} %finish.1), channel_id=1, replica_groups=mesh['dp'=2,'seq'=16] {'seq'}, dimensions={0} | all-to-all | bytes 1310720 | tf_op jit(solution)/shard_map/all_to_all | solution.py:472
  166.8 1.0 unpack.1
  (58 shorter events, 3.7 us)
Async XLA Ops:
  1.3 1.0 copy-start.6
  3.3 3.4 %copy-start = (bf16[1184,3584]{1,0:T(8,128)(2,1)S(1)}, bf16[1184,3584]{1,0:T(8,128)(2,1)}, u32[]{:S(2)}) copy-start(bf16[1184,3584]{1,0:T(8,128)(2,1)} %weight_ref.1) | copy-start | bytes 25460740
  6.7 1.1 copy-start.5
  7.8 13.7 %copy-start.2 = (bf16[3584,192]{0,1:T(8,128)(2,1)S(1)}, bf16[3584,192]{0,1:T(8,128)(2,1)}, u32[]{:S(2)}) copy-start(bf16[3584,192]{0,1:T(8,128)(2,1)} %param.13) | copy-start | bytes 4128772
  7.8 14.2 %copy-start.1 = (bf16[192,4096]{1,0:T(8,128)(2,1)S(1)}, bf16[192,4096]{1,0:T(8,128)(2,1)}, u32[]{:S(2)}) copy-start(bf16[192,4096]{1,0:T(8,128)(2,1)} %refs_7_.1) | copy-start | bytes 4718596
  7.8 14.7 %copy-start.14 = (bf16[3584]{0:T(1024)(128)(2,1)S(1)}, bf16[3584]{0:T(1024)(128)(2,1)}, u32[]{:S(2)}) copy-start(bf16[3584]{0:T(1024)(128)(2,1)} %param.12) | copy-start | bytes 21508
  12.0 0.8 copy-start.7
  12.8 0.8 copy-start.9
  13.6 9.5 %collective-permute-start = (bf16[8,16,1792]{2,1,0:T(8,128)(2,1)}, bf16[8,16,1792]{2,1,0:T(8,128)(2,1)}, u32[]{:S(2)}, u32[]{:S(2)}) collective-permute-start(bf16[8,16,1792]{2,1,0:T(8,128)(2,1)} %get-tuple-element.51), channel_id=1, source_target_pairs={{0,1},{1,0},{2,3},{3,2},{4,5},{5,4},{6,7},{7,6},{8,9},{9,8},{10,11... | collective-permute-start | bytes 1376264 | tf_op jit(solution)/shard_map/ppermute | solution.py:28
  14.1 11.3 %collective-permute-start.1 = (bf16[8,16,1792]{2,1,0:T(8,128)(2,1)}, bf16[8,16,1792]{2,1,0:T(8,128)(2,1)}, u32[]{:S(2)}, u32[]{:S(2)}) collective-permute-start(bf16[8,16,1792]{2,1,0:T(8,128)(2,1)} %get-tuple-element.53), channel_id=1, source_target_pairs={{0,1},{1,0},{2,3},{3,2},{4,5},{5,4},{6,7},{7,6},{8,9},{9,8},{10,11... | collective-permute-start | bytes 1376264 | tf_op jit(solution)/shard_map/ppermute | solution.py:28
  14.1 21.8 %all-to-all-start = ((bf16[16,128,128]{2,1,0:T(8,128)(2,1)}), bf16[16,128,128]{2,1,0:T(8,128)(2,1)S(1)}, u32[]{:S(2)}, u32[]{:S(2)}) async-start(bf16[16,128,128]{2,1,0:T(8,128)(2,1)} %pack.3), calls=%async_computation | async-start | bytes 1048576 | tf_op jit(solution)/shard_map/all_to_all | solution.py:472
  21.5 3.9 %copy-start.8 = (bf16[8,16,1792]{2,1,0:T(8,128)(2,1)S(1)}, bf16[8,16,1792]{2,1,0:T(8,128)(2,1)}, u32[]{:S(2)}) copy-start(bf16[8,16,1792]{2,1,0:T(8,128)(2,1)} %copy-done.7) | copy-start | bytes 1376260
  21.5 23.6 %collective-permute-start.4 = (bf16[192,3584]{1,0:T(8,128)(2,1)S(1)}, bf16[192,3584]{1,0:T(8,128)(2,1)}, u32[]{:S(2)}, u32[]{:S(2)}) collective-permute-start(bf16[192,3584]{1,0:T(8,128)(2,1)S(1)} %bitcast.44), channel_id=1, source_target_pairs={{0,1},{1,0},{2,3},{3,2},{4,5},{5,4},{6,7},{7,6},{8,9},{9,8},{10,11... | collective-permute-start | bytes 4128776 | tf_op jit(solution)/shard_map/ppermute | solution.py:28
  22.0 23.2 %collective-permute-start.5 = (bf16[192,4096]{1,0:T(8,128)(2,1)S(1)}, bf16[192,4096]{1,0:T(8,128)(2,1)}, u32[]{:S(2)}, u32[]{:S(2)}) collective-permute-start(bf16[192,4096]{1,0:T(8,128)(2,1)S(1)} %copy-done.1), channel_id=1, source_target_pairs={{0,1},{1,0},{2,3},{3,2},{4,5},{5,4},{6,7},{7,6},{8,9},{9,8},{10,11... | collective-permute-start | bytes 4718600 | tf_op jit(solution)/shard_map/ppermute | solution.py:28
  22.1 23.0 %collective-permute-start.6 = (bf16[2,192,256]{2,1,0:T(8,128)(2,1)}, bf16[2,192,256]{2,1,0:T(8,128)(2,1)}, u32[]{:S(2)}, u32[]{:S(2)}) collective-permute-start(bf16[2,192,256]{2,1,0:T(8,128)(2,1)} %bitcast.48), channel_id=1, source_target_pairs={{0,1},{1,0},{2,3},{3,2},{4,5},{5,4},{6,7},{7,6},{8,9},{9,8},{10,11... | collective-permute-start | bytes 589832 | tf_op jit(solution)/shard_map/ppermute | solution.py:28
  35.9 9.2 %collective-permute-start.2 = (bf16[4,16,1792]{2,1,0:T(8,128)(2,1)}, bf16[4,16,1792]{2,1,0:T(8,128)(2,1)}, u32[]{:S(2)}, u32[]{:S(2)}) collective-permute-start(bf16[4,16,1792]{2,1,0:T(8,128)(2,1)} %get-tuple-element.55), channel_id=1, source_target_pairs={{0,2},{1,3},{2,0},{3,1},{4,6},{5,7},{6,4},{7,5},{8,10},{9,11},{10,... | collective-permute-start | bytes 688136 | tf_op jit(solution)/shard_map/ppermute | solution.py:28
  36.3 8.8 %collective-permute-start.3 = (bf16[4,16,1792]{2,1,0:T(8,128)(2,1)}, bf16[4,16,1792]{2,1,0:T(8,128)(2,1)}, u32[]{:S(2)}, u32[]{:S(2)}) collective-permute-start(bf16[4,16,1792]{2,1,0:T(8,128)(2,1)} %get-tuple-element.56), channel_id=1, source_target_pairs={{0,4},{1,5},{2,6},{3,7},{4,0},{5,1},{6,2},{7,3},{8,12},{9,13},{10,... | collective-permute-start | bytes 688136 | tf_op jit(solution)/shard_map/ppermute | solution.py:28
  40.8 19.1 %all-to-all-start.1 = ((bf16[16,128,128]{2,1,0:T(8,128)(2,1)}), bf16[16,128,128]{2,1,0:T(8,128)(2,1)}, u32[]{:S(2)}, u32[]{:S(2)}) async-start(bf16[16,128,128]{2,1,0:T(8,128)(2,1)} %pack.4), calls=%async_computation.1 | async-start | bytes 1048576 | tf_op jit(solution)/shard_map/all_to_all | solution.py:472
  45.1 7.3 %copy-start.12 = (bf16[256,2,192]{0,2,1:T(8,128)(2,1)S(1)}, bf16[256,2,192]{0,2,1:T(8,128)(2,1)}, u32[]{:S(2)}) copy-start(bf16[256,2,192]{0,2,1:T(8,128)(2,1)} %param.14) | copy-start | bytes 589828
  47.1 11.7 %collective-permute-start.7 = (bf16[2,16,1792]{2,1,0:T(8,128)(2,1)S(1)}, bf16[2,16,1792]{2,1,0:T(8,128)(2,1)}, u32[]{:S(2)}, u32[]{:S(2)}) collective-permute-start(bf16[2,16,1792]{2,1,0:T(8,128)(2,1)S(1)} %get-tuple-element.102), channel_id=1, source_target_pairs={{0,4},{1,5},{2,6},{3,7},{4,0},{5,1},{6,2},{7,3},{8,12},{9,13},{10,... | collective-permute-start | bytes 344072 | tf_op jit(solution)/shard_map/ppermute | solution.py:28
  50.9 7.9 %collective-permute-start.8 = (bf16[2,16,1792]{2,1,0:T(8,128)(2,1)S(1)}, bf16[2,16,1792]{2,1,0:T(8,128)(2,1)}, u32[]{:S(2)}, u32[]{:S(2)}) collective-permute-start(bf16[2,16,1792]{2,1,0:T(8,128)(2,1)S(1)} %get-tuple-element.101), channel_id=1, source_target_pairs={{0,2},{1,3},{2,0},{3,1},{4,6},{5,7},{6,4},{7,5},{8,10},{9,11},{10,... | collective-permute-start | bytes 344072 | tf_op jit(solution)/shard_map/ppermute | solution.py:28
  60.0 25.1 %copy-start.13 = (bf16[1,128,2,2048]{3,2,1,0:T(2,128)(2,1)S(1)}, bf16[1,128,2,2048]{3,2,1,0:T(2,128)(2,1)}, u32[]{:S(2)}) copy-start(bf16[1,128,2,2048]{3,2,1,0:T(2,128)(2,1)} %param.19) | copy-start | bytes 3145732
  61.0 8.0 %collective-permute-start.9 = (bf16[1,16,1792]{2,1,0:T(8,128)(2,1)S(1)}, bf16[1,16,1792]{2,1,0:T(8,128)(2,1)S(1)}, u32[]{:S(2)}, u32[]{:S(2)}) collective-permute-start(bf16[1,16,1792]{2,1,0:T(8,128)(2,1)S(1)} %fusion.9), channel_id=1, source_target_pairs={{0,8},{1,9},{2,10},{3,11},{4,12},{5,13},{6,14},{7,15},{8,0},{9,1},... | collective-permute-start | bytes 172040 | tf_op jit(solution)/shard_map/ppermute | solution.py:28
  63.9 6.2 %collective-permute-start.10 = (bf16[1,16,1792]{2,1,0:T(8,128)(2,1)S(1)}, bf16[1,16,1792]{2,1,0:T(8,128)(2,1)S(1)}, u32[]{:S(2)}, u32[]{:S(2)}) collective-permute-start(bf16[1,16,1792]{2,1,0:T(8,128)(2,1)S(1)} %fusion.6), channel_id=1, source_target_pairs={{0,8},{1,9},{2,10},{3,11},{4,12},{5,13},{6,14},{7,15},{8,0},{9,1},... | collective-permute-start | bytes 172040 | tf_op jit(solution)/shard_map/ppermute | solution.py:28
  72.2 6.5 %collective-permute-start.11 = (bf16[16,1792]{1,0:T(8,128)(2,1)S(1)}, bf16[16,1792]{1,0:T(8,128)(2,1)S(1)}, u32[]{:S(2)}, u32[]{:S(2)}) collective-permute-start(bf16[16,1792]{1,0:T(8,128)(2,1)S(1)} %get-tuple-element.115), channel_id=1, source_target_pairs={{0,8},{1,9},{2,10},{3,11},{4,12},{5,13},{6,14},{7,15},{8,0},{9,1},... | collective-permute-start | bytes 172040 | tf_op jit(solution)/shard_map/ppermute | solution.py:28
  72.4 7.1 %collective-permute-start.13 = (bf16[16,1792]{1,0:T(8,128)(2,1)S(1)}, bf16[16,1792]{1,0:T(8,128)(2,1)S(1)}, u32[]{:S(2)}, u32[]{:S(2)}) collective-permute-start(bf16[16,1792]{1,0:T(8,128)(2,1)S(1)} %get-tuple-element.114), channel_id=1, source_target_pairs={{0,8},{1,9},{2,10},{3,11},{4,12},{5,13},{6,14},{7,15},{8,0},{9,1},... | collective-permute-start | bytes 172040 | tf_op jit(solution)/shard_map/ppermute | solution.py:28
  78.7 4.9 %collective-permute-start.12 = (bf16[32,1792]{1,0:T(8,128)(2,1)S(1)}, bf16[32,1792]{1,0:T(8,128)(2,1)S(1)}, u32[]{:S(2)}, u32[]{:S(2)}) collective-permute-start(bf16[32,1792]{1,0:T(8,128)(2,1)S(1)} %pad_maximum_fusion.2), channel_id=1, source_target_pairs={{0,4},{1,5},{2,6},{3,7},{4,0},{5,1},{6,2},{7,3},{8,12},{9,13},{10,... | collective-permute-start | bytes 344072 | tf_op jit(solution)/shard_map/ppermute | solution.py:28
  79.6 4.9 %collective-permute-start.14 = (bf16[32,1792]{1,0:T(8,128)(2,1)S(1)}, bf16[32,1792]{1,0:T(8,128)(2,1)S(1)}, u32[]{:S(2)}, u32[]{:S(2)}) collective-permute-start(bf16[32,1792]{1,0:T(8,128)(2,1)S(1)} %pad_maximum_fusion.3), channel_id=1, source_target_pairs={{0,2},{1,3},{2,0},{3,1},{4,6},{5,7},{6,4},{7,5},{8,10},{9,11},{10,... | collective-permute-start | bytes 344072 | tf_op jit(solution)/shard_map/ppermute | solution.py:28
  86.4 37.4 %all-to-all-start.2 = ((bf16[16,128,128]{2,1,0:T(8,128)(2,1)}), bf16[16,128,128]{2,1,0:T(8,128)(2,1)}, u32[]{:S(2)}, u32[]{:S(2)}) async-start(bf16[16,128,128]{2,1,0:T(8,128)(2,1)} %pack.5), calls=%async_computation.2 | async-start | bytes 1048576 | tf_op jit(solution)/shard_map/all_to_all | solution.py:472
  90.9 12.2 %collective-permute-start.15 = (bf16[64,1792]{1,0:T(8,128)(2,1)}, bf16[64,1792]{1,0:T(8,128)(2,1)S(1)}, u32[]{:S(2)}, u32[]{:S(2)}) collective-permute-start(bf16[64,1792]{1,0:T(8,128)(2,1)} %pad_maximum_fusion.refs_0_), channel_id=1, source_target_pairs={{0,2},{1,3},{2,0},{3,1},{4,6},{5,7},{6,4},{7,5},{8,10},{9,11},{10,... | collective-permute-start | bytes 688136 | tf_op jit(solution)/shard_map/ppermute | solution.py:28
  92.6 14.5 %collective-permute-start.16 = (bf16[64,1792]{1,0:T(8,128)(2,1)}, bf16[64,1792]{1,0:T(8,128)(2,1)S(1)}, u32[]{:S(2)}, u32[]{:S(2)}) collective-permute-start(bf16[64,1792]{1,0:T(8,128)(2,1)} %pad_maximum_fusion.1.refs_2_), channel_id=1, source_target_pairs={{0,4},{1,5},{2,6},{3,7},{4,0},{5,1},{6,2},{7,3},{8,12},{9,13},{10,... | collective-permute-start | bytes 688136 | tf_op jit(solution)/shard_map/ppermute | solution.py:28
  107.1 0.9 copy-start.3
  108.0 0.9 copy-start.4
  112.6 0.7 copy-start.10
  113.3 0.7 copy-start.11
  114.1 8.5 %collective-permute-start.17 = (bf16[4,144,256]{2,1,0:T(8,128)(2,1)S(1)}, bf16[4,144,256]{2,1,0:T(8,128)(2,1)S(1)}, u32[]{:S(2)}, u32[]{:S(2)}) collective-permute-start(bf16[4,144,256]{2,1,0:T(8,128)(2,1)S(1)} %get-tuple-element.69), channel_id=1, source_target_pairs={{0,2},{1,3},{2,0},{3,1},{4,6},{5,7},{6,4},{7,5},{8,10},{9,11},{10,... | collective-permute-start | bytes 884744 | tf_op jit(solution)/shard_map/ppermute | solution.py:28
  115.5 8.3 %collective-permute-start.18 = (bf16[4,144,256]{2,1,0:T(8,128)(2,1)S(1)}, bf16[4,144,256]{2,1,0:T(8,128)(2,1)S(1)}, u32[]{:S(2)}, u32[]{:S(2)}) collective-permute-start(bf16[4,144,256]{2,1,0:T(8,128)(2,1)S(1)} %get-tuple-element.70), channel_id=1, source_target_pairs={{0,4},{1,5},{2,6},{3,7},{4,0},{5,1},{6,2},{7,3},{8,12},{9,13},{10,... | collective-permute-start | bytes 884744 | tf_op jit(solution)/shard_map/ppermute | solution.py:28
  124.8 7.0 %collective-permute-start.19 = (bf16[2,144,256]{2,1,0:T(8,128)(2,1)S(1)}, bf16[2,144,256]{2,1,0:T(8,128)(2,1)S(1)}, u32[]{:S(2)}, u32[]{:S(2)}) collective-permute-start(bf16[2,144,256]{2,1,0:T(8,128)(2,1)S(1)} %get-tuple-element.106), channel_id=1, source_target_pairs={{0,4},{1,5},{2,6},{3,7},{4,0},{5,1},{6,2},{7,3},{8,12},{9,13},{10,... | collective-permute-start | bytes 442376 | tf_op jit(solution)/shard_map/ppermute | solution.py:28
  126.5 5.3 %collective-permute-start.20 = (bf16[2,144,256]{2,1,0:T(8,128)(2,1)S(1)}, bf16[2,144,256]{2,1,0:T(8,128)(2,1)S(1)}, u32[]{:S(2)}, u32[]{:S(2)}) collective-permute-start(bf16[2,144,256]{2,1,0:T(8,128)(2,1)S(1)} %get-tuple-element.105), channel_id=1, source_target_pairs={{0,2},{1,3},{2,0},{3,1},{4,6},{5,7},{6,4},{7,5},{8,10},{9,11},{10,... | collective-permute-start | bytes 442376 | tf_op jit(solution)/shard_map/ppermute | solution.py:28
  131.9 7.7 %collective-permute-start.21 = (bf16[1,144,256]{2,1,0:T(8,128)(2,1)S(1)}, bf16[1,144,256]{2,1,0:T(8,128)(2,1)S(1)}, u32[]{:S(2)}, u32[]{:S(2)}) collective-permute-start(bf16[1,144,256]{2,1,0:T(8,128)(2,1)S(1)} %get-tuple-element.111), channel_id=1, source_target_pairs={{0,8},{1,9},{2,10},{3,11},{4,12},{5,13},{6,14},{7,15},{8,0},{9,1},... | collective-permute-start | bytes 221192 | tf_op jit(solution)/shard_map/ppermute | solution.py:28
  134.3 5.3 %collective-permute-start.22 = (bf16[1,144,256]{2,1,0:T(8,128)(2,1)S(1)}, bf16[1,144,256]{2,1,0:T(8,128)(2,1)S(1)}, u32[]{:S(2)}, u32[]{:S(2)}) collective-permute-start(bf16[1,144,256]{2,1,0:T(8,128)(2,1)S(1)} %get-tuple-element.109), channel_id=1, source_target_pairs={{0,8},{1,9},{2,10},{3,11},{4,12},{5,13},{6,14},{7,15},{8,0},{9,1},... | collective-permute-start | bytes 221192 | tf_op jit(solution)/shard_map/ppermute | solution.py:28
  140.4 1.3 collective-permute-start.23

commit v11 on v7

--- a/solution.py
+++ b/solution.py
@@ -336,49 +336,48 @@
     )(blocks)
 
 
-def image_kernel(factor, call, img_dev, packed_ref, sum_ref, norm_ref, keys_ref, values_ref):
-    devices = packed_ref.shape[0]
-    part_rows = packed_ref.shape[1] - 2 * img_dev
-    for device in range(devices):
+def image_kernel(factor, call, img_dev, packed_ref, sum_ref, top_ref, keys_ref, wide_ref):
+    wide_ref[:, HEAD_DIM:] = jnp.ones((wide_ref.shape[0], HEAD_DIM), wide_ref.dtype)
+    for device in range(packed_ref.shape[0]):
         rows = slice(device * img_dev, (device + 1) * img_dev)
         keys_ref[rows, :] = packed_ref[device, :img_dev, :]
-        values_ref[rows, :] = packed_ref[device, img_dev : 2 * img_dev, :]
-    group = max(1, 256 // part_rows)
-    rows = group * part_rows
+        wide_ref[rows, :HEAD_DIM] = packed_ref[device, img_dev : 2 * img_dev, :]
+    group = max(1, 256 // (packed_ref.shape[1] - 2 * img_dev))
+    rows = 256
     contract = (((1,), (1,)), ((), ()))
-    steps = sum_ref.shape[0] // rows
-    for step in range(steps):
-        at = (call * steps + step) * group
-        span = slice(step * rows, (step + 1) * rows)
+    count = sum_ref.shape[0]
+    for start in range(0, count, rows):
+        span = slice(start, start + rows)
+        at = (call * count + start) // rows * group
         queries = packed_ref[at : at + group, 2 * img_dev :, :].reshape(rows, HEAD_DIM)
         scores = lax.dot_general(queries, keys_ref[...], contract, preferred_element_type=jnp.float32)
         scores = scores * factor
         top = jnp.max(scores, 1, keepdims=True)
-        weights = jnp.exp2(scores - top)
-        total = jnp.sum(weights, 1, keepdims=True)
-        sum_ref[span, :] = jnp.dot(
-            weights.astype(jnp.bfloat16), values_ref[...], preferred_element_type=jnp.float32
-        )
-        lane = lax.broadcasted_iota(jnp.int32, (rows, 128), 1)
-        norm_ref[span, :] = jnp.where(lane < 64, top, total)
+        weights = jnp.exp2(scores - top).astype(jnp.bfloat16)
+        sum_ref[span, :] = jnp.dot(weights, wide_ref[...], preferred_element_type=jnp.float32)
+        top_ref[span, :] = jnp.broadcast_to(top, (rows, HEAD_DIM))
 
 
 def image_attention(packed, img_dev, factor, call, calls):
-    devices = packed.shape[0]
-    keys = devices * img_dev
-    count = devices * (packed.shape[1] - 2 * img_dev) // calls
-    out = jax.ShapeDtypeStruct((count, HEAD_DIM), jnp.float32)
+    count = packed.shape[0] * (packed.shape[1] - 2 * img_dev) // calls
+    total = packed.shape[0] * img_dev
     return pl.pallas_call(
         functools.partial(image_kernel, factor, call, img_dev),
-        out_shape=(out, out),
+        out_shape=(
+            jax.ShapeDtypeStruct((count, 2 * HEAD_DIM), jnp.float32),
+            jax.ShapeDtypeStruct((count, HEAD_DIM), jnp.float32),
+        ),
         in_specs=[VMEM_SPEC],
         out_specs=(VMEM_SPEC, VMEM_SPEC),
-        scratch_shapes=[pltpu.VMEM((keys, HEAD_DIM), jnp.bfloat16)] * 2,
+        scratch_shapes=[
+            pltpu.VMEM((total, HEAD_DIM), jnp.bfloat16),
+            pltpu.VMEM((total, 2 * HEAD_DIM), jnp.bfloat16),
+        ],
         compiler_params=params(24),
         cost_estimate=pl.CostEstimate(
-            flops=4 * count * keys * HEAD_DIM,
-            bytes_accessed=4 * keys * HEAD_DIM + 10 * count * HEAD_DIM,
-            transcendentals=count * keys,
+            flops=4 * count * total * HEAD_DIM,
+            bytes_accessed=4 * total * HEAD_DIM + 10 * count * HEAD_DIM,
+            transcendentals=count * total,
         ),
         name="image_attention",
     )(packed)
@@ -387,32 +386,34 @@
 def finish_kernel(factor, calls, img_dev, place_ref, packed_ref, *refs):
     images, (mine_ref, got_ref, out_ref) = refs[: 2 * calls], refs[2 * calls :]
     core, valid = place_ref[2], place_ref[4]
-    devices, part_rows = packed_ref.shape[0], packed_ref.shape[1] - 2 * img_dev
+    devices = out_ref.shape[0]
+    part_rows = packed_ref.shape[1] - 2 * img_dev
     half = mine_ref.shape[0]
     contract = (((1,), (1,)), ((), ()))
     mine, got = mine_ref[...], got_ref[...]
     keys = jnp.concatenate([mine[:, :HEAD_DIM], got[:, :HEAD_DIM]], 0)
     values = jnp.concatenate([mine[:, HEAD_DIM:], got[:, HEAD_DIM:]], 0)
+    values = jnp.concatenate([values, jnp.ones(values.shape, values.dtype)], 1)
     lane = lax.broadcasted_iota(jnp.int32, (1, 2 * half), 1)
     text_position = jnp.where((lane >= half) == (core == 0), half, 0) + lane % half
+    bias = jnp.where(text_position < valid, 0.0, -jnp.inf)
     group = max(1, 512 // part_rows)
     rows = group * part_rows
     each = devices // group // calls
     for step in range(devices // group):
-        sum_ref, norm_ref = images[2 * (step // each)], images[2 * (step // each) + 1]
+        sum_ref, top_ref = images[2 * (step // each)], images[2 * (step // each) + 1]
         span = slice(step % each * rows, (step % each + 1) * rows)
         queries = packed_ref[step * group : (step + 1) * group, 2 * img_dev :, :]
         queries = queries.reshape(rows, HEAD_DIM)
-        scores = lax.dot_general(queries, keys, contract, preferred_element_type=jnp.float32) * factor
-        scores = jnp.where(text_position < valid, scores, -jnp.inf)
-        before = norm_ref[span, 0:1]
+        scores = lax.dot_general(queries, keys, contract, preferred_element_type=jnp.float32)
+        scores = scores * factor + bias
+        before = top_ref[span, :]
         top = jnp.maximum(before, jnp.max(scores, 1, keepdims=True))
         rescale = jnp.exp2(before - top)
-        weights = jnp.exp2(scores - top)
-        total = norm_ref[span, 64:65] * rescale + jnp.sum(weights, 1, keepdims=True)
-        mixed = sum_ref[span, :] * rescale + jnp.dot(
-            weights.astype(jnp.bfloat16), values, preferred_element_type=jnp.float32
-        )
+        weights = jnp.exp2(scores - jnp.concatenate([top] * (2 * half // HEAD_DIM), 1))
+        total = jnp.dot(weights.astype(jnp.bfloat16), values, preferred_element_type=jnp.float32)
+        mixed = sum_ref[span, :HEAD_DIM] * rescale + total[:, :HEAD_DIM]
+        total = sum_ref[span, HEAD_DIM:] * rescale + total[:, HEAD_DIM:]
         mixed = (mixed / total).astype(out_ref.dtype)
         out_ref[step * group : (step + 1) * group, :part_rows, :] = mixed.reshape(group, part_rows, HEAD_DIM)
     low = jnp.where(core == 0, mine.astype(jnp.float32), got.astype(jnp.float32))
@@ -428,8 +429,8 @@
 
 def finish(place, packed, images, mine, got, img_dev, factor):
     devices, part_rows = packed.shape[0], packed.shape[1] - 2 * img_dev
+    count = devices * part_rows
     share = 2 * mine.shape[0] // devices
-    count = devices * part_rows
     return pl.pallas_call(
         functools.partial(finish_kernel, factor, len(images) // 2, img_dev),
         out_shape=jax.ShapeDtypeStruct((devices, part_rows + 2 * share, HEAD_DIM), jnp.bfloat16),
@@ -498,7 +499,7 @@
     for step in range(rounds):
         got = [swap(part, 2 * order[step]) for part, order in zip(sent, lanes)]
         if step == 0:
-            got, win1, kv1, mod1, packed = tie((got, win1, kv1, mod1, packed))
+            got, packed = tie((got, packed))
             lines = modulation(time, mod0, mod1)
         if step == 1:
             got, lines = tie((got, lines))

time: 139 us -> 139 us (level)
  local copies, waits for them, and re-layouts: 10.7 us -> 7.42 us
  waiting for transfers between devices: 45.1 us -> 47.2 us
  starting transfers between devices: 33.1 us -> 34.8 us
    unnamed x30 -> x16, local copies, waits for them, and re-layouts: 8.36 us -> 5.09 us
    pallas_call x1, Pallas kernels: 3.76 us -> 1.58 us  [finish(): pl.pallas_call(functools.partial(finish_kernel, factor, len(images) // 2,...]
    pallas_call x1, Pallas kernels: 2.33 us -> 4.03 us  [project(): pl.pallas_call(functools.partial(project_kernel, lanes), out_shape=(out,)...]
    ppermute x24, waiting for transfers between devices: 45.1 us -> 46.6 us  [swap(): return lax.ppermute(value, 'seq', [(i, i ^ mask) for i in range(devices)])]
    ppermute x24, starting transfers between devices: 25.8 us -> 27.3 us  [swap(): return lax.ppermute(value, 'seq', [(i, i ^ mask) for i in range(devices)])]
  transfers between devices with their start and end apart: 25 -> 25, of which waited for: 20 -> 19; matrix products, arithmetic and copies ran while one was open for 3% -> 4% of each run, Pallas kernels for 8% -> 8%
where the time goes in v11:
time: 139 us; the launch traced here: 138 us
  waiting for transfers between devices  47.2 us (34%)
  starting transfers between devices  34.8 us (25%)
  blocking collectives  22 us (16%)
  Pallas kernels  19.6 us (14%)
  local copies, waits for them, and re-layouts  7.42 us (5%)
  other arithmetic  4.92 us (4%)
  between operations  2.16 us (2%)
    ppermute x24, waiting for transfers between devices, swap(): return lax.ppermute(value, 'seq', [(i, i ^ mask) for i in range(devices)])  46.6 us
    ppermute x24, starting transfers between devices, swap(): return lax.ppermute(value, 'seq', [(i, i ^ mask) for i in range(devices)])  27.3 us
    all_to_all x1, blocking collectives, exchange(): return lax.all_to_all(rows, 'seq', split_axis=0, concat_axis=0, tiled=True)  22 us
    all_to_all x1, starting transfers between devices, exchange(): return lax.all_to_all(rows, 'seq', split_axis=0, concat_axis=0, tiled=True)  7.49 us
    pallas_call x2, Pallas kernels, image_attention(): pl.pallas_call(functools.partial(image_kernel, factor, call, img_dev), ou...  7.13 us
    unnamed x16, local copies, waits for them, and re-layouts  5.09 us
    pallas_call x1, Pallas kernels, project(): pl.pallas_call(functools.partial(project_kernel, lanes), out_shape=(out,)...  4.03 us
    pallas_call x1, Pallas kernels, encoder(): pl.pallas_call(functools.partial(encoder_kernel, lanes), out_shape=(out,)...  3.49 us
  transfers between devices with their start and end apart: 25, of which 19 were waited for; matrix products, arithmetic and copies ran while one was open for 4% of the time, Pallas kernels for 8%

profile of v11, /device:TPU:0, one launch (start us, length us, event | category | flops | bytes accessed | tf_op | source)
XLA Modules:
  0.0 138.1 jit_solution(1550570300209410882)
XLA Ops:
  0.6 1.6 %copy.12 = bf16[1,128,2,2048]{3,1,2,0:T(8,128)(2,1)S(1)} copy(bf16[1,128,2,2048]{3,2,1,0:T(2,128)(2,1)} %param.19) | data formatting | bytes 2097152 | tf_op jit(solution)/shard_map/optimization_barrier | solution.py:489
  2.3 1.0 copy-done.3
  3.3 1.5 %pack.1 = bf16[16,384,128]{2,1,0:T(8,128)(2,1)} custom-call(bf16[128,2048]{1,0:T(8,128)(2,1)S(1)} %bitcast.39, bf16[128,2048]{1,0:T(8,128)(2,1)S(1)} %get-tuple-element.83.keys_ref, bf16[128,2048]{1,0:T(8,128)(2,1)S(1)} %get-tuple-element.82.values_ref), custom_call_target="tpu_custom_call" | custom-call | bytes 3145728 | tf_op jit(solution)/shard_map/pack/pallas_call | solution.py:296
  4.7 7.5 %all-to-all-start = ((bf16[16,384,128]{2,1,0:T(8,128)(2,1)}), bf16[16,384,128]{2,1,0:T(8,128)(2,1)S(1)}, u32[]{:S(2)}, u32[]{:S(2)}) async-start(bf16[16,384,128]{2,1,0:T(8,128)(2,1)} %pack.1), calls=%async_computation | async-start | bytes 3145728 | tf_op jit(solution)/shard_map/all_to_all | solution.py:487
  12.9 0.1 stack.19.place_ref
  13.0 3.4 %copy-done = bf16[1184,3584]{1,0:T(8,128)(2,1)S(1)} copy-done((bf16[1184,3584]{1,0:T(8,128)(2,1)S(1)}, bf16[1184,3584]{1,0:T(8,128)(2,1)}, u32[]{:S(2)}) %copy-start) | copy-done | bytes 8486936
  16.4 3.5 %encoder.1 = (bf16[8,16,1792]{2,1,0:T(8,128)(2,1)S(1)}, bf16[8,16,1792]{2,1,0:T(8,128)(2,1)S(1)}, bf16[8,16,1792]{2,1,0:T(8,128)(2,1)S(1)}, bf16[8,16,1792]{2,1,0:T(8,128)(2,1)S(1)}) custom-call(s32[5]{0:T(128)S(1)} %stack.19.place_ref, bf16[1184,256]{1,0:T(8,128)(2,1)S(1)} %bitcast.38, bf16[1184,3584]{1,0:T(8,128)(2,1)S(1)} %copy-done), custom_call_target="tpu_custom_call" | custom-call | flops 2172649472 | bytes 10928128 | tf_op jit(solution)/shard_map/encoder/pallas_call | solution.py:89
  19.9 0.5 collective-permute-start
  20.3 0.1 collective-permute-start.2
  20.5 1.3 collective-permute-done
  21.8 0.9 add_convert_fusion.1
  22.7 1.9 %collective-permute-start.1 = (bf16[4,16,1792]{2,1,0:T(8,128)(2,1)S(1)}, bf16[4,16,1792]{2,1,0:T(8,128)(2,1)S(1)}, u32[]{:S(2)}, u32[]{:S(2)}) collective-permute-start(bf16[4,16,1792]{2,1,0:T(8,128)(2,1)S(1)} %get-tuple-element.86), channel_id=1, source_target_pairs={{0,2},{1,3},{2,0},{3,1},{4,6},{5,7},{6,4},{7,5},{8,10},{9,11},{10,... | collective-permute-start | bytes 688136 | tf_op jit(solution)/shard_map/ppermute | solution.py:28
  24.6 0.9 convert_add_fusion
  25.4 1.5 %collective-permute-start.3 = (bf16[4,16,1792]{2,1,0:T(8,128)(2,1)S(1)}, bf16[4,16,1792]{2,1,0:T(8,128)(2,1)}, u32[]{:S(2)}, u32[]{:S(2)}) collective-permute-start(bf16[4,16,1792]{2,1,0:T(8,128)(2,1)S(1)} %get-tuple-element.85), channel_id=1, source_target_pairs={{0,4},{1,5},{2,6},{3,7},{4,0},{5,1},{6,2},{7,3},{8,12},{9,13},{10,... | collective-permute-start | bytes 688136 | tf_op jit(solution)/shard_map/ppermute | solution.py:28
  26.9 0.5 collective-permute-start.15
  28.1 0.6 fusion.13
  28.7 7.3 %collective-permute-done.1 = bf16[4,16,1792]{2,1,0:T(8,128)(2,1)S(1)} collective-permute-done((bf16[4,16,1792]{2,1,0:T(8,128)(2,1)S(1)}, bf16[4,16,1792]{2,1,0:T(8,128)(2,1)S(1)}, u32[]{:S(2)}, u32[]{:S(2)}) %collective-permute-start.1) | collective-permute-done | bytes 229408 | tf_op jit(solution)/shard_map/ppermute | solution.py:28
  36.0 0.7 copy-done.5
  36.7 7.0 %collective-permute-done.3 = bf16[4,16,1792]{2,1,0:T(8,128)(2,1)} collective-permute-done((bf16[4,16,1792]{2,1,0:T(8,128)(2,1)S(1)}, bf16[4,16,1792]{2,1,0:T(8,128)(2,1)}, u32[]{:S(2)}, u32[]{:S(2)}) %collective-permute-start.3) | collective-permute-done | bytes 229408 | tf_op jit(solution)/shard_map/ppermute | solution.py:28
  43.7 0.5 all-to-all-done.packed_ref
  44.2 1.2 slice_add_fusion
  45.5 2.7 %collective-permute-start.5 = (bf16[2,16,1792]{2,1,0:T(8,128)(2,1)S(1)}, bf16[2,16,1792]{2,1,0:T(8,128)(2,1)S(1)}, u32[]{:S(2)}, u32[]{:S(2)}) collective-permute-start(bf16[2,16,1792]{2,1,0:T(8,128)(2,1)S(1)} %get-tuple-element.89), channel_id=1, source_target_pairs={{0,2},{1,3},{2,0},{3,1},{4,6},{5,7},{6,4},{7,5},{8,10},{9,11},{10,... | collective-permute-start | bytes 344072 | tf_op jit(solution)/shard_map/ppermute | solution.py:28
  48.2 1.2 fusion.1
  49.4 4.8 %collective-permute-start.4 = (bf16[2,16,1792]{2,1,0:T(8,128)(2,1)S(1)}, bf16[2,16,1792]{2,1,0:T(8,128)(2,1)S(1)}, u32[]{:S(2)}, u32[]{:S(2)}) collective-permute-start(bf16[2,16,1792]{2,1,0:T(8,128)(2,1)S(1)} %get-tuple-element.90), channel_id=1, source_target_pairs={{0,4},{1,5},{2,6},{3,7},{4,0},{5,1},{6,2},{7,3},{8,12},{9,13},{10,... | collective-permute-start | bytes 344072 | tf_op jit(solution)/shard_map/ppermute | solution.py:28
  54.4 0.2 modulation.1.refs_4_
  54.6 3.0 %collective-permute-done.4 = bf16[2,16,1792]{2,1,0:T(8,128)(2,1)S(1)} collective-permute-done((bf16[2,16,1792]{2,1,0:T(8,128)(2,1)S(1)}, bf16[2,16,1792]{2,1,0:T(8,128)(2,1)S(1)}, u32[]{:S(2)}, u32[]{:S(2)}) %collective-permute-start.4) | collective-permute-done | bytes 114720 | tf_op jit(solution)/shard_map/ppermute | solution.py:28
  57.6 1.5 %collective-permute-start.8 = (bf16[1,16,1792]{2,1,0:T(8,128)(2,1)S(1)}, bf16[1,16,1792]{2,1,0:T(8,128)(2,1)S(1)}, u32[]{:S(2)}, u32[]{:S(2)}) collective-permute-start(bf16[1,16,1792]{2,1,0:T(8,128)(2,1)S(1)} %fusion.6), channel_id=1, source_target_pairs={{0,8},{1,9},{2,10},{3,11},{4,12},{5,13},{6,14},{7,15},{8,0},{9,1},... | collective-permute-start | bytes 172040 | tf_op jit(solution)/shard_map/ppermute | solution.py:28
  59.1 1.6 %collective-permute-start.7 = (bf16[1,16,1792]{2,1,0:T(8,128)(2,1)S(1)}, bf16[1,16,1792]{2,1,0:T(8,128)(2,1)S(1)}, u32[]{:S(2)}, u32[]{:S(2)}) collective-permute-start(bf16[1,16,1792]{2,1,0:T(8,128)(2,1)S(1)} %fusion.9), channel_id=1, source_target_pairs={{0,8},{1,9},{2,10},{3,11},{4,12},{5,13},{6,14},{7,15},{8,0},{9,1},... | collective-permute-start | bytes 172040 | tf_op jit(solution)/shard_map/ppermute | solution.py:28
  60.7 3.8 %collective-permute-done.8 = bf16[1,16,1792]{2,1,0:T(8,128)(2,1)S(1)} collective-permute-done((bf16[1,16,1792]{2,1,0:T(8,128)(2,1)S(1)}, bf16[1,16,1792]{2,1,0:T(8,128)(2,1)S(1)}, u32[]{:S(2)}, u32[]{:S(2)}) %collective-permute-start.8) | collective-permute-done | bytes 57376 | tf_op jit(solution)/shard_map/ppermute | solution.py:28
  64.4 0.1 multiply_reduce_fusion
  64.6 1.1 collective-permute-done.7
  65.7 0.1 multiply_reduce_fusion.1
  65.8 0.1 multiply_convert_fusion
  65.9 0.2 collective-permute-start.11
  66.1 2.8 %collective-permute-start.9 = (bf16[16,1792]{1,0:T(8,128)(2,1)S(1)}, bf16[16,1792]{1,0:T(8,128)(2,1)S(1)}, u32[]{:S(2)}, u32[]{:S(2)}) collective-permute-start(bf16[16,1792]{1,0:T(8,128)(2,1)S(1)} %get-tuple-element.103), channel_id=1, source_target_pairs={{0,8},{1,9},{2,10},{3,11},{4,12},{5,13},{6,14},{7,15},{8,0},{9,1},... | collective-permute-start | bytes 172040 | tf_op jit(solution)/shard_map/ppermute | solution.py:28
  68.9 3.2 %collective-permute-done.11 = bf16[16,1792]{1,0:T(8,128)(2,1)S(1)} collective-permute-done((bf16[16,1792]{1,0:T(8,128)(2,1)S(1)}, bf16[16,1792]{1,0:T(8,128)(2,1)S(1)}, u32[]{:S(2)}, u32[]{:S(2)}) %collective-permute-start.11) | collective-permute-done | bytes 57376 | tf_op jit(solution)/shard_map/ppermute | solution.py:28
  72.2 0.7 collective-permute-start.12
  72.9 1.2 collective-permute-start.10
  74.0 3.0 %collective-permute-done.12 = bf16[32,1792]{1,0:T(8,128)(2,1)S(1)} collective-permute-done((bf16[32,1792]{1,0:T(8,128)(2,1)S(1)}, bf16[32,1792]{1,0:T(8,128)(2,1)S(1)}, u32[]{:S(2)}, u32[]{:S(2)}) %collective-permute-start.12) | collective-permute-done | bytes 114720 | tf_op jit(solution)/shard_map/ppermute | solution.py:28
  77.0 0.7 collective-permute-done.10
  77.7 1.7 %collective-permute-start.13 = (bf16[64,1792]{1,0:T(8,128)(2,1)S(1)}, bf16[64,1792]{1,0:T(8,128)(2,1)S(1)}, u32[]{:S(2)}, u32[]{:S(2)}) collective-permute-start(bf16[64,1792]{1,0:T(8,128)(2,1)S(1)} %pad_maximum_fusion.refs_0_), channel_id=1, source_target_pairs={{0,2},{1,3},{2,0},{3,1},{4,6},{5,7},{6,4},{7,5},{8,10},{9,11},{10,... | collective-permute-start | bytes 688136 | tf_op jit(solution)/shard_map/ppermute | solution.py:28
  79.4 0.1 collective-permute-start.14
  79.5 3.5 %image_attention.2 = (f32[1024,256]{1,0:T(8,128)S(1)}, f32[1024,128]{1,0:T(8,128)S(1)}) custom-call(bf16[16,384,128]{2,1,0:T(8,128)(2,1)S(1)} %all-to-all-done.packed_ref), custom_call_target="tpu_custom_call" | custom-call | flops 1073741824 | bytes 2359296 | tf_op jit(solution)/shard_map/image_attention/pallas_call | solution.py:364
  83.0 0.8 collective-permute-done.13.refs_1_
  83.8 1.6 %collective-permute-done.14.refs_3_ = bf16[64,1792]{1,0:T(8,128)(2,1)S(1)} collective-permute-done((bf16[64,1792]{1,0:T(8,128)(2,1)S(1)}, bf16[64,1792]{1,0:T(8,128)(2,1)S(1)}, u32[]{:S(2)}, u32[]{:S(2)}) %collective-permute-start.14) | collective-permute-done | bytes 229408 | tf_op jit(solution)/shard_map/ppermute | solution.py:28
  85.5 4.0 %project.1 = (bf16[4,144,256]{2,1,0:T(8,128)(2,1)S(1)}, bf16[4,144,256]{2,1,0:T(8,128)(2,1)S(1)}, bf16[4,144,256]{2,1,0:T(8,128)(2,1)S(1)}, bf16[4,144,256]{2,1,0:T(8,128)(2,1)S(1)}) custom-call(s32[5]{0:T(128)S(1)} %stack.19.place_ref, bf16[64,1792]{1,0:T(8,128)(2,1)S(1)} %pad_maximum_fusion.refs_0_, bf16[64,1792]{1,0:T(8,128)(2,1)S(1)} %collective-permute-done.13.refs_1_, ...), custom_call_target="tpu_custom_call" | custom-call | flops 754974720 | bytes 7864320 | tf_op jit(solution)/shard_map/project/pallas_call | solution.py:211
  89.5 0.5 collective-permute-start.17
  90.0 1.1 collective-permute-start.18
  91.1 3.7 %image_attention.3 = (f32[1024,256]{1,0:T(8,128)S(1)}, f32[1024,128]{1,0:T(8,128)S(1)}) custom-call(bf16[16,384,128]{2,1,0:T(8,128)(2,1)S(1)} %all-to-all-done.packed_ref), custom_call_target="tpu_custom_call" | custom-call | flops 1073741824 | bytes 2359296 | tf_op jit(solution)/shard_map/image_attention/pallas_call | solution.py:364
  94.7 3.1 %collective-permute-done.17 = bf16[4,144,256]{2,1,0:T(8,128)(2,1)S(1)} collective-permute-done((bf16[4,144,256]{2,1,0:T(8,128)(2,1)S(1)}, bf16[4,144,256]{2,1,0:T(8,128)(2,1)S(1)}, u32[]{:S(2)}, u32[]{:S(2)}) %collective-permute-start.17) | collective-permute-done | bytes 294944 | tf_op jit(solution)/shard_map/ppermute | solution.py:28
  97.9 0.4 collective-permute-done.18
  98.3 1.7 %collective-permute-start.21 = (bf16[2,144,256]{2,1,0:T(8,128)(2,1)S(1)}, bf16[2,144,256]{2,1,0:T(8,128)(2,1)S(1)}, u32[]{:S(2)}, u32[]{:S(2)}) collective-permute-start(bf16[2,144,256]{2,1,0:T(8,128)(2,1)S(1)} %get-tuple-element.92), channel_id=1, source_target_pairs={{0,2},{1,3},{2,0},{3,1},{4,6},{5,7},{6,4},{7,5},{8,10},{9,11},{10,... | collective-permute-start | bytes 442376 | tf_op jit(solution)/shard_map/ppermute | solution.py:28
  100.1 0.1 collective-permute-start.19
  100.2 3.3 %collective-permute-done.21 = bf16[2,144,256]{2,1,0:T(8,128)(2,1)S(1)} collective-permute-done((bf16[2,144,256]{2,1,0:T(8,128)(2,1)S(1)}, bf16[2,144,256]{2,1,0:T(8,128)(2,1)S(1)}, u32[]{:S(2)}, u32[]{:S(2)}) %collective-permute-start.21) | collective-permute-done | bytes 147488 | tf_op jit(solution)/shard_map/ppermute | solution.py:28
  103.6 0.8 collective-permute-start.22
  104.4 0.9 collective-permute-done.19
  105.3 1.3 collective-permute-start.20
  106.7 3.0 %collective-permute-done.22 = bf16[1,144,256]{2,1,0:T(8,128)(2,1)S(1)} collective-permute-done((bf16[1,144,256]{2,1,0:T(8,128)(2,1)S(1)}, bf16[1,144,256]{2,1,0:T(8,128)(2,1)S(1)}, u32[]{:S(2)}, u32[]{:S(2)}) %collective-permute-start.22) | collective-permute-done | bytes 73760 | tf_op jit(solution)/shard_map/ppermute | solution.py:28
  109.7 1.8 %collective-permute-done.20 = bf16[1,144,256]{2,1,0:T(8,128)(2,1)S(1)} collective-permute-done((bf16[1,144,256]{2,1,0:T(8,128)(2,1)S(1)}, bf16[1,144,256]{2,1,0:T(8,128)(2,1)S(1)}, u32[]{:S(2)}, u32[]{:S(2)}) %collective-permute-start.20) | collective-permute-done | bytes 73760 | tf_op jit(solution)/shard_map/ppermute | solution.py:28
  111.5 0.7 combine.1
  112.3 1.2 collective-permute-done.23.refs_5_
  113.5 1.6 %finish.1 = bf16[16,160,128]{2,1,0:T(8,128)(2,1)S(1)} custom-call(s32[5]{0:T(128)S(1)} %stack.19.place_ref, bf16[16,384,128]{2,1,0:T(8,128)(2,1)S(1)} %all-to-all-done.packed_ref, f32[1024,256]{1,0:T(8,128)S(1)} %get-tuple-element.66.refs_0_, f32[1024,128]{1,0:T(8,128)S(1)} %get-tuple-element.67.refs_1_, f32[1024,256]{1,0:T(8,128)S(1)} %get-tuple-element.72.refs_2_, ...), custom_call_target="tpu_custom_call" | custom-call | flops 268435456 | bytes 3145728 | tf_op jit(solution)/shard_map/finish/pallas_call | solution.py:434
  115.1 22.0 %all_to_all.10.blocks_ref = bf16[16,160,128]{2,1,0:T(8,128)(2,1)S(1)} all-to-all(bf16[16,160,128]{2,1,0:T(8,128)(2,1)S(1)} %finish.1), channel_id=1, replica_groups=mesh['dp'=2,'seq'=16] {'seq'}, dimensions={0} | all-to-all | bytes 1310720 | tf_op jit(solution)/shard_map/all_to_all | solution.py:487
  137.1 1.0 unpack.1
  (36 shorter events, 0.6 us)
Async XLA Ops:
  2.2 1.0 copy-start.3
  4.7 8.3 %copy-start.2 = (bf16[1,256,1184]{1,2,0:T(8,128)(2,1)S(1)}, bf16[1,256,1184]{1,2,0:T(8,128)(2,1)}, u32[]{:S(2)}) copy-start(bf16[1,256,1184]{1,2,0:T(8,128)(2,1)} %param.10) | copy-start | bytes 1818628
  4.7 39.5 %all-to-all-start = ((bf16[16,384,128]{2,1,0:T(8,128)(2,1)}), bf16[16,384,128]{2,1,0:T(8,128)(2,1)S(1)}, u32[]{:S(2)}, u32[]{:S(2)}) async-start(bf16[16,384,128]{2,1,0:T(8,128)(2,1)} %pack.1), calls=%async_computation | async-start | bytes 3145728 | tf_op jit(solution)/shard_map/all_to_all | solution.py:487
  13.0 3.4 %copy-start = (bf16[1184,3584]{1,0:T(8,128)(2,1)S(1)}, bf16[1184,3584]{1,0:T(8,128)(2,1)}, u32[]{:S(2)}) copy-start(bf16[1184,3584]{1,0:T(8,128)(2,1)} %weight_ref.1) | copy-start | bytes 25460740
  19.9 1.9 %collective-permute-start = (bf16[8,16,1792]{2,1,0:T(8,128)(2,1)S(1)}, bf16[8,16,1792]{2,1,0:T(8,128)(2,1)S(1)}, u32[]{:S(2)}, u32[]{:S(2)}) collective-permute-start(bf16[8,16,1792]{2,1,0:T(8,128)(2,1)S(1)} %get-tuple-element.46), channel_id=1, source_target_pairs={{0,1},{1,0},{2,3},{3,2},{4,5},{5,4},{6,7},{7,6},{8,9},{9,8},{10,11... | collective-permute-start | bytes 1376264 | tf_op jit(solution)/shard_map/ppermute | solution.py:28
  20.3 4.2 %collective-permute-start.2 = (bf16[8,16,1792]{2,1,0:T(8,128)(2,1)S(1)}, bf16[8,16,1792]{2,1,0:T(8,128)(2,1)S(1)}, u32[]{:S(2)}, u32[]{:S(2)}) collective-permute-start(bf16[8,16,1792]{2,1,0:T(8,128)(2,1)S(1)} %get-tuple-element.48), channel_id=1, source_target_pairs={{0,1},{1,0},{2,3},{3,2},{4,5},{5,4},{6,7},{7,6},{8,9},{9,8},{10,11... | collective-permute-start | bytes 1376264 | tf_op jit(solution)/shard_map/ppermute | solution.py:28
  21.8 5.1 %copy-start.4 = (bf16[256,2,192]{0,2,1:T(8,128)(2,1)S(1)}, bf16[256,2,192]{0,2,1:T(8,128)(2,1)}, u32[]{:S(2)}) copy-start(bf16[256,2,192]{0,2,1:T(8,128)(2,1)} %param.14) | copy-start | bytes 589828
  21.8 5.6 %copy-start.1 = (bf16[192,4096]{1,0:T(8,128)(2,1)S(1)}, bf16[192,4096]{1,0:T(8,128)(2,1)}, u32[]{:S(2)}) copy-start(bf16[192,4096]{1,0:T(8,128)(2,1)} %refs_7_.1) | copy-start | bytes 4718596
  21.8 6.3 %copy-start.7 = (bf16[3584]{0:T(1024)(128)(2,1)S(1)}, bf16[3584]{0:T(1024)(128)(2,1)}, u32[]{:S(2)}) copy-start(bf16[3584]{0:T(1024)(128)(2,1)} %param.12) | copy-start | bytes 21508
  22.7 13.4 %collective-permute-start.1 = (bf16[4,16,1792]{2,1,0:T(8,128)(2,1)S(1)}, bf16[4,16,1792]{2,1,0:T(8,128)(2,1)S(1)}, u32[]{:S(2)}, u32[]{:S(2)}) collective-permute-start(bf16[4,16,1792]{2,1,0:T(8,128)(2,1)S(1)} %get-tuple-element.86), channel_id=1, source_target_pairs={{0,2},{1,3},{2,0},{3,1},{4,6},{5,7},{6,4},{7,5},{8,10},{9,11},{10,... | collective-permute-start | bytes 688136 | tf_op jit(solution)/shard_map/ppermute | solution.py:28
  25.4 18.2 %collective-permute-start.3 = (bf16[4,16,1792]{2,1,0:T(8,128)(2,1)S(1)}, bf16[4,16,1792]{2,1,0:T(8,128)(2,1)}, u32[]{:S(2)}, u32[]{:S(2)}) collective-permute-start(bf16[4,16,1792]{2,1,0:T(8,128)(2,1)S(1)} %get-tuple-element.85), channel_id=1, source_target_pairs={{0,4},{1,5},{2,6},{3,7},{4,0},{5,1},{6,2},{7,3},{8,12},{9,13},{10,... | collective-permute-start | bytes 688136 | tf_op jit(solution)/shard_map/ppermute | solution.py:28
  26.9 27.4 %collective-permute-start.6 = (bf16[2,192,256]{2,1,0:T(8,128)(2,1)S(1)}, bf16[2,192,256]{2,1,0:T(8,128)(2,1)S(1)}, u32[]{:S(2)}, u32[]{:S(2)}) collective-permute-start(bf16[2,192,256]{2,1,0:T(8,128)(2,1)S(1)} %bitcast.40), channel_id=1, source_target_pairs={{0,1},{1,0},{2,3},{3,2},{4,5},{5,4},{6,7},{7,6},{8,9},{9,8},{10,11... | collective-permute-start | bytes 589832 | tf_op jit(solution)/shard_map/ppermute | solution.py:28
  26.9 58.5 %collective-permute-start.15 = (bf16[192,3584]{1,0:T(8,128)(2,1)}, bf16[192,3584]{1,0:T(8,128)(2,1)}, u32[]{:S(2)}, u32[]{:S(2)}) collective-permute-start(bf16[192,3584]{1,0:T(8,128)(2,1)} %bitcast.15.refs_5_), channel_id=1, source_target_pairs={{0,1},{1,0},{2,3},{3,2},{4,5},{5,4},{6,7},{7,6},{8,9},{9,8},{10,11... | collective-permute-start | bytes 4128776 | tf_op jit(solution)/shard_map/ppermute | solution.py:28
  27.4 58.0 %collective-permute-start.16 = (bf16[192,4096]{1,0:T(8,128)(2,1)S(1)}, bf16[192,4096]{1,0:T(8,128)(2,1)}, u32[]{:S(2)}, u32[]{:S(2)}) collective-permute-start(bf16[192,4096]{1,0:T(8,128)(2,1)S(1)} %copy-done.1), channel_id=1, source_target_pairs={{0,1},{1,0},{2,3},{3,2},{4,5},{5,4},{6,7},{7,6},{8,9},{9,8},{10,11... | collective-permute-start | bytes 4718600 | tf_op jit(solution)/shard_map/ppermute | solution.py:28
  36.0 0.7 copy-start.5
  44.2 21.6 %copy-start.6 = (f32[1792]{0:T(1024)S(1)}, f32[1792]{0:T(1024)}, u32[]{:S(2)}) copy-start(f32[1792]{0:T(1024)} %get-tuple-element.101) | copy-start | bytes 21508
  45.5 9.1 %collective-permute-start.5 = (bf16[2,16,1792]{2,1,0:T(8,128)(2,1)S(1)}, bf16[2,16,1792]{2,1,0:T(8,128)(2,1)S(1)}, u32[]{:S(2)}, u32[]{:S(2)}) collective-permute-start(bf16[2,16,1792]{2,1,0:T(8,128)(2,1)S(1)} %get-tuple-element.89), channel_id=1, source_target_pairs={{0,2},{1,3},{2,0},{3,1},{4,6},{5,7},{6,4},{7,5},{8,10},{9,11},{10,... | collective-permute-start | bytes 344072 | tf_op jit(solution)/shard_map/ppermute | solution.py:28
  49.4 8.2 %collective-permute-start.4 = (bf16[2,16,1792]{2,1,0:T(8,128)(2,1)S(1)}, bf16[2,16,1792]{2,1,0:T(8,128)(2,1)S(1)}, u32[]{:S(2)}, u32[]{:S(2)}) collective-permute-start(bf16[2,16,1792]{2,1,0:T(8,128)(2,1)S(1)} %get-tuple-element.90), channel_id=1, source_target_pairs={{0,4},{1,5},{2,6},{3,7},{4,0},{5,1},{6,2},{7,3},{8,12},{9,13},{10,... | collective-permute-start | bytes 344072 | tf_op jit(solution)/shard_map/ppermute | solution.py:28
  57.6 6.8 %collective-permute-start.8 = (bf16[1,16,1792]{2,1,0:T(8,128)(2,1)S(1)}, bf16[1,16,1792]{2,1,0:T(8,128)(2,1)S(1)}, u32[]{:S(2)}, u32[]{:S(2)}) collective-permute-start(bf16[1,16,1792]{2,1,0:T(8,128)(2,1)S(1)} %fusion.6), channel_id=1, source_target_pairs={{0,8},{1,9},{2,10},{3,11},{4,12},{5,13},{6,14},{7,15},{8,0},{9,1},... | collective-permute-start | bytes 172040 | tf_op jit(solution)/shard_map/ppermute | solution.py:28
  59.1 6.6 %collective-permute-start.7 = (bf16[1,16,1792]{2,1,0:T(8,128)(2,1)S(1)}, bf16[1,16,1792]{2,1,0:T(8,128)(2,1)S(1)}, u32[]{:S(2)}, u32[]{:S(2)}) collective-permute-start(bf16[1,16,1792]{2,1,0:T(8,128)(2,1)S(1)} %fusion.9), channel_id=1, source_target_pairs={{0,8},{1,9},{2,10},{3,11},{4,12},{5,13},{6,14},{7,15},{8,0},{9,1},... | collective-permute-start | bytes 172040 | tf_op jit(solution)/shard_map/ppermute | solution.py:28
  65.9 6.2 %collective-permute-start.11 = (bf16[16,1792]{1,0:T(8,128)(2,1)S(1)}, bf16[16,1792]{1,0:T(8,128)(2,1)S(1)}, u32[]{:S(2)}, u32[]{:S(2)}) collective-permute-start(bf16[16,1792]{1,0:T(8,128)(2,1)S(1)} %get-tuple-element.102), channel_id=1, source_target_pairs={{0,8},{1,9},{2,10},{3,11},{4,12},{5,13},{6,14},{7,15},{8,0},{9,1},... | collective-permute-start | bytes 172040 | tf_op jit(solution)/shard_map/ppermute | solution.py:28
  66.1 6.8 %collective-permute-start.9 = (bf16[16,1792]{1,0:T(8,128)(2,1)S(1)}, bf16[16,1792]{1,0:T(8,128)(2,1)S(1)}, u32[]{:S(2)}, u32[]{:S(2)}) collective-permute-start(bf16[16,1792]{1,0:T(8,128)(2,1)S(1)} %get-tuple-element.103), channel_id=1, source_target_pairs={{0,8},{1,9},{2,10},{3,11},{4,12},{5,13},{6,14},{7,15},{8,0},{9,1},... | collective-permute-start | bytes 172040 | tf_op jit(solution)/shard_map/ppermute | solution.py:28
  72.2 4.9 %collective-permute-start.12 = (bf16[32,1792]{1,0:T(8,128)(2,1)S(1)}, bf16[32,1792]{1,0:T(8,128)(2,1)S(1)}, u32[]{:S(2)}, u32[]{:S(2)}) collective-permute-start(bf16[32,1792]{1,0:T(8,128)(2,1)S(1)} %pad_maximum_fusion.3), channel_id=1, source_target_pairs={{0,2},{1,3},{2,0},{3,1},{4,6},{5,7},{6,4},{7,5},{8,10},{9,11},{10,... | collective-permute-start | bytes 344072 | tf_op jit(solution)/shard_map/ppermute | solution.py:28
  72.9 4.9 %collective-permute-start.10 = (bf16[32,1792]{1,0:T(8,128)(2,1)S(1)}, bf16[32,1792]{1,0:T(8,128)(2,1)S(1)}, u32[]{:S(2)}, u32[]{:S(2)}) collective-permute-start(bf16[32,1792]{1,0:T(8,128)(2,1)S(1)} %pad_maximum_fusion.2), channel_id=1, source_target_pairs={{0,4},{1,5},{2,6},{3,7},{4,0},{5,1},{6,2},{7,3},{8,12},{9,13},{10,... | collective-permute-start | bytes 344072 | tf_op jit(solution)/shard_map/ppermute | solution.py:28
  77.7 6.1 %collective-permute-start.13 = (bf16[64,1792]{1,0:T(8,128)(2,1)S(1)}, bf16[64,1792]{1,0:T(8,128)(2,1)S(1)}, u32[]{:S(2)}, u32[]{:S(2)}) collective-permute-start(bf16[64,1792]{1,0:T(8,128)(2,1)S(1)} %pad_maximum_fusion.refs_0_), channel_id=1, source_target_pairs={{0,2},{1,3},{2,0},{3,1},{4,6},{5,7},{6,4},{7,5},{8,10},{9,11},{10,... | collective-permute-start | bytes 688136 | tf_op jit(solution)/shard_map/ppermute | solution.py:28
  79.4 6.0 %collective-permute-start.14 = (bf16[64,1792]{1,0:T(8,128)(2,1)S(1)}, bf16[64,1792]{1,0:T(8,128)(2,1)S(1)}, u32[]{:S(2)}, u32[]{:S(2)}) collective-permute-start(bf16[64,1792]{1,0:T(8,128)(2,1)S(1)} %pad_maximum_fusion.1.refs_2_), channel_id=1, source_target_pairs={{0,4},{1,5},{2,6},{3,7},{4,0},{5,1},{6,2},{7,3},{8,12},{9,13},{10,... | collective-permute-start | bytes 688136 | tf_op jit(solution)/shard_map/ppermute | solution.py:28
  89.5 8.4 %collective-permute-start.17 = (bf16[4,144,256]{2,1,0:T(8,128)(2,1)S(1)}, bf16[4,144,256]{2,1,0:T(8,128)(2,1)S(1)}, u32[]{:S(2)}, u32[]{:S(2)}) collective-permute-start(bf16[4,144,256]{2,1,0:T(8,128)(2,1)S(1)} %get-tuple-element.68), channel_id=1, source_target_pairs={{0,2},{1,3},{2,0},{3,1},{4,6},{5,7},{6,4},{7,5},{8,10},{9,11},{10,... | collective-permute-start | bytes 884744 | tf_op jit(solution)/shard_map/ppermute | solution.py:28
  90.0 8.3 %collective-permute-start.18 = (bf16[4,144,256]{2,1,0:T(8,128)(2,1)S(1)}, bf16[4,144,256]{2,1,0:T(8,128)(2,1)S(1)}, u32[]{:S(2)}, u32[]{:S(2)}) collective-permute-start(bf16[4,144,256]{2,1,0:T(8,128)(2,1)S(1)} %get-tuple-element.69), channel_id=1, source_target_pairs={{0,4},{1,5},{2,6},{3,7},{4,0},{5,1},{6,2},{7,3},{8,12},{9,13},{10,... | collective-permute-start | bytes 884744 | tf_op jit(solution)/shard_map/ppermute | solution.py:28
  98.3 5.2 %collective-permute-start.21 = (bf16[2,144,256]{2,1,0:T(8,128)(2,1)S(1)}, bf16[2,144,256]{2,1,0:T(8,128)(2,1)S(1)}, u32[]{:S(2)}, u32[]{:S(2)}) collective-permute-start(bf16[2,144,256]{2,1,0:T(8,128)(2,1)S(1)} %get-tuple-element.92), channel_id=1, source_target_pairs={{0,2},{1,3},{2,0},{3,1},{4,6},{5,7},{6,4},{7,5},{8,10},{9,11},{10,... | collective-permute-start | bytes 442376 | tf_op jit(solution)/shard_map/ppermute | solution.py:28
  100.1 5.2 %collective-permute-start.19 = (bf16[2,144,256]{2,1,0:T(8,128)(2,1)S(1)}, bf16[2,144,256]{2,1,0:T(8,128)(2,1)S(1)}, u32[]{:S(2)}, u32[]{:S(2)}) collective-permute-start(bf16[2,144,256]{2,1,0:T(8,128)(2,1)S(1)} %get-tuple-element.94), channel_id=1, source_target_pairs={{0,4},{1,5},{2,6},{3,7},{4,0},{5,1},{6,2},{7,3},{8,12},{9,13},{10,... | collective-permute-start | bytes 442376 | tf_op jit(solution)/shard_map/ppermute | solution.py:28
  103.6 6.1 %collective-permute-start.22 = (bf16[1,144,256]{2,1,0:T(8,128)(2,1)S(1)}, bf16[1,144,256]{2,1,0:T(8,128)(2,1)S(1)}, u32[]{:S(2)}, u32[]{:S(2)}) collective-permute-start(bf16[1,144,256]{2,1,0:T(8,128)(2,1)S(1)} %get-tuple-element.96), channel_id=1, source_target_pairs={{0,8},{1,9},{2,10},{3,11},{4,12},{5,13},{6,14},{7,15},{8,0},{9,1},... | collective-permute-start | bytes 221192 | tf_op jit(solution)/shard_map/ppermute | solution.py:28
  105.3 6.1 %collective-permute-start.20 = (bf16[1,144,256]{2,1,0:T(8,128)(2,1)S(1)}, bf16[1,144,256]{2,1,0:T(8,128)(2,1)S(1)}, u32[]{:S(2)}, u32[]{:S(2)}) collective-permute-start(bf16[1,144,256]{2,1,0:T(8,128)(2,1)S(1)} %get-tuple-element.98), channel_id=1, source_target_pairs={{0,8},{1,9},{2,10},{3,11},{4,12},{5,13},{6,14},{7,15},{8,0},{9,1},... | collective-permute-start | bytes 221192 | tf_op jit(solution)/shard_map/ppermute | solution.py:28
  112.2 1.3 collective-permute-start.23

commit v12 on v11

--- a/solution.py
+++ b/solution.py
@@ -41,11 +41,6 @@
 def member(at, order):
     last = len(order) - 1
     return sum(bit for i, bit in enumerate(order) if (at >> (last - i)) & 1)
-
-
-def normalize(summed, norm_gain):
-    scale_rows = lax.rsqrt(jnp.mean(summed * summed, 1, keepdims=True) + epsilon)
-    return (summed * scale_rows * norm_gain.astype(jnp.float32)).astype(jnp.bfloat16)
 
 
 def time_embedding(timesteps):
@@ -446,8 +441,84 @@
     )(place, packed, *images, mine, got)
 
 
-def add(one, other, dtype):
-    return (one.astype(jnp.float32) + other.astype(jnp.float32)).astype(dtype)
+def add_kernel(*refs):
+    ins, outs = refs[:4], refs[4:]
+    for lane in range(2):
+        mine, got = ins[2 * lane], ins[2 * lane + 1]
+        half = mine.shape[0] // 2
+        outs[2 * lane][...] = (
+            mine[half:].astype(jnp.float32) + got[half:].astype(jnp.float32)
+        ).astype(jnp.bfloat16)
+        outs[2 * lane + 1][...] = mine[:half].astype(jnp.float32) + got[:half].astype(jnp.float32)
+
+
+def add_halves(mine, got):
+    shape = (mine[0].shape[0] // 2,) + mine[0].shape[1:]
+    outs = (jax.ShapeDtypeStruct(shape, jnp.bfloat16), jax.ShapeDtypeStruct(shape, jnp.float32))
+    sent0, keep0, sent1, keep1 = pl.pallas_call(
+        add_kernel,
+        out_shape=outs * 2,
+        in_specs=[VMEM_SPEC] * 4,
+        out_specs=(VMEM_SPEC,) * 4,
+        compiler_params=params(8),
+        cost_estimate=pl.CostEstimate(
+            flops=2 * mine[0].size, bytes_accessed=12 * mine[0].size, transcendentals=0
+        ),
+        name="add_halves",
+    )(mine[0], got[0], mine[1], got[1])
+    return [sent0, sent1], [keep0, keep1]
+
+
+def norm_kernel(keep0, got0, keep1, got1, gain_ref, out0, out1):
+    totals = [keep0[0] + got0[0].astype(jnp.float32), keep1[0] + got1[0].astype(jnp.float32)]
+    width = totals[0].shape[1]
+    square = sum(jnp.sum(total * total, 1, keepdims=True) for total in totals)
+    scale_rows = lax.rsqrt(square / (2 * width) + epsilon)
+    for lane, (total, out_ref) in enumerate(zip(totals, (out0, out1))):
+        gain = gain_ref[:, lane * width : (lane + 1) * width].astype(jnp.float32)
+        out_ref[...] = (total * scale_rows * gain).astype(out_ref.dtype)
+
+
+def normalize(keep, got, norm_gain):
+    out = jax.ShapeDtypeStruct(keep[0].shape[1:], jnp.bfloat16)
+    return pl.pallas_call(
+        norm_kernel,
+        out_shape=(out, out),
+        in_specs=[VMEM_SPEC] * 5,
+        out_specs=(VMEM_SPEC,) * 2,
+        compiler_params=params(8),
+        cost_estimate=pl.CostEstimate(
+            flops=8 * keep[0].size, bytes_accessed=16 * keep[0].size, transcendentals=0
+        ),
+        name="normalize",
+    )(keep[0], got[0], keep[1], got[1], norm_gain)
+
+
+def join_kernel(mine0, got0, mine1, got1, out0, out1):
+    for mine, got, out_ref in ((mine0, got0, out0), (mine1, got1, out1)):
+        rows = mine.shape[0]
+        if rows % 16:
+            both = [mine[...].astype(jnp.float32), got[...].astype(jnp.float32)]
+            out_ref[...] = jnp.concatenate(both, 0).astype(out_ref.dtype)
+        else:
+            out_ref[:rows, :] = mine[...]
+            out_ref[rows:, :] = got[...]
+
+
+def join(mine, got):
+    rows, width = mine[0].shape
+    out = jax.ShapeDtypeStruct((2 * rows, width), mine[0].dtype)
+    return pl.pallas_call(
+        join_kernel,
+        out_shape=(out, out),
+        in_specs=[VMEM_SPEC] * 4,
+        out_specs=(VMEM_SPEC,) * 2,
+        compiler_params=params(8),
+        cost_estimate=pl.CostEstimate(
+            flops=0, bytes_accessed=16 * rows * width, transcendentals=0
+        ),
+        name="join",
+    )(mine[0], got[0], mine[1], got[1])
 
 
 def local(
@@ -490,33 +561,18 @@
     packed = pack(copies, image_queries[0], image_key_values[0, :, 0], image_key_values[0, :, 1])
     act, packed = tie((enc_act[0].T, packed))
     packed = exchange(packed)
-    keep, sent = [], []
     encoded = encoder(lanes, place, act, down_weight)
-    for own, other in (encoded[:2], encoded[2:]):
-        got = swap(other, 1)
-        sent.append(add(own[chips // 2 :], got[chips // 2 :], jnp.bfloat16))
-        keep.append(add(own[: chips // 2], got[: chips // 2], jnp.float32))
+    keep, got = encoded[::2], [swap(other, 1) for other in encoded[1::2]]
     for step in range(rounds):
+        sent, keep = add_halves(keep, got)
         got = [swap(part, 2 * order[step]) for part, order in zip(sent, lanes)]
         if step == 0:
-            got, packed = tie((got, packed))
+            got, win1, kv1, mod1, packed = tie((got, win1, kv1, mod1, packed))
             lines = modulation(time, mod0, mod1)
         if step == 1:
             got, lines = tie((got, lines))
-        half = keep[0].shape[0] // 2
-        if half:
-            sent = [add(mine[half:], part[half:], jnp.bfloat16) for mine, part in zip(keep, got)]
-            keep = [add(mine[:half], part[:half], jnp.float32) for mine, part in zip(keep, got)]
-    summed = [add(mine[0], part[0], jnp.float32) for mine, part in zip(keep, got)]
-
-    width = summed[0].shape[1]
-    square = sum(jnp.sum(part * part, 1, keepdims=True) for part in summed)
-    scale_rows = lax.rsqrt(square / (2 * width) + epsilon)
-    gains = norm_gain.astype(jnp.float32)
-    states = [
-        (part * scale_rows * gains[lane * width : (lane + 1) * width]).astype(jnp.bfloat16)
-        for lane, part in enumerate(summed)
-    ]
+
+    states = normalize(keep, got, norm_gain[None, :])
     images = []
 
     for step in reversed(range(rounds)):
@@ -525,7 +581,7 @@
             image = image_attention(packed, img_dev, factor, 0, 2)
         got = [swap(state, 2 * order[step]) for state, order in zip(states, lanes)]
         if step:
-            states = [jnp.concatenate(pair, 0) for pair in zip(states, got)]
+            states = join(states, got)
     got, image = tie((got, image))
     images += image
     states = [state for pair in zip(states, got) for state in pair]
@@ -540,10 +596,8 @@
         if step == 0:
             got, image = tie((got, image))
             images += image
-        half = keep[0].shape[0] // 2
-        if half:
-            sent = [add(mine[half:], part[half:], jnp.bfloat16) for mine, part in zip(keep, got)]
-            keep = [add(mine[:half], part[:half], jnp.float32) for mine, part in zip(keep, got)]
+        if step < rounds - 1:
+            sent, keep = add_halves(keep, got)
     parts = [part[0] for pair in zip(keep, got) for part in pair]
     model_width = text_in_weight.shape[1] * devices
     mine, sent = combine(place, parts, chips, text_len // 2, model_width)

time: 139 us -> 140 us (level)
  local copies, waits for them, and re-layouts: 7.42 us -> 14.9 us
  waiting for transfers between devices: 47.2 us -> 40.5 us
  starting transfers between devices: 34.8 us -> 40.4 us
  other arithmetic: 4.92 us -> 0.06 us
    unnamed x16 -> x32, local copies, waits for them, and re-layouts: 5.09 us -> 13.2 us
    ppermute x24, waiting for transfers between devices: 46.6 us -> 40.5 us  [swap(): return lax.ppermute(value, 'seq', [(i, i ^ mask) for i in range(devices)])]
    ppermute x24, starting transfers between devices: 27.3 us -> 32.9 us  [swap(): return lax.ppermute(value, 'seq', [(i, i ^ mask) for i in range(devices)])]
    convert_element_type x9 -> x0, other arithmetic: 2.4 us -> none  [the longest x8 2.3 us: add(): return (one.astype(jnp.float32) + other.astype(jnp.float32)).astype(dtype)]
    add x2 -> x0, other arithmetic: 2.12 us -> none  [add(): return (one.astype(jnp.float32) + other.astype(jnp.float32)).astype(dtype)]
  transfers between devices with their start and end apart: 25 -> 25, of which waited for: 19 -> 19; matrix products, arithmetic and copies ran while one was open for 4% -> 0% of each run, Pallas kernels for 8% -> 8%
where the time goes in v12:
time: 140 us; the launch traced here: 139 us
  waiting for transfers between devices  40.5 us (29%)
  starting transfers between devices  40.4 us (29%)
  blocking collectives  21.6 us (15%)
  Pallas kernels  19.7 us (14%)
  local copies, waits for them, and re-layouts  14.9 us (11%)
  between operations  2.17 us (2%)
    ppermute x24, waiting for transfers between devices, swap(): return lax.ppermute(value, 'seq', [(i, i ^ mask) for i in range(devices)])  40.5 us
    ppermute x24, starting transfers between devices, swap(): return lax.ppermute(value, 'seq', [(i, i ^ mask) for i in range(devices)])  32.9 us
    all_to_all x1, blocking collectives, exchange(): return lax.all_to_all(rows, 'seq', split_axis=0, concat_axis=0, tiled=True)  21.6 us
    unnamed x32, local copies, waits for them, and re-layouts  13.2 us
    all_to_all x1, starting transfers between devices, exchange(): return lax.all_to_all(rows, 'seq', split_axis=0, concat_axis=0, tiled=True)  7.49 us
    pallas_call x2, Pallas kernels, image_attention(): pl.pallas_call(functools.partial(image_kernel, factor, call, img_dev), ou...  7.05 us
    pallas_call x1, Pallas kernels, project(): pl.pallas_call(functools.partial(project_kernel, lanes), out_shape=(out,)...  3.65 us
    pallas_call x1, Pallas kernels, encoder(): pl.pallas_call(functools.partial(encoder_kernel, lanes), out_shape=(out,)...  3.47 us
  transfers between devices with their start and end apart: 25, of which 19 were waited for; matrix products, arithmetic and copies ran while one was open for 0% of the time, Pallas kernels for 8%

profile of v12, /device:TPU:0, one launch (start us, length us, event | category | flops | bytes accessed | tf_op | source)
XLA Modules:
  0.0 139.4 jit_solution(5918301693774534823)
XLA Ops:
  0.6 1.6 %copy.12 = bf16[1,128,2,2048]{3,1,2,0:T(8,128)(2,1)S(1)} copy(bf16[1,128,2,2048]{3,2,1,0:T(2,128)(2,1)} %param.19) | data formatting | bytes 2097152 | tf_op jit(solution)/shard_map/optimization_barrier | solution.py:560
  2.3 1.0 copy-done.4
  3.3 1.4 %pack.1 = bf16[16,384,128]{2,1,0:T(8,128)(2,1)} custom-call(bf16[128,2048]{1,0:T(8,128)(2,1)S(1)} %bitcast.27, bf16[128,2048]{1,0:T(8,128)(2,1)S(1)} %get-tuple-element.141.keys_ref, bf16[128,2048]{1,0:T(8,128)(2,1)S(1)} %get-tuple-element.140.values_ref), custom_call_target="tpu_custom_call" | custom-call | bytes 3145728 | tf_op jit(solution)/shard_map/pack/pallas_call | solution.py:291
  4.7 7.5 %all-to-all-start = ((bf16[16,384,128]{2,1,0:T(8,128)(2,1)}), bf16[16,384,128]{2,1,0:T(8,128)(2,1)S(1)}, u32[]{:S(2)}, u32[]{:S(2)}) async-start(bf16[16,384,128]{2,1,0:T(8,128)(2,1)} %pack.1), calls=%async_computation | async-start | bytes 3145728 | tf_op jit(solution)/shard_map/all_to_all | solution.py:558
  12.2 0.5 collective-permute-start.5
  13.5 3.4 %copy-done = bf16[1184,3584]{1,0:T(8,128)(2,1)S(1)} copy-done((bf16[1184,3584]{1,0:T(8,128)(2,1)S(1)}, bf16[1184,3584]{1,0:T(8,128)(2,1)}, u32[]{:S(2)}) %copy-start) | copy-done | bytes 8486936
  16.9 1.1 copy-done.3
  18.0 3.5 %encoder.1 = (bf16[8,16,1792]{2,1,0:T(8,128)(2,1)S(1)}, bf16[8,16,1792]{2,1,0:T(8,128)(2,1)S(1)}, bf16[8,16,1792]{2,1,0:T(8,128)(2,1)S(1)}, bf16[8,16,1792]{2,1,0:T(8,128)(2,1)S(1)}) custom-call(s32[5]{0:T(128)S(1)} %stack.19.place_ref, bf16[1184,256]{1,0:T(8,128)(2,1)S(1)} %bitcast.26, bf16[1184,3584]{1,0:T(8,128)(2,1)S(1)} %copy-done), custom_call_target="tpu_custom_call" | custom-call | flops 2172649472 | bytes 10928128 | tf_op jit(solution)/shard_map/encoder/pallas_call | solution.py:84
  21.5 0.5 collective-permute-start
  22.0 1.3 collective-permute-done.refs_1_
  23.4 0.7 collective-permute-done.1.refs_3_
  24.0 0.2 add_halves.5
  24.2 0.8 copy-done.5
  25.0 0.8 copy-done.7
  25.8 1.9 %collective-permute-start.2 = (bf16[4,16,1792]{2,1,0:T(8,128)(2,1)S(1)}, bf16[4,16,1792]{2,1,0:T(8,128)(2,1)S(1)}, u32[]{:S(2)}, u32[]{:S(2)}) collective-permute-start(bf16[4,16,1792]{2,1,0:T(8,128)(2,1)S(1)} %get-tuple-element.79), channel_id=1, source_target_pairs={{0,2},{1,3},{2,0},{3,1},{4,6},{5,7},{6,4},{7,5},{8,10},{9,11},{10,... | collective-permute-start | bytes 688136 | tf_op jit(solution)/shard_map/ppermute | solution.py:28
  27.7 1.5 %collective-permute-start.3 = (bf16[4,16,1792]{2,1,0:T(8,128)(2,1)S(1)}, bf16[4,16,1792]{2,1,0:T(8,128)(2,1)S(1)}, u32[]{:S(2)}, u32[]{:S(2)}) collective-permute-start(bf16[4,16,1792]{2,1,0:T(8,128)(2,1)S(1)} %get-tuple-element.80), channel_id=1, source_target_pairs={{0,4},{1,5},{2,6},{3,7},{4,0},{5,1},{6,2},{7,3},{8,12},{9,13},{10,... | collective-permute-start | bytes 688136 | tf_op jit(solution)/shard_map/ppermute | solution.py:28
  29.8 0.8 collective-permute-done.6.mod1_ref
  30.6 0.7 copy-done.13
  31.3 6.0 %collective-permute-done.2.refs_1_ = bf16[4,16,1792]{2,1,0:T(8,128)(2,1)S(1)} collective-permute-done((bf16[4,16,1792]{2,1,0:T(8,128)(2,1)S(1)}, bf16[4,16,1792]{2,1,0:T(8,128)(2,1)S(1)}, u32[]{:S(2)}, u32[]{:S(2)}) %collective-permute-start.2) | collective-permute-done | bytes 229408 | tf_op jit(solution)/shard_map/ppermute | solution.py:28
  37.3 6.4 %collective-permute-done.3.refs_3_ = bf16[4,16,1792]{2,1,0:T(8,128)(2,1)S(1)} collective-permute-done((bf16[4,16,1792]{2,1,0:T(8,128)(2,1)S(1)}, bf16[4,16,1792]{2,1,0:T(8,128)(2,1)S(1)}, u32[]{:S(2)}, u32[]{:S(2)}) %collective-permute-start.3) | collective-permute-done | bytes 229408 | tf_op jit(solution)/shard_map/ppermute | solution.py:28
  43.7 0.7 copy-done.9
  44.4 1.0 copy-done.6
  45.4 1.0 copy-done.8
  46.4 0.9 copy-done.10
  47.4 4.6 %collective-permute-start.7 = (bf16[2,16,1792]{2,1,0:T(8,128)(2,1)S(1)}, bf16[2,16,1792]{2,1,0:T(8,128)(2,1)S(1)}, u32[]{:S(2)}, u32[]{:S(2)}) collective-permute-start(bf16[2,16,1792]{2,1,0:T(8,128)(2,1)S(1)} %get-tuple-element.86), channel_id=1, source_target_pairs={{0,4},{1,5},{2,6},{3,7},{4,0},{5,1},{6,2},{7,3},{8,12},{9,13},{10,... | collective-permute-start | bytes 344072 | tf_op jit(solution)/shard_map/ppermute | solution.py:28
  52.1 2.7 %collective-permute-start.8 = (bf16[2,16,1792]{2,1,0:T(8,128)(2,1)S(1)}, bf16[2,16,1792]{2,1,0:T(8,128)(2,1)S(1)}, u32[]{:S(2)}, u32[]{:S(2)}) collective-permute-start(bf16[2,16,1792]{2,1,0:T(8,128)(2,1)S(1)} %get-tuple-element.87), channel_id=1, source_target_pairs={{0,2},{1,3},{2,0},{3,1},{4,6},{5,7},{6,4},{7,5},{8,10},{9,11},{10,... | collective-permute-start | bytes 344072 | tf_op jit(solution)/shard_map/ppermute | solution.py:28
  54.8 0.9 copy-done.12
  55.8 0.9 copy-done.14
  56.7 0.2 modulation.1.refs_4_
  56.9 1.2 collective-permute-done.8.refs_3_
  58.1 1.5 %collective-permute-start.9 = (bf16[1,16,1792]{2,1,0:T(8,128)(2,1)S(1)}, bf16[1,16,1792]{2,1,0:T(8,128)(2,1)S(1)}, u32[]{:S(2)}, u32[]{:S(2)}) collective-permute-start(bf16[1,16,1792]{2,1,0:T(8,128)(2,1)S(1)} %get-tuple-element.93), channel_id=1, source_target_pairs={{0,8},{1,9},{2,10},{3,11},{4,12},{5,13},{6,14},{7,15},{8,0},{9,1},... | collective-permute-start | bytes 172040 | tf_op jit(solution)/shard_map/ppermute | solution.py:28
  59.6 1.5 %collective-permute-start.10 = (bf16[1,16,1792]{2,1,0:T(8,128)(2,1)S(1)}, bf16[1,16,1792]{2,1,0:T(8,128)(2,1)S(1)}, u32[]{:S(2)}, u32[]{:S(2)}) collective-permute-start(bf16[1,16,1792]{2,1,0:T(8,128)(2,1)S(1)} %get-tuple-element.95), channel_id=1, source_target_pairs={{0,8},{1,9},{2,10},{3,11},{4,12},{5,13},{6,14},{7,15},{8,0},{9,1},... | collective-permute-start | bytes 172040 | tf_op jit(solution)/shard_map/ppermute | solution.py:28
  61.1 3.7 %collective-permute-done.9.got0 = bf16[1,16,1792]{2,1,0:T(8,128)(2,1)S(1)} collective-permute-done((bf16[1,16,1792]{2,1,0:T(8,128)(2,1)S(1)}, bf16[1,16,1792]{2,1,0:T(8,128)(2,1)S(1)}, u32[]{:S(2)}, u32[]{:S(2)}) %collective-permute-start.9) | collective-permute-done | bytes 57376 | tf_op jit(solution)/shard_map/ppermute | solution.py:28
  64.9 0.6 collective-permute-done.10.got1
  65.6 0.9 collective-permute-start.11
  66.5 2.1 %collective-permute-start.12 = (bf16[16,1792]{1,0:T(8,128)(2,1)S(1)}, bf16[16,1792]{1,0:T(8,128)(2,1)S(1)}, u32[]{:S(2)}, u32[]{:S(2)}) collective-permute-start(bf16[16,1792]{1,0:T(8,128)(2,1)S(1)} %get-tuple-element.97.mine1), channel_id=1, source_target_pairs={{0,8},{1,9},{2,10},{3,11},{4,12},{5,13},{6,14},{7,15},{8,0},{9,1},... | collective-permute-start | bytes 172040 | tf_op jit(solution)/shard_map/ppermute | solution.py:28
  68.6 2.2 %collective-permute-done.11.got0 = bf16[16,1792]{1,0:T(8,128)(2,1)S(1)} collective-permute-done((bf16[16,1792]{1,0:T(8,128)(2,1)S(1)}, bf16[16,1792]{1,0:T(8,128)(2,1)S(1)}, u32[]{:S(2)}, u32[]{:S(2)}) %collective-permute-start.11) | collective-permute-done | bytes 57376 | tf_op jit(solution)/shard_map/ppermute | solution.py:28
  70.8 1.2 collective-permute-done.12.got1
  72.0 1.7 %collective-permute-start.13 = (bf16[32,1792]{1,0:T(8,128)(2,1)S(1)}, bf16[32,1792]{1,0:T(8,128)(2,1)S(1)}, u32[]{:S(2)}, u32[]{:S(2)}) collective-permute-start(bf16[32,1792]{1,0:T(8,128)(2,1)S(1)} %get-tuple-element.98.mine0), channel_id=1, source_target_pairs={{0,4},{1,5},{2,6},{3,7},{4,0},{5,1},{6,2},{7,3},{8,12},{9,13},{10,... | collective-permute-start | bytes 344072 | tf_op jit(solution)/shard_map/ppermute | solution.py:28
  73.7 1.5 %collective-permute-start.14 = (bf16[32,1792]{1,0:T(8,128)(2,1)S(1)}, bf16[32,1792]{1,0:T(8,128)(2,1)S(1)}, u32[]{:S(2)}, u32[]{:S(2)}) collective-permute-start(bf16[32,1792]{1,0:T(8,128)(2,1)S(1)} %get-tuple-element.99.mine1), channel_id=1, source_target_pairs={{0,2},{1,3},{2,0},{3,1},{4,6},{5,7},{6,4},{7,5},{8,10},{9,11},{10,... | collective-permute-start | bytes 344072 | tf_op jit(solution)/shard_map/ppermute | solution.py:28
  75.2 1.6 %collective-permute-done.13.got0 = bf16[32,1792]{1,0:T(8,128)(2,1)S(1)} collective-permute-done((bf16[32,1792]{1,0:T(8,128)(2,1)S(1)}, bf16[32,1792]{1,0:T(8,128)(2,1)S(1)}, u32[]{:S(2)}, u32[]{:S(2)}) %collective-permute-start.13) | collective-permute-done | bytes 114720 | tf_op jit(solution)/shard_map/ppermute | solution.py:28
  76.9 1.6 %collective-permute-done.14.got1 = bf16[32,1792]{1,0:T(8,128)(2,1)S(1)} collective-permute-done((bf16[32,1792]{1,0:T(8,128)(2,1)S(1)}, bf16[32,1792]{1,0:T(8,128)(2,1)S(1)}, u32[]{:S(2)}, u32[]{:S(2)}) %collective-permute-start.14) | collective-permute-done | bytes 114720 | tf_op jit(solution)/shard_map/ppermute | solution.py:28
  78.6 1.6 %collective-permute-start.15 = (bf16[64,1792]{1,0:T(8,128)(2,1)S(1)}, bf16[64,1792]{1,0:T(8,128)(2,1)S(1)}, u32[]{:S(2)}, u32[]{:S(2)}) collective-permute-start(bf16[64,1792]{1,0:T(8,128)(2,1)S(1)} %get-tuple-element.103.refs_0_), channel_id=1, source_target_pairs={{0,2},{1,3},{2,0},{3,1},{4,6},{5,7},{6,4},{7,5},{8,10},{9,11},{10,... | collective-permute-start | bytes 688136 | tf_op jit(solution)/shard_map/ppermute | solution.py:28
  80.1 1.9 %collective-permute-start.16 = (bf16[64,1792]{1,0:T(8,128)(2,1)S(1)}, bf16[64,1792]{1,0:T(8,128)(2,1)S(1)}, u32[]{:S(2)}, u32[]{:S(2)}) collective-permute-start(bf16[64,1792]{1,0:T(8,128)(2,1)S(1)} %get-tuple-element.104.refs_2_), channel_id=1, source_target_pairs={{0,4},{1,5},{2,6},{3,7},{4,0},{5,1},{6,2},{7,3},{8,12},{9,13},{10,... | collective-permute-start | bytes 688136 | tf_op jit(solution)/shard_map/ppermute | solution.py:28
  82.0 3.5 %image_attention.2 = (f32[1024,256]{1,0:T(8,128)S(1)}, f32[1024,128]{1,0:T(8,128)S(1)}) custom-call(bf16[16,384,128]{2,1,0:T(8,128)(2,1)S(1)} %all-to-all-done.packed_ref), custom_call_target="tpu_custom_call" | custom-call | flops 1073741824 | bytes 2359296 | tf_op jit(solution)/shard_map/image_attention/pallas_call | solution.py:359
  85.5 0.6 collective-permute-done.16.refs_3_
  86.2 3.7 %project.1 = (bf16[4,144,256]{2,1,0:T(8,128)(2,1)S(1)}, bf16[4,144,256]{2,1,0:T(8,128)(2,1)S(1)}, bf16[4,144,256]{2,1,0:T(8,128)(2,1)S(1)}, bf16[4,144,256]{2,1,0:T(8,128)(2,1)S(1)}) custom-call(s32[5]{0:T(128)S(1)} %stack.19.place_ref, bf16[64,1792]{1,0:T(8,128)(2,1)S(1)} %get-tuple-element.103.refs_0_, ...), custom_call_target="tpu_custom_call" | custom-call | flops 754974720 | bytes 7864320 | tf_op jit(solution)/shard_map/project/pallas_call | solution.py:206
  89.8 0.6 collective-permute-start.17
  90.4 1.4 %collective-permute-start.18 = (bf16[4,144,256]{2,1,0:T(8,128)(2,1)S(1)}, bf16[4,144,256]{2,1,0:T(8,128)(2,1)S(1)}, u32[]{:S(2)}, u32[]{:S(2)}) collective-permute-start(bf16[4,144,256]{2,1,0:T(8,128)(2,1)S(1)} %get-tuple-element.119), channel_id=1, source_target_pairs={{0,4},{1,5},{2,6},{3,7},{4,0},{5,1},{6,2},{7,3},{8,12},{9,13},{10,... | collective-permute-start | bytes 884744 | tf_op jit(solution)/shard_map/ppermute | solution.py:28
  91.8 3.6 %image_attention.3 = (f32[1024,256]{1,0:T(8,128)S(1)}, f32[1024,128]{1,0:T(8,128)S(1)}) custom-call(bf16[16,384,128]{2,1,0:T(8,128)(2,1)S(1)} %all-to-all-done.packed_ref), custom_call_target="tpu_custom_call" | custom-call | flops 1073741824 | bytes 2359296 | tf_op jit(solution)/shard_map/image_attention/pallas_call | solution.py:359
  95.4 1.2 collective-permute-done.17.refs_1_
  96.6 2.1 %collective-permute-done.18.refs_3_ = bf16[4,144,256]{2,1,0:T(8,128)(2,1)S(1)} collective-permute-done((bf16[4,144,256]{2,1,0:T(8,128)(2,1)S(1)}, bf16[4,144,256]{2,1,0:T(8,128)(2,1)S(1)}, u32[]{:S(2)}, u32[]{:S(2)}) %collective-permute-start.18) | collective-permute-done | bytes 294944 | tf_op jit(solution)/shard_map/ppermute | solution.py:28
  98.8 1.4 %collective-permute-start.19 = (bf16[2,144,256]{2,1,0:T(8,128)(2,1)S(1)}, bf16[2,144,256]{2,1,0:T(8,128)(2,1)S(1)}, u32[]{:S(2)}, u32[]{:S(2)}) collective-permute-start(bf16[2,144,256]{2,1,0:T(8,128)(2,1)S(1)} %get-tuple-element.129), channel_id=1, source_target_pairs={{0,4},{1,5},{2,6},{3,7},{4,0},{5,1},{6,2},{7,3},{8,12},{9,13},{10,... | collective-permute-start | bytes 442376 | tf_op jit(solution)/shard_map/ppermute | solution.py:28
  100.2 1.9 %collective-permute-start.20 = (bf16[2,144,256]{2,1,0:T(8,128)(2,1)S(1)}, bf16[2,144,256]{2,1,0:T(8,128)(2,1)S(1)}, u32[]{:S(2)}, u32[]{:S(2)}) collective-permute-start(bf16[2,144,256]{2,1,0:T(8,128)(2,1)S(1)} %get-tuple-element.131), channel_id=1, source_target_pairs={{0,2},{1,3},{2,0},{3,1},{4,6},{5,7},{6,4},{7,5},{8,10},{9,11},{10,... | collective-permute-start | bytes 442376 | tf_op jit(solution)/shard_map/ppermute | solution.py:28
  102.2 3.2 %collective-permute-done.19.refs_1_ = bf16[2,144,256]{2,1,0:T(8,128)(2,1)S(1)} collective-permute-done((bf16[2,144,256]{2,1,0:T(8,128)(2,1)S(1)}, bf16[2,144,256]{2,1,0:T(8,128)(2,1)S(1)}, u32[]{:S(2)}, u32[]{:S(2)}) %collective-permute-start.19) | collective-permute-done | bytes 147488 | tf_op jit(solution)/shard_map/ppermute | solution.py:28
  105.5 1.6 %collective-permute-start.21 = (bf16[1,144,256]{2,1,0:T(8,128)(2,1)S(1)}, bf16[1,144,256]{2,1,0:T(8,128)(2,1)S(1)}, u32[]{:S(2)}, u32[]{:S(2)}) collective-permute-start(bf16[1,144,256]{2,1,0:T(8,128)(2,1)S(1)} %get-tuple-element.133), channel_id=1, source_target_pairs={{0,8},{1,9},{2,10},{3,11},{4,12},{5,13},{6,14},{7,15},{8,0},{9,1},... | collective-permute-start | bytes 221192 | tf_op jit(solution)/shard_map/ppermute | solution.py:28
  107.0 1.4 %collective-permute-start.22 = (bf16[1,144,256]{2,1,0:T(8,128)(2,1)S(1)}, bf16[1,144,256]{2,1,0:T(8,128)(2,1)S(1)}, u32[]{:S(2)}, u32[]{:S(2)}) collective-permute-start(bf16[1,144,256]{2,1,0:T(8,128)(2,1)S(1)} %get-tuple-element.135), channel_id=1, source_target_pairs={{0,8},{1,9},{2,10},{3,11},{4,12},{5,13},{6,14},{7,15},{8,0},{9,1},... | collective-permute-start | bytes 221192 | tf_op jit(solution)/shard_map/ppermute | solution.py:28
  108.5 3.1 %collective-permute-done.21 = bf16[1,144,256]{2,1,0:T(8,128)(2,1)S(1)} collective-permute-done((bf16[1,144,256]{2,1,0:T(8,128)(2,1)S(1)}, bf16[1,144,256]{2,1,0:T(8,128)(2,1)S(1)}, u32[]{:S(2)}, u32[]{:S(2)}) %collective-permute-start.21) | collective-permute-done | bytes 73760 | tf_op jit(solution)/shard_map/ppermute | solution.py:28
  111.6 1.6 %collective-permute-done.22 = bf16[1,144,256]{2,1,0:T(8,128)(2,1)S(1)} collective-permute-done((bf16[1,144,256]{2,1,0:T(8,128)(2,1)S(1)}, bf16[1,144,256]{2,1,0:T(8,128)(2,1)S(1)}, u32[]{:S(2)}, u32[]{:S(2)}) %collective-permute-start.22) | collective-permute-done | bytes 73760 | tf_op jit(solution)/shard_map/ppermute | solution.py:28
  113.1 0.7 combine.1
  114.0 1.2 collective-permute-done.23.refs_5_
  115.2 1.6 %finish.1 = bf16[16,160,128]{2,1,0:T(8,128)(2,1)S(1)} custom-call(s32[5]{0:T(128)S(1)} %stack.19.place_ref, bf16[16,384,128]{2,1,0:T(8,128)(2,1)S(1)} %all-to-all-done.packed_ref, f32[1024,256]{1,0:T(8,128)S(1)} %get-tuple-element.116.refs_0_, f32[1024,128]{1,0:T(8,128)S(1)} %get-tuple-element.117.refs_1_, f32[1024,256]{1,0:T(8,128)S(1)} %get-tuple-element.122.refs_2_, ...), custom_call_target="tpu_custom_call" | custom-call | flops 268435456 | bytes 3145728 | tf_op jit(solution)/shard_map/finish/pallas_call | solution.py:429
  116.8 21.6 %all_to_all.10.blocks_ref = bf16[16,160,128]{2,1,0:T(8,128)(2,1)S(1)} all-to-all(bf16[16,160,128]{2,1,0:T(8,128)(2,1)S(1)} %finish.1), channel_id=1, replica_groups=mesh['dp'=2,'seq'=16] {'seq'}, dimensions={0} | all-to-all | bytes 1310720 | tf_op jit(solution)/shard_map/all_to_all | solution.py:558
  138.4 1.0 unpack.1
  (42 shorter events, 1.1 us)
Async XLA Ops:
  2.2 1.0 copy-start.4
  4.7 7.5 %copy-start.1 = (bf16[192,4096]{1,0:T(8,128)(2,1)S(1)}, bf16[192,4096]{1,0:T(8,128)(2,1)}, u32[]{:S(2)}) copy-start(bf16[192,4096]{1,0:T(8,128)(2,1)} %refs_7_.1) | copy-start | bytes 4718596
  4.7 39.7 %all-to-all-start = ((bf16[16,384,128]{2,1,0:T(8,128)(2,1)}), bf16[16,384,128]{2,1,0:T(8,128)(2,1)S(1)}, u32[]{:S(2)}, u32[]{:S(2)}) async-start(bf16[16,384,128]{2,1,0:T(8,128)(2,1)} %pack.1), calls=%async_computation | async-start | bytes 3145728 | tf_op jit(solution)/shard_map/all_to_all | solution.py:558
  12.2 32.2 %collective-permute-start.5 = (bf16[192,4096]{1,0:T(8,128)(2,1)S(1)}, bf16[192,4096]{1,0:T(8,128)(2,1)}, u32[]{:S(2)}, u32[]{:S(2)}) collective-permute-start(bf16[192,4096]{1,0:T(8,128)(2,1)S(1)} %copy-done.1), channel_id=1, source_target_pairs={{0,1},{1,0},{2,3},{3,2},{4,5},{5,4},{6,7},{7,6},{8,9},{9,8},{10,11... | collective-permute-start | bytes 4718600 | tf_op jit(solution)/shard_map/ppermute | solution.py:28
  12.7 31.7 %collective-permute-start.4 = (bf16[192,3584]{1,0:T(8,128)(2,1)}, bf16[192,3584]{1,0:T(8,128)(2,1)}, u32[]{:S(2)}, u32[]{:S(2)}) collective-permute-start(bf16[192,3584]{1,0:T(8,128)(2,1)} %bitcast.24), channel_id=1, source_target_pairs={{0,1},{1,0},{2,3},{3,2},{4,5},{5,4},{6,7},{7,6},{8,9},{9,8},{10,11... | collective-permute-start | bytes 4128776 | tf_op jit(solution)/shard_map/ppermute | solution.py:28
  13.5 3.4 %copy-start = (bf16[1184,3584]{1,0:T(8,128)(2,1)S(1)}, bf16[1184,3584]{1,0:T(8,128)(2,1)}, u32[]{:S(2)}) copy-start(bf16[1184,3584]{1,0:T(8,128)(2,1)} %weight_ref.1) | copy-start | bytes 25460740
  16.9 1.1 copy-start.3
  21.5 7.7 %copy-start.11 = (bf16[256,2,192]{0,2,1:T(8,128)(2,1)S(1)}, bf16[256,2,192]{0,2,1:T(8,128)(2,1)}, u32[]{:S(2)}) copy-start(bf16[256,2,192]{0,2,1:T(8,128)(2,1)} %param.14) | copy-start | bytes 589828
  21.5 1.9 %collective-permute-start = (bf16[8,16,1792]{2,1,0:T(8,128)(2,1)S(1)}, bf16[8,16,1792]{2,1,0:T(8,128)(2,1)S(1)}, u32[]{:S(2)}, u32[]{:S(2)}) collective-permute-start(bf16[8,16,1792]{2,1,0:T(8,128)(2,1)S(1)} %get-tuple-element.75), channel_id=1, source_target_pairs={{0,1},{1,0},{2,3},{3,2},{4,5},{5,4},{6,7},{7,6},{8,9},{9,8},{10,11... | collective-permute-start | bytes 1376264 | tf_op jit(solution)/shard_map/ppermute | solution.py:28
  21.9 2.1 %collective-permute-start.1 = (bf16[8,16,1792]{2,1,0:T(8,128)(2,1)S(1)}, bf16[8,16,1792]{2,1,0:T(8,128)(2,1)S(1)}, u32[]{:S(2)}, u32[]{:S(2)}) collective-permute-start(bf16[8,16,1792]{2,1,0:T(8,128)(2,1)S(1)} %get-tuple-element.77), channel_id=1, source_target_pairs={{0,1},{1,0},{2,3},{3,2},{4,5},{5,4},{6,7},{7,6},{8,9},{9,8},{10,11... | collective-permute-start | bytes 1376264 | tf_op jit(solution)/shard_map/ppermute | solution.py:28
  24.2 0.8 copy-start.5
  25.0 0.8 copy-start.7
  25.8 35.3 %copy-start.15 = (bf16[3584]{0:T(1024)(128)(2,1)S(1)}, bf16[3584]{0:T(1024)(128)(2,1)}, u32[]{:S(2)}) copy-start(bf16[3584]{0:T(1024)(128)(2,1)} %param.12) | copy-start | bytes 21508
  25.8 11.5 %collective-permute-start.2 = (bf16[4,16,1792]{2,1,0:T(8,128)(2,1)S(1)}, bf16[4,16,1792]{2,1,0:T(8,128)(2,1)S(1)}, u32[]{:S(2)}, u32[]{:S(2)}) collective-permute-start(bf16[4,16,1792]{2,1,0:T(8,128)(2,1)S(1)} %get-tuple-element.79), channel_id=1, source_target_pairs={{0,2},{1,3},{2,0},{3,1},{4,6},{5,7},{6,4},{7,5},{8,10},{9,11},{10,... | collective-permute-start | bytes 688136 | tf_op jit(solution)/shard_map/ppermute | solution.py:28
  27.7 16.0 %collective-permute-start.3 = (bf16[4,16,1792]{2,1,0:T(8,128)(2,1)S(1)}, bf16[4,16,1792]{2,1,0:T(8,128)(2,1)S(1)}, u32[]{:S(2)}, u32[]{:S(2)}) collective-permute-start(bf16[4,16,1792]{2,1,0:T(8,128)(2,1)S(1)} %get-tuple-element.80), channel_id=1, source_target_pairs={{0,4},{1,5},{2,6},{3,7},{4,0},{5,1},{6,2},{7,3},{8,12},{9,13},{10,... | collective-permute-start | bytes 688136 | tf_op jit(solution)/shard_map/ppermute | solution.py:28
  29.2 1.4 %collective-permute-start.6 = (bf16[2,192,256]{2,1,0:T(8,128)(2,1)S(1)}, bf16[2,192,256]{2,1,0:T(8,128)(2,1)S(1)}, u32[]{:S(2)}, u32[]{:S(2)}) collective-permute-start(bf16[2,192,256]{2,1,0:T(8,128)(2,1)S(1)} %bitcast.28), channel_id=1, source_target_pairs={{0,1},{1,0},{2,3},{3,2},{4,5},{5,4},{6,7},{7,6},{8,9},{9,8},{10,11... | collective-permute-start | bytes 589832 | tf_op jit(solution)/shard_map/ppermute | solution.py:28
  30.6 0.7 copy-start.13
  43.7 0.7 copy-start.9
  44.4 1.0 copy-start.6
  45.4 1.0 copy-start.8
  46.4 0.9 copy-start.10
  47.4 9.5 %collective-permute-start.7 = (bf16[2,16,1792]{2,1,0:T(8,128)(2,1)S(1)}, bf16[2,16,1792]{2,1,0:T(8,128)(2,1)S(1)}, u32[]{:S(2)}, u32[]{:S(2)}) collective-permute-start(bf16[2,16,1792]{2,1,0:T(8,128)(2,1)S(1)} %get-tuple-element.86), channel_id=1, source_target_pairs={{0,4},{1,5},{2,6},{3,7},{4,0},{5,1},{6,2},{7,3},{8,12},{9,13},{10,... | collective-permute-start | bytes 344072 | tf_op jit(solution)/shard_map/ppermute | solution.py:28
  52.1 6.0 %collective-permute-start.8 = (bf16[2,16,1792]{2,1,0:T(8,128)(2,1)S(1)}, bf16[2,16,1792]{2,1,0:T(8,128)(2,1)S(1)}, u32[]{:S(2)}, u32[]{:S(2)}) collective-permute-start(bf16[2,16,1792]{2,1,0:T(8,128)(2,1)S(1)} %get-tuple-element.87), channel_id=1, source_target_pairs={{0,2},{1,3},{2,0},{3,1},{4,6},{5,7},{6,4},{7,5},{8,10},{9,11},{10,... | collective-permute-start | bytes 344072 | tf_op jit(solution)/shard_map/ppermute | solution.py:28
  54.8 0.9 copy-start.12
  55.8 0.9 copy-start.14
  58.1 6.7 %collective-permute-start.9 = (bf16[1,16,1792]{2,1,0:T(8,128)(2,1)S(1)}, bf16[1,16,1792]{2,1,0:T(8,128)(2,1)S(1)}, u32[]{:S(2)}, u32[]{:S(2)}) collective-permute-start(bf16[1,16,1792]{2,1,0:T(8,128)(2,1)S(1)} %get-tuple-element.93), channel_id=1, source_target_pairs={{0,8},{1,9},{2,10},{3,11},{4,12},{5,13},{6,14},{7,15},{8,0},{9,1},... | collective-permute-start | bytes 172040 | tf_op jit(solution)/shard_map/ppermute | solution.py:28
  59.6 5.9 %collective-permute-start.10 = (bf16[1,16,1792]{2,1,0:T(8,128)(2,1)S(1)}, bf16[1,16,1792]{2,1,0:T(8,128)(2,1)S(1)}, u32[]{:S(2)}, u32[]{:S(2)}) collective-permute-start(bf16[1,16,1792]{2,1,0:T(8,128)(2,1)S(1)} %get-tuple-element.95), channel_id=1, source_target_pairs={{0,8},{1,9},{2,10},{3,11},{4,12},{5,13},{6,14},{7,15},{8,0},{9,1},... | collective-permute-start | bytes 172040 | tf_op jit(solution)/shard_map/ppermute | solution.py:28
  65.6 5.2 %collective-permute-start.11 = (bf16[16,1792]{1,0:T(8,128)(2,1)S(1)}, bf16[16,1792]{1,0:T(8,128)(2,1)S(1)}, u32[]{:S(2)}, u32[]{:S(2)}) collective-permute-start(bf16[16,1792]{1,0:T(8,128)(2,1)S(1)} %get-tuple-element.96.mine0), channel_id=1, source_target_pairs={{0,8},{1,9},{2,10},{3,11},{4,12},{5,13},{6,14},{7,15},{8,0},{9,1},... | collective-permute-start | bytes 172040 | tf_op jit(solution)/shard_map/ppermute | solution.py:28
  66.5 5.5 %collective-permute-start.12 = (bf16[16,1792]{1,0:T(8,128)(2,1)S(1)}, bf16[16,1792]{1,0:T(8,128)(2,1)S(1)}, u32[]{:S(2)}, u32[]{:S(2)}) collective-permute-start(bf16[16,1792]{1,0:T(8,128)(2,1)S(1)} %get-tuple-element.97.mine1), channel_id=1, source_target_pairs={{0,8},{1,9},{2,10},{3,11},{4,12},{5,13},{6,14},{7,15},{8,0},{9,1},... | collective-permute-start | bytes 172040 | tf_op jit(solution)/shard_map/ppermute | solution.py:28
  72.0 4.9 %collective-permute-start.13 = (bf16[32,1792]{1,0:T(8,128)(2,1)S(1)}, bf16[32,1792]{1,0:T(8,128)(2,1)S(1)}, u32[]{:S(2)}, u32[]{:S(2)}) collective-permute-start(bf16[32,1792]{1,0:T(8,128)(2,1)S(1)} %get-tuple-element.98.mine0), channel_id=1, source_target_pairs={{0,4},{1,5},{2,6},{3,7},{4,0},{5,1},{6,2},{7,3},{8,12},{9,13},{10,... | collective-permute-start | bytes 344072 | tf_op jit(solution)/shard_map/ppermute | solution.py:28
  73.7 4.8 %collective-permute-start.14 = (bf16[32,1792]{1,0:T(8,128)(2,1)S(1)}, bf16[32,1792]{1,0:T(8,128)(2,1)S(1)}, u32[]{:S(2)}, u32[]{:S(2)}) collective-permute-start(bf16[32,1792]{1,0:T(8,128)(2,1)S(1)} %get-tuple-element.99.mine1), channel_id=1, source_target_pairs={{0,2},{1,3},{2,0},{3,1},{4,6},{5,7},{6,4},{7,5},{8,10},{9,11},{10,... | collective-permute-start | bytes 344072 | tf_op jit(solution)/shard_map/ppermute | solution.py:28
  78.5 7.6 %copy-start.2 = (bf16[3584,192]{0,1:T(8,128)(2,1)S(1)}, bf16[3584,192]{0,1:T(8,128)(2,1)}, u32[]{:S(2)}) copy-start(bf16[3584,192]{0,1:T(8,128)(2,1)} %param.13) | copy-start | bytes 4128772
  78.6 7.0 %collective-permute-start.15 = (bf16[64,1792]{1,0:T(8,128)(2,1)S(1)}, bf16[64,1792]{1,0:T(8,128)(2,1)S(1)}, u32[]{:S(2)}, u32[]{:S(2)}) collective-permute-start(bf16[64,1792]{1,0:T(8,128)(2,1)S(1)} %get-tuple-element.103.refs_0_), channel_id=1, source_target_pairs={{0,2},{1,3},{2,0},{3,1},{4,6},{5,7},{6,4},{7,5},{8,10},{9,11},{10,... | collective-permute-start | bytes 688136 | tf_op jit(solution)/shard_map/ppermute | solution.py:28
  80.1 6.0 %collective-permute-start.16 = (bf16[64,1792]{1,0:T(8,128)(2,1)S(1)}, bf16[64,1792]{1,0:T(8,128)(2,1)S(1)}, u32[]{:S(2)}, u32[]{:S(2)}) collective-permute-start(bf16[64,1792]{1,0:T(8,128)(2,1)S(1)} %get-tuple-element.104.refs_2_), channel_id=1, source_target_pairs={{0,4},{1,5},{2,6},{3,7},{4,0},{5,1},{6,2},{7,3},{8,12},{9,13},{10,... | collective-permute-start | bytes 688136 | tf_op jit(solution)/shard_map/ppermute | solution.py:28
  89.8 6.8 %collective-permute-start.17 = (bf16[4,144,256]{2,1,0:T(8,128)(2,1)S(1)}, bf16[4,144,256]{2,1,0:T(8,128)(2,1)S(1)}, u32[]{:S(2)}, u32[]{:S(2)}) collective-permute-start(bf16[4,144,256]{2,1,0:T(8,128)(2,1)S(1)} %get-tuple-element.118), channel_id=1, source_target_pairs={{0,2},{1,3},{2,0},{3,1},{4,6},{5,7},{6,4},{7,5},{8,10},{9,11},{10,... | collective-permute-start | bytes 884744 | tf_op jit(solution)/shard_map/ppermute | solution.py:28
  90.4 8.3 %collective-permute-start.18 = (bf16[4,144,256]{2,1,0:T(8,128)(2,1)S(1)}, bf16[4,144,256]{2,1,0:T(8,128)(2,1)S(1)}, u32[]{:S(2)}, u32[]{:S(2)}) collective-permute-start(bf16[4,144,256]{2,1,0:T(8,128)(2,1)S(1)} %get-tuple-element.119), channel_id=1, source_target_pairs={{0,4},{1,5},{2,6},{3,7},{4,0},{5,1},{6,2},{7,3},{8,12},{9,13},{10,... | collective-permute-start | bytes 884744 | tf_op jit(solution)/shard_map/ppermute | solution.py:28
  98.8 6.6 %collective-permute-start.19 = (bf16[2,144,256]{2,1,0:T(8,128)(2,1)S(1)}, bf16[2,144,256]{2,1,0:T(8,128)(2,1)S(1)}, u32[]{:S(2)}, u32[]{:S(2)}) collective-permute-start(bf16[2,144,256]{2,1,0:T(8,128)(2,1)S(1)} %get-tuple-element.129), channel_id=1, source_target_pairs={{0,4},{1,5},{2,6},{3,7},{4,0},{5,1},{6,2},{7,3},{8,12},{9,13},{10,... | collective-permute-start | bytes 442376 | tf_op jit(solution)/shard_map/ppermute | solution.py:28
  100.2 5.2 %collective-permute-start.20 = (bf16[2,144,256]{2,1,0:T(8,128)(2,1)S(1)}, bf16[2,144,256]{2,1,0:T(8,128)(2,1)S(1)}, u32[]{:S(2)}, u32[]{:S(2)}) collective-permute-start(bf16[2,144,256]{2,1,0:T(8,128)(2,1)S(1)} %get-tuple-element.131), channel_id=1, source_target_pairs={{0,2},{1,3},{2,0},{3,1},{4,6},{5,7},{6,4},{7,5},{8,10},{9,11},{10,... | collective-permute-start | bytes 442376 | tf_op jit(solution)/shard_map/ppermute | solution.py:28
  105.5 6.1 %collective-permute-start.21 = (bf16[1,144,256]{2,1,0:T(8,128)(2,1)S(1)}, bf16[1,144,256]{2,1,0:T(8,128)(2,1)S(1)}, u32[]{:S(2)}, u32[]{:S(2)}) collective-permute-start(bf16[1,144,256]{2,1,0:T(8,128)(2,1)S(1)} %get-tuple-element.133), channel_id=1, source_target_pairs={{0,8},{1,9},{2,10},{3,11},{4,12},{5,13},{6,14},{7,15},{8,0},{9,1},... | collective-permute-start | bytes 221192 | tf_op jit(solution)/shard_map/ppermute | solution.py:28
  107.0 6.1 %collective-permute-start.22 = (bf16[1,144,256]{2,1,0:T(8,128)(2,1)S(1)}, bf16[1,144,256]{2,1,0:T(8,128)(2,1)S(1)}, u32[]{:S(2)}, u32[]{:S(2)}) collective-permute-start(bf16[1,144,256]{2,1,0:T(8,128)(2,1)S(1)} %get-tuple-element.135), channel_id=1, source_target_pairs={{0,8},{1,9},{2,10},{3,11},{4,12},{5,13},{6,14},{7,15},{8,0},{9,1},... | collective-permute-start | bytes 221192 | tf_op jit(solution)/shard_map/ppermute | solution.py:28
  113.9 1.3 collective-permute-start.23

commit v13 on v12

--- a/solution.py
+++ b/solution.py
@@ -87,7 +87,7 @@
         in_specs=[SMEM_SPEC, VMEM_SPEC, VMEM_SPEC],
         out_specs=(VMEM_SPEC,) * 4,
         scratch_shapes=[pltpu.VMEM((rows, depth), jnp.bfloat16)],
-        compiler_params=params(24),
+        compiler_params=params(16),
         cost_estimate=pl.CostEstimate(
             flops=2 * rows * depth * width,
             bytes_accessed=2 * (depth * rows + depth * width + rows * width),
@@ -119,7 +119,7 @@
         out_shape=jax.ShapeDtypeStruct((2, 16, mod0.shape[1]), jnp.float32),
         in_specs=[VMEM_SPEC] * 3,
         out_specs=VMEM_SPEC,
-        compiler_params=params(8),
+        compiler_params=params(4),
         name="modulation",
     )(time, mod0, mod1)
 
@@ -214,7 +214,7 @@
             pltpu.VMEM((rows, features), jnp.float32),
             pltpu.VMEM((rows, 128), jnp.float32),
         ],
-        compiler_params=params(20),
+        compiler_params=params(14),
         cost_estimate=pl.CostEstimate(
             flops=4 * rows * features * (depth + total),
             bytes_accessed=2 * (rows * depth + 2 * features * (depth + total) + rows * total),
@@ -266,7 +266,7 @@
         out_shape=(out, out),
         in_specs=[SMEM_SPEC] + [VMEM_SPEC] * 4,
         out_specs=(VMEM_SPEC, VMEM_SPEC),
-        compiler_params=params(8),
+        compiler_params=params(4),
         cost_estimate=pl.CostEstimate(
             flops=8 * rows * 512, bytes_accessed=12 * rows * 512, transcendentals=0
         ),
@@ -326,7 +326,7 @@
         ),
         in_specs=[VMEM_SPEC],
         out_specs=(VMEM_SPEC, VMEM_SPEC),
-        compiler_params=params(8),
+        compiler_params=params(4),
         name="unpack",
     )(blocks)
 
@@ -368,7 +368,7 @@
             pltpu.VMEM((total, HEAD_DIM), jnp.bfloat16),
             pltpu.VMEM((total, 2 * HEAD_DIM), jnp.bfloat16),
         ],
-        compiler_params=params(24),
+        compiler_params=params(14),
         cost_estimate=pl.CostEstimate(
             flops=4 * count * total * HEAD_DIM,
             bytes_accessed=4 * total * HEAD_DIM + 10 * count * HEAD_DIM,
@@ -431,7 +431,7 @@
         out_shape=jax.ShapeDtypeStruct((devices, part_rows + 2 * share, HEAD_DIM), jnp.bfloat16),
         in_specs=[SMEM_SPEC] + [VMEM_SPEC] * (len(images) + 3),
         out_specs=VMEM_SPEC,
-        compiler_params=params(16),
+        compiler_params=params(10),
         cost_estimate=pl.CostEstimate(
             flops=4 * count * 2 * mine.shape[0] * HEAD_DIM,
             bytes_accessed=12 * count * HEAD_DIM,
@@ -460,7 +460,7 @@
         out_shape=outs * 2,
         in_specs=[VMEM_SPEC] * 4,
         out_specs=(VMEM_SPEC,) * 4,
-        compiler_params=params(8),
+        compiler_params=params(6),
         cost_estimate=pl.CostEstimate(
             flops=2 * mine[0].size, bytes_accessed=12 * mine[0].size, transcendentals=0
         ),
@@ -486,7 +486,7 @@
         out_shape=(out, out),
         in_specs=[VMEM_SPEC] * 5,
         out_specs=(VMEM_SPEC,) * 2,
-        compiler_params=params(8),
+        compiler_params=params(4),
         cost_estimate=pl.CostEstimate(
             flops=8 * keep[0].size, bytes_accessed=16 * keep[0].size, transcendentals=0
         ),
@@ -513,7 +513,7 @@
         out_shape=(out, out),
         in_specs=[VMEM_SPEC] * 4,
         out_specs=(VMEM_SPEC,) * 2,
-        compiler_params=params(8),
+        compiler_params=params(4),
         cost_estimate=pl.CostEstimate(
             flops=0, bytes_accessed=16 * rows * width, transcendentals=0
         ),
@@ -548,7 +548,6 @@
 
     win0, kv0 = text_in_weight.T, key_value_weight
     mod0 = modulation_weight.transpose(1, 2, 0)
-    win1, kv1, mod1 = swap(win0, 1), swap(kv0, 1), swap(mod0, 1)
     time = time_embedding(timesteps)
 
     rounds = len(lanes[0])
@@ -567,19 +566,25 @@
         sent, keep = add_halves(keep, got)
         got = [swap(part, 2 * order[step]) for part, order in zip(sent, lanes)]
         if step == 0:
-            got, win1, kv1, mod1, packed = tie((got, win1, kv1, mod1, packed))
-            lines = modulation(time, mod0, mod1)
-        if step == 1:
-            got, lines = tie((got, lines))
+            got, packed = tie((got, packed))
 
     states = normalize(keep, got, norm_gain[None, :])
     images = []
 
     for step in reversed(range(rounds)):
+        if step == rounds - 1:
+            states, held, mod1 = tie((states, win0, mod0))
+            win1, mod1 = swap(held, 1), swap(mod1, 1)
+        if step == rounds - 2:
+            states, held = tie((states, kv0))
+            kv1 = swap(held, 1)
+            lines = modulation(time, mod0, mod1)
         if step == 0:
             states, packed = tie((states, packed))
             image = image_attention(packed, img_dev, factor, 0, 2)
         got = [swap(state, 2 * order[step]) for state, order in zip(states, lanes)]
+        if step == rounds - 2:
+            got, lines = tie((got, lines))
         if step:
             states = join(states, got)
     got, image = tie((got, image))

time: 140 us -> 140 us (level)
  waiting for transfers between devices: 40.5 us -> 46.2 us
  local copies, waits for them, and re-layouts: 14.9 us -> 11.4 us
    ppermute x24, waiting for transfers between devices: 40.5 us -> 46.2 us  [swap(): return lax.ppermute(value, 'seq', [(i, i ^ mask) for i in range(devices)])]
    unnamed x32 -> x26, local copies, waits for them, and re-layouts: 13.2 us -> 9.6 us
  transfers between devices with their start and end apart: 25 -> 25, of which waited for: 19 -> 22; matrix products, arithmetic and copies ran while one was open for 0% -> 0% of each run, Pallas kernels for 8% -> 8%
where the time goes in v13:
time: 140 us
  waiting for transfers between devices  46.2 us (33%)
  starting transfers between devices  40 us (29%)
  blocking collectives  21.8 us (16%)
  Pallas kernels  18.4 us (13%)
  local copies, waits for them, and re-layouts  11.4 us (8%)
  between operations  2.16 us (2%)
    ppermute x24, waiting for transfers between devices, swap(): return lax.ppermute(value, 'seq', [(i, i ^ mask) for i in range(devices)])  46.2 us
    ppermute x24, starting transfers between devices, swap(): return lax.ppermute(value, 'seq', [(i, i ^ mask) for i in range(devices)])  32.5 us
    all_to_all x1, blocking collectives, exchange(): return lax.all_to_all(rows, 'seq', split_axis=0, concat_axis=0, tiled=True)  21.8 us
    unnamed x26, local copies, waits for them, and re-layouts  9.6 us
    all_to_all x1, starting transfers between devices, exchange(): return lax.all_to_all(rows, 'seq', split_axis=0, concat_axis=0, tiled=True)  7.49 us
    pallas_call x2, Pallas kernels, image_attention(): pl.pallas_call(functools.partial(image_kernel, factor, call, img_dev), ou...  6.95 us
    pallas_call x1, Pallas kernels, encoder(): pl.pallas_call(functools.partial(encoder_kernel, lanes), out_shape=(out,)...  3.49 us
  transfers between devices with their start and end apart: 25, of which 22 were waited for; matrix products, arithmetic and copies ran while one was open for 0% of the time, Pallas kernels for 8%

profile of v13, /device:TPU:0, one launch (start us, length us, event | category | flops | bytes accessed | tf_op | source)
XLA Modules:
  0.0 140.0 jit_solution(11418239057515467733)
XLA Ops:
  0.6 1.6 %copy.12 = bf16[1,128,2,2048]{3,1,2,0:T(8,128)(2,1)S(1)} copy(bf16[1,128,2,2048]{3,2,1,0:T(2,128)(2,1)} %param.19) | data formatting | bytes 2097152 | tf_op jit(solution)/shard_map/optimization_barrier | solution.py:559
  2.3 0.9 copy-done.4
  3.3 1.4 %pack.1 = bf16[16,384,128]{2,1,0:T(8,128)(2,1)} custom-call(bf16[128,2048]{1,0:T(8,128)(2,1)S(1)} %bitcast.27, bf16[128,2048]{1,0:T(8,128)(2,1)S(1)} %get-tuple-element.149.keys_ref, bf16[128,2048]{1,0:T(8,128)(2,1)S(1)} %get-tuple-element.148.values_ref), custom_call_target="tpu_custom_call" | custom-call | bytes 3145728 | tf_op jit(solution)/shard_map/pack/pallas_call | solution.py:291
  4.7 7.5 %all-to-all-start = ((bf16[16,384,128]{2,1,0:T(8,128)(2,1)}), bf16[16,384,128]{2,1,0:T(8,128)(2,1)S(1)}, u32[]{:S(2)}, u32[]{:S(2)}) async-start(bf16[16,384,128]{2,1,0:T(8,128)(2,1)} %pack.1), calls=%async_computation | async-start | bytes 3145728 | tf_op jit(solution)/shard_map/all_to_all | solution.py:557
  13.0 3.4 %copy-done = bf16[1184,3584]{1,0:T(8,128)(2,1)S(1)} copy-done((bf16[1184,3584]{1,0:T(8,128)(2,1)S(1)}, bf16[1184,3584]{1,0:T(8,128)(2,1)}, u32[]{:S(2)}) %copy-start) | copy-done | bytes 8486936
  16.4 3.5 %encoder.1 = (bf16[8,16,1792]{2,1,0:T(8,128)(2,1)S(1)}, bf16[8,16,1792]{2,1,0:T(8,128)(2,1)S(1)}, bf16[8,16,1792]{2,1,0:T(8,128)(2,1)S(1)}, bf16[8,16,1792]{2,1,0:T(8,128)(2,1)S(1)}) custom-call(s32[5]{0:T(128)S(1)} %stack.19.place_ref, bf16[1184,256]{1,0:T(8,128)(2,1)S(1)} %bitcast.26, bf16[1184,3584]{1,0:T(8,128)(2,1)S(1)} %copy-done), custom_call_target="tpu_custom_call" | custom-call | flops 2172649472 | bytes 10928128 | tf_op jit(solution)/shard_map/encoder/pallas_call | solution.py:84
  19.9 0.5 collective-permute-start
  20.4 1.3 collective-permute-done.refs_1_
  21.8 0.7 collective-permute-done.1.refs_3_
  22.4 0.2 add_halves.5
  22.6 0.8 copy-done.5
  23.4 0.8 copy-done.7
  24.2 1.9 %collective-permute-start.2 = (bf16[4,16,1792]{2,1,0:T(8,128)(2,1)S(1)}, bf16[4,16,1792]{2,1,0:T(8,128)(2,1)S(1)}, u32[]{:S(2)}, u32[]{:S(2)}) collective-permute-start(bf16[4,16,1792]{2,1,0:T(8,128)(2,1)S(1)} %get-tuple-element.83), channel_id=1, source_target_pairs={{0,2},{1,3},{2,0},{3,1},{4,6},{5,7},{6,4},{7,5},{8,10},{9,11},{10,... | collective-permute-start | bytes 688136 | tf_op jit(solution)/shard_map/ppermute | solution.py:28
  26.1 1.5 %collective-permute-start.3 = (bf16[4,16,1792]{2,1,0:T(8,128)(2,1)S(1)}, bf16[4,16,1792]{2,1,0:T(8,128)(2,1)S(1)}, u32[]{:S(2)}, u32[]{:S(2)}) collective-permute-start(bf16[4,16,1792]{2,1,0:T(8,128)(2,1)S(1)} %get-tuple-element.84), channel_id=1, source_target_pairs={{0,4},{1,5},{2,6},{3,7},{4,0},{5,1},{6,2},{7,3},{8,12},{9,13},{10,... | collective-permute-start | bytes 688136 | tf_op jit(solution)/shard_map/ppermute | solution.py:28
  27.5 9.6 %collective-permute-done.2.refs_1_ = bf16[4,16,1792]{2,1,0:T(8,128)(2,1)S(1)} collective-permute-done((bf16[4,16,1792]{2,1,0:T(8,128)(2,1)S(1)}, bf16[4,16,1792]{2,1,0:T(8,128)(2,1)S(1)}, u32[]{:S(2)}, u32[]{:S(2)}) %collective-permute-start.2) | collective-permute-done | bytes 229408 | tf_op jit(solution)/shard_map/ppermute | solution.py:28
  37.1 6.6 %collective-permute-done.3.refs_3_ = bf16[4,16,1792]{2,1,0:T(8,128)(2,1)S(1)} collective-permute-done((bf16[4,16,1792]{2,1,0:T(8,128)(2,1)S(1)}, bf16[4,16,1792]{2,1,0:T(8,128)(2,1)S(1)}, u32[]{:S(2)}, u32[]{:S(2)}) %collective-permute-start.3) | collective-permute-done | bytes 229408 | tf_op jit(solution)/shard_map/ppermute | solution.py:28
  43.7 0.7 copy-done.9
  44.4 1.0 copy-done.6
  45.4 1.0 copy-done.8
  46.4 0.9 copy-done.10
  47.4 4.7 %collective-permute-start.4 = (bf16[2,16,1792]{2,1,0:T(8,128)(2,1)S(1)}, bf16[2,16,1792]{2,1,0:T(8,128)(2,1)S(1)}, u32[]{:S(2)}, u32[]{:S(2)}) collective-permute-start(bf16[2,16,1792]{2,1,0:T(8,128)(2,1)S(1)} %get-tuple-element.90), channel_id=1, source_target_pairs={{0,4},{1,5},{2,6},{3,7},{4,0},{5,1},{6,2},{7,3},{8,12},{9,13},{10,... | collective-permute-start | bytes 344072 | tf_op jit(solution)/shard_map/ppermute | solution.py:28
  52.1 2.7 %collective-permute-start.5 = (bf16[2,16,1792]{2,1,0:T(8,128)(2,1)S(1)}, bf16[2,16,1792]{2,1,0:T(8,128)(2,1)S(1)}, u32[]{:S(2)}, u32[]{:S(2)}) collective-permute-start(bf16[2,16,1792]{2,1,0:T(8,128)(2,1)S(1)} %get-tuple-element.92), channel_id=1, source_target_pairs={{0,2},{1,3},{2,0},{3,1},{4,6},{5,7},{6,4},{7,5},{8,10},{9,11},{10,... | collective-permute-start | bytes 344072 | tf_op jit(solution)/shard_map/ppermute | solution.py:28
  54.8 1.2 collective-permute-done.4.refs_1_
  56.0 2.1 %collective-permute-done.5.refs_3_ = bf16[2,16,1792]{2,1,0:T(8,128)(2,1)S(1)} collective-permute-done((bf16[2,16,1792]{2,1,0:T(8,128)(2,1)S(1)}, bf16[2,16,1792]{2,1,0:T(8,128)(2,1)S(1)}, u32[]{:S(2)}, u32[]{:S(2)}) %collective-permute-start.5) | collective-permute-done | bytes 114720 | tf_op jit(solution)/shard_map/ppermute | solution.py:28
  58.2 1.5 %collective-permute-start.6 = (bf16[1,16,1792]{2,1,0:T(8,128)(2,1)S(1)}, bf16[1,16,1792]{2,1,0:T(8,128)(2,1)S(1)}, u32[]{:S(2)}, u32[]{:S(2)}) collective-permute-start(bf16[1,16,1792]{2,1,0:T(8,128)(2,1)S(1)} %get-tuple-element.94), channel_id=1, source_target_pairs={{0,8},{1,9},{2,10},{3,11},{4,12},{5,13},{6,14},{7,15},{8,0},{9,1},... | collective-permute-start | bytes 172040 | tf_op jit(solution)/shard_map/ppermute | solution.py:28
  59.6 1.5 %collective-permute-start.7 = (bf16[1,16,1792]{2,1,0:T(8,128)(2,1)S(1)}, bf16[1,16,1792]{2,1,0:T(8,128)(2,1)S(1)}, u32[]{:S(2)}, u32[]{:S(2)}) collective-permute-start(bf16[1,16,1792]{2,1,0:T(8,128)(2,1)S(1)} %get-tuple-element.96), channel_id=1, source_target_pairs={{0,8},{1,9},{2,10},{3,11},{4,12},{5,13},{6,14},{7,15},{8,0},{9,1},... | collective-permute-start | bytes 172040 | tf_op jit(solution)/shard_map/ppermute | solution.py:28
  61.2 3.7 %collective-permute-done.6.got0 = bf16[1,16,1792]{2,1,0:T(8,128)(2,1)S(1)} collective-permute-done((bf16[1,16,1792]{2,1,0:T(8,128)(2,1)S(1)}, bf16[1,16,1792]{2,1,0:T(8,128)(2,1)S(1)}, u32[]{:S(2)}, u32[]{:S(2)}) %collective-permute-start.6) | collective-permute-done | bytes 57376 | tf_op jit(solution)/shard_map/ppermute | solution.py:28
  64.9 0.6 collective-permute-done.7.got1
  65.7 0.9 collective-permute-start.8
  66.5 2.1 %collective-permute-start.9 = (bf16[16,1792]{1,0:T(8,128)(2,1)S(1)}, bf16[16,1792]{1,0:T(8,128)(2,1)S(1)}, u32[]{:S(2)}, u32[]{:S(2)}) collective-permute-start(bf16[16,1792]{1,0:T(8,128)(2,1)S(1)} %get-tuple-element.100.mine1), channel_id=1, source_target_pairs={{0,8},{1,9},{2,10},{3,11},{4,12},{5,13},{6,14},{7,15},{8,0},{9,1},... | collective-permute-start | bytes 172040 | tf_op jit(solution)/shard_map/ppermute | solution.py:28
  68.6 2.2 %collective-permute-done.8.got0 = bf16[16,1792]{1,0:T(8,128)(2,1)S(1)} collective-permute-done((bf16[16,1792]{1,0:T(8,128)(2,1)S(1)}, bf16[16,1792]{1,0:T(8,128)(2,1)S(1)}, u32[]{:S(2)}, u32[]{:S(2)}) %collective-permute-start.8) | collective-permute-done | bytes 57376 | tf_op jit(solution)/shard_map/ppermute | solution.py:28
  70.8 1.2 collective-permute-done.9.got1
  72.1 0.5 collective-permute-start.15
  73.3 0.1 collective-permute-start.12
  73.4 1.6 %collective-permute-start.10 = (bf16[32,1792]{1,0:T(8,128)(2,1)S(1)}, bf16[32,1792]{1,0:T(8,128)(2,1)S(1)}, u32[]{:S(2)}, u32[]{:S(2)}) collective-permute-start(bf16[32,1792]{1,0:T(8,128)(2,1)S(1)} %get-tuple-element.103.mine0), channel_id=1, source_target_pairs={{0,4},{1,5},{2,6},{3,7},{4,0},{5,1},{6,2},{7,3},{8,12},{9,13},{10,... | collective-permute-start | bytes 344072 | tf_op jit(solution)/shard_map/ppermute | solution.py:28
  75.1 1.5 %collective-permute-start.11 = (bf16[32,1792]{1,0:T(8,128)(2,1)S(1)}, bf16[32,1792]{1,0:T(8,128)(2,1)S(1)}, u32[]{:S(2)}, u32[]{:S(2)}) collective-permute-start(bf16[32,1792]{1,0:T(8,128)(2,1)S(1)} %get-tuple-element.104.mine1), channel_id=1, source_target_pairs={{0,2},{1,3},{2,0},{3,1},{4,6},{5,7},{6,4},{7,5},{8,10},{9,11},{10,... | collective-permute-start | bytes 344072 | tf_op jit(solution)/shard_map/ppermute | solution.py:28
  76.7 0.9 collective-permute-done.12.mod1_ref
  77.6 0.2 modulation.1.refs_4_
  77.8 1.2 collective-permute-done.10.got0
  78.9 1.4 collective-permute-done.11.got1
  80.3 1.7 %collective-permute-start.13 = (bf16[64,1792]{1,0:T(8,128)(2,1)S(1)}, bf16[64,1792]{1,0:T(8,128)(2,1)S(1)}, u32[]{:S(2)}, u32[]{:S(2)}) collective-permute-start(bf16[64,1792]{1,0:T(8,128)(2,1)S(1)} %get-tuple-element.111.refs_0_), channel_id=1, source_target_pairs={{0,2},{1,3},{2,0},{3,1},{4,6},{5,7},{6,4},{7,5},{8,10},{9,11},{10,... | collective-permute-start | bytes 688136 | tf_op jit(solution)/shard_map/ppermute | solution.py:28
  82.1 1.7 %collective-permute-start.14 = (bf16[64,1792]{1,0:T(8,128)(2,1)S(1)}, bf16[64,1792]{1,0:T(8,128)(2,1)S(1)}, u32[]{:S(2)}, u32[]{:S(2)}) collective-permute-start(bf16[64,1792]{1,0:T(8,128)(2,1)S(1)} %get-tuple-element.112.refs_2_), channel_id=1, source_target_pairs={{0,4},{1,5},{2,6},{3,7},{4,0},{5,1},{6,2},{7,3},{8,12},{9,13},{10,... | collective-permute-start | bytes 688136 | tf_op jit(solution)/shard_map/ppermute | solution.py:28
  83.8 3.4 %image_attention.2 = (f32[1024,256]{1,0:T(8,128)S(1)}, f32[1024,128]{1,0:T(8,128)S(1)}) custom-call(bf16[16,384,128]{2,1,0:T(8,128)(2,1)S(1)} %all-to-all-done.packed_ref), custom_call_target="tpu_custom_call" | custom-call | flops 1073741824 | bytes 2359296 | tf_op jit(solution)/shard_map/image_attention/pallas_call | solution.py:359
  87.2 0.3 collective-permute-done.13.refs_1_
  87.5 1.5 %collective-permute-done.14.refs_3_ = bf16[64,1792]{1,0:T(8,128)(2,1)S(1)} collective-permute-done((bf16[64,1792]{1,0:T(8,128)(2,1)S(1)}, bf16[64,1792]{1,0:T(8,128)(2,1)S(1)}, u32[]{:S(2)}, u32[]{:S(2)}) %collective-permute-start.14) | collective-permute-done | bytes 229408 | tf_op jit(solution)/shard_map/ppermute | solution.py:28
  89.0 2.3 %project.1 = (bf16[4,144,256]{2,1,0:T(8,128)(2,1)S(1)}, bf16[4,144,256]{2,1,0:T(8,128)(2,1)S(1)}, bf16[4,144,256]{2,1,0:T(8,128)(2,1)S(1)}, bf16[4,144,256]{2,1,0:T(8,128)(2,1)S(1)}) custom-call(s32[5]{0:T(128)S(1)} %stack.19.place_ref, bf16[64,1792]{1,0:T(8,128)(2,1)S(1)} %get-tuple-element.111.refs_0_, ...), custom_call_target="tpu_custom_call" | custom-call | flops 754974720 | bytes 7864320 | tf_op jit(solution)/shard_map/project/pallas_call | solution.py:206
  91.3 0.4 collective-permute-start.17
  91.7 1.7 %collective-permute-start.18 = (bf16[4,144,256]{2,1,0:T(8,128)(2,1)S(1)}, bf16[4,144,256]{2,1,0:T(8,128)(2,1)S(1)}, u32[]{:S(2)}, u32[]{:S(2)}) collective-permute-start(bf16[4,144,256]{2,1,0:T(8,128)(2,1)S(1)} %get-tuple-element.127), channel_id=1, source_target_pairs={{0,4},{1,5},{2,6},{3,7},{4,0},{5,1},{6,2},{7,3},{8,12},{9,13},{10,... | collective-permute-start | bytes 884744 | tf_op jit(solution)/shard_map/ppermute | solution.py:28
  93.4 3.6 %image_attention.3 = (f32[1024,256]{1,0:T(8,128)S(1)}, f32[1024,128]{1,0:T(8,128)S(1)}) custom-call(bf16[16,384,128]{2,1,0:T(8,128)(2,1)S(1)} %all-to-all-done.packed_ref), custom_call_target="tpu_custom_call" | custom-call | flops 1073741824 | bytes 2359296 | tf_op jit(solution)/shard_map/image_attention/pallas_call | solution.py:359
  97.0 1.8 %collective-permute-done.17.refs_1_ = bf16[4,144,256]{2,1,0:T(8,128)(2,1)S(1)} collective-permute-done((bf16[4,144,256]{2,1,0:T(8,128)(2,1)S(1)}, bf16[4,144,256]{2,1,0:T(8,128)(2,1)S(1)}, u32[]{:S(2)}, u32[]{:S(2)}) %collective-permute-start.17) | collective-permute-done | bytes 294944 | tf_op jit(solution)/shard_map/ppermute | solution.py:28
  98.8 0.3 collective-permute-done.18.refs_3_
  99.2 1.5 %collective-permute-start.19 = (bf16[2,144,256]{2,1,0:T(8,128)(2,1)S(1)}, bf16[2,144,256]{2,1,0:T(8,128)(2,1)S(1)}, u32[]{:S(2)}, u32[]{:S(2)}) collective-permute-start(bf16[2,144,256]{2,1,0:T(8,128)(2,1)S(1)} %get-tuple-element.137), channel_id=1, source_target_pairs={{0,4},{1,5},{2,6},{3,7},{4,0},{5,1},{6,2},{7,3},{8,12},{9,13},{10,... | collective-permute-start | bytes 442376 | tf_op jit(solution)/shard_map/ppermute | solution.py:28
  100.7 1.3 collective-permute-start.20
  102.0 2.4 %collective-permute-done.19.refs_1_ = bf16[2,144,256]{2,1,0:T(8,128)(2,1)S(1)} collective-permute-done((bf16[2,144,256]{2,1,0:T(8,128)(2,1)S(1)}, bf16[2,144,256]{2,1,0:T(8,128)(2,1)S(1)}, u32[]{:S(2)}, u32[]{:S(2)}) %collective-permute-start.19) | collective-permute-done | bytes 147488 | tf_op jit(solution)/shard_map/ppermute | solution.py:28
  104.4 1.4 %collective-permute-done.20.refs_3_ = bf16[2,144,256]{2,1,0:T(8,128)(2,1)S(1)} collective-permute-done((bf16[2,144,256]{2,1,0:T(8,128)(2,1)S(1)}, bf16[2,144,256]{2,1,0:T(8,128)(2,1)S(1)}, u32[]{:S(2)}, u32[]{:S(2)}) %collective-permute-start.20) | collective-permute-done | bytes 147488 | tf_op jit(solution)/shard_map/ppermute | solution.py:28
  105.9 0.7 collective-permute-start.21
  106.6 2.2 %collective-permute-start.22 = (bf16[1,144,256]{2,1,0:T(8,128)(2,1)S(1)}, bf16[1,144,256]{2,1,0:T(8,128)(2,1)S(1)}, u32[]{:S(2)}, u32[]{:S(2)}) collective-permute-start(bf16[1,144,256]{2,1,0:T(8,128)(2,1)S(1)} %get-tuple-element.143), channel_id=1, source_target_pairs={{0,8},{1,9},{2,10},{3,11},{4,12},{5,13},{6,14},{7,15},{8,0},{9,1},... | collective-permute-start | bytes 221192 | tf_op jit(solution)/shard_map/ppermute | solution.py:28
  108.9 3.9 %collective-permute-done.21 = bf16[1,144,256]{2,1,0:T(8,128)(2,1)S(1)} collective-permute-done((bf16[1,144,256]{2,1,0:T(8,128)(2,1)S(1)}, bf16[1,144,256]{2,1,0:T(8,128)(2,1)S(1)}, u32[]{:S(2)}, u32[]{:S(2)}) %collective-permute-start.21) | collective-permute-done | bytes 73760 | tf_op jit(solution)/shard_map/ppermute | solution.py:28
  112.8 0.8 collective-permute-done.22
  113.6 0.7 combine.1
  114.4 1.2 collective-permute-done.23.refs_5_
  115.6 1.6 %finish.1 = bf16[16,160,128]{2,1,0:T(8,128)(2,1)S(1)} custom-call(s32[5]{0:T(128)S(1)} %stack.19.place_ref, bf16[16,384,128]{2,1,0:T(8,128)(2,1)S(1)} %all-to-all-done.packed_ref, f32[1024,256]{1,0:T(8,128)S(1)} %get-tuple-element.124.refs_0_, f32[1024,128]{1,0:T(8,128)S(1)} %get-tuple-element.125.refs_1_, f32[1024,256]{1,0:T(8,128)S(1)} %get-tuple-element.130.refs_2_, ...), custom_call_target="tpu_custom_call" | custom-call | flops 268435456 | bytes 3145728 | tf_op jit(solution)/shard_map/finish/pallas_call | solution.py:429
  117.2 21.8 %all_to_all.10.blocks_ref = bf16[16,160,128]{2,1,0:T(8,128)(2,1)S(1)} all-to-all(bf16[16,160,128]{2,1,0:T(8,128)(2,1)S(1)} %finish.1), channel_id=1, replica_groups=mesh['dp'=2,'seq'=16] {'seq'}, dimensions={0} | all-to-all | bytes 1310720 | tf_op jit(solution)/shard_map/all_to_all | solution.py:557
  139.0 1.0 unpack.1
  (36 shorter events, 1.0 us)
Async XLA Ops:
  2.2 1.0 copy-start.4
  4.7 8.3 %copy-start.3 = (bf16[1,256,1184]{1,2,0:T(8,128)(2,1)S(1)}, bf16[1,256,1184]{1,2,0:T(8,128)(2,1)}, u32[]{:S(2)}) copy-start(bf16[1,256,1184]{1,2,0:T(8,128)(2,1)} %param.10) | copy-start | bytes 1818628
  4.7 39.7 %all-to-all-start = ((bf16[16,384,128]{2,1,0:T(8,128)(2,1)}), bf16[16,384,128]{2,1,0:T(8,128)(2,1)S(1)}, u32[]{:S(2)}, u32[]{:S(2)}) async-start(bf16[16,384,128]{2,1,0:T(8,128)(2,1)} %pack.1), calls=%async_computation | async-start | bytes 3145728 | tf_op jit(solution)/shard_map/all_to_all | solution.py:557
  13.0 3.4 %copy-start = (bf16[1184,3584]{1,0:T(8,128)(2,1)S(1)}, bf16[1184,3584]{1,0:T(8,128)(2,1)}, u32[]{:S(2)}) copy-start(bf16[1184,3584]{1,0:T(8,128)(2,1)} %weight_ref.1) | copy-start | bytes 25460740
  19.9 1.9 %collective-permute-start = (bf16[8,16,1792]{2,1,0:T(8,128)(2,1)S(1)}, bf16[8,16,1792]{2,1,0:T(8,128)(2,1)S(1)}, u32[]{:S(2)}, u32[]{:S(2)}) collective-permute-start(bf16[8,16,1792]{2,1,0:T(8,128)(2,1)S(1)} %get-tuple-element.79), channel_id=1, source_target_pairs={{0,1},{1,0},{2,3},{3,2},{4,5},{5,4},{6,7},{7,6},{8,9},{9,8},{10,11... | collective-permute-start | bytes 1376264 | tf_op jit(solution)/shard_map/ppermute | solution.py:28
  20.3 2.1 %collective-permute-start.1 = (bf16[8,16,1792]{2,1,0:T(8,128)(2,1)S(1)}, bf16[8,16,1792]{2,1,0:T(8,128)(2,1)S(1)}, u32[]{:S(2)}, u32[]{:S(2)}) collective-permute-start(bf16[8,16,1792]{2,1,0:T(8,128)(2,1)S(1)} %get-tuple-element.81), channel_id=1, source_target_pairs={{0,1},{1,0},{2,3},{3,2},{4,5},{5,4},{6,7},{7,6},{8,9},{9,8},{10,11... | collective-permute-start | bytes 1376264 | tf_op jit(solution)/shard_map/ppermute | solution.py:28
  22.4 38.7 %copy-start.12 = (bf16[3584]{0:T(1024)(128)(2,1)S(1)}, bf16[3584]{0:T(1024)(128)(2,1)}, u32[]{:S(2)}) copy-start(bf16[3584]{0:T(1024)(128)(2,1)} %param.12) | copy-start | bytes 21508
  22.6 0.8 copy-start.5
  23.4 0.8 copy-start.7
  24.2 47.9 %copy-start.1 = (bf16[192,4096]{1,0:T(8,128)(2,1)S(1)}, bf16[192,4096]{1,0:T(8,128)(2,1)}, u32[]{:S(2)}) copy-start(bf16[192,4096]{1,0:T(8,128)(2,1)} %refs_7_.1) | copy-start | bytes 4718596
  24.2 12.9 %collective-permute-start.2 = (bf16[4,16,1792]{2,1,0:T(8,128)(2,1)S(1)}, bf16[4,16,1792]{2,1,0:T(8,128)(2,1)S(1)}, u32[]{:S(2)}, u32[]{:S(2)}) collective-permute-start(bf16[4,16,1792]{2,1,0:T(8,128)(2,1)S(1)} %get-tuple-element.83), channel_id=1, source_target_pairs={{0,2},{1,3},{2,0},{3,1},{4,6},{5,7},{6,4},{7,5},{8,10},{9,11},{10,... | collective-permute-start | bytes 688136 | tf_op jit(solution)/shard_map/ppermute | solution.py:28
  26.1 17.6 %collective-permute-start.3 = (bf16[4,16,1792]{2,1,0:T(8,128)(2,1)S(1)}, bf16[4,16,1792]{2,1,0:T(8,128)(2,1)S(1)}, u32[]{:S(2)}, u32[]{:S(2)}) collective-permute-start(bf16[4,16,1792]{2,1,0:T(8,128)(2,1)S(1)} %get-tuple-element.84), channel_id=1, source_target_pairs={{0,4},{1,5},{2,6},{3,7},{4,0},{5,1},{6,2},{7,3},{8,12},{9,13},{10,... | collective-permute-start | bytes 688136 | tf_op jit(solution)/shard_map/ppermute | solution.py:28
  43.7 0.7 copy-start.9
  44.4 1.0 copy-start.6
  45.4 1.0 copy-start.8
  46.4 0.9 copy-start.10
  47.4 25.9 %copy-start.11 = (bf16[256,2,192]{0,2,1:T(8,128)(2,1)S(1)}, bf16[256,2,192]{0,2,1:T(8,128)(2,1)}, u32[]{:S(2)}) copy-start(bf16[256,2,192]{0,2,1:T(8,128)(2,1)} %param.14) | copy-start | bytes 589828
  47.4 8.6 %collective-permute-start.4 = (bf16[2,16,1792]{2,1,0:T(8,128)(2,1)S(1)}, bf16[2,16,1792]{2,1,0:T(8,128)(2,1)S(1)}, u32[]{:S(2)}, u32[]{:S(2)}) collective-permute-start(bf16[2,16,1792]{2,1,0:T(8,128)(2,1)S(1)} %get-tuple-element.90), channel_id=1, source_target_pairs={{0,4},{1,5},{2,6},{3,7},{4,0},{5,1},{6,2},{7,3},{8,12},{9,13},{10,... | collective-permute-start | bytes 344072 | tf_op jit(solution)/shard_map/ppermute | solution.py:28
  52.1 6.0 %collective-permute-start.5 = (bf16[2,16,1792]{2,1,0:T(8,128)(2,1)S(1)}, bf16[2,16,1792]{2,1,0:T(8,128)(2,1)S(1)}, u32[]{:S(2)}, u32[]{:S(2)}) collective-permute-start(bf16[2,16,1792]{2,1,0:T(8,128)(2,1)S(1)} %get-tuple-element.92), channel_id=1, source_target_pairs={{0,2},{1,3},{2,0},{3,1},{4,6},{5,7},{6,4},{7,5},{8,10},{9,11},{10,... | collective-permute-start | bytes 344072 | tf_op jit(solution)/shard_map/ppermute | solution.py:28
  58.2 6.7 %collective-permute-start.6 = (bf16[1,16,1792]{2,1,0:T(8,128)(2,1)S(1)}, bf16[1,16,1792]{2,1,0:T(8,128)(2,1)S(1)}, u32[]{:S(2)}, u32[]{:S(2)}) collective-permute-start(bf16[1,16,1792]{2,1,0:T(8,128)(2,1)S(1)} %get-tuple-element.94), channel_id=1, source_target_pairs={{0,8},{1,9},{2,10},{3,11},{4,12},{5,13},{6,14},{7,15},{8,0},{9,1},... | collective-permute-start | bytes 172040 | tf_op jit(solution)/shard_map/ppermute | solution.py:28
  59.6 5.9 %collective-permute-start.7 = (bf16[1,16,1792]{2,1,0:T(8,128)(2,1)S(1)}, bf16[1,16,1792]{2,1,0:T(8,128)(2,1)S(1)}, u32[]{:S(2)}, u32[]{:S(2)}) collective-permute-start(bf16[1,16,1792]{2,1,0:T(8,128)(2,1)S(1)} %get-tuple-element.96), channel_id=1, source_target_pairs={{0,8},{1,9},{2,10},{3,11},{4,12},{5,13},{6,14},{7,15},{8,0},{9,1},... | collective-permute-start | bytes 172040 | tf_op jit(solution)/shard_map/ppermute | solution.py:28
  65.7 5.2 %collective-permute-start.8 = (bf16[16,1792]{1,0:T(8,128)(2,1)S(1)}, bf16[16,1792]{1,0:T(8,128)(2,1)S(1)}, u32[]{:S(2)}, u32[]{:S(2)}) collective-permute-start(bf16[16,1792]{1,0:T(8,128)(2,1)S(1)} %get-tuple-element.99.mine0), channel_id=1, source_target_pairs={{0,8},{1,9},{2,10},{3,11},{4,12},{5,13},{6,14},{7,15},{8,0},{9,1},... | collective-permute-start | bytes 172040 | tf_op jit(solution)/shard_map/ppermute | solution.py:28
  66.5 5.5 %collective-permute-start.9 = (bf16[16,1792]{1,0:T(8,128)(2,1)S(1)}, bf16[16,1792]{1,0:T(8,128)(2,1)S(1)}, u32[]{:S(2)}, u32[]{:S(2)}) collective-permute-start(bf16[16,1792]{1,0:T(8,128)(2,1)S(1)} %get-tuple-element.100.mine1), channel_id=1, source_target_pairs={{0,8},{1,9},{2,10},{3,11},{4,12},{5,13},{6,14},{7,15},{8,0},{9,1},... | collective-permute-start | bytes 172040 | tf_op jit(solution)/shard_map/ppermute | solution.py:28
  72.1 16.9 %collective-permute-start.16 = (bf16[192,4096]{1,0:T(8,128)(2,1)S(1)}, bf16[192,4096]{1,0:T(8,128)(2,1)S(1)}, u32[]{:S(2)}, u32[]{:S(2)}) collective-permute-start(bf16[192,4096]{1,0:T(8,128)(2,1)S(1)} %copy-done.1), channel_id=1, source_target_pairs={{0,1},{1,0},{2,3},{3,2},{4,5},{5,4},{6,7},{7,6},{8,9},{9,8},{10,11... | collective-permute-start | bytes 4718600 | tf_op jit(solution)/shard_map/ppermute | solution.py:28
  72.1 16.8 %collective-permute-start.15 = (bf16[192,3584]{1,0:T(8,128)(2,1)}, bf16[192,3584]{1,0:T(8,128)(2,1)S(1)}, u32[]{:S(2)}, u32[]{:S(2)}) collective-permute-start(bf16[192,3584]{1,0:T(8,128)(2,1)} %bitcast.24), channel_id=1, source_target_pairs={{0,1},{1,0},{2,3},{3,2},{4,5},{5,4},{6,7},{7,6},{8,9},{9,8},{10,11... | collective-permute-start | bytes 4128776 | tf_op jit(solution)/shard_map/ppermute | solution.py:28
  73.3 4.3 %collective-permute-start.12 = (bf16[2,192,256]{2,1,0:T(8,128)(2,1)S(1)}, bf16[2,192,256]{2,1,0:T(8,128)(2,1)S(1)}, u32[]{:S(2)}, u32[]{:S(2)}) collective-permute-start(bf16[2,192,256]{2,1,0:T(8,128)(2,1)S(1)} %bitcast.28), channel_id=1, source_target_pairs={{0,1},{1,0},{2,3},{3,2},{4,5},{5,4},{6,7},{7,6},{8,9},{9,8},{10,11... | collective-permute-start | bytes 589832 | tf_op jit(solution)/shard_map/ppermute | solution.py:28
  73.4 5.5 %collective-permute-start.10 = (bf16[32,1792]{1,0:T(8,128)(2,1)S(1)}, bf16[32,1792]{1,0:T(8,128)(2,1)S(1)}, u32[]{:S(2)}, u32[]{:S(2)}) collective-permute-start(bf16[32,1792]{1,0:T(8,128)(2,1)S(1)} %get-tuple-element.103.mine0), channel_id=1, source_target_pairs={{0,4},{1,5},{2,6},{3,7},{4,0},{5,1},{6,2},{7,3},{8,12},{9,13},{10,... | collective-permute-start | bytes 344072 | tf_op jit(solution)/shard_map/ppermute | solution.py:28
  75.1 5.2 %collective-permute-start.11 = (bf16[32,1792]{1,0:T(8,128)(2,1)S(1)}, bf16[32,1792]{1,0:T(8,128)(2,1)S(1)}, u32[]{:S(2)}, u32[]{:S(2)}) collective-permute-start(bf16[32,1792]{1,0:T(8,128)(2,1)S(1)} %get-tuple-element.104.mine1), channel_id=1, source_target_pairs={{0,2},{1,3},{2,0},{3,1},{4,6},{5,7},{6,4},{7,5},{8,10},{9,11},{10,... | collective-permute-start | bytes 344072 | tf_op jit(solution)/shard_map/ppermute | solution.py:28
  80.3 8.6 %copy-start.2 = (bf16[3584,192]{0,1:T(8,128)(2,1)S(1)}, bf16[3584,192]{0,1:T(8,128)(2,1)}, u32[]{:S(2)}) copy-start(bf16[3584,192]{0,1:T(8,128)(2,1)} %param.13) | copy-start | bytes 4128772
  80.3 7.1 %collective-permute-start.13 = (bf16[64,1792]{1,0:T(8,128)(2,1)S(1)}, bf16[64,1792]{1,0:T(8,128)(2,1)S(1)}, u32[]{:S(2)}, u32[]{:S(2)}) collective-permute-start(bf16[64,1792]{1,0:T(8,128)(2,1)S(1)} %get-tuple-element.111.refs_0_), channel_id=1, source_target_pairs={{0,2},{1,3},{2,0},{3,1},{4,6},{5,7},{6,4},{7,5},{8,10},{9,11},{10,... | collective-permute-start | bytes 688136 | tf_op jit(solution)/shard_map/ppermute | solution.py:28
  82.1 6.9 %collective-permute-start.14 = (bf16[64,1792]{1,0:T(8,128)(2,1)S(1)}, bf16[64,1792]{1,0:T(8,128)(2,1)S(1)}, u32[]{:S(2)}, u32[]{:S(2)}) collective-permute-start(bf16[64,1792]{1,0:T(8,128)(2,1)S(1)} %get-tuple-element.112.refs_2_), channel_id=1, source_target_pairs={{0,4},{1,5},{2,6},{3,7},{4,0},{5,1},{6,2},{7,3},{8,12},{9,13},{10,... | collective-permute-start | bytes 688136 | tf_op jit(solution)/shard_map/ppermute | solution.py:28
  91.3 7.4 %collective-permute-start.17 = (bf16[4,144,256]{2,1,0:T(8,128)(2,1)S(1)}, bf16[4,144,256]{2,1,0:T(8,128)(2,1)S(1)}, u32[]{:S(2)}, u32[]{:S(2)}) collective-permute-start(bf16[4,144,256]{2,1,0:T(8,128)(2,1)S(1)} %get-tuple-element.126), channel_id=1, source_target_pairs={{0,2},{1,3},{2,0},{3,1},{4,6},{5,7},{6,4},{7,5},{8,10},{9,11},{10,... | collective-permute-start | bytes 884744 | tf_op jit(solution)/shard_map/ppermute | solution.py:28
  91.7 7.3 %collective-permute-start.18 = (bf16[4,144,256]{2,1,0:T(8,128)(2,1)S(1)}, bf16[4,144,256]{2,1,0:T(8,128)(2,1)S(1)}, u32[]{:S(2)}, u32[]{:S(2)}) collective-permute-start(bf16[4,144,256]{2,1,0:T(8,128)(2,1)S(1)} %get-tuple-element.127), channel_id=1, source_target_pairs={{0,4},{1,5},{2,6},{3,7},{4,0},{5,1},{6,2},{7,3},{8,12},{9,13},{10,... | collective-permute-start | bytes 884744 | tf_op jit(solution)/shard_map/ppermute | solution.py:28
  99.2 5.2 %collective-permute-start.19 = (bf16[2,144,256]{2,1,0:T(8,128)(2,1)S(1)}, bf16[2,144,256]{2,1,0:T(8,128)(2,1)S(1)}, u32[]{:S(2)}, u32[]{:S(2)}) collective-permute-start(bf16[2,144,256]{2,1,0:T(8,128)(2,1)S(1)} %get-tuple-element.137), channel_id=1, source_target_pairs={{0,4},{1,5},{2,6},{3,7},{4,0},{5,1},{6,2},{7,3},{8,12},{9,13},{10,... | collective-permute-start | bytes 442376 | tf_op jit(solution)/shard_map/ppermute | solution.py:28
  100.7 5.1 %collective-permute-start.20 = (bf16[2,144,256]{2,1,0:T(8,128)(2,1)S(1)}, bf16[2,144,256]{2,1,0:T(8,128)(2,1)S(1)}, u32[]{:S(2)}, u32[]{:S(2)}) collective-permute-start(bf16[2,144,256]{2,1,0:T(8,128)(2,1)S(1)} %get-tuple-element.139), channel_id=1, source_target_pairs={{0,2},{1,3},{2,0},{3,1},{4,6},{5,7},{6,4},{7,5},{8,10},{9,11},{10,... | collective-permute-start | bytes 442376 | tf_op jit(solution)/shard_map/ppermute | solution.py:28
  105.9 6.9 %collective-permute-start.21 = (bf16[1,144,256]{2,1,0:T(8,128)(2,1)S(1)}, bf16[1,144,256]{2,1,0:T(8,128)(2,1)S(1)}, u32[]{:S(2)}, u32[]{:S(2)}) collective-permute-start(bf16[1,144,256]{2,1,0:T(8,128)(2,1)S(1)} %get-tuple-element.141), channel_id=1, source_target_pairs={{0,8},{1,9},{2,10},{3,11},{4,12},{5,13},{6,14},{7,15},{8,0},{9,1},... | collective-permute-start | bytes 221192 | tf_op jit(solution)/shard_map/ppermute | solution.py:28
  106.6 6.9 %collective-permute-start.22 = (bf16[1,144,256]{2,1,0:T(8,128)(2,1)S(1)}, bf16[1,144,256]{2,1,0:T(8,128)(2,1)S(1)}, u32[]{:S(2)}, u32[]{:S(2)}) collective-permute-start(bf16[1,144,256]{2,1,0:T(8,128)(2,1)S(1)} %get-tuple-element.143), channel_id=1, source_target_pairs={{0,8},{1,9},{2,10},{3,11},{4,12},{5,13},{6,14},{7,15},{8,0},{9,1},... | collective-permute-start | bytes 221192 | tf_op jit(solution)/shard_map/ppermute | solution.py:28
  114.3 1.3 collective-permute-start.23

commit v14 on v13

--- a/solution.py
+++ b/solution.py
@@ -274,31 +274,81 @@
     )(place, *parts)
 
 
-def pack_kernel(copies, queries_ref, keys_ref, values_ref, out_ref):
-    img_dev = keys_ref.shape[0]
-    part_rows = img_dev // copies
+def pack_kernel(copies, rows_ref, out_ref):
+    count = out_ref.shape[1]
     for device in range(out_ref.shape[0]):
         head, copy = device // copies, device % copies
         span = slice(head * HEAD_DIM, (head + 1) * HEAD_DIM)
-        out_ref[device, :img_dev, :] = keys_ref[:, span]
-        out_ref[device, img_dev : 2 * img_dev, :] = values_ref[:, span]
-        out_ref[device, 2 * img_dev :, :] = queries_ref[copy * part_rows : (copy + 1) * part_rows, span]
-
-
-def pack(copies, queries, keys, values):
-    img_dev = keys.shape[0]
-    rows = 2 * img_dev + img_dev // copies
+        start = copy * count if count < rows_ref.shape[0] else 0
+        out_ref[device] = rows_ref[start : start + count, span]
+
+
+def pack(copies, rows, count):
     return pl.pallas_call(
         functools.partial(pack_kernel, copies),
-        out_shape=jax.ShapeDtypeStruct((HEADS * copies, rows, HEAD_DIM), jnp.bfloat16),
-        in_specs=[VMEM_SPEC] * 3,
+        out_shape=jax.ShapeDtypeStruct((HEADS * copies, count, HEAD_DIM), jnp.bfloat16),
+        in_specs=[VMEM_SPEC],
         out_specs=VMEM_SPEC,
         compiler_params=params(8),
-        cost_estimate=pl.CostEstimate(
-            flops=0, bytes_accessed=4 * HEADS * copies * rows * HEAD_DIM, transcendentals=0
-        ),
+        cost_estimate=pl.CostEstimate(flops=0, bytes_accessed=4 * rows.size, transcendentals=0),
         name="pack",
-    )(queries, keys, values)
+    )(rows)
+
+
+def split_kernel(copies, place_ref, queries_ref, values_ref, *outs):
+    chip, core = place_ref[3], place_ref[2]
+    img_dev = values_ref.shape[0]
+    part_rows = img_dev // copies
+    for mask, out_ref in enumerate(outs):
+        for side in range(2):
+            device = 2 * (chip ^ mask) + (core ^ side)
+            head, copy = device // copies, device % copies
+            span = pl.ds(pl.multiple_of(head * HEAD_DIM, HEAD_DIM), HEAD_DIM)
+            rows = pl.ds(pl.multiple_of(copy * part_rows, part_rows), part_rows)
+            out_ref[side, :img_dev, :] = values_ref[:, span]
+            out_ref[side, img_dev:, :] = queries_ref[rows, span]
+
+
+def split(chips, copies, place, queries, values):
+    img_dev = values.shape[0]
+    rows = img_dev + img_dev // copies
+    out = jax.ShapeDtypeStruct((2, rows, HEAD_DIM), jnp.bfloat16)
+    return pl.pallas_call(
+        functools.partial(split_kernel, copies),
+        out_shape=(out,) * chips,
+        in_specs=[SMEM_SPEC] + [VMEM_SPEC] * 2,
+        out_specs=(VMEM_SPEC,) * chips,
+        compiler_params=params(6),
+        cost_estimate=pl.CostEstimate(
+            flops=0, bytes_accessed=8 * chips * rows * HEAD_DIM, transcendentals=0
+        ),
+        name="split",
+    )(place, queries, values)
+
+
+def gather_kernel(*refs):
+    for at, piece in enumerate(refs[:-1]):
+        refs[-1][at] = piece[1]
+
+
+def gather_other(pieces):
+    shape = (len(pieces),) + pieces[0].shape[1:]
+    return pl.pallas_call(
+        gather_kernel,
+        out_shape=jax.ShapeDtypeStruct(shape, pieces[0].dtype),
+        in_specs=[VMEM_SPEC] * len(pieces),
+        out_specs=VMEM_SPEC,
+        compiler_params=params(6),
+        cost_estimate=pl.CostEstimate(
+            flops=0, bytes_accessed=2 * len(pieces) * pieces[0].size, transcendentals=0
+        ),
+        name="gather_other",
+    )(*pieces)
+
+
+def by_distance(pieces, passed_ref):
+    views = [(piece.at[0], passed_ref.at[at]) for at, piece in enumerate(pieces)]
+    return [view for pair in views for view in pair]
 
 
 def unpack_kernel(copies, part_rows, blocks_ref, attended_ref, text_ref):
@@ -331,20 +381,23 @@
     )(blocks)
 
 
-def image_kernel(factor, call, img_dev, packed_ref, sum_ref, top_ref, keys_ref, wide_ref):
+def image_kernel(factor, call, place_ref, keys_ref, *refs):
+    *pieces, passed_ref, sum_ref, top_ref, wide_ref = refs
+    blocks = by_distance(pieces, passed_ref)
+    me = 2 * place_ref[3] + place_ref[2]
+    img_dev = keys_ref.shape[0] // len(blocks)
     wide_ref[:, HEAD_DIM:] = jnp.ones((wide_ref.shape[0], HEAD_DIM), wide_ref.dtype)
-    for device in range(packed_ref.shape[0]):
-        rows = slice(device * img_dev, (device + 1) * img_dev)
-        keys_ref[rows, :] = packed_ref[device, :img_dev, :]
-        wide_ref[rows, :HEAD_DIM] = packed_ref[device, img_dev : 2 * img_dev, :]
-    group = max(1, 256 // (packed_ref.shape[1] - 2 * img_dev))
+    for at, block in enumerate(blocks):
+        start = pl.multiple_of((me ^ at) * img_dev, img_dev)
+        wide_ref[pl.ds(start, img_dev), :HEAD_DIM] = block[:img_dev, :]
+    group = max(1, 256 // (pieces[0].shape[1] - img_dev))
     rows = 256
     contract = (((1,), (1,)), ((), ()))
     count = sum_ref.shape[0]
     for start in range(0, count, rows):
         span = slice(start, start + rows)
         at = (call * count + start) // rows * group
-        queries = packed_ref[at : at + group, 2 * img_dev :, :].reshape(rows, HEAD_DIM)
+        queries = jnp.concatenate([block[img_dev:, :] for block in blocks[at : at + group]], 0)
         scores = lax.dot_general(queries, keys_ref[...], contract, preferred_element_type=jnp.float32)
         scores = scores * factor
         top = jnp.max(scores, 1, keepdims=True)
@@ -353,21 +406,19 @@
         top_ref[span, :] = jnp.broadcast_to(top, (rows, HEAD_DIM))
 
 
-def image_attention(packed, img_dev, factor, call, calls):
-    count = packed.shape[0] * (packed.shape[1] - 2 * img_dev) // calls
-    total = packed.shape[0] * img_dev
-    return pl.pallas_call(
-        functools.partial(image_kernel, factor, call, img_dev),
+def image_attention(place, keys, pieces, passed, factor, call, calls):
+    total = keys.shape[0]
+    part_rows = passed.shape[1] - total // (2 * len(pieces))
+    count = 2 * len(pieces) * part_rows // calls
+    return pl.pallas_call(
+        functools.partial(image_kernel, factor, call),
         out_shape=(
             jax.ShapeDtypeStruct((count, 2 * HEAD_DIM), jnp.float32),
             jax.ShapeDtypeStruct((count, HEAD_DIM), jnp.float32),
         ),
-        in_specs=[VMEM_SPEC],
+        in_specs=[SMEM_SPEC] + [VMEM_SPEC] * (len(pieces) + 2),
         out_specs=(VMEM_SPEC, VMEM_SPEC),
-        scratch_shapes=[
-            pltpu.VMEM((total, HEAD_DIM), jnp.bfloat16),
-            pltpu.VMEM((total, 2 * HEAD_DIM), jnp.bfloat16),
-        ],
+        scratch_shapes=[pltpu.VMEM((total, 2 * HEAD_DIM), jnp.bfloat16)],
         compiler_params=params(14),
         cost_estimate=pl.CostEstimate(
             flops=4 * count * total * HEAD_DIM,
@@ -375,14 +426,17 @@
             transcendentals=count * total,
         ),
         name="image_attention",
-    )(packed)
-
-
-def finish_kernel(factor, calls, img_dev, place_ref, packed_ref, *refs):
-    images, (mine_ref, got_ref, out_ref) = refs[: 2 * calls], refs[2 * calls :]
+    )(place, keys, *pieces, passed)
+
+
+def finish_kernel(factor, calls, img_dev, place_ref, *refs):
+    *pieces, passed_ref = refs[: -3 - 2 * calls]
+    images, (mine_ref, got_ref, out_ref) = refs[-3 - 2 * calls : -3], refs[-3:]
+    blocks = by_distance(pieces, passed_ref)
+    me = 2 * place_ref[3] + place_ref[2]
     core, valid = place_ref[2], place_ref[4]
     devices = out_ref.shape[0]
-    part_rows = packed_ref.shape[1] - 2 * img_dev
+    part_rows = passed_ref.shape[1] - img_dev
     half = mine_ref.shape[0]
     contract = (((1,), (1,)), ((), ()))
     mine, got = mine_ref[...], got_ref[...]
@@ -398,8 +452,8 @@
     for step in range(devices // group):
         sum_ref, top_ref = images[2 * (step // each)], images[2 * (step // each) + 1]
         span = slice(step % each * rows, (step % each + 1) * rows)
-        queries = packed_ref[step * group : (step + 1) * group, 2 * img_dev :, :]
-        queries = queries.reshape(rows, HEAD_DIM)
+        queries = blocks[step * group : (step + 1) * group]
+        queries = jnp.concatenate([block[img_dev:, :] for block in queries], 0)
         scores = lax.dot_general(queries, keys, contract, preferred_element_type=jnp.float32)
         scores = scores * factor + bias
         before = top_ref[span, :]
@@ -410,7 +464,9 @@
         mixed = sum_ref[span, :HEAD_DIM] * rescale + total[:, :HEAD_DIM]
         total = sum_ref[span, HEAD_DIM:] * rescale + total[:, HEAD_DIM:]
         mixed = (mixed / total).astype(out_ref.dtype)
-        out_ref[step * group : (step + 1) * group, :part_rows, :] = mixed.reshape(group, part_rows, HEAD_DIM)
+        for at in range(group):
+            to = me ^ (step * group + at)
+            out_ref[to, :part_rows, :] = mixed[at * part_rows : (at + 1) * part_rows]
     low = jnp.where(core == 0, mine.astype(jnp.float32), got.astype(jnp.float32))
     high = jnp.where(core == 0, got.astype(jnp.float32), mine.astype(jnp.float32))
     share = 2 * half // devices
@@ -422,14 +478,14 @@
         out_ref[device, part_rows:, :] = block.astype(out_ref.dtype)
 
 
-def finish(place, packed, images, mine, got, img_dev, factor):
-    devices, part_rows = packed.shape[0], packed.shape[1] - 2 * img_dev
+def finish(place, pieces, passed, images, mine, got, img_dev, factor):
+    devices, part_rows = 2 * len(pieces), passed.shape[1] - img_dev
     count = devices * part_rows
     share = 2 * mine.shape[0] // devices
     return pl.pallas_call(
         functools.partial(finish_kernel, factor, len(images) // 2, img_dev),
         out_shape=jax.ShapeDtypeStruct((devices, part_rows + 2 * share, HEAD_DIM), jnp.bfloat16),
-        in_specs=[SMEM_SPEC] + [VMEM_SPEC] * (len(images) + 3),
+        in_specs=[SMEM_SPEC] + [VMEM_SPEC] * (len(pieces) + len(images) + 3),
         out_specs=VMEM_SPEC,
         compiler_params=params(10),
         cost_estimate=pl.CostEstimate(
@@ -438,7 +494,7 @@
             transcendentals=count * 2 * mine.shape[0],
         ),
         name="finish",
-    )(place, packed, *images, mine, got)
+    )(place, *pieces, passed, *images, mine, got)
 
 
 def add_kernel(*refs):
@@ -469,29 +525,54 @@
     return [sent0, sent1], [keep0, keep1]
 
 
-def norm_kernel(keep0, got0, keep1, got1, gain_ref, out0, out1):
-    totals = [keep0[0] + got0[0].astype(jnp.float32), keep1[0] + got1[0].astype(jnp.float32)]
-    width = totals[0].shape[1]
-    square = sum(jnp.sum(total * total, 1, keepdims=True) for total in totals)
-    scale_rows = lax.rsqrt(square / (2 * width) + epsilon)
-    for lane, (total, out_ref) in enumerate(zip(totals, (out0, out1))):
-        gain = gain_ref[:, lane * width : (lane + 1) * width].astype(jnp.float32)
-        out_ref[...] = (total * scale_rows * gain).astype(out_ref.dtype)
-
-
-def normalize(keep, got, norm_gain):
-    out = jax.ShapeDtypeStruct(keep[0].shape[1:], jnp.bfloat16)
-    return pl.pallas_call(
+def total_kernel(mine0, got0, mine1, got1, out0, out1):
+    for mine, got, out_ref in ((mine0, got0, out0), (mine1, got1, out1)):
+        out_ref[...] = (mine[...] + got[...].astype(jnp.float32)).astype(out_ref.dtype)
+
+
+def add_all(mine, got):
+    out = jax.ShapeDtypeStruct(mine[0].shape, jnp.bfloat16)
+    return pl.pallas_call(
+        total_kernel,
+        out_shape=(out, out),
+        in_specs=[VMEM_SPEC] * 4,
+        out_specs=(VMEM_SPEC,) * 2,
+        compiler_params=params(4),
+        cost_estimate=pl.CostEstimate(
+            flops=2 * mine[0].size, bytes_accessed=16 * mine[0].size, transcendentals=0
+        ),
+        name="add_all",
+    )(mine[0], got[0], mine[1], got[1])
+
+
+def norm_kernel(mine0, got0, mine1, got1, gain_ref, out0, out1):
+    share, width = mine0.shape[1:]
+    for at in range(2):
+        totals = [
+            mine[at].astype(jnp.float32) + got[1 - at].astype(jnp.float32)
+            for mine, got in ((mine0, got0), (mine1, got1))
+        ]
+        square = sum(jnp.sum(total * total, 1, keepdims=True) for total in totals)
+        scale_rows = lax.rsqrt(square / (2 * width) + epsilon)
+        for lane, (total, out_ref) in enumerate(zip(totals, (out0, out1))):
+            gain = gain_ref[:, lane * width : (lane + 1) * width].astype(jnp.float32)
+            out_ref[at] = (total * scale_rows * gain).astype(out_ref.dtype)
+
+
+def normalize(mine, got, norm_gain):
+    out = jax.ShapeDtypeStruct(mine[0].shape, jnp.bfloat16)
+    states = pl.pallas_call(
         norm_kernel,
         out_shape=(out, out),
         in_specs=[VMEM_SPEC] * 5,
         out_specs=(VMEM_SPEC,) * 2,
         compiler_params=params(4),
         cost_estimate=pl.CostEstimate(
-            flops=8 * keep[0].size, bytes_accessed=16 * keep[0].size, transcendentals=0
+            flops=8 * mine[0].size, bytes_accessed=16 * mine[0].size, transcendentals=0
         ),
         name="normalize",
-    )(keep[0], got[0], keep[1], got[1], norm_gain)
+    )(mine[0], got[0], mine[1], got[1], norm_gain)
+    return [part.reshape(-1, part.shape[2]) for part in states]
 
 
 def join_kernel(mine0, got0, mine1, got1, out0, out1):
@@ -557,48 +638,73 @@
         return lax.all_to_all(rows, "seq", split_axis=0, concat_axis=0, tiled=True)
 
     image_key_values, image_queries = tie((image_key_values, image_queries))
-    packed = pack(copies, image_queries[0], image_key_values[0, :, 0], image_key_values[0, :, 1])
-    act, packed = tie((enc_act[0].T, packed))
-    packed = exchange(packed)
-    encoded = encoder(lanes, place, act, down_weight)
+    act, keys = tie((enc_act[0].T, pack(copies, image_key_values[0, :, 0], img_dev)))
+    keys = exchange(keys)
+    pieces = {}
+
+    def beside(chain, masks):
+        chain, held = tie((chain, [pieces[mask] for mask in masks]))
+        pieces.update((mask, swap(piece, 2 * mask)) for mask, piece in zip(masks, held))
+        return chain
+
+    def arrived(chain, masks):
+        chain, held = tie((chain, [pieces[mask] for mask in masks]))
+        pieces.update(zip(masks, held))
+        return chain
+
+    encoded = list(encoder(lanes, place, act, down_weight))
+    encoded[1::2], keys = tie((encoded[1::2], keys))
     keep, got = encoded[::2], [swap(other, 1) for other in encoded[1::2]]
+    crossing = list(range(chips // 2, chips))
+    for step in range(rounds - 1):
+        sent, keep = add_halves(keep, got)
+        if step == 0:
+            sent, image_queries, image_key_values = tie((sent, image_queries, image_key_values))
+            held = split(chips, copies, place, image_queries[0], image_key_values[0, :, 1])
+            pieces.update(enumerate(held))
+        masks = crossing[step : step + 1]
+        sent = beside(sent, masks)
+        got = [swap(part, 2 * order[step]) for part, order in zip(sent, lanes)]
+        got = arrived(got, masks)
+        if step == 0:
+            sent, held = tie((sent, win0))
+            win1 = swap(held, 1)
+            got, win1 = tie((got, win1))
+        if step == 1:
+            sent, held, mod1 = tie((sent, kv0, mod0))
+            kv1, mod1 = swap(held, 1), swap(mod1, 1)
+            got, kv1, mod1 = tie((got, kv1, mod1))
+    summed = add_all(keep, got)
+    masks = list(range(1, chips // 2))
+    summed = beside(summed, masks)
+    got = [swap(part, 2 * order[-1]) for part, order in zip(summed, lanes)]
+    lines = modulation(time, mod0, mod1)
+    got, lines = tie((arrived(got, masks), lines))
+
+    states = normalize(summed, got, norm_gain[None, :])
+    for step in reversed(range(rounds - 1)):
+        masks = crossing[rounds:] if step == 0 else crossing[rounds - 1 : rounds] * (step == 1)
+        states = beside(states, masks)
+        got = [swap(state, 2 * order[step]) for state, order in zip(states, lanes)]
+        got = arrived(got, masks)
+        if step:
+            states = join(states, got)
+    states = [state for pair in zip(states, got) for state in pair]
+
+    blocks = project(lanes, place, states, lines, win0, win1, kv0, kv1)
+    keep, sent = [blocks[0], blocks[2]], [blocks[1], blocks[3]]
+    images = []
     for step in range(rounds):
-        sent, keep = add_halves(keep, got)
         got = [swap(part, 2 * order[step]) for part, order in zip(sent, lanes)]
         if step == 0:
-            got, packed = tie((got, packed))
-
-    states = normalize(keep, got, norm_gain[None, :])
-    images = []
-
-    for step in reversed(range(rounds)):
-        if step == rounds - 1:
-            states, held, mod1 = tie((states, win0, mod0))
-            win1, mod1 = swap(held, 1), swap(mod1, 1)
-        if step == rounds - 2:
-            states, held = tie((states, kv0))
-            kv1 = swap(held, 1)
-            lines = modulation(time, mod0, mod1)
-        if step == 0:
-            states, packed = tie((states, packed))
-            image = image_attention(packed, img_dev, factor, 0, 2)
-        got = [swap(state, 2 * order[step]) for state, order in zip(states, lanes)]
-        if step == rounds - 2:
-            got, lines = tie((got, lines))
-        if step:
-            states = join(states, got)
-    got, image = tie((got, image))
-    images += image
-    states = [state for pair in zip(states, got) for state in pair]
-
-    blocks = project(lanes, place, states, lines, win0, win1, kv0, kv1)
-    keep, sent = [blocks[0], blocks[2]], [blocks[1], blocks[3]]
-    for step in range(rounds):
-        if step == 0:
-            sent, packed = tie((sent, packed))
-            image = image_attention(packed, img_dev, factor, 1, 2)
-        got = [swap(part, 2 * order[step]) for part, order in zip(sent, lanes)]
-        if step == 0:
+            pieces = [pieces[mask] for mask in range(chips)]
+            sent, pieces = tie((sent, pieces))
+            passed = swap(gather_other(pieces), 1)
+            got, passed = tie((got, passed))
+            keys = keys.reshape(-1, HEAD_DIM)
+        elif step <= 2:
+            sent, passed = tie((sent, passed))
+            image = image_attention(place, keys, pieces, passed, factor, step - 1, 2)
             got, image = tie((got, image))
             images += image
         if step < rounds - 1:
@@ -608,7 +714,7 @@
     mine, sent = combine(place, parts, chips, text_len // 2, model_width)
     got = swap(sent, 1)
 
-    back = exchange(finish(place, packed, images, mine, got, img_dev, factor))
+    back = exchange(finish(place, pieces, passed, images, mine, got, img_dev, factor))
     attended, text_kv = unpack(copies, part_rows, back)
     return (attended[None], text_kv)
 

time: 140 us -> 141 us (level)
  waiting for transfers between devices: 46.2 us -> 53.7 us
  local copies, waits for them, and re-layouts: 11.4 us -> 6.14 us
  starting transfers between devices: 40 us -> 36.7 us
  Pallas kernels: 18.4 us -> 20.1 us
    all_to_all x1, waiting for transfers between devices: 0.01 us -> 6.8 us  [exchange(): return lax.all_to_all(rows, 'seq', split_axis=0, concat_axis=0, tiled=True)]
    unnamed x26 -> x16, local copies, waits for them, and re-layouts: 9.6 us -> 4.04 us
    ppermute x24 -> x30, starting transfers between devices: 32.5 us -> 29.4 us  [swap(): return lax.ppermute(value, 'seq', [(i, i ^ mask) for i in range(devices)])]
    pallas_call x2 -> x5, Pallas kernels: 6.95 us -> 9.19 us  [the longest x2 8.3 us: image_attention(): pl.pallas_call(functools.partial(image_kernel, factor, call), out_shape=(...]
    ppermute x24 -> x30, waiting for transfers between devices: 46.2 us -> 46.9 us  [swap(): return lax.ppermute(value, 'seq', [(i, i ^ mask) for i in range(devices)])]
  transfers between devices with their start and end apart: 25 -> 31, of which waited for: 22 -> 18; matrix products, arithmetic and copies ran while one was open for 0% -> 0% of each run, Pallas kernels for 8% -> 9%
where the time goes in v14:
time: 141 us; the launch traced here: 140 us
  waiting for transfers between devices  53.7 us (38%)
  starting transfers between devices  36.7 us (26%)
  blocking collectives  21.4 us (15%)
  Pallas kernels  20.1 us (14%)
  local copies, waits for them, and re-layouts  6.14 us (4%)
  between operations  2.26 us (2%)
    ppermute x30, waiting for transfers between devices, swap(): return lax.ppermute(value, 'seq', [(i, i ^ mask) for i in range(devices)])  46.9 us
    ppermute x30, starting transfers between devices, swap(): return lax.ppermute(value, 'seq', [(i, i ^ mask) for i in range(devices)])  29.4 us
    all_to_all x1, blocking collectives, exchange(): return lax.all_to_all(rows, 'seq', split_axis=0, concat_axis=0, tiled=True)  21.4 us
    pallas_call x2, Pallas kernels, image_attention(): pl.pallas_call(functools.partial(image_kernel, factor, call), out_shape=(...  8.3 us
    all_to_all x1, starting transfers between devices, exchange(): return lax.all_to_all(rows, 'seq', split_axis=0, concat_axis=0, tiled=True)  7.36 us
    all_to_all x1, waiting for transfers between devices, exchange(): return lax.all_to_all(rows, 'seq', split_axis=0, concat_axis=0, tiled=True)  6.8 us
    unnamed x16, local copies, waits for them, and re-layouts  4.04 us
    pallas_call x1, Pallas kernels, encoder(): pl.pallas_call(functools.partial(encoder_kernel, lanes), out_shape=(out,)...  3.49 us
  transfers between devices with their start and end apart: 31, of which 18 were waited for; matrix products, arithmetic and copies ran while one was open for 0% of the time, Pallas kernels for 9%

profile of v14, /device:TPU:0, one launch (start us, length us, event | category | flops | bytes accessed | tf_op | source)
XLA Modules:
  0.0 140.5 jit_solution(12536669464793147039)
XLA Ops:
  0.6 1.6 %copy.12 = bf16[1,128,2,2048]{3,1,2,0:T(8,128)(2,1)S(1)} copy(bf16[1,128,2,2048]{3,2,1,0:T(2,128)(2,1)} %param.19) | data formatting | bytes 2097152 | tf_op jit(solution)/shard_map/optimization_barrier | solution.py:640
  2.3 0.9 pack.1
  3.2 7.4 %all-to-all-start = ((bf16[16,128,128]{2,1,0:T(8,128)(2,1)}), bf16[16,128,128]{2,1,0:T(8,128)(2,1)S(1)}, u32[]{:S(2)}, u32[]{:S(2)}) async-start(bf16[16,128,128]{2,1,0:T(8,128)(2,1)} %pack.1), calls=%async_computation | async-start | bytes 1048576 | tf_op jit(solution)/shard_map/all_to_all | solution.py:638
  11.2 0.1 stack.19.place_ref
  11.3 3.4 %copy-done = bf16[1184,3584]{1,0:T(8,128)(2,1)S(1)} copy-done((bf16[1184,3584]{1,0:T(8,128)(2,1)S(1)}, bf16[1184,3584]{1,0:T(8,128)(2,1)}, u32[]{:S(2)}) %copy-start) | copy-done | bytes 8486936
  14.7 3.5 %encoder.1 = (bf16[8,16,1792]{2,1,0:T(8,128)(2,1)S(1)}, bf16[8,16,1792]{2,1,0:T(8,128)(2,1)S(1)}, bf16[8,16,1792]{2,1,0:T(8,128)(2,1)S(1)}, bf16[8,16,1792]{2,1,0:T(8,128)(2,1)S(1)}) custom-call(s32[5]{0:T(128)S(1)} %stack.19.place_ref, bf16[1184,256]{1,0:T(8,128)(2,1)S(1)} %bitcast.29, bf16[1184,3584]{1,0:T(8,128)(2,1)S(1)} %copy-done), custom_call_target="tpu_custom_call" | custom-call | flops 2172649472 | bytes 10928128 | tf_op jit(solution)/shard_map/encoder/pallas_call | solution.py:84
  18.2 6.8 %all-to-all-done = bf16[16,128,128]{2,1,0:T(8,128)(2,1)S(1)} async-done(((bf16[16,128,128]{2,1,0:T(8,128)(2,1)}), bf16[16,128,128]{2,1,0:T(8,128)(2,1)S(1)}, u32[]{:S(2)}, u32[]{:S(2)}) %all-to-all-start) | async-done | bytes 524320 | tf_op jit(solution)/shard_map/all_to_all | solution.py:638
  25.0 0.5 collective-permute-start.1
  25.5 1.3 collective-permute-done.refs_1_
  26.8 0.7 collective-permute-done.1.refs_3_
  27.5 0.2 add_halves.4
  27.7 0.4 copy.13
  28.1 0.6 copy-done.4
  28.7 0.8 split.1
  29.6 0.2 collective-permute-start.5
  29.8 1.0 collective-permute-start.2
  30.8 1.5 %collective-permute-start.3 = (bf16[4,16,1792]{2,1,0:T(8,128)(2,1)S(1)}, bf16[4,16,1792]{2,1,0:T(8,128)(2,1)S(1)}, u32[]{:S(2)}, u32[]{:S(2)}) collective-permute-start(bf16[4,16,1792]{2,1,0:T(8,128)(2,1)S(1)} %get-tuple-element.146), channel_id=1, source_target_pairs={{0,4},{1,5},{2,6},{3,7},{4,0},{5,1},{6,2},{7,3},{8,12},{9,13},{10,... | collective-permute-start | bytes 688136 | tf_op jit(solution)/shard_map/ppermute | solution.py:28
  32.3 1.5 %collective-permute-start.4 = (bf16[2,256,128]{2,1,0:T(8,128)(2,1)S(1)}, bf16[2,256,128]{2,1,0:T(8,128)(2,1)S(1)}, u32[]{:S(2)}, u32[]{:S(2)}) collective-permute-start(bf16[2,256,128]{2,1,0:T(8,128)(2,1)S(1)} %get-tuple-element.147), channel_id=1, source_target_pairs={{0,8},{1,9},{2,10},{3,11},{4,12},{5,13},{6,14},{7,15},{8,0},{9,1},... | collective-permute-start | bytes 393224 | tf_op jit(solution)/shard_map/ppermute | solution.py:28
  33.8 6.3 %collective-permute-done.4.refs_4_ = bf16[2,256,128]{2,1,0:T(8,128)(2,1)S(1)} collective-permute-done((bf16[2,256,128]{2,1,0:T(8,128)(2,1)S(1)}, bf16[2,256,128]{2,1,0:T(8,128)(2,1)S(1)}, u32[]{:S(2)}, u32[]{:S(2)}) %collective-permute-start.4) | collective-permute-done | bytes 131104 | tf_op jit(solution)/shard_map/ppermute | solution.py:28
  40.1 0.9 collective-permute-done.3.refs_3_
  41.0 0.1 add_halves.5
  41.1 0.1 collective-permute-start.9
  41.2 0.5 collective-permute-start.10
  41.6 3.0 %collective-permute-start.8 = (bf16[2,256,128]{2,1,0:T(8,128)(2,1)S(1)}, bf16[2,256,128]{2,1,0:T(8,128)(2,1)S(1)}, u32[]{:S(2)}, u32[]{:S(2)}) collective-permute-start(bf16[2,256,128]{2,1,0:T(8,128)(2,1)S(1)} %get-tuple-element.160), channel_id=1, source_target_pairs={{0,10},{1,11},{2,8},{3,9},{4,14},{5,15},{6,12},{7,13},{8,2},{9,3},... | collective-permute-start | bytes 393224 | tf_op jit(solution)/shard_map/ppermute | solution.py:28
  44.6 0.3 collective-permute-start.6
  44.9 1.3 collective-permute-start.7
  46.8 3.8 %collective-permute-done.6.got0 = bf16[2,16,1792]{2,1,0:T(8,128)(2,1)S(1)} collective-permute-done((bf16[2,16,1792]{2,1,0:T(8,128)(2,1)S(1)}, bf16[2,16,1792]{2,1,0:T(8,128)(2,1)S(1)}, u32[]{:S(2)}, u32[]{:S(2)}) %collective-permute-start.6) | collective-permute-done | bytes 114720 | tf_op jit(solution)/shard_map/ppermute | solution.py:28
  50.6 1.1 collective-permute-done.8.refs_5_
  51.8 2.3 %collective-permute-start.11 = (bf16[2,16,1792]{2,1,0:T(8,128)(2,1)S(1)}, bf16[2,16,1792]{2,1,0:T(8,128)(2,1)S(1)}, u32[]{:S(2)}, u32[]{:S(2)}) collective-permute-start(bf16[2,16,1792]{2,1,0:T(8,128)(2,1)S(1)} %get-tuple-element.173.mine0), channel_id=1, source_target_pairs={{0,8},{1,9},{2,10},{3,11},{4,12},{5,13},{6,14},{7,15},{8,0},{9,1},... | collective-permute-start | bytes 344072 | tf_op jit(solution)/shard_map/ppermute | solution.py:28
  54.1 0.7 collective-permute-start.12
  54.8 1.2 collective-permute-start.13
  56.0 2.0 %collective-permute-start.14 = (bf16[2,256,128]{2,1,0:T(8,128)(2,1)S(1)}, bf16[2,256,128]{2,1,0:T(8,128)(2,1)S(1)}, u32[]{:S(2)}, u32[]{:S(2)}) collective-permute-start(bf16[2,256,128]{2,1,0:T(8,128)(2,1)S(1)} %get-tuple-element.176), channel_id=1, source_target_pairs={{0,4},{1,5},{2,6},{3,7},{4,0},{5,1},{6,2},{7,3},{8,12},{9,13},{10,... | collective-permute-start | bytes 393224 | tf_op jit(solution)/shard_map/ppermute | solution.py:28
  58.0 0.2 collective-permute-start.15
  58.4 0.2 modulation.1.refs_4_
  58.6 5.1 %collective-permute-done.11.got0 = bf16[2,16,1792]{2,1,0:T(8,128)(2,1)S(1)} collective-permute-done((bf16[2,16,1792]{2,1,0:T(8,128)(2,1)S(1)}, bf16[2,16,1792]{2,1,0:T(8,128)(2,1)S(1)}, u32[]{:S(2)}, u32[]{:S(2)}) %collective-permute-start.11) | collective-permute-done | bytes 114720 | tf_op jit(solution)/shard_map/ppermute | solution.py:28
  63.7 1.3 collective-permute-done.12.got1
  65.0 0.9 collective-permute-done.14.refs_2_
  65.9 1.2 collective-permute-done.15.refs_3_
  67.1 0.2 normalize.1
  67.3 2.7 %collective-permute-start.18 = (bf16[2,256,128]{2,1,0:T(8,128)(2,1)S(1)}, bf16[2,256,128]{2,1,0:T(8,128)(2,1)S(1)}, u32[]{:S(2)}, u32[]{:S(2)}) collective-permute-start(bf16[2,256,128]{2,1,0:T(8,128)(2,1)S(1)} %get-tuple-element.188), channel_id=1, source_target_pairs={{0,12},{1,13},{2,14},{3,15},{4,8},{5,9},{6,10},{7,11},{8,4},{9,5},... | collective-permute-start | bytes 393224 | tf_op jit(solution)/shard_map/ppermute | solution.py:28
  70.0 0.9 collective-permute-start.17
  70.9 4.9 %collective-permute-done.16.got0 = bf16[32,1792]{1,0:T(8,128)(2,1)S(1)} collective-permute-done((bf16[32,1792]{1,0:T(8,128)(2,1)S(1)}, bf16[32,1792]{1,0:T(8,128)(2,1)S(1)}, u32[]{:S(2)}, u32[]{:S(2)}) %collective-permute-start.16) | collective-permute-done | bytes 114720 | tf_op jit(solution)/shard_map/ppermute | solution.py:28
  75.8 1.3 collective-permute-start.19
  77.2 1.2 collective-permute-start.20
  78.3 1.5 %collective-permute-start.21 = (bf16[2,256,128]{2,1,0:T(8,128)(2,1)S(1)}, bf16[2,256,128]{2,1,0:T(8,128)(2,1)S(1)}, u32[]{:S(2)}, u32[]{:S(2)}) collective-permute-start(bf16[2,256,128]{2,1,0:T(8,128)(2,1)S(1)} %get-tuple-element.196), channel_id=1, source_target_pairs={{0,14},{1,15},{2,12},{3,13},{4,10},{5,11},{6,8},{7,9},{8,6},{9,7},... | collective-permute-start | bytes 393224 | tf_op jit(solution)/shard_map/ppermute | solution.py:28
  79.8 7.3 %collective-permute-done.21.refs_7_ = bf16[2,256,128]{2,1,0:T(8,128)(2,1)S(1)} collective-permute-done((bf16[2,256,128]{2,1,0:T(8,128)(2,1)S(1)}, bf16[2,256,128]{2,1,0:T(8,128)(2,1)S(1)}, u32[]{:S(2)}, u32[]{:S(2)}) %collective-permute-start.21) | collective-permute-done | bytes 131104 | tf_op jit(solution)/shard_map/ppermute | solution.py:28
  87.1 2.3 %project.1 = (bf16[4,144,256]{2,1,0:T(8,128)(2,1)S(1)}, bf16[4,144,256]{2,1,0:T(8,128)(2,1)S(1)}, bf16[4,144,256]{2,1,0:T(8,128)(2,1)S(1)}, bf16[4,144,256]{2,1,0:T(8,128)(2,1)S(1)}) custom-call(s32[5]{0:T(128)S(1)} %stack.19.place_ref, bf16[64,1792]{1,0:T(8,128)(2,1)S(1)} %get-tuple-element.194.refs_0_, ...), custom_call_target="tpu_custom_call" | custom-call | flops 754974720 | bytes 7864320 | tf_op jit(solution)/shard_map/project/pallas_call | solution.py:206
  89.5 0.4 collective-permute-start.22
  90.0 9.0 %collective-permute-done.22.refs_1_ = bf16[4,144,256]{2,1,0:T(8,128)(2,1)S(1)} collective-permute-done((bf16[4,144,256]{2,1,0:T(8,128)(2,1)S(1)}, bf16[4,144,256]{2,1,0:T(8,128)(2,1)S(1)}, u32[]{:S(2)}, u32[]{:S(2)}) %collective-permute-start.22) | collective-permute-done | bytes 294944 | tf_op jit(solution)/shard_map/ppermute | solution.py:28
  98.9 0.1 collective-permute-done.23.refs_3_
  99.1 0.1 add_halves.6
  99.2 0.3 collective-permute-start.25
  99.5 1.6 %collective-permute-start.26 = (bf16[2,144,256]{2,1,0:T(8,128)(2,1)S(1)}, bf16[2,144,256]{2,1,0:T(8,128)(2,1)S(1)}, u32[]{:S(2)}, u32[]{:S(2)}) collective-permute-start(bf16[2,144,256]{2,1,0:T(8,128)(2,1)S(1)} %get-tuple-element.226), channel_id=1, source_target_pairs={{0,2},{1,3},{2,0},{3,1},{4,6},{5,7},{6,4},{7,5},{8,10},{9,11},{10,... | collective-permute-start | bytes 442376 | tf_op jit(solution)/shard_map/ppermute | solution.py:28
  101.2 4.0 %image_attention.2 = (f32[1024,256]{1,0:T(8,128)S(1)}, f32[1024,128]{1,0:T(8,128)S(1)}) custom-call(s32[5]{0:T(128)S(1)} %stack.19.place_ref, bf16[2048,128]{1,0:T(8,128)(2,1)S(1)} %bitcast.30, bf16[2,256,128]{2,1,0:T(8,128)(2,1)S(1)} %get-tuple-element.212.refs_0_, bf16[2,256,128]{2,1,0:T(8,128)(2,1)S(1)} %collective-permute-done.13.refs_1_, ...), custom_call_target="tpu_custom_call" | custom-call | flops 1073741824 | bytes 2359296 | tf_op jit(solution)/shard_map/image_attention/pallas_call | solution.py:413
  105.3 2.0 %collective-permute-start.27 = (bf16[1,144,256]{2,1,0:T(8,128)(2,1)S(1)}, bf16[1,144,256]{2,1,0:T(8,128)(2,1)S(1)}, u32[]{:S(2)}, u32[]{:S(2)}) collective-permute-start(bf16[1,144,256]{2,1,0:T(8,128)(2,1)S(1)} %get-tuple-element.235), channel_id=1, source_target_pairs={{0,8},{1,9},{2,10},{3,11},{4,12},{5,13},{6,14},{7,15},{8,0},{9,1},... | collective-permute-start | bytes 221192 | tf_op jit(solution)/shard_map/ppermute | solution.py:28
  107.3 1.0 collective-permute-start.28
  108.3 4.2 %image_attention.3 = (f32[1024,256]{1,0:T(8,128)S(1)}, f32[1024,128]{1,0:T(8,128)S(1)}) custom-call(s32[5]{0:T(128)S(1)} %stack.19.place_ref, bf16[2048,128]{1,0:T(8,128)(2,1)S(1)} %bitcast.31, bf16[2,256,128]{2,1,0:T(8,128)(2,1)S(1)} %get-tuple-element.212.refs_0_, bf16[2,256,128]{2,1,0:T(8,128)(2,1)S(1)} %collective-permute-done.13.refs_1_, ...), custom_call_target="tpu_custom_call" | custom-call | flops 1073741824 | bytes 2359296 | tf_op jit(solution)/shard_map/image_attention/pallas_call | solution.py:413
  112.6 1.0 collective-permute-done.27
  113.6 0.8 collective-permute-done.28
  114.4 0.7 combine.1
  115.2 1.2 collective-permute-done.29.refs_14_
  116.4 1.6 %finish.1 = bf16[16,160,128]{2,1,0:T(8,128)(2,1)S(1)} custom-call(s32[5]{0:T(128)S(1)} %stack.19.place_ref, bf16[2,256,128]{2,1,0:T(8,128)(2,1)S(1)} %get-tuple-element.212.refs_0_, bf16[2,256,128]{2,1,0:T(8,128)(2,1)S(1)} %collective-permute-done.13.refs_1_, bf16[2,256,128]{2,1,0:T(8,128)(2,1)S(1)} %collective-permute-done.14.refs_2_, ...), custom_call_target="tpu_custom_call" | custom-call | flops 268435456 | bytes 3145728 | tf_op jit(solution)/shard_map/finish/pallas_call | solution.py:485
  118.0 21.4 %all_to_all.10.blocks_ref = bf16[16,160,128]{2,1,0:T(8,128)(2,1)S(1)} all-to-all(bf16[16,160,128]{2,1,0:T(8,128)(2,1)S(1)} %finish.1), channel_id=1, replica_groups=mesh['dp'=2,'seq'=16] {'seq'}, dimensions={0} | all-to-all | bytes 1310720 | tf_op jit(solution)/shard_map/all_to_all | solution.py:638
  139.5 1.0 unpack.1
  (41 shorter events, 0.5 us)
Async XLA Ops:
  2.2 9.1 %copy-start.3 = (bf16[1,256,1184]{1,2,0:T(8,128)(2,1)S(1)}, bf16[1,256,1184]{1,2,0:T(8,128)(2,1)}, u32[]{:S(2)}) copy-start(bf16[1,256,1184]{1,2,0:T(8,128)(2,1)} %param.10) | copy-start | bytes 1818628
  3.2 21.8 %all-to-all-start = ((bf16[16,128,128]{2,1,0:T(8,128)(2,1)}), bf16[16,128,128]{2,1,0:T(8,128)(2,1)S(1)}, u32[]{:S(2)}, u32[]{:S(2)}) async-start(bf16[16,128,128]{2,1,0:T(8,128)(2,1)} %pack.1), calls=%async_computation | async-start | bytes 1048576 | tf_op jit(solution)/shard_map/all_to_all | solution.py:638
  11.3 3.4 %copy-start = (bf16[1184,3584]{1,0:T(8,128)(2,1)S(1)}, bf16[1184,3584]{1,0:T(8,128)(2,1)}, u32[]{:S(2)}) copy-start(bf16[1184,3584]{1,0:T(8,128)(2,1)} %weight_ref.1) | copy-start | bytes 25460740
  25.0 2.7 %copy-start.6 = (bf16[1,128,2,2048]{3,2,1,0:T(2,128)(2,1)S(1)}, bf16[1,128,2,2048]{3,2,1,0:T(2,128)(2,1)}, u32[]{:S(2)}) copy-start(bf16[1,128,2,2048]{3,2,1,0:T(2,128)(2,1)} %param.19) | copy-start | bytes 3145732
  25.0 1.8 %collective-permute-start = (bf16[8,16,1792]{2,1,0:T(8,128)(2,1)S(1)}, bf16[8,16,1792]{2,1,0:T(8,128)(2,1)S(1)}, u32[]{:S(2)}, u32[]{:S(2)}) collective-permute-start(bf16[8,16,1792]{2,1,0:T(8,128)(2,1)S(1)} %get-tuple-element.133), channel_id=1, source_target_pairs={{0,1},{1,0},{2,3},{3,2},{4,5},{5,4},{6,7},{7,6},{8,9},{9,8},{10,11... | collective-permute-start | bytes 1376264 | tf_op jit(solution)/shard_map/ppermute | solution.py:28
  25.0 2.5 %collective-permute-start.1 = (bf16[8,16,1792]{2,1,0:T(8,128)(2,1)S(1)}, bf16[8,16,1792]{2,1,0:T(8,128)(2,1)S(1)}, u32[]{:S(2)}, u32[]{:S(2)}) collective-permute-start(bf16[8,16,1792]{2,1,0:T(8,128)(2,1)S(1)} %get-tuple-element.135), channel_id=1, source_target_pairs={{0,1},{1,0},{2,3},{3,2},{4,5},{5,4},{6,7},{7,6},{8,9},{9,8},{10,11... | collective-permute-start | bytes 1376264 | tf_op jit(solution)/shard_map/ppermute | solution.py:28
  27.7 1.0 copy-start.4
  27.7 1.9 %copy-start.2 = (bf16[3584,192]{0,1:T(8,128)(2,1)S(1)}, bf16[3584,192]{0,1:T(8,128)(2,1)}, u32[]{:S(2)}) copy-start(bf16[3584,192]{0,1:T(8,128)(2,1)} %param.13) | copy-start | bytes 4128772
  28.1 13.0 %copy-start.1 = (bf16[192,4096]{1,0:T(8,128)(2,1)S(1)}, bf16[192,4096]{1,0:T(8,128)(2,1)}, u32[]{:S(2)}) copy-start(bf16[192,4096]{1,0:T(8,128)(2,1)} %refs_7_.1) | copy-start | bytes 4718596
  28.1 13.1 %copy-start.5 = (bf16[256,2,192]{0,2,1:T(8,128)(2,1)S(1)}, bf16[256,2,192]{0,2,1:T(8,128)(2,1)}, u32[]{:S(2)}) copy-start(bf16[256,2,192]{0,2,1:T(8,128)(2,1)} %param.14) | copy-start | bytes 589828
  28.7 29.6 %copy-start.7 = (bf16[3584]{0:T(1024)(128)(2,1)S(1)}, bf16[3584]{0:T(1024)(128)(2,1)}, u32[]{:S(2)}) copy-start(bf16[3584]{0:T(1024)(128)(2,1)} %param.12) | copy-start | bytes 21508
  29.6 11.4 %collective-permute-start.5 = (bf16[192,3584]{1,0:T(8,128)(2,1)S(1)}, bf16[192,3584]{1,0:T(8,128)(2,1)S(1)}, u32[]{:S(2)}, u32[]{:S(2)}) collective-permute-start(bf16[192,3584]{1,0:T(8,128)(2,1)S(1)} %bitcast.27), channel_id=1, source_target_pairs={{0,1},{1,0},{2,3},{3,2},{4,5},{5,4},{6,7},{7,6},{8,9},{9,8},{10,11... | collective-permute-start | bytes 4128776 | tf_op jit(solution)/shard_map/ppermute | solution.py:28
  29.8 10.3 %collective-permute-start.2 = (bf16[4,16,1792]{2,1,0:T(8,128)(2,1)S(1)}, bf16[4,16,1792]{2,1,0:T(8,128)(2,1)S(1)}, u32[]{:S(2)}, u32[]{:S(2)}) collective-permute-start(bf16[4,16,1792]{2,1,0:T(8,128)(2,1)S(1)} %get-tuple-element.145), channel_id=1, source_target_pairs={{0,2},{1,3},{2,0},{3,1},{4,6},{5,7},{6,4},{7,5},{8,10},{9,11},{10,... | collective-permute-start | bytes 688136 | tf_op jit(solution)/shard_map/ppermute | solution.py:28
  30.8 10.2 %collective-permute-start.3 = (bf16[4,16,1792]{2,1,0:T(8,128)(2,1)S(1)}, bf16[4,16,1792]{2,1,0:T(8,128)(2,1)S(1)}, u32[]{:S(2)}, u32[]{:S(2)}) collective-permute-start(bf16[4,16,1792]{2,1,0:T(8,128)(2,1)S(1)} %get-tuple-element.146), channel_id=1, source_target_pairs={{0,4},{1,5},{2,6},{3,7},{4,0},{5,1},{6,2},{7,3},{8,12},{9,13},{10,... | collective-permute-start | bytes 688136 | tf_op jit(solution)/shard_map/ppermute | solution.py:28
  32.3 7.8 %collective-permute-start.4 = (bf16[2,256,128]{2,1,0:T(8,128)(2,1)S(1)}, bf16[2,256,128]{2,1,0:T(8,128)(2,1)S(1)}, u32[]{:S(2)}, u32[]{:S(2)}) collective-permute-start(bf16[2,256,128]{2,1,0:T(8,128)(2,1)S(1)} %get-tuple-element.147), channel_id=1, source_target_pairs={{0,8},{1,9},{2,10},{3,11},{4,12},{5,13},{6,14},{7,15},{8,0},{9,1},... | collective-permute-start | bytes 393224 | tf_op jit(solution)/shard_map/ppermute | solution.py:28
  41.1 10.7 %collective-permute-start.9 = (bf16[192,4096]{1,0:T(8,128)(2,1)S(1)}, bf16[192,4096]{1,0:T(8,128)(2,1)S(1)}, u32[]{:S(2)}, u32[]{:S(2)}) collective-permute-start(bf16[192,4096]{1,0:T(8,128)(2,1)S(1)} %copy-done.1), channel_id=1, source_target_pairs={{0,1},{1,0},{2,3},{3,2},{4,5},{5,4},{6,7},{7,6},{8,9},{9,8},{10,11... | collective-permute-start | bytes 4718600 | tf_op jit(solution)/shard_map/ppermute | solution.py:28
  41.2 10.6 %collective-permute-start.10 = (bf16[2,192,256]{2,1,0:T(8,128)(2,1)S(1)}, bf16[2,192,256]{2,1,0:T(8,128)(2,1)S(1)}, u32[]{:S(2)}, u32[]{:S(2)}) collective-permute-start(bf16[2,192,256]{2,1,0:T(8,128)(2,1)S(1)} %bitcast.33), channel_id=1, source_target_pairs={{0,1},{1,0},{2,3},{3,2},{4,5},{5,4},{6,7},{7,6},{8,9},{9,8},{10,11... | collective-permute-start | bytes 589832 | tf_op jit(solution)/shard_map/ppermute | solution.py:28
  41.6 10.1 %collective-permute-start.8 = (bf16[2,256,128]{2,1,0:T(8,128)(2,1)S(1)}, bf16[2,256,128]{2,1,0:T(8,128)(2,1)S(1)}, u32[]{:S(2)}, u32[]{:S(2)}) collective-permute-start(bf16[2,256,128]{2,1,0:T(8,128)(2,1)S(1)} %get-tuple-element.160), channel_id=1, source_target_pairs={{0,10},{1,11},{2,8},{3,9},{4,14},{5,15},{6,12},{7,13},{8,2},{9,3},... | collective-permute-start | bytes 393224 | tf_op jit(solution)/shard_map/ppermute | solution.py:28
  44.6 6.0 %collective-permute-start.6 = (bf16[2,16,1792]{2,1,0:T(8,128)(2,1)S(1)}, bf16[2,16,1792]{2,1,0:T(8,128)(2,1)S(1)}, u32[]{:S(2)}, u32[]{:S(2)}) collective-permute-start(bf16[2,16,1792]{2,1,0:T(8,128)(2,1)S(1)} %get-tuple-element.158), channel_id=1, source_target_pairs={{0,4},{1,5},{2,6},{3,7},{4,0},{5,1},{6,2},{7,3},{8,12},{9,13},{10,... | collective-permute-start | bytes 344072 | tf_op jit(solution)/shard_map/ppermute | solution.py:28
  44.9 5.8 %collective-permute-start.7 = (bf16[2,16,1792]{2,1,0:T(8,128)(2,1)S(1)}, bf16[2,16,1792]{2,1,0:T(8,128)(2,1)S(1)}, u32[]{:S(2)}, u32[]{:S(2)}) collective-permute-start(bf16[2,16,1792]{2,1,0:T(8,128)(2,1)S(1)} %get-tuple-element.159), channel_id=1, source_target_pairs={{0,2},{1,3},{2,0},{3,1},{4,6},{5,7},{6,4},{7,5},{8,10},{9,11},{10,... | collective-permute-start | bytes 344072 | tf_op jit(solution)/shard_map/ppermute | solution.py:28
  51.8 11.9 %collective-permute-start.11 = (bf16[2,16,1792]{2,1,0:T(8,128)(2,1)S(1)}, bf16[2,16,1792]{2,1,0:T(8,128)(2,1)S(1)}, u32[]{:S(2)}, u32[]{:S(2)}) collective-permute-start(bf16[2,16,1792]{2,1,0:T(8,128)(2,1)S(1)} %get-tuple-element.173.mine0), channel_id=1, source_target_pairs={{0,8},{1,9},{2,10},{3,11},{4,12},{5,13},{6,14},{7,15},{8,0},{9,1},... | collective-permute-start | bytes 344072 | tf_op jit(solution)/shard_map/ppermute | solution.py:28
  54.1 10.9 %collective-permute-start.12 = (bf16[2,16,1792]{2,1,0:T(8,128)(2,1)S(1)}, bf16[2,16,1792]{2,1,0:T(8,128)(2,1)S(1)}, u32[]{:S(2)}, u32[]{:S(2)}) collective-permute-start(bf16[2,16,1792]{2,1,0:T(8,128)(2,1)S(1)} %get-tuple-element.174.mine1), channel_id=1, source_target_pairs={{0,8},{1,9},{2,10},{3,11},{4,12},{5,13},{6,14},{7,15},{8,0},{9,1},... | collective-permute-start | bytes 344072 | tf_op jit(solution)/shard_map/ppermute | solution.py:28
  54.8 10.2 %collective-permute-start.13 = (bf16[2,256,128]{2,1,0:T(8,128)(2,1)S(1)}, bf16[2,256,128]{2,1,0:T(8,128)(2,1)S(1)}, u32[]{:S(2)}, u32[]{:S(2)}) collective-permute-start(bf16[2,256,128]{2,1,0:T(8,128)(2,1)S(1)} %get-tuple-element.175), channel_id=1, source_target_pairs={{0,2},{1,3},{2,0},{3,1},{4,6},{5,7},{6,4},{7,5},{8,10},{9,11},{10,... | collective-permute-start | bytes 393224 | tf_op jit(solution)/shard_map/ppermute | solution.py:28
  56.0 9.9 %collective-permute-start.14 = (bf16[2,256,128]{2,1,0:T(8,128)(2,1)S(1)}, bf16[2,256,128]{2,1,0:T(8,128)(2,1)S(1)}, u32[]{:S(2)}, u32[]{:S(2)}) collective-permute-start(bf16[2,256,128]{2,1,0:T(8,128)(2,1)S(1)} %get-tuple-element.176), channel_id=1, source_target_pairs={{0,4},{1,5},{2,6},{3,7},{4,0},{5,1},{6,2},{7,3},{8,12},{9,13},{10,... | collective-permute-start | bytes 393224 | tf_op jit(solution)/shard_map/ppermute | solution.py:28
  58.0 9.1 %collective-permute-start.15 = (bf16[2,256,128]{2,1,0:T(8,128)(2,1)S(1)}, bf16[2,256,128]{2,1,0:T(8,128)(2,1)S(1)}, u32[]{:S(2)}, u32[]{:S(2)}) collective-permute-start(bf16[2,256,128]{2,1,0:T(8,128)(2,1)S(1)} %get-tuple-element.177), channel_id=1, source_target_pairs={{0,6},{1,7},{2,4},{3,5},{4,2},{5,3},{6,0},{7,1},{8,14},{9,15},{10,... | collective-permute-start | bytes 393224 | tf_op jit(solution)/shard_map/ppermute | solution.py:28
  67.3 8.5 %collective-permute-start.18 = (bf16[2,256,128]{2,1,0:T(8,128)(2,1)S(1)}, bf16[2,256,128]{2,1,0:T(8,128)(2,1)S(1)}, u32[]{:S(2)}, u32[]{:S(2)}) collective-permute-start(bf16[2,256,128]{2,1,0:T(8,128)(2,1)S(1)} %get-tuple-element.188), channel_id=1, source_target_pairs={{0,12},{1,13},{2,14},{3,15},{4,8},{5,9},{6,10},{7,11},{8,4},{9,5},... | collective-permute-start | bytes 393224 | tf_op jit(solution)/shard_map/ppermute | solution.py:28
  70.0 5.8 %collective-permute-start.16 = (bf16[32,1792]{1,0:T(8,128)(2,1)S(1)}, bf16[32,1792]{1,0:T(8,128)(2,1)S(1)}, u32[]{:S(2)}, u32[]{:S(2)}) collective-permute-start(bf16[32,1792]{1,0:T(8,128)(2,1)S(1)} %bitcast.37), channel_id=1, source_target_pairs={{0,4},{1,5},{2,6},{3,7},{4,0},{5,1},{6,2},{7,3},{8,12},{9,13},{10,... | collective-permute-start | bytes 344072 | tf_op jit(solution)/shard_map/ppermute | solution.py:28
  70.0 5.8 %collective-permute-start.17 = (bf16[32,1792]{1,0:T(8,128)(2,1)S(1)}, bf16[32,1792]{1,0:T(8,128)(2,1)S(1)}, u32[]{:S(2)}, u32[]{:S(2)}) collective-permute-start(bf16[32,1792]{1,0:T(8,128)(2,1)S(1)} %bitcast.39), channel_id=1, source_target_pairs={{0,2},{1,3},{2,0},{3,1},{4,6},{5,7},{6,4},{7,5},{8,10},{9,11},{10,... | collective-permute-start | bytes 344072 | tf_op jit(solution)/shard_map/ppermute | solution.py:28
  75.8 11.2 %collective-permute-start.19 = (bf16[64,1792]{1,0:T(8,128)(2,1)S(1)}, bf16[64,1792]{1,0:T(8,128)(2,1)S(1)}, u32[]{:S(2)}, u32[]{:S(2)}) collective-permute-start(bf16[64,1792]{1,0:T(8,128)(2,1)S(1)} %get-tuple-element.194.refs_0_), channel_id=1, source_target_pairs={{0,2},{1,3},{2,0},{3,1},{4,6},{5,7},{6,4},{7,5},{8,10},{9,11},{10,... | collective-permute-start | bytes 688136 | tf_op jit(solution)/shard_map/ppermute | solution.py:28
  77.2 9.9 %collective-permute-start.20 = (bf16[64,1792]{1,0:T(8,128)(2,1)S(1)}, bf16[64,1792]{1,0:T(8,128)(2,1)S(1)}, u32[]{:S(2)}, u32[]{:S(2)}) collective-permute-start(bf16[64,1792]{1,0:T(8,128)(2,1)S(1)} %get-tuple-element.195.refs_2_), channel_id=1, source_target_pairs={{0,4},{1,5},{2,6},{3,7},{4,0},{5,1},{6,2},{7,3},{8,12},{9,13},{10,... | collective-permute-start | bytes 688136 | tf_op jit(solution)/shard_map/ppermute | solution.py:28
  78.3 8.7 %collective-permute-start.21 = (bf16[2,256,128]{2,1,0:T(8,128)(2,1)S(1)}, bf16[2,256,128]{2,1,0:T(8,128)(2,1)S(1)}, u32[]{:S(2)}, u32[]{:S(2)}) collective-permute-start(bf16[2,256,128]{2,1,0:T(8,128)(2,1)S(1)} %get-tuple-element.196), channel_id=1, source_target_pairs={{0,14},{1,15},{2,12},{3,13},{4,10},{5,11},{6,8},{7,9},{8,6},{9,7},... | collective-permute-start | bytes 393224 | tf_op jit(solution)/shard_map/ppermute | solution.py:28
  89.4 9.6 %collective-permute-start.24 = (bf16[8,256,128]{2,1,0:T(8,128)(2,1)S(1)}, bf16[8,256,128]{2,1,0:T(8,128)(2,1)S(1)}, u32[]{:S(2)}, u32[]{:S(2)}) collective-permute-start(bf16[8,256,128]{2,1,0:T(8,128)(2,1)S(1)} %gather_other.1), channel_id=1, source_target_pairs={{0,1},{1,0},{2,3},{3,2},{4,5},{5,4},{6,7},{7,6},{8,9},{9,8},{10,11... | collective-permute-start | bytes 1572872 | tf_op jit(solution)/shard_map/ppermute | solution.py:28
  89.5 9.4 %collective-permute-start.22 = (bf16[4,144,256]{2,1,0:T(8,128)(2,1)S(1)}, bf16[4,144,256]{2,1,0:T(8,128)(2,1)S(1)}, u32[]{:S(2)}, u32[]{:S(2)}) collective-permute-start(bf16[4,144,256]{2,1,0:T(8,128)(2,1)S(1)} %get-tuple-element.202), channel_id=1, source_target_pairs={{0,2},{1,3},{2,0},{3,1},{4,6},{5,7},{6,4},{7,5},{8,10},{9,11},{10,... | collective-permute-start | bytes 884744 | tf_op jit(solution)/shard_map/ppermute | solution.py:28
  90.0 9.1 %collective-permute-start.23 = (bf16[4,144,256]{2,1,0:T(8,128)(2,1)S(1)}, bf16[4,144,256]{2,1,0:T(8,128)(2,1)S(1)}, u32[]{:S(2)}, u32[]{:S(2)}) collective-permute-start(bf16[4,144,256]{2,1,0:T(8,128)(2,1)S(1)} %get-tuple-element.203), channel_id=1, source_target_pairs={{0,4},{1,5},{2,6},{3,7},{4,0},{5,1},{6,2},{7,3},{8,12},{9,13},{10,... | collective-permute-start | bytes 884744 | tf_op jit(solution)/shard_map/ppermute | solution.py:28
  99.2 6.1 %collective-permute-start.25 = (bf16[2,144,256]{2,1,0:T(8,128)(2,1)S(1)}, bf16[2,144,256]{2,1,0:T(8,128)(2,1)S(1)}, u32[]{:S(2)}, u32[]{:S(2)}) collective-permute-start(bf16[2,144,256]{2,1,0:T(8,128)(2,1)S(1)} %get-tuple-element.225), channel_id=1, source_target_pairs={{0,4},{1,5},{2,6},{3,7},{4,0},{5,1},{6,2},{7,3},{8,12},{9,13},{10,... | collective-permute-start | bytes 442376 | tf_op jit(solution)/shard_map/ppermute | solution.py:28
  99.5 5.7 %collective-permute-start.26 = (bf16[2,144,256]{2,1,0:T(8,128)(2,1)S(1)}, bf16[2,144,256]{2,1,0:T(8,128)(2,1)S(1)}, u32[]{:S(2)}, u32[]{:S(2)}) collective-permute-start(bf16[2,144,256]{2,1,0:T(8,128)(2,1)S(1)} %get-tuple-element.226), channel_id=1, source_target_pairs={{0,2},{1,3},{2,0},{3,1},{4,6},{5,7},{6,4},{7,5},{8,10},{9,11},{10,... | collective-permute-start | bytes 442376 | tf_op jit(solution)/shard_map/ppermute | solution.py:28
  105.3 8.3 %collective-permute-start.27 = (bf16[1,144,256]{2,1,0:T(8,128)(2,1)S(1)}, bf16[1,144,256]{2,1,0:T(8,128)(2,1)S(1)}, u32[]{:S(2)}, u32[]{:S(2)}) collective-permute-start(bf16[1,144,256]{2,1,0:T(8,128)(2,1)S(1)} %get-tuple-element.235), channel_id=1, source_target_pairs={{0,8},{1,9},{2,10},{3,11},{4,12},{5,13},{6,14},{7,15},{8,0},{9,1},... | collective-permute-start | bytes 221192 | tf_op jit(solution)/shard_map/ppermute | solution.py:28
  107.3 7.1 %collective-permute-start.28 = (bf16[1,144,256]{2,1,0:T(8,128)(2,1)S(1)}, bf16[1,144,256]{2,1,0:T(8,128)(2,1)S(1)}, u32[]{:S(2)}, u32[]{:S(2)}) collective-permute-start(bf16[1,144,256]{2,1,0:T(8,128)(2,1)S(1)} %get-tuple-element.236), channel_id=1, source_target_pairs={{0,8},{1,9},{2,10},{3,11},{4,12},{5,13},{6,14},{7,15},{8,0},{9,1},... | collective-permute-start | bytes 221192 | tf_op jit(solution)/shard_map/ppermute | solution.py:28
  115.1 1.3 collective-permute-start.29

commit v15 on v13

--- a/solution.py
+++ b/solution.py
@@ -225,15 +225,12 @@
 
 
 def combine_kernel(chips, model_width, place_ref, *refs):
-    refs, mine_ref, sent_ref = refs[:4], refs[4], refs[5]
+    keep0, keep1, came_ref, mine_ref, sent_ref = refs
     core = place_ref[2]
     rows = mine_ref.shape[0]
-    width = refs[0].shape[1]
+    width = keep0.shape[2]
     slots = slot_rows(chips, width)[0]
-    totals = [
-        refs[2 * lane][...].astype(jnp.float32) + refs[2 * lane + 1][...].astype(jnp.float32)
-        for lane in range(2)
-    ]
+    totals = [keep[0] + came_ref[lane, 0].astype(jnp.float32) for lane, keep in enumerate((keep0, keep1))]
     sums = []
     for total in totals:
         line = jnp.sum(total[rows : rows + slots], 0, keepdims=True)
@@ -264,7 +261,7 @@
     return pl.pallas_call(
         functools.partial(combine_kernel, chips, model_width),
         out_shape=(out, out),
-        in_specs=[SMEM_SPEC] + [VMEM_SPEC] * 4,
+        in_specs=[SMEM_SPEC] + [VMEM_SPEC] * 3,
         out_specs=(VMEM_SPEC, VMEM_SPEC),
         compiler_params=params(4),
         cost_estimate=pl.CostEstimate(
@@ -441,8 +438,10 @@
     )(place, packed, *images, mine, got)
 
 
-def add_kernel(*refs):
+def add_kernel(joint, *refs):
     ins, outs = refs[:4], refs[4:]
+    if joint:
+        outs = (outs[0].at[0], outs[1], outs[0].at[1], outs[2])
     for lane in range(2):
         mine, got = ins[2 * lane], ins[2 * lane + 1]
         half = mine.shape[0] // 2
@@ -452,46 +451,75 @@
         outs[2 * lane + 1][...] = mine[:half].astype(jnp.float32) + got[:half].astype(jnp.float32)
 
 
-def add_halves(mine, got):
+def add_halves(mine, got, joint=False):
     shape = (mine[0].shape[0] // 2,) + mine[0].shape[1:]
-    outs = (jax.ShapeDtypeStruct(shape, jnp.bfloat16), jax.ShapeDtypeStruct(shape, jnp.float32))
-    sent0, keep0, sent1, keep1 = pl.pallas_call(
-        add_kernel,
-        out_shape=outs * 2,
+    sent, keep = jax.ShapeDtypeStruct(shape, jnp.bfloat16), jax.ShapeDtypeStruct(shape, jnp.float32)
+    outs = (sent, keep) * 2
+    if joint:
+        outs = (jax.ShapeDtypeStruct((2,) + shape, jnp.bfloat16), keep, keep)
+    outs = pl.pallas_call(
+        functools.partial(add_kernel, joint),
+        out_shape=outs,
         in_specs=[VMEM_SPEC] * 4,
-        out_specs=(VMEM_SPEC,) * 4,
+        out_specs=(VMEM_SPEC,) * len(outs),
         compiler_params=params(6),
         cost_estimate=pl.CostEstimate(
             flops=2 * mine[0].size, bytes_accessed=12 * mine[0].size, transcendentals=0
         ),
         name="add_halves",
     )(mine[0], got[0], mine[1], got[1])
-    return [sent0, sent1], [keep0, keep1]
-
-
-def norm_kernel(keep0, got0, keep1, got1, gain_ref, out0, out1):
-    totals = [keep0[0] + got0[0].astype(jnp.float32), keep1[0] + got1[0].astype(jnp.float32)]
-    width = totals[0].shape[1]
-    square = sum(jnp.sum(total * total, 1, keepdims=True) for total in totals)
-    scale_rows = lax.rsqrt(square / (2 * width) + epsilon)
-    for lane, (total, out_ref) in enumerate(zip(totals, (out0, out1))):
-        gain = gain_ref[:, lane * width : (lane + 1) * width].astype(jnp.float32)
-        out_ref[...] = (total * scale_rows * gain).astype(out_ref.dtype)
-
-
-def normalize(keep, got, norm_gain):
-    out = jax.ShapeDtypeStruct(keep[0].shape[1:], jnp.bfloat16)
-    return pl.pallas_call(
+    if joint:
+        return outs[0], outs[1:]
+    return [outs[0], outs[2]], [outs[1], outs[3]]
+
+
+def total_kernel(mine0, got0, mine1, got1, out_ref):
+    for lane, (mine, got) in enumerate(((mine0, got0), (mine1, got1))):
+        out_ref[lane] = (mine[...] + got[...].astype(jnp.float32)).astype(out_ref.dtype)
+
+
+def add_all(mine, got):
+    return pl.pallas_call(
+        total_kernel,
+        out_shape=jax.ShapeDtypeStruct((2,) + mine[0].shape, jnp.bfloat16),
+        in_specs=[VMEM_SPEC] * 4,
+        out_specs=VMEM_SPEC,
+        compiler_params=params(4),
+        cost_estimate=pl.CostEstimate(
+            flops=2 * mine[0].size, bytes_accessed=16 * mine[0].size, transcendentals=0
+        ),
+        name="add_all",
+    )(mine[0], got[0], mine[1], got[1])
+
+
+def norm_kernel(mine_ref, got_ref, gain_ref, out0, out1):
+    width = mine_ref.shape[3]
+    for at in range(2):
+        totals = [
+            mine_ref[lane, at].astype(jnp.float32) + got_ref[lane, 1 - at].astype(jnp.float32)
+            for lane in range(2)
+        ]
+        square = sum(jnp.sum(total * total, 1, keepdims=True) for total in totals)
+        scale_rows = lax.rsqrt(square / (2 * width) + epsilon)
+        for lane, (total, out_ref) in enumerate(zip(totals, (out0, out1))):
+            gain = gain_ref[:, lane * width : (lane + 1) * width].astype(jnp.float32)
+            out_ref[at] = (total * scale_rows * gain).astype(out_ref.dtype)
+
+
+def normalize(mine, got, norm_gain):
+    out = jax.ShapeDtypeStruct(mine.shape[1:], jnp.bfloat16)
+    states = pl.pallas_call(
         norm_kernel,
         out_shape=(out, out),
-        in_specs=[VMEM_SPEC] * 5,
+        in_specs=[VMEM_SPEC] * 3,
         out_specs=(VMEM_SPEC,) * 2,
         compiler_params=params(4),
         cost_estimate=pl.CostEstimate(
-            flops=8 * keep[0].size, bytes_accessed=16 * keep[0].size, transcendentals=0
+            flops=4 * mine.size, bytes_accessed=8 * mine.size, transcendentals=0
         ),
         name="normalize",
-    )(keep[0], got[0], keep[1], got[1], norm_gain)
+    )(mine, got, norm_gain)
+    return [part.reshape(-1, part.shape[2]) for part in states]
 
 
 def join_kernel(mine0, got0, mine1, got1, out0, out1):
@@ -562,29 +590,25 @@
     packed = exchange(packed)
     encoded = encoder(lanes, place, act, down_weight)
     keep, got = encoded[::2], [swap(other, 1) for other in encoded[1::2]]
-    for step in range(rounds):
+    last = 2 * lanes[0][-1]
+    for step in range(rounds - 1):
         sent, keep = add_halves(keep, got)
         got = [swap(part, 2 * order[step]) for part, order in zip(sent, lanes)]
-        if step == 0:
-            got, packed = tie((got, packed))
-
-    states = normalize(keep, got, norm_gain[None, :])
+    summed = add_all(keep, got)
+    summed, held, held_kv, held_mod = tie((summed, win0, kv0, mod0))
+    win1, kv1, mod1 = swap(held, 1), swap(held_kv, 1), swap(held_mod, 1)
+    got, packed = tie((swap(summed, last), packed))
+
+    states = normalize(summed, got, norm_gain[None, :])
     images = []
-
-    for step in reversed(range(rounds)):
-        if step == rounds - 1:
-            states, held, mod1 = tie((states, win0, mod0))
-            win1, mod1 = swap(held, 1), swap(mod1, 1)
-        if step == rounds - 2:
-            states, held = tie((states, kv0))
-            kv1 = swap(held, 1)
-            lines = modulation(time, mod0, mod1)
+    for step in reversed(range(rounds - 1)):
         if step == 0:
             states, packed = tie((states, packed))
             image = image_attention(packed, img_dev, factor, 0, 2)
         got = [swap(state, 2 * order[step]) for state, order in zip(states, lanes)]
         if step == rounds - 2:
-            got, lines = tie((got, lines))
+            lines = modulation(time, mod0, mod1)
+            got, win1, kv1, lines = tie((got, win1, kv1, lines))
         if step:
             states = join(states, got)
     got, image = tie((got, image))
@@ -593,7 +617,7 @@
 
     blocks = project(lanes, place, states, lines, win0, win1, kv0, kv1)
     keep, sent = [blocks[0], blocks[2]], [blocks[1], blocks[3]]
-    for step in range(rounds):
+    for step in range(rounds - 1):
         if step == 0:
             sent, packed = tie((sent, packed))
             image = image_attention(packed, img_dev, factor, 1, 2)
@@ -601,9 +625,8 @@
         if step == 0:
             got, image = tie((got, image))
             images += image
-        if step < rounds - 1:
-            sent, keep = add_halves(keep, got)
-    parts = [part[0] for pair in zip(keep, got) for part in pair]
+        sent, keep = add_halves(keep, got, step == rounds - 2)
+    parts = (*keep, swap(sent, last))
     model_width = text_in_weight.shape[1] * devices
     mine, sent = combine(place, parts, chips, text_len // 2, model_width)
     got = swap(sent, 1)

time: 140 us -> 134 us (0.957)
  starting transfers between devices: 40 us -> 25.4 us
  waiting for transfers between devices: 46.2 us -> 56.6 us
  local copies, waits for them, and re-layouts: 11.4 us -> 7.75 us
  Pallas kernels: 18.4 us -> 21.1 us
    ppermute x24 -> x20, starting transfers between devices: 32.5 us -> 17.9 us  [swap(): return lax.ppermute(value, 'seq', [(i, i ^ mask) for i in range(devices)])]
    ppermute x24 -> x20, waiting for transfers between devices: 46.2 us -> 56.6 us  [swap(): return lax.ppermute(value, 'seq', [(i, i ^ mask) for i in range(devices)])]
    unnamed x26 -> x14, local copies, waits for them, and re-layouts: 9.6 us -> 5.98 us
    pallas_call x1, Pallas kernels: 2.34 us -> 4.04 us  [project(): pl.pallas_call(functools.partial(project_kernel, lanes), out_shape=(out,)...]
  transfers between devices with their start and end apart: 25 -> 21, of which waited for: 22 -> 16; matrix products, arithmetic and copies ran while one was open for 0% -> 0% of each run, Pallas kernels for 8% -> 9%
where the time goes in v15:
time: 134 us
  waiting for transfers between devices  56.6 us (42%)
  starting transfers between devices  25.4 us (19%)
  Pallas kernels  21.1 us (16%)
  blocking collectives  21 us (16%)
  local copies, waits for them, and re-layouts  7.75 us (6%)
  between operations  2.19 us (2%)
    ppermute x20, waiting for transfers between devices, swap(): return lax.ppermute(value, 'seq', [(i, i ^ mask) for i in range(devices)])  56.6 us
    all_to_all x1, blocking collectives, exchange(): return lax.all_to_all(rows, 'seq', split_axis=0, concat_axis=0, tiled=True)  21 us
    ppermute x20, starting transfers between devices, swap(): return lax.ppermute(value, 'seq', [(i, i ^ mask) for i in range(devices)])  17.9 us
    all_to_all x1, starting transfers between devices, exchange(): return lax.all_to_all(rows, 'seq', split_axis=0, concat_axis=0, tiled=True)  7.49 us
    pallas_call x2, Pallas kernels, image_attention(): pl.pallas_call(functools.partial(image_kernel, factor, call, img_dev), ou...  6.87 us
    unnamed x14, local copies, waits for them, and re-layouts  5.98 us
    pallas_call x1, Pallas kernels, project(): pl.pallas_call(functools.partial(project_kernel, lanes), out_shape=(out,)...  4.04 us
    pallas_call x1, Pallas kernels, encoder(): pl.pallas_call(functools.partial(encoder_kernel, lanes), out_shape=(out,)...  3.49 us
  transfers between devices with their start and end apart: 21, of which 16 were waited for; matrix products, arithmetic and copies ran while one was open for 0% of the time, Pallas kernels for 9%

profile of v15, /device:TPU:0, one launch (start us, length us, event | category | flops | bytes accessed | tf_op | source)
XLA Modules:
  0.0 134.0 jit_solution(9019574274947136616)
XLA Ops:
  0.6 1.6 %copy.12 = bf16[1,128,2,2048]{3,1,2,0:T(8,128)(2,1)S(1)} copy(bf16[1,128,2,2048]{3,2,1,0:T(2,128)(2,1)} %param.19) | data formatting | bytes 2097152 | tf_op jit(solution)/shard_map/optimization_barrier | solution.py:587
  2.2 0.0 copy-start.3
  2.2 0.1 slice_bitcast_fusion
  2.3 0.9 copy-done.3
  3.3 1.5 %pack.1 = bf16[16,384,128]{2,1,0:T(8,128)(2,1)} custom-call(bf16[128,2048]{1,0:T(8,128)(2,1)S(1)} %bitcast.23, bf16[128,2048]{1,0:T(8,128)(2,1)S(1)} %get-tuple-element.131.keys_ref, bf16[128,2048]{1,0:T(8,128)(2,1)S(1)} %get-tuple-element.130.values_ref), custom_call_target="tpu_custom_call" | custom-call | bytes 3145728 | tf_op jit(solution)/shard_map/pack/pallas_call | solution.py:288
  4.7 7.5 %all-to-all-start = ((bf16[16,384,128]{2,1,0:T(8,128)(2,1)}), bf16[16,384,128]{2,1,0:T(8,128)(2,1)S(1)}, u32[]{:S(2)}, u32[]{:S(2)}) async-start(bf16[16,384,128]{2,1,0:T(8,128)(2,1)} %pack.1), calls=%async_computation | async-start | bytes 3145728 | tf_op jit(solution)/shard_map/all_to_all | solution.py:585
  12.9 0.1 stack.19.place_ref
  13.0 3.4 %copy-done = bf16[1184,3584]{1,0:T(8,128)(2,1)S(1)} copy-done((bf16[1184,3584]{1,0:T(8,128)(2,1)S(1)}, bf16[1184,3584]{1,0:T(8,128)(2,1)}, u32[]{:S(2)}) %copy-start) | copy-done | bytes 8486936
  16.4 3.5 %encoder.1 = (bf16[8,16,1792]{2,1,0:T(8,128)(2,1)S(1)}, bf16[8,16,1792]{2,1,0:T(8,128)(2,1)S(1)}, bf16[8,16,1792]{2,1,0:T(8,128)(2,1)S(1)}, bf16[8,16,1792]{2,1,0:T(8,128)(2,1)S(1)}) custom-call(s32[5]{0:T(128)S(1)} %stack.19.place_ref, bf16[1184,256]{1,0:T(8,128)(2,1)S(1)} %bitcast.22, bf16[1184,3584]{1,0:T(8,128)(2,1)S(1)} %copy-done), custom_call_target="tpu_custom_call" | custom-call | flops 2172649472 | bytes 10928128 | tf_op jit(solution)/shard_map/encoder/pallas_call | solution.py:84
  19.9 0.5 collective-permute-start
  20.3 0.1 collective-permute-start.1
  20.5 1.3 collective-permute-done.refs_1_
  21.8 0.7 collective-permute-done.1.refs_3_
  22.4 0.2 add_halves.4
  22.6 0.0 copy-start.1
  22.6 0.0 copy-start.6
  22.7 2.0 %collective-permute-start.2 = (bf16[4,16,1792]{2,1,0:T(8,128)(2,1)S(1)}, bf16[4,16,1792]{2,1,0:T(8,128)(2,1)S(1)}, u32[]{:S(2)}, u32[]{:S(2)}) collective-permute-start(bf16[4,16,1792]{2,1,0:T(8,128)(2,1)S(1)} %get-tuple-element.74), channel_id=1, source_target_pairs={{0,2},{1,3},{2,0},{3,1},{4,6},{5,7},{6,4},{7,5},{8,10},{9,11},{10,... | collective-permute-start | bytes 688136 | tf_op jit(solution)/shard_map/ppermute | solution.py:28
  24.6 1.5 %collective-permute-start.3 = (bf16[4,16,1792]{2,1,0:T(8,128)(2,1)S(1)}, bf16[4,16,1792]{2,1,0:T(8,128)(2,1)S(1)}, u32[]{:S(2)}, u32[]{:S(2)}) collective-permute-start(bf16[4,16,1792]{2,1,0:T(8,128)(2,1)S(1)} %get-tuple-element.76), channel_id=1, source_target_pairs={{0,4},{1,5},{2,6},{3,7},{4,0},{5,1},{6,2},{7,3},{8,12},{9,13},{10,... | collective-permute-start | bytes 688136 | tf_op jit(solution)/shard_map/ppermute | solution.py:28
  26.1 10.1 %collective-permute-done.2.refs_1_ = bf16[4,16,1792]{2,1,0:T(8,128)(2,1)S(1)} collective-permute-done((bf16[4,16,1792]{2,1,0:T(8,128)(2,1)S(1)}, bf16[4,16,1792]{2,1,0:T(8,128)(2,1)S(1)}, u32[]{:S(2)}, u32[]{:S(2)}) %collective-permute-start.2) | collective-permute-done | bytes 229408 | tf_op jit(solution)/shard_map/ppermute | solution.py:28
  36.1 7.5 %collective-permute-done.3.refs_3_ = bf16[4,16,1792]{2,1,0:T(8,128)(2,1)S(1)} collective-permute-done((bf16[4,16,1792]{2,1,0:T(8,128)(2,1)S(1)}, bf16[4,16,1792]{2,1,0:T(8,128)(2,1)S(1)}, u32[]{:S(2)}, u32[]{:S(2)}) %collective-permute-start.3) | collective-permute-done | bytes 229408 | tf_op jit(solution)/shard_map/ppermute | solution.py:28
  43.7 0.1 add_halves.5
  43.8 2.5 %collective-permute-start.4 = (bf16[2,16,1792]{2,1,0:T(8,128)(2,1)S(1)}, bf16[2,16,1792]{2,1,0:T(8,128)(2,1)S(1)}, u32[]{:S(2)}, u32[]{:S(2)}) collective-permute-start(bf16[2,16,1792]{2,1,0:T(8,128)(2,1)S(1)} %get-tuple-element.78), channel_id=1, source_target_pairs={{0,4},{1,5},{2,6},{3,7},{4,0},{5,1},{6,2},{7,3},{8,12},{9,13},{10,... | collective-permute-start | bytes 344072 | tf_op jit(solution)/shard_map/ppermute | solution.py:28
  46.3 1.7 %collective-permute-start.5 = (bf16[2,16,1792]{2,1,0:T(8,128)(2,1)S(1)}, bf16[2,16,1792]{2,1,0:T(8,128)(2,1)S(1)}, u32[]{:S(2)}, u32[]{:S(2)}) collective-permute-start(bf16[2,16,1792]{2,1,0:T(8,128)(2,1)S(1)} %get-tuple-element.80), channel_id=1, source_target_pairs={{0,2},{1,3},{2,0},{3,1},{4,6},{5,7},{6,4},{7,5},{8,10},{9,11},{10,... | collective-permute-start | bytes 344072 | tf_op jit(solution)/shard_map/ppermute | solution.py:28
  48.0 1.5 %collective-permute-done.4.got0 = bf16[2,16,1792]{2,1,0:T(8,128)(2,1)S(1)} collective-permute-done((bf16[2,16,1792]{2,1,0:T(8,128)(2,1)S(1)}, bf16[2,16,1792]{2,1,0:T(8,128)(2,1)S(1)}, u32[]{:S(2)}, u32[]{:S(2)}) %collective-permute-start.4) | collective-permute-done | bytes 114720 | tf_op jit(solution)/shard_map/ppermute | solution.py:28
  49.5 1.6 %collective-permute-done.5.got1 = bf16[2,16,1792]{2,1,0:T(8,128)(2,1)S(1)} collective-permute-done((bf16[2,16,1792]{2,1,0:T(8,128)(2,1)S(1)}, bf16[2,16,1792]{2,1,0:T(8,128)(2,1)S(1)}, u32[]{:S(2)}, u32[]{:S(2)}) %collective-permute-start.5) | collective-permute-done | bytes 114720 | tf_op jit(solution)/shard_map/ppermute | solution.py:28
  51.1 0.1 collective-permute-start.10
  51.2 0.5 collective-permute-start.9
  51.7 2.9 %collective-permute-start.6 = (bf16[2,2,16,1792]{3,2,1,0:T(8,128)(2,1)S(1)}, bf16[2,2,16,1792]{3,2,1,0:T(8,128)(2,1)S(1)}, u32[]{:S(2)}, u32[]{:S(2)}) collective-permute-start(bf16[2,2,16,1792]{3,2,1,0:T(8,128)(2,1)S(1)} %add_all.1.mine_ref), channel_id=1, source_target_pairs={{0,8},{1,9},{2,10},{3,11},{4,12},{5,13},{6,14},{7,15},{8,0},{9,1},... | collective-permute-start | bytes 688136 | tf_op jit(solution)/shard_map/ppermute | solution.py:28
  55.3 0.1 collective-permute-start.11
  55.3 10.0 %collective-permute-done.6.got_ref = bf16[2,2,16,1792]{3,2,1,0:T(8,128)(2,1)S(1)} collective-permute-done((bf16[2,2,16,1792]{3,2,1,0:T(8,128)(2,1)S(1)}, bf16[2,2,16,1792]{3,2,1,0:T(8,128)(2,1)S(1)}, u32[]{:S(2)}, u32[]{:S(2)}) %collective-permute-start.6) | collective-permute-done | bytes 229408 | tf_op jit(solution)/shard_map/ppermute | solution.py:28
  65.3 0.7 copy-done.4
  66.0 0.0 all-to-all-done.packed_ref
  66.0 0.9 copy-done.5
  67.0 0.2 normalize.1
  67.2 1.6 %collective-permute-start.8 = (bf16[32,1792]{1,0:T(8,128)(2,1)S(1)}, bf16[32,1792]{1,0:T(8,128)(2,1)S(1)}, u32[]{:S(2)}, u32[]{:S(2)}) collective-permute-start(bf16[32,1792]{1,0:T(8,128)(2,1)S(1)} %bitcast.26), channel_id=1, source_target_pairs={{0,2},{1,3},{2,0},{3,1},{4,6},{5,7},{6,4},{7,5},{8,10},{9,11},{10,... | collective-permute-start | bytes 344072 | tf_op jit(solution)/shard_map/ppermute | solution.py:28
  68.7 0.0 collective-permute-start.7
  68.8 1.2 modulation.1.refs_4_
  70.0 0.0 collective-permute-done.9.refs_6_
  70.1 1.9 %collective-permute-done.8.got1 = bf16[32,1792]{1,0:T(8,128)(2,1)S(1)} collective-permute-done((bf16[32,1792]{1,0:T(8,128)(2,1)S(1)}, bf16[32,1792]{1,0:T(8,128)(2,1)S(1)}, u32[]{:S(2)}, u32[]{:S(2)}) %collective-permute-start.8) | collective-permute-done | bytes 114720 | tf_op jit(solution)/shard_map/ppermute | solution.py:28
  72.0 1.5 %collective-permute-done.7.got0 = bf16[32,1792]{1,0:T(8,128)(2,1)S(1)} collective-permute-done((bf16[32,1792]{1,0:T(8,128)(2,1)S(1)}, bf16[32,1792]{1,0:T(8,128)(2,1)S(1)}, u32[]{:S(2)}, u32[]{:S(2)}) %collective-permute-start.7) | collective-permute-done | bytes 114720 | tf_op jit(solution)/shard_map/ppermute | solution.py:28
  73.6 0.6 collective-permute-start.12
  74.1 0.3 collective-permute-start.13
  74.5 3.5 %image_attention.2 = (f32[1024,256]{1,0:T(8,128)S(1)}, f32[1024,128]{1,0:T(8,128)S(1)}) custom-call(bf16[16,384,128]{2,1,0:T(8,128)(2,1)S(1)} %all-to-all-done.packed_ref), custom_call_target="tpu_custom_call" | custom-call | flops 1073741824 | bytes 2359296 | tf_op jit(solution)/shard_map/image_attention/pallas_call | solution.py:356
  78.0 1.7 %collective-permute-done.12.refs_1_ = bf16[64,1792]{1,0:T(8,128)(2,1)S(1)} collective-permute-done((bf16[64,1792]{1,0:T(8,128)(2,1)S(1)}, bf16[64,1792]{1,0:T(8,128)(2,1)S(1)}, u32[]{:S(2)}, u32[]{:S(2)}) %collective-permute-start.12) | collective-permute-done | bytes 229408 | tf_op jit(solution)/shard_map/ppermute | solution.py:28
  79.6 0.5 collective-permute-done.13.refs_3_
  80.2 4.0 %project.1 = (bf16[4,144,256]{2,1,0:T(8,128)(2,1)S(1)}, bf16[4,144,256]{2,1,0:T(8,128)(2,1)S(1)}, bf16[4,144,256]{2,1,0:T(8,128)(2,1)S(1)}, bf16[4,144,256]{2,1,0:T(8,128)(2,1)S(1)}) custom-call(s32[5]{0:T(128)S(1)} %stack.19.place_ref, bf16[64,1792]{1,0:T(8,128)(2,1)S(1)} %get-tuple-element.94.refs_0_, ...), custom_call_target="tpu_custom_call" | custom-call | flops 754974720 | bytes 7864320 | tf_op jit(solution)/shard_map/project/pallas_call | solution.py:206
  84.2 1.6 %collective-permute-start.14 = (bf16[4,144,256]{2,1,0:T(8,128)(2,1)S(1)}, bf16[4,144,256]{2,1,0:T(8,128)(2,1)S(1)}, u32[]{:S(2)}, u32[]{:S(2)}) collective-permute-start(bf16[4,144,256]{2,1,0:T(8,128)(2,1)S(1)} %get-tuple-element.109), channel_id=1, source_target_pairs={{0,2},{1,3},{2,0},{3,1},{4,6},{5,7},{6,4},{7,5},{8,10},{9,11},{10,... | collective-permute-start | bytes 884744 | tf_op jit(solution)/shard_map/ppermute | solution.py:28
  85.8 0.1 collective-permute-start.15
  85.9 3.4 %image_attention.3 = (f32[1024,256]{1,0:T(8,128)S(1)}, f32[1024,128]{1,0:T(8,128)S(1)}) custom-call(bf16[16,384,128]{2,1,0:T(8,128)(2,1)S(1)} %all-to-all-done.packed_ref), custom_call_target="tpu_custom_call" | custom-call | flops 1073741824 | bytes 2359296 | tf_op jit(solution)/shard_map/image_attention/pallas_call | solution.py:356
  89.2 1.8 %collective-permute-done.14.refs_1_ = bf16[4,144,256]{2,1,0:T(8,128)(2,1)S(1)} collective-permute-done((bf16[4,144,256]{2,1,0:T(8,128)(2,1)S(1)}, bf16[4,144,256]{2,1,0:T(8,128)(2,1)S(1)}, u32[]{:S(2)}, u32[]{:S(2)}) %collective-permute-start.14) | collective-permute-done | bytes 294944 | tf_op jit(solution)/shard_map/ppermute | solution.py:28
  91.0 2.8 %collective-permute-done.15.refs_3_ = bf16[4,144,256]{2,1,0:T(8,128)(2,1)S(1)} collective-permute-done((bf16[4,144,256]{2,1,0:T(8,128)(2,1)S(1)}, bf16[4,144,256]{2,1,0:T(8,128)(2,1)S(1)}, u32[]{:S(2)}, u32[]{:S(2)}) %collective-permute-start.15) | collective-permute-done | bytes 294944 | tf_op jit(solution)/shard_map/ppermute | solution.py:28
  93.8 0.1 add_halves.6
  94.0 0.1 collective-permute-start.16
  94.0 0.6 collective-permute-start.17
  94.6 6.1 %collective-permute-done.16.refs_1_ = bf16[2,144,256]{2,1,0:T(8,128)(2,1)S(1)} collective-permute-done((bf16[2,144,256]{2,1,0:T(8,128)(2,1)S(1)}, bf16[2,144,256]{2,1,0:T(8,128)(2,1)S(1)}, u32[]{:S(2)}, u32[]{:S(2)}) %collective-permute-start.16) | collective-permute-done | bytes 147488 | tf_op jit(solution)/shard_map/ppermute | solution.py:28
  100.7 0.1 add_halves.7
  100.7 1.2 collective-permute-start.18
  102.0 6.4 %collective-permute-done.18.refs_2_ = bf16[2,1,144,256]{3,2,1,0:T(8,128)(2,1)S(1)} collective-permute-done((bf16[2,1,144,256]{3,2,1,0:T(8,128)(2,1)S(1)}, bf16[2,1,144,256]{3,2,1,0:T(8,128)(2,1)S(1)}, u32[]{:S(2)}, u32[]{:S(2)}) %collective-permute-start.18) | collective-permute-done | bytes 147488 | tf_op jit(solution)/shard_map/ppermute | solution.py:28
  108.4 0.7 combine.1
  109.1 0.1 collective-permute-start.19
  109.2 1.2 collective-permute-done.19.refs_5_
  110.5 1.6 %finish.1 = bf16[16,160,128]{2,1,0:T(8,128)(2,1)S(1)} custom-call(s32[5]{0:T(128)S(1)} %stack.19.place_ref, bf16[16,384,128]{2,1,0:T(8,128)(2,1)S(1)} %all-to-all-done.packed_ref, f32[1024,256]{1,0:T(8,128)S(1)} %get-tuple-element.107.refs_0_, f32[1024,128]{1,0:T(8,128)S(1)} %get-tuple-element.108.refs_1_, f32[1024,256]{1,0:T(8,128)S(1)} %get-tuple-element.113.refs_2_, ...), custom_call_target="tpu_custom_call" | custom-call | flops 268435456 | bytes 3145728 | tf_op jit(solution)/shard_map/finish/pallas_call | solution.py:426
  112.0 21.0 %all_to_all.10.blocks_ref = bf16[16,160,128]{2,1,0:T(8,128)(2,1)S(1)} all-to-all(bf16[16,160,128]{2,1,0:T(8,128)(2,1)S(1)} %finish.1), channel_id=1, replica_groups=mesh['dp'=2,'seq'=16] {'seq'}, dimensions={0} | all-to-all | bytes 1310720 | tf_op jit(solution)/shard_map/all_to_all | solution.py:585
  133.0 1.0 unpack.1
  (15 shorter events, 0.2 us)
Async XLA Ops:
  2.2 1.0 copy-start.3
  4.7 8.3 %copy-start.2 = (bf16[1,256,1184]{1,2,0:T(8,128)(2,1)S(1)}, bf16[1,256,1184]{1,2,0:T(8,128)(2,1)}, u32[]{:S(2)}) copy-start(bf16[1,256,1184]{1,2,0:T(8,128)(2,1)} %param.10) | copy-start | bytes 1818628
  4.7 61.3 %all-to-all-start = ((bf16[16,384,128]{2,1,0:T(8,128)(2,1)}), bf16[16,384,128]{2,1,0:T(8,128)(2,1)S(1)}, u32[]{:S(2)}, u32[]{:S(2)}) async-start(bf16[16,384,128]{2,1,0:T(8,128)(2,1)} %pack.1), calls=%async_computation | async-start | bytes 3145728 | tf_op jit(solution)/shard_map/all_to_all | solution.py:585
  13.0 3.4 %copy-start = (bf16[1184,3584]{1,0:T(8,128)(2,1)S(1)}, bf16[1184,3584]{1,0:T(8,128)(2,1)}, u32[]{:S(2)}) copy-start(bf16[1184,3584]{1,0:T(8,128)(2,1)} %weight_ref.1) | copy-start | bytes 25460740
  19.9 1.9 %collective-permute-start = (bf16[8,16,1792]{2,1,0:T(8,128)(2,1)S(1)}, bf16[8,16,1792]{2,1,0:T(8,128)(2,1)S(1)}, u32[]{:S(2)}, u32[]{:S(2)}) collective-permute-start(bf16[8,16,1792]{2,1,0:T(8,128)(2,1)S(1)} %get-tuple-element.70), channel_id=1, source_target_pairs={{0,1},{1,0},{2,3},{3,2},{4,5},{5,4},{6,7},{7,6},{8,9},{9,8},{10,11... | collective-permute-start | bytes 1376264 | tf_op jit(solution)/shard_map/ppermute | solution.py:28
  20.3 2.1 %collective-permute-start.1 = (bf16[8,16,1792]{2,1,0:T(8,128)(2,1)S(1)}, bf16[8,16,1792]{2,1,0:T(8,128)(2,1)S(1)}, u32[]{:S(2)}, u32[]{:S(2)}) collective-permute-start(bf16[8,16,1792]{2,1,0:T(8,128)(2,1)S(1)} %get-tuple-element.72), channel_id=1, source_target_pairs={{0,1},{1,0},{2,3},{3,2},{4,5},{5,4},{6,7},{7,6},{8,9},{9,8},{10,11... | collective-permute-start | bytes 1376264 | tf_op jit(solution)/shard_map/ppermute | solution.py:28
  22.6 28.5 %copy-start.1 = (bf16[192,4096]{1,0:T(8,128)(2,1)S(1)}, bf16[192,4096]{1,0:T(8,128)(2,1)}, u32[]{:S(2)}) copy-start(bf16[192,4096]{1,0:T(8,128)(2,1)} %refs_7_.1) | copy-start | bytes 4718596
  22.6 32.6 %copy-start.6 = (bf16[3584]{0:T(1024)(128)(2,1)S(1)}, bf16[3584]{0:T(1024)(128)(2,1)}, u32[]{:S(2)}) copy-start(bf16[3584]{0:T(1024)(128)(2,1)} %param.12) | copy-start | bytes 21508
  22.7 13.5 %collective-permute-start.2 = (bf16[4,16,1792]{2,1,0:T(8,128)(2,1)S(1)}, bf16[4,16,1792]{2,1,0:T(8,128)(2,1)S(1)}, u32[]{:S(2)}, u32[]{:S(2)}) collective-permute-start(bf16[4,16,1792]{2,1,0:T(8,128)(2,1)S(1)} %get-tuple-element.74), channel_id=1, source_target_pairs={{0,2},{1,3},{2,0},{3,1},{4,6},{5,7},{6,4},{7,5},{8,10},{9,11},{10,... | collective-permute-start | bytes 688136 | tf_op jit(solution)/shard_map/ppermute | solution.py:28
  24.6 19.1 %collective-permute-start.3 = (bf16[4,16,1792]{2,1,0:T(8,128)(2,1)S(1)}, bf16[4,16,1792]{2,1,0:T(8,128)(2,1)S(1)}, u32[]{:S(2)}, u32[]{:S(2)}) collective-permute-start(bf16[4,16,1792]{2,1,0:T(8,128)(2,1)S(1)} %get-tuple-element.76), channel_id=1, source_target_pairs={{0,4},{1,5},{2,6},{3,7},{4,0},{5,1},{6,2},{7,3},{8,12},{9,13},{10,... | collective-permute-start | bytes 688136 | tf_op jit(solution)/shard_map/ppermute | solution.py:28
  43.8 5.8 %collective-permute-start.4 = (bf16[2,16,1792]{2,1,0:T(8,128)(2,1)S(1)}, bf16[2,16,1792]{2,1,0:T(8,128)(2,1)S(1)}, u32[]{:S(2)}, u32[]{:S(2)}) collective-permute-start(bf16[2,16,1792]{2,1,0:T(8,128)(2,1)S(1)} %get-tuple-element.78), channel_id=1, source_target_pairs={{0,4},{1,5},{2,6},{3,7},{4,0},{5,1},{6,2},{7,3},{8,12},{9,13},{10,... | collective-permute-start | bytes 344072 | tf_op jit(solution)/shard_map/ppermute | solution.py:28
  46.3 4.8 %collective-permute-start.5 = (bf16[2,16,1792]{2,1,0:T(8,128)(2,1)S(1)}, bf16[2,16,1792]{2,1,0:T(8,128)(2,1)S(1)}, u32[]{:S(2)}, u32[]{:S(2)}) collective-permute-start(bf16[2,16,1792]{2,1,0:T(8,128)(2,1)S(1)} %get-tuple-element.80), channel_id=1, source_target_pairs={{0,2},{1,3},{2,0},{3,1},{4,6},{5,7},{6,4},{7,5},{8,10},{9,11},{10,... | collective-permute-start | bytes 344072 | tf_op jit(solution)/shard_map/ppermute | solution.py:28
  51.1 18.9 %collective-permute-start.10 = (bf16[192,4096]{1,0:T(8,128)(2,1)S(1)}, bf16[192,4096]{1,0:T(8,128)(2,1)}, u32[]{:S(2)}, u32[]{:S(2)}) collective-permute-start(bf16[192,4096]{1,0:T(8,128)(2,1)S(1)} %copy-done.1), channel_id=1, source_target_pairs={{0,1},{1,0},{2,3},{3,2},{4,5},{5,4},{6,7},{7,6},{8,9},{9,8},{10,11... | collective-permute-start | bytes 4718600 | tf_op jit(solution)/shard_map/ppermute | solution.py:28
  51.2 18.8 %collective-permute-start.9 = (bf16[192,3584]{1,0:T(8,128)(2,1)}, bf16[192,3584]{1,0:T(8,128)(2,1)}, u32[]{:S(2)}, u32[]{:S(2)}) collective-permute-start(bf16[192,3584]{1,0:T(8,128)(2,1)} %bitcast.9.refs_5_), channel_id=1, source_target_pairs={{0,1},{1,0},{2,3},{3,2},{4,5},{5,4},{6,7},{7,6},{8,9},{9,8},{10,11... | collective-permute-start | bytes 4128776 | tf_op jit(solution)/shard_map/ppermute | solution.py:28
  51.7 13.6 %collective-permute-start.6 = (bf16[2,2,16,1792]{3,2,1,0:T(8,128)(2,1)S(1)}, bf16[2,2,16,1792]{3,2,1,0:T(8,128)(2,1)S(1)}, u32[]{:S(2)}, u32[]{:S(2)}) collective-permute-start(bf16[2,2,16,1792]{3,2,1,0:T(8,128)(2,1)S(1)} %add_all.1.mine_ref), channel_id=1, source_target_pairs={{0,8},{1,9},{2,10},{3,11},{4,12},{5,13},{6,14},{7,15},{8,0},{9,1},... | collective-permute-start | bytes 688136 | tf_op jit(solution)/shard_map/ppermute | solution.py:28
  55.3 13.6 %collective-permute-start.11 = (bf16[2,192,256]{2,1,0:T(8,128)(2,1)}, bf16[2,192,256]{2,1,0:T(8,128)(2,1)}, u32[]{:S(2)}, u32[]{:S(2)}) collective-permute-start(bf16[2,192,256]{2,1,0:T(8,128)(2,1)} %bitcast.10.mod0_ref), channel_id=1, source_target_pairs={{0,1},{1,0},{2,3},{3,2},{4,5},{5,4},{6,7},{7,6},{8,9},{9,8},{10,11... | collective-permute-start | bytes 589832 | tf_op jit(solution)/shard_map/ppermute | solution.py:28
  65.3 0.7 copy-start.4
  66.0 0.9 copy-start.5
  67.2 4.9 %collective-permute-start.8 = (bf16[32,1792]{1,0:T(8,128)(2,1)S(1)}, bf16[32,1792]{1,0:T(8,128)(2,1)S(1)}, u32[]{:S(2)}, u32[]{:S(2)}) collective-permute-start(bf16[32,1792]{1,0:T(8,128)(2,1)S(1)} %bitcast.26), channel_id=1, source_target_pairs={{0,2},{1,3},{2,0},{3,1},{4,6},{5,7},{6,4},{7,5},{8,10},{9,11},{10,... | collective-permute-start | bytes 344072 | tf_op jit(solution)/shard_map/ppermute | solution.py:28
  68.7 4.8 %collective-permute-start.7 = (bf16[32,1792]{1,0:T(8,128)(2,1)S(1)}, bf16[32,1792]{1,0:T(8,128)(2,1)S(1)}, u32[]{:S(2)}, u32[]{:S(2)}) collective-permute-start(bf16[32,1792]{1,0:T(8,128)(2,1)S(1)} %bitcast.24), channel_id=1, source_target_pairs={{0,4},{1,5},{2,6},{3,7},{4,0},{5,1},{6,2},{7,3},{8,12},{9,13},{10,... | collective-permute-start | bytes 344072 | tf_op jit(solution)/shard_map/ppermute | solution.py:28
  73.6 6.1 %collective-permute-start.12 = (bf16[64,1792]{1,0:T(8,128)(2,1)S(1)}, bf16[64,1792]{1,0:T(8,128)(2,1)S(1)}, u32[]{:S(2)}, u32[]{:S(2)}) collective-permute-start(bf16[64,1792]{1,0:T(8,128)(2,1)S(1)} %get-tuple-element.94.refs_0_), channel_id=1, source_target_pairs={{0,2},{1,3},{2,0},{3,1},{4,6},{5,7},{6,4},{7,5},{8,10},{9,11},{10,... | collective-permute-start | bytes 688136 | tf_op jit(solution)/shard_map/ppermute | solution.py:28
  74.1 6.0 %collective-permute-start.13 = (bf16[64,1792]{1,0:T(8,128)(2,1)S(1)}, bf16[64,1792]{1,0:T(8,128)(2,1)S(1)}, u32[]{:S(2)}, u32[]{:S(2)}) collective-permute-start(bf16[64,1792]{1,0:T(8,128)(2,1)S(1)} %get-tuple-element.95.refs_2_), channel_id=1, source_target_pairs={{0,4},{1,5},{2,6},{3,7},{4,0},{5,1},{6,2},{7,3},{8,12},{9,13},{10,... | collective-permute-start | bytes 688136 | tf_op jit(solution)/shard_map/ppermute | solution.py:28
  84.2 6.8 %collective-permute-start.14 = (bf16[4,144,256]{2,1,0:T(8,128)(2,1)S(1)}, bf16[4,144,256]{2,1,0:T(8,128)(2,1)S(1)}, u32[]{:S(2)}, u32[]{:S(2)}) collective-permute-start(bf16[4,144,256]{2,1,0:T(8,128)(2,1)S(1)} %get-tuple-element.109), channel_id=1, source_target_pairs={{0,2},{1,3},{2,0},{3,1},{4,6},{5,7},{6,4},{7,5},{8,10},{9,11},{10,... | collective-permute-start | bytes 884744 | tf_op jit(solution)/shard_map/ppermute | solution.py:28
  85.8 8.0 %collective-permute-start.15 = (bf16[4,144,256]{2,1,0:T(8,128)(2,1)S(1)}, bf16[4,144,256]{2,1,0:T(8,128)(2,1)S(1)}, u32[]{:S(2)}, u32[]{:S(2)}) collective-permute-start(bf16[4,144,256]{2,1,0:T(8,128)(2,1)S(1)} %get-tuple-element.110), channel_id=1, source_target_pairs={{0,4},{1,5},{2,6},{3,7},{4,0},{5,1},{6,2},{7,3},{8,12},{9,13},{10,... | collective-permute-start | bytes 884744 | tf_op jit(solution)/shard_map/ppermute | solution.py:28
  94.0 6.7 %collective-permute-start.16 = (bf16[2,144,256]{2,1,0:T(8,128)(2,1)S(1)}, bf16[2,144,256]{2,1,0:T(8,128)(2,1)S(1)}, u32[]{:S(2)}, u32[]{:S(2)}) collective-permute-start(bf16[2,144,256]{2,1,0:T(8,128)(2,1)S(1)} %get-tuple-element.120), channel_id=1, source_target_pairs={{0,4},{1,5},{2,6},{3,7},{4,0},{5,1},{6,2},{7,3},{8,12},{9,13},{10,... | collective-permute-start | bytes 442376 | tf_op jit(solution)/shard_map/ppermute | solution.py:28
  94.0 6.6 %collective-permute-start.17 = (bf16[2,144,256]{2,1,0:T(8,128)(2,1)S(1)}, bf16[2,144,256]{2,1,0:T(8,128)(2,1)S(1)}, u32[]{:S(2)}, u32[]{:S(2)}) collective-permute-start(bf16[2,144,256]{2,1,0:T(8,128)(2,1)S(1)} %get-tuple-element.122), channel_id=1, source_target_pairs={{0,2},{1,3},{2,0},{3,1},{4,6},{5,7},{6,4},{7,5},{8,10},{9,11},{10,... | collective-permute-start | bytes 442376 | tf_op jit(solution)/shard_map/ppermute | solution.py:28
  100.7 7.6 %collective-permute-start.18 = (bf16[2,1,144,256]{3,2,1,0:T(8,128)(2,1)S(1)}, bf16[2,1,144,256]{3,2,1,0:T(8,128)(2,1)S(1)}, u32[]{:S(2)}, u32[]{:S(2)}) collective-permute-start(bf16[2,1,144,256]{3,2,1,0:T(8,128)(2,1)S(1)} %get-tuple-element.125), channel_id=1, source_target_pairs={{0,8},{1,9},{2,10},{3,11},{4,12},{5,13},{6,14},{7,15},{8,0},{9,1},... | collective-permute-start | bytes 442376 | tf_op jit(solution)/shard_map/ppermute | solution.py:28
  109.1 1.3 collective-permute-start.19

commit v16 on v15

--- a/solution.py
+++ b/solution.py
@@ -298,37 +298,42 @@
     )(queries, keys, values)
 
 
-def unpack_kernel(copies, part_rows, blocks_ref, attended_ref, text_ref):
+def unpack_kernel(copies, part_rows, place_ref, *refs):
+    *pieces, near_ref, far_ref, attended_ref, text_ref = refs
+    me = 2 * place_ref[3] + place_ref[2]
     share = text_ref.shape[0]
     half = text_ref.shape[1] // 2
-    for device in range(blocks_ref.shape[0]):
-        head, copy = device // copies, device % copies
-        start = head * HEAD_DIM
-        rows = slice(copy * part_rows, (copy + 1) * part_rows)
-        attended_ref[rows, start : start + HEAD_DIM] = blocks_ref[device, :part_rows, :]
-        if copy == 0:
-            block = blocks_ref[device, part_rows:, :].astype(jnp.float32)
-            text_ref[:, start : start + HEAD_DIM] = block[:share].astype(text_ref.dtype)
-            start += half
-            text_ref[:, start : start + HEAD_DIM] = block[share:].astype(text_ref.dtype)
-
-
-def unpack(copies, part_rows, blocks):
-    share = (blocks.shape[1] - part_rows) // 2
+    count = len(pieces) // 2
+    passed = [near_ref.at[at] for at in range(count)] + [far_ref.at[at] for at in range(count)]
+    blocks = [block for piece, other in zip(pieces, passed) for block in (piece.at[0], other)]
+    for at, block_ref in enumerate(blocks):
+        head, copy = (me ^ at) // copies, (me ^ at) % copies
+        start = pl.multiple_of(head * HEAD_DIM, HEAD_DIM)
+        rows = pl.ds(pl.multiple_of(copy * part_rows, part_rows), part_rows)
+        attended_ref[rows, pl.ds(start, HEAD_DIM)] = block_ref[:part_rows, :]
+        block = block_ref[part_rows:, :].astype(jnp.float32)
+        text_ref[:, pl.ds(start, HEAD_DIM)] = block[:share].astype(text_ref.dtype)
+        start = pl.multiple_of(half + head * HEAD_DIM, HEAD_DIM)
+        text_ref[:, pl.ds(start, HEAD_DIM)] = block[share:].astype(text_ref.dtype)
+
+
+def unpack(copies, part_rows, place, pieces, near, far):
+    share = (near.shape[1] - part_rows) // 2
     return pl.pallas_call(
         functools.partial(unpack_kernel, copies, part_rows),
         out_shape=(
             jax.ShapeDtypeStruct((part_rows * copies, HEADS * HEAD_DIM), jnp.bfloat16),
             jax.ShapeDtypeStruct((share, 2 * HEADS * HEAD_DIM), jnp.bfloat16),
         ),
-        in_specs=[VMEM_SPEC],
+        in_specs=[SMEM_SPEC] + [VMEM_SPEC] * (len(pieces) + 2),
         out_specs=(VMEM_SPEC, VMEM_SPEC),
-        compiler_params=params(4),
+        compiler_params=params(6),
         name="unpack",
-    )(blocks)
-
-
-def image_kernel(factor, call, img_dev, packed_ref, sum_ref, top_ref, keys_ref, wide_ref):
+    )(place, *pieces, near, far)
+
+
+def image_kernel(factor, call, img_dev, place_ref, packed_ref, sum_ref, top_ref, keys_ref, wide_ref):
+    me = 2 * place_ref[3] + place_ref[2]
     wide_ref[:, HEAD_DIM:] = jnp.ones((wide_ref.shape[0], HEAD_DIM), wide_ref.dtype)
     for device in range(packed_ref.shape[0]):
         rows = slice(device * img_dev, (device + 1) * img_dev)
@@ -341,7 +346,8 @@
     for start in range(0, count, rows):
         span = slice(start, start + rows)
         at = (call * count + start) // rows * group
-        queries = packed_ref[at : at + group, 2 * img_dev :, :].reshape(rows, HEAD_DIM)
+        queries = [packed_ref[me ^ (at + i), 2 * img_dev :, :] for i in range(group)]
+        queries = jnp.concatenate(queries, 0)
         scores = lax.dot_general(queries, keys_ref[...], contract, preferred_element_type=jnp.float32)
         scores = scores * factor
         top = jnp.max(scores, 1, keepdims=True)
@@ -350,7 +356,7 @@
         top_ref[span, :] = jnp.broadcast_to(top, (rows, HEAD_DIM))
 
 
-def image_attention(packed, img_dev, factor, call, calls):
+def image_attention(place, packed, img_dev, factor, call, calls):
     count = packed.shape[0] * (packed.shape[1] - 2 * img_dev) // calls
     total = packed.shape[0] * img_dev
     return pl.pallas_call(
@@ -359,7 +365,7 @@
             jax.ShapeDtypeStruct((count, 2 * HEAD_DIM), jnp.float32),
             jax.ShapeDtypeStruct((count, HEAD_DIM), jnp.float32),
         ),
-        in_specs=[VMEM_SPEC],
+        in_specs=[SMEM_SPEC, VMEM_SPEC],
         out_specs=(VMEM_SPEC, VMEM_SPEC),
         scratch_shapes=[
             pltpu.VMEM((total, HEAD_DIM), jnp.bfloat16),
@@ -372,13 +378,13 @@
             transcendentals=count * total,
         ),
         name="image_attention",
-    )(packed)
-
-
-def finish_kernel(factor, calls, img_dev, place_ref, packed_ref, *refs):
-    images, (mine_ref, got_ref, out_ref) = refs[: 2 * calls], refs[2 * calls :]
+    )(place, packed)
+
+
+def finish_kernel(factor, first, img_dev, place_ref, packed_ref, sum_ref, top_ref, mine_ref, got_ref, *refs):
+    *outs, text_ref = refs
     core, valid = place_ref[2], place_ref[4]
-    devices = out_ref.shape[0]
+    me = 2 * place_ref[3] + core
     part_rows = packed_ref.shape[1] - 2 * img_dev
     half = mine_ref.shape[0]
     contract = (((1,), (1,)), ((), ()))
@@ -391,12 +397,12 @@
     bias = jnp.where(text_position < valid, 0.0, -jnp.inf)
     group = max(1, 512 // part_rows)
     rows = group * part_rows
-    each = devices // group // calls
-    for step in range(devices // group):
-        sum_ref, top_ref = images[2 * (step // each)], images[2 * (step // each) + 1]
-        span = slice(step % each * rows, (step % each + 1) * rows)
-        queries = packed_ref[step * group : (step + 1) * group, 2 * img_dev :, :]
-        queries = queries.reshape(rows, HEAD_DIM)
+    for step in range(2 * len(outs) // group):
+        span = slice(step * rows, (step + 1) * rows)
+        queries = [
+            packed_ref[me ^ (2 * first + step * group + at), 2 * img_dev :, :] for at in range(group)
+        ]
+        queries = jnp.concatenate(queries, 0)
         scores = lax.dot_general(queries, keys, contract, preferred_element_type=jnp.float32)
         scores = scores * factor + bias
         before = top_ref[span, :]
@@ -406,36 +412,61 @@
         total = jnp.dot(weights.astype(jnp.bfloat16), values, preferred_element_type=jnp.float32)
         mixed = sum_ref[span, :HEAD_DIM] * rescale + total[:, :HEAD_DIM]
         total = sum_ref[span, HEAD_DIM:] * rescale + total[:, HEAD_DIM:]
-        mixed = (mixed / total).astype(out_ref.dtype)
-        out_ref[step * group : (step + 1) * group, :part_rows, :] = mixed.reshape(group, part_rows, HEAD_DIM)
-    low = jnp.where(core == 0, mine.astype(jnp.float32), got.astype(jnp.float32))
-    high = jnp.where(core == 0, got.astype(jnp.float32), mine.astype(jnp.float32))
-    share = 2 * half // devices
-    for device in range(devices):
-        source = low if device < devices // 2 else high
-        start = device * share % half
-        block = source[start : start + share]
+        mixed = (mixed / total).astype(jnp.bfloat16)
+        for at in range(group):
+            to = step * group + at
+            outs[to // 2][to % 2, :part_rows, :] = mixed[at * part_rows : (at + 1) * part_rows]
+    low, high = mine.astype(jnp.float32), got.astype(jnp.float32)
+    text_ref[:half, :] = jnp.where(core == 0, low, high)
+    text_ref[half:, :] = jnp.where(core == 0, high, low)
+    share = (outs[0].shape[1] - part_rows) // 2
+    for to in range(2 * len(outs)):
+        start = pl.multiple_of((me ^ (2 * first + to)) * share, share)
+        block = text_ref[pl.ds(start, share), :]
         block = jnp.concatenate([block[:, :HEAD_DIM], block[:, HEAD_DIM:]], 0)
-        out_ref[device, part_rows:, :] = block.astype(out_ref.dtype)
-
-
-def finish(place, packed, images, mine, got, img_dev, factor):
+        outs[to // 2][to % 2, part_rows:, :] = block.astype(jnp.bfloat16)
+
+
+def finish(place, first, packed, image, mine, got, img_dev, factor):
     devices, part_rows = packed.shape[0], packed.shape[1] - 2 * img_dev
-    count = devices * part_rows
-    share = 2 * mine.shape[0] // devices
-    return pl.pallas_call(
-        functools.partial(finish_kernel, factor, len(images) // 2, img_dev),
-        out_shape=jax.ShapeDtypeStruct((devices, part_rows + 2 * share, HEAD_DIM), jnp.bfloat16),
-        in_specs=[SMEM_SPEC] + [VMEM_SPEC] * (len(images) + 3),
+    half = mine.shape[0]
+    count = image[0].shape[0]
+    outs = count // part_rows // 2
+    out = jax.ShapeDtypeStruct((2, part_rows + 4 * half // devices, HEAD_DIM), jnp.bfloat16)
+    return pl.pallas_call(
+        functools.partial(finish_kernel, factor, first, img_dev),
+        out_shape=(out,) * outs,
+        in_specs=[SMEM_SPEC] + [VMEM_SPEC] * 5,
+        out_specs=(VMEM_SPEC,) * outs,
+        scratch_shapes=[pltpu.VMEM((2 * half, 2 * HEAD_DIM), jnp.float32)],
+        compiler_params=params(10),
+        cost_estimate=pl.CostEstimate(
+            flops=8 * count * half * HEAD_DIM,
+            bytes_accessed=12 * count * HEAD_DIM,
+            transcendentals=2 * count * half,
+        ),
+        name="finish",
+    )(place, packed, *image, mine, got)
+
+
+def gather_kernel(*refs):
+    for at, piece in enumerate(refs[:-1]):
+        refs[-1][at] = piece[1]
+
+
+def gather_other(pieces):
+    shape = (len(pieces),) + pieces[0].shape[1:]
+    return pl.pallas_call(
+        gather_kernel,
+        out_shape=jax.ShapeDtypeStruct(shape, pieces[0].dtype),
+        in_specs=[VMEM_SPEC] * len(pieces),
         out_specs=VMEM_SPEC,
-        compiler_params=params(10),
-        cost_estimate=pl.CostEstimate(
-            flops=4 * count * 2 * mine.shape[0] * HEAD_DIM,
-            bytes_accessed=12 * count * HEAD_DIM,
-            transcendentals=count * 2 * mine.shape[0],
-        ),
-        name="finish",
-    )(place, packed, *images, mine, got)
+        compiler_params=params(4),
+        cost_estimate=pl.CostEstimate(
+            flops=0, bytes_accessed=2 * len(pieces) * pieces[0].size, transcendentals=0
+        ),
+        name="gather_other",
+    )(*pieces)
 
 
 def add_kernel(joint, *refs):
@@ -594,17 +625,17 @@
     for step in range(rounds - 1):
         sent, keep = add_halves(keep, got)
         got = [swap(part, 2 * order[step]) for part, order in zip(sent, lanes)]
-    summed = add_all(keep, got)
+    summed, packed = tie((add_all(keep, got), packed))
     summed, held, held_kv, held_mod = tie((summed, win0, kv0, mod0))
     win1, kv1, mod1 = swap(held, 1), swap(held_kv, 1), swap(held_mod, 1)
-    got, packed = tie((swap(summed, last), packed))
+    got = swap(summed, last)
 
     states = normalize(summed, got, norm_gain[None, :])
     images = []
     for step in reversed(range(rounds - 1)):
         if step == 0:
             states, packed = tie((states, packed))
-            image = image_attention(packed, img_dev, factor, 0, 2)
+            image = image_attention(place, packed, img_dev, factor, 0, 2)
         got = [swap(state, 2 * order[step]) for state, order in zip(states, lanes)]
         if step == rounds - 2:
             lines = modulation(time, mod0, mod1)
@@ -620,7 +651,7 @@
     for step in range(rounds - 1):
         if step == 0:
             sent, packed = tie((sent, packed))
-            image = image_attention(packed, img_dev, factor, 1, 2)
+            image = image_attention(place, packed, img_dev, factor, 1, 2)
         got = [swap(part, 2 * order[step]) for part, order in zip(sent, lanes)]
         if step == 0:
             got, image = tie((got, image))
@@ -631,8 +662,18 @@
     mine, sent = combine(place, parts, chips, text_len // 2, model_width)
     got = swap(sent, 1)
 
-    back = exchange(finish(place, packed, images, mine, got, img_dev, factor))
-    attended, text_kv = unpack(copies, part_rows, back)
+    pieces = [None] * chips
+    passed = [None] * 2
+    for call in (1, 0):
+        first = call * chips // 2
+        image = images[2 * call : 2 * call + 2]
+        blocks = finish(place, first, packed, image, mine, got, img_dev, factor)
+        for at, block in enumerate(blocks):
+            mask = first + at
+            pieces[mask] = swap(block, 2 * mask) if mask else block
+    for call in range(2):
+        passed[call] = swap(gather_other(pieces[call * chips // 2 : (call + 1) * chips // 2]), 1)
+    attended, text_kv = unpack(copies, part_rows, place, pieces, *passed)
     return (attended[None], text_kv)
 
 

time: 134 us -> 130 us (0.970)
  blocking collectives: 21 us -> 0 us
  waiting for transfers between devices: 56.6 us -> 65.9 us
  starting transfers between devices: 25.4 us -> 33.9 us
    all_to_all x1 -> x0, blocking collectives: 21 us -> none  [exchange(): return lax.all_to_all(rows, 'seq', split_axis=0, concat_axis=0, tiled=True)]
    ppermute x20 -> x29, waiting for transfers between devices: 56.6 us -> 65.9 us  [swap(): return lax.ppermute(value, 'seq', [(i, i ^ mask) for i in range(devices)])]
    ppermute x20 -> x29, starting transfers between devices: 17.9 us -> 26.4 us  [swap(): return lax.ppermute(value, 'seq', [(i, i ^ mask) for i in range(devices)])]
    pallas_call x1, Pallas kernels: 4.04 us -> 2.34 us  [project(): pl.pallas_call(functools.partial(project_kernel, lanes), out_shape=(out,)...]
  transfers between devices with their start and end apart: 21 -> 30, of which waited for: 16 -> 22; matrix products, arithmetic and copies ran while one was open for 0% -> 0% of each run, Pallas kernels for 9% -> 10%
where the time goes in v16:
time: 130 us
  waiting for transfers between devices  65.9 us (51%)
  starting transfers between devices  33.9 us (26%)
  Pallas kernels  20.8 us (16%)
  local copies, waits for them, and re-layouts  7.06 us (5%)
  between operations  2.26 us (2%)
    ppermute x29, waiting for transfers between devices, swap(): return lax.ppermute(value, 'seq', [(i, i ^ mask) for i in range(devices)])  65.9 us
    ppermute x29, starting transfers between devices, swap(): return lax.ppermute(value, 'seq', [(i, i ^ mask) for i in range(devices)])  26.4 us
    pallas_call x2, Pallas kernels, image_attention(): pl.pallas_call(functools.partial(image_kernel, factor, call, img_dev), ou...  8.03 us
    all_to_all x1, starting transfers between devices, exchange(): return lax.all_to_all(rows, 'seq', split_axis=0, concat_axis=0, tiled=True)  7.49 us
    unnamed x14, local copies, waits for them, and re-layouts  5.31 us
    pallas_call x1, Pallas kernels, encoder(): pl.pallas_call(functools.partial(encoder_kernel, lanes), out_shape=(out,)...  3.47 us
  transfers between devices with their start and end apart: 30, of which 22 were waited for; matrix products, arithmetic and copies ran while one was open for 0% of the time, Pallas kernels for 10%

profile of v16, /device:TPU:0, one launch (start us, length us, event | category | flops | bytes accessed | tf_op | source)
XLA Modules:
  0.0 130.0 jit_solution(14707880112320825848)
XLA Ops:
  0.6 1.6 %copy.12 = bf16[1,128,2,2048]{3,1,2,0:T(8,128)(2,1)S(1)} copy(bf16[1,128,2,2048]{3,2,1,0:T(2,128)(2,1)} %param.19) | data formatting | bytes 2097152 | tf_op jit(solution)/shard_map/optimization_barrier | solution.py:618
  2.3 1.0 copy-done.4
  3.3 1.4 %pack.1 = bf16[16,384,128]{2,1,0:T(8,128)(2,1)} custom-call(bf16[128,2048]{1,0:T(8,128)(2,1)S(1)} %bitcast.25, bf16[128,2048]{1,0:T(8,128)(2,1)S(1)} %get-tuple-element.147.keys_ref, bf16[128,2048]{1,0:T(8,128)(2,1)S(1)} %get-tuple-element.146.values_ref), custom_call_target="tpu_custom_call" | custom-call | bytes 3145728 | tf_op jit(solution)/shard_map/pack/pallas_call | solution.py:288
  4.7 7.5 %all-to-all-start = ((bf16[16,384,128]{2,1,0:T(8,128)(2,1)}), bf16[16,384,128]{2,1,0:T(8,128)(2,1)S(1)}, u32[]{:S(2)}, u32[]{:S(2)}) async-start(bf16[16,384,128]{2,1,0:T(8,128)(2,1)} %pack.1), calls=%async_computation | async-start | bytes 3145728 | tf_op jit(solution)/shard_map/all_to_all | solution.py:616
  12.9 0.1 stack.19.place_ref
  13.0 3.4 %copy-done = bf16[1184,3584]{1,0:T(8,128)(2,1)S(1)} copy-done((bf16[1184,3584]{1,0:T(8,128)(2,1)S(1)}, bf16[1184,3584]{1,0:T(8,128)(2,1)}, u32[]{:S(2)}) %copy-start) | copy-done | bytes 8486936
  16.4 3.5 %encoder.1 = (bf16[8,16,1792]{2,1,0:T(8,128)(2,1)S(1)}, bf16[8,16,1792]{2,1,0:T(8,128)(2,1)S(1)}, bf16[8,16,1792]{2,1,0:T(8,128)(2,1)S(1)}, bf16[8,16,1792]{2,1,0:T(8,128)(2,1)S(1)}) custom-call(s32[5]{0:T(128)S(1)} %stack.19.place_ref, bf16[1184,256]{1,0:T(8,128)(2,1)S(1)} %bitcast.24, bf16[1184,3584]{1,0:T(8,128)(2,1)S(1)} %copy-done), custom_call_target="tpu_custom_call" | custom-call | flops 2172649472 | bytes 10928128 | tf_op jit(solution)/shard_map/encoder/pallas_call | solution.py:84
  19.8 0.5 collective-permute-start
  20.3 0.1 collective-permute-start.1
  20.4 1.3 %collective-permute-done.refs_1_ = bf16[8,16,1792]{2,1,0:T(8,128)(2,1)S(1)} collective-permute-done((bf16[8,16,1792]{2,1,0:T(8,128)(2,1)S(1)}, bf16[8,16,1792]{2,1,0:T(8,128)(2,1)S(1)}, u32[]{:S(2)}, u32[]{:S(2)}) %collective-permute-start) | collective-permute-done | bytes 458784 | tf_op jit(solution)/shard_map/ppermute | solution.py:28
  21.7 0.7 collective-permute-done.1.refs_3_
  22.4 0.2 add_halves.4
  22.6 2.0 %collective-permute-start.2 = (bf16[4,16,1792]{2,1,0:T(8,128)(2,1)S(1)}, bf16[4,16,1792]{2,1,0:T(8,128)(2,1)S(1)}, u32[]{:S(2)}, u32[]{:S(2)}) collective-permute-start(bf16[4,16,1792]{2,1,0:T(8,128)(2,1)S(1)} %get-tuple-element.82), channel_id=1, source_target_pairs={{0,2},{1,3},{2,0},{3,1},{4,6},{5,7},{6,4},{7,5},{8,10},{9,11},{10,... | collective-permute-start | bytes 688136 | tf_op jit(solution)/shard_map/ppermute | solution.py:28
  24.6 1.5 %collective-permute-start.3 = (bf16[4,16,1792]{2,1,0:T(8,128)(2,1)S(1)}, bf16[4,16,1792]{2,1,0:T(8,128)(2,1)S(1)}, u32[]{:S(2)}, u32[]{:S(2)}) collective-permute-start(bf16[4,16,1792]{2,1,0:T(8,128)(2,1)S(1)} %get-tuple-element.84), channel_id=1, source_target_pairs={{0,4},{1,5},{2,6},{3,7},{4,0},{5,1},{6,2},{7,3},{8,12},{9,13},{10,... | collective-permute-start | bytes 688136 | tf_op jit(solution)/shard_map/ppermute | solution.py:28
  26.0 10.1 %collective-permute-done.2.refs_1_ = bf16[4,16,1792]{2,1,0:T(8,128)(2,1)S(1)} collective-permute-done((bf16[4,16,1792]{2,1,0:T(8,128)(2,1)S(1)}, bf16[4,16,1792]{2,1,0:T(8,128)(2,1)S(1)}, u32[]{:S(2)}, u32[]{:S(2)}) %collective-permute-start.2) | collective-permute-done | bytes 229408 | tf_op jit(solution)/shard_map/ppermute | solution.py:28
  36.1 7.6 %collective-permute-done.3.refs_3_ = bf16[4,16,1792]{2,1,0:T(8,128)(2,1)S(1)} collective-permute-done((bf16[4,16,1792]{2,1,0:T(8,128)(2,1)S(1)}, bf16[4,16,1792]{2,1,0:T(8,128)(2,1)S(1)}, u32[]{:S(2)}, u32[]{:S(2)}) %collective-permute-start.3) | collective-permute-done | bytes 229408 | tf_op jit(solution)/shard_map/ppermute | solution.py:28
  43.7 0.1 add_halves.5
  43.7 2.5 %collective-permute-start.4 = (bf16[2,16,1792]{2,1,0:T(8,128)(2,1)S(1)}, bf16[2,16,1792]{2,1,0:T(8,128)(2,1)S(1)}, u32[]{:S(2)}, u32[]{:S(2)}) collective-permute-start(bf16[2,16,1792]{2,1,0:T(8,128)(2,1)S(1)} %get-tuple-element.86), channel_id=1, source_target_pairs={{0,4},{1,5},{2,6},{3,7},{4,0},{5,1},{6,2},{7,3},{8,12},{9,13},{10,... | collective-permute-start | bytes 344072 | tf_op jit(solution)/shard_map/ppermute | solution.py:28
  46.3 1.7 %collective-permute-start.5 = (bf16[2,16,1792]{2,1,0:T(8,128)(2,1)S(1)}, bf16[2,16,1792]{2,1,0:T(8,128)(2,1)S(1)}, u32[]{:S(2)}, u32[]{:S(2)}) collective-permute-start(bf16[2,16,1792]{2,1,0:T(8,128)(2,1)S(1)} %get-tuple-element.88), channel_id=1, source_target_pairs={{0,2},{1,3},{2,0},{3,1},{4,6},{5,7},{6,4},{7,5},{8,10},{9,11},{10,... | collective-permute-start | bytes 344072 | tf_op jit(solution)/shard_map/ppermute | solution.py:28
  48.0 1.5 %collective-permute-done.4.got0 = bf16[2,16,1792]{2,1,0:T(8,128)(2,1)S(1)} collective-permute-done((bf16[2,16,1792]{2,1,0:T(8,128)(2,1)S(1)}, bf16[2,16,1792]{2,1,0:T(8,128)(2,1)S(1)}, u32[]{:S(2)}, u32[]{:S(2)}) %collective-permute-start.4) | collective-permute-done | bytes 114720 | tf_op jit(solution)/shard_map/ppermute | solution.py:28
  49.5 1.6 %collective-permute-done.5.got1 = bf16[2,16,1792]{2,1,0:T(8,128)(2,1)S(1)} collective-permute-done((bf16[2,16,1792]{2,1,0:T(8,128)(2,1)S(1)}, bf16[2,16,1792]{2,1,0:T(8,128)(2,1)S(1)}, u32[]{:S(2)}, u32[]{:S(2)}) %collective-permute-start.5) | collective-permute-done | bytes 114720 | tf_op jit(solution)/shard_map/ppermute | solution.py:28
  51.1 0.1 collective-permute-start.10
  51.2 0.5 collective-permute-start.9
  51.7 2.9 %collective-permute-start.6 = (bf16[2,2,16,1792]{3,2,1,0:T(8,128)(2,1)S(1)}, bf16[2,2,16,1792]{3,2,1,0:T(8,128)(2,1)S(1)}, u32[]{:S(2)}, u32[]{:S(2)}) collective-permute-start(bf16[2,2,16,1792]{3,2,1,0:T(8,128)(2,1)S(1)} %add_all.1.mine_ref), channel_id=1, source_target_pairs={{0,8},{1,9},{2,10},{3,11},{4,12},{5,13},{6,14},{7,15},{8,0},{9,1},... | collective-permute-start | bytes 688136 | tf_op jit(solution)/shard_map/ppermute | solution.py:28
  55.3 0.1 collective-permute-start.11
  55.3 10.0 %collective-permute-done.6.got_ref = bf16[2,2,16,1792]{3,2,1,0:T(8,128)(2,1)S(1)} collective-permute-done((bf16[2,2,16,1792]{3,2,1,0:T(8,128)(2,1)S(1)}, bf16[2,2,16,1792]{3,2,1,0:T(8,128)(2,1)S(1)}, u32[]{:S(2)}, u32[]{:S(2)}) %collective-permute-start.6) | collective-permute-done | bytes 229408 | tf_op jit(solution)/shard_map/ppermute | solution.py:28
  65.3 0.2 normalize.1
  65.5 1.6 %collective-permute-start.8 = (bf16[32,1792]{1,0:T(8,128)(2,1)S(1)}, bf16[32,1792]{1,0:T(8,128)(2,1)S(1)}, u32[]{:S(2)}, u32[]{:S(2)}) collective-permute-start(bf16[32,1792]{1,0:T(8,128)(2,1)S(1)} %bitcast.30), channel_id=1, source_target_pairs={{0,2},{1,3},{2,0},{3,1},{4,6},{5,7},{6,4},{7,5},{8,10},{9,11},{10,... | collective-permute-start | bytes 344072 | tf_op jit(solution)/shard_map/ppermute | solution.py:28
  67.2 0.9 copy-done.5
  68.1 0.2 modulation.1.refs_4_
  68.3 2.1 %collective-permute-done.8.got1 = bf16[32,1792]{1,0:T(8,128)(2,1)S(1)} collective-permute-done((bf16[32,1792]{1,0:T(8,128)(2,1)S(1)}, bf16[32,1792]{1,0:T(8,128)(2,1)S(1)}, u32[]{:S(2)}, u32[]{:S(2)}) %collective-permute-start.8) | collective-permute-done | bytes 114720 | tf_op jit(solution)/shard_map/ppermute | solution.py:28
  70.4 1.5 %collective-permute-done.7.got0 = bf16[32,1792]{1,0:T(8,128)(2,1)S(1)} collective-permute-done((bf16[32,1792]{1,0:T(8,128)(2,1)S(1)}, bf16[32,1792]{1,0:T(8,128)(2,1)S(1)}, u32[]{:S(2)}, u32[]{:S(2)}) %collective-permute-start.7) | collective-permute-done | bytes 114720 | tf_op jit(solution)/shard_map/ppermute | solution.py:28
  71.9 0.6 collective-permute-start.12
  72.5 0.4 collective-permute-start.13
  72.9 3.9 %image_attention.2 = (f32[1024,256]{1,0:T(8,128)S(1)}, f32[1024,128]{1,0:T(8,128)S(1)}) custom-call(s32[5]{0:T(128)S(1)} %stack.19.place_ref, bf16[16,384,128]{2,1,0:T(8,128)(2,1)S(1)} %all-to-all-done.packed_ref), custom_call_target="tpu_custom_call" | custom-call | flops 1073741824 | bytes 2359296 | tf_op jit(solution)/shard_map/image_attention/pallas_call | solution.py:362
  76.8 1.2 collective-permute-done.12.refs_1_
  78.0 0.5 collective-permute-done.13.refs_3_
  78.6 2.3 %project.1 = (bf16[4,144,256]{2,1,0:T(8,128)(2,1)S(1)}, bf16[4,144,256]{2,1,0:T(8,128)(2,1)S(1)}, bf16[4,144,256]{2,1,0:T(8,128)(2,1)S(1)}, bf16[4,144,256]{2,1,0:T(8,128)(2,1)S(1)}) custom-call(s32[5]{0:T(128)S(1)} %stack.19.place_ref, bf16[64,1792]{1,0:T(8,128)(2,1)S(1)} %get-tuple-element.102.refs_0_, ...), custom_call_target="tpu_custom_call" | custom-call | flops 754974720 | bytes 7864320 | tf_op jit(solution)/shard_map/project/pallas_call | solution.py:206
  80.9 1.6 %collective-permute-start.14 = (bf16[4,144,256]{2,1,0:T(8,128)(2,1)S(1)}, bf16[4,144,256]{2,1,0:T(8,128)(2,1)S(1)}, u32[]{:S(2)}, u32[]{:S(2)}) collective-permute-start(bf16[4,144,256]{2,1,0:T(8,128)(2,1)S(1)} %get-tuple-element.118), channel_id=1, source_target_pairs={{0,2},{1,3},{2,0},{3,1},{4,6},{5,7},{6,4},{7,5},{8,10},{9,11},{10,... | collective-permute-start | bytes 884744 | tf_op jit(solution)/shard_map/ppermute | solution.py:28
  82.5 0.1 collective-permute-start.15
  82.5 4.1 %image_attention.3 = (f32[1024,256]{1,0:T(8,128)S(1)}, f32[1024,128]{1,0:T(8,128)S(1)}) custom-call(s32[5]{0:T(128)S(1)} %stack.19.place_ref, bf16[16,384,128]{2,1,0:T(8,128)(2,1)S(1)} %all-to-all-done.packed_ref), custom_call_target="tpu_custom_call" | custom-call | flops 1073741824 | bytes 2359296 | tf_op jit(solution)/shard_map/image_attention/pallas_call | solution.py:362
  86.7 1.0 collective-permute-done.14.refs_1_
  87.7 2.8 %collective-permute-done.15.refs_3_ = bf16[4,144,256]{2,1,0:T(8,128)(2,1)S(1)} collective-permute-done((bf16[4,144,256]{2,1,0:T(8,128)(2,1)S(1)}, bf16[4,144,256]{2,1,0:T(8,128)(2,1)S(1)}, u32[]{:S(2)}, u32[]{:S(2)}) %collective-permute-start.15) | collective-permute-done | bytes 294944 | tf_op jit(solution)/shard_map/ppermute | solution.py:28
  90.5 0.1 add_halves.6
  90.6 0.1 collective-permute-start.16
  90.7 0.6 collective-permute-start.17
  91.3 6.1 %collective-permute-done.16.refs_1_ = bf16[2,144,256]{2,1,0:T(8,128)(2,1)S(1)} collective-permute-done((bf16[2,144,256]{2,1,0:T(8,128)(2,1)S(1)}, bf16[2,144,256]{2,1,0:T(8,128)(2,1)S(1)}, u32[]{:S(2)}, u32[]{:S(2)}) %collective-permute-start.16) | collective-permute-done | bytes 147488 | tf_op jit(solution)/shard_map/ppermute | solution.py:28
  97.4 1.3 collective-permute-start.18
  98.7 6.4 %collective-permute-done.18.refs_2_ = bf16[2,1,144,256]{3,2,1,0:T(8,128)(2,1)S(1)} collective-permute-done((bf16[2,1,144,256]{3,2,1,0:T(8,128)(2,1)S(1)}, bf16[2,1,144,256]{3,2,1,0:T(8,128)(2,1)S(1)}, u32[]{:S(2)}, u32[]{:S(2)}) %collective-permute-start.18) | collective-permute-done | bytes 147488 | tf_op jit(solution)/shard_map/ppermute | solution.py:28
  105.0 0.7 combine.1
  105.9 1.2 collective-permute-done.19.got_ref
  107.1 1.2 finish.3
  108.4 2.9 %collective-permute-start.24 = (bf16[2,160,128]{2,1,0:T(8,128)(2,1)S(1)}, bf16[2,160,128]{2,1,0:T(8,128)(2,1)S(1)}, u32[]{:S(2)}, u32[]{:S(2)}) collective-permute-start(bf16[2,160,128]{2,1,0:T(8,128)(2,1)S(1)} %get-tuple-element.141), channel_id=1, source_target_pairs={{0,10},{1,11},{2,8},{3,9},{4,14},{5,15},{6,12},{7,13},{8,2},{9,3},... | collective-permute-start | bytes 245768 | tf_op jit(solution)/shard_map/ppermute | solution.py:28
  111.2 1.6 %collective-permute-start.25 = (bf16[2,160,128]{2,1,0:T(8,128)(2,1)S(1)}, bf16[2,160,128]{2,1,0:T(8,128)(2,1)S(1)}, u32[]{:S(2)}, u32[]{:S(2)}) collective-permute-start(bf16[2,160,128]{2,1,0:T(8,128)(2,1)S(1)} %get-tuple-element.142), channel_id=1, source_target_pairs={{0,12},{1,13},{2,14},{3,15},{4,8},{5,9},{6,10},{7,11},{8,4},{9,5},... | collective-permute-start | bytes 245768 | tf_op jit(solution)/shard_map/ppermute | solution.py:28
  112.9 3.1 %collective-permute-start.26 = (bf16[2,160,128]{2,1,0:T(8,128)(2,1)S(1)}, bf16[2,160,128]{2,1,0:T(8,128)(2,1)S(1)}, u32[]{:S(2)}, u32[]{:S(2)}) collective-permute-start(bf16[2,160,128]{2,1,0:T(8,128)(2,1)S(1)} %get-tuple-element.143), channel_id=1, source_target_pairs={{0,14},{1,15},{2,12},{3,13},{4,10},{5,11},{6,8},{7,9},{8,6},{9,7},... | collective-permute-start | bytes 245768 | tf_op jit(solution)/shard_map/ppermute | solution.py:28
  116.0 1.2 finish.2
  117.2 0.6 collective-permute-start.20
  117.8 1.2 collective-permute-done.23.refs_0_.refs_4_
  119.0 2.7 %collective-permute-done.24.refs_1_.refs_5_ = bf16[2,160,128]{2,1,0:T(8,128)(2,1)S(1)} collective-permute-done((bf16[2,160,128]{2,1,0:T(8,128)(2,1)S(1)}, bf16[2,160,128]{2,1,0:T(8,128)(2,1)S(1)}, u32[]{:S(2)}, u32[]{:S(2)}) %collective-permute-start.24) | collective-permute-done | bytes 81952 | tf_op jit(solution)/shard_map/ppermute | solution.py:28
  121.8 1.3 collective-permute-done.20.refs_1_
  123.0 0.4 collective-permute-done.21.refs_2_
  123.4 3.6 %collective-permute-done.22.refs_3_ = bf16[2,160,128]{2,1,0:T(8,128)(2,1)S(1)} collective-permute-done((bf16[2,160,128]{2,1,0:T(8,128)(2,1)S(1)}, bf16[2,160,128]{2,1,0:T(8,128)(2,1)S(1)}, u32[]{:S(2)}, u32[]{:S(2)}) %collective-permute-start.22) | collective-permute-done | bytes 81952 | tf_op jit(solution)/shard_map/ppermute | solution.py:28
  127.1 1.4 %collective-permute-done.27.refs_8_ = bf16[4,160,128]{2,1,0:T(8,128)(2,1)S(1)} collective-permute-done((bf16[4,160,128]{2,1,0:T(8,128)(2,1)S(1)}, bf16[4,160,128]{2,1,0:T(8,128)(2,1)S(1)}, u32[]{:S(2)}, u32[]{:S(2)}) %collective-permute-start.27) | collective-permute-done | bytes 163872 | tf_op jit(solution)/shard_map/ppermute | solution.py:28
  128.5 1.5 %unpack.1 = (bf16[128,2048]{1,0:T(8,128)(2,1)}, bf16[16,4096]{1,0:T(8,128)(2,1)}) custom-call(s32[5]{0:T(128)S(1)} %stack.19.place_ref, bf16[2,160,128]{2,1,0:T(8,128)(2,1)S(1)} %get-tuple-element.134.refs_0_, bf16[2,160,128]{2,1,0:T(8,128)(2,1)S(1)} %collective-permute-done.20.refs_1_, bf16[2,160,128]{2,1,0:T(8,128)(2,1)S(1)} %collective-permute-done.21.refs_2_, ...), custom_call_target="tpu_custom_call" | custom-call | tf_op jit(solution)/shard_map/unpack/pallas_call | solution.py:322
  (35 shorter events, 0.6 us)
Async XLA Ops:
  2.2 1.0 copy-start.4
  4.7 8.3 %copy-start.3 = (bf16[1,256,1184]{1,2,0:T(8,128)(2,1)S(1)}, bf16[1,256,1184]{1,2,0:T(8,128)(2,1)}, u32[]{:S(2)}) copy-start(bf16[1,256,1184]{1,2,0:T(8,128)(2,1)} %param.10) | copy-start | bytes 1818628
  4.7 46.4 %all-to-all-start = ((bf16[16,384,128]{2,1,0:T(8,128)(2,1)}), bf16[16,384,128]{2,1,0:T(8,128)(2,1)S(1)}, u32[]{:S(2)}, u32[]{:S(2)}) async-start(bf16[16,384,128]{2,1,0:T(8,128)(2,1)} %pack.1), calls=%async_computation | async-start | bytes 3145728 | tf_op jit(solution)/shard_map/all_to_all | solution.py:616
  13.0 3.4 %copy-start = (bf16[1184,3584]{1,0:T(8,128)(2,1)S(1)}, bf16[1184,3584]{1,0:T(8,128)(2,1)}, u32[]{:S(2)}) copy-start(bf16[1184,3584]{1,0:T(8,128)(2,1)} %weight_ref.1) | copy-start | bytes 25460740
  19.8 1.9 %collective-permute-start = (bf16[8,16,1792]{2,1,0:T(8,128)(2,1)S(1)}, bf16[8,16,1792]{2,1,0:T(8,128)(2,1)S(1)}, u32[]{:S(2)}, u32[]{:S(2)}) collective-permute-start(bf16[8,16,1792]{2,1,0:T(8,128)(2,1)S(1)} %get-tuple-element.78), channel_id=1, source_target_pairs={{0,1},{1,0},{2,3},{3,2},{4,5},{5,4},{6,7},{7,6},{8,9},{9,8},{10,11... | collective-permute-start | bytes 1376264 | tf_op jit(solution)/shard_map/ppermute | solution.py:28
  20.3 2.1 %collective-permute-start.1 = (bf16[8,16,1792]{2,1,0:T(8,128)(2,1)S(1)}, bf16[8,16,1792]{2,1,0:T(8,128)(2,1)S(1)}, u32[]{:S(2)}, u32[]{:S(2)}) collective-permute-start(bf16[8,16,1792]{2,1,0:T(8,128)(2,1)S(1)} %get-tuple-element.80), channel_id=1, source_target_pairs={{0,1},{1,0},{2,3},{3,2},{4,5},{5,4},{6,7},{7,6},{8,9},{9,8},{10,11... | collective-permute-start | bytes 1376264 | tf_op jit(solution)/shard_map/ppermute | solution.py:28
  22.6 28.5 %copy-start.1 = (bf16[192,4096]{1,0:T(8,128)(2,1)S(1)}, bf16[192,4096]{1,0:T(8,128)(2,1)}, u32[]{:S(2)}) copy-start(bf16[192,4096]{1,0:T(8,128)(2,1)} %refs_7_.1) | copy-start | bytes 4718596
  22.6 32.6 %copy-start.6 = (bf16[3584]{0:T(1024)(128)(2,1)S(1)}, bf16[3584]{0:T(1024)(128)(2,1)}, u32[]{:S(2)}) copy-start(bf16[3584]{0:T(1024)(128)(2,1)} %param.12) | copy-start | bytes 21508
  22.6 13.5 %collective-permute-start.2 = (bf16[4,16,1792]{2,1,0:T(8,128)(2,1)S(1)}, bf16[4,16,1792]{2,1,0:T(8,128)(2,1)S(1)}, u32[]{:S(2)}, u32[]{:S(2)}) collective-permute-start(bf16[4,16,1792]{2,1,0:T(8,128)(2,1)S(1)} %get-tuple-element.82), channel_id=1, source_target_pairs={{0,2},{1,3},{2,0},{3,1},{4,6},{5,7},{6,4},{7,5},{8,10},{9,11},{10,... | collective-permute-start | bytes 688136 | tf_op jit(solution)/shard_map/ppermute | solution.py:28
  24.6 19.1 %collective-permute-start.3 = (bf16[4,16,1792]{2,1,0:T(8,128)(2,1)S(1)}, bf16[4,16,1792]{2,1,0:T(8,128)(2,1)S(1)}, u32[]{:S(2)}, u32[]{:S(2)}) collective-permute-start(bf16[4,16,1792]{2,1,0:T(8,128)(2,1)S(1)} %get-tuple-element.84), channel_id=1, source_target_pairs={{0,4},{1,5},{2,6},{3,7},{4,0},{5,1},{6,2},{7,3},{8,12},{9,13},{10,... | collective-permute-start | bytes 688136 | tf_op jit(solution)/shard_map/ppermute | solution.py:28
  43.7 5.8 %collective-permute-start.4 = (bf16[2,16,1792]{2,1,0:T(8,128)(2,1)S(1)}, bf16[2,16,1792]{2,1,0:T(8,128)(2,1)S(1)}, u32[]{:S(2)}, u32[]{:S(2)}) collective-permute-start(bf16[2,16,1792]{2,1,0:T(8,128)(2,1)S(1)} %get-tuple-element.86), channel_id=1, source_target_pairs={{0,4},{1,5},{2,6},{3,7},{4,0},{5,1},{6,2},{7,3},{8,12},{9,13},{10,... | collective-permute-start | bytes 344072 | tf_op jit(solution)/shard_map/ppermute | solution.py:28
  46.3 4.8 %collective-permute-start.5 = (bf16[2,16,1792]{2,1,0:T(8,128)(2,1)S(1)}, bf16[2,16,1792]{2,1,0:T(8,128)(2,1)S(1)}, u32[]{:S(2)}, u32[]{:S(2)}) collective-permute-start(bf16[2,16,1792]{2,1,0:T(8,128)(2,1)S(1)} %get-tuple-element.88), channel_id=1, source_target_pairs={{0,2},{1,3},{2,0},{3,1},{4,6},{5,7},{6,4},{7,5},{8,10},{9,11},{10,... | collective-permute-start | bytes 344072 | tf_op jit(solution)/shard_map/ppermute | solution.py:28
  51.1 20.7 %collective-permute-start.10 = (bf16[192,4096]{1,0:T(8,128)(2,1)S(1)}, bf16[192,4096]{1,0:T(8,128)(2,1)S(1)}, u32[]{:S(2)}, u32[]{:S(2)}) collective-permute-start(bf16[192,4096]{1,0:T(8,128)(2,1)S(1)} %copy-done.1), channel_id=1, source_target_pairs={{0,1},{1,0},{2,3},{3,2},{4,5},{5,4},{6,7},{7,6},{8,9},{9,8},{10,11... | collective-permute-start | bytes 4718600 | tf_op jit(solution)/shard_map/ppermute | solution.py:28
  51.2 20.7 %collective-permute-start.9 = (bf16[192,3584]{1,0:T(8,128)(2,1)}, bf16[192,3584]{1,0:T(8,128)(2,1)S(1)}, u32[]{:S(2)}, u32[]{:S(2)}) collective-permute-start(bf16[192,3584]{1,0:T(8,128)(2,1)} %bitcast.22), channel_id=1, source_target_pairs={{0,1},{1,0},{2,3},{3,2},{4,5},{5,4},{6,7},{7,6},{8,9},{9,8},{10,11... | collective-permute-start | bytes 4128776 | tf_op jit(solution)/shard_map/ppermute | solution.py:28
  51.7 13.6 %collective-permute-start.6 = (bf16[2,2,16,1792]{3,2,1,0:T(8,128)(2,1)S(1)}, bf16[2,2,16,1792]{3,2,1,0:T(8,128)(2,1)S(1)}, u32[]{:S(2)}, u32[]{:S(2)}) collective-permute-start(bf16[2,2,16,1792]{3,2,1,0:T(8,128)(2,1)S(1)} %add_all.1.mine_ref), channel_id=1, source_target_pairs={{0,8},{1,9},{2,10},{3,11},{4,12},{5,13},{6,14},{7,15},{8,0},{9,1},... | collective-permute-start | bytes 688136 | tf_op jit(solution)/shard_map/ppermute | solution.py:28
  55.3 11.9 %collective-permute-start.11 = (bf16[2,192,256]{2,1,0:T(8,128)(2,1)}, bf16[2,192,256]{2,1,0:T(8,128)(2,1)S(1)}, u32[]{:S(2)}, u32[]{:S(2)}) collective-permute-start(bf16[2,192,256]{2,1,0:T(8,128)(2,1)} %bitcast.26), channel_id=1, source_target_pairs={{0,1},{1,0},{2,3},{3,2},{4,5},{5,4},{6,7},{7,6},{8,9},{9,8},{10,11... | collective-permute-start | bytes 589832 | tf_op jit(solution)/shard_map/ppermute | solution.py:28
  65.5 4.9 %collective-permute-start.8 = (bf16[32,1792]{1,0:T(8,128)(2,1)S(1)}, bf16[32,1792]{1,0:T(8,128)(2,1)S(1)}, u32[]{:S(2)}, u32[]{:S(2)}) collective-permute-start(bf16[32,1792]{1,0:T(8,128)(2,1)S(1)} %bitcast.30), channel_id=1, source_target_pairs={{0,2},{1,3},{2,0},{3,1},{4,6},{5,7},{6,4},{7,5},{8,10},{9,11},{10,... | collective-permute-start | bytes 344072 | tf_op jit(solution)/shard_map/ppermute | solution.py:28
  67.1 4.8 %collective-permute-start.7 = (bf16[32,1792]{1,0:T(8,128)(2,1)S(1)}, bf16[32,1792]{1,0:T(8,128)(2,1)S(1)}, u32[]{:S(2)}, u32[]{:S(2)}) collective-permute-start(bf16[32,1792]{1,0:T(8,128)(2,1)S(1)} %bitcast.28), channel_id=1, source_target_pairs={{0,4},{1,5},{2,6},{3,7},{4,0},{5,1},{6,2},{7,3},{8,12},{9,13},{10,... | collective-permute-start | bytes 344072 | tf_op jit(solution)/shard_map/ppermute | solution.py:28
  67.2 0.9 copy-start.5
  71.9 6.6 %copy-start.2 = (bf16[3584,192]{0,1:T(8,128)(2,1)S(1)}, bf16[3584,192]{0,1:T(8,128)(2,1)}, u32[]{:S(2)}) copy-start(bf16[3584,192]{0,1:T(8,128)(2,1)} %param.13) | copy-start | bytes 4128772
  71.9 6.1 %collective-permute-start.12 = (bf16[64,1792]{1,0:T(8,128)(2,1)S(1)}, bf16[64,1792]{1,0:T(8,128)(2,1)S(1)}, u32[]{:S(2)}, u32[]{:S(2)}) collective-permute-start(bf16[64,1792]{1,0:T(8,128)(2,1)S(1)} %get-tuple-element.102.refs_0_), channel_id=1, source_target_pairs={{0,2},{1,3},{2,0},{3,1},{4,6},{5,7},{6,4},{7,5},{8,10},{9,11},{10,... | collective-permute-start | bytes 688136 | tf_op jit(solution)/shard_map/ppermute | solution.py:28
  72.5 6.0 %collective-permute-start.13 = (bf16[64,1792]{1,0:T(8,128)(2,1)S(1)}, bf16[64,1792]{1,0:T(8,128)(2,1)S(1)}, u32[]{:S(2)}, u32[]{:S(2)}) collective-permute-start(bf16[64,1792]{1,0:T(8,128)(2,1)S(1)} %get-tuple-element.103.refs_2_), channel_id=1, source_target_pairs={{0,4},{1,5},{2,6},{3,7},{4,0},{5,1},{6,2},{7,3},{8,12},{9,13},{10,... | collective-permute-start | bytes 688136 | tf_op jit(solution)/shard_map/ppermute | solution.py:28
  80.9 6.8 %collective-permute-start.14 = (bf16[4,144,256]{2,1,0:T(8,128)(2,1)S(1)}, bf16[4,144,256]{2,1,0:T(8,128)(2,1)S(1)}, u32[]{:S(2)}, u32[]{:S(2)}) collective-permute-start(bf16[4,144,256]{2,1,0:T(8,128)(2,1)S(1)} %get-tuple-element.118), channel_id=1, source_target_pairs={{0,2},{1,3},{2,0},{3,1},{4,6},{5,7},{6,4},{7,5},{8,10},{9,11},{10,... | collective-permute-start | bytes 884744 | tf_op jit(solution)/shard_map/ppermute | solution.py:28
  82.5 8.0 %collective-permute-start.15 = (bf16[4,144,256]{2,1,0:T(8,128)(2,1)S(1)}, bf16[4,144,256]{2,1,0:T(8,128)(2,1)S(1)}, u32[]{:S(2)}, u32[]{:S(2)}) collective-permute-start(bf16[4,144,256]{2,1,0:T(8,128)(2,1)S(1)} %get-tuple-element.119), channel_id=1, source_target_pairs={{0,4},{1,5},{2,6},{3,7},{4,0},{5,1},{6,2},{7,3},{8,12},{9,13},{10,... | collective-permute-start | bytes 884744 | tf_op jit(solution)/shard_map/ppermute | solution.py:28
  90.6 6.7 %collective-permute-start.16 = (bf16[2,144,256]{2,1,0:T(8,128)(2,1)S(1)}, bf16[2,144,256]{2,1,0:T(8,128)(2,1)S(1)}, u32[]{:S(2)}, u32[]{:S(2)}) collective-permute-start(bf16[2,144,256]{2,1,0:T(8,128)(2,1)S(1)} %get-tuple-element.126), channel_id=1, source_target_pairs={{0,4},{1,5},{2,6},{3,7},{4,0},{5,1},{6,2},{7,3},{8,12},{9,13},{10,... | collective-permute-start | bytes 442376 | tf_op jit(solution)/shard_map/ppermute | solution.py:28
  90.7 6.7 %collective-permute-start.17 = (bf16[2,144,256]{2,1,0:T(8,128)(2,1)S(1)}, bf16[2,144,256]{2,1,0:T(8,128)(2,1)S(1)}, u32[]{:S(2)}, u32[]{:S(2)}) collective-permute-start(bf16[2,144,256]{2,1,0:T(8,128)(2,1)S(1)} %get-tuple-element.128), channel_id=1, source_target_pairs={{0,2},{1,3},{2,0},{3,1},{4,6},{5,7},{6,4},{7,5},{8,10},{9,11},{10,... | collective-permute-start | bytes 442376 | tf_op jit(solution)/shard_map/ppermute | solution.py:28
  97.4 7.6 %collective-permute-start.18 = (bf16[2,1,144,256]{3,2,1,0:T(8,128)(2,1)S(1)}, bf16[2,1,144,256]{3,2,1,0:T(8,128)(2,1)S(1)}, u32[]{:S(2)}, u32[]{:S(2)}) collective-permute-start(bf16[2,1,144,256]{3,2,1,0:T(8,128)(2,1)S(1)} %get-tuple-element.131), channel_id=1, source_target_pairs={{0,8},{1,9},{2,10},{3,11},{4,12},{5,13},{6,14},{7,15},{8,0},{9,1},... | collective-permute-start | bytes 442376 | tf_op jit(solution)/shard_map/ppermute | solution.py:28
  105.8 1.3 %collective-permute-start.19 = (bf16[128,256]{1,0:T(8,128)(2,1)S(1)}, bf16[128,256]{1,0:T(8,128)(2,1)S(1)}, u32[]{:S(2)}, u32[]{:S(2)}) collective-permute-start(bf16[128,256]{1,0:T(8,128)(2,1)S(1)} %get-tuple-element.133), channel_id=1, source_target_pairs={{0,1},{1,0},{2,3},{3,2},{4,5},{5,4},{6,7},{7,6},{8,9},{9,8},{10,11... | collective-permute-start | bytes 196616 | tf_op jit(solution)/shard_map/ppermute | solution.py:28
  108.3 10.7 %collective-permute-start.23 = (bf16[2,160,128]{2,1,0:T(8,128)(2,1)S(1)}, bf16[2,160,128]{2,1,0:T(8,128)(2,1)S(1)}, u32[]{:S(2)}, u32[]{:S(2)}) collective-permute-start(bf16[2,160,128]{2,1,0:T(8,128)(2,1)S(1)} %get-tuple-element.140), channel_id=1, source_target_pairs={{0,8},{1,9},{2,10},{3,11},{4,12},{5,13},{6,14},{7,15},{8,0},{9,1},... | collective-permute-start | bytes 245768 | tf_op jit(solution)/shard_map/ppermute | solution.py:28
  108.4 13.3 %collective-permute-start.24 = (bf16[2,160,128]{2,1,0:T(8,128)(2,1)S(1)}, bf16[2,160,128]{2,1,0:T(8,128)(2,1)S(1)}, u32[]{:S(2)}, u32[]{:S(2)}) collective-permute-start(bf16[2,160,128]{2,1,0:T(8,128)(2,1)S(1)} %get-tuple-element.141), channel_id=1, source_target_pairs={{0,10},{1,11},{2,8},{3,9},{4,14},{5,15},{6,12},{7,13},{8,2},{9,3},... | collective-permute-start | bytes 245768 | tf_op jit(solution)/shard_map/ppermute | solution.py:28
  111.2 10.4 %collective-permute-start.25 = (bf16[2,160,128]{2,1,0:T(8,128)(2,1)S(1)}, bf16[2,160,128]{2,1,0:T(8,128)(2,1)S(1)}, u32[]{:S(2)}, u32[]{:S(2)}) collective-permute-start(bf16[2,160,128]{2,1,0:T(8,128)(2,1)S(1)} %get-tuple-element.142), channel_id=1, source_target_pairs={{0,12},{1,13},{2,14},{3,15},{4,8},{5,9},{6,10},{7,11},{8,4},{9,5},... | collective-permute-start | bytes 245768 | tf_op jit(solution)/shard_map/ppermute | solution.py:28
  112.9 8.8 %collective-permute-start.26 = (bf16[2,160,128]{2,1,0:T(8,128)(2,1)S(1)}, bf16[2,160,128]{2,1,0:T(8,128)(2,1)S(1)}, u32[]{:S(2)}, u32[]{:S(2)}) collective-permute-start(bf16[2,160,128]{2,1,0:T(8,128)(2,1)S(1)} %get-tuple-element.143), channel_id=1, source_target_pairs={{0,14},{1,15},{2,12},{3,13},{4,10},{5,11},{6,8},{7,9},{8,6},{9,7},... | collective-permute-start | bytes 245768 | tf_op jit(solution)/shard_map/ppermute | solution.py:28
  117.2 5.9 %collective-permute-start.20 = (bf16[2,160,128]{2,1,0:T(8,128)(2,1)S(1)}, bf16[2,160,128]{2,1,0:T(8,128)(2,1)S(1)}, u32[]{:S(2)}, u32[]{:S(2)}) collective-permute-start(bf16[2,160,128]{2,1,0:T(8,128)(2,1)S(1)} %get-tuple-element.135), channel_id=1, source_target_pairs={{0,2},{1,3},{2,0},{3,1},{4,6},{5,7},{6,4},{7,5},{8,10},{9,11},{10,... | collective-permute-start | bytes 245768 | tf_op jit(solution)/shard_map/ppermute | solution.py:28
  119.0 4.4 %collective-permute-start.21 = (bf16[2,160,128]{2,1,0:T(8,128)(2,1)S(1)}, bf16[2,160,128]{2,1,0:T(8,128)(2,1)S(1)}, u32[]{:S(2)}, u32[]{:S(2)}) collective-permute-start(bf16[2,160,128]{2,1,0:T(8,128)(2,1)S(1)} %get-tuple-element.136), channel_id=1, source_target_pairs={{0,4},{1,5},{2,6},{3,7},{4,0},{5,1},{6,2},{7,3},{8,12},{9,13},{10,... | collective-permute-start | bytes 245768 | tf_op jit(solution)/shard_map/ppermute | solution.py:28
  121.7 5.3 %collective-permute-start.22 = (bf16[2,160,128]{2,1,0:T(8,128)(2,1)S(1)}, bf16[2,160,128]{2,1,0:T(8,128)(2,1)S(1)}, u32[]{:S(2)}, u32[]{:S(2)}) collective-permute-start(bf16[2,160,128]{2,1,0:T(8,128)(2,1)S(1)} %get-tuple-element.137), channel_id=1, source_target_pairs={{0,6},{1,7},{2,4},{3,5},{4,2},{5,3},{6,0},{7,1},{8,14},{9,15},{10,... | collective-permute-start | bytes 245768 | tf_op jit(solution)/shard_map/ppermute | solution.py:28
  121.7 5.4 %collective-permute-start.28 = (bf16[4,160,128]{2,1,0:T(8,128)(2,1)S(1)}, bf16[4,160,128]{2,1,0:T(8,128)(2,1)S(1)}, u32[]{:S(2)}, u32[]{:S(2)}) collective-permute-start(bf16[4,160,128]{2,1,0:T(8,128)(2,1)S(1)} %gather_other.3), channel_id=1, source_target_pairs={{0,1},{1,0},{2,3},{3,2},{4,5},{5,4},{6,7},{7,6},{8,9},{9,8},{10,11... | collective-permute-start | bytes 491528 | tf_op jit(solution)/shard_map/ppermute | solution.py:28
  127.0 1.5 %collective-permute-start.27 = (bf16[4,160,128]{2,1,0:T(8,128)(2,1)S(1)}, bf16[4,160,128]{2,1,0:T(8,128)(2,1)S(1)}, u32[]{:S(2)}, u32[]{:S(2)}) collective-permute-start(bf16[4,160,128]{2,1,0:T(8,128)(2,1)S(1)} %gather_other.2), channel_id=1, source_target_pairs={{0,1},{1,0},{2,3},{3,2},{4,5},{5,4},{6,7},{7,6},{8,9},{9,8},{10,11... | collective-permute-start | bytes 491528 | tf_op jit(solution)/shard_map/ppermute | solution.py:28

commit v17 on v16

--- a/solution.py
+++ b/solution.py
@@ -271,31 +271,55 @@
     )(place, *parts)
 
 
-def pack_kernel(copies, queries_ref, keys_ref, values_ref, out_ref):
+def pack_kernel(copies, keys_ref, values_ref, out_ref):
     img_dev = keys_ref.shape[0]
-    part_rows = img_dev // copies
     for device in range(out_ref.shape[0]):
-        head, copy = device // copies, device % copies
+        head = device // copies
         span = slice(head * HEAD_DIM, (head + 1) * HEAD_DIM)
         out_ref[device, :img_dev, :] = keys_ref[:, span]
-        out_ref[device, img_dev : 2 * img_dev, :] = values_ref[:, span]
-        out_ref[device, 2 * img_dev :, :] = queries_ref[copy * part_rows : (copy + 1) * part_rows, span]
-
-
-def pack(copies, queries, keys, values):
+        out_ref[device, img_dev:, :] = values_ref[:, span]
+
+
+def pack(copies, keys, values):
     img_dev = keys.shape[0]
-    rows = 2 * img_dev + img_dev // copies
     return pl.pallas_call(
         functools.partial(pack_kernel, copies),
-        out_shape=jax.ShapeDtypeStruct((HEADS * copies, rows, HEAD_DIM), jnp.bfloat16),
-        in_specs=[VMEM_SPEC] * 3,
+        out_shape=jax.ShapeDtypeStruct((HEADS * copies, 2 * img_dev, HEAD_DIM), jnp.bfloat16),
+        in_specs=[VMEM_SPEC] * 2,
         out_specs=VMEM_SPEC,
         compiler_params=params(8),
-        cost_estimate=pl.CostEstimate(
-            flops=0, bytes_accessed=4 * HEADS * copies * rows * HEAD_DIM, transcendentals=0
-        ),
+        cost_estimate=pl.CostEstimate(flops=0, bytes_accessed=8 * keys.size, transcendentals=0),
         name="pack",
-    )(queries, keys, values)
+    )(keys, values)
+
+
+def split_kernel(copies, place_ref, queries_ref, *outs):
+    chip, core = place_ref[3], place_ref[2]
+    part_rows = queries_ref.shape[0] // copies
+    for mask, out_ref in enumerate(outs):
+        for side in range(2):
+            device = 2 * (chip ^ mask) + (core ^ side)
+            head, copy = device // copies, device % copies
+            span = pl.ds(pl.multiple_of(head * HEAD_DIM, HEAD_DIM), HEAD_DIM)
+            rows = pl.ds(pl.multiple_of(copy * part_rows, part_rows), part_rows)
+            out_ref[side] = queries_ref[rows, span]
+
+
+def split(chips, copies, place, queries):
+    out = jax.ShapeDtypeStruct((2, queries.shape[0] // copies, HEAD_DIM), jnp.bfloat16)
+    return pl.pallas_call(
+        functools.partial(split_kernel, copies),
+        out_shape=(out,) * chips,
+        in_specs=[SMEM_SPEC, VMEM_SPEC],
+        out_specs=(VMEM_SPEC,) * chips,
+        compiler_params=params(4),
+        cost_estimate=pl.CostEstimate(flops=0, bytes_accessed=4 * queries.size, transcendentals=0),
+        name="split",
+    )(place, queries)
+
+
+def by_distance(pieces, passed):
+    return [view for piece, other in zip(pieces, passed) for view in (piece.at[0], other)]
 
 
 def unpack_kernel(copies, part_rows, place_ref, *refs):
@@ -332,22 +356,23 @@
     )(place, *pieces, near, far)
 
 
-def image_kernel(factor, call, img_dev, place_ref, packed_ref, sum_ref, top_ref, keys_ref, wide_ref):
-    me = 2 * place_ref[3] + place_ref[2]
+def image_kernel(factor, first, packed_ref, *refs):
+    *pieces, passed_ref, sum_ref, top_ref, keys_ref, wide_ref = refs
+    blocks = by_distance(pieces, [passed_ref.at[first + at] for at in range(len(pieces))])
+    img_dev = packed_ref.shape[1] // 2
     wide_ref[:, HEAD_DIM:] = jnp.ones((wide_ref.shape[0], HEAD_DIM), wide_ref.dtype)
     for device in range(packed_ref.shape[0]):
         rows = slice(device * img_dev, (device + 1) * img_dev)
         keys_ref[rows, :] = packed_ref[device, :img_dev, :]
-        wide_ref[rows, :HEAD_DIM] = packed_ref[device, img_dev : 2 * img_dev, :]
-    group = max(1, 256 // (packed_ref.shape[1] - 2 * img_dev))
+        wide_ref[rows, :HEAD_DIM] = packed_ref[device, img_dev:, :]
+    group = max(1, 256 // passed_ref.shape[1])
     rows = 256
     contract = (((1,), (1,)), ((), ()))
     count = sum_ref.shape[0]
     for start in range(0, count, rows):
         span = slice(start, start + rows)
-        at = (call * count + start) // rows * group
-        queries = [packed_ref[me ^ (at + i), 2 * img_dev :, :] for i in range(group)]
-        queries = jnp.concatenate(queries, 0)
+        at = start // rows * group
+        queries = jnp.concatenate([block[...] for block in blocks[at : at + group]], 0)
         scores = lax.dot_general(queries, keys_ref[...], contract, preferred_element_type=jnp.float32)
         scores = scores * factor
         top = jnp.max(scores, 1, keepdims=True)
@@ -356,16 +381,16 @@
         top_ref[span, :] = jnp.broadcast_to(top, (rows, HEAD_DIM))
 
 
-def image_attention(place, packed, img_dev, factor, call, calls):
-    count = packed.shape[0] * (packed.shape[1] - 2 * img_dev) // calls
-    total = packed.shape[0] * img_dev
-    return pl.pallas_call(
-        functools.partial(image_kernel, factor, call, img_dev),
+def image_attention(packed, first, pieces, passed, factor):
+    count = 2 * len(pieces) * passed.shape[1]
+    total = packed.size // HEAD_DIM // 2
+    return pl.pallas_call(
+        functools.partial(image_kernel, factor, first),
         out_shape=(
             jax.ShapeDtypeStruct((count, 2 * HEAD_DIM), jnp.float32),
             jax.ShapeDtypeStruct((count, HEAD_DIM), jnp.float32),
         ),
-        in_specs=[SMEM_SPEC, VMEM_SPEC],
+        in_specs=[VMEM_SPEC] * (len(pieces) + 2),
         out_specs=(VMEM_SPEC, VMEM_SPEC),
         scratch_shapes=[
             pltpu.VMEM((total, HEAD_DIM), jnp.bfloat16),
@@ -378,14 +403,15 @@
             transcendentals=count * total,
         ),
         name="image_attention",
-    )(place, packed)
-
-
-def finish_kernel(factor, first, img_dev, place_ref, packed_ref, sum_ref, top_ref, mine_ref, got_ref, *refs):
-    *outs, text_ref = refs
+    )(packed, *pieces, passed)
+
+
+def finish_kernel(factor, first, count, place_ref, sum_ref, top_ref, mine_ref, got_ref, *refs):
+    pieces, passed_ref, outs, text_ref = refs[:count], refs[count], refs[count + 1 : -1], refs[-1]
+    blocks = by_distance(pieces, [passed_ref.at[first + at] for at in range(count)])
     core, valid = place_ref[2], place_ref[4]
     me = 2 * place_ref[3] + core
-    part_rows = packed_ref.shape[1] - 2 * img_dev
+    part_rows = passed_ref.shape[1]
     half = mine_ref.shape[0]
     contract = (((1,), (1,)), ((), ()))
     mine, got = mine_ref[...], got_ref[...]
@@ -399,9 +425,7 @@
     rows = group * part_rows
     for step in range(2 * len(outs) // group):
         span = slice(step * rows, (step + 1) * rows)
-        queries = [
-            packed_ref[me ^ (2 * first + step * group + at), 2 * img_dev :, :] for at in range(group)
-        ]
+        queries = [block[...] for block in blocks[step * group : (step + 1) * group]]
         queries = jnp.concatenate(queries, 0)
         scores = lax.dot_general(queries, keys, contract, preferred_element_type=jnp.float32)
         scores = scores * factor + bias
@@ -427,16 +451,17 @@
         outs[to // 2][to % 2, part_rows:, :] = block.astype(jnp.bfloat16)
 
 
-def finish(place, first, packed, image, mine, got, img_dev, factor):
-    devices, part_rows = packed.shape[0], packed.shape[1] - 2 * img_dev
+def finish(place, first, pieces, passed, image, mine, got):
+    chips, part_rows = passed.shape[0], passed.shape[1]
     half = mine.shape[0]
+    outs = len(pieces)
     count = image[0].shape[0]
-    outs = count // part_rows // 2
-    out = jax.ShapeDtypeStruct((2, part_rows + 4 * half // devices, HEAD_DIM), jnp.bfloat16)
-    return pl.pallas_call(
-        functools.partial(finish_kernel, factor, first, img_dev),
+    out = jax.ShapeDtypeStruct((2, part_rows + 2 * half // chips, HEAD_DIM), jnp.bfloat16)
+    factor = math.log2(math.e) / math.sqrt(HEAD_DIM)
+    return pl.pallas_call(
+        functools.partial(finish_kernel, factor, first, outs),
         out_shape=(out,) * outs,
-        in_specs=[SMEM_SPEC] + [VMEM_SPEC] * 5,
+        in_specs=[SMEM_SPEC] + [VMEM_SPEC] * (outs + 5),
         out_specs=(VMEM_SPEC,) * outs,
         scratch_shapes=[pltpu.VMEM((2 * half, 2 * HEAD_DIM), jnp.float32)],
         compiler_params=params(10),
@@ -446,7 +471,7 @@
             transcendentals=2 * count * half,
         ),
         name="finish",
-    )(place, packed, *image, mine, got)
+    )(place, *image, mine, got, *pieces, passed)
 
 
 def gather_kernel(*refs):
@@ -616,64 +641,86 @@
         return lax.all_to_all(rows, "seq", split_axis=0, concat_axis=0, tiled=True)
 
     image_key_values, image_queries = tie((image_key_values, image_queries))
-    packed = pack(copies, image_queries[0], image_key_values[0, :, 0], image_key_values[0, :, 1])
+    packed = pack(copies, image_key_values[0, :, 0], image_key_values[0, :, 1])
     act, packed = tie((enc_act[0].T, packed))
     packed = exchange(packed)
+    pieces = {}
+
+    def beside(chain, masks):
+        chain, held = tie((chain, [pieces[mask] for mask in masks]))
+        pieces.update((mask, swap(piece, 2 * mask)) for mask, piece in zip(masks, held))
+        return chain
+
+    def arrived(chain, masks):
+        chain, held = tie((chain, [pieces[mask] for mask in masks]))
+        pieces.update(zip(masks, held))
+        return chain
+
+    near, far = list(range(1, chips // 2)), list(range(chips // 2, chips))
     encoded = encoder(lanes, place, act, down_weight)
     keep, got = encoded[::2], [swap(other, 1) for other in encoded[1::2]]
     last = 2 * lanes[0][-1]
     for step in range(rounds - 1):
         sent, keep = add_halves(keep, got)
+        if step == 0:
+            sent, image_queries = tie((sent, image_queries))
+            pieces.update(enumerate(split(chips, copies, place, image_queries[0])))
+        masks = far[:1] * (step == 1)
+        sent = beside(sent, masks)
         got = [swap(part, 2 * order[step]) for part, order in zip(sent, lanes)]
+        got = arrived(got, masks)
     summed, packed = tie((add_all(keep, got), packed))
     summed, held, held_kv, held_mod = tie((summed, win0, kv0, mod0))
     win1, kv1, mod1 = swap(held, 1), swap(held_kv, 1), swap(held_mod, 1)
-    got = swap(summed, last)
+    summed = beside(summed, near)
+    got = arrived(swap(summed, last), near)
 
     states = normalize(summed, got, norm_gain[None, :])
     images = []
     for step in reversed(range(rounds - 1)):
-        if step == 0:
-            states, packed = tie((states, packed))
-            image = image_attention(place, packed, img_dev, factor, 0, 2)
+        masks = far[1:2] * (step == 1) if step else far[2:]
+        states = beside(states, masks)
         got = [swap(state, 2 * order[step]) for state, order in zip(states, lanes)]
+        got = arrived(got, masks)
         if step == rounds - 2:
             lines = modulation(time, mod0, mod1)
             got, win1, kv1, lines = tie((got, win1, kv1, lines))
         if step:
             states = join(states, got)
-    got, image = tie((got, image))
-    images += image
     states = [state for pair in zip(states, got) for state in pair]
 
     blocks = project(lanes, place, states, lines, win0, win1, kv0, kv1)
     keep, sent = [blocks[0], blocks[2]], [blocks[1], blocks[3]]
+    pieces = [pieces[mask] for mask in range(chips)]
     for step in range(rounds - 1):
-        if step == 0:
-            sent, packed = tie((sent, packed))
-            image = image_attention(place, packed, img_dev, factor, 1, 2)
         got = [swap(part, 2 * order[step]) for part, order in zip(sent, lanes)]
         if step == 0:
+            passed = swap(gather_other(pieces), 1)
+            got, passed = tie((got, passed))
+        if step == 1:
+            sent, passed = tie((sent, passed))
+            image = image_attention(packed, 0, pieces[: chips // 2], passed, factor)
             got, image = tie((got, image))
             images += image
         sent, keep = add_halves(keep, got, step == rounds - 2)
-    parts = (*keep, swap(sent, last))
+    sent, passed = tie((sent, passed))
+    image = image_attention(packed, chips // 2, pieces[chips // 2 :], passed, factor)
+    got, image = tie((swap(sent, last), image))
+    images += image
+    parts = (*keep, got)
     model_width = text_in_weight.shape[1] * devices
     mine, sent = combine(place, parts, chips, text_len // 2, model_width)
     got = swap(sent, 1)
 
-    pieces = [None] * chips
-    passed = [None] * 2
+    back = [None] * chips
     for call in (1, 0):
-        first = call * chips // 2
+        span = slice(call * chips // 2, (call + 1) * chips // 2)
         image = images[2 * call : 2 * call + 2]
-        blocks = finish(place, first, packed, image, mine, got, img_dev, factor)
-        for at, block in enumerate(blocks):
-            mask = first + at
-            pieces[mask] = swap(block, 2 * mask) if mask else block
-    for call in range(2):
-        passed[call] = swap(gather_other(pieces[call * chips // 2 : (call + 1) * chips // 2]), 1)
-    attended, text_kv = unpack(copies, part_rows, place, pieces, *passed)
+        blocks = finish(place, span.start, pieces[span], passed, image, mine, got)
+        for mask, block in zip(range(chips)[span], blocks):
+            back[mask] = swap(block, 2 * mask) if mask else block
+    passed = [swap(gather_other(back[at : at + chips // 2]), 1) for at in (0, chips // 2)]
+    attended, text_kv = unpack(copies, part_rows, place, back, *passed)
     return (attended[None], text_kv)
 
 

time: 130 us -> 133 us (1.023)
  waiting for transfers between devices: 65.9 us -> 51.3 us
  starting transfers between devices: 33.9 us -> 47.7 us
  Pallas kernels: 20.8 us -> 23 us
    ppermute x29 -> x37, waiting for transfers between devices: 65.9 us -> 51.3 us  [swap(): return lax.ppermute(value, 'seq', [(i, i ^ mask) for i in range(devices)])]
    ppermute x29 -> x37, starting transfers between devices: 26.4 us -> 40.2 us  [swap(): return lax.ppermute(value, 'seq', [(i, i ^ mask) for i in range(devices)])]
    pallas_call x4 -> x5, Pallas kernels: 10.4 us -> 12.8 us  [the longest x2 9.71 us: image_attention(): pl.pallas_call(functools.partial(image_kernel, factor, first), out_shape=...]
    unnamed x14 -> x26, local copies, waits for them, and re-layouts: 5.31 us -> 6.58 us
  transfers between devices with their start and end apart: 30 -> 38, of which waited for: 22 -> 22; matrix products, arithmetic and copies ran while one was open for 0% -> 0% of each run, Pallas kernels for 10% -> 12%
where the time goes in v17:
time: 133 us
  waiting for transfers between devices  51.3 us (39%)
  starting transfers between devices  47.7 us (36%)
  Pallas kernels  23 us (17%)
  local copies, waits for them, and re-layouts  8.35 us (6%)
  between operations  2.31 us (2%)
    ppermute x37, waiting for transfers between devices, swap(): return lax.ppermute(value, 'seq', [(i, i ^ mask) for i in range(devices)])  51.3 us
    ppermute x37, starting transfers between devices, swap(): return lax.ppermute(value, 'seq', [(i, i ^ mask) for i in range(devices)])  40.2 us
    pallas_call x2, Pallas kernels, image_attention(): pl.pallas_call(functools.partial(image_kernel, factor, first), out_shape=...  9.71 us
    all_to_all x1, starting transfers between devices, exchange(): return lax.all_to_all(rows, 'seq', split_axis=0, concat_axis=0, tiled=True)  7.54 us
    unnamed x26, local copies, waits for them, and re-layouts  6.58 us
    pallas_call x1, Pallas kernels, encoder(): pl.pallas_call(functools.partial(encoder_kernel, lanes), out_shape=(out,)...  3.49 us
  transfers between devices with their start and end apart: 38, of which 22 were waited for; matrix products, arithmetic and copies ran while one was open for 0% of the time, Pallas kernels for 12%

profile of v17, /device:TPU:0, one launch (start us, length us, event | category | flops | bytes accessed | tf_op | source)
XLA Modules:
  0.0 132.7 jit_solution(4066836903803054298)
XLA Ops:
  0.6 1.6 %copy.12 = bf16[1,128,2,2048]{3,1,2,0:T(8,128)(2,1)S(1)} copy(bf16[1,128,2,2048]{3,2,1,0:T(2,128)(2,1)} %param.19) | data formatting | bytes 2097152 | tf_op jit(solution)/shard_map/optimization_barrier | solution.py:643
  2.3 1.2 pack.1
  3.5 7.5 %all-to-all-start = ((bf16[16,256,128]{2,1,0:T(8,128)(2,1)}), bf16[16,256,128]{2,1,0:T(8,128)(2,1)}, u32[]{:S(2)}, u32[]{:S(2)}) async-start(bf16[16,256,128]{2,1,0:T(8,128)(2,1)} %pack.1), calls=%async_computation | async-start | bytes 2097152 | tf_op jit(solution)/shard_map/all_to_all | solution.py:641
  11.8 3.4 %copy-done = bf16[1184,3584]{1,0:T(8,128)(2,1)S(1)} copy-done((bf16[1184,3584]{1,0:T(8,128)(2,1)S(1)}, bf16[1184,3584]{1,0:T(8,128)(2,1)}, u32[]{:S(2)}) %copy-start) | copy-done | bytes 8486936
  15.2 3.5 %encoder.1 = (bf16[8,16,1792]{2,1,0:T(8,128)(2,1)S(1)}, bf16[8,16,1792]{2,1,0:T(8,128)(2,1)S(1)}, bf16[8,16,1792]{2,1,0:T(8,128)(2,1)S(1)}, bf16[8,16,1792]{2,1,0:T(8,128)(2,1)S(1)}) custom-call(s32[5]{0:T(128)S(1)} %stack.19.place_ref, bf16[1184,256]{1,0:T(8,128)(2,1)S(1)} %bitcast.24, bf16[1184,3584]{1,0:T(8,128)(2,1)S(1)} %copy-done), custom_call_target="tpu_custom_call" | custom-call | flops 2172649472 | bytes 10928128 | tf_op jit(solution)/shard_map/encoder/pallas_call | solution.py:84
  18.7 0.4 collective-permute-start
  19.3 1.3 collective-permute-done.refs_1_
  20.6 0.7 collective-permute-done.1.refs_3_
  21.5 1.9 %collective-permute-start.2 = (bf16[4,16,1792]{2,1,0:T(8,128)(2,1)S(1)}, bf16[4,16,1792]{2,1,0:T(8,128)(2,1)S(1)}, u32[]{:S(2)}, u32[]{:S(2)}) collective-permute-start(bf16[4,16,1792]{2,1,0:T(8,128)(2,1)S(1)} %get-tuple-element.128), channel_id=1, source_target_pairs={{0,2},{1,3},{2,0},{3,1},{4,6},{5,7},{6,4},{7,5},{8,10},{9,11},{10,... | collective-permute-start | bytes 688136 | tf_op jit(solution)/shard_map/ppermute | solution.py:28
  23.4 1.5 %collective-permute-start.3 = (bf16[4,16,1792]{2,1,0:T(8,128)(2,1)S(1)}, bf16[4,16,1792]{2,1,0:T(8,128)(2,1)S(1)}, u32[]{:S(2)}, u32[]{:S(2)}) collective-permute-start(bf16[4,16,1792]{2,1,0:T(8,128)(2,1)S(1)} %get-tuple-element.129), channel_id=1, source_target_pairs={{0,4},{1,5},{2,6},{3,7},{4,0},{5,1},{6,2},{7,3},{8,12},{9,13},{10,... | collective-permute-start | bytes 688136 | tf_op jit(solution)/shard_map/ppermute | solution.py:28
  24.9 0.7 split.1
  25.6 0.6 copy-done.6
  26.2 0.6 copy-done.7
  26.8 0.6 copy-done.8
  27.5 0.6 copy-done.9
  28.1 0.6 copy-done.11
  28.7 2.3 %collective-permute-done.2.refs_1_ = bf16[4,16,1792]{2,1,0:T(8,128)(2,1)S(1)} collective-permute-done((bf16[4,16,1792]{2,1,0:T(8,128)(2,1)S(1)}, bf16[4,16,1792]{2,1,0:T(8,128)(2,1)S(1)}, u32[]{:S(2)}, u32[]{:S(2)}) %collective-permute-start.2) | collective-permute-done | bytes 229408 | tf_op jit(solution)/shard_map/ppermute | solution.py:28
  31.0 4.9 %collective-permute-done.3.refs_3_ = bf16[4,16,1792]{2,1,0:T(8,128)(2,1)S(1)} collective-permute-done((bf16[4,16,1792]{2,1,0:T(8,128)(2,1)S(1)}, bf16[4,16,1792]{2,1,0:T(8,128)(2,1)S(1)}, u32[]{:S(2)}, u32[]{:S(2)}) %collective-permute-start.3) | collective-permute-done | bytes 229408 | tf_op jit(solution)/shard_map/ppermute | solution.py:28
  36.0 0.7 collective-permute-start.4
  36.7 1.5 %collective-permute-start.5 = (bf16[2,16,1792]{2,1,0:T(8,128)(2,1)S(1)}, bf16[2,16,1792]{2,1,0:T(8,128)(2,1)S(1)}, u32[]{:S(2)}, u32[]{:S(2)}) collective-permute-start(bf16[2,16,1792]{2,1,0:T(8,128)(2,1)S(1)} %get-tuple-element.139), channel_id=1, source_target_pairs={{0,2},{1,3},{2,0},{3,1},{4,6},{5,7},{6,4},{7,5},{8,10},{9,11},{10,... | collective-permute-start | bytes 344072 | tf_op jit(solution)/shard_map/ppermute | solution.py:28
  38.1 3.0 %collective-permute-start.6 = (bf16[2,128,128]{2,1,0:T(8,128)(2,1)S(1)}, bf16[2,128,128]{2,1,0:T(8,128)(2,1)S(1)}, u32[]{:S(2)}, u32[]{:S(2)}) collective-permute-start(bf16[2,128,128]{2,1,0:T(8,128)(2,1)S(1)} %get-tuple-element.140), channel_id=1, source_target_pairs={{0,8},{1,9},{2,10},{3,11},{4,12},{5,13},{6,14},{7,15},{8,0},{9,1},... | collective-permute-start | bytes 196616 | tf_op jit(solution)/shard_map/ppermute | solution.py:28
  41.1 2.4 %collective-permute-done.6.refs_4_.refs_0_ = bf16[2,128,128]{2,1,0:T(8,128)(2,1)S(1)} collective-permute-done((bf16[2,128,128]{2,1,0:T(8,128)(2,1)S(1)}, bf16[2,128,128]{2,1,0:T(8,128)(2,1)S(1)}, u32[]{:S(2)}, u32[]{:S(2)}) %collective-permute-start.6) | collective-permute-done | bytes 65568 | tf_op jit(solution)/shard_map/ppermute | solution.py:28
  43.7 0.5 collective-permute-start.14
  44.2 2.9 %collective-permute-start.7 = (bf16[2,2,16,1792]{3,2,1,0:T(8,128)(2,1)S(1)}, bf16[2,2,16,1792]{3,2,1,0:T(8,128)(2,1)S(1)}, u32[]{:S(2)}, u32[]{:S(2)}) collective-permute-start(bf16[2,2,16,1792]{3,2,1,0:T(8,128)(2,1)S(1)} %add_all.1.mine_ref), channel_id=1, source_target_pairs={{0,8},{1,9},{2,10},{3,11},{4,12},{5,13},{6,14},{7,15},{8,0},{9,1},... | collective-permute-start | bytes 688136 | tf_op jit(solution)/shard_map/ppermute | solution.py:28
  47.1 1.4 %collective-permute-start.8 = (bf16[2,128,128]{2,1,0:T(8,128)(2,1)}, bf16[2,128,128]{2,1,0:T(8,128)(2,1)S(1)}, u32[]{:S(2)}, u32[]{:S(2)}) collective-permute-start(bf16[2,128,128]{2,1,0:T(8,128)(2,1)} %copy-done.11), channel_id=1, source_target_pairs={{0,2},{1,3},{2,0},{3,1},{4,6},{5,7},{6,4},{7,5},{8,10},{9,11},{10,... | collective-permute-start | bytes 196616 | tf_op jit(solution)/shard_map/ppermute | solution.py:28
  48.6 3.0 %collective-permute-done.8.refs_1_ = bf16[2,128,128]{2,1,0:T(8,128)(2,1)S(1)} collective-permute-done((bf16[2,128,128]{2,1,0:T(8,128)(2,1)}, bf16[2,128,128]{2,1,0:T(8,128)(2,1)S(1)}, u32[]{:S(2)}, u32[]{:S(2)}) %collective-permute-start.8) | collective-permute-done | bytes 65568 | tf_op jit(solution)/shard_map/ppermute | solution.py:28
  51.6 2.2 %collective-permute-done.9.refs_2_ = bf16[2,128,128]{2,1,0:T(8,128)(2,1)S(1)} collective-permute-done((bf16[2,128,128]{2,1,0:T(8,128)(2,1)}, bf16[2,128,128]{2,1,0:T(8,128)(2,1)S(1)}, u32[]{:S(2)}, u32[]{:S(2)}) %collective-permute-start.9) | collective-permute-done | bytes 65568 | tf_op jit(solution)/shard_map/ppermute | solution.py:28
  53.7 3.2 %collective-permute-start.10 = (bf16[2,128,128]{2,1,0:T(8,128)(2,1)}, bf16[2,128,128]{2,1,0:T(8,128)(2,1)S(1)}, u32[]{:S(2)}, u32[]{:S(2)}) collective-permute-start(bf16[2,128,128]{2,1,0:T(8,128)(2,1)} %copy-done.9), channel_id=1, source_target_pairs={{0,6},{1,7},{2,4},{3,5},{4,2},{5,3},{6,0},{7,1},{8,14},{9,15},{10,... | collective-permute-start | bytes 196616 | tf_op jit(solution)/shard_map/ppermute | solution.py:28
  57.6 2.4 %collective-permute-done.10.refs_3_ = bf16[2,128,128]{2,1,0:T(8,128)(2,1)S(1)} collective-permute-done((bf16[2,128,128]{2,1,0:T(8,128)(2,1)}, bf16[2,128,128]{2,1,0:T(8,128)(2,1)S(1)}, u32[]{:S(2)}, u32[]{:S(2)}) %collective-permute-start.10) | collective-permute-done | bytes 65568 | tf_op jit(solution)/shard_map/ppermute | solution.py:28
  60.3 1.5 %collective-permute-start.11 = (bf16[32,1792]{1,0:T(8,128)(2,1)S(1)}, bf16[32,1792]{1,0:T(8,128)(2,1)S(1)}, u32[]{:S(2)}, u32[]{:S(2)}) collective-permute-start(bf16[32,1792]{1,0:T(8,128)(2,1)S(1)} %bitcast.28), channel_id=1, source_target_pairs={{0,4},{1,5},{2,6},{3,7},{4,0},{5,1},{6,2},{7,3},{8,12},{9,13},{10,... | collective-permute-start | bytes 344072 | tf_op jit(solution)/shard_map/ppermute | solution.py:28
  61.7 1.4 %collective-permute-start.12 = (bf16[32,1792]{1,0:T(8,128)(2,1)S(1)}, bf16[32,1792]{1,0:T(8,128)(2,1)S(1)}, u32[]{:S(2)}, u32[]{:S(2)}) collective-permute-start(bf16[32,1792]{1,0:T(8,128)(2,1)S(1)} %bitcast.30), channel_id=1, source_target_pairs={{0,2},{1,3},{2,0},{3,1},{4,6},{5,7},{6,4},{7,5},{8,10},{9,11},{10,... | collective-permute-start | bytes 344072 | tf_op jit(solution)/shard_map/ppermute | solution.py:28
  63.2 1.4 %collective-permute-start.13 = (bf16[2,128,128]{2,1,0:T(8,128)(2,1)}, bf16[2,128,128]{2,1,0:T(8,128)(2,1)S(1)}, u32[]{:S(2)}, u32[]{:S(2)}) collective-permute-start(bf16[2,128,128]{2,1,0:T(8,128)(2,1)} %copy-done.8), channel_id=1, source_target_pairs={{0,10},{1,11},{2,8},{3,9},{4,14},{5,15},{6,12},{7,13},{8,2},{9,3},... | collective-permute-start | bytes 196616 | tf_op jit(solution)/shard_map/ppermute | solution.py:28
  64.9 5.0 %collective-permute-done.13.refs_5_.refs_1_ = bf16[2,128,128]{2,1,0:T(8,128)(2,1)S(1)} collective-permute-done((bf16[2,128,128]{2,1,0:T(8,128)(2,1)}, bf16[2,128,128]{2,1,0:T(8,128)(2,1)S(1)}, u32[]{:S(2)}, u32[]{:S(2)}) %collective-permute-start.13) | collective-permute-done | bytes 65568 | tf_op jit(solution)/shard_map/ppermute | solution.py:28
  70.0 1.1 collective-permute-start.17
  71.0 2.2 %collective-permute-start.19 = (bf16[2,128,128]{2,1,0:T(8,128)(2,1)}, bf16[2,128,128]{2,1,0:T(8,128)(2,1)S(1)}, u32[]{:S(2)}, u32[]{:S(2)}) collective-permute-start(bf16[2,128,128]{2,1,0:T(8,128)(2,1)} %copy-done.7), channel_id=1, source_target_pairs={{0,12},{1,13},{2,14},{3,15},{4,8},{5,9},{6,10},{7,11},{8,4},{9,5},... | collective-permute-start | bytes 196616 | tf_op jit(solution)/shard_map/ppermute | solution.py:28
  73.2 2.1 %collective-permute-start.20 = (bf16[2,128,128]{2,1,0:T(8,128)(2,1)}, bf16[2,128,128]{2,1,0:T(8,128)(2,1)S(1)}, u32[]{:S(2)}, u32[]{:S(2)}) collective-permute-start(bf16[2,128,128]{2,1,0:T(8,128)(2,1)} %copy-done.6), channel_id=1, source_target_pairs={{0,14},{1,15},{2,12},{3,13},{4,10},{5,11},{6,8},{7,9},{8,6},{9,7},... | collective-permute-start | bytes 196616 | tf_op jit(solution)/shard_map/ppermute | solution.py:28
  75.3 3.9 %collective-permute-done.19.refs_6_.refs_2_ = bf16[2,128,128]{2,1,0:T(8,128)(2,1)S(1)} collective-permute-done((bf16[2,128,128]{2,1,0:T(8,128)(2,1)}, bf16[2,128,128]{2,1,0:T(8,128)(2,1)S(1)}, u32[]{:S(2)}, u32[]{:S(2)}) %collective-permute-start.19) | collective-permute-done | bytes 65568 | tf_op jit(solution)/shard_map/ppermute | solution.py:28
  79.2 1.7 %collective-permute-done.20.refs_7_.refs_3_ = bf16[2,128,128]{2,1,0:T(8,128)(2,1)S(1)} collective-permute-done((bf16[2,128,128]{2,1,0:T(8,128)(2,1)}, bf16[2,128,128]{2,1,0:T(8,128)(2,1)S(1)}, u32[]{:S(2)}, u32[]{:S(2)}) %collective-permute-start.20) | collective-permute-done | bytes 65568 | tf_op jit(solution)/shard_map/ppermute | solution.py:28
  80.9 2.3 %project.1 = (bf16[4,144,256]{2,1,0:T(8,128)(2,1)S(1)}, bf16[4,144,256]{2,1,0:T(8,128)(2,1)S(1)}, bf16[4,144,256]{2,1,0:T(8,128)(2,1)S(1)}, bf16[4,144,256]{2,1,0:T(8,128)(2,1)S(1)}) custom-call(s32[5]{0:T(128)S(1)} %stack.19.place_ref, bf16[64,1792]{1,0:T(8,128)(2,1)S(1)} %get-tuple-element.172.refs_0_, ...), custom_call_target="tpu_custom_call" | custom-call | flops 754974720 | bytes 7864320 | tf_op jit(solution)/shard_map/project/pallas_call | solution.py:206
  83.2 1.4 %collective-permute-start.21 = (bf16[4,144,256]{2,1,0:T(8,128)(2,1)S(1)}, bf16[4,144,256]{2,1,0:T(8,128)(2,1)S(1)}, u32[]{:S(2)}, u32[]{:S(2)}) collective-permute-start(bf16[4,144,256]{2,1,0:T(8,128)(2,1)S(1)} %get-tuple-element.182), channel_id=1, source_target_pairs={{0,2},{1,3},{2,0},{3,1},{4,6},{5,7},{6,4},{7,5},{8,10},{9,11},{10,... | collective-permute-start | bytes 884744 | tf_op jit(solution)/shard_map/ppermute | solution.py:28
  84.8 1.5 %collective-permute-done.23.refs_4_ = bf16[8,128,128]{2,1,0:T(8,128)(2,1)S(1)} collective-permute-done((bf16[8,128,128]{2,1,0:T(8,128)(2,1)S(1)}, bf16[8,128,128]{2,1,0:T(8,128)(2,1)S(1)}, u32[]{:S(2)}, u32[]{:S(2)}) %collective-permute-start.23) | collective-permute-done | bytes 262176 | tf_op jit(solution)/shard_map/ppermute | solution.py:28
  86.3 3.7 %collective-permute-done.21.refs_1_ = bf16[4,144,256]{2,1,0:T(8,128)(2,1)S(1)} collective-permute-done((bf16[4,144,256]{2,1,0:T(8,128)(2,1)S(1)}, bf16[4,144,256]{2,1,0:T(8,128)(2,1)S(1)}, u32[]{:S(2)}, u32[]{:S(2)}) %collective-permute-start.21) | collective-permute-done | bytes 294944 | tf_op jit(solution)/shard_map/ppermute | solution.py:28
  90.0 2.5 %collective-permute-done.22.refs_3_ = bf16[4,144,256]{2,1,0:T(8,128)(2,1)S(1)} collective-permute-done((bf16[4,144,256]{2,1,0:T(8,128)(2,1)S(1)}, bf16[4,144,256]{2,1,0:T(8,128)(2,1)S(1)}, u32[]{:S(2)}, u32[]{:S(2)}) %collective-permute-start.22) | collective-permute-done | bytes 294944 | tf_op jit(solution)/shard_map/ppermute | solution.py:28
  92.7 1.2 collective-permute-start.25
  93.9 4.8 %image_attention.2 = (f32[1024,256]{1,0:T(8,128)S(1)}, f32[1024,128]{1,0:T(8,128)S(1)}) custom-call(bf16[16,256,128]{2,1,0:T(8,128)(2,1)} %all-to-all-done.packed_ref, bf16[2,128,128]{2,1,0:T(8,128)(2,1)S(1)} %get-tuple-element.184.refs_0_, bf16[2,128,128]{2,1,0:T(8,128)(2,1)S(1)} %collective-permute-done.8.refs_1_, ...), custom_call_target="tpu_custom_call" | custom-call | flops 1073741824 | bytes 2359296 | tf_op jit(solution)/shard_map/image_attention/pallas_call | solution.py:387
  98.7 1.2 collective-permute-start.26
  100.0 5.0 %image_attention.3 = (f32[1024,256]{1,0:T(8,128)S(1)}, f32[1024,128]{1,0:T(8,128)S(1)}) custom-call(bf16[16,256,128]{2,1,0:T(8,128)(2,1)} %all-to-all-done.packed_ref, bf16[2,128,128]{2,1,0:T(8,128)(2,1)S(1)} %collective-permute-done.6.refs_4_.refs_0_, bf16[2,128,128]{2,1,0:T(8,128)(2,1)S(1)} %collective-permute-done.13.refs_5_.refs_1_, ...), custom_call_target="tpu_custom_call" | custom-call | flops 1073741824 | bytes 2359296 | tf_op jit(solution)/shard_map/image_attention/pallas_call | solution.py:387
  104.9 1.5 %collective-permute-done.26.refs_2_ = bf16[2,1,144,256]{3,2,1,0:T(8,128)(2,1)S(1)} collective-permute-done((bf16[2,1,144,256]{3,2,1,0:T(8,128)(2,1)S(1)}, bf16[2,1,144,256]{3,2,1,0:T(8,128)(2,1)S(1)}, u32[]{:S(2)}, u32[]{:S(2)}) %collective-permute-start.26) | collective-permute-done | bytes 147488 | tf_op jit(solution)/shard_map/ppermute | solution.py:28
  106.4 0.7 combine.1
  107.3 1.2 collective-permute-done.27.got_ref
  108.5 1.2 finish.3
  109.7 0.4 collective-permute-start.31
  110.1 3.0 %collective-permute-start.32 = (bf16[2,160,128]{2,1,0:T(8,128)(2,1)S(1)}, bf16[2,160,128]{2,1,0:T(8,128)(2,1)S(1)}, u32[]{:S(2)}, u32[]{:S(2)}) collective-permute-start(bf16[2,160,128]{2,1,0:T(8,128)(2,1)S(1)} %get-tuple-element.225), channel_id=1, source_target_pairs={{0,10},{1,11},{2,8},{3,9},{4,14},{5,15},{6,12},{7,13},{8,2},{9,3},... | collective-permute-start | bytes 245768 | tf_op jit(solution)/shard_map/ppermute | solution.py:28
  113.1 1.7 %collective-permute-start.33 = (bf16[2,160,128]{2,1,0:T(8,128)(2,1)S(1)}, bf16[2,160,128]{2,1,0:T(8,128)(2,1)S(1)}, u32[]{:S(2)}, u32[]{:S(2)}) collective-permute-start(bf16[2,160,128]{2,1,0:T(8,128)(2,1)S(1)} %get-tuple-element.226), channel_id=1, source_target_pairs={{0,12},{1,13},{2,14},{3,15},{4,8},{5,9},{6,10},{7,11},{8,4},{9,5},... | collective-permute-start | bytes 245768 | tf_op jit(solution)/shard_map/ppermute | solution.py:28
  114.7 2.7 %collective-permute-start.34 = (bf16[2,160,128]{2,1,0:T(8,128)(2,1)S(1)}, bf16[2,160,128]{2,1,0:T(8,128)(2,1)S(1)}, u32[]{:S(2)}, u32[]{:S(2)}) collective-permute-start(bf16[2,160,128]{2,1,0:T(8,128)(2,1)S(1)} %get-tuple-element.227), channel_id=1, source_target_pairs={{0,14},{1,15},{2,12},{3,13},{4,10},{5,11},{6,8},{7,9},{8,6},{9,7},... | collective-permute-start | bytes 245768 | tf_op jit(solution)/shard_map/ppermute | solution.py:28
  117.4 1.2 finish.2
  118.6 1.0 collective-permute-start.28
  119.6 2.5 %collective-permute-done.31.refs_0_.refs_4_ = bf16[2,160,128]{2,1,0:T(8,128)(2,1)S(1)} collective-permute-done((bf16[2,160,128]{2,1,0:T(8,128)(2,1)S(1)}, bf16[2,160,128]{2,1,0:T(8,128)(2,1)S(1)}, u32[]{:S(2)}, u32[]{:S(2)}) %collective-permute-start.31) | collective-permute-done | bytes 81952 | tf_op jit(solution)/shard_map/ppermute | solution.py:28
  122.2 2.2 %collective-permute-done.32.refs_1_.refs_5_ = bf16[2,160,128]{2,1,0:T(8,128)(2,1)S(1)} collective-permute-done((bf16[2,160,128]{2,1,0:T(8,128)(2,1)S(1)}, bf16[2,160,128]{2,1,0:T(8,128)(2,1)S(1)}, u32[]{:S(2)}, u32[]{:S(2)}) %collective-permute-start.32) | collective-permute-done | bytes 81952 | tf_op jit(solution)/shard_map/ppermute | solution.py:28
  124.7 0.4 collective-permute-done.28.refs_1_
  125.1 1.6 %collective-permute-done.29.refs_2_ = bf16[2,160,128]{2,1,0:T(8,128)(2,1)S(1)} collective-permute-done((bf16[2,160,128]{2,1,0:T(8,128)(2,1)S(1)}, bf16[2,160,128]{2,1,0:T(8,128)(2,1)S(1)}, u32[]{:S(2)}, u32[]{:S(2)}) %collective-permute-start.29) | collective-permute-done | bytes 81952 | tf_op jit(solution)/shard_map/ppermute | solution.py:28
  126.6 3.1 %collective-permute-done.30.refs_3_ = bf16[2,160,128]{2,1,0:T(8,128)(2,1)S(1)} collective-permute-done((bf16[2,160,128]{2,1,0:T(8,128)(2,1)S(1)}, bf16[2,160,128]{2,1,0:T(8,128)(2,1)S(1)}, u32[]{:S(2)}, u32[]{:S(2)}) %collective-permute-start.30) | collective-permute-done | bytes 81952 | tf_op jit(solution)/shard_map/ppermute | solution.py:28
  129.8 1.4 %collective-permute-done.35.refs_8_ = bf16[4,160,128]{2,1,0:T(8,128)(2,1)S(1)} collective-permute-done((bf16[4,160,128]{2,1,0:T(8,128)(2,1)S(1)}, bf16[4,160,128]{2,1,0:T(8,128)(2,1)S(1)}, u32[]{:S(2)}, u32[]{:S(2)}) %collective-permute-start.35) | collective-permute-done | bytes 163872 | tf_op jit(solution)/shard_map/ppermute | solution.py:28
  131.2 1.5 %unpack.1 = (bf16[128,2048]{1,0:T(8,128)(2,1)}, bf16[16,4096]{1,0:T(8,128)(2,1)}) custom-call(s32[5]{0:T(128)S(1)} %stack.19.place_ref, bf16[2,160,128]{2,1,0:T(8,128)(2,1)S(1)} %get-tuple-element.218.refs_0_, bf16[2,160,128]{2,1,0:T(8,128)(2,1)S(1)} %collective-permute-done.28.refs_1_, bf16[2,160,128]{2,1,0:T(8,128)(2,1)S(1)} %collective-permute-done.29.refs_2_, ...), custom_call_target="tpu_custom_call" | custom-call | tf_op jit(solution)/shard_map/unpack/pallas_call | solution.py:346
  (65 shorter events, 2.2 us)
Async XLA Ops:
  3.5 8.3 %copy-start.3 = (bf16[1,256,1184]{1,2,0:T(8,128)(2,1)S(1)}, bf16[1,256,1184]{1,2,0:T(8,128)(2,1)}, u32[]{:S(2)}) copy-start(bf16[1,256,1184]{1,2,0:T(8,128)(2,1)} %param.10) | copy-start | bytes 1818628
  3.5 40.1 %all-to-all-start = ((bf16[16,256,128]{2,1,0:T(8,128)(2,1)}), bf16[16,256,128]{2,1,0:T(8,128)(2,1)}, u32[]{:S(2)}, u32[]{:S(2)}) async-start(bf16[16,256,128]{2,1,0:T(8,128)(2,1)} %pack.1), calls=%async_computation | async-start | bytes 2097152 | tf_op jit(solution)/shard_map/all_to_all | solution.py:641
  11.8 3.4 %copy-start = (bf16[1184,3584]{1,0:T(8,128)(2,1)S(1)}, bf16[1184,3584]{1,0:T(8,128)(2,1)}, u32[]{:S(2)}) copy-start(bf16[1184,3584]{1,0:T(8,128)(2,1)} %weight_ref.1) | copy-start | bytes 25460740
  18.7 6.2 %copy-start.4 = (bf16[1,128,2048]{2,1,0:T(8,128)(2,1)S(1)}, bf16[1,128,2048]{2,1,0:T(8,128)(2,1)}, u32[]{:S(2)}) copy-start(bf16[1,128,2048]{2,1,0:T(8,128)(2,1)} %param.18) | copy-start | bytes 1572868
  18.7 1.9 %collective-permute-start = (bf16[8,16,1792]{2,1,0:T(8,128)(2,1)S(1)}, bf16[8,16,1792]{2,1,0:T(8,128)(2,1)S(1)}, u32[]{:S(2)}, u32[]{:S(2)}) collective-permute-start(bf16[8,16,1792]{2,1,0:T(8,128)(2,1)S(1)} %get-tuple-element.119), channel_id=1, source_target_pairs={{0,1},{1,0},{2,3},{3,2},{4,5},{5,4},{6,7},{7,6},{8,9},{9,8},{10,11... | collective-permute-start | bytes 1376264 | tf_op jit(solution)/shard_map/ppermute | solution.py:28
  19.1 2.1 %collective-permute-start.1 = (bf16[8,16,1792]{2,1,0:T(8,128)(2,1)S(1)}, bf16[8,16,1792]{2,1,0:T(8,128)(2,1)S(1)}, u32[]{:S(2)}, u32[]{:S(2)}) collective-permute-start(bf16[8,16,1792]{2,1,0:T(8,128)(2,1)S(1)} %get-tuple-element.121), channel_id=1, source_target_pairs={{0,1},{1,0},{2,3},{3,2},{4,5},{5,4},{6,7},{7,6},{8,9},{9,8},{10,11... | collective-permute-start | bytes 1376264 | tf_op jit(solution)/shard_map/ppermute | solution.py:28
  21.3 22.4 %copy-start.2 = (bf16[3584,192]{0,1:T(8,128)(2,1)S(1)}, bf16[3584,192]{0,1:T(8,128)(2,1)}, u32[]{:S(2)}) copy-start(bf16[3584,192]{0,1:T(8,128)(2,1)} %param.13) | copy-start | bytes 4128772
  21.5 22.1 %copy-start.1 = (bf16[192,4096]{1,0:T(8,128)(2,1)S(1)}, bf16[192,4096]{1,0:T(8,128)(2,1)}, u32[]{:S(2)}) copy-start(bf16[192,4096]{1,0:T(8,128)(2,1)} %refs_7_.1) | copy-start | bytes 4718596
  21.5 30.1 %copy-start.5 = (bf16[256,2,192]{0,2,1:T(8,128)(2,1)S(1)}, bf16[256,2,192]{0,2,1:T(8,128)(2,1)}, u32[]{:S(2)}) copy-start(bf16[256,2,192]{0,2,1:T(8,128)(2,1)} %param.14) | copy-start | bytes 589828
  21.5 36.1 %copy-start.12 = (bf16[3584]{0:T(1024)(128)(2,1)S(1)}, bf16[3584]{0:T(1024)(128)(2,1)}, u32[]{:S(2)}) copy-start(bf16[3584]{0:T(1024)(128)(2,1)} %param.12) | copy-start | bytes 21508
  21.5 9.5 %collective-permute-start.2 = (bf16[4,16,1792]{2,1,0:T(8,128)(2,1)S(1)}, bf16[4,16,1792]{2,1,0:T(8,128)(2,1)S(1)}, u32[]{:S(2)}, u32[]{:S(2)}) collective-permute-start(bf16[4,16,1792]{2,1,0:T(8,128)(2,1)S(1)} %get-tuple-element.128), channel_id=1, source_target_pairs={{0,2},{1,3},{2,0},{3,1},{4,6},{5,7},{6,4},{7,5},{8,10},{9,11},{10,... | collective-permute-start | bytes 688136 | tf_op jit(solution)/shard_map/ppermute | solution.py:28
  23.4 12.5 %collective-permute-start.3 = (bf16[4,16,1792]{2,1,0:T(8,128)(2,1)S(1)}, bf16[4,16,1792]{2,1,0:T(8,128)(2,1)S(1)}, u32[]{:S(2)}, u32[]{:S(2)}) collective-permute-start(bf16[4,16,1792]{2,1,0:T(8,128)(2,1)S(1)} %get-tuple-element.129), channel_id=1, source_target_pairs={{0,4},{1,5},{2,6},{3,7},{4,0},{5,1},{6,2},{7,3},{8,12},{9,13},{10,... | collective-permute-start | bytes 688136 | tf_op jit(solution)/shard_map/ppermute | solution.py:28
  25.6 0.6 copy-start.6
  26.2 0.6 copy-start.7
  26.8 0.6 copy-start.8
  27.5 0.6 copy-start.9
  28.1 0.6 copy-start.11
  28.7 14.8 %copy-start.10 = (bf16[2,128,128]{2,1,0:T(8,128)(2,1)}, bf16[2,128,128]{2,1,0:T(8,128)(2,1)S(1)}, u32[]{:S(2)}) copy-start(bf16[2,128,128]{2,1,0:T(8,128)(2,1)S(1)} %get-tuple-element.152) | copy-start | bytes 196612
  36.0 7.5 %collective-permute-start.4 = (bf16[2,16,1792]{2,1,0:T(8,128)(2,1)S(1)}, bf16[2,16,1792]{2,1,0:T(8,128)(2,1)S(1)}, u32[]{:S(2)}, u32[]{:S(2)}) collective-permute-start(bf16[2,16,1792]{2,1,0:T(8,128)(2,1)S(1)} %get-tuple-element.138), channel_id=1, source_target_pairs={{0,4},{1,5},{2,6},{3,7},{4,0},{5,1},{6,2},{7,3},{8,12},{9,13},{10,... | collective-permute-start | bytes 344072 | tf_op jit(solution)/shard_map/ppermute | solution.py:28
  36.7 6.8 %collective-permute-start.5 = (bf16[2,16,1792]{2,1,0:T(8,128)(2,1)S(1)}, bf16[2,16,1792]{2,1,0:T(8,128)(2,1)S(1)}, u32[]{:S(2)}, u32[]{:S(2)}) collective-permute-start(bf16[2,16,1792]{2,1,0:T(8,128)(2,1)S(1)} %get-tuple-element.139), channel_id=1, source_target_pairs={{0,2},{1,3},{2,0},{3,1},{4,6},{5,7},{6,4},{7,5},{8,10},{9,11},{10,... | collective-permute-start | bytes 344072 | tf_op jit(solution)/shard_map/ppermute | solution.py:28
  38.1 5.4 %collective-permute-start.6 = (bf16[2,128,128]{2,1,0:T(8,128)(2,1)S(1)}, bf16[2,128,128]{2,1,0:T(8,128)(2,1)S(1)}, u32[]{:S(2)}, u32[]{:S(2)}) collective-permute-start(bf16[2,128,128]{2,1,0:T(8,128)(2,1)S(1)} %get-tuple-element.140), channel_id=1, source_target_pairs={{0,8},{1,9},{2,10},{3,11},{4,12},{5,13},{6,14},{7,15},{8,0},{9,1},... | collective-permute-start | bytes 196616 | tf_op jit(solution)/shard_map/ppermute | solution.py:28
  43.6 26.3 %collective-permute-start.15 = (bf16[192,4096]{1,0:T(8,128)(2,1)S(1)}, bf16[192,4096]{1,0:T(8,128)(2,1)S(1)}, u32[]{:S(2)}, u32[]{:S(2)}) collective-permute-start(bf16[192,4096]{1,0:T(8,128)(2,1)S(1)} %copy-done.1), channel_id=1, source_target_pairs={{0,1},{1,0},{2,3},{3,2},{4,5},{5,4},{6,7},{7,6},{8,9},{9,8},{10,11... | collective-permute-start | bytes 4718600 | tf_op jit(solution)/shard_map/ppermute | solution.py:28
  43.7 26.2 %collective-permute-start.14 = (bf16[192,3584]{1,0:T(8,128)(2,1)S(1)}, bf16[192,3584]{1,0:T(8,128)(2,1)S(1)}, u32[]{:S(2)}, u32[]{:S(2)}) collective-permute-start(bf16[192,3584]{1,0:T(8,128)(2,1)S(1)} %bitcast.22), channel_id=1, source_target_pairs={{0,1},{1,0},{2,3},{3,2},{4,5},{5,4},{6,7},{7,6},{8,9},{9,8},{10,11... | collective-permute-start | bytes 4128776 | tf_op jit(solution)/shard_map/ppermute | solution.py:28
  44.2 15.9 %collective-permute-start.7 = (bf16[2,2,16,1792]{3,2,1,0:T(8,128)(2,1)S(1)}, bf16[2,2,16,1792]{3,2,1,0:T(8,128)(2,1)S(1)}, u32[]{:S(2)}, u32[]{:S(2)}) collective-permute-start(bf16[2,2,16,1792]{3,2,1,0:T(8,128)(2,1)S(1)} %add_all.1.mine_ref), channel_id=1, source_target_pairs={{0,8},{1,9},{2,10},{3,11},{4,12},{5,13},{6,14},{7,15},{8,0},{9,1},... | collective-permute-start | bytes 688136 | tf_op jit(solution)/shard_map/ppermute | solution.py:28
  47.1 4.5 %collective-permute-start.8 = (bf16[2,128,128]{2,1,0:T(8,128)(2,1)}, bf16[2,128,128]{2,1,0:T(8,128)(2,1)S(1)}, u32[]{:S(2)}, u32[]{:S(2)}) collective-permute-start(bf16[2,128,128]{2,1,0:T(8,128)(2,1)} %copy-done.11), channel_id=1, source_target_pairs={{0,2},{1,3},{2,0},{3,1},{4,6},{5,7},{6,4},{7,5},{8,10},{9,11},{10,... | collective-permute-start | bytes 196616 | tf_op jit(solution)/shard_map/ppermute | solution.py:28
  48.5 5.2 %collective-permute-start.9 = (bf16[2,128,128]{2,1,0:T(8,128)(2,1)}, bf16[2,128,128]{2,1,0:T(8,128)(2,1)S(1)}, u32[]{:S(2)}, u32[]{:S(2)}) collective-permute-start(bf16[2,128,128]{2,1,0:T(8,128)(2,1)} %copy-done.10), channel_id=1, source_target_pairs={{0,4},{1,5},{2,6},{3,7},{4,0},{5,1},{6,2},{7,3},{8,12},{9,13},{10,... | collective-permute-start | bytes 196616 | tf_op jit(solution)/shard_map/ppermute | solution.py:28
  51.5 11.7 %collective-permute-start.16 = (bf16[2,192,256]{2,1,0:T(8,128)(2,1)S(1)}, bf16[2,192,256]{2,1,0:T(8,128)(2,1)S(1)}, u32[]{:S(2)}, u32[]{:S(2)}) collective-permute-start(bf16[2,192,256]{2,1,0:T(8,128)(2,1)S(1)} %bitcast.26), channel_id=1, source_target_pairs={{0,1},{1,0},{2,3},{3,2},{4,5},{5,4},{6,7},{7,6},{8,9},{9,8},{10,11... | collective-permute-start | bytes 589832 | tf_op jit(solution)/shard_map/ppermute | solution.py:28
  53.7 6.4 %collective-permute-start.10 = (bf16[2,128,128]{2,1,0:T(8,128)(2,1)}, bf16[2,128,128]{2,1,0:T(8,128)(2,1)S(1)}, u32[]{:S(2)}, u32[]{:S(2)}) collective-permute-start(bf16[2,128,128]{2,1,0:T(8,128)(2,1)} %copy-done.9), channel_id=1, source_target_pairs={{0,6},{1,7},{2,4},{3,5},{4,2},{5,3},{6,0},{7,1},{8,14},{9,15},{10,... | collective-permute-start | bytes 196616 | tf_op jit(solution)/shard_map/ppermute | solution.py:28
  60.3 9.6 %collective-permute-start.11 = (bf16[32,1792]{1,0:T(8,128)(2,1)S(1)}, bf16[32,1792]{1,0:T(8,128)(2,1)S(1)}, u32[]{:S(2)}, u32[]{:S(2)}) collective-permute-start(bf16[32,1792]{1,0:T(8,128)(2,1)S(1)} %bitcast.28), channel_id=1, source_target_pairs={{0,4},{1,5},{2,6},{3,7},{4,0},{5,1},{6,2},{7,3},{8,12},{9,13},{10,... | collective-permute-start | bytes 344072 | tf_op jit(solution)/shard_map/ppermute | solution.py:28
  61.7 8.2 %collective-permute-start.12 = (bf16[32,1792]{1,0:T(8,128)(2,1)S(1)}, bf16[32,1792]{1,0:T(8,128)(2,1)S(1)}, u32[]{:S(2)}, u32[]{:S(2)}) collective-permute-start(bf16[32,1792]{1,0:T(8,128)(2,1)S(1)} %bitcast.30), channel_id=1, source_target_pairs={{0,2},{1,3},{2,0},{3,1},{4,6},{5,7},{6,4},{7,5},{8,10},{9,11},{10,... | collective-permute-start | bytes 344072 | tf_op jit(solution)/shard_map/ppermute | solution.py:28
  63.2 6.7 %collective-permute-start.13 = (bf16[2,128,128]{2,1,0:T(8,128)(2,1)}, bf16[2,128,128]{2,1,0:T(8,128)(2,1)S(1)}, u32[]{:S(2)}, u32[]{:S(2)}) collective-permute-start(bf16[2,128,128]{2,1,0:T(8,128)(2,1)} %copy-done.8), channel_id=1, source_target_pairs={{0,10},{1,11},{2,8},{3,9},{4,14},{5,15},{6,12},{7,13},{8,2},{9,3},... | collective-permute-start | bytes 196616 | tf_op jit(solution)/shard_map/ppermute | solution.py:28
  70.0 10.9 %collective-permute-start.17 = (bf16[64,1792]{1,0:T(8,128)(2,1)S(1)}, bf16[64,1792]{1,0:T(8,128)(2,1)S(1)}, u32[]{:S(2)}, u32[]{:S(2)}) collective-permute-start(bf16[64,1792]{1,0:T(8,128)(2,1)S(1)} %get-tuple-element.172.refs_0_), channel_id=1, source_target_pairs={{0,2},{1,3},{2,0},{3,1},{4,6},{5,7},{6,4},{7,5},{8,10},{9,11},{10,... | collective-permute-start | bytes 688136 | tf_op jit(solution)/shard_map/ppermute | solution.py:28
  71.0 9.9 %collective-permute-start.18 = (bf16[64,1792]{1,0:T(8,128)(2,1)S(1)}, bf16[64,1792]{1,0:T(8,128)(2,1)S(1)}, u32[]{:S(2)}, u32[]{:S(2)}) collective-permute-start(bf16[64,1792]{1,0:T(8,128)(2,1)S(1)} %get-tuple-element.173.refs_2_), channel_id=1, source_target_pairs={{0,4},{1,5},{2,6},{3,7},{4,0},{5,1},{6,2},{7,3},{8,12},{9,13},{10,... | collective-permute-start | bytes 688136 | tf_op jit(solution)/shard_map/ppermute | solution.py:28
  71.0 8.2 %collective-permute-start.19 = (bf16[2,128,128]{2,1,0:T(8,128)(2,1)}, bf16[2,128,128]{2,1,0:T(8,128)(2,1)S(1)}, u32[]{:S(2)}, u32[]{:S(2)}) collective-permute-start(bf16[2,128,128]{2,1,0:T(8,128)(2,1)} %copy-done.7), channel_id=1, source_target_pairs={{0,12},{1,13},{2,14},{3,15},{4,8},{5,9},{6,10},{7,11},{8,4},{9,5},... | collective-permute-start | bytes 196616 | tf_op jit(solution)/shard_map/ppermute | solution.py:28
  73.2 7.7 %collective-permute-start.20 = (bf16[2,128,128]{2,1,0:T(8,128)(2,1)}, bf16[2,128,128]{2,1,0:T(8,128)(2,1)S(1)}, u32[]{:S(2)}, u32[]{:S(2)}) collective-permute-start(bf16[2,128,128]{2,1,0:T(8,128)(2,1)} %copy-done.6), channel_id=1, source_target_pairs={{0,14},{1,15},{2,12},{3,13},{4,10},{5,11},{6,8},{7,9},{8,6},{9,7},... | collective-permute-start | bytes 196616 | tf_op jit(solution)/shard_map/ppermute | solution.py:28
  83.2 6.8 %collective-permute-start.21 = (bf16[4,144,256]{2,1,0:T(8,128)(2,1)S(1)}, bf16[4,144,256]{2,1,0:T(8,128)(2,1)S(1)}, u32[]{:S(2)}, u32[]{:S(2)}) collective-permute-start(bf16[4,144,256]{2,1,0:T(8,128)(2,1)S(1)} %get-tuple-element.182), channel_id=1, source_target_pairs={{0,2},{1,3},{2,0},{3,1},{4,6},{5,7},{6,4},{7,5},{8,10},{9,11},{10,... | collective-permute-start | bytes 884744 | tf_op jit(solution)/shard_map/ppermute | solution.py:28
  84.7 7.9 %collective-permute-start.22 = (bf16[4,144,256]{2,1,0:T(8,128)(2,1)S(1)}, bf16[4,144,256]{2,1,0:T(8,128)(2,1)S(1)}, u32[]{:S(2)}, u32[]{:S(2)}) collective-permute-start(bf16[4,144,256]{2,1,0:T(8,128)(2,1)S(1)} %get-tuple-element.183), channel_id=1, source_target_pairs={{0,4},{1,5},{2,6},{3,7},{4,0},{5,1},{6,2},{7,3},{8,12},{9,13},{10,... | collective-permute-start | bytes 884744 | tf_op jit(solution)/shard_map/ppermute | solution.py:28
  84.7 1.6 %collective-permute-start.23 = (bf16[8,128,128]{2,1,0:T(8,128)(2,1)S(1)}, bf16[8,128,128]{2,1,0:T(8,128)(2,1)S(1)}, u32[]{:S(2)}, u32[]{:S(2)}) collective-permute-start(bf16[8,128,128]{2,1,0:T(8,128)(2,1)S(1)} %gather_other.3), channel_id=1, source_target_pairs={{0,1},{1,0},{2,3},{3,2},{4,5},{5,4},{6,7},{7,6},{8,9},{9,8},{10,11... | collective-permute-start | bytes 786440 | tf_op jit(solution)/shard_map/ppermute | solution.py:28
  92.7 6.0 %collective-permute-start.24 = (bf16[2,144,256]{2,1,0:T(8,128)(2,1)S(1)}, bf16[2,144,256]{2,1,0:T(8,128)(2,1)S(1)}, u32[]{:S(2)}, u32[]{:S(2)}) collective-permute-start(bf16[2,144,256]{2,1,0:T(8,128)(2,1)S(1)} %get-tuple-element.195), channel_id=1, source_target_pairs={{0,4},{1,5},{2,6},{3,7},{4,0},{5,1},{6,2},{7,3},{8,12},{9,13},{10,... | collective-permute-start | bytes 442376 | tf_op jit(solution)/shard_map/ppermute | solution.py:28
  92.7 5.9 %collective-permute-start.25 = (bf16[2,144,256]{2,1,0:T(8,128)(2,1)S(1)}, bf16[2,144,256]{2,1,0:T(8,128)(2,1)S(1)}, u32[]{:S(2)}, u32[]{:S(2)}) collective-permute-start(bf16[2,144,256]{2,1,0:T(8,128)(2,1)S(1)} %get-tuple-element.196), channel_id=1, source_target_pairs={{0,2},{1,3},{2,0},{3,1},{4,6},{5,7},{6,4},{7,5},{8,10},{9,11},{10,... | collective-permute-start | bytes 442376 | tf_op jit(solution)/shard_map/ppermute | solution.py:28
  98.7 7.7 %collective-permute-start.26 = (bf16[2,1,144,256]{3,2,1,0:T(8,128)(2,1)S(1)}, bf16[2,1,144,256]{3,2,1,0:T(8,128)(2,1)S(1)}, u32[]{:S(2)}, u32[]{:S(2)}) collective-permute-start(bf16[2,1,144,256]{3,2,1,0:T(8,128)(2,1)S(1)} %get-tuple-element.211), channel_id=1, source_target_pairs={{0,8},{1,9},{2,10},{3,11},{4,12},{5,13},{6,14},{7,15},{8,0},{9,1},... | collective-permute-start | bytes 442376 | tf_op jit(solution)/shard_map/ppermute | solution.py:28
  107.2 1.3 collective-permute-start.27
  109.7 12.5 %collective-permute-start.31 = (bf16[2,160,128]{2,1,0:T(8,128)(2,1)S(1)}, bf16[2,160,128]{2,1,0:T(8,128)(2,1)S(1)}, u32[]{:S(2)}, u32[]{:S(2)}) collective-permute-start(bf16[2,160,128]{2,1,0:T(8,128)(2,1)S(1)} %get-tuple-element.224), channel_id=1, source_target_pairs={{0,8},{1,9},{2,10},{3,11},{4,12},{5,13},{6,14},{7,15},{8,0},{9,1},... | collective-permute-start | bytes 245768 | tf_op jit(solution)/shard_map/ppermute | solution.py:28
  110.1 14.3 %collective-permute-start.32 = (bf16[2,160,128]{2,1,0:T(8,128)(2,1)S(1)}, bf16[2,160,128]{2,1,0:T(8,128)(2,1)S(1)}, u32[]{:S(2)}, u32[]{:S(2)}) collective-permute-start(bf16[2,160,128]{2,1,0:T(8,128)(2,1)S(1)} %get-tuple-element.225), channel_id=1, source_target_pairs={{0,10},{1,11},{2,8},{3,9},{4,14},{5,15},{6,12},{7,13},{8,2},{9,3},... | collective-permute-start | bytes 245768 | tf_op jit(solution)/shard_map/ppermute | solution.py:28
  113.1 11.5 %collective-permute-start.33 = (bf16[2,160,128]{2,1,0:T(8,128)(2,1)S(1)}, bf16[2,160,128]{2,1,0:T(8,128)(2,1)S(1)}, u32[]{:S(2)}, u32[]{:S(2)}) collective-permute-start(bf16[2,160,128]{2,1,0:T(8,128)(2,1)S(1)} %get-tuple-element.226), channel_id=1, source_target_pairs={{0,12},{1,13},{2,14},{3,15},{4,8},{5,9},{6,10},{7,11},{8,4},{9,5},... | collective-permute-start | bytes 245768 | tf_op jit(solution)/shard_map/ppermute | solution.py:28
  114.7 9.9 %collective-permute-start.34 = (bf16[2,160,128]{2,1,0:T(8,128)(2,1)S(1)}, bf16[2,160,128]{2,1,0:T(8,128)(2,1)S(1)}, u32[]{:S(2)}, u32[]{:S(2)}) collective-permute-start(bf16[2,160,128]{2,1,0:T(8,128)(2,1)S(1)} %get-tuple-element.227), channel_id=1, source_target_pairs={{0,14},{1,15},{2,12},{3,13},{4,10},{5,11},{6,8},{7,9},{8,6},{9,7},... | collective-permute-start | bytes 245768 | tf_op jit(solution)/shard_map/ppermute | solution.py:28
  118.6 6.4 %collective-permute-start.28 = (bf16[2,160,128]{2,1,0:T(8,128)(2,1)S(1)}, bf16[2,160,128]{2,1,0:T(8,128)(2,1)S(1)}, u32[]{:S(2)}, u32[]{:S(2)}) collective-permute-start(bf16[2,160,128]{2,1,0:T(8,128)(2,1)S(1)} %get-tuple-element.219), channel_id=1, source_target_pairs={{0,2},{1,3},{2,0},{3,1},{4,6},{5,7},{6,4},{7,5},{8,10},{9,11},{10,... | collective-permute-start | bytes 245768 | tf_op jit(solution)/shard_map/ppermute | solution.py:28
  122.2 4.4 %collective-permute-start.29 = (bf16[2,160,128]{2,1,0:T(8,128)(2,1)S(1)}, bf16[2,160,128]{2,1,0:T(8,128)(2,1)S(1)}, u32[]{:S(2)}, u32[]{:S(2)}) collective-permute-start(bf16[2,160,128]{2,1,0:T(8,128)(2,1)S(1)} %get-tuple-element.220), channel_id=1, source_target_pairs={{0,4},{1,5},{2,6},{3,7},{4,0},{5,1},{6,2},{7,3},{8,12},{9,13},{10,... | collective-permute-start | bytes 245768 | tf_op jit(solution)/shard_map/ppermute | solution.py:28
  124.3 5.3 %collective-permute-start.30 = (bf16[2,160,128]{2,1,0:T(8,128)(2,1)S(1)}, bf16[2,160,128]{2,1,0:T(8,128)(2,1)S(1)}, u32[]{:S(2)}, u32[]{:S(2)}) collective-permute-start(bf16[2,160,128]{2,1,0:T(8,128)(2,1)S(1)} %get-tuple-element.221), channel_id=1, source_target_pairs={{0,6},{1,7},{2,4},{3,5},{4,2},{5,3},{6,0},{7,1},{8,14},{9,15},{10,... | collective-permute-start | bytes 245768 | tf_op jit(solution)/shard_map/ppermute | solution.py:28
  124.6 5.2 %collective-permute-start.36 = (bf16[4,160,128]{2,1,0:T(8,128)(2,1)S(1)}, bf16[4,160,128]{2,1,0:T(8,128)(2,1)S(1)}, u32[]{:S(2)}, u32[]{:S(2)}) collective-permute-start(bf16[4,160,128]{2,1,0:T(8,128)(2,1)S(1)} %gather_other.5), channel_id=1, source_target_pairs={{0,1},{1,0},{2,3},{3,2},{4,5},{5,4},{6,7},{7,6},{8,9},{9,8},{10,11... | collective-permute-start | bytes 491528 | tf_op jit(solution)/shard_map/ppermute | solution.py:28
  129.7 1.5 %collective-permute-start.35 = (bf16[4,160,128]{2,1,0:T(8,128)(2,1)S(1)}, bf16[4,160,128]{2,1,0:T(8,128)(2,1)S(1)}, u32[]{:S(2)}, u32[]{:S(2)}) collective-permute-start(bf16[4,160,128]{2,1,0:T(8,128)(2,1)S(1)} %gather_other.4), channel_id=1, source_target_pairs={{0,1},{1,0},{2,3},{3,2},{4,5},{5,4},{6,7},{7,6},{8,9},{9,8},{10,11... | collective-permute-start | bytes 491528 | tf_op jit(solution)/shard_map/ppermute | solution.py:28

commit v18 on v16

--- a/solution.py
+++ b/solution.py
@@ -298,7 +298,7 @@
     )(queries, keys, values)
 
 
-def unpack_kernel(copies, part_rows, place_ref, *refs):
+def unpack_kernel(copies, part_rows, masks, place_ref, *refs):
     *pieces, near_ref, far_ref, attended_ref, text_ref = refs
     me = 2 * place_ref[3] + place_ref[2]
     share = text_ref.shape[0]
@@ -307,7 +307,8 @@
     passed = [near_ref.at[at] for at in range(count)] + [far_ref.at[at] for at in range(count)]
     blocks = [block for piece, other in zip(pieces, passed) for block in (piece.at[0], other)]
     for at, block_ref in enumerate(blocks):
-        head, copy = (me ^ at) // copies, (me ^ at) % copies
+        device = me ^ (2 * masks[at // 2] + at % 2)
+        head, copy = device // copies, device % copies
         start = pl.multiple_of(head * HEAD_DIM, HEAD_DIM)
         rows = pl.ds(pl.multiple_of(copy * part_rows, part_rows), part_rows)
         attended_ref[rows, pl.ds(start, HEAD_DIM)] = block_ref[:part_rows, :]
@@ -317,10 +318,10 @@
         text_ref[:, pl.ds(start, HEAD_DIM)] = block[share:].astype(text_ref.dtype)
 
 
-def unpack(copies, part_rows, place, pieces, near, far):
+def unpack(copies, part_rows, masks, place, pieces, near, far):
     share = (near.shape[1] - part_rows) // 2
     return pl.pallas_call(
-        functools.partial(unpack_kernel, copies, part_rows),
+        functools.partial(unpack_kernel, copies, part_rows, masks),
         out_shape=(
             jax.ShapeDtypeStruct((part_rows * copies, HEADS * HEAD_DIM), jnp.bfloat16),
             jax.ShapeDtypeStruct((share, 2 * HEADS * HEAD_DIM), jnp.bfloat16),
@@ -332,7 +333,7 @@
     )(place, *pieces, near, far)
 
 
-def image_kernel(factor, call, img_dev, place_ref, packed_ref, sum_ref, top_ref, keys_ref, wide_ref):
+def image_kernel(factor, masks, img_dev, place_ref, packed_ref, sum_ref, top_ref, keys_ref, wide_ref):
     me = 2 * place_ref[3] + place_ref[2]
     wide_ref[:, HEAD_DIM:] = jnp.ones((wide_ref.shape[0], HEAD_DIM), wide_ref.dtype)
     for device in range(packed_ref.shape[0]):
@@ -345,8 +346,10 @@
     count = sum_ref.shape[0]
     for start in range(0, count, rows):
         span = slice(start, start + rows)
-        at = (call * count + start) // rows * group
-        queries = [packed_ref[me ^ (at + i), 2 * img_dev :, :] for i in range(group)]
+        at = start // rows * group
+        queries = [
+            packed_ref[me ^ (2 * masks[i // 2] + i % 2), 2 * img_dev :, :] for i in range(at, at + group)
+        ]
         queries = jnp.concatenate(queries, 0)
         scores = lax.dot_general(queries, keys_ref[...], contract, preferred_element_type=jnp.float32)
         scores = scores * factor
@@ -356,11 +359,11 @@
         top_ref[span, :] = jnp.broadcast_to(top, (rows, HEAD_DIM))
 
 
-def image_attention(place, packed, img_dev, factor, call, calls):
-    count = packed.shape[0] * (packed.shape[1] - 2 * img_dev) // calls
+def image_attention(place, packed, img_dev, factor, masks):
+    count = 2 * len(masks) * (packed.shape[1] - 2 * img_dev)
     total = packed.shape[0] * img_dev
     return pl.pallas_call(
-        functools.partial(image_kernel, factor, call, img_dev),
+        functools.partial(image_kernel, factor, masks, img_dev),
         out_shape=(
             jax.ShapeDtypeStruct((count, 2 * HEAD_DIM), jnp.float32),
             jax.ShapeDtypeStruct((count, HEAD_DIM), jnp.float32),
@@ -381,7 +384,13 @@
     )(place, packed)
 
 
-def finish_kernel(factor, first, img_dev, place_ref, packed_ref, sum_ref, top_ref, mine_ref, got_ref, *refs):
+def send_order(chips):
+    half = chips // 2
+    turns = [mask for at in range(half) for mask in (half + at, half - 1 - at)]
+    return turns[:half], turns[half:]
+
+
+def finish_kernel(factor, masks, img_dev, place_ref, packed_ref, sum_ref, top_ref, mine_ref, got_ref, *refs):
     *outs, text_ref = refs
     core, valid = place_ref[2], place_ref[4]
     me = 2 * place_ref[3] + core
@@ -400,7 +409,8 @@
     for step in range(2 * len(outs) // group):
         span = slice(step * rows, (step + 1) * rows)
         queries = [
-            packed_ref[me ^ (2 * first + step * group + at), 2 * img_dev :, :] for at in range(group)
+            packed_ref[me ^ (2 * masks[at // 2] + at % 2), 2 * img_dev :, :]
+            for at in range(step * group, (step + 1) * group)
         ]
         queries = jnp.concatenate(queries, 0)
         scores = lax.dot_general(queries, keys, contract, preferred_element_type=jnp.float32)
@@ -421,20 +431,20 @@
     text_ref[half:, :] = jnp.where(core == 0, high, low)
     share = (outs[0].shape[1] - part_rows) // 2
     for to in range(2 * len(outs)):
-        start = pl.multiple_of((me ^ (2 * first + to)) * share, share)
+        start = pl.multiple_of((me ^ (2 * masks[to // 2] + to % 2)) * share, share)
         block = text_ref[pl.ds(start, share), :]
         block = jnp.concatenate([block[:, :HEAD_DIM], block[:, HEAD_DIM:]], 0)
         outs[to // 2][to % 2, part_rows:, :] = block.astype(jnp.bfloat16)
 
 
-def finish(place, first, packed, image, mine, got, img_dev, factor):
+def finish(place, masks, packed, image, mine, got, img_dev, factor):
     devices, part_rows = packed.shape[0], packed.shape[1] - 2 * img_dev
     half = mine.shape[0]
     count = image[0].shape[0]
     outs = count // part_rows // 2
     out = jax.ShapeDtypeStruct((2, part_rows + 4 * half // devices, HEAD_DIM), jnp.bfloat16)
     return pl.pallas_call(
-        functools.partial(finish_kernel, factor, first, img_dev),
+        functools.partial(finish_kernel, factor, masks, img_dev),
         out_shape=(out,) * outs,
         in_specs=[SMEM_SPEC] + [VMEM_SPEC] * 5,
         out_specs=(VMEM_SPEC,) * outs,
@@ -610,6 +620,7 @@
     time = time_embedding(timesteps)
 
     rounds = len(lanes[0])
+    turns = send_order(chips)
     tie = lax.optimization_barrier
 
     def exchange(rows):
@@ -635,7 +646,7 @@
     for step in reversed(range(rounds - 1)):
         if step == 0:
             states, packed = tie((states, packed))
-            image = image_attention(place, packed, img_dev, factor, 0, 2)
+            image = image_attention(place, packed, img_dev, factor, turns[0])
         got = [swap(state, 2 * order[step]) for state, order in zip(states, lanes)]
         if step == rounds - 2:
             lines = modulation(time, mod0, mod1)
@@ -651,7 +662,7 @@
     for step in range(rounds - 1):
         if step == 0:
             sent, packed = tie((sent, packed))
-            image = image_attention(place, packed, img_dev, factor, 1, 2)
+            image = image_attention(place, packed, img_dev, factor, turns[1])
         got = [swap(part, 2 * order[step]) for part, order in zip(sent, lanes)]
         if step == 0:
             got, image = tie((got, image))
@@ -662,18 +673,14 @@
     mine, sent = combine(place, parts, chips, text_len // 2, model_width)
     got = swap(sent, 1)
 
-    pieces = [None] * chips
-    passed = [None] * 2
-    for call in (1, 0):
-        first = call * chips // 2
+    pieces, passed = [], []
+    for call, masks in enumerate(turns):
         image = images[2 * call : 2 * call + 2]
-        blocks = finish(place, first, packed, image, mine, got, img_dev, factor)
-        for at, block in enumerate(blocks):
-            mask = first + at
-            pieces[mask] = swap(block, 2 * mask) if mask else block
+        blocks = finish(place, masks, packed, image, mine, got, img_dev, factor)
+        pieces += [swap(block, 2 * mask) if mask else block for mask, block in zip(masks, blocks)]
     for call in range(2):
-        passed[call] = swap(gather_other(pieces[call * chips // 2 : (call + 1) * chips // 2]), 1)
-    attended, text_kv = unpack(copies, part_rows, place, pieces, *passed)
+        passed.append(swap(gather_other(pieces[call * chips // 2 : (call + 1) * chips // 2]), 1))
+    attended, text_kv = unpack(copies, part_rows, turns[0] + turns[1], place, pieces, *passed)
     return (attended[None], text_kv)
 
 

time: 130 us -> 128 us (0.985)
  waiting for transfers between devices: 65.9 us -> 60.7 us
  starting transfers between devices: 33.9 us -> 36.8 us
    ppermute x29, waiting for transfers between devices: 65.9 us -> 60.7 us  [swap(): return lax.ppermute(value, 'seq', [(i, i ^ mask) for i in range(devices)])]
    ppermute x29, starting transfers between devices: 26.4 us -> 29.3 us  [swap(): return lax.ppermute(value, 'seq', [(i, i ^ mask) for i in range(devices)])]
  transfers between devices with their start and end apart: 30 -> 30, of which waited for: 22 -> 20; matrix products, arithmetic and copies ran while one was open for 0% -> 0% of each run, Pallas kernels for 10% -> 10%
where the time goes in v18:
time: 128 us
  waiting for transfers between devices  60.7 us (47%)
  starting transfers between devices  36.8 us (29%)
  Pallas kernels  20.8 us (16%)
  local copies, waits for them, and re-layouts  7.06 us (6%)
  between operations  2.25 us (2%)
    ppermute x29, waiting for transfers between devices, swap(): return lax.ppermute(value, 'seq', [(i, i ^ mask) for i in range(devices)])  60.7 us
    ppermute x29, starting transfers between devices, swap(): return lax.ppermute(value, 'seq', [(i, i ^ mask) for i in range(devices)])  29.3 us
    pallas_call x2, Pallas kernels, image_attention(): pl.pallas_call(functools.partial(image_kernel, factor, masks, img_dev), o...  8.03 us
    all_to_all x1, starting transfers between devices, exchange(): return lax.all_to_all(rows, 'seq', split_axis=0, concat_axis=0, tiled=True)  7.49 us
    unnamed x14, local copies, waits for them, and re-layouts  5.31 us
    pallas_call x1, Pallas kernels, encoder(): pl.pallas_call(functools.partial(encoder_kernel, lanes), out_shape=(out,)...  3.47 us
  transfers between devices with their start and end apart: 30, of which 20 were waited for; matrix products, arithmetic and copies ran while one was open for 0% of the time, Pallas kernels for 10%

profile of v18, /device:TPU:0, one launch (start us, length us, event | category | flops | bytes accessed | tf_op | source)
XLA Modules:
  0.0 127.8 jit_solution(9240740854653690538)
XLA Ops:
  0.6 1.6 %copy.12 = bf16[1,128,2,2048]{3,1,2,0:T(8,128)(2,1)S(1)} copy(bf16[1,128,2,2048]{3,2,1,0:T(2,128)(2,1)} %param.19) | data formatting | bytes 2097152 | tf_op jit(solution)/shard_map/optimization_barrier | solution.py:629
  2.3 1.0 copy-done.4
  3.3 1.4 %pack.1 = bf16[16,384,128]{2,1,0:T(8,128)(2,1)} custom-call(bf16[128,2048]{1,0:T(8,128)(2,1)S(1)} %bitcast.25, bf16[128,2048]{1,0:T(8,128)(2,1)S(1)} %get-tuple-element.147.keys_ref, bf16[128,2048]{1,0:T(8,128)(2,1)S(1)} %get-tuple-element.146.values_ref), custom_call_target="tpu_custom_call" | custom-call | bytes 3145728 | tf_op jit(solution)/shard_map/pack/pallas_call | solution.py:288
  4.7 7.5 %all-to-all-start = ((bf16[16,384,128]{2,1,0:T(8,128)(2,1)}), bf16[16,384,128]{2,1,0:T(8,128)(2,1)S(1)}, u32[]{:S(2)}, u32[]{:S(2)}) async-start(bf16[16,384,128]{2,1,0:T(8,128)(2,1)} %pack.1), calls=%async_computation | async-start | bytes 3145728 | tf_op jit(solution)/shard_map/all_to_all | solution.py:627
  12.9 0.1 stack.19.place_ref
  13.0 3.4 %copy-done = bf16[1184,3584]{1,0:T(8,128)(2,1)S(1)} copy-done((bf16[1184,3584]{1,0:T(8,128)(2,1)S(1)}, bf16[1184,3584]{1,0:T(8,128)(2,1)}, u32[]{:S(2)}) %copy-start) | copy-done | bytes 8486936
  16.4 3.5 %encoder.1 = (bf16[8,16,1792]{2,1,0:T(8,128)(2,1)S(1)}, bf16[8,16,1792]{2,1,0:T(8,128)(2,1)S(1)}, bf16[8,16,1792]{2,1,0:T(8,128)(2,1)S(1)}, bf16[8,16,1792]{2,1,0:T(8,128)(2,1)S(1)}) custom-call(s32[5]{0:T(128)S(1)} %stack.19.place_ref, bf16[1184,256]{1,0:T(8,128)(2,1)S(1)} %bitcast.24, bf16[1184,3584]{1,0:T(8,128)(2,1)S(1)} %copy-done), custom_call_target="tpu_custom_call" | custom-call | flops 2172649472 | bytes 10928128 | tf_op jit(solution)/shard_map/encoder/pallas_call | solution.py:84
  19.8 0.5 collective-permute-start
  20.3 0.1 collective-permute-start.1
  20.4 1.3 %collective-permute-done.refs_1_ = bf16[8,16,1792]{2,1,0:T(8,128)(2,1)S(1)} collective-permute-done((bf16[8,16,1792]{2,1,0:T(8,128)(2,1)S(1)}, bf16[8,16,1792]{2,1,0:T(8,128)(2,1)S(1)}, u32[]{:S(2)}, u32[]{:S(2)}) %collective-permute-start) | collective-permute-done | bytes 458784 | tf_op jit(solution)/shard_map/ppermute | solution.py:28
  21.7 0.7 collective-permute-done.1.refs_3_
  22.4 0.2 add_halves.4
  22.6 2.0 %collective-permute-start.2 = (bf16[4,16,1792]{2,1,0:T(8,128)(2,1)S(1)}, bf16[4,16,1792]{2,1,0:T(8,128)(2,1)S(1)}, u32[]{:S(2)}, u32[]{:S(2)}) collective-permute-start(bf16[4,16,1792]{2,1,0:T(8,128)(2,1)S(1)} %get-tuple-element.82), channel_id=1, source_target_pairs={{0,2},{1,3},{2,0},{3,1},{4,6},{5,7},{6,4},{7,5},{8,10},{9,11},{10,... | collective-permute-start | bytes 688136 | tf_op jit(solution)/shard_map/ppermute | solution.py:28
  24.6 1.5 %collective-permute-start.3 = (bf16[4,16,1792]{2,1,0:T(8,128)(2,1)S(1)}, bf16[4,16,1792]{2,1,0:T(8,128)(2,1)S(1)}, u32[]{:S(2)}, u32[]{:S(2)}) collective-permute-start(bf16[4,16,1792]{2,1,0:T(8,128)(2,1)S(1)} %get-tuple-element.84), channel_id=1, source_target_pairs={{0,4},{1,5},{2,6},{3,7},{4,0},{5,1},{6,2},{7,3},{8,12},{9,13},{10,... | collective-permute-start | bytes 688136 | tf_op jit(solution)/shard_map/ppermute | solution.py:28
  26.0 10.1 %collective-permute-done.2.refs_1_ = bf16[4,16,1792]{2,1,0:T(8,128)(2,1)S(1)} collective-permute-done((bf16[4,16,1792]{2,1,0:T(8,128)(2,1)S(1)}, bf16[4,16,1792]{2,1,0:T(8,128)(2,1)S(1)}, u32[]{:S(2)}, u32[]{:S(2)}) %collective-permute-start.2) | collective-permute-done | bytes 229408 | tf_op jit(solution)/shard_map/ppermute | solution.py:28
  36.1 7.6 %collective-permute-done.3.refs_3_ = bf16[4,16,1792]{2,1,0:T(8,128)(2,1)S(1)} collective-permute-done((bf16[4,16,1792]{2,1,0:T(8,128)(2,1)S(1)}, bf16[4,16,1792]{2,1,0:T(8,128)(2,1)S(1)}, u32[]{:S(2)}, u32[]{:S(2)}) %collective-permute-start.3) | collective-permute-done | bytes 229408 | tf_op jit(solution)/shard_map/ppermute | solution.py:28
  43.7 0.1 add_halves.5
  43.7 2.5 %collective-permute-start.4 = (bf16[2,16,1792]{2,1,0:T(8,128)(2,1)S(1)}, bf16[2,16,1792]{2,1,0:T(8,128)(2,1)S(1)}, u32[]{:S(2)}, u32[]{:S(2)}) collective-permute-start(bf16[2,16,1792]{2,1,0:T(8,128)(2,1)S(1)} %get-tuple-element.86), channel_id=1, source_target_pairs={{0,4},{1,5},{2,6},{3,7},{4,0},{5,1},{6,2},{7,3},{8,12},{9,13},{10,... | collective-permute-start | bytes 344072 | tf_op jit(solution)/shard_map/ppermute | solution.py:28
  46.3 1.7 %collective-permute-start.5 = (bf16[2,16,1792]{2,1,0:T(8,128)(2,1)S(1)}, bf16[2,16,1792]{2,1,0:T(8,128)(2,1)S(1)}, u32[]{:S(2)}, u32[]{:S(2)}) collective-permute-start(bf16[2,16,1792]{2,1,0:T(8,128)(2,1)S(1)} %get-tuple-element.88), channel_id=1, source_target_pairs={{0,2},{1,3},{2,0},{3,1},{4,6},{5,7},{6,4},{7,5},{8,10},{9,11},{10,... | collective-permute-start | bytes 344072 | tf_op jit(solution)/shard_map/ppermute | solution.py:28
  48.0 1.5 %collective-permute-done.4.got0 = bf16[2,16,1792]{2,1,0:T(8,128)(2,1)S(1)} collective-permute-done((bf16[2,16,1792]{2,1,0:T(8,128)(2,1)S(1)}, bf16[2,16,1792]{2,1,0:T(8,128)(2,1)S(1)}, u32[]{:S(2)}, u32[]{:S(2)}) %collective-permute-start.4) | collective-permute-done | bytes 114720 | tf_op jit(solution)/shard_map/ppermute | solution.py:28
  49.5 1.6 %collective-permute-done.5.got1 = bf16[2,16,1792]{2,1,0:T(8,128)(2,1)S(1)} collective-permute-done((bf16[2,16,1792]{2,1,0:T(8,128)(2,1)S(1)}, bf16[2,16,1792]{2,1,0:T(8,128)(2,1)S(1)}, u32[]{:S(2)}, u32[]{:S(2)}) %collective-permute-start.5) | collective-permute-done | bytes 114720 | tf_op jit(solution)/shard_map/ppermute | solution.py:28
  51.1 0.1 collective-permute-start.10
  51.2 0.5 collective-permute-start.9
  51.7 2.9 %collective-permute-start.6 = (bf16[2,2,16,1792]{3,2,1,0:T(8,128)(2,1)S(1)}, bf16[2,2,16,1792]{3,2,1,0:T(8,128)(2,1)S(1)}, u32[]{:S(2)}, u32[]{:S(2)}) collective-permute-start(bf16[2,2,16,1792]{3,2,1,0:T(8,128)(2,1)S(1)} %add_all.1.mine_ref), channel_id=1, source_target_pairs={{0,8},{1,9},{2,10},{3,11},{4,12},{5,13},{6,14},{7,15},{8,0},{9,1},... | collective-permute-start | bytes 688136 | tf_op jit(solution)/shard_map/ppermute | solution.py:28
  55.3 0.1 collective-permute-start.11
  55.3 10.0 %collective-permute-done.6.got_ref = bf16[2,2,16,1792]{3,2,1,0:T(8,128)(2,1)S(1)} collective-permute-done((bf16[2,2,16,1792]{3,2,1,0:T(8,128)(2,1)S(1)}, bf16[2,2,16,1792]{3,2,1,0:T(8,128)(2,1)S(1)}, u32[]{:S(2)}, u32[]{:S(2)}) %collective-permute-start.6) | collective-permute-done | bytes 229408 | tf_op jit(solution)/shard_map/ppermute | solution.py:28
  65.3 0.2 normalize.1
  65.5 1.6 %collective-permute-start.8 = (bf16[32,1792]{1,0:T(8,128)(2,1)S(1)}, bf16[32,1792]{1,0:T(8,128)(2,1)S(1)}, u32[]{:S(2)}, u32[]{:S(2)}) collective-permute-start(bf16[32,1792]{1,0:T(8,128)(2,1)S(1)} %bitcast.30), channel_id=1, source_target_pairs={{0,2},{1,3},{2,0},{3,1},{4,6},{5,7},{6,4},{7,5},{8,10},{9,11},{10,... | collective-permute-start | bytes 344072 | tf_op jit(solution)/shard_map/ppermute | solution.py:28
  67.2 0.9 copy-done.5
  68.1 0.2 modulation.1.refs_4_
  68.3 2.1 %collective-permute-done.8.got1 = bf16[32,1792]{1,0:T(8,128)(2,1)S(1)} collective-permute-done((bf16[32,1792]{1,0:T(8,128)(2,1)S(1)}, bf16[32,1792]{1,0:T(8,128)(2,1)S(1)}, u32[]{:S(2)}, u32[]{:S(2)}) %collective-permute-start.8) | collective-permute-done | bytes 114720 | tf_op jit(solution)/shard_map/ppermute | solution.py:28
  70.4 1.5 %collective-permute-done.7.got0 = bf16[32,1792]{1,0:T(8,128)(2,1)S(1)} collective-permute-done((bf16[32,1792]{1,0:T(8,128)(2,1)S(1)}, bf16[32,1792]{1,0:T(8,128)(2,1)S(1)}, u32[]{:S(2)}, u32[]{:S(2)}) %collective-permute-start.7) | collective-permute-done | bytes 114720 | tf_op jit(solution)/shard_map/ppermute | solution.py:28
  71.9 0.6 collective-permute-start.12
  72.5 0.4 collective-permute-start.13
  72.9 3.9 %image_attention.2 = (f32[1024,256]{1,0:T(8,128)S(1)}, f32[1024,128]{1,0:T(8,128)S(1)}) custom-call(s32[5]{0:T(128)S(1)} %stack.19.place_ref, bf16[16,384,128]{2,1,0:T(8,128)(2,1)S(1)} %all-to-all-done.packed_ref), custom_call_target="tpu_custom_call" | custom-call | flops 1073741824 | bytes 2359296 | tf_op jit(solution)/shard_map/image_attention/pallas_call | solution.py:365
  76.8 1.2 collective-permute-done.12.refs_1_
  78.0 0.5 collective-permute-done.13.refs_3_
  78.6 2.3 %project.1 = (bf16[4,144,256]{2,1,0:T(8,128)(2,1)S(1)}, bf16[4,144,256]{2,1,0:T(8,128)(2,1)S(1)}, bf16[4,144,256]{2,1,0:T(8,128)(2,1)S(1)}, bf16[4,144,256]{2,1,0:T(8,128)(2,1)S(1)}) custom-call(s32[5]{0:T(128)S(1)} %stack.19.place_ref, bf16[64,1792]{1,0:T(8,128)(2,1)S(1)} %get-tuple-element.102.refs_0_, ...), custom_call_target="tpu_custom_call" | custom-call | flops 754974720 | bytes 7864320 | tf_op jit(solution)/shard_map/project/pallas_call | solution.py:206
  80.9 1.6 %collective-permute-start.14 = (bf16[4,144,256]{2,1,0:T(8,128)(2,1)S(1)}, bf16[4,144,256]{2,1,0:T(8,128)(2,1)S(1)}, u32[]{:S(2)}, u32[]{:S(2)}) collective-permute-start(bf16[4,144,256]{2,1,0:T(8,128)(2,1)S(1)} %get-tuple-element.118), channel_id=1, source_target_pairs={{0,2},{1,3},{2,0},{3,1},{4,6},{5,7},{6,4},{7,5},{8,10},{9,11},{10,... | collective-permute-start | bytes 884744 | tf_op jit(solution)/shard_map/ppermute | solution.py:28
  82.5 0.1 collective-permute-start.15
  82.5 4.1 %image_attention.3 = (f32[1024,256]{1,0:T(8,128)S(1)}, f32[1024,128]{1,0:T(8,128)S(1)}) custom-call(s32[5]{0:T(128)S(1)} %stack.19.place_ref, bf16[16,384,128]{2,1,0:T(8,128)(2,1)S(1)} %all-to-all-done.packed_ref), custom_call_target="tpu_custom_call" | custom-call | flops 1073741824 | bytes 2359296 | tf_op jit(solution)/shard_map/image_attention/pallas_call | solution.py:365
  86.7 1.0 collective-permute-done.14.refs_1_
  87.7 2.8 %collective-permute-done.15.refs_3_ = bf16[4,144,256]{2,1,0:T(8,128)(2,1)S(1)} collective-permute-done((bf16[4,144,256]{2,1,0:T(8,128)(2,1)S(1)}, bf16[4,144,256]{2,1,0:T(8,128)(2,1)S(1)}, u32[]{:S(2)}, u32[]{:S(2)}) %collective-permute-start.15) | collective-permute-done | bytes 294944 | tf_op jit(solution)/shard_map/ppermute | solution.py:28
  90.5 0.1 add_halves.6
  90.6 0.1 collective-permute-start.16
  90.7 0.6 collective-permute-start.17
  91.3 6.1 %collective-permute-done.16.refs_1_ = bf16[2,144,256]{2,1,0:T(8,128)(2,1)S(1)} collective-permute-done((bf16[2,144,256]{2,1,0:T(8,128)(2,1)S(1)}, bf16[2,144,256]{2,1,0:T(8,128)(2,1)S(1)}, u32[]{:S(2)}, u32[]{:S(2)}) %collective-permute-start.16) | collective-permute-done | bytes 147488 | tf_op jit(solution)/shard_map/ppermute | solution.py:28
  97.4 1.3 collective-permute-start.18
  98.7 6.4 %collective-permute-done.18.refs_2_ = bf16[2,1,144,256]{3,2,1,0:T(8,128)(2,1)S(1)} collective-permute-done((bf16[2,1,144,256]{3,2,1,0:T(8,128)(2,1)S(1)}, bf16[2,1,144,256]{3,2,1,0:T(8,128)(2,1)S(1)}, u32[]{:S(2)}, u32[]{:S(2)}) %collective-permute-start.18) | collective-permute-done | bytes 147488 | tf_op jit(solution)/shard_map/ppermute | solution.py:28
  105.0 0.7 combine.1
  105.9 1.2 collective-permute-done.19.got_ref
  107.1 1.2 finish.3
  108.3 1.4 %collective-permute-start.24 = (bf16[2,160,128]{2,1,0:T(8,128)(2,1)S(1)}, bf16[2,160,128]{2,1,0:T(8,128)(2,1)S(1)}, u32[]{:S(2)}, u32[]{:S(2)}) collective-permute-start(bf16[2,160,128]{2,1,0:T(8,128)(2,1)S(1)} %get-tuple-element.140), channel_id=1, source_target_pairs={{0,12},{1,13},{2,14},{3,15},{4,8},{5,9},{6,10},{7,11},{8,4},{9,5},... | collective-permute-start | bytes 245768 | tf_op jit(solution)/shard_map/ppermute | solution.py:28
  109.7 0.8 collective-permute-start.25
  110.5 3.1 %collective-permute-start.26 = (bf16[2,160,128]{2,1,0:T(8,128)(2,1)S(1)}, bf16[2,160,128]{2,1,0:T(8,128)(2,1)S(1)}, u32[]{:S(2)}, u32[]{:S(2)}) collective-permute-start(bf16[2,160,128]{2,1,0:T(8,128)(2,1)S(1)} %get-tuple-element.142), channel_id=1, source_target_pairs={{0,14},{1,15},{2,12},{3,13},{4,10},{5,11},{6,8},{7,9},{8,6},{9,7},... | collective-permute-start | bytes 245768 | tf_op jit(solution)/shard_map/ppermute | solution.py:28
  113.6 1.2 finish.2
  114.9 2.2 %collective-permute-start.21 = (bf16[2,160,128]{2,1,0:T(8,128)(2,1)S(1)}, bf16[2,160,128]{2,1,0:T(8,128)(2,1)S(1)}, u32[]{:S(2)}, u32[]{:S(2)}) collective-permute-start(bf16[2,160,128]{2,1,0:T(8,128)(2,1)S(1)} %get-tuple-element.135), channel_id=1, source_target_pairs={{0,6},{1,7},{2,4},{3,5},{4,2},{5,3},{6,0},{7,1},{8,14},{9,15},{10,... | collective-permute-start | bytes 245768 | tf_op jit(solution)/shard_map/ppermute | solution.py:28
  117.1 0.7 collective-permute-start.22
  117.8 3.0 %collective-permute-start.23 = (bf16[2,160,128]{2,1,0:T(8,128)(2,1)S(1)}, bf16[2,160,128]{2,1,0:T(8,128)(2,1)S(1)}, u32[]{:S(2)}, u32[]{:S(2)}) collective-permute-start(bf16[2,160,128]{2,1,0:T(8,128)(2,1)S(1)} %get-tuple-element.137), channel_id=1, source_target_pairs={{0,4},{1,5},{2,6},{3,7},{4,0},{5,1},{6,2},{7,3},{8,12},{9,13},{10,... | collective-permute-start | bytes 245768 | tf_op jit(solution)/shard_map/ppermute | solution.py:28
  120.8 1.2 collective-permute-done.20.refs_0_
  122.1 2.1 %collective-permute-done.21.refs_1_ = bf16[2,160,128]{2,1,0:T(8,128)(2,1)S(1)} collective-permute-done((bf16[2,160,128]{2,1,0:T(8,128)(2,1)S(1)}, bf16[2,160,128]{2,1,0:T(8,128)(2,1)S(1)}, u32[]{:S(2)}, u32[]{:S(2)}) %collective-permute-start.21) | collective-permute-done | bytes 81952 | tf_op jit(solution)/shard_map/ppermute | solution.py:28
  124.2 0.6 collective-permute-done.22.refs_2_
  124.9 1.4 %collective-permute-done.27.refs_8_ = bf16[4,160,128]{2,1,0:T(8,128)(2,1)S(1)} collective-permute-done((bf16[4,160,128]{2,1,0:T(8,128)(2,1)S(1)}, bf16[4,160,128]{2,1,0:T(8,128)(2,1)S(1)}, u32[]{:S(2)}, u32[]{:S(2)}) %collective-permute-start.27) | collective-permute-done | bytes 163872 | tf_op jit(solution)/shard_map/ppermute | solution.py:28
  126.2 1.5 %unpack.1 = (bf16[128,2048]{1,0:T(8,128)(2,1)}, bf16[16,4096]{1,0:T(8,128)(2,1)}) custom-call(s32[5]{0:T(128)S(1)} %stack.19.place_ref, bf16[2,160,128]{2,1,0:T(8,128)(2,1)S(1)} %collective-permute-done.20.refs_0_, bf16[2,160,128]{2,1,0:T(8,128)(2,1)S(1)} %collective-permute-done.21.refs_1_, bf16[2,160,128]{2,1,0:T(8,128)(2,1)S(1)} %collective-permute-done.22.refs_2_, ...), custom_call_target="tpu_custom_call" | custom-call | tf_op jit(solution)/shard_map/unpack/pallas_call | solution.py:323
  (35 shorter events, 0.6 us)
Async XLA Ops:
  2.2 1.0 copy-start.4
  4.7 8.3 %copy-start.3 = (bf16[1,256,1184]{1,2,0:T(8,128)(2,1)S(1)}, bf16[1,256,1184]{1,2,0:T(8,128)(2,1)}, u32[]{:S(2)}) copy-start(bf16[1,256,1184]{1,2,0:T(8,128)(2,1)} %param.10) | copy-start | bytes 1818628
  4.7 46.4 %all-to-all-start = ((bf16[16,384,128]{2,1,0:T(8,128)(2,1)}), bf16[16,384,128]{2,1,0:T(8,128)(2,1)S(1)}, u32[]{:S(2)}, u32[]{:S(2)}) async-start(bf16[16,384,128]{2,1,0:T(8,128)(2,1)} %pack.1), calls=%async_computation | async-start | bytes 3145728 | tf_op jit(solution)/shard_map/all_to_all | solution.py:627
  13.0 3.4 %copy-start = (bf16[1184,3584]{1,0:T(8,128)(2,1)S(1)}, bf16[1184,3584]{1,0:T(8,128)(2,1)}, u32[]{:S(2)}) copy-start(bf16[1184,3584]{1,0:T(8,128)(2,1)} %weight_ref.1) | copy-start | bytes 25460740
  19.8 1.9 %collective-permute-start = (bf16[8,16,1792]{2,1,0:T(8,128)(2,1)S(1)}, bf16[8,16,1792]{2,1,0:T(8,128)(2,1)S(1)}, u32[]{:S(2)}, u32[]{:S(2)}) collective-permute-start(bf16[8,16,1792]{2,1,0:T(8,128)(2,1)S(1)} %get-tuple-element.78), channel_id=1, source_target_pairs={{0,1},{1,0},{2,3},{3,2},{4,5},{5,4},{6,7},{7,6},{8,9},{9,8},{10,11... | collective-permute-start | bytes 1376264 | tf_op jit(solution)/shard_map/ppermute | solution.py:28
  20.3 2.1 %collective-permute-start.1 = (bf16[8,16,1792]{2,1,0:T(8,128)(2,1)S(1)}, bf16[8,16,1792]{2,1,0:T(8,128)(2,1)S(1)}, u32[]{:S(2)}, u32[]{:S(2)}) collective-permute-start(bf16[8,16,1792]{2,1,0:T(8,128)(2,1)S(1)} %get-tuple-element.80), channel_id=1, source_target_pairs={{0,1},{1,0},{2,3},{3,2},{4,5},{5,4},{6,7},{7,6},{8,9},{9,8},{10,11... | collective-permute-start | bytes 1376264 | tf_op jit(solution)/shard_map/ppermute | solution.py:28
  22.6 28.5 %copy-start.1 = (bf16[192,4096]{1,0:T(8,128)(2,1)S(1)}, bf16[192,4096]{1,0:T(8,128)(2,1)}, u32[]{:S(2)}) copy-start(bf16[192,4096]{1,0:T(8,128)(2,1)} %refs_7_.1) | copy-start | bytes 4718596
  22.6 32.6 %copy-start.6 = (bf16[3584]{0:T(1024)(128)(2,1)S(1)}, bf16[3584]{0:T(1024)(128)(2,1)}, u32[]{:S(2)}) copy-start(bf16[3584]{0:T(1024)(128)(2,1)} %param.12) | copy-start | bytes 21508
  22.6 13.5 %collective-permute-start.2 = (bf16[4,16,1792]{2,1,0:T(8,128)(2,1)S(1)}, bf16[4,16,1792]{2,1,0:T(8,128)(2,1)S(1)}, u32[]{:S(2)}, u32[]{:S(2)}) collective-permute-start(bf16[4,16,1792]{2,1,0:T(8,128)(2,1)S(1)} %get-tuple-element.82), channel_id=1, source_target_pairs={{0,2},{1,3},{2,0},{3,1},{4,6},{5,7},{6,4},{7,5},{8,10},{9,11},{10,... | collective-permute-start | bytes 688136 | tf_op jit(solution)/shard_map/ppermute | solution.py:28
  24.6 19.1 %collective-permute-start.3 = (bf16[4,16,1792]{2,1,0:T(8,128)(2,1)S(1)}, bf16[4,16,1792]{2,1,0:T(8,128)(2,1)S(1)}, u32[]{:S(2)}, u32[]{:S(2)}) collective-permute-start(bf16[4,16,1792]{2,1,0:T(8,128)(2,1)S(1)} %get-tuple-element.84), channel_id=1, source_target_pairs={{0,4},{1,5},{2,6},{3,7},{4,0},{5,1},{6,2},{7,3},{8,12},{9,13},{10,... | collective-permute-start | bytes 688136 | tf_op jit(solution)/shard_map/ppermute | solution.py:28
  43.7 5.8 %collective-permute-start.4 = (bf16[2,16,1792]{2,1,0:T(8,128)(2,1)S(1)}, bf16[2,16,1792]{2,1,0:T(8,128)(2,1)S(1)}, u32[]{:S(2)}, u32[]{:S(2)}) collective-permute-start(bf16[2,16,1792]{2,1,0:T(8,128)(2,1)S(1)} %get-tuple-element.86), channel_id=1, source_target_pairs={{0,4},{1,5},{2,6},{3,7},{4,0},{5,1},{6,2},{7,3},{8,12},{9,13},{10,... | collective-permute-start | bytes 344072 | tf_op jit(solution)/shard_map/ppermute | solution.py:28
  46.3 4.8 %collective-permute-start.5 = (bf16[2,16,1792]{2,1,0:T(8,128)(2,1)S(1)}, bf16[2,16,1792]{2,1,0:T(8,128)(2,1)S(1)}, u32[]{:S(2)}, u32[]{:S(2)}) collective-permute-start(bf16[2,16,1792]{2,1,0:T(8,128)(2,1)S(1)} %get-tuple-element.88), channel_id=1, source_target_pairs={{0,2},{1,3},{2,0},{3,1},{4,6},{5,7},{6,4},{7,5},{8,10},{9,11},{10,... | collective-permute-start | bytes 344072 | tf_op jit(solution)/shard_map/ppermute | solution.py:28
  51.1 20.7 %collective-permute-start.10 = (bf16[192,4096]{1,0:T(8,128)(2,1)S(1)}, bf16[192,4096]{1,0:T(8,128)(2,1)S(1)}, u32[]{:S(2)}, u32[]{:S(2)}) collective-permute-start(bf16[192,4096]{1,0:T(8,128)(2,1)S(1)} %copy-done.1), channel_id=1, source_target_pairs={{0,1},{1,0},{2,3},{3,2},{4,5},{5,4},{6,7},{7,6},{8,9},{9,8},{10,11... | collective-permute-start | bytes 4718600 | tf_op jit(solution)/shard_map/ppermute | solution.py:28
  51.2 20.7 %collective-permute-start.9 = (bf16[192,3584]{1,0:T(8,128)(2,1)}, bf16[192,3584]{1,0:T(8,128)(2,1)S(1)}, u32[]{:S(2)}, u32[]{:S(2)}) collective-permute-start(bf16[192,3584]{1,0:T(8,128)(2,1)} %bitcast.22), channel_id=1, source_target_pairs={{0,1},{1,0},{2,3},{3,2},{4,5},{5,4},{6,7},{7,6},{8,9},{9,8},{10,11... | collective-permute-start | bytes 4128776 | tf_op jit(solution)/shard_map/ppermute | solution.py:28
  51.7 13.6 %collective-permute-start.6 = (bf16[2,2,16,1792]{3,2,1,0:T(8,128)(2,1)S(1)}, bf16[2,2,16,1792]{3,2,1,0:T(8,128)(2,1)S(1)}, u32[]{:S(2)}, u32[]{:S(2)}) collective-permute-start(bf16[2,2,16,1792]{3,2,1,0:T(8,128)(2,1)S(1)} %add_all.1.mine_ref), channel_id=1, source_target_pairs={{0,8},{1,9},{2,10},{3,11},{4,12},{5,13},{6,14},{7,15},{8,0},{9,1},... | collective-permute-start | bytes 688136 | tf_op jit(solution)/shard_map/ppermute | solution.py:28
  55.3 11.9 %collective-permute-start.11 = (bf16[2,192,256]{2,1,0:T(8,128)(2,1)}, bf16[2,192,256]{2,1,0:T(8,128)(2,1)S(1)}, u32[]{:S(2)}, u32[]{:S(2)}) collective-permute-start(bf16[2,192,256]{2,1,0:T(8,128)(2,1)} %bitcast.26), channel_id=1, source_target_pairs={{0,1},{1,0},{2,3},{3,2},{4,5},{5,4},{6,7},{7,6},{8,9},{9,8},{10,11... | collective-permute-start | bytes 589832 | tf_op jit(solution)/shard_map/ppermute | solution.py:28
  65.5 4.9 %collective-permute-start.8 = (bf16[32,1792]{1,0:T(8,128)(2,1)S(1)}, bf16[32,1792]{1,0:T(8,128)(2,1)S(1)}, u32[]{:S(2)}, u32[]{:S(2)}) collective-permute-start(bf16[32,1792]{1,0:T(8,128)(2,1)S(1)} %bitcast.30), channel_id=1, source_target_pairs={{0,2},{1,3},{2,0},{3,1},{4,6},{5,7},{6,4},{7,5},{8,10},{9,11},{10,... | collective-permute-start | bytes 344072 | tf_op jit(solution)/shard_map/ppermute | solution.py:28
  67.1 4.8 %collective-permute-start.7 = (bf16[32,1792]{1,0:T(8,128)(2,1)S(1)}, bf16[32,1792]{1,0:T(8,128)(2,1)S(1)}, u32[]{:S(2)}, u32[]{:S(2)}) collective-permute-start(bf16[32,1792]{1,0:T(8,128)(2,1)S(1)} %bitcast.28), channel_id=1, source_target_pairs={{0,4},{1,5},{2,6},{3,7},{4,0},{5,1},{6,2},{7,3},{8,12},{9,13},{10,... | collective-permute-start | bytes 344072 | tf_op jit(solution)/shard_map/ppermute | solution.py:28
  67.2 0.9 copy-start.5
  71.9 6.6 %copy-start.2 = (bf16[3584,192]{0,1:T(8,128)(2,1)S(1)}, bf16[3584,192]{0,1:T(8,128)(2,1)}, u32[]{:S(2)}) copy-start(bf16[3584,192]{0,1:T(8,128)(2,1)} %param.13) | copy-start | bytes 4128772
  71.9 6.1 %collective-permute-start.12 = (bf16[64,1792]{1,0:T(8,128)(2,1)S(1)}, bf16[64,1792]{1,0:T(8,128)(2,1)S(1)}, u32[]{:S(2)}, u32[]{:S(2)}) collective-permute-start(bf16[64,1792]{1,0:T(8,128)(2,1)S(1)} %get-tuple-element.102.refs_0_), channel_id=1, source_target_pairs={{0,2},{1,3},{2,0},{3,1},{4,6},{5,7},{6,4},{7,5},{8,10},{9,11},{10,... | collective-permute-start | bytes 688136 | tf_op jit(solution)/shard_map/ppermute | solution.py:28
  72.5 6.0 %collective-permute-start.13 = (bf16[64,1792]{1,0:T(8,128)(2,1)S(1)}, bf16[64,1792]{1,0:T(8,128)(2,1)S(1)}, u32[]{:S(2)}, u32[]{:S(2)}) collective-permute-start(bf16[64,1792]{1,0:T(8,128)(2,1)S(1)} %get-tuple-element.103.refs_2_), channel_id=1, source_target_pairs={{0,4},{1,5},{2,6},{3,7},{4,0},{5,1},{6,2},{7,3},{8,12},{9,13},{10,... | collective-permute-start | bytes 688136 | tf_op jit(solution)/shard_map/ppermute | solution.py:28
  80.9 6.8 %collective-permute-start.14 = (bf16[4,144,256]{2,1,0:T(8,128)(2,1)S(1)}, bf16[4,144,256]{2,1,0:T(8,128)(2,1)S(1)}, u32[]{:S(2)}, u32[]{:S(2)}) collective-permute-start(bf16[4,144,256]{2,1,0:T(8,128)(2,1)S(1)} %get-tuple-element.118), channel_id=1, source_target_pairs={{0,2},{1,3},{2,0},{3,1},{4,6},{5,7},{6,4},{7,5},{8,10},{9,11},{10,... | collective-permute-start | bytes 884744 | tf_op jit(solution)/shard_map/ppermute | solution.py:28
  82.5 8.0 %collective-permute-start.15 = (bf16[4,144,256]{2,1,0:T(8,128)(2,1)S(1)}, bf16[4,144,256]{2,1,0:T(8,128)(2,1)S(1)}, u32[]{:S(2)}, u32[]{:S(2)}) collective-permute-start(bf16[4,144,256]{2,1,0:T(8,128)(2,1)S(1)} %get-tuple-element.119), channel_id=1, source_target_pairs={{0,4},{1,5},{2,6},{3,7},{4,0},{5,1},{6,2},{7,3},{8,12},{9,13},{10,... | collective-permute-start | bytes 884744 | tf_op jit(solution)/shard_map/ppermute | solution.py:28
  90.6 6.7 %collective-permute-start.16 = (bf16[2,144,256]{2,1,0:T(8,128)(2,1)S(1)}, bf16[2,144,256]{2,1,0:T(8,128)(2,1)S(1)}, u32[]{:S(2)}, u32[]{:S(2)}) collective-permute-start(bf16[2,144,256]{2,1,0:T(8,128)(2,1)S(1)} %get-tuple-element.126), channel_id=1, source_target_pairs={{0,4},{1,5},{2,6},{3,7},{4,0},{5,1},{6,2},{7,3},{8,12},{9,13},{10,... | collective-permute-start | bytes 442376 | tf_op jit(solution)/shard_map/ppermute | solution.py:28
  90.7 6.7 %collective-permute-start.17 = (bf16[2,144,256]{2,1,0:T(8,128)(2,1)S(1)}, bf16[2,144,256]{2,1,0:T(8,128)(2,1)S(1)}, u32[]{:S(2)}, u32[]{:S(2)}) collective-permute-start(bf16[2,144,256]{2,1,0:T(8,128)(2,1)S(1)} %get-tuple-element.128), channel_id=1, source_target_pairs={{0,2},{1,3},{2,0},{3,1},{4,6},{5,7},{6,4},{7,5},{8,10},{9,11},{10,... | collective-permute-start | bytes 442376 | tf_op jit(solution)/shard_map/ppermute | solution.py:28
  97.4 7.6 %collective-permute-start.18 = (bf16[2,1,144,256]{3,2,1,0:T(8,128)(2,1)S(1)}, bf16[2,1,144,256]{3,2,1,0:T(8,128)(2,1)S(1)}, u32[]{:S(2)}, u32[]{:S(2)}) collective-permute-start(bf16[2,1,144,256]{3,2,1,0:T(8,128)(2,1)S(1)} %get-tuple-element.131), channel_id=1, source_target_pairs={{0,8},{1,9},{2,10},{3,11},{4,12},{5,13},{6,14},{7,15},{8,0},{9,1},... | collective-permute-start | bytes 442376 | tf_op jit(solution)/shard_map/ppermute | solution.py:28
  105.8 1.3 %collective-permute-start.19 = (bf16[128,256]{1,0:T(8,128)(2,1)S(1)}, bf16[128,256]{1,0:T(8,128)(2,1)S(1)}, u32[]{:S(2)}, u32[]{:S(2)}) collective-permute-start(bf16[128,256]{1,0:T(8,128)(2,1)S(1)} %get-tuple-element.133), channel_id=1, source_target_pairs={{0,1},{1,0},{2,3},{3,2},{4,5},{5,4},{6,7},{7,6},{8,9},{9,8},{10,11... | collective-permute-start | bytes 196616 | tf_op jit(solution)/shard_map/ppermute | solution.py:28
  108.3 8.8 %collective-permute-start.24 = (bf16[2,160,128]{2,1,0:T(8,128)(2,1)S(1)}, bf16[2,160,128]{2,1,0:T(8,128)(2,1)S(1)}, u32[]{:S(2)}, u32[]{:S(2)}) collective-permute-start(bf16[2,160,128]{2,1,0:T(8,128)(2,1)S(1)} %get-tuple-element.140), channel_id=1, source_target_pairs={{0,12},{1,13},{2,14},{3,15},{4,8},{5,9},{6,10},{7,11},{8,4},{9,5},... | collective-permute-start | bytes 245768 | tf_op jit(solution)/shard_map/ppermute | solution.py:28
  109.7 8.1 %collective-permute-start.25 = (bf16[2,160,128]{2,1,0:T(8,128)(2,1)S(1)}, bf16[2,160,128]{2,1,0:T(8,128)(2,1)S(1)}, u32[]{:S(2)}, u32[]{:S(2)}) collective-permute-start(bf16[2,160,128]{2,1,0:T(8,128)(2,1)S(1)} %get-tuple-element.141), channel_id=1, source_target_pairs={{0,2},{1,3},{2,0},{3,1},{4,6},{5,7},{6,4},{7,5},{8,10},{9,11},{10,... | collective-permute-start | bytes 245768 | tf_op jit(solution)/shard_map/ppermute | solution.py:28
  110.5 10.2 %collective-permute-start.26 = (bf16[2,160,128]{2,1,0:T(8,128)(2,1)S(1)}, bf16[2,160,128]{2,1,0:T(8,128)(2,1)S(1)}, u32[]{:S(2)}, u32[]{:S(2)}) collective-permute-start(bf16[2,160,128]{2,1,0:T(8,128)(2,1)S(1)} %get-tuple-element.142), channel_id=1, source_target_pairs={{0,14},{1,15},{2,12},{3,13},{4,10},{5,11},{6,8},{7,9},{8,6},{9,7},... | collective-permute-start | bytes 245768 | tf_op jit(solution)/shard_map/ppermute | solution.py:28
  114.8 7.3 %collective-permute-start.20 = (bf16[2,160,128]{2,1,0:T(8,128)(2,1)S(1)}, bf16[2,160,128]{2,1,0:T(8,128)(2,1)S(1)}, u32[]{:S(2)}, u32[]{:S(2)}) collective-permute-start(bf16[2,160,128]{2,1,0:T(8,128)(2,1)S(1)} %get-tuple-element.134), channel_id=1, source_target_pairs={{0,8},{1,9},{2,10},{3,11},{4,12},{5,13},{6,14},{7,15},{8,0},{9,1},... | collective-permute-start | bytes 245768 | tf_op jit(solution)/shard_map/ppermute | solution.py:28
  114.9 9.3 %collective-permute-start.21 = (bf16[2,160,128]{2,1,0:T(8,128)(2,1)S(1)}, bf16[2,160,128]{2,1,0:T(8,128)(2,1)S(1)}, u32[]{:S(2)}, u32[]{:S(2)}) collective-permute-start(bf16[2,160,128]{2,1,0:T(8,128)(2,1)S(1)} %get-tuple-element.135), channel_id=1, source_target_pairs={{0,6},{1,7},{2,4},{3,5},{4,2},{5,3},{6,0},{7,1},{8,14},{9,15},{10,... | collective-permute-start | bytes 245768 | tf_op jit(solution)/shard_map/ppermute | solution.py:28
  117.1 7.7 %collective-permute-start.22 = (bf16[2,160,128]{2,1,0:T(8,128)(2,1)S(1)}, bf16[2,160,128]{2,1,0:T(8,128)(2,1)S(1)}, u32[]{:S(2)}, u32[]{:S(2)}) collective-permute-start(bf16[2,160,128]{2,1,0:T(8,128)(2,1)S(1)} %get-tuple-element.136), channel_id=1, source_target_pairs={{0,10},{1,11},{2,8},{3,9},{4,14},{5,15},{6,12},{7,13},{8,2},{9,3},... | collective-permute-start | bytes 245768 | tf_op jit(solution)/shard_map/ppermute | solution.py:28
  117.8 6.9 %collective-permute-start.23 = (bf16[2,160,128]{2,1,0:T(8,128)(2,1)S(1)}, bf16[2,160,128]{2,1,0:T(8,128)(2,1)S(1)}, u32[]{:S(2)}, u32[]{:S(2)}) collective-permute-start(bf16[2,160,128]{2,1,0:T(8,128)(2,1)S(1)} %get-tuple-element.137), channel_id=1, source_target_pairs={{0,4},{1,5},{2,6},{3,7},{4,0},{5,1},{6,2},{7,3},{8,12},{9,13},{10,... | collective-permute-start | bytes 245768 | tf_op jit(solution)/shard_map/ppermute | solution.py:28
  120.8 4.1 %collective-permute-start.28 = (bf16[4,160,128]{2,1,0:T(8,128)(2,1)S(1)}, bf16[4,160,128]{2,1,0:T(8,128)(2,1)S(1)}, u32[]{:S(2)}, u32[]{:S(2)}) collective-permute-start(bf16[4,160,128]{2,1,0:T(8,128)(2,1)S(1)} %gather_other.3), channel_id=1, source_target_pairs={{0,1},{1,0},{2,3},{3,2},{4,5},{5,4},{6,7},{7,6},{8,9},{9,8},{10,11... | collective-permute-start | bytes 491528 | tf_op jit(solution)/shard_map/ppermute | solution.py:28
  124.8 1.5 %collective-permute-start.27 = (bf16[4,160,128]{2,1,0:T(8,128)(2,1)S(1)}, bf16[4,160,128]{2,1,0:T(8,128)(2,1)S(1)}, u32[]{:S(2)}, u32[]{:S(2)}) collective-permute-start(bf16[4,160,128]{2,1,0:T(8,128)(2,1)S(1)} %gather_other.2), channel_id=1, source_target_pairs={{0,1},{1,0},{2,3},{3,2},{4,5},{5,4},{6,7},{7,6},{8,9},{9,8},{10,11... | collective-permute-start | bytes 491528 | tf_op jit(solution)/shard_map/ppermute | solution.py:28

commit v19 on v18

--- a/solution.py
+++ b/solution.py
@@ -33,11 +33,6 @@
     return (bits, [bits[1], bits[0]] + bits[2:])
 
 
-def position(chip, order):
-    last = len(order) - 1
-    return sum(((chip >> (bit.bit_length() - 1)) & 1) << (last - i) for i, bit in enumerate(order))
-
-
 def member(at, order):
     last = len(order) - 1
     return sum(bit for i, bit in enumerate(order) if (at >> (last - i)) & 1)
@@ -51,41 +46,37 @@
     return jax.nn.silu(embedding).astype(jnp.bfloat16)
 
 
-def encoder_kernel(lanes, place_ref, act_ref, weight_ref, *refs):
-    outs, lhs_ref = refs[:-1], refs[-1]
-    chips, share, width = outs[0].shape
-    core = place_ref[2]
-    half = chips * share
+def encoder_kernel(chips, place_ref, act_ref, weight_ref, own_ref, other_ref, lhs_ref):
+    chip, core = place_ref[1], place_ref[0]
+    half = lhs_ref.shape[0] // 2
+    half_chips = chips // 2
+    width = weight_ref.shape[1]
     first = core == 0
-    tile = width // 2
+    tile = width // 4
     lhs_ref[...] = act_ref[...].T
-    for lane, order in enumerate(lanes):
-        own_ref, other_ref = outs[2 * lane], outs[2 * lane + 1]
-        for column in range(0, width, tile):
-            start = lane * width + column
-            result = jnp.dot(
-                lhs_ref[...], weight_ref[:, start : start + tile], preferred_element_type=jnp.float32
-            )
-            own = jnp.where(first, result[:half], result[half:]).astype(own_ref.dtype)
-            other = jnp.where(first, result[half:], result[:half]).astype(own_ref.dtype)
-            own = own.reshape(chips, share, tile)
-            other = other.reshape(chips, share, tile)
-            for block in range(chips):
-                to = place_ref[lane] ^ position(block, order)
-                own_ref[to, :, column : column + tile] = own[block]
-                other_ref[to, :, column : column + tile] = other[block]
-
-
-def encoder(lanes, place, act, weight):
-    chips = 1 << len(lanes[0])
+    for column in range(0, width, tile):
+        columns = slice(column, column + tile)
+        result = jnp.dot(lhs_ref[...], weight_ref[:, columns], preferred_element_type=jnp.float32)
+        own = jnp.where(first, result[:half], result[half:]).astype(own_ref.dtype)
+        other = jnp.where(first, result[half:], result[:half]).astype(own_ref.dtype)
+        own = own.reshape(chips, half // chips, tile)
+        other = other.reshape(chips, half // chips, tile)
+        for block in range(chips):
+            away = chip ^ block
+            to = away % half_chips * 2 + away // half_chips
+            own_ref[to, :, columns] = own[block]
+            other_ref[to, :, columns] = other[block]
+
+
+def encoder(chips, place, act, weight):
     depth, rows = act.shape
     width = weight.shape[1]
-    out = jax.ShapeDtypeStruct((chips, rows // 2 // chips, width // 2), jnp.bfloat16)
-    return pl.pallas_call(
-        functools.partial(encoder_kernel, lanes),
-        out_shape=(out,) * 4,
+    out = jax.ShapeDtypeStruct((chips, rows // 2 // chips, width), jnp.bfloat16)
+    return pl.pallas_call(
+        functools.partial(encoder_kernel, chips),
+        out_shape=(out, out),
         in_specs=[SMEM_SPEC, VMEM_SPEC, VMEM_SPEC],
-        out_specs=(VMEM_SPEC,) * 4,
+        out_specs=(VMEM_SPEC,) * 2,
         scratch_shapes=[pltpu.VMEM((rows, depth), jnp.bfloat16)],
         compiler_params=params(16),
         cost_estimate=pl.CostEstimate(
@@ -95,6 +86,30 @@
         ),
         name="encoder",
     )(place, act, weight)
+
+
+def fold_kernel(own_ref, got_ref, keep_ref, *sent):
+    keep_ref[...] = own_ref[:2].astype(jnp.float32) + got_ref[:2].astype(jnp.float32)
+    for at, out_ref in enumerate(sent):
+        span = slice(2 * at + 2, 2 * at + 4)
+        total = own_ref[span].astype(jnp.float32) + got_ref[span].astype(jnp.float32)
+        out_ref[...] = total.astype(out_ref.dtype)
+
+
+def fold(own, got):
+    shape = (2,) + own.shape[1:]
+    count = own.shape[0] // 2 - 1
+    keep, *sent = pl.pallas_call(
+        fold_kernel,
+        out_shape=(jax.ShapeDtypeStruct(shape, jnp.float32),)
+        + (jax.ShapeDtypeStruct(shape, jnp.bfloat16),) * count,
+        in_specs=[VMEM_SPEC] * 2,
+        out_specs=(VMEM_SPEC,) * (1 + count),
+        compiler_params=params(8),
+        cost_estimate=pl.CostEstimate(flops=own.size, bytes_accessed=8 * own.size, transcendentals=0),
+        name="fold",
+    )(own, got)
+    return keep, sent
 
 
 def modulation_kernel(time_ref, mod0_ref, mod1_ref, out_ref):
@@ -132,7 +147,7 @@
 def project_kernel(lanes, place_ref, *refs):
     pieces, refs = (refs[:2], refs[2:4]), refs[4:]
     lines_ref, win0, win1, kv0, kv1, *outs, states, proj0, proj1, sums = refs
-    chip = place_ref[3]
+    chip = place_ref[1]
     half_chips = outs[0].shape[0]
     chips = 2 * half_chips
     rows = proj0.shape[0]
@@ -226,7 +241,7 @@
 
 def combine_kernel(chips, model_width, place_ref, *refs):
     keep0, keep1, came_ref, mine_ref, sent_ref = refs
-    core = place_ref[2]
+    core = place_ref[0]
     rows = mine_ref.shape[0]
     width = keep0.shape[2]
     slots = slot_rows(chips, width)[0]
@@ -300,7 +315,7 @@
 
 def unpack_kernel(copies, part_rows, masks, place_ref, *refs):
     *pieces, near_ref, far_ref, attended_ref, text_ref = refs
-    me = 2 * place_ref[3] + place_ref[2]
+    me = 2 * place_ref[1] + place_ref[0]
     share = text_ref.shape[0]
     half = text_ref.shape[1] // 2
     count = len(pieces) // 2
@@ -334,7 +349,7 @@
 
 
 def image_kernel(factor, masks, img_dev, place_ref, packed_ref, sum_ref, top_ref, keys_ref, wide_ref):
-    me = 2 * place_ref[3] + place_ref[2]
+    me = 2 * place_ref[1] + place_ref[0]
     wide_ref[:, HEAD_DIM:] = jnp.ones((wide_ref.shape[0], HEAD_DIM), wide_ref.dtype)
     for device in range(packed_ref.shape[0]):
         rows = slice(device * img_dev, (device + 1) * img_dev)
@@ -392,8 +407,8 @@
 
 def finish_kernel(factor, masks, img_dev, place_ref, packed_ref, sum_ref, top_ref, mine_ref, got_ref, *refs):
     *outs, text_ref = refs
-    core, valid = place_ref[2], place_ref[4]
-    me = 2 * place_ref[3] + core
+    core, valid = place_ref[0], place_ref[2]
+    me = 2 * place_ref[1] + core
     part_rows = packed_ref.shape[1] - 2 * img_dev
     half = mine_ref.shape[0]
     contract = (((1,), (1,)), ((), ()))
@@ -514,41 +529,39 @@
     return [outs[0], outs[2]], [outs[1], outs[3]]
 
 
-def total_kernel(mine0, got0, mine1, got1, out_ref):
-    for lane, (mine, got) in enumerate(((mine0, got0), (mine1, got1))):
-        out_ref[lane] = (mine[...] + got[...].astype(jnp.float32)).astype(out_ref.dtype)
-
-
-def add_all(mine, got):
+def total_kernel(keep_ref, *refs):
+    total = keep_ref[...]
+    for got_ref in refs[:-1]:
+        total += got_ref[...].astype(jnp.float32)
+    refs[-1][...] = total.astype(refs[-1].dtype)
+
+
+def add_all(keep, got):
     return pl.pallas_call(
         total_kernel,
-        out_shape=jax.ShapeDtypeStruct((2,) + mine[0].shape, jnp.bfloat16),
-        in_specs=[VMEM_SPEC] * 4,
+        out_shape=jax.ShapeDtypeStruct(keep.shape, jnp.bfloat16),
+        in_specs=[VMEM_SPEC] * (1 + len(got)),
         out_specs=VMEM_SPEC,
         compiler_params=params(4),
         cost_estimate=pl.CostEstimate(
-            flops=2 * mine[0].size, bytes_accessed=16 * mine[0].size, transcendentals=0
+            flops=4 * keep.size, bytes_accessed=12 * keep.size, transcendentals=0
         ),
         name="add_all",
-    )(mine[0], got[0], mine[1], got[1])
-
-
-def norm_kernel(mine_ref, got_ref, gain_ref, out0, out1):
-    width = mine_ref.shape[3]
+    )(keep, *got)
+
+
+def norm_kernel(mine_ref, got_ref, gain_ref, *outs):
+    width = mine_ref.shape[2] // 2
     for at in range(2):
-        totals = [
-            mine_ref[lane, at].astype(jnp.float32) + got_ref[lane, 1 - at].astype(jnp.float32)
-            for lane in range(2)
-        ]
-        square = sum(jnp.sum(total * total, 1, keepdims=True) for total in totals)
-        scale_rows = lax.rsqrt(square / (2 * width) + epsilon)
-        for lane, (total, out_ref) in enumerate(zip(totals, (out0, out1))):
-            gain = gain_ref[:, lane * width : (lane + 1) * width].astype(jnp.float32)
-            out_ref[at] = (total * scale_rows * gain).astype(out_ref.dtype)
+        total = mine_ref[at].astype(jnp.float32) + got_ref[1 - at].astype(jnp.float32)
+        scale_rows = lax.rsqrt(jnp.mean(total * total, 1, keepdims=True) + epsilon)
+        total = total * scale_rows * gain_ref[...].astype(jnp.float32)
+        for lane, out_ref in enumerate(outs):
+            out_ref[at] = total[:, lane * width : (lane + 1) * width].astype(out_ref.dtype)
 
 
 def normalize(mine, got, norm_gain):
-    out = jax.ShapeDtypeStruct(mine.shape[1:], jnp.bfloat16)
+    out = jax.ShapeDtypeStruct(mine.shape[:2] + (mine.shape[2] // 2,), jnp.bfloat16)
     states = pl.pallas_call(
         norm_kernel,
         out_shape=(out, out),
@@ -612,7 +625,7 @@
     lanes = orders(chips)
     index = lax.axis_index("seq")
     chip, core = index // 2, index % 2
-    place = jnp.stack([position(chip, lanes[0]), position(chip, lanes[1]), core, chip, lengths[0]])
+    place = jnp.stack([core, chip, lengths[0]])
     place = place.astype(jnp.int32)
 
     win0, kv0 = text_in_weight.T, key_value_weight
@@ -630,12 +643,10 @@
     packed = pack(copies, image_queries[0], image_key_values[0, :, 0], image_key_values[0, :, 1])
     act, packed = tie((enc_act[0].T, packed))
     packed = exchange(packed)
-    encoded = encoder(lanes, place, act, down_weight)
-    keep, got = encoded[::2], [swap(other, 1) for other in encoded[1::2]]
+    own, other = encoder(chips, place, act, down_weight)
     last = 2 * lanes[0][-1]
-    for step in range(rounds - 1):
-        sent, keep = add_halves(keep, got)
-        got = [swap(part, 2 * order[step]) for part, order in zip(sent, lanes)]
+    keep, sent = fold(own, swap(other, 1))
+    got = [swap(part, 2 * mask) for mask, part in enumerate(sent, 1)]
     summed, packed = tie((add_all(keep, got), packed))
     summed, held, held_kv, held_mod = tie((summed, win0, kv0, mod0))
     win1, kv1, mod1 = swap(held, 1), swap(held_kv, 1), swap(held_mod, 1)

time: 128 us -> 129 us (level)
  waiting for transfers between devices: 60.7 us -> 63.1 us
  starting transfers between devices: 36.8 us -> 35.1 us
    ppermute x29 -> x27, waiting for transfers between devices: 60.7 us -> 63.1 us  [swap(): return lax.ppermute(value, 'seq', [(i, i ^ mask) for i in range(devices)])]
    ppermute x29 -> x27, starting transfers between devices: 29.3 us -> 27.6 us  [swap(): return lax.ppermute(value, 'seq', [(i, i ^ mask) for i in range(devices)])]
    pallas_call x2 -> x3, Pallas kernels: 3.51 us -> 3.77 us  [the longest x1 3.47 us: encoder(): pl.pallas_call(functools.partial(encoder_kernel, chips), out_shape=(out,...]
  transfers between devices with their start and end apart: 30 -> 28, of which waited for: 20 -> 17; matrix products, arithmetic and copies ran while one was open for 0% -> 0% of each run, Pallas kernels for 10% -> 10%
where the time goes in v19:
time: 129 us; the launch traced here: 128 us
  waiting for transfers between devices  63.1 us (49%)
  starting transfers between devices  35.1 us (27%)
  Pallas kernels  20.9 us (16%)
  local copies, waits for them, and re-layouts  6.97 us (5%)
  between operations  2.23 us (2%)
    ppermute x27, waiting for transfers between devices, swap(): return lax.ppermute(value, 'seq', [(i, i ^ mask) for i in range(devices)])  63.1 us
    ppermute x27, starting transfers between devices, swap(): return lax.ppermute(value, 'seq', [(i, i ^ mask) for i in range(devices)])  27.6 us
    pallas_call x2, Pallas kernels, image_attention(): pl.pallas_call(functools.partial(image_kernel, factor, masks, img_dev), o...  8.03 us
    all_to_all x1, starting transfers between devices, exchange(): return lax.all_to_all(rows, 'seq', split_axis=0, concat_axis=0, tiled=True)  7.49 us
    unnamed x14, local copies, waits for them, and re-layouts  5.31 us
    pallas_call x1, Pallas kernels, encoder(): pl.pallas_call(functools.partial(encoder_kernel, chips), out_shape=(out,...  3.47 us
  transfers between devices with their start and end apart: 28, of which 17 were waited for; matrix products, arithmetic and copies ran while one was open for 0% of the time, Pallas kernels for 10%

profile of v19, /device:TPU:0, one launch (start us, length us, event | category | flops | bytes accessed | tf_op | source)
XLA Modules:
  0.0 128.4 jit_solution(5850296492095116184)
XLA Ops:
  0.6 1.6 %copy.12 = bf16[1,128,2,2048]{3,1,2,0:T(8,128)(2,1)S(1)} copy(bf16[1,128,2,2048]{3,2,1,0:T(2,128)(2,1)} %param.19) | data formatting | bytes 2097152 | tf_op jit(solution)/shard_map/optimization_barrier | solution.py:642
  2.3 1.0 copy-done.4
  3.3 1.5 %pack.1 = bf16[16,384,128]{2,1,0:T(8,128)(2,1)} custom-call(bf16[128,2048]{1,0:T(8,128)(2,1)S(1)} %bitcast.23, bf16[128,2048]{1,0:T(8,128)(2,1)S(1)} %get-tuple-element.135.keys_ref, bf16[128,2048]{1,0:T(8,128)(2,1)S(1)} %get-tuple-element.134.values_ref), custom_call_target="tpu_custom_call" | custom-call | bytes 3145728 | tf_op jit(solution)/shard_map/pack/pallas_call | solution.py:303
  4.7 7.5 %all-to-all-start = ((bf16[16,384,128]{2,1,0:T(8,128)(2,1)}), bf16[16,384,128]{2,1,0:T(8,128)(2,1)S(1)}, u32[]{:S(2)}, u32[]{:S(2)}) async-start(bf16[16,384,128]{2,1,0:T(8,128)(2,1)} %pack.1), calls=%async_computation | async-start | bytes 3145728 | tf_op jit(solution)/shard_map/all_to_all | solution.py:640
  12.9 0.1 pad_add_fusion.place_ref
  13.0 3.4 %copy-done = bf16[1184,3584]{1,0:T(8,128)(2,1)S(1)} copy-done((bf16[1184,3584]{1,0:T(8,128)(2,1)S(1)}, bf16[1184,3584]{1,0:T(8,128)(2,1)}, u32[]{:S(2)}) %copy-start) | copy-done | bytes 8486936
  16.4 3.5 %encoder.1 = (bf16[8,16,3584]{2,1,0:T(8,128)(2,1)S(1)}, bf16[8,16,3584]{2,1,0:T(8,128)(2,1)S(1)}) custom-call(s32[3]{0:T(128)S(1)} %pad_add_fusion.place_ref, bf16[1184,256]{1,0:T(8,128)(2,1)S(1)} %bitcast.22, bf16[1184,3584]{1,0:T(8,128)(2,1)S(1)} %copy-done), custom_call_target="tpu_custom_call" | custom-call | flops 2172649472 | bytes 10928128 | tf_op jit(solution)/shard_map/encoder/pallas_call | solution.py:75
  19.8 0.5 collective-permute-start
  20.3 2.1 %collective-permute-done.got_ref = bf16[8,16,3584]{2,1,0:T(8,128)(2,1)S(1)} collective-permute-done((bf16[8,16,3584]{2,1,0:T(8,128)(2,1)S(1)}, bf16[8,16,3584]{2,1,0:T(8,128)(2,1)S(1)}, u32[]{:S(2)}, u32[]{:S(2)}) %collective-permute-start) | collective-permute-done | bytes 917536 | tf_op jit(solution)/shard_map/ppermute | solution.py:28
  22.4 0.2 fold.1
  22.6 2.0 %collective-permute-start.1 = (bf16[2,16,3584]{2,1,0:T(8,128)(2,1)S(1)}, bf16[2,16,3584]{2,1,0:T(8,128)(2,1)S(1)}, u32[]{:S(2)}, u32[]{:S(2)}) collective-permute-start(bf16[2,16,3584]{2,1,0:T(8,128)(2,1)S(1)} %get-tuple-element.74), channel_id=1, source_target_pairs={{0,2},{1,3},{2,0},{3,1},{4,6},{5,7},{6,4},{7,5},{8,10},{9,11},{10,... | collective-permute-start | bytes 688136 | tf_op jit(solution)/shard_map/ppermute | solution.py:28
  24.6 1.5 %collective-permute-start.2 = (bf16[2,16,3584]{2,1,0:T(8,128)(2,1)S(1)}, bf16[2,16,3584]{2,1,0:T(8,128)(2,1)S(1)}, u32[]{:S(2)}, u32[]{:S(2)}) collective-permute-start(bf16[2,16,3584]{2,1,0:T(8,128)(2,1)S(1)} %get-tuple-element.75), channel_id=1, source_target_pairs={{0,4},{1,5},{2,6},{3,7},{4,0},{5,1},{6,2},{7,3},{8,12},{9,13},{10,... | collective-permute-start | bytes 688136 | tf_op jit(solution)/shard_map/ppermute | solution.py:28
  26.0 0.1 collective-permute-start.3
  26.2 9.9 %collective-permute-done.1.refs_0_ = bf16[2,16,3584]{2,1,0:T(8,128)(2,1)S(1)} collective-permute-done((bf16[2,16,3584]{2,1,0:T(8,128)(2,1)S(1)}, bf16[2,16,3584]{2,1,0:T(8,128)(2,1)S(1)}, u32[]{:S(2)}, u32[]{:S(2)}) %collective-permute-start.1) | collective-permute-done | bytes 229408 | tf_op jit(solution)/shard_map/ppermute | solution.py:28
  36.1 9.7 %collective-permute-done.2.refs_1_ = bf16[2,16,3584]{2,1,0:T(8,128)(2,1)S(1)} collective-permute-done((bf16[2,16,3584]{2,1,0:T(8,128)(2,1)S(1)}, bf16[2,16,3584]{2,1,0:T(8,128)(2,1)S(1)}, u32[]{:S(2)}, u32[]{:S(2)}) %collective-permute-start.2) | collective-permute-done | bytes 229408 | tf_op jit(solution)/shard_map/ppermute | solution.py:28
  45.8 5.6 %collective-permute-done.3.refs_2_ = bf16[2,16,3584]{2,1,0:T(8,128)(2,1)S(1)} collective-permute-done((bf16[2,16,3584]{2,1,0:T(8,128)(2,1)S(1)}, bf16[2,16,3584]{2,1,0:T(8,128)(2,1)S(1)}, u32[]{:S(2)}, u32[]{:S(2)}) %collective-permute-start.3) | collective-permute-done | bytes 229408 | tf_op jit(solution)/shard_map/ppermute | solution.py:28
  51.4 0.1 add_all.1.mine_ref
  51.5 0.1 collective-permute-start.8
  51.6 0.5 collective-permute-start.7
  52.1 4.4 %collective-permute-start.4 = (bf16[2,16,3584]{2,1,0:T(8,128)(2,1)S(1)}, bf16[2,16,3584]{2,1,0:T(8,128)(2,1)S(1)}, u32[]{:S(2)}, u32[]{:S(2)}) collective-permute-start(bf16[2,16,3584]{2,1,0:T(8,128)(2,1)S(1)} %add_all.1.mine_ref), channel_id=1, source_target_pairs={{0,8},{1,9},{2,10},{3,11},{4,12},{5,13},{6,14},{7,15},{8,0},{9,1},... | collective-permute-start | bytes 688136 | tf_op jit(solution)/shard_map/ppermute | solution.py:28
  57.2 0.1 collective-permute-start.9
  57.3 10.0 %collective-permute-done.4.got_ref = bf16[2,16,3584]{2,1,0:T(8,128)(2,1)S(1)} collective-permute-done((bf16[2,16,3584]{2,1,0:T(8,128)(2,1)S(1)}, bf16[2,16,3584]{2,1,0:T(8,128)(2,1)S(1)}, u32[]{:S(2)}, u32[]{:S(2)}) %collective-permute-start.4) | collective-permute-done | bytes 229408 | tf_op jit(solution)/shard_map/ppermute | solution.py:28
  67.3 0.2 normalize.1
  67.5 0.1 collective-permute-start.6
  67.6 0.1 collective-permute-start.5
  67.8 0.9 copy-done.5
  68.7 0.2 modulation.1.refs_4_
  68.9 3.6 %collective-permute-done.6.got1 = bf16[32,1792]{1,0:T(8,128)(2,1)S(1)} collective-permute-done((bf16[32,1792]{1,0:T(8,128)(2,1)S(1)}, bf16[32,1792]{1,0:T(8,128)(2,1)S(1)}, u32[]{:S(2)}, u32[]{:S(2)}) %collective-permute-start.6) | collective-permute-done | bytes 114720 | tf_op jit(solution)/shard_map/ppermute | solution.py:28
  72.5 0.1 collective-permute-done.5.got0
  72.6 1.9 %collective-permute-start.10 = (bf16[64,1792]{1,0:T(8,128)(2,1)S(1)}, bf16[64,1792]{1,0:T(8,128)(2,1)S(1)}, u32[]{:S(2)}, u32[]{:S(2)}) collective-permute-start(bf16[64,1792]{1,0:T(8,128)(2,1)S(1)} %get-tuple-element.90.refs_0_), channel_id=1, source_target_pairs={{0,2},{1,3},{2,0},{3,1},{4,6},{5,7},{6,4},{7,5},{8,10},{9,11},{10,... | collective-permute-start | bytes 688136 | tf_op jit(solution)/shard_map/ppermute | solution.py:28
  74.5 0.1 collective-permute-start.11
  74.6 3.9 %image_attention.2 = (f32[1024,256]{1,0:T(8,128)S(1)}, f32[1024,128]{1,0:T(8,128)S(1)}) custom-call(s32[3]{0:T(128)S(1)} %pad_add_fusion.place_ref, bf16[16,384,128]{2,1,0:T(8,128)(2,1)S(1)} %all-to-all-done.packed_ref), custom_call_target="tpu_custom_call" | custom-call | flops 1073741824 | bytes 2359296 | tf_op jit(solution)/shard_map/image_attention/pallas_call | solution.py:380
  78.6 0.6 collective-permute-done.10.refs_1_
  79.2 1.4 %collective-permute-done.11.refs_3_ = bf16[64,1792]{1,0:T(8,128)(2,1)S(1)} collective-permute-done((bf16[64,1792]{1,0:T(8,128)(2,1)S(1)}, bf16[64,1792]{1,0:T(8,128)(2,1)S(1)}, u32[]{:S(2)}, u32[]{:S(2)}) %collective-permute-start.11) | collective-permute-done | bytes 229408 | tf_op jit(solution)/shard_map/ppermute | solution.py:28
  80.5 2.4 %project.1 = (bf16[4,144,256]{2,1,0:T(8,128)(2,1)S(1)}, bf16[4,144,256]{2,1,0:T(8,128)(2,1)S(1)}, bf16[4,144,256]{2,1,0:T(8,128)(2,1)S(1)}, bf16[4,144,256]{2,1,0:T(8,128)(2,1)S(1)}) custom-call(s32[3]{0:T(128)S(1)} %pad_add_fusion.place_ref, bf16[64,1792]{1,0:T(8,128)(2,1)S(1)} %get-tuple-element.90.refs_0_, ...), custom_call_target="tpu_custom_call" | custom-call | flops 754974720 | bytes 7864320 | tf_op jit(solution)/shard_map/project/pallas_call | solution.py:221
  82.9 0.5 collective-permute-start.12
  83.3 0.6 collective-permute-start.13
  83.9 4.1 %image_attention.3 = (f32[1024,256]{1,0:T(8,128)S(1)}, f32[1024,128]{1,0:T(8,128)S(1)}) custom-call(s32[3]{0:T(128)S(1)} %pad_add_fusion.place_ref, bf16[16,384,128]{2,1,0:T(8,128)(2,1)S(1)} %all-to-all-done.packed_ref), custom_call_target="tpu_custom_call" | custom-call | flops 1073741824 | bytes 2359296 | tf_op jit(solution)/shard_map/image_attention/pallas_call | solution.py:380
  88.0 1.6 %collective-permute-done.12.refs_1_ = bf16[4,144,256]{2,1,0:T(8,128)(2,1)S(1)} collective-permute-done((bf16[4,144,256]{2,1,0:T(8,128)(2,1)S(1)}, bf16[4,144,256]{2,1,0:T(8,128)(2,1)S(1)}, u32[]{:S(2)}, u32[]{:S(2)}) %collective-permute-start.12) | collective-permute-done | bytes 294944 | tf_op jit(solution)/shard_map/ppermute | solution.py:28
  89.7 0.9 collective-permute-done.13.refs_3_
  90.6 0.1 add_halves.2
  90.7 0.4 collective-permute-start.14
  91.0 1.8 %collective-permute-start.15 = (bf16[2,144,256]{2,1,0:T(8,128)(2,1)S(1)}, bf16[2,144,256]{2,1,0:T(8,128)(2,1)S(1)}, u32[]{:S(2)}, u32[]{:S(2)}) collective-permute-start(bf16[2,144,256]{2,1,0:T(8,128)(2,1)S(1)} %get-tuple-element.116), channel_id=1, source_target_pairs={{0,2},{1,3},{2,0},{3,1},{4,6},{5,7},{6,4},{7,5},{8,10},{9,11},{10,... | collective-permute-start | bytes 442376 | tf_op jit(solution)/shard_map/ppermute | solution.py:28
  92.9 4.0 %collective-permute-done.14.refs_1_ = bf16[2,144,256]{2,1,0:T(8,128)(2,1)S(1)} collective-permute-done((bf16[2,144,256]{2,1,0:T(8,128)(2,1)S(1)}, bf16[2,144,256]{2,1,0:T(8,128)(2,1)S(1)}, u32[]{:S(2)}, u32[]{:S(2)}) %collective-permute-start.14) | collective-permute-done | bytes 147488 | tf_op jit(solution)/shard_map/ppermute | solution.py:28
  97.0 1.6 %collective-permute-start.16 = (bf16[2,1,144,256]{3,2,1,0:T(8,128)(2,1)S(1)}, bf16[2,1,144,256]{3,2,1,0:T(8,128)(2,1)S(1)}, u32[]{:S(2)}, u32[]{:S(2)}) collective-permute-start(bf16[2,1,144,256]{3,2,1,0:T(8,128)(2,1)S(1)} %get-tuple-element.119), channel_id=1, source_target_pairs={{0,8},{1,9},{2,10},{3,11},{4,12},{5,13},{6,14},{7,15},{8,0},{9,1},... | collective-permute-start | bytes 442376 | tf_op jit(solution)/shard_map/ppermute | solution.py:28
  98.6 6.1 %collective-permute-done.16.refs_2_ = bf16[2,1,144,256]{3,2,1,0:T(8,128)(2,1)S(1)} collective-permute-done((bf16[2,1,144,256]{3,2,1,0:T(8,128)(2,1)S(1)}, bf16[2,1,144,256]{3,2,1,0:T(8,128)(2,1)S(1)}, u32[]{:S(2)}, u32[]{:S(2)}) %collective-permute-start.16) | collective-permute-done | bytes 147488 | tf_op jit(solution)/shard_map/ppermute | solution.py:28
  104.6 0.7 combine.1
  105.4 0.1 collective-permute-start.17
  105.5 1.2 collective-permute-done.17.got_ref
  106.7 1.2 finish.3
  107.9 2.3 %collective-permute-start.22 = (bf16[2,160,128]{2,1,0:T(8,128)(2,1)S(1)}, bf16[2,160,128]{2,1,0:T(8,128)(2,1)S(1)}, u32[]{:S(2)}, u32[]{:S(2)}) collective-permute-start(bf16[2,160,128]{2,1,0:T(8,128)(2,1)S(1)} %get-tuple-element.128), channel_id=1, source_target_pairs={{0,12},{1,13},{2,14},{3,15},{4,8},{5,9},{6,10},{7,11},{8,4},{9,5},... | collective-permute-start | bytes 245768 | tf_op jit(solution)/shard_map/ppermute | solution.py:28
  110.2 0.4 collective-permute-start.23
  110.6 2.7 %collective-permute-start.24 = (bf16[2,160,128]{2,1,0:T(8,128)(2,1)S(1)}, bf16[2,160,128]{2,1,0:T(8,128)(2,1)S(1)}, u32[]{:S(2)}, u32[]{:S(2)}) collective-permute-start(bf16[2,160,128]{2,1,0:T(8,128)(2,1)S(1)} %get-tuple-element.130), channel_id=1, source_target_pairs={{0,14},{1,15},{2,12},{3,13},{4,10},{5,11},{6,8},{7,9},{8,6},{9,7},... | collective-permute-start | bytes 245768 | tf_op jit(solution)/shard_map/ppermute | solution.py:28
  113.3 1.2 finish.2
  114.4 0.1 collective-permute-start.18
  114.5 2.6 %collective-permute-start.19 = (bf16[2,160,128]{2,1,0:T(8,128)(2,1)S(1)}, bf16[2,160,128]{2,1,0:T(8,128)(2,1)S(1)}, u32[]{:S(2)}, u32[]{:S(2)}) collective-permute-start(bf16[2,160,128]{2,1,0:T(8,128)(2,1)S(1)} %get-tuple-element.123), channel_id=1, source_target_pairs={{0,6},{1,7},{2,4},{3,5},{4,2},{5,3},{6,0},{7,1},{8,14},{9,15},{10,... | collective-permute-start | bytes 245768 | tf_op jit(solution)/shard_map/ppermute | solution.py:28
  117.1 1.1 collective-permute-start.20
  118.3 2.1 %collective-permute-start.21 = (bf16[2,160,128]{2,1,0:T(8,128)(2,1)S(1)}, bf16[2,160,128]{2,1,0:T(8,128)(2,1)S(1)}, u32[]{:S(2)}, u32[]{:S(2)}) collective-permute-start(bf16[2,160,128]{2,1,0:T(8,128)(2,1)S(1)} %get-tuple-element.125), channel_id=1, source_target_pairs={{0,4},{1,5},{2,6},{3,7},{4,0},{5,1},{6,2},{7,3},{8,12},{9,13},{10,... | collective-permute-start | bytes 245768 | tf_op jit(solution)/shard_map/ppermute | solution.py:28
  120.4 0.1 collective-permute-start.26
  120.5 1.9 %collective-permute-done.18.refs_0_ = bf16[2,160,128]{2,1,0:T(8,128)(2,1)S(1)} collective-permute-done((bf16[2,160,128]{2,1,0:T(8,128)(2,1)S(1)}, bf16[2,160,128]{2,1,0:T(8,128)(2,1)S(1)}, u32[]{:S(2)}, u32[]{:S(2)}) %collective-permute-start.18) | collective-permute-done | bytes 81952 | tf_op jit(solution)/shard_map/ppermute | solution.py:28
  122.4 3.0 %collective-permute-done.20.refs_2_ = bf16[2,160,128]{2,1,0:T(8,128)(2,1)S(1)} collective-permute-done((bf16[2,160,128]{2,1,0:T(8,128)(2,1)S(1)}, bf16[2,160,128]{2,1,0:T(8,128)(2,1)S(1)}, u32[]{:S(2)}, u32[]{:S(2)}) %collective-permute-start.20) | collective-permute-done | bytes 81952 | tf_op jit(solution)/shard_map/ppermute | solution.py:28
  125.4 0.1 collective-permute-start.25
  125.5 1.4 %collective-permute-done.25.refs_8_ = bf16[4,160,128]{2,1,0:T(8,128)(2,1)S(1)} collective-permute-done((bf16[4,160,128]{2,1,0:T(8,128)(2,1)S(1)}, bf16[4,160,128]{2,1,0:T(8,128)(2,1)S(1)}, u32[]{:S(2)}, u32[]{:S(2)}) %collective-permute-start.25) | collective-permute-done | bytes 163872 | tf_op jit(solution)/shard_map/ppermute | solution.py:28
  126.9 1.5 %unpack.1 = (bf16[128,2048]{1,0:T(8,128)(2,1)}, bf16[16,4096]{1,0:T(8,128)(2,1)}) custom-call(s32[3]{0:T(128)S(1)} %pad_add_fusion.place_ref, bf16[2,160,128]{2,1,0:T(8,128)(2,1)S(1)} %collective-permute-done.18.refs_0_, bf16[2,160,128]{2,1,0:T(8,128)(2,1)S(1)} %collective-permute-done.19.refs_1_, bf16[2,160,128]{2,1,0:T(8,128)(2,1)S(1)} %collective-permute-done.20.refs_2_, ...), custom_call_target="tpu_custom_call" | custom-call | tf_op jit(solution)/shard_map/unpack/pallas_call | solution.py:338
  (30 shorter events, 0.3 us)
Async XLA Ops:
  2.2 1.0 copy-start.4
  4.7 8.2 %copy-start.3 = (bf16[1,256,1184]{1,2,0:T(8,128)(2,1)S(1)}, bf16[1,256,1184]{1,2,0:T(8,128)(2,1)}, u32[]{:S(2)}) copy-start(bf16[1,256,1184]{1,2,0:T(8,128)(2,1)} %param.10) | copy-start | bytes 1818628
  4.7 46.8 %all-to-all-start = ((bf16[16,384,128]{2,1,0:T(8,128)(2,1)}), bf16[16,384,128]{2,1,0:T(8,128)(2,1)S(1)}, u32[]{:S(2)}, u32[]{:S(2)}) async-start(bf16[16,384,128]{2,1,0:T(8,128)(2,1)} %pack.1), calls=%async_computation | async-start | bytes 3145728 | tf_op jit(solution)/shard_map/all_to_all | solution.py:640
  13.0 3.4 %copy-start = (bf16[1184,3584]{1,0:T(8,128)(2,1)S(1)}, bf16[1184,3584]{1,0:T(8,128)(2,1)}, u32[]{:S(2)}) copy-start(bf16[1184,3584]{1,0:T(8,128)(2,1)} %weight_ref.1) | copy-start | bytes 25460740
  19.8 2.6 %collective-permute-start = (bf16[8,16,3584]{2,1,0:T(8,128)(2,1)S(1)}, bf16[8,16,3584]{2,1,0:T(8,128)(2,1)S(1)}, u32[]{:S(2)}, u32[]{:S(2)}) collective-permute-start(bf16[8,16,3584]{2,1,0:T(8,128)(2,1)S(1)} %get-tuple-element.72), channel_id=1, source_target_pairs={{0,1},{1,0},{2,3},{3,2},{4,5},{5,4},{6,7},{7,6},{8,9},{9,8},{10,11... | collective-permute-start | bytes 2752520 | tf_op jit(solution)/shard_map/ppermute | solution.py:28
  22.4 29.1 %copy-start.1 = (bf16[192,4096]{1,0:T(8,128)(2,1)S(1)}, bf16[192,4096]{1,0:T(8,128)(2,1)}, u32[]{:S(2)}) copy-start(bf16[192,4096]{1,0:T(8,128)(2,1)} %refs_7_.1) | copy-start | bytes 4718596
  22.4 34.8 %copy-start.6 = (bf16[3584]{0:T(1024)(128)(2,1)S(1)}, bf16[3584]{0:T(1024)(128)(2,1)}, u32[]{:S(2)}) copy-start(bf16[3584]{0:T(1024)(128)(2,1)} %param.12) | copy-start | bytes 21508
  22.6 13.5 %collective-permute-start.1 = (bf16[2,16,3584]{2,1,0:T(8,128)(2,1)S(1)}, bf16[2,16,3584]{2,1,0:T(8,128)(2,1)S(1)}, u32[]{:S(2)}, u32[]{:S(2)}) collective-permute-start(bf16[2,16,3584]{2,1,0:T(8,128)(2,1)S(1)} %get-tuple-element.74), channel_id=1, source_target_pairs={{0,2},{1,3},{2,0},{3,1},{4,6},{5,7},{6,4},{7,5},{8,10},{9,11},{10,... | collective-permute-start | bytes 688136 | tf_op jit(solution)/shard_map/ppermute | solution.py:28
  24.6 21.2 %collective-permute-start.2 = (bf16[2,16,3584]{2,1,0:T(8,128)(2,1)S(1)}, bf16[2,16,3584]{2,1,0:T(8,128)(2,1)S(1)}, u32[]{:S(2)}, u32[]{:S(2)}) collective-permute-start(bf16[2,16,3584]{2,1,0:T(8,128)(2,1)S(1)} %get-tuple-element.75), channel_id=1, source_target_pairs={{0,4},{1,5},{2,6},{3,7},{4,0},{5,1},{6,2},{7,3},{8,12},{9,13},{10,... | collective-permute-start | bytes 688136 | tf_op jit(solution)/shard_map/ppermute | solution.py:28
  26.0 25.4 %collective-permute-start.3 = (bf16[2,16,3584]{2,1,0:T(8,128)(2,1)S(1)}, bf16[2,16,3584]{2,1,0:T(8,128)(2,1)S(1)}, u32[]{:S(2)}, u32[]{:S(2)}) collective-permute-start(bf16[2,16,3584]{2,1,0:T(8,128)(2,1)S(1)} %get-tuple-element.76), channel_id=1, source_target_pairs={{0,6},{1,7},{2,4},{3,5},{4,2},{5,3},{6,0},{7,1},{8,14},{9,15},{10,... | collective-permute-start | bytes 688136 | tf_op jit(solution)/shard_map/ppermute | solution.py:28
  51.5 21.0 %collective-permute-start.8 = (bf16[192,4096]{1,0:T(8,128)(2,1)S(1)}, bf16[192,4096]{1,0:T(8,128)(2,1)S(1)}, u32[]{:S(2)}, u32[]{:S(2)}) collective-permute-start(bf16[192,4096]{1,0:T(8,128)(2,1)S(1)} %copy-done.1), channel_id=1, source_target_pairs={{0,1},{1,0},{2,3},{3,2},{4,5},{5,4},{6,7},{7,6},{8,9},{9,8},{10,11... | collective-permute-start | bytes 4718600 | tf_op jit(solution)/shard_map/ppermute | solution.py:28
  51.6 21.0 %collective-permute-start.7 = (bf16[192,3584]{1,0:T(8,128)(2,1)}, bf16[192,3584]{1,0:T(8,128)(2,1)S(1)}, u32[]{:S(2)}, u32[]{:S(2)}) collective-permute-start(bf16[192,3584]{1,0:T(8,128)(2,1)} %bitcast.20), channel_id=1, source_target_pairs={{0,1},{1,0},{2,3},{3,2},{4,5},{5,4},{6,7},{7,6},{8,9},{9,8},{10,11... | collective-permute-start | bytes 4128776 | tf_op jit(solution)/shard_map/ppermute | solution.py:28
  52.1 15.2 %collective-permute-start.4 = (bf16[2,16,3584]{2,1,0:T(8,128)(2,1)S(1)}, bf16[2,16,3584]{2,1,0:T(8,128)(2,1)S(1)}, u32[]{:S(2)}, u32[]{:S(2)}) collective-permute-start(bf16[2,16,3584]{2,1,0:T(8,128)(2,1)S(1)} %add_all.1.mine_ref), channel_id=1, source_target_pairs={{0,8},{1,9},{2,10},{3,11},{4,12},{5,13},{6,14},{7,15},{8,0},{9,1},... | collective-permute-start | bytes 688136 | tf_op jit(solution)/shard_map/ppermute | solution.py:28
  57.2 10.5 %collective-permute-start.9 = (bf16[2,192,256]{2,1,0:T(8,128)(2,1)}, bf16[2,192,256]{2,1,0:T(8,128)(2,1)S(1)}, u32[]{:S(2)}, u32[]{:S(2)}) collective-permute-start(bf16[2,192,256]{2,1,0:T(8,128)(2,1)} %bitcast.24), channel_id=1, source_target_pairs={{0,1},{1,0},{2,3},{3,2},{4,5},{5,4},{6,7},{7,6},{8,9},{9,8},{10,11... | collective-permute-start | bytes 589832 | tf_op jit(solution)/shard_map/ppermute | solution.py:28
  67.5 5.0 %collective-permute-start.6 = (bf16[32,1792]{1,0:T(8,128)(2,1)S(1)}, bf16[32,1792]{1,0:T(8,128)(2,1)S(1)}, u32[]{:S(2)}, u32[]{:S(2)}) collective-permute-start(bf16[32,1792]{1,0:T(8,128)(2,1)S(1)} %bitcast.28), channel_id=1, source_target_pairs={{0,2},{1,3},{2,0},{3,1},{4,6},{5,7},{6,4},{7,5},{8,10},{9,11},{10,... | collective-permute-start | bytes 344072 | tf_op jit(solution)/shard_map/ppermute | solution.py:28
  67.6 5.0 %collective-permute-start.5 = (bf16[32,1792]{1,0:T(8,128)(2,1)S(1)}, bf16[32,1792]{1,0:T(8,128)(2,1)S(1)}, u32[]{:S(2)}, u32[]{:S(2)}) collective-permute-start(bf16[32,1792]{1,0:T(8,128)(2,1)S(1)} %bitcast.26), channel_id=1, source_target_pairs={{0,4},{1,5},{2,6},{3,7},{4,0},{5,1},{6,2},{7,3},{8,12},{9,13},{10,... | collective-permute-start | bytes 344072 | tf_op jit(solution)/shard_map/ppermute | solution.py:28
  67.7 0.9 copy-start.5
  72.6 7.9 %copy-start.2 = (bf16[3584,192]{0,1:T(8,128)(2,1)S(1)}, bf16[3584,192]{0,1:T(8,128)(2,1)}, u32[]{:S(2)}) copy-start(bf16[3584,192]{0,1:T(8,128)(2,1)} %param.13) | copy-start | bytes 4128772
  72.6 6.6 %collective-permute-start.10 = (bf16[64,1792]{1,0:T(8,128)(2,1)S(1)}, bf16[64,1792]{1,0:T(8,128)(2,1)S(1)}, u32[]{:S(2)}, u32[]{:S(2)}) collective-permute-start(bf16[64,1792]{1,0:T(8,128)(2,1)S(1)} %get-tuple-element.90.refs_0_), channel_id=1, source_target_pairs={{0,2},{1,3},{2,0},{3,1},{4,6},{5,7},{6,4},{7,5},{8,10},{9,11},{10,... | collective-permute-start | bytes 688136 | tf_op jit(solution)/shard_map/ppermute | solution.py:28
  74.5 6.0 %collective-permute-start.11 = (bf16[64,1792]{1,0:T(8,128)(2,1)S(1)}, bf16[64,1792]{1,0:T(8,128)(2,1)S(1)}, u32[]{:S(2)}, u32[]{:S(2)}) collective-permute-start(bf16[64,1792]{1,0:T(8,128)(2,1)S(1)} %get-tuple-element.91.refs_2_), channel_id=1, source_target_pairs={{0,4},{1,5},{2,6},{3,7},{4,0},{5,1},{6,2},{7,3},{8,12},{9,13},{10,... | collective-permute-start | bytes 688136 | tf_op jit(solution)/shard_map/ppermute | solution.py:28
  82.9 6.8 %collective-permute-start.12 = (bf16[4,144,256]{2,1,0:T(8,128)(2,1)S(1)}, bf16[4,144,256]{2,1,0:T(8,128)(2,1)S(1)}, u32[]{:S(2)}, u32[]{:S(2)}) collective-permute-start(bf16[4,144,256]{2,1,0:T(8,128)(2,1)S(1)} %get-tuple-element.106), channel_id=1, source_target_pairs={{0,2},{1,3},{2,0},{3,1},{4,6},{5,7},{6,4},{7,5},{8,10},{9,11},{10,... | collective-permute-start | bytes 884744 | tf_op jit(solution)/shard_map/ppermute | solution.py:28
  83.3 7.2 %collective-permute-start.13 = (bf16[4,144,256]{2,1,0:T(8,128)(2,1)S(1)}, bf16[4,144,256]{2,1,0:T(8,128)(2,1)S(1)}, u32[]{:S(2)}, u32[]{:S(2)}) collective-permute-start(bf16[4,144,256]{2,1,0:T(8,128)(2,1)S(1)} %get-tuple-element.107), channel_id=1, source_target_pairs={{0,4},{1,5},{2,6},{3,7},{4,0},{5,1},{6,2},{7,3},{8,12},{9,13},{10,... | collective-permute-start | bytes 884744 | tf_op jit(solution)/shard_map/ppermute | solution.py:28
  90.7 6.2 %collective-permute-start.14 = (bf16[2,144,256]{2,1,0:T(8,128)(2,1)S(1)}, bf16[2,144,256]{2,1,0:T(8,128)(2,1)S(1)}, u32[]{:S(2)}, u32[]{:S(2)}) collective-permute-start(bf16[2,144,256]{2,1,0:T(8,128)(2,1)S(1)} %get-tuple-element.114), channel_id=1, source_target_pairs={{0,4},{1,5},{2,6},{3,7},{4,0},{5,1},{6,2},{7,3},{8,12},{9,13},{10,... | collective-permute-start | bytes 442376 | tf_op jit(solution)/shard_map/ppermute | solution.py:28
  91.0 5.9 %collective-permute-start.15 = (bf16[2,144,256]{2,1,0:T(8,128)(2,1)S(1)}, bf16[2,144,256]{2,1,0:T(8,128)(2,1)S(1)}, u32[]{:S(2)}, u32[]{:S(2)}) collective-permute-start(bf16[2,144,256]{2,1,0:T(8,128)(2,1)S(1)} %get-tuple-element.116), channel_id=1, source_target_pairs={{0,2},{1,3},{2,0},{3,1},{4,6},{5,7},{6,4},{7,5},{8,10},{9,11},{10,... | collective-permute-start | bytes 442376 | tf_op jit(solution)/shard_map/ppermute | solution.py:28
  97.0 7.7 %collective-permute-start.16 = (bf16[2,1,144,256]{3,2,1,0:T(8,128)(2,1)S(1)}, bf16[2,1,144,256]{3,2,1,0:T(8,128)(2,1)S(1)}, u32[]{:S(2)}, u32[]{:S(2)}) collective-permute-start(bf16[2,1,144,256]{3,2,1,0:T(8,128)(2,1)S(1)} %get-tuple-element.119), channel_id=1, source_target_pairs={{0,8},{1,9},{2,10},{3,11},{4,12},{5,13},{6,14},{7,15},{8,0},{9,1},... | collective-permute-start | bytes 442376 | tf_op jit(solution)/shard_map/ppermute | solution.py:28
  105.4 1.3 %collective-permute-start.17 = (bf16[128,256]{1,0:T(8,128)(2,1)S(1)}, bf16[128,256]{1,0:T(8,128)(2,1)S(1)}, u32[]{:S(2)}, u32[]{:S(2)}) collective-permute-start(bf16[128,256]{1,0:T(8,128)(2,1)S(1)} %get-tuple-element.121), channel_id=1, source_target_pairs={{0,1},{1,0},{2,3},{3,2},{4,5},{5,4},{6,7},{7,6},{8,9},{9,8},{10,11... | collective-permute-start | bytes 196616 | tf_op jit(solution)/shard_map/ppermute | solution.py:28
  107.9 9.2 %collective-permute-start.22 = (bf16[2,160,128]{2,1,0:T(8,128)(2,1)S(1)}, bf16[2,160,128]{2,1,0:T(8,128)(2,1)S(1)}, u32[]{:S(2)}, u32[]{:S(2)}) collective-permute-start(bf16[2,160,128]{2,1,0:T(8,128)(2,1)S(1)} %get-tuple-element.128), channel_id=1, source_target_pairs={{0,12},{1,13},{2,14},{3,15},{4,8},{5,9},{6,10},{7,11},{8,4},{9,5},... | collective-permute-start | bytes 245768 | tf_op jit(solution)/shard_map/ppermute | solution.py:28
  110.2 8.1 %collective-permute-start.23 = (bf16[2,160,128]{2,1,0:T(8,128)(2,1)S(1)}, bf16[2,160,128]{2,1,0:T(8,128)(2,1)S(1)}, u32[]{:S(2)}, u32[]{:S(2)}) collective-permute-start(bf16[2,160,128]{2,1,0:T(8,128)(2,1)S(1)} %get-tuple-element.129), channel_id=1, source_target_pairs={{0,2},{1,3},{2,0},{3,1},{4,6},{5,7},{6,4},{7,5},{8,10},{9,11},{10,... | collective-permute-start | bytes 245768 | tf_op jit(solution)/shard_map/ppermute | solution.py:28
  110.6 9.8 %collective-permute-start.24 = (bf16[2,160,128]{2,1,0:T(8,128)(2,1)S(1)}, bf16[2,160,128]{2,1,0:T(8,128)(2,1)S(1)}, u32[]{:S(2)}, u32[]{:S(2)}) collective-permute-start(bf16[2,160,128]{2,1,0:T(8,128)(2,1)S(1)} %get-tuple-element.130), channel_id=1, source_target_pairs={{0,14},{1,15},{2,12},{3,13},{4,10},{5,11},{6,8},{7,9},{8,6},{9,7},... | collective-permute-start | bytes 245768 | tf_op jit(solution)/shard_map/ppermute | solution.py:28
  114.4 7.9 %collective-permute-start.18 = (bf16[2,160,128]{2,1,0:T(8,128)(2,1)S(1)}, bf16[2,160,128]{2,1,0:T(8,128)(2,1)S(1)}, u32[]{:S(2)}, u32[]{:S(2)}) collective-permute-start(bf16[2,160,128]{2,1,0:T(8,128)(2,1)S(1)} %get-tuple-element.122), channel_id=1, source_target_pairs={{0,8},{1,9},{2,10},{3,11},{4,12},{5,13},{6,14},{7,15},{8,0},{9,1},... | collective-permute-start | bytes 245768 | tf_op jit(solution)/shard_map/ppermute | solution.py:28
  114.5 7.8 %collective-permute-start.19 = (bf16[2,160,128]{2,1,0:T(8,128)(2,1)S(1)}, bf16[2,160,128]{2,1,0:T(8,128)(2,1)S(1)}, u32[]{:S(2)}, u32[]{:S(2)}) collective-permute-start(bf16[2,160,128]{2,1,0:T(8,128)(2,1)S(1)} %get-tuple-element.123), channel_id=1, source_target_pairs={{0,6},{1,7},{2,4},{3,5},{4,2},{5,3},{6,0},{7,1},{8,14},{9,15},{10,... | collective-permute-start | bytes 245768 | tf_op jit(solution)/shard_map/ppermute | solution.py:28
  117.1 8.3 %collective-permute-start.20 = (bf16[2,160,128]{2,1,0:T(8,128)(2,1)S(1)}, bf16[2,160,128]{2,1,0:T(8,128)(2,1)S(1)}, u32[]{:S(2)}, u32[]{:S(2)}) collective-permute-start(bf16[2,160,128]{2,1,0:T(8,128)(2,1)S(1)} %get-tuple-element.124), channel_id=1, source_target_pairs={{0,10},{1,11},{2,8},{3,9},{4,14},{5,15},{6,12},{7,13},{8,2},{9,3},... | collective-permute-start | bytes 245768 | tf_op jit(solution)/shard_map/ppermute | solution.py:28
  118.3 7.1 %collective-permute-start.21 = (bf16[2,160,128]{2,1,0:T(8,128)(2,1)S(1)}, bf16[2,160,128]{2,1,0:T(8,128)(2,1)S(1)}, u32[]{:S(2)}, u32[]{:S(2)}) collective-permute-start(bf16[2,160,128]{2,1,0:T(8,128)(2,1)S(1)} %get-tuple-element.125), channel_id=1, source_target_pairs={{0,4},{1,5},{2,6},{3,7},{4,0},{5,1},{6,2},{7,3},{8,12},{9,13},{10,... | collective-permute-start | bytes 245768 | tf_op jit(solution)/shard_map/ppermute | solution.py:28
  120.4 5.1 %collective-permute-start.26 = (bf16[4,160,128]{2,1,0:T(8,128)(2,1)S(1)}, bf16[4,160,128]{2,1,0:T(8,128)(2,1)S(1)}, u32[]{:S(2)}, u32[]{:S(2)}) collective-permute-start(bf16[4,160,128]{2,1,0:T(8,128)(2,1)S(1)} %gather_other.3), channel_id=1, source_target_pairs={{0,1},{1,0},{2,3},{3,2},{4,5},{5,4},{6,7},{7,6},{8,9},{9,8},{10,11... | collective-permute-start | bytes 491528 | tf_op jit(solution)/shard_map/ppermute | solution.py:28
  125.4 1.5 %collective-permute-start.25 = (bf16[4,160,128]{2,1,0:T(8,128)(2,1)S(1)}, bf16[4,160,128]{2,1,0:T(8,128)(2,1)S(1)}, u32[]{:S(2)}, u32[]{:S(2)}) collective-permute-start(bf16[4,160,128]{2,1,0:T(8,128)(2,1)S(1)} %gather_other.2), channel_id=1, source_target_pairs={{0,1},{1,0},{2,3},{3,2},{4,5},{5,4},{6,7},{7,6},{8,9},{9,8},{10,11... | collective-permute-start | bytes 491528 | tf_op jit(solution)/shard_map/ppermute | solution.py:28

commit v20 on v18

--- a/solution.py
+++ b/solution.py
@@ -125,13 +125,13 @@
 
 
 def slot_rows(chips, width):
-    per_slot = 2 * 128 // width
-    return chips * per_slot, -(-(chips * per_slot + 2) // 16) * 16
+    means, squares = chips * 2 * 128 // width, chips * 128 // width
+    return means, squares, -(-max(means + chips, squares + chips + 2) // 16) * 16
 
 
 def project_kernel(lanes, place_ref, *refs):
     pieces, refs = (refs[:2], refs[2:4]), refs[4:]
-    lines_ref, win0, win1, kv0, kv1, *outs, states, proj0, proj1, sums = refs
+    lines_ref, win0, win1, kv0, kv1, *outs, states, proj0, proj1, sums, keys_shift = refs
     chip = place_ref[3]
     half_chips = outs[0].shape[0]
     chips = 2 * half_chips
@@ -155,11 +155,12 @@
                     proj[pl.ds(start, share), :] = block
                 else:
                     proj[pl.ds(start, share), :] += block
-    value0, value1 = proj0[...], proj1[...]
-    first = jnp.sum(value0, 1, keepdims=True) + jnp.sum(value1, 1, keepdims=True)
-    second = jnp.sum(value0 * value0, 1, keepdims=True) + jnp.sum(value1 * value1, 1, keepdims=True)
+    mean = jnp.sum(proj0[...], 1, keepdims=True) + jnp.sum(proj1[...], 1, keepdims=True)
+    mean = mean / (2 * proj0.shape[1])
+    value0, value1 = proj0[...] - mean, proj1[...] - mean
+    square = jnp.sum(value0 * value0, 1, keepdims=True) + jnp.sum(value1 * value1, 1, keepdims=True)
     lane = lax.broadcasted_iota(jnp.int32, sums.shape, 1)
-    sums[...] = jnp.where(lane == 0, first, second).T
+    sums[...] = jnp.where(lane == 0, mean, square).T
     left = []
     for side, value in enumerate((value0, value1)):
         lines = lines_ref[side]
@@ -167,31 +168,40 @@
         lines, scale = jnp.where(row < 4, lines, 0.0), lines[4:5]
         left.append(jnp.concatenate([value * scale, lines], 0).astype(jnp.bfloat16))
     width = outs[0].shape[2]
-    slots, extra = slot_rows(chips, width)
-    per_slot = slots // chips
+    means, squares, extra = slot_rows(chips, width)
     row = lax.broadcasted_iota(jnp.int32, (extra, width), 0)
     column = lax.broadcasted_iota(jnp.int32, (extra, width), 1)
     half = kv0.shape[1] // 2
     for lane, order in enumerate(lanes):
         line = sums[lane : lane + 1, :]
-        high = line.astype(jnp.bfloat16).astype(jnp.float32)
-        low = line - high
-        if per_slot == 1:
-            line = jnp.concatenate([high, low], 1)
+        if lane == 0:
+            high = line.astype(jnp.bfloat16).astype(jnp.float32)
+            low = line - high
+            if width > 128:
+                line = jnp.concatenate([high, low], 1)
+            else:
+                line = jnp.where(row % 2 == 0, high, low)
+            line = jnp.where(row // (means // chips) == chip, line, 0.0)
         else:
-            line = jnp.where(row % 2 == 0, high, low)
-        line = jnp.where(row // per_slot == chip, line, 0.0)
+            place = row * (width // 128) + column // 128
+            line = jnp.concatenate([line] * (width // 128), 1)
+            line = jnp.where(place == chip, line, 0.0)
+        base = (means, squares)[lane]
         for at in reversed(range(chips)):
             out_ref, to = outs[2 * lane + at // half_chips], at % half_chips
-            start = lane * half + (chip ^ member(at, order)) * width
-            columns = pl.ds(pl.multiple_of(start, width), width)
+            target = chip ^ member(at, order)
+            columns = pl.ds(pl.multiple_of(lane * half + target * width, width), width)
             value = jnp.dot(left[0], kv0[:, columns], preferred_element_type=jnp.float32)
             value += jnp.dot(left[1], kv1[:, columns], preferred_element_type=jnp.float32)
             out_ref[to, :rows, :] = value[:rows].astype(out_ref.dtype)
-            below = jnp.where(row == slots, value[rows : rows + 1] + value[rows + 1 : rows + 2], line)
-            below = jnp.where(
-                row == slots + 1, value[rows + 2 : rows + 3] + value[rows + 3 : rows + 4], below
-            )
+            scale = value[rows : rows + 1] + value[rows + 1 : rows + 2]
+            shift = value[rows + 2 : rows + 3] + value[rows + 3 : rows + 4]
+            below = jnp.where(row == base + chip, scale, line)
+            if lane == 0:
+                keys_shift[target] = jnp.broadcast_to(shift, keys_shift.shape[1:])
+            else:
+                below = jnp.where(row == base + chips, shift, below)
+                below = jnp.where(row == base + chips + 1, keys_shift[target][:1], below)
             out_ref[to, rows:, :] = below.astype(out_ref.dtype)
 
 
@@ -201,7 +211,7 @@
     features, depth = win0.shape
     total = kv0.shape[1]
     width = total // 2 // chips
-    extra = slot_rows(chips, width)[1]
+    extra = slot_rows(chips, width)[2]
     out = jax.ShapeDtypeStruct((chips // 2, rows + extra, width), jnp.bfloat16)
     return pl.pallas_call(
         functools.partial(project_kernel, lanes),
@@ -213,6 +223,7 @@
             pltpu.VMEM((rows, features), jnp.float32),
             pltpu.VMEM((rows, features), jnp.float32),
             pltpu.VMEM((rows, 128), jnp.float32),
+            pltpu.VMEM((chips, 8, width), jnp.float32),
         ],
         compiler_params=params(14),
         cost_estimate=pl.CostEstimate(
@@ -229,22 +240,29 @@
     core = place_ref[2]
     rows = mine_ref.shape[0]
     width = keep0.shape[2]
-    slots = slot_rows(chips, width)[0]
+    means, squares, _ = slot_rows(chips, width)
     totals = [keep[0] + came_ref[lane, 0].astype(jnp.float32) for lane, keep in enumerate((keep0, keep1))]
-    sums = []
-    for total in totals:
-        line = jnp.sum(total[rows : rows + slots], 0, keepdims=True)
-        if width > 128:
-            line = line[:, :128] + line[:, 128:]
-        sums.append(line)
-    mean_val = sums[0] / model_width
-    scale = lax.rsqrt(sums[1] / model_width - mean_val * mean_val + epsilon)
-    mean_val = jnp.broadcast_to(mean_val, (rows, rows)).T[:, 0:1]
-    scale = jnp.broadcast_to(scale, (rows, rows)).T[:, 0:1]
+    below = [total[rows:] for total in totals]
+    if width > 128:
+        mean = below[0][:chips, :128] + below[0][:chips, 128:]
+    else:
+        lines = [below[0][2 * at : 2 * at + 1] + below[0][2 * at + 1 : 2 * at + 2] for at in range(chips)]
+        mean = jnp.concatenate(lines, 0)
+    away = mean - jnp.mean(mean, 0, keepdims=True)
+    square = jnp.sum(below[1][:squares], 0, keepdims=True)
+    square = sum(square[:, at : at + 128] for at in range(0, width, 128))
+    square += jnp.sum(away * away, 0, keepdims=True) * (model_width / chips)
+    scale = lax.rsqrt(square / model_width + epsilon)
+    turned = jnp.concatenate([away, scale, jnp.zeros((rows - chips - 1, rows), jnp.float32)], 0).T
+    scale = turned[:, chips : chips + 1]
     texts = []
-    for total in totals:
-        text = (total[:rows] - mean_val * total[rows + slots : rows + slots + 1]) * scale
-        texts.append(text + total[rows + slots + 1 : rows + slots + 2])
+    for lane, total in enumerate(totals):
+        base = (means, squares)[lane]
+        text = total[:rows]
+        for at in range(chips):
+            text += turned[:, at : at + 1] * below[lane][base + at : base + at + 1]
+        shift = below[1][squares + chips + 1 - lane : squares + chips + 2 - lane]
+        texts.append(text * scale + shift)
     for part, text in enumerate(texts):
         span = slice(part * HEAD_DIM, (part + 1) * HEAD_DIM)
         if width > HEAD_DIM:

time: 128 us -> 128 us (level)
  no operation moved by 1% of the time
where the time goes in v20:
time: 128 us
  waiting for transfers between devices  60.8 us (48%)
  starting transfers between devices  36.8 us (29%)
  Pallas kernels  21.1 us (16%)
  local copies, waits for them, and re-layouts  7.06 us (6%)
  between operations  2.25 us (2%)
    ppermute x29, waiting for transfers between devices, swap(): return lax.ppermute(value, 'seq', [(i, i ^ mask) for i in range(devices)])  60.8 us
    ppermute x29, starting transfers between devices, swap(): return lax.ppermute(value, 'seq', [(i, i ^ mask) for i in range(devices)])  29.3 us
    pallas_call x2, Pallas kernels, image_attention(): pl.pallas_call(functools.partial(image_kernel, factor, masks, img_dev), o...  8.03 us
    all_to_all x1, starting transfers between devices, exchange(): return lax.all_to_all(rows, 'seq', split_axis=0, concat_axis=0, tiled=True)  7.49 us
    unnamed x14, local copies, waits for them, and re-layouts  5.31 us
    pallas_call x1, Pallas kernels, encoder(): pl.pallas_call(functools.partial(encoder_kernel, lanes), out_shape=(out,)...  3.47 us
  transfers between devices with their start and end apart: 30, of which 20 were waited for; matrix products, arithmetic and copies ran while one was open for 0% of the time, Pallas kernels for 10%

profile of v20, /device:TPU:0, one launch (start us, length us, event | category | flops | bytes accessed | tf_op | source)
XLA Modules:
  0.0 128.0 jit_solution(15159928306832801511)
XLA Ops:
  0.6 1.6 %copy.12 = bf16[1,128,2,2048]{3,1,2,0:T(8,128)(2,1)S(1)} copy(bf16[1,128,2,2048]{3,2,1,0:T(2,128)(2,1)} %param.19) | data formatting | bytes 2097152 | tf_op jit(solution)/shard_map/optimization_barrier | solution.py:647
  2.3 1.0 copy-done.4
  3.3 1.4 %pack.1 = bf16[16,384,128]{2,1,0:T(8,128)(2,1)} custom-call(bf16[128,2048]{1,0:T(8,128)(2,1)S(1)} %bitcast.25, bf16[128,2048]{1,0:T(8,128)(2,1)S(1)} %get-tuple-element.147.keys_ref, bf16[128,2048]{1,0:T(8,128)(2,1)S(1)} %get-tuple-element.146.values_ref), custom_call_target="tpu_custom_call" | custom-call | bytes 3145728 | tf_op jit(solution)/shard_map/pack/pallas_call | solution.py:306
  4.7 7.5 %all-to-all-start = ((bf16[16,384,128]{2,1,0:T(8,128)(2,1)}), bf16[16,384,128]{2,1,0:T(8,128)(2,1)S(1)}, u32[]{:S(2)}, u32[]{:S(2)}) async-start(bf16[16,384,128]{2,1,0:T(8,128)(2,1)} %pack.1), calls=%async_computation | async-start | bytes 3145728 | tf_op jit(solution)/shard_map/all_to_all | solution.py:645
  12.9 0.1 stack.19.place_ref
  13.0 3.4 %copy-done = bf16[1184,3584]{1,0:T(8,128)(2,1)S(1)} copy-done((bf16[1184,3584]{1,0:T(8,128)(2,1)S(1)}, bf16[1184,3584]{1,0:T(8,128)(2,1)}, u32[]{:S(2)}) %copy-start) | copy-done | bytes 8486936
  16.4 3.5 %encoder.1 = (bf16[8,16,1792]{2,1,0:T(8,128)(2,1)S(1)}, bf16[8,16,1792]{2,1,0:T(8,128)(2,1)S(1)}, bf16[8,16,1792]{2,1,0:T(8,128)(2,1)S(1)}, bf16[8,16,1792]{2,1,0:T(8,128)(2,1)S(1)}) custom-call(s32[5]{0:T(128)S(1)} %stack.19.place_ref, bf16[1184,256]{1,0:T(8,128)(2,1)S(1)} %bitcast.24, bf16[1184,3584]{1,0:T(8,128)(2,1)S(1)} %copy-done), custom_call_target="tpu_custom_call" | custom-call | flops 2172649472 | bytes 10928128 | tf_op jit(solution)/shard_map/encoder/pallas_call | solution.py:84
  19.8 0.5 collective-permute-start
  20.3 0.1 collective-permute-start.1
  20.4 1.3 %collective-permute-done.refs_1_ = bf16[8,16,1792]{2,1,0:T(8,128)(2,1)S(1)} collective-permute-done((bf16[8,16,1792]{2,1,0:T(8,128)(2,1)S(1)}, bf16[8,16,1792]{2,1,0:T(8,128)(2,1)S(1)}, u32[]{:S(2)}, u32[]{:S(2)}) %collective-permute-start) | collective-permute-done | bytes 458784 | tf_op jit(solution)/shard_map/ppermute | solution.py:28
  21.7 0.7 collective-permute-done.1.refs_3_
  22.4 0.2 add_halves.4
  22.6 2.0 %collective-permute-start.2 = (bf16[4,16,1792]{2,1,0:T(8,128)(2,1)S(1)}, bf16[4,16,1792]{2,1,0:T(8,128)(2,1)S(1)}, u32[]{:S(2)}, u32[]{:S(2)}) collective-permute-start(bf16[4,16,1792]{2,1,0:T(8,128)(2,1)S(1)} %get-tuple-element.82), channel_id=1, source_target_pairs={{0,2},{1,3},{2,0},{3,1},{4,6},{5,7},{6,4},{7,5},{8,10},{9,11},{10,... | collective-permute-start | bytes 688136 | tf_op jit(solution)/shard_map/ppermute | solution.py:28
  24.6 1.5 %collective-permute-start.3 = (bf16[4,16,1792]{2,1,0:T(8,128)(2,1)S(1)}, bf16[4,16,1792]{2,1,0:T(8,128)(2,1)S(1)}, u32[]{:S(2)}, u32[]{:S(2)}) collective-permute-start(bf16[4,16,1792]{2,1,0:T(8,128)(2,1)S(1)} %get-tuple-element.84), channel_id=1, source_target_pairs={{0,4},{1,5},{2,6},{3,7},{4,0},{5,1},{6,2},{7,3},{8,12},{9,13},{10,... | collective-permute-start | bytes 688136 | tf_op jit(solution)/shard_map/ppermute | solution.py:28
  26.0 10.1 %collective-permute-done.2.refs_1_ = bf16[4,16,1792]{2,1,0:T(8,128)(2,1)S(1)} collective-permute-done((bf16[4,16,1792]{2,1,0:T(8,128)(2,1)S(1)}, bf16[4,16,1792]{2,1,0:T(8,128)(2,1)S(1)}, u32[]{:S(2)}, u32[]{:S(2)}) %collective-permute-start.2) | collective-permute-done | bytes 229408 | tf_op jit(solution)/shard_map/ppermute | solution.py:28
  36.1 7.6 %collective-permute-done.3.refs_3_ = bf16[4,16,1792]{2,1,0:T(8,128)(2,1)S(1)} collective-permute-done((bf16[4,16,1792]{2,1,0:T(8,128)(2,1)S(1)}, bf16[4,16,1792]{2,1,0:T(8,128)(2,1)S(1)}, u32[]{:S(2)}, u32[]{:S(2)}) %collective-permute-start.3) | collective-permute-done | bytes 229408 | tf_op jit(solution)/shard_map/ppermute | solution.py:28
  43.7 0.1 add_halves.5
  43.7 2.5 %collective-permute-start.4 = (bf16[2,16,1792]{2,1,0:T(8,128)(2,1)S(1)}, bf16[2,16,1792]{2,1,0:T(8,128)(2,1)S(1)}, u32[]{:S(2)}, u32[]{:S(2)}) collective-permute-start(bf16[2,16,1792]{2,1,0:T(8,128)(2,1)S(1)} %get-tuple-element.86), channel_id=1, source_target_pairs={{0,4},{1,5},{2,6},{3,7},{4,0},{5,1},{6,2},{7,3},{8,12},{9,13},{10,... | collective-permute-start | bytes 344072 | tf_op jit(solution)/shard_map/ppermute | solution.py:28
  46.3 1.7 %collective-permute-start.5 = (bf16[2,16,1792]{2,1,0:T(8,128)(2,1)S(1)}, bf16[2,16,1792]{2,1,0:T(8,128)(2,1)S(1)}, u32[]{:S(2)}, u32[]{:S(2)}) collective-permute-start(bf16[2,16,1792]{2,1,0:T(8,128)(2,1)S(1)} %get-tuple-element.88), channel_id=1, source_target_pairs={{0,2},{1,3},{2,0},{3,1},{4,6},{5,7},{6,4},{7,5},{8,10},{9,11},{10,... | collective-permute-start | bytes 344072 | tf_op jit(solution)/shard_map/ppermute | solution.py:28
  48.0 1.5 %collective-permute-done.4.got0 = bf16[2,16,1792]{2,1,0:T(8,128)(2,1)S(1)} collective-permute-done((bf16[2,16,1792]{2,1,0:T(8,128)(2,1)S(1)}, bf16[2,16,1792]{2,1,0:T(8,128)(2,1)S(1)}, u32[]{:S(2)}, u32[]{:S(2)}) %collective-permute-start.4) | collective-permute-done | bytes 114720 | tf_op jit(solution)/shard_map/ppermute | solution.py:28
  49.5 1.6 %collective-permute-done.5.got1 = bf16[2,16,1792]{2,1,0:T(8,128)(2,1)S(1)} collective-permute-done((bf16[2,16,1792]{2,1,0:T(8,128)(2,1)S(1)}, bf16[2,16,1792]{2,1,0:T(8,128)(2,1)S(1)}, u32[]{:S(2)}, u32[]{:S(2)}) %collective-permute-start.5) | collective-permute-done | bytes 114720 | tf_op jit(solution)/shard_map/ppermute | solution.py:28
  51.1 0.1 collective-permute-start.10
  51.2 0.5 collective-permute-start.9
  51.7 2.9 %collective-permute-start.6 = (bf16[2,2,16,1792]{3,2,1,0:T(8,128)(2,1)S(1)}, bf16[2,2,16,1792]{3,2,1,0:T(8,128)(2,1)S(1)}, u32[]{:S(2)}, u32[]{:S(2)}) collective-permute-start(bf16[2,2,16,1792]{3,2,1,0:T(8,128)(2,1)S(1)} %add_all.1.mine_ref), channel_id=1, source_target_pairs={{0,8},{1,9},{2,10},{3,11},{4,12},{5,13},{6,14},{7,15},{8,0},{9,1},... | collective-permute-start | bytes 688136 | tf_op jit(solution)/shard_map/ppermute | solution.py:28
  55.3 0.1 collective-permute-start.11
  55.3 10.0 %collective-permute-done.6.got_ref = bf16[2,2,16,1792]{3,2,1,0:T(8,128)(2,1)S(1)} collective-permute-done((bf16[2,2,16,1792]{3,2,1,0:T(8,128)(2,1)S(1)}, bf16[2,2,16,1792]{3,2,1,0:T(8,128)(2,1)S(1)}, u32[]{:S(2)}, u32[]{:S(2)}) %collective-permute-start.6) | collective-permute-done | bytes 229408 | tf_op jit(solution)/shard_map/ppermute | solution.py:28
  65.3 0.2 normalize.1
  65.5 1.6 %collective-permute-start.8 = (bf16[32,1792]{1,0:T(8,128)(2,1)S(1)}, bf16[32,1792]{1,0:T(8,128)(2,1)S(1)}, u32[]{:S(2)}, u32[]{:S(2)}) collective-permute-start(bf16[32,1792]{1,0:T(8,128)(2,1)S(1)} %bitcast.30), channel_id=1, source_target_pairs={{0,2},{1,3},{2,0},{3,1},{4,6},{5,7},{6,4},{7,5},{8,10},{9,11},{10,... | collective-permute-start | bytes 344072 | tf_op jit(solution)/shard_map/ppermute | solution.py:28
  67.2 0.9 copy-done.5
  68.1 0.2 modulation.1.refs_4_
  68.3 2.1 %collective-permute-done.8.got1 = bf16[32,1792]{1,0:T(8,128)(2,1)S(1)} collective-permute-done((bf16[32,1792]{1,0:T(8,128)(2,1)S(1)}, bf16[32,1792]{1,0:T(8,128)(2,1)S(1)}, u32[]{:S(2)}, u32[]{:S(2)}) %collective-permute-start.8) | collective-permute-done | bytes 114720 | tf_op jit(solution)/shard_map/ppermute | solution.py:28
  70.4 1.5 %collective-permute-done.7.got0 = bf16[32,1792]{1,0:T(8,128)(2,1)S(1)} collective-permute-done((bf16[32,1792]{1,0:T(8,128)(2,1)S(1)}, bf16[32,1792]{1,0:T(8,128)(2,1)S(1)}, u32[]{:S(2)}, u32[]{:S(2)}) %collective-permute-start.7) | collective-permute-done | bytes 114720 | tf_op jit(solution)/shard_map/ppermute | solution.py:28
  71.9 0.6 collective-permute-start.12
  72.5 0.4 collective-permute-start.13
  72.9 3.9 %image_attention.2 = (f32[1024,256]{1,0:T(8,128)S(1)}, f32[1024,128]{1,0:T(8,128)S(1)}) custom-call(s32[5]{0:T(128)S(1)} %stack.19.place_ref, bf16[16,384,128]{2,1,0:T(8,128)(2,1)S(1)} %all-to-all-done.packed_ref), custom_call_target="tpu_custom_call" | custom-call | flops 1073741824 | bytes 2359296 | tf_op jit(solution)/shard_map/image_attention/pallas_call | solution.py:383
  76.8 1.2 collective-permute-done.12.refs_1_
  78.0 0.5 collective-permute-done.13.refs_3_
  78.6 2.4 %project.1 = (bf16[4,144,256]{2,1,0:T(8,128)(2,1)S(1)}, bf16[4,144,256]{2,1,0:T(8,128)(2,1)S(1)}, bf16[4,144,256]{2,1,0:T(8,128)(2,1)S(1)}, bf16[4,144,256]{2,1,0:T(8,128)(2,1)S(1)}) custom-call(s32[5]{0:T(128)S(1)} %stack.19.place_ref, bf16[64,1792]{1,0:T(8,128)(2,1)S(1)} %get-tuple-element.102.refs_0_, ...), custom_call_target="tpu_custom_call" | custom-call | flops 754974720 | bytes 7864320 | tf_op jit(solution)/shard_map/project/pallas_call | solution.py:216
  81.0 1.6 %collective-permute-start.14 = (bf16[4,144,256]{2,1,0:T(8,128)(2,1)S(1)}, bf16[4,144,256]{2,1,0:T(8,128)(2,1)S(1)}, u32[]{:S(2)}, u32[]{:S(2)}) collective-permute-start(bf16[4,144,256]{2,1,0:T(8,128)(2,1)S(1)} %get-tuple-element.118), channel_id=1, source_target_pairs={{0,2},{1,3},{2,0},{3,1},{4,6},{5,7},{6,4},{7,5},{8,10},{9,11},{10,... | collective-permute-start | bytes 884744 | tf_op jit(solution)/shard_map/ppermute | solution.py:28
  82.5 0.1 collective-permute-start.15
  82.6 4.1 %image_attention.3 = (f32[1024,256]{1,0:T(8,128)S(1)}, f32[1024,128]{1,0:T(8,128)S(1)}) custom-call(s32[5]{0:T(128)S(1)} %stack.19.place_ref, bf16[16,384,128]{2,1,0:T(8,128)(2,1)S(1)} %all-to-all-done.packed_ref), custom_call_target="tpu_custom_call" | custom-call | flops 1073741824 | bytes 2359296 | tf_op jit(solution)/shard_map/image_attention/pallas_call | solution.py:383
  86.7 1.0 collective-permute-done.14.refs_1_
  87.8 2.8 %collective-permute-done.15.refs_3_ = bf16[4,144,256]{2,1,0:T(8,128)(2,1)S(1)} collective-permute-done((bf16[4,144,256]{2,1,0:T(8,128)(2,1)S(1)}, bf16[4,144,256]{2,1,0:T(8,128)(2,1)S(1)}, u32[]{:S(2)}, u32[]{:S(2)}) %collective-permute-start.15) | collective-permute-done | bytes 294944 | tf_op jit(solution)/shard_map/ppermute | solution.py:28
  90.6 0.1 add_halves.6
  90.7 0.1 collective-permute-start.16
  90.8 0.6 collective-permute-start.17
  91.4 6.1 %collective-permute-done.16.refs_1_ = bf16[2,144,256]{2,1,0:T(8,128)(2,1)S(1)} collective-permute-done((bf16[2,144,256]{2,1,0:T(8,128)(2,1)S(1)}, bf16[2,144,256]{2,1,0:T(8,128)(2,1)S(1)}, u32[]{:S(2)}, u32[]{:S(2)}) %collective-permute-start.16) | collective-permute-done | bytes 147488 | tf_op jit(solution)/shard_map/ppermute | solution.py:28
  97.5 1.3 collective-permute-start.18
  98.8 6.3 %collective-permute-done.18.refs_2_ = bf16[2,1,144,256]{3,2,1,0:T(8,128)(2,1)S(1)} collective-permute-done((bf16[2,1,144,256]{3,2,1,0:T(8,128)(2,1)S(1)}, bf16[2,1,144,256]{3,2,1,0:T(8,128)(2,1)S(1)}, u32[]{:S(2)}, u32[]{:S(2)}) %collective-permute-start.18) | collective-permute-done | bytes 147488 | tf_op jit(solution)/shard_map/ppermute | solution.py:28
  105.1 0.9 combine.1
  106.1 1.2 collective-permute-done.19.got_ref
  107.4 1.2 finish.3
  108.6 1.4 %collective-permute-start.24 = (bf16[2,160,128]{2,1,0:T(8,128)(2,1)S(1)}, bf16[2,160,128]{2,1,0:T(8,128)(2,1)S(1)}, u32[]{:S(2)}, u32[]{:S(2)}) collective-permute-start(bf16[2,160,128]{2,1,0:T(8,128)(2,1)S(1)} %get-tuple-element.140), channel_id=1, source_target_pairs={{0,12},{1,13},{2,14},{3,15},{4,8},{5,9},{6,10},{7,11},{8,4},{9,5},... | collective-permute-start | bytes 245768 | tf_op jit(solution)/shard_map/ppermute | solution.py:28
  110.0 0.8 collective-permute-start.25
  110.8 3.1 %collective-permute-start.26 = (bf16[2,160,128]{2,1,0:T(8,128)(2,1)S(1)}, bf16[2,160,128]{2,1,0:T(8,128)(2,1)S(1)}, u32[]{:S(2)}, u32[]{:S(2)}) collective-permute-start(bf16[2,160,128]{2,1,0:T(8,128)(2,1)S(1)} %get-tuple-element.142), channel_id=1, source_target_pairs={{0,14},{1,15},{2,12},{3,13},{4,10},{5,11},{6,8},{7,9},{8,6},{9,7},... | collective-permute-start | bytes 245768 | tf_op jit(solution)/shard_map/ppermute | solution.py:28
  113.9 1.2 finish.2
  115.2 2.2 %collective-permute-start.21 = (bf16[2,160,128]{2,1,0:T(8,128)(2,1)S(1)}, bf16[2,160,128]{2,1,0:T(8,128)(2,1)S(1)}, u32[]{:S(2)}, u32[]{:S(2)}) collective-permute-start(bf16[2,160,128]{2,1,0:T(8,128)(2,1)S(1)} %get-tuple-element.135), channel_id=1, source_target_pairs={{0,6},{1,7},{2,4},{3,5},{4,2},{5,3},{6,0},{7,1},{8,14},{9,15},{10,... | collective-permute-start | bytes 245768 | tf_op jit(solution)/shard_map/ppermute | solution.py:28
  117.3 0.7 collective-permute-start.22
  118.1 3.0 %collective-permute-start.23 = (bf16[2,160,128]{2,1,0:T(8,128)(2,1)S(1)}, bf16[2,160,128]{2,1,0:T(8,128)(2,1)S(1)}, u32[]{:S(2)}, u32[]{:S(2)}) collective-permute-start(bf16[2,160,128]{2,1,0:T(8,128)(2,1)S(1)} %get-tuple-element.137), channel_id=1, source_target_pairs={{0,4},{1,5},{2,6},{3,7},{4,0},{5,1},{6,2},{7,3},{8,12},{9,13},{10,... | collective-permute-start | bytes 245768 | tf_op jit(solution)/shard_map/ppermute | solution.py:28
  121.1 1.2 collective-permute-done.20.refs_0_
  122.4 2.1 %collective-permute-done.21.refs_1_ = bf16[2,160,128]{2,1,0:T(8,128)(2,1)S(1)} collective-permute-done((bf16[2,160,128]{2,1,0:T(8,128)(2,1)S(1)}, bf16[2,160,128]{2,1,0:T(8,128)(2,1)S(1)}, u32[]{:S(2)}, u32[]{:S(2)}) %collective-permute-start.21) | collective-permute-done | bytes 81952 | tf_op jit(solution)/shard_map/ppermute | solution.py:28
  124.4 0.6 collective-permute-done.22.refs_2_
  125.1 1.4 %collective-permute-done.27.refs_8_ = bf16[4,160,128]{2,1,0:T(8,128)(2,1)S(1)} collective-permute-done((bf16[4,160,128]{2,1,0:T(8,128)(2,1)S(1)}, bf16[4,160,128]{2,1,0:T(8,128)(2,1)S(1)}, u32[]{:S(2)}, u32[]{:S(2)}) %collective-permute-start.27) | collective-permute-done | bytes 163872 | tf_op jit(solution)/shard_map/ppermute | solution.py:28
  126.5 1.5 %unpack.1 = (bf16[128,2048]{1,0:T(8,128)(2,1)}, bf16[16,4096]{1,0:T(8,128)(2,1)}) custom-call(s32[5]{0:T(128)S(1)} %stack.19.place_ref, bf16[2,160,128]{2,1,0:T(8,128)(2,1)S(1)} %collective-permute-done.20.refs_0_, bf16[2,160,128]{2,1,0:T(8,128)(2,1)S(1)} %collective-permute-done.21.refs_1_, bf16[2,160,128]{2,1,0:T(8,128)(2,1)S(1)} %collective-permute-done.22.refs_2_, ...), custom_call_target="tpu_custom_call" | custom-call | tf_op jit(solution)/shard_map/unpack/pallas_call | solution.py:341
  (35 shorter events, 0.6 us)
Async XLA Ops:
  2.2 1.0 copy-start.4
  4.7 8.3 %copy-start.3 = (bf16[1,256,1184]{1,2,0:T(8,128)(2,1)S(1)}, bf16[1,256,1184]{1,2,0:T(8,128)(2,1)}, u32[]{:S(2)}) copy-start(bf16[1,256,1184]{1,2,0:T(8,128)(2,1)} %param.10) | copy-start | bytes 1818628
  4.7 46.4 %all-to-all-start = ((bf16[16,384,128]{2,1,0:T(8,128)(2,1)}), bf16[16,384,128]{2,1,0:T(8,128)(2,1)S(1)}, u32[]{:S(2)}, u32[]{:S(2)}) async-start(bf16[16,384,128]{2,1,0:T(8,128)(2,1)} %pack.1), calls=%async_computation | async-start | bytes 3145728 | tf_op jit(solution)/shard_map/all_to_all | solution.py:645
  13.0 3.4 %copy-start = (bf16[1184,3584]{1,0:T(8,128)(2,1)S(1)}, bf16[1184,3584]{1,0:T(8,128)(2,1)}, u32[]{:S(2)}) copy-start(bf16[1184,3584]{1,0:T(8,128)(2,1)} %weight_ref.1) | copy-start | bytes 25460740
  19.8 1.9 %collective-permute-start = (bf16[8,16,1792]{2,1,0:T(8,128)(2,1)S(1)}, bf16[8,16,1792]{2,1,0:T(8,128)(2,1)S(1)}, u32[]{:S(2)}, u32[]{:S(2)}) collective-permute-start(bf16[8,16,1792]{2,1,0:T(8,128)(2,1)S(1)} %get-tuple-element.78), channel_id=1, source_target_pairs={{0,1},{1,0},{2,3},{3,2},{4,5},{5,4},{6,7},{7,6},{8,9},{9,8},{10,11... | collective-permute-start | bytes 1376264 | tf_op jit(solution)/shard_map/ppermute | solution.py:28
  20.3 2.1 %collective-permute-start.1 = (bf16[8,16,1792]{2,1,0:T(8,128)(2,1)S(1)}, bf16[8,16,1792]{2,1,0:T(8,128)(2,1)S(1)}, u32[]{:S(2)}, u32[]{:S(2)}) collective-permute-start(bf16[8,16,1792]{2,1,0:T(8,128)(2,1)S(1)} %get-tuple-element.80), channel_id=1, source_target_pairs={{0,1},{1,0},{2,3},{3,2},{4,5},{5,4},{6,7},{7,6},{8,9},{9,8},{10,11... | collective-permute-start | bytes 1376264 | tf_op jit(solution)/shard_map/ppermute | solution.py:28
  22.6 28.5 %copy-start.1 = (bf16[192,4096]{1,0:T(8,128)(2,1)S(1)}, bf16[192,4096]{1,0:T(8,128)(2,1)}, u32[]{:S(2)}) copy-start(bf16[192,4096]{1,0:T(8,128)(2,1)} %refs_7_.1) | copy-start | bytes 4718596
  22.6 32.6 %copy-start.6 = (bf16[3584]{0:T(1024)(128)(2,1)S(1)}, bf16[3584]{0:T(1024)(128)(2,1)}, u32[]{:S(2)}) copy-start(bf16[3584]{0:T(1024)(128)(2,1)} %param.12) | copy-start | bytes 21508
  22.6 13.5 %collective-permute-start.2 = (bf16[4,16,1792]{2,1,0:T(8,128)(2,1)S(1)}, bf16[4,16,1792]{2,1,0:T(8,128)(2,1)S(1)}, u32[]{:S(2)}, u32[]{:S(2)}) collective-permute-start(bf16[4,16,1792]{2,1,0:T(8,128)(2,1)S(1)} %get-tuple-element.82), channel_id=1, source_target_pairs={{0,2},{1,3},{2,0},{3,1},{4,6},{5,7},{6,4},{7,5},{8,10},{9,11},{10,... | collective-permute-start | bytes 688136 | tf_op jit(solution)/shard_map/ppermute | solution.py:28
  24.6 19.1 %collective-permute-start.3 = (bf16[4,16,1792]{2,1,0:T(8,128)(2,1)S(1)}, bf16[4,16,1792]{2,1,0:T(8,128)(2,1)S(1)}, u32[]{:S(2)}, u32[]{:S(2)}) collective-permute-start(bf16[4,16,1792]{2,1,0:T(8,128)(2,1)S(1)} %get-tuple-element.84), channel_id=1, source_target_pairs={{0,4},{1,5},{2,6},{3,7},{4,0},{5,1},{6,2},{7,3},{8,12},{9,13},{10,... | collective-permute-start | bytes 688136 | tf_op jit(solution)/shard_map/ppermute | solution.py:28
  43.7 5.8 %collective-permute-start.4 = (bf16[2,16,1792]{2,1,0:T(8,128)(2,1)S(1)}, bf16[2,16,1792]{2,1,0:T(8,128)(2,1)S(1)}, u32[]{:S(2)}, u32[]{:S(2)}) collective-permute-start(bf16[2,16,1792]{2,1,0:T(8,128)(2,1)S(1)} %get-tuple-element.86), channel_id=1, source_target_pairs={{0,4},{1,5},{2,6},{3,7},{4,0},{5,1},{6,2},{7,3},{8,12},{9,13},{10,... | collective-permute-start | bytes 344072 | tf_op jit(solution)/shard_map/ppermute | solution.py:28
  46.3 4.8 %collective-permute-start.5 = (bf16[2,16,1792]{2,1,0:T(8,128)(2,1)S(1)}, bf16[2,16,1792]{2,1,0:T(8,128)(2,1)S(1)}, u32[]{:S(2)}, u32[]{:S(2)}) collective-permute-start(bf16[2,16,1792]{2,1,0:T(8,128)(2,1)S(1)} %get-tuple-element.88), channel_id=1, source_target_pairs={{0,2},{1,3},{2,0},{3,1},{4,6},{5,7},{6,4},{7,5},{8,10},{9,11},{10,... | collective-permute-start | bytes 344072 | tf_op jit(solution)/shard_map/ppermute | solution.py:28
  51.1 20.7 %collective-permute-start.10 = (bf16[192,4096]{1,0:T(8,128)(2,1)S(1)}, bf16[192,4096]{1,0:T(8,128)(2,1)S(1)}, u32[]{:S(2)}, u32[]{:S(2)}) collective-permute-start(bf16[192,4096]{1,0:T(8,128)(2,1)S(1)} %copy-done.1), channel_id=1, source_target_pairs={{0,1},{1,0},{2,3},{3,2},{4,5},{5,4},{6,7},{7,6},{8,9},{9,8},{10,11... | collective-permute-start | bytes 4718600 | tf_op jit(solution)/shard_map/ppermute | solution.py:28
  51.2 20.7 %collective-permute-start.9 = (bf16[192,3584]{1,0:T(8,128)(2,1)}, bf16[192,3584]{1,0:T(8,128)(2,1)S(1)}, u32[]{:S(2)}, u32[]{:S(2)}) collective-permute-start(bf16[192,3584]{1,0:T(8,128)(2,1)} %bitcast.22), channel_id=1, source_target_pairs={{0,1},{1,0},{2,3},{3,2},{4,5},{5,4},{6,7},{7,6},{8,9},{9,8},{10,11... | collective-permute-start | bytes 4128776 | tf_op jit(solution)/shard_map/ppermute | solution.py:28
  51.7 13.6 %collective-permute-start.6 = (bf16[2,2,16,1792]{3,2,1,0:T(8,128)(2,1)S(1)}, bf16[2,2,16,1792]{3,2,1,0:T(8,128)(2,1)S(1)}, u32[]{:S(2)}, u32[]{:S(2)}) collective-permute-start(bf16[2,2,16,1792]{3,2,1,0:T(8,128)(2,1)S(1)} %add_all.1.mine_ref), channel_id=1, source_target_pairs={{0,8},{1,9},{2,10},{3,11},{4,12},{5,13},{6,14},{7,15},{8,0},{9,1},... | collective-permute-start | bytes 688136 | tf_op jit(solution)/shard_map/ppermute | solution.py:28
  55.3 11.9 %collective-permute-start.11 = (bf16[2,192,256]{2,1,0:T(8,128)(2,1)}, bf16[2,192,256]{2,1,0:T(8,128)(2,1)S(1)}, u32[]{:S(2)}, u32[]{:S(2)}) collective-permute-start(bf16[2,192,256]{2,1,0:T(8,128)(2,1)} %bitcast.26), channel_id=1, source_target_pairs={{0,1},{1,0},{2,3},{3,2},{4,5},{5,4},{6,7},{7,6},{8,9},{9,8},{10,11... | collective-permute-start | bytes 589832 | tf_op jit(solution)/shard_map/ppermute | solution.py:28
  65.5 4.9 %collective-permute-start.8 = (bf16[32,1792]{1,0:T(8,128)(2,1)S(1)}, bf16[32,1792]{1,0:T(8,128)(2,1)S(1)}, u32[]{:S(2)}, u32[]{:S(2)}) collective-permute-start(bf16[32,1792]{1,0:T(8,128)(2,1)S(1)} %bitcast.30), channel_id=1, source_target_pairs={{0,2},{1,3},{2,0},{3,1},{4,6},{5,7},{6,4},{7,5},{8,10},{9,11},{10,... | collective-permute-start | bytes 344072 | tf_op jit(solution)/shard_map/ppermute | solution.py:28
  67.1 4.8 %collective-permute-start.7 = (bf16[32,1792]{1,0:T(8,128)(2,1)S(1)}, bf16[32,1792]{1,0:T(8,128)(2,1)S(1)}, u32[]{:S(2)}, u32[]{:S(2)}) collective-permute-start(bf16[32,1792]{1,0:T(8,128)(2,1)S(1)} %bitcast.28), channel_id=1, source_target_pairs={{0,4},{1,5},{2,6},{3,7},{4,0},{5,1},{6,2},{7,3},{8,12},{9,13},{10,... | collective-permute-start | bytes 344072 | tf_op jit(solution)/shard_map/ppermute | solution.py:28
  67.2 0.9 copy-start.5
  71.9 6.6 %copy-start.2 = (bf16[3584,192]{0,1:T(8,128)(2,1)S(1)}, bf16[3584,192]{0,1:T(8,128)(2,1)}, u32[]{:S(2)}) copy-start(bf16[3584,192]{0,1:T(8,128)(2,1)} %param.13) | copy-start | bytes 4128772
  71.9 6.1 %collective-permute-start.12 = (bf16[64,1792]{1,0:T(8,128)(2,1)S(1)}, bf16[64,1792]{1,0:T(8,128)(2,1)S(1)}, u32[]{:S(2)}, u32[]{:S(2)}) collective-permute-start(bf16[64,1792]{1,0:T(8,128)(2,1)S(1)} %get-tuple-element.102.refs_0_), channel_id=1, source_target_pairs={{0,2},{1,3},{2,0},{3,1},{4,6},{5,7},{6,4},{7,5},{8,10},{9,11},{10,... | collective-permute-start | bytes 688136 | tf_op jit(solution)/shard_map/ppermute | solution.py:28
  72.5 6.0 %collective-permute-start.13 = (bf16[64,1792]{1,0:T(8,128)(2,1)S(1)}, bf16[64,1792]{1,0:T(8,128)(2,1)S(1)}, u32[]{:S(2)}, u32[]{:S(2)}) collective-permute-start(bf16[64,1792]{1,0:T(8,128)(2,1)S(1)} %get-tuple-element.103.refs_2_), channel_id=1, source_target_pairs={{0,4},{1,5},{2,6},{3,7},{4,0},{5,1},{6,2},{7,3},{8,12},{9,13},{10,... | collective-permute-start | bytes 688136 | tf_op jit(solution)/shard_map/ppermute | solution.py:28
  81.0 6.8 %collective-permute-start.14 = (bf16[4,144,256]{2,1,0:T(8,128)(2,1)S(1)}, bf16[4,144,256]{2,1,0:T(8,128)(2,1)S(1)}, u32[]{:S(2)}, u32[]{:S(2)}) collective-permute-start(bf16[4,144,256]{2,1,0:T(8,128)(2,1)S(1)} %get-tuple-element.118), channel_id=1, source_target_pairs={{0,2},{1,3},{2,0},{3,1},{4,6},{5,7},{6,4},{7,5},{8,10},{9,11},{10,... | collective-permute-start | bytes 884744 | tf_op jit(solution)/shard_map/ppermute | solution.py:28
  82.5 8.0 %collective-permute-start.15 = (bf16[4,144,256]{2,1,0:T(8,128)(2,1)S(1)}, bf16[4,144,256]{2,1,0:T(8,128)(2,1)S(1)}, u32[]{:S(2)}, u32[]{:S(2)}) collective-permute-start(bf16[4,144,256]{2,1,0:T(8,128)(2,1)S(1)} %get-tuple-element.119), channel_id=1, source_target_pairs={{0,4},{1,5},{2,6},{3,7},{4,0},{5,1},{6,2},{7,3},{8,12},{9,13},{10,... | collective-permute-start | bytes 884744 | tf_op jit(solution)/shard_map/ppermute | solution.py:28
  90.7 6.8 %collective-permute-start.16 = (bf16[2,144,256]{2,1,0:T(8,128)(2,1)S(1)}, bf16[2,144,256]{2,1,0:T(8,128)(2,1)S(1)}, u32[]{:S(2)}, u32[]{:S(2)}) collective-permute-start(bf16[2,144,256]{2,1,0:T(8,128)(2,1)S(1)} %get-tuple-element.126), channel_id=1, source_target_pairs={{0,4},{1,5},{2,6},{3,7},{4,0},{5,1},{6,2},{7,3},{8,12},{9,13},{10,... | collective-permute-start | bytes 442376 | tf_op jit(solution)/shard_map/ppermute | solution.py:28
  90.8 6.7 %collective-permute-start.17 = (bf16[2,144,256]{2,1,0:T(8,128)(2,1)S(1)}, bf16[2,144,256]{2,1,0:T(8,128)(2,1)S(1)}, u32[]{:S(2)}, u32[]{:S(2)}) collective-permute-start(bf16[2,144,256]{2,1,0:T(8,128)(2,1)S(1)} %get-tuple-element.128), channel_id=1, source_target_pairs={{0,2},{1,3},{2,0},{3,1},{4,6},{5,7},{6,4},{7,5},{8,10},{9,11},{10,... | collective-permute-start | bytes 442376 | tf_op jit(solution)/shard_map/ppermute | solution.py:28
  97.5 7.6 %collective-permute-start.18 = (bf16[2,1,144,256]{3,2,1,0:T(8,128)(2,1)S(1)}, bf16[2,1,144,256]{3,2,1,0:T(8,128)(2,1)S(1)}, u32[]{:S(2)}, u32[]{:S(2)}) collective-permute-start(bf16[2,1,144,256]{3,2,1,0:T(8,128)(2,1)S(1)} %get-tuple-element.131), channel_id=1, source_target_pairs={{0,8},{1,9},{2,10},{3,11},{4,12},{5,13},{6,14},{7,15},{8,0},{9,1},... | collective-permute-start | bytes 442376 | tf_op jit(solution)/shard_map/ppermute | solution.py:28
  106.0 1.3 %collective-permute-start.19 = (bf16[128,256]{1,0:T(8,128)(2,1)S(1)}, bf16[128,256]{1,0:T(8,128)(2,1)S(1)}, u32[]{:S(2)}, u32[]{:S(2)}) collective-permute-start(bf16[128,256]{1,0:T(8,128)(2,1)S(1)} %get-tuple-element.133), channel_id=1, source_target_pairs={{0,1},{1,0},{2,3},{3,2},{4,5},{5,4},{6,7},{7,6},{8,9},{9,8},{10,11... | collective-permute-start | bytes 196616 | tf_op jit(solution)/shard_map/ppermute | solution.py:28
  108.6 8.8 %collective-permute-start.24 = (bf16[2,160,128]{2,1,0:T(8,128)(2,1)S(1)}, bf16[2,160,128]{2,1,0:T(8,128)(2,1)S(1)}, u32[]{:S(2)}, u32[]{:S(2)}) collective-permute-start(bf16[2,160,128]{2,1,0:T(8,128)(2,1)S(1)} %get-tuple-element.140), channel_id=1, source_target_pairs={{0,12},{1,13},{2,14},{3,15},{4,8},{5,9},{6,10},{7,11},{8,4},{9,5},... | collective-permute-start | bytes 245768 | tf_op jit(solution)/shard_map/ppermute | solution.py:28
  110.0 8.1 %collective-permute-start.25 = (bf16[2,160,128]{2,1,0:T(8,128)(2,1)S(1)}, bf16[2,160,128]{2,1,0:T(8,128)(2,1)S(1)}, u32[]{:S(2)}, u32[]{:S(2)}) collective-permute-start(bf16[2,160,128]{2,1,0:T(8,128)(2,1)S(1)} %get-tuple-element.141), channel_id=1, source_target_pairs={{0,2},{1,3},{2,0},{3,1},{4,6},{5,7},{6,4},{7,5},{8,10},{9,11},{10,... | collective-permute-start | bytes 245768 | tf_op jit(solution)/shard_map/ppermute | solution.py:28
  110.8 10.2 %collective-permute-start.26 = (bf16[2,160,128]{2,1,0:T(8,128)(2,1)S(1)}, bf16[2,160,128]{2,1,0:T(8,128)(2,1)S(1)}, u32[]{:S(2)}, u32[]{:S(2)}) collective-permute-start(bf16[2,160,128]{2,1,0:T(8,128)(2,1)S(1)} %get-tuple-element.142), channel_id=1, source_target_pairs={{0,14},{1,15},{2,12},{3,13},{4,10},{5,11},{6,8},{7,9},{8,6},{9,7},... | collective-permute-start | bytes 245768 | tf_op jit(solution)/shard_map/ppermute | solution.py:28
  115.1 7.3 %collective-permute-start.20 = (bf16[2,160,128]{2,1,0:T(8,128)(2,1)S(1)}, bf16[2,160,128]{2,1,0:T(8,128)(2,1)S(1)}, u32[]{:S(2)}, u32[]{:S(2)}) collective-permute-start(bf16[2,160,128]{2,1,0:T(8,128)(2,1)S(1)} %get-tuple-element.134), channel_id=1, source_target_pairs={{0,8},{1,9},{2,10},{3,11},{4,12},{5,13},{6,14},{7,15},{8,0},{9,1},... | collective-permute-start | bytes 245768 | tf_op jit(solution)/shard_map/ppermute | solution.py:28
  115.2 9.3 %collective-permute-start.21 = (bf16[2,160,128]{2,1,0:T(8,128)(2,1)S(1)}, bf16[2,160,128]{2,1,0:T(8,128)(2,1)S(1)}, u32[]{:S(2)}, u32[]{:S(2)}) collective-permute-start(bf16[2,160,128]{2,1,0:T(8,128)(2,1)S(1)} %get-tuple-element.135), channel_id=1, source_target_pairs={{0,6},{1,7},{2,4},{3,5},{4,2},{5,3},{6,0},{7,1},{8,14},{9,15},{10,... | collective-permute-start | bytes 245768 | tf_op jit(solution)/shard_map/ppermute | solution.py:28
  117.3 7.7 %collective-permute-start.22 = (bf16[2,160,128]{2,1,0:T(8,128)(2,1)S(1)}, bf16[2,160,128]{2,1,0:T(8,128)(2,1)S(1)}, u32[]{:S(2)}, u32[]{:S(2)}) collective-permute-start(bf16[2,160,128]{2,1,0:T(8,128)(2,1)S(1)} %get-tuple-element.136), channel_id=1, source_target_pairs={{0,10},{1,11},{2,8},{3,9},{4,14},{5,15},{6,12},{7,13},{8,2},{9,3},... | collective-permute-start | bytes 245768 | tf_op jit(solution)/shard_map/ppermute | solution.py:28
  118.1 7.0 %collective-permute-start.23 = (bf16[2,160,128]{2,1,0:T(8,128)(2,1)S(1)}, bf16[2,160,128]{2,1,0:T(8,128)(2,1)S(1)}, u32[]{:S(2)}, u32[]{:S(2)}) collective-permute-start(bf16[2,160,128]{2,1,0:T(8,128)(2,1)S(1)} %get-tuple-element.137), channel_id=1, source_target_pairs={{0,4},{1,5},{2,6},{3,7},{4,0},{5,1},{6,2},{7,3},{8,12},{9,13},{10,... | collective-permute-start | bytes 245768 | tf_op jit(solution)/shard_map/ppermute | solution.py:28
  121.0 4.1 %collective-permute-start.28 = (bf16[4,160,128]{2,1,0:T(8,128)(2,1)S(1)}, bf16[4,160,128]{2,1,0:T(8,128)(2,1)S(1)}, u32[]{:S(2)}, u32[]{:S(2)}) collective-permute-start(bf16[4,160,128]{2,1,0:T(8,128)(2,1)S(1)} %gather_other.3), channel_id=1, source_target_pairs={{0,1},{1,0},{2,3},{3,2},{4,5},{5,4},{6,7},{7,6},{8,9},{9,8},{10,11... | collective-permute-start | bytes 491528 | tf_op jit(solution)/shard_map/ppermute | solution.py:28
  125.0 1.5 %collective-permute-start.27 = (bf16[4,160,128]{2,1,0:T(8,128)(2,1)S(1)}, bf16[4,160,128]{2,1,0:T(8,128)(2,1)S(1)}, u32[]{:S(2)}, u32[]{:S(2)}) collective-permute-start(bf16[4,160,128]{2,1,0:T(8,128)(2,1)S(1)} %gather_other.2), channel_id=1, source_target_pairs={{0,1},{1,0},{2,3},{3,2},{4,5},{5,4},{6,7},{7,6},{8,9},{9,8},{10,11... | collective-permute-start | bytes 491528 | tf_op jit(solution)/shard_map/ppermute | solution.py:28

commit v21 on v20

--- a/solution.py
+++ b/solution.py
@@ -51,41 +51,37 @@
     return jax.nn.silu(embedding).astype(jnp.bfloat16)
 
 
-def encoder_kernel(lanes, place_ref, act_ref, weight_ref, *refs):
-    outs, lhs_ref = refs[:-1], refs[-1]
-    chips, share, width = outs[0].shape
-    core = place_ref[2]
-    half = chips * share
+def encoder_kernel(order, place_ref, act_ref, weight_ref, own_ref, other_ref, lhs_ref):
+    at, core = place_ref[0], place_ref[2]
+    chips = 1 << len(order)
+    half = lhs_ref.shape[0] // 2
+    width = weight_ref.shape[1]
     first = core == 0
-    tile = width // 2
+    tile = width // 4
     lhs_ref[...] = act_ref[...].T
-    for lane, order in enumerate(lanes):
-        own_ref, other_ref = outs[2 * lane], outs[2 * lane + 1]
-        for column in range(0, width, tile):
-            start = lane * width + column
-            result = jnp.dot(
-                lhs_ref[...], weight_ref[:, start : start + tile], preferred_element_type=jnp.float32
-            )
-            own = jnp.where(first, result[:half], result[half:]).astype(own_ref.dtype)
-            other = jnp.where(first, result[half:], result[:half]).astype(own_ref.dtype)
-            own = own.reshape(chips, share, tile)
-            other = other.reshape(chips, share, tile)
-            for block in range(chips):
-                to = place_ref[lane] ^ position(block, order)
-                own_ref[to, :, column : column + tile] = own[block]
-                other_ref[to, :, column : column + tile] = other[block]
-
-
-def encoder(lanes, place, act, weight):
-    chips = 1 << len(lanes[0])
+    for column in range(0, width, tile):
+        columns = slice(column, column + tile)
+        result = jnp.dot(lhs_ref[...], weight_ref[:, columns], preferred_element_type=jnp.float32)
+        own = jnp.where(first, result[:half], result[half:]).astype(own_ref.dtype)
+        other = jnp.where(first, result[half:], result[:half]).astype(own_ref.dtype)
+        own = own.reshape(chips, half // chips, tile)
+        other = other.reshape(chips, half // chips, tile)
+        for block in range(chips):
+            to = at ^ position(block, order)
+            own_ref[to, :, columns] = own[block]
+            other_ref[to, :, columns] = other[block]
+
+
+def encoder(order, place, act, weight):
+    chips = 1 << len(order)
     depth, rows = act.shape
     width = weight.shape[1]
-    out = jax.ShapeDtypeStruct((chips, rows // 2 // chips, width // 2), jnp.bfloat16)
-    return pl.pallas_call(
-        functools.partial(encoder_kernel, lanes),
-        out_shape=(out,) * 4,
+    out = jax.ShapeDtypeStruct((chips, rows // 2 // chips, width), jnp.bfloat16)
+    return pl.pallas_call(
+        functools.partial(encoder_kernel, order),
+        out_shape=(out, out),
         in_specs=[SMEM_SPEC, VMEM_SPEC, VMEM_SPEC],
-        out_specs=(VMEM_SPEC,) * 4,
+        out_specs=(VMEM_SPEC,) * 2,
         scratch_shapes=[pltpu.VMEM((rows, depth), jnp.bfloat16)],
         compiler_params=params(16),
         cost_estimate=pl.CostEstimate(
@@ -532,41 +528,59 @@
     return [outs[0], outs[2]], [outs[1], outs[3]]
 
 
-def total_kernel(mine0, got0, mine1, got1, out_ref):
-    for lane, (mine, got) in enumerate(((mine0, got0), (mine1, got1))):
-        out_ref[lane] = (mine[...] + got[...].astype(jnp.float32)).astype(out_ref.dtype)
-
-
-def add_all(mine, got):
+def fold_kernel(mine_ref, got_ref, sent_ref, keep_ref):
+    half = mine_ref.shape[0] // 2
+    total = mine_ref[half:].astype(jnp.float32) + got_ref[half:].astype(jnp.float32)
+    sent_ref[...] = total.astype(sent_ref.dtype)
+    keep_ref[...] = mine_ref[:half].astype(jnp.float32) + got_ref[:half].astype(jnp.float32)
+
+
+def fold(mine, got):
+    shape = (mine.shape[0] // 2,) + mine.shape[1:]
+    return pl.pallas_call(
+        fold_kernel,
+        out_shape=(jax.ShapeDtypeStruct(shape, jnp.bfloat16), jax.ShapeDtypeStruct(shape, jnp.float32)),
+        in_specs=[VMEM_SPEC] * 2,
+        out_specs=(VMEM_SPEC,) * 2,
+        compiler_params=params(8),
+        cost_estimate=pl.CostEstimate(flops=mine.size, bytes_accessed=8 * mine.size, transcendentals=0),
+        name="fold",
+    )(mine, got)
+
+
+def total_kernel(keep_ref, *refs):
+    total = keep_ref[...]
+    for got_ref in refs[:-1]:
+        total += got_ref[...].astype(jnp.float32)
+    refs[-1][...] = total.astype(refs[-1].dtype)
+
+
+def add_all(keep, got):
     return pl.pallas_call(
         total_kernel,
-        out_shape=jax.ShapeDtypeStruct((2,) + mine[0].shape, jnp.bfloat16),
-        in_specs=[VMEM_SPEC] * 4,
+        out_shape=jax.ShapeDtypeStruct(keep.shape, jnp.bfloat16),
+        in_specs=[VMEM_SPEC] * (1 + len(got)),
         out_specs=VMEM_SPEC,
         compiler_params=params(4),
         cost_estimate=pl.CostEstimate(
-            flops=2 * mine[0].size, bytes_accessed=16 * mine[0].size, transcendentals=0
+            flops=4 * keep.size, bytes_accessed=12 * keep.size, transcendentals=0
         ),
         name="add_all",
-    )(mine[0], got[0], mine[1], got[1])
-
-
-def norm_kernel(mine_ref, got_ref, gain_ref, out0, out1):
-    width = mine_ref.shape[3]
+    )(keep, *got)
+
+
+def norm_kernel(mine_ref, got_ref, gain_ref, *outs):
+    width = mine_ref.shape[2] // 2
     for at in range(2):
-        totals = [
-            mine_ref[lane, at].astype(jnp.float32) + got_ref[lane, 1 - at].astype(jnp.float32)
-            for lane in range(2)
-        ]
-        square = sum(jnp.sum(total * total, 1, keepdims=True) for total in totals)
-        scale_rows = lax.rsqrt(square / (2 * width) + epsilon)
-        for lane, (total, out_ref) in enumerate(zip(totals, (out0, out1))):
-            gain = gain_ref[:, lane * width : (lane + 1) * width].astype(jnp.float32)
-            out_ref[at] = (total * scale_rows * gain).astype(out_ref.dtype)
+        total = mine_ref[at].astype(jnp.float32) + got_ref[1 - at].astype(jnp.float32)
+        scale_rows = lax.rsqrt(jnp.mean(total * total, 1, keepdims=True) + epsilon)
+        total = total * scale_rows * gain_ref[...].astype(jnp.float32)
+        for lane, out_ref in enumerate(outs):
+            out_ref[at] = total[:, lane * width : (lane + 1) * width].astype(out_ref.dtype)
 
 
 def normalize(mine, got, norm_gain):
-    out = jax.ShapeDtypeStruct(mine.shape[1:], jnp.bfloat16)
+    out = jax.ShapeDtypeStruct(mine.shape[:2] + (mine.shape[2] // 2,), jnp.bfloat16)
     states = pl.pallas_call(
         norm_kernel,
         out_shape=(out, out),
@@ -648,13 +662,13 @@
     packed = pack(copies, image_queries[0], image_key_values[0, :, 0], image_key_values[0, :, 1])
     act, packed = tie((enc_act[0].T, packed))
     packed = exchange(packed)
-    encoded = encoder(lanes, place, act, down_weight)
-    keep, got = encoded[::2], [swap(other, 1) for other in encoded[1::2]]
+    keep, other = encoder(lanes[0], place, act, down_weight)
+    got = swap(other, 1)
     last = 2 * lanes[0][-1]
-    for step in range(rounds - 1):
-        sent, keep = add_halves(keep, got)
-        got = [swap(part, 2 * order[step]) for part, order in zip(sent, lanes)]
-    summed, packed = tie((add_all(keep, got), packed))
+    for bit in lanes[0][:-1]:
+        sent, keep = fold(keep, got)
+        got = swap(sent, 2 * bit)
+    summed, packed = tie((add_all(keep, [got]), packed))
     summed, held, held_kv, held_mod = tie((summed, win0, kv0, mod0))
     win1, kv1, mod1 = swap(held, 1), swap(held_kv, 1), swap(held_mod, 1)
     got = swap(summed, last)

time: 128 us -> 129 us (level)
    ppermute x29 -> x26, starting transfers between devices: 29.3 us -> 30.2 us  [swap(): return lax.ppermute(value, 'seq', [(i, i ^ mask) for i in range(devices)])]
    ppermute x29 -> x26, waiting for transfers between devices: 60.8 us -> 60.3 us  [swap(): return lax.ppermute(value, 'seq', [(i, i ^ mask) for i in range(devices)])]
    pallas_call x2 -> x4, Pallas kernels: 3.51 us -> 3.78 us  [the longest x1 3.47 us: encoder(): pl.pallas_call(functools.partial(encoder_kernel, order), out_shape=(out,...]
  transfers between devices with their start and end apart: 30 -> 27, of which waited for: 20 -> 16; matrix products, arithmetic and copies ran while one was open for 0% -> 0% of each run, Pallas kernels for 10% -> 10%
where the time goes in v21:
time: 129 us
  waiting for transfers between devices  60.3 us (47%)
  starting transfers between devices  37.7 us (29%)
  Pallas kernels  21.1 us (16%)
  local copies, waits for them, and re-layouts  7.06 us (5%)
  between operations  2.25 us (2%)
    ppermute x26, waiting for transfers between devices, swap(): return lax.ppermute(value, 'seq', [(i, i ^ mask) for i in range(devices)])  60.3 us
    ppermute x26, starting transfers between devices, swap(): return lax.ppermute(value, 'seq', [(i, i ^ mask) for i in range(devices)])  30.2 us
    pallas_call x2, Pallas kernels, image_attention(): pl.pallas_call(functools.partial(image_kernel, factor, masks, img_dev), o...  8.03 us
    all_to_all x1, starting transfers between devices, exchange(): return lax.all_to_all(rows, 'seq', split_axis=0, concat_axis=0, tiled=True)  7.49 us
    unnamed x14, local copies, waits for them, and re-layouts  5.31 us
    pallas_call x1, Pallas kernels, encoder(): pl.pallas_call(functools.partial(encoder_kernel, order), out_shape=(out,...  3.47 us
  transfers between devices with their start and end apart: 27, of which 16 were waited for; matrix products, arithmetic and copies ran while one was open for 0% of the time, Pallas kernels for 10%

profile of v21, /device:TPU:0, one launch (start us, length us, event | category | flops | bytes accessed | tf_op | source)
XLA Modules:
  0.0 128.6 jit_solution(5982730805214611075)
XLA Ops:
  0.6 1.6 %copy.12 = bf16[1,128,2,2048]{3,1,2,0:T(8,128)(2,1)S(1)} copy(bf16[1,128,2,2048]{3,2,1,0:T(2,128)(2,1)} %param.19) | data formatting | bytes 2097152 | tf_op jit(solution)/shard_map/optimization_barrier | solution.py:661
  2.2 0.1 slice_bitcast_fusion
  2.3 1.0 copy-done.4
  3.3 1.5 %pack.1 = bf16[16,384,128]{2,1,0:T(8,128)(2,1)} custom-call(bf16[128,2048]{1,0:T(8,128)(2,1)S(1)} %bitcast.25, bf16[128,2048]{1,0:T(8,128)(2,1)S(1)} %get-tuple-element.135.keys_ref, bf16[128,2048]{1,0:T(8,128)(2,1)S(1)} %get-tuple-element.134.values_ref), custom_call_target="tpu_custom_call" | custom-call | bytes 3145728 | tf_op jit(solution)/shard_map/pack/pallas_call | solution.py:302
  4.7 7.5 %all-to-all-start = ((bf16[16,384,128]{2,1,0:T(8,128)(2,1)}), bf16[16,384,128]{2,1,0:T(8,128)(2,1)S(1)}, u32[]{:S(2)}, u32[]{:S(2)}) async-start(bf16[16,384,128]{2,1,0:T(8,128)(2,1)} %pack.1), calls=%async_computation | async-start | bytes 3145728 | tf_op jit(solution)/shard_map/all_to_all | solution.py:659
  12.9 0.1 stack.19.place_ref
  13.0 3.4 %copy-done = bf16[1184,3584]{1,0:T(8,128)(2,1)S(1)} copy-done((bf16[1184,3584]{1,0:T(8,128)(2,1)S(1)}, bf16[1184,3584]{1,0:T(8,128)(2,1)}, u32[]{:S(2)}) %copy-start) | copy-done | bytes 8486936
  16.4 3.5 %encoder.1 = (bf16[8,16,3584]{2,1,0:T(8,128)(2,1)S(1)}, bf16[8,16,3584]{2,1,0:T(8,128)(2,1)S(1)}) custom-call(s32[5]{0:T(128)S(1)} %stack.19.place_ref, bf16[1184,256]{1,0:T(8,128)(2,1)S(1)} %bitcast.24, bf16[1184,3584]{1,0:T(8,128)(2,1)S(1)} %copy-done), custom_call_target="tpu_custom_call" | custom-call | flops 2172649472 | bytes 10928128 | tf_op jit(solution)/shard_map/encoder/pallas_call | solution.py:80
  19.9 0.5 collective-permute-start
  20.3 2.1 %collective-permute-done.got_ref = bf16[8,16,3584]{2,1,0:T(8,128)(2,1)S(1)} collective-permute-done((bf16[8,16,3584]{2,1,0:T(8,128)(2,1)S(1)}, bf16[8,16,3584]{2,1,0:T(8,128)(2,1)S(1)}, u32[]{:S(2)}, u32[]{:S(2)}) %collective-permute-start) | collective-permute-done | bytes 917536 | tf_op jit(solution)/shard_map/ppermute | solution.py:28
  22.4 0.2 fold.2
  22.6 0.0 copy-start.6
  22.6 2.0 %collective-permute-start.1 = (bf16[4,16,3584]{2,1,0:T(8,128)(2,1)S(1)}, bf16[4,16,3584]{2,1,0:T(8,128)(2,1)S(1)}, u32[]{:S(2)}, u32[]{:S(2)}) collective-permute-start(bf16[4,16,3584]{2,1,0:T(8,128)(2,1)S(1)} %get-tuple-element.74), channel_id=1, source_target_pairs={{0,2},{1,3},{2,0},{3,1},{4,6},{5,7},{6,4},{7,5},{8,10},{9,11},{10,... | collective-permute-start | bytes 1376264 | tf_op jit(solution)/shard_map/ppermute | solution.py:28
  24.6 16.4 %collective-permute-done.1.got_ref = bf16[4,16,3584]{2,1,0:T(8,128)(2,1)S(1)} collective-permute-done((bf16[4,16,3584]{2,1,0:T(8,128)(2,1)S(1)}, bf16[4,16,3584]{2,1,0:T(8,128)(2,1)S(1)}, u32[]{:S(2)}, u32[]{:S(2)}) %collective-permute-start.1) | collective-permute-done | bytes 458784 | tf_op jit(solution)/shard_map/ppermute | solution.py:28
  41.0 0.1 fold.3
  41.1 4.5 %collective-permute-start.2 = (bf16[2,16,3584]{2,1,0:T(8,128)(2,1)S(1)}, bf16[2,16,3584]{2,1,0:T(8,128)(2,1)S(1)}, u32[]{:S(2)}, u32[]{:S(2)}) collective-permute-start(bf16[2,16,3584]{2,1,0:T(8,128)(2,1)S(1)} %get-tuple-element.76), channel_id=1, source_target_pairs={{0,4},{1,5},{2,6},{3,7},{4,0},{5,1},{6,2},{7,3},{8,12},{9,13},{10,... | collective-permute-start | bytes 688136 | tf_op jit(solution)/shard_map/ppermute | solution.py:28
  45.5 5.6 %collective-permute-done.2.refs_0_ = bf16[2,16,3584]{2,1,0:T(8,128)(2,1)S(1)} collective-permute-done((bf16[2,16,3584]{2,1,0:T(8,128)(2,1)S(1)}, bf16[2,16,3584]{2,1,0:T(8,128)(2,1)S(1)}, u32[]{:S(2)}, u32[]{:S(2)}) %collective-permute-start.2) | collective-permute-done | bytes 229408 | tf_op jit(solution)/shard_map/ppermute | solution.py:28
  51.2 0.1 collective-permute-start.7
  51.3 0.5 collective-permute-start.6
  51.8 3.1 %collective-permute-start.3 = (bf16[2,16,3584]{2,1,0:T(8,128)(2,1)S(1)}, bf16[2,16,3584]{2,1,0:T(8,128)(2,1)S(1)}, u32[]{:S(2)}, u32[]{:S(2)}) collective-permute-start(bf16[2,16,3584]{2,1,0:T(8,128)(2,1)S(1)} %add_all.1.mine_ref), channel_id=1, source_target_pairs={{0,8},{1,9},{2,10},{3,11},{4,12},{5,13},{6,14},{7,15},{8,0},{9,1},... | collective-permute-start | bytes 688136 | tf_op jit(solution)/shard_map/ppermute | solution.py:28
  55.5 0.1 collective-permute-start.8
  55.6 10.0 %collective-permute-done.3.got_ref = bf16[2,16,3584]{2,1,0:T(8,128)(2,1)S(1)} collective-permute-done((bf16[2,16,3584]{2,1,0:T(8,128)(2,1)S(1)}, bf16[2,16,3584]{2,1,0:T(8,128)(2,1)S(1)}, u32[]{:S(2)}, u32[]{:S(2)}) %collective-permute-start.3) | collective-permute-done | bytes 229408 | tf_op jit(solution)/shard_map/ppermute | solution.py:28
  65.6 0.2 normalize.1
  65.8 0.8 collective-permute-start.5
  66.6 0.1 collective-permute-start.4
  66.8 0.9 copy-done.5
  67.7 0.2 modulation.1.refs_4_
  67.9 2.8 %collective-permute-done.5.got1 = bf16[32,1792]{1,0:T(8,128)(2,1)S(1)} collective-permute-done((bf16[32,1792]{1,0:T(8,128)(2,1)S(1)}, bf16[32,1792]{1,0:T(8,128)(2,1)S(1)}, u32[]{:S(2)}, u32[]{:S(2)}) %collective-permute-start.5) | collective-permute-done | bytes 114720 | tf_op jit(solution)/shard_map/ppermute | solution.py:28
  70.7 0.7 collective-permute-done.4.got0
  71.5 1.4 %collective-permute-start.9 = (bf16[64,1792]{1,0:T(8,128)(2,1)S(1)}, bf16[64,1792]{1,0:T(8,128)(2,1)S(1)}, u32[]{:S(2)}, u32[]{:S(2)}) collective-permute-start(bf16[64,1792]{1,0:T(8,128)(2,1)S(1)} %get-tuple-element.90.refs_0_), channel_id=1, source_target_pairs={{0,2},{1,3},{2,0},{3,1},{4,6},{5,7},{6,4},{7,5},{8,10},{9,11},{10,... | collective-permute-start | bytes 688136 | tf_op jit(solution)/shard_map/ppermute | solution.py:28
  72.8 0.7 collective-permute-start.10
  73.6 3.9 %image_attention.2 = (f32[1024,256]{1,0:T(8,128)S(1)}, f32[1024,128]{1,0:T(8,128)S(1)}) custom-call(s32[5]{0:T(128)S(1)} %stack.19.place_ref, bf16[16,384,128]{2,1,0:T(8,128)(2,1)S(1)} %all-to-all-done.packed_ref), custom_call_target="tpu_custom_call" | custom-call | flops 1073741824 | bytes 2359296 | tf_op jit(solution)/shard_map/image_attention/pallas_call | solution.py:379
  77.5 0.0 collective-permute-done.9.refs_1_
  77.5 1.3 %collective-permute-done.10.refs_3_ = bf16[64,1792]{1,0:T(8,128)(2,1)S(1)} collective-permute-done((bf16[64,1792]{1,0:T(8,128)(2,1)S(1)}, bf16[64,1792]{1,0:T(8,128)(2,1)S(1)}, u32[]{:S(2)}, u32[]{:S(2)}) %collective-permute-start.10) | collective-permute-done | bytes 229408 | tf_op jit(solution)/shard_map/ppermute | solution.py:28
  78.9 2.4 %project.1 = (bf16[4,144,256]{2,1,0:T(8,128)(2,1)S(1)}, bf16[4,144,256]{2,1,0:T(8,128)(2,1)S(1)}, bf16[4,144,256]{2,1,0:T(8,128)(2,1)S(1)}, bf16[4,144,256]{2,1,0:T(8,128)(2,1)S(1)}) custom-call(s32[5]{0:T(128)S(1)} %stack.19.place_ref, bf16[64,1792]{1,0:T(8,128)(2,1)S(1)} %get-tuple-element.90.refs_0_, bf16[64,1792]{1,0:T(8,128)(2,1)S(1)} %collective-permute-done.9.refs_1_, ...), custom_call_target="tpu_custom_call" | custom-call | flops 754974720 | bytes 7864320 | tf_op jit(solution)/shard_map/project/pallas_call | solution.py:212
  81.3 0.8 collective-permute-start.11
  82.1 0.8 collective-permute-start.12
  82.8 4.1 %image_attention.3 = (f32[1024,256]{1,0:T(8,128)S(1)}, f32[1024,128]{1,0:T(8,128)S(1)}) custom-call(s32[5]{0:T(128)S(1)} %stack.19.place_ref, bf16[16,384,128]{2,1,0:T(8,128)(2,1)S(1)} %all-to-all-done.packed_ref), custom_call_target="tpu_custom_call" | custom-call | flops 1073741824 | bytes 2359296 | tf_op jit(solution)/shard_map/image_attention/pallas_call | solution.py:379
  86.9 1.1 collective-permute-done.11.refs_1_
  88.1 2.0 %collective-permute-done.12.refs_3_ = bf16[4,144,256]{2,1,0:T(8,128)(2,1)S(1)} collective-permute-done((bf16[4,144,256]{2,1,0:T(8,128)(2,1)S(1)}, bf16[4,144,256]{2,1,0:T(8,128)(2,1)S(1)}, u32[]{:S(2)}, u32[]{:S(2)}) %collective-permute-start.12) | collective-permute-done | bytes 294944 | tf_op jit(solution)/shard_map/ppermute | solution.py:28
  90.0 0.1 add_halves.2
  90.2 0.1 collective-permute-start.13
  90.2 1.5 %collective-permute-start.14 = (bf16[2,144,256]{2,1,0:T(8,128)(2,1)S(1)}, bf16[2,144,256]{2,1,0:T(8,128)(2,1)S(1)}, u32[]{:S(2)}, u32[]{:S(2)}) collective-permute-start(bf16[2,144,256]{2,1,0:T(8,128)(2,1)S(1)} %get-tuple-element.116), channel_id=1, source_target_pairs={{0,2},{1,3},{2,0},{3,1},{4,6},{5,7},{6,4},{7,5},{8,10},{9,11},{10,... | collective-permute-start | bytes 442376 | tf_op jit(solution)/shard_map/ppermute | solution.py:28
  91.8 4.8 %collective-permute-done.13.refs_1_ = bf16[2,144,256]{2,1,0:T(8,128)(2,1)S(1)} collective-permute-done((bf16[2,144,256]{2,1,0:T(8,128)(2,1)S(1)}, bf16[2,144,256]{2,1,0:T(8,128)(2,1)S(1)}, u32[]{:S(2)}, u32[]{:S(2)}) %collective-permute-start.13) | collective-permute-done | bytes 147488 | tf_op jit(solution)/shard_map/ppermute | solution.py:28
  96.7 2.1 %collective-permute-start.15 = (bf16[2,1,144,256]{3,2,1,0:T(8,128)(2,1)S(1)}, bf16[2,1,144,256]{3,2,1,0:T(8,128)(2,1)S(1)}, u32[]{:S(2)}, u32[]{:S(2)}) collective-permute-start(bf16[2,1,144,256]{3,2,1,0:T(8,128)(2,1)S(1)} %get-tuple-element.119), channel_id=1, source_target_pairs={{0,8},{1,9},{2,10},{3,11},{4,12},{5,13},{6,14},{7,15},{8,0},{9,1},... | collective-permute-start | bytes 442376 | tf_op jit(solution)/shard_map/ppermute | solution.py:28
  98.7 5.6 %collective-permute-done.15.refs_2_ = bf16[2,1,144,256]{3,2,1,0:T(8,128)(2,1)S(1)} collective-permute-done((bf16[2,1,144,256]{3,2,1,0:T(8,128)(2,1)S(1)}, bf16[2,1,144,256]{3,2,1,0:T(8,128)(2,1)S(1)}, u32[]{:S(2)}, u32[]{:S(2)}) %collective-permute-start.15) | collective-permute-done | bytes 147488 | tf_op jit(solution)/shard_map/ppermute | solution.py:28
  104.4 0.9 combine.1
  105.3 0.1 collective-permute-start.16
  105.4 1.2 collective-permute-done.16.got_ref
  106.6 1.2 finish.3
  107.8 2.0 %collective-permute-start.21 = (bf16[2,160,128]{2,1,0:T(8,128)(2,1)S(1)}, bf16[2,160,128]{2,1,0:T(8,128)(2,1)S(1)}, u32[]{:S(2)}, u32[]{:S(2)}) collective-permute-start(bf16[2,160,128]{2,1,0:T(8,128)(2,1)S(1)} %get-tuple-element.128), channel_id=1, source_target_pairs={{0,12},{1,13},{2,14},{3,15},{4,8},{5,9},{6,10},{7,11},{8,4},{9,5},... | collective-permute-start | bytes 245768 | tf_op jit(solution)/shard_map/ppermute | solution.py:28
  109.8 1.6 %collective-permute-start.22 = (bf16[2,160,128]{2,1,0:T(8,128)(2,1)S(1)}, bf16[2,160,128]{2,1,0:T(8,128)(2,1)S(1)}, u32[]{:S(2)}, u32[]{:S(2)}) collective-permute-start(bf16[2,160,128]{2,1,0:T(8,128)(2,1)S(1)} %get-tuple-element.129), channel_id=1, source_target_pairs={{0,2},{1,3},{2,0},{3,1},{4,6},{5,7},{6,4},{7,5},{8,10},{9,11},{10,... | collective-permute-start | bytes 245768 | tf_op jit(solution)/shard_map/ppermute | solution.py:28
  111.4 1.7 %collective-permute-start.23 = (bf16[2,160,128]{2,1,0:T(8,128)(2,1)S(1)}, bf16[2,160,128]{2,1,0:T(8,128)(2,1)S(1)}, u32[]{:S(2)}, u32[]{:S(2)}) collective-permute-start(bf16[2,160,128]{2,1,0:T(8,128)(2,1)S(1)} %get-tuple-element.130), channel_id=1, source_target_pairs={{0,14},{1,15},{2,12},{3,13},{4,10},{5,11},{6,8},{7,9},{8,6},{9,7},... | collective-permute-start | bytes 245768 | tf_op jit(solution)/shard_map/ppermute | solution.py:28
  113.2 1.2 finish.2
  114.3 0.1 collective-permute-start.17
  114.4 3.5 %collective-permute-start.18 = (bf16[2,160,128]{2,1,0:T(8,128)(2,1)S(1)}, bf16[2,160,128]{2,1,0:T(8,128)(2,1)S(1)}, u32[]{:S(2)}, u32[]{:S(2)}) collective-permute-start(bf16[2,160,128]{2,1,0:T(8,128)(2,1)S(1)} %get-tuple-element.123), channel_id=1, source_target_pairs={{0,6},{1,7},{2,4},{3,5},{4,2},{5,3},{6,0},{7,1},{8,14},{9,15},{10,... | collective-permute-start | bytes 245768 | tf_op jit(solution)/shard_map/ppermute | solution.py:28
  118.0 2.3 %collective-permute-start.20 = (bf16[2,160,128]{2,1,0:T(8,128)(2,1)S(1)}, bf16[2,160,128]{2,1,0:T(8,128)(2,1)S(1)}, u32[]{:S(2)}, u32[]{:S(2)}) collective-permute-start(bf16[2,160,128]{2,1,0:T(8,128)(2,1)S(1)} %get-tuple-element.125), channel_id=1, source_target_pairs={{0,4},{1,5},{2,6},{3,7},{4,0},{5,1},{6,2},{7,3},{8,12},{9,13},{10,... | collective-permute-start | bytes 245768 | tf_op jit(solution)/shard_map/ppermute | solution.py:28
  120.3 0.1 collective-permute-start.25
  120.4 1.5 %collective-permute-done.17.refs_0_ = bf16[2,160,128]{2,1,0:T(8,128)(2,1)S(1)} collective-permute-done((bf16[2,160,128]{2,1,0:T(8,128)(2,1)S(1)}, bf16[2,160,128]{2,1,0:T(8,128)(2,1)S(1)}, u32[]{:S(2)}, u32[]{:S(2)}) %collective-permute-start.17) | collective-permute-done | bytes 81952 | tf_op jit(solution)/shard_map/ppermute | solution.py:28
  121.9 0.5 collective-permute-done.18.refs_1_
  122.4 3.1 %collective-permute-done.19.refs_2_ = bf16[2,160,128]{2,1,0:T(8,128)(2,1)S(1)} collective-permute-done((bf16[2,160,128]{2,1,0:T(8,128)(2,1)S(1)}, bf16[2,160,128]{2,1,0:T(8,128)(2,1)S(1)}, u32[]{:S(2)}, u32[]{:S(2)}) %collective-permute-start.19) | collective-permute-done | bytes 81952 | tf_op jit(solution)/shard_map/ppermute | solution.py:28
  125.5 0.1 collective-permute-start.24
  125.6 1.4 %collective-permute-done.24.refs_8_ = bf16[4,160,128]{2,1,0:T(8,128)(2,1)S(1)} collective-permute-done((bf16[4,160,128]{2,1,0:T(8,128)(2,1)S(1)}, bf16[4,160,128]{2,1,0:T(8,128)(2,1)S(1)}, u32[]{:S(2)}, u32[]{:S(2)}) %collective-permute-start.24) | collective-permute-done | bytes 163872 | tf_op jit(solution)/shard_map/ppermute | solution.py:28
  127.0 1.5 %unpack.1 = (bf16[128,2048]{1,0:T(8,128)(2,1)}, bf16[16,4096]{1,0:T(8,128)(2,1)}) custom-call(s32[5]{0:T(128)S(1)} %stack.19.place_ref, bf16[2,160,128]{2,1,0:T(8,128)(2,1)S(1)} %collective-permute-done.17.refs_0_, bf16[2,160,128]{2,1,0:T(8,128)(2,1)S(1)} %collective-permute-done.18.refs_1_, bf16[2,160,128]{2,1,0:T(8,128)(2,1)S(1)} %collective-permute-done.19.refs_2_, ...), custom_call_target="tpu_custom_call" | custom-call | tf_op jit(solution)/shard_map/unpack/pallas_call | solution.py:337
  (29 shorter events, 0.3 us)
Async XLA Ops:
  2.2 1.0 copy-start.4
  4.7 8.3 %copy-start.3 = (bf16[1,256,1184]{1,2,0:T(8,128)(2,1)S(1)}, bf16[1,256,1184]{1,2,0:T(8,128)(2,1)}, u32[]{:S(2)}) copy-start(bf16[1,256,1184]{1,2,0:T(8,128)(2,1)} %param.10) | copy-start | bytes 1818628
  4.7 46.5 %all-to-all-start = ((bf16[16,384,128]{2,1,0:T(8,128)(2,1)}), bf16[16,384,128]{2,1,0:T(8,128)(2,1)S(1)}, u32[]{:S(2)}, u32[]{:S(2)}) async-start(bf16[16,384,128]{2,1,0:T(8,128)(2,1)} %pack.1), calls=%async_computation | async-start | bytes 3145728 | tf_op jit(solution)/shard_map/all_to_all | solution.py:659
  13.0 3.4 %copy-start = (bf16[1184,3584]{1,0:T(8,128)(2,1)S(1)}, bf16[1184,3584]{1,0:T(8,128)(2,1)}, u32[]{:S(2)}) copy-start(bf16[1184,3584]{1,0:T(8,128)(2,1)} %weight_ref.1) | copy-start | bytes 25460740
  19.9 2.6 %collective-permute-start = (bf16[8,16,3584]{2,1,0:T(8,128)(2,1)S(1)}, bf16[8,16,3584]{2,1,0:T(8,128)(2,1)S(1)}, u32[]{:S(2)}, u32[]{:S(2)}) collective-permute-start(bf16[8,16,3584]{2,1,0:T(8,128)(2,1)S(1)} %get-tuple-element.72), channel_id=1, source_target_pairs={{0,1},{1,0},{2,3},{3,2},{4,5},{5,4},{6,7},{7,6},{8,9},{9,8},{10,11... | collective-permute-start | bytes 2752520 | tf_op jit(solution)/shard_map/ppermute | solution.py:28
  22.6 28.6 %copy-start.1 = (bf16[192,4096]{1,0:T(8,128)(2,1)S(1)}, bf16[192,4096]{1,0:T(8,128)(2,1)}, u32[]{:S(2)}) copy-start(bf16[192,4096]{1,0:T(8,128)(2,1)} %refs_7_.1) | copy-start | bytes 4718596
  22.6 32.9 %copy-start.6 = (bf16[3584]{0:T(1024)(128)(2,1)S(1)}, bf16[3584]{0:T(1024)(128)(2,1)}, u32[]{:S(2)}) copy-start(bf16[3584]{0:T(1024)(128)(2,1)} %param.12) | copy-start | bytes 21508
  22.6 18.4 %collective-permute-start.1 = (bf16[4,16,3584]{2,1,0:T(8,128)(2,1)S(1)}, bf16[4,16,3584]{2,1,0:T(8,128)(2,1)S(1)}, u32[]{:S(2)}, u32[]{:S(2)}) collective-permute-start(bf16[4,16,3584]{2,1,0:T(8,128)(2,1)S(1)} %get-tuple-element.74), channel_id=1, source_target_pairs={{0,2},{1,3},{2,0},{3,1},{4,6},{5,7},{6,4},{7,5},{8,10},{9,11},{10,... | collective-permute-start | bytes 1376264 | tf_op jit(solution)/shard_map/ppermute | solution.py:28
  41.1 10.1 %collective-permute-start.2 = (bf16[2,16,3584]{2,1,0:T(8,128)(2,1)S(1)}, bf16[2,16,3584]{2,1,0:T(8,128)(2,1)S(1)}, u32[]{:S(2)}, u32[]{:S(2)}) collective-permute-start(bf16[2,16,3584]{2,1,0:T(8,128)(2,1)S(1)} %get-tuple-element.76), channel_id=1, source_target_pairs={{0,4},{1,5},{2,6},{3,7},{4,0},{5,1},{6,2},{7,3},{8,12},{9,13},{10,... | collective-permute-start | bytes 688136 | tf_op jit(solution)/shard_map/ppermute | solution.py:28
  51.2 20.2 %collective-permute-start.7 = (bf16[192,4096]{1,0:T(8,128)(2,1)S(1)}, bf16[192,4096]{1,0:T(8,128)(2,1)S(1)}, u32[]{:S(2)}, u32[]{:S(2)}) collective-permute-start(bf16[192,4096]{1,0:T(8,128)(2,1)S(1)} %copy-done.1), channel_id=1, source_target_pairs={{0,1},{1,0},{2,3},{3,2},{4,5},{5,4},{6,7},{7,6},{8,9},{9,8},{10,11... | collective-permute-start | bytes 4718600 | tf_op jit(solution)/shard_map/ppermute | solution.py:28
  51.3 20.1 %collective-permute-start.6 = (bf16[192,3584]{1,0:T(8,128)(2,1)}, bf16[192,3584]{1,0:T(8,128)(2,1)S(1)}, u32[]{:S(2)}, u32[]{:S(2)}) collective-permute-start(bf16[192,3584]{1,0:T(8,128)(2,1)} %bitcast.22), channel_id=1, source_target_pairs={{0,1},{1,0},{2,3},{3,2},{4,5},{5,4},{6,7},{7,6},{8,9},{9,8},{10,11... | collective-permute-start | bytes 4128776 | tf_op jit(solution)/shard_map/ppermute | solution.py:28
  51.8 13.8 %collective-permute-start.3 = (bf16[2,16,3584]{2,1,0:T(8,128)(2,1)S(1)}, bf16[2,16,3584]{2,1,0:T(8,128)(2,1)S(1)}, u32[]{:S(2)}, u32[]{:S(2)}) collective-permute-start(bf16[2,16,3584]{2,1,0:T(8,128)(2,1)S(1)} %add_all.1.mine_ref), channel_id=1, source_target_pairs={{0,8},{1,9},{2,10},{3,11},{4,12},{5,13},{6,14},{7,15},{8,0},{9,1},... | collective-permute-start | bytes 688136 | tf_op jit(solution)/shard_map/ppermute | solution.py:28
  55.5 11.2 %collective-permute-start.8 = (bf16[2,192,256]{2,1,0:T(8,128)(2,1)}, bf16[2,192,256]{2,1,0:T(8,128)(2,1)S(1)}, u32[]{:S(2)}, u32[]{:S(2)}) collective-permute-start(bf16[2,192,256]{2,1,0:T(8,128)(2,1)} %bitcast.26), channel_id=1, source_target_pairs={{0,1},{1,0},{2,3},{3,2},{4,5},{5,4},{6,7},{7,6},{8,9},{9,8},{10,11... | collective-permute-start | bytes 589832 | tf_op jit(solution)/shard_map/ppermute | solution.py:28
  65.8 4.9 %collective-permute-start.5 = (bf16[32,1792]{1,0:T(8,128)(2,1)S(1)}, bf16[32,1792]{1,0:T(8,128)(2,1)S(1)}, u32[]{:S(2)}, u32[]{:S(2)}) collective-permute-start(bf16[32,1792]{1,0:T(8,128)(2,1)S(1)} %bitcast.30), channel_id=1, source_target_pairs={{0,2},{1,3},{2,0},{3,1},{4,6},{5,7},{6,4},{7,5},{8,10},{9,11},{10,... | collective-permute-start | bytes 344072 | tf_op jit(solution)/shard_map/ppermute | solution.py:28
  66.6 4.8 %collective-permute-start.4 = (bf16[32,1792]{1,0:T(8,128)(2,1)S(1)}, bf16[32,1792]{1,0:T(8,128)(2,1)S(1)}, u32[]{:S(2)}, u32[]{:S(2)}) collective-permute-start(bf16[32,1792]{1,0:T(8,128)(2,1)S(1)} %bitcast.28), channel_id=1, source_target_pairs={{0,4},{1,5},{2,6},{3,7},{4,0},{5,1},{6,2},{7,3},{8,12},{9,13},{10,... | collective-permute-start | bytes 344072 | tf_op jit(solution)/shard_map/ppermute | solution.py:28
  66.8 0.9 copy-start.5
  71.4 7.4 %copy-start.2 = (bf16[3584,192]{0,1:T(8,128)(2,1)S(1)}, bf16[3584,192]{0,1:T(8,128)(2,1)}, u32[]{:S(2)}) copy-start(bf16[3584,192]{0,1:T(8,128)(2,1)} %param.13) | copy-start | bytes 4128772
  71.5 6.1 %collective-permute-start.9 = (bf16[64,1792]{1,0:T(8,128)(2,1)S(1)}, bf16[64,1792]{1,0:T(8,128)(2,1)S(1)}, u32[]{:S(2)}, u32[]{:S(2)}) collective-permute-start(bf16[64,1792]{1,0:T(8,128)(2,1)S(1)} %get-tuple-element.90.refs_0_), channel_id=1, source_target_pairs={{0,2},{1,3},{2,0},{3,1},{4,6},{5,7},{6,4},{7,5},{8,10},{9,11},{10,... | collective-permute-start | bytes 688136 | tf_op jit(solution)/shard_map/ppermute | solution.py:28
  72.8 6.0 %collective-permute-start.10 = (bf16[64,1792]{1,0:T(8,128)(2,1)S(1)}, bf16[64,1792]{1,0:T(8,128)(2,1)S(1)}, u32[]{:S(2)}, u32[]{:S(2)}) collective-permute-start(bf16[64,1792]{1,0:T(8,128)(2,1)S(1)} %get-tuple-element.91.refs_2_), channel_id=1, source_target_pairs={{0,4},{1,5},{2,6},{3,7},{4,0},{5,1},{6,2},{7,3},{8,12},{9,13},{10,... | collective-permute-start | bytes 688136 | tf_op jit(solution)/shard_map/ppermute | solution.py:28
  81.3 6.8 %collective-permute-start.11 = (bf16[4,144,256]{2,1,0:T(8,128)(2,1)S(1)}, bf16[4,144,256]{2,1,0:T(8,128)(2,1)S(1)}, u32[]{:S(2)}, u32[]{:S(2)}) collective-permute-start(bf16[4,144,256]{2,1,0:T(8,128)(2,1)S(1)} %get-tuple-element.106), channel_id=1, source_target_pairs={{0,2},{1,3},{2,0},{3,1},{4,6},{5,7},{6,4},{7,5},{8,10},{9,11},{10,... | collective-permute-start | bytes 884744 | tf_op jit(solution)/shard_map/ppermute | solution.py:28
  82.1 8.0 %collective-permute-start.12 = (bf16[4,144,256]{2,1,0:T(8,128)(2,1)S(1)}, bf16[4,144,256]{2,1,0:T(8,128)(2,1)S(1)}, u32[]{:S(2)}, u32[]{:S(2)}) collective-permute-start(bf16[4,144,256]{2,1,0:T(8,128)(2,1)S(1)} %get-tuple-element.107), channel_id=1, source_target_pairs={{0,4},{1,5},{2,6},{3,7},{4,0},{5,1},{6,2},{7,3},{8,12},{9,13},{10,... | collective-permute-start | bytes 884744 | tf_op jit(solution)/shard_map/ppermute | solution.py:28
  90.2 6.4 %collective-permute-start.13 = (bf16[2,144,256]{2,1,0:T(8,128)(2,1)S(1)}, bf16[2,144,256]{2,1,0:T(8,128)(2,1)S(1)}, u32[]{:S(2)}, u32[]{:S(2)}) collective-permute-start(bf16[2,144,256]{2,1,0:T(8,128)(2,1)S(1)} %get-tuple-element.114), channel_id=1, source_target_pairs={{0,4},{1,5},{2,6},{3,7},{4,0},{5,1},{6,2},{7,3},{8,12},{9,13},{10,... | collective-permute-start | bytes 442376 | tf_op jit(solution)/shard_map/ppermute | solution.py:28
  90.2 6.4 %collective-permute-start.14 = (bf16[2,144,256]{2,1,0:T(8,128)(2,1)S(1)}, bf16[2,144,256]{2,1,0:T(8,128)(2,1)S(1)}, u32[]{:S(2)}, u32[]{:S(2)}) collective-permute-start(bf16[2,144,256]{2,1,0:T(8,128)(2,1)S(1)} %get-tuple-element.116), channel_id=1, source_target_pairs={{0,2},{1,3},{2,0},{3,1},{4,6},{5,7},{6,4},{7,5},{8,10},{9,11},{10,... | collective-permute-start | bytes 442376 | tf_op jit(solution)/shard_map/ppermute | solution.py:28
  96.7 7.7 %collective-permute-start.15 = (bf16[2,1,144,256]{3,2,1,0:T(8,128)(2,1)S(1)}, bf16[2,1,144,256]{3,2,1,0:T(8,128)(2,1)S(1)}, u32[]{:S(2)}, u32[]{:S(2)}) collective-permute-start(bf16[2,1,144,256]{3,2,1,0:T(8,128)(2,1)S(1)} %get-tuple-element.119), channel_id=1, source_target_pairs={{0,8},{1,9},{2,10},{3,11},{4,12},{5,13},{6,14},{7,15},{8,0},{9,1},... | collective-permute-start | bytes 442376 | tf_op jit(solution)/shard_map/ppermute | solution.py:28
  105.3 1.3 %collective-permute-start.16 = (bf16[128,256]{1,0:T(8,128)(2,1)S(1)}, bf16[128,256]{1,0:T(8,128)(2,1)S(1)}, u32[]{:S(2)}, u32[]{:S(2)}) collective-permute-start(bf16[128,256]{1,0:T(8,128)(2,1)S(1)} %get-tuple-element.121), channel_id=1, source_target_pairs={{0,1},{1,0},{2,3},{3,2},{4,5},{5,4},{6,7},{7,6},{8,9},{9,8},{10,11... | collective-permute-start | bytes 196616 | tf_op jit(solution)/shard_map/ppermute | solution.py:28
  107.8 10.2 %collective-permute-start.21 = (bf16[2,160,128]{2,1,0:T(8,128)(2,1)S(1)}, bf16[2,160,128]{2,1,0:T(8,128)(2,1)S(1)}, u32[]{:S(2)}, u32[]{:S(2)}) collective-permute-start(bf16[2,160,128]{2,1,0:T(8,128)(2,1)S(1)} %get-tuple-element.128), channel_id=1, source_target_pairs={{0,12},{1,13},{2,14},{3,15},{4,8},{5,9},{6,10},{7,11},{8,4},{9,5},... | collective-permute-start | bytes 245768 | tf_op jit(solution)/shard_map/ppermute | solution.py:28
  109.8 8.1 %collective-permute-start.22 = (bf16[2,160,128]{2,1,0:T(8,128)(2,1)S(1)}, bf16[2,160,128]{2,1,0:T(8,128)(2,1)S(1)}, u32[]{:S(2)}, u32[]{:S(2)}) collective-permute-start(bf16[2,160,128]{2,1,0:T(8,128)(2,1)S(1)} %get-tuple-element.129), channel_id=1, source_target_pairs={{0,2},{1,3},{2,0},{3,1},{4,6},{5,7},{6,4},{7,5},{8,10},{9,11},{10,... | collective-permute-start | bytes 245768 | tf_op jit(solution)/shard_map/ppermute | solution.py:28
  111.4 8.9 %collective-permute-start.23 = (bf16[2,160,128]{2,1,0:T(8,128)(2,1)S(1)}, bf16[2,160,128]{2,1,0:T(8,128)(2,1)S(1)}, u32[]{:S(2)}, u32[]{:S(2)}) collective-permute-start(bf16[2,160,128]{2,1,0:T(8,128)(2,1)S(1)} %get-tuple-element.130), channel_id=1, source_target_pairs={{0,14},{1,15},{2,12},{3,13},{4,10},{5,11},{6,8},{7,9},{8,6},{9,7},... | collective-permute-start | bytes 245768 | tf_op jit(solution)/shard_map/ppermute | solution.py:28
  114.3 7.6 %collective-permute-start.17 = (bf16[2,160,128]{2,1,0:T(8,128)(2,1)S(1)}, bf16[2,160,128]{2,1,0:T(8,128)(2,1)S(1)}, u32[]{:S(2)}, u32[]{:S(2)}) collective-permute-start(bf16[2,160,128]{2,1,0:T(8,128)(2,1)S(1)} %get-tuple-element.122), channel_id=1, source_target_pairs={{0,8},{1,9},{2,10},{3,11},{4,12},{5,13},{6,14},{7,15},{8,0},{9,1},... | collective-permute-start | bytes 245768 | tf_op jit(solution)/shard_map/ppermute | solution.py:28
  114.4 8.0 %collective-permute-start.18 = (bf16[2,160,128]{2,1,0:T(8,128)(2,1)S(1)}, bf16[2,160,128]{2,1,0:T(8,128)(2,1)S(1)}, u32[]{:S(2)}, u32[]{:S(2)}) collective-permute-start(bf16[2,160,128]{2,1,0:T(8,128)(2,1)S(1)} %get-tuple-element.123), channel_id=1, source_target_pairs={{0,6},{1,7},{2,4},{3,5},{4,2},{5,3},{6,0},{7,1},{8,14},{9,15},{10,... | collective-permute-start | bytes 245768 | tf_op jit(solution)/shard_map/ppermute | solution.py:28
  118.0 7.6 %collective-permute-start.19 = (bf16[2,160,128]{2,1,0:T(8,128)(2,1)S(1)}, bf16[2,160,128]{2,1,0:T(8,128)(2,1)S(1)}, u32[]{:S(2)}, u32[]{:S(2)}) collective-permute-start(bf16[2,160,128]{2,1,0:T(8,128)(2,1)S(1)} %get-tuple-element.124), channel_id=1, source_target_pairs={{0,10},{1,11},{2,8},{3,9},{4,14},{5,15},{6,12},{7,13},{8,2},{9,3},... | collective-permute-start | bytes 245768 | tf_op jit(solution)/shard_map/ppermute | solution.py:28
  118.0 7.6 %collective-permute-start.20 = (bf16[2,160,128]{2,1,0:T(8,128)(2,1)S(1)}, bf16[2,160,128]{2,1,0:T(8,128)(2,1)S(1)}, u32[]{:S(2)}, u32[]{:S(2)}) collective-permute-start(bf16[2,160,128]{2,1,0:T(8,128)(2,1)S(1)} %get-tuple-element.125), channel_id=1, source_target_pairs={{0,4},{1,5},{2,6},{3,7},{4,0},{5,1},{6,2},{7,3},{8,12},{9,13},{10,... | collective-permute-start | bytes 245768 | tf_op jit(solution)/shard_map/ppermute | solution.py:28
  120.3 5.3 %collective-permute-start.25 = (bf16[4,160,128]{2,1,0:T(8,128)(2,1)S(1)}, bf16[4,160,128]{2,1,0:T(8,128)(2,1)S(1)}, u32[]{:S(2)}, u32[]{:S(2)}) collective-permute-start(bf16[4,160,128]{2,1,0:T(8,128)(2,1)S(1)} %gather_other.3), channel_id=1, source_target_pairs={{0,1},{1,0},{2,3},{3,2},{4,5},{5,4},{6,7},{7,6},{8,9},{9,8},{10,11... | collective-permute-start | bytes 491528 | tf_op jit(solution)/shard_map/ppermute | solution.py:28
  125.5 1.5 %collective-permute-start.24 = (bf16[4,160,128]{2,1,0:T(8,128)(2,1)S(1)}, bf16[4,160,128]{2,1,0:T(8,128)(2,1)S(1)}, u32[]{:S(2)}, u32[]{:S(2)}) collective-permute-start(bf16[4,160,128]{2,1,0:T(8,128)(2,1)S(1)} %gather_other.2), channel_id=1, source_target_pairs={{0,1},{1,0},{2,3},{3,2},{4,5},{5,4},{6,7},{7,6},{8,9},{9,8},{10,11... | collective-permute-start | bytes 491528 | tf_op jit(solution)/shard_map/ppermute | solution.py:28

commit v22 on v20

--- a/solution.py
+++ b/solution.py
@@ -404,7 +404,7 @@
 
 def send_order(chips):
     half = chips // 2
-    turns = [mask for at in range(half) for mask in (half + at, half - 1 - at)]
+    turns = [mask for at in range(half) for mask in (half + at, (at + 1) % half)]
     return turns[:half], turns[half:]
 
 

time: 128 us -> 129 us (level)
  waiting for transfers between devices: 60.8 us -> 62.5 us
    ppermute x29, waiting for transfers between devices: 60.8 us -> 62.5 us  [swap(): return lax.ppermute(value, 'seq', [(i, i ^ mask) for i in range(devices)])]
  transfers between devices with their start and end apart: 30 -> 30, of which waited for: 20 -> 19; matrix products, arithmetic and copies ran while one was open for 0% -> 0% of each run, Pallas kernels for 10% -> 10%
where the time goes in v22:
time: 129 us
  waiting for transfers between devices  62.5 us (48%)
  starting transfers between devices  35.9 us (28%)
  Pallas kernels  21.1 us (16%)
  local copies, waits for them, and re-layouts  7.06 us (5%)
  between operations  2.24 us (2%)
    ppermute x29, waiting for transfers between devices, swap(): return lax.ppermute(value, 'seq', [(i, i ^ mask) for i in range(devices)])  62.5 us
    ppermute x29, starting transfers between devices, swap(): return lax.ppermute(value, 'seq', [(i, i ^ mask) for i in range(devices)])  28.4 us
    pallas_call x2, Pallas kernels, image_attention(): pl.pallas_call(functools.partial(image_kernel, factor, masks, img_dev), o...  8.03 us
    all_to_all x1, starting transfers between devices, exchange(): return lax.all_to_all(rows, 'seq', split_axis=0, concat_axis=0, tiled=True)  7.49 us
    unnamed x14, local copies, waits for them, and re-layouts  5.31 us
    pallas_call x1, Pallas kernels, encoder(): pl.pallas_call(functools.partial(encoder_kernel, lanes), out_shape=(out,)...  3.47 us
  transfers between devices with their start and end apart: 30, of which 19 were waited for; matrix products, arithmetic and copies ran while one was open for 0% of the time, Pallas kernels for 10%

profile of v22, /device:TPU:0, one launch (start us, length us, event | category | flops | bytes accessed | tf_op | source)
XLA Modules:
  0.0 128.9 jit_solution(2627390412385673692)
XLA Ops:
  0.6 1.6 %copy.12 = bf16[1,128,2,2048]{3,1,2,0:T(8,128)(2,1)S(1)} copy(bf16[1,128,2,2048]{3,2,1,0:T(2,128)(2,1)} %param.19) | data formatting | bytes 2097152 | tf_op jit(solution)/shard_map/optimization_barrier | solution.py:647
  2.3 1.0 copy-done.4
  3.3 1.4 %pack.1 = bf16[16,384,128]{2,1,0:T(8,128)(2,1)} custom-call(bf16[128,2048]{1,0:T(8,128)(2,1)S(1)} %bitcast.25, bf16[128,2048]{1,0:T(8,128)(2,1)S(1)} %get-tuple-element.147.keys_ref, bf16[128,2048]{1,0:T(8,128)(2,1)S(1)} %get-tuple-element.146.values_ref), custom_call_target="tpu_custom_call" | custom-call | bytes 3145728 | tf_op jit(solution)/shard_map/pack/pallas_call | solution.py:306
  4.7 7.5 %all-to-all-start = ((bf16[16,384,128]{2,1,0:T(8,128)(2,1)}), bf16[16,384,128]{2,1,0:T(8,128)(2,1)S(1)}, u32[]{:S(2)}, u32[]{:S(2)}) async-start(bf16[16,384,128]{2,1,0:T(8,128)(2,1)} %pack.1), calls=%async_computation | async-start | bytes 3145728 | tf_op jit(solution)/shard_map/all_to_all | solution.py:645
  12.9 0.1 stack.19.place_ref
  13.0 3.4 %copy-done = bf16[1184,3584]{1,0:T(8,128)(2,1)S(1)} copy-done((bf16[1184,3584]{1,0:T(8,128)(2,1)S(1)}, bf16[1184,3584]{1,0:T(8,128)(2,1)}, u32[]{:S(2)}) %copy-start) | copy-done | bytes 8486936
  16.4 3.5 %encoder.1 = (bf16[8,16,1792]{2,1,0:T(8,128)(2,1)S(1)}, bf16[8,16,1792]{2,1,0:T(8,128)(2,1)S(1)}, bf16[8,16,1792]{2,1,0:T(8,128)(2,1)S(1)}, bf16[8,16,1792]{2,1,0:T(8,128)(2,1)S(1)}) custom-call(s32[5]{0:T(128)S(1)} %stack.19.place_ref, bf16[1184,256]{1,0:T(8,128)(2,1)S(1)} %bitcast.24, bf16[1184,3584]{1,0:T(8,128)(2,1)S(1)} %copy-done), custom_call_target="tpu_custom_call" | custom-call | flops 2172649472 | bytes 10928128 | tf_op jit(solution)/shard_map/encoder/pallas_call | solution.py:84
  19.8 0.5 collective-permute-start
  20.3 0.1 collective-permute-start.1
  20.4 1.3 %collective-permute-done.refs_1_ = bf16[8,16,1792]{2,1,0:T(8,128)(2,1)S(1)} collective-permute-done((bf16[8,16,1792]{2,1,0:T(8,128)(2,1)S(1)}, bf16[8,16,1792]{2,1,0:T(8,128)(2,1)S(1)}, u32[]{:S(2)}, u32[]{:S(2)}) %collective-permute-start) | collective-permute-done | bytes 458784 | tf_op jit(solution)/shard_map/ppermute | solution.py:28
  21.7 0.7 collective-permute-done.1.refs_3_
  22.4 0.2 add_halves.4
  22.6 2.0 %collective-permute-start.2 = (bf16[4,16,1792]{2,1,0:T(8,128)(2,1)S(1)}, bf16[4,16,1792]{2,1,0:T(8,128)(2,1)S(1)}, u32[]{:S(2)}, u32[]{:S(2)}) collective-permute-start(bf16[4,16,1792]{2,1,0:T(8,128)(2,1)S(1)} %get-tuple-element.82), channel_id=1, source_target_pairs={{0,2},{1,3},{2,0},{3,1},{4,6},{5,7},{6,4},{7,5},{8,10},{9,11},{10,... | collective-permute-start | bytes 688136 | tf_op jit(solution)/shard_map/ppermute | solution.py:28
  24.6 1.5 %collective-permute-start.3 = (bf16[4,16,1792]{2,1,0:T(8,128)(2,1)S(1)}, bf16[4,16,1792]{2,1,0:T(8,128)(2,1)S(1)}, u32[]{:S(2)}, u32[]{:S(2)}) collective-permute-start(bf16[4,16,1792]{2,1,0:T(8,128)(2,1)S(1)} %get-tuple-element.84), channel_id=1, source_target_pairs={{0,4},{1,5},{2,6},{3,7},{4,0},{5,1},{6,2},{7,3},{8,12},{9,13},{10,... | collective-permute-start | bytes 688136 | tf_op jit(solution)/shard_map/ppermute | solution.py:28
  26.0 10.1 %collective-permute-done.2.refs_1_ = bf16[4,16,1792]{2,1,0:T(8,128)(2,1)S(1)} collective-permute-done((bf16[4,16,1792]{2,1,0:T(8,128)(2,1)S(1)}, bf16[4,16,1792]{2,1,0:T(8,128)(2,1)S(1)}, u32[]{:S(2)}, u32[]{:S(2)}) %collective-permute-start.2) | collective-permute-done | bytes 229408 | tf_op jit(solution)/shard_map/ppermute | solution.py:28
  36.1 7.6 %collective-permute-done.3.refs_3_ = bf16[4,16,1792]{2,1,0:T(8,128)(2,1)S(1)} collective-permute-done((bf16[4,16,1792]{2,1,0:T(8,128)(2,1)S(1)}, bf16[4,16,1792]{2,1,0:T(8,128)(2,1)S(1)}, u32[]{:S(2)}, u32[]{:S(2)}) %collective-permute-start.3) | collective-permute-done | bytes 229408 | tf_op jit(solution)/shard_map/ppermute | solution.py:28
  43.7 2.5 %collective-permute-start.4 = (bf16[2,16,1792]{2,1,0:T(8,128)(2,1)S(1)}, bf16[2,16,1792]{2,1,0:T(8,128)(2,1)S(1)}, u32[]{:S(2)}, u32[]{:S(2)}) collective-permute-start(bf16[2,16,1792]{2,1,0:T(8,128)(2,1)S(1)} %get-tuple-element.86), channel_id=1, source_target_pairs={{0,4},{1,5},{2,6},{3,7},{4,0},{5,1},{6,2},{7,3},{8,12},{9,13},{10,... | collective-permute-start | bytes 344072 | tf_op jit(solution)/shard_map/ppermute | solution.py:28
  46.3 1.7 %collective-permute-start.5 = (bf16[2,16,1792]{2,1,0:T(8,128)(2,1)S(1)}, bf16[2,16,1792]{2,1,0:T(8,128)(2,1)S(1)}, u32[]{:S(2)}, u32[]{:S(2)}) collective-permute-start(bf16[2,16,1792]{2,1,0:T(8,128)(2,1)S(1)} %get-tuple-element.88), channel_id=1, source_target_pairs={{0,2},{1,3},{2,0},{3,1},{4,6},{5,7},{6,4},{7,5},{8,10},{9,11},{10,... | collective-permute-start | bytes 344072 | tf_op jit(solution)/shard_map/ppermute | solution.py:28
  48.0 1.5 %collective-permute-done.4.got0 = bf16[2,16,1792]{2,1,0:T(8,128)(2,1)S(1)} collective-permute-done((bf16[2,16,1792]{2,1,0:T(8,128)(2,1)S(1)}, bf16[2,16,1792]{2,1,0:T(8,128)(2,1)S(1)}, u32[]{:S(2)}, u32[]{:S(2)}) %collective-permute-start.4) | collective-permute-done | bytes 114720 | tf_op jit(solution)/shard_map/ppermute | solution.py:28
  49.5 1.6 %collective-permute-done.5.got1 = bf16[2,16,1792]{2,1,0:T(8,128)(2,1)S(1)} collective-permute-done((bf16[2,16,1792]{2,1,0:T(8,128)(2,1)S(1)}, bf16[2,16,1792]{2,1,0:T(8,128)(2,1)S(1)}, u32[]{:S(2)}, u32[]{:S(2)}) %collective-permute-start.5) | collective-permute-done | bytes 114720 | tf_op jit(solution)/shard_map/ppermute | solution.py:28
  51.1 0.1 collective-permute-start.10
  51.2 0.5 collective-permute-start.9
  51.7 2.9 %collective-permute-start.6 = (bf16[2,2,16,1792]{3,2,1,0:T(8,128)(2,1)S(1)}, bf16[2,2,16,1792]{3,2,1,0:T(8,128)(2,1)S(1)}, u32[]{:S(2)}, u32[]{:S(2)}) collective-permute-start(bf16[2,2,16,1792]{3,2,1,0:T(8,128)(2,1)S(1)} %add_all.1.mine_ref), channel_id=1, source_target_pairs={{0,8},{1,9},{2,10},{3,11},{4,12},{5,13},{6,14},{7,15},{8,0},{9,1},... | collective-permute-start | bytes 688136 | tf_op jit(solution)/shard_map/ppermute | solution.py:28
  55.3 0.1 collective-permute-start.11
  55.3 10.0 %collective-permute-done.6.got_ref = bf16[2,2,16,1792]{3,2,1,0:T(8,128)(2,1)S(1)} collective-permute-done((bf16[2,2,16,1792]{3,2,1,0:T(8,128)(2,1)S(1)}, bf16[2,2,16,1792]{3,2,1,0:T(8,128)(2,1)S(1)}, u32[]{:S(2)}, u32[]{:S(2)}) %collective-permute-start.6) | collective-permute-done | bytes 229408 | tf_op jit(solution)/shard_map/ppermute | solution.py:28
  65.3 0.2 normalize.1
  65.5 1.6 %collective-permute-start.8 = (bf16[32,1792]{1,0:T(8,128)(2,1)S(1)}, bf16[32,1792]{1,0:T(8,128)(2,1)S(1)}, u32[]{:S(2)}, u32[]{:S(2)}) collective-permute-start(bf16[32,1792]{1,0:T(8,128)(2,1)S(1)} %bitcast.30), channel_id=1, source_target_pairs={{0,2},{1,3},{2,0},{3,1},{4,6},{5,7},{6,4},{7,5},{8,10},{9,11},{10,... | collective-permute-start | bytes 344072 | tf_op jit(solution)/shard_map/ppermute | solution.py:28
  67.2 0.9 copy-done.5
  68.1 0.2 modulation.1.refs_4_
  68.3 2.1 %collective-permute-done.8.got1 = bf16[32,1792]{1,0:T(8,128)(2,1)S(1)} collective-permute-done((bf16[32,1792]{1,0:T(8,128)(2,1)S(1)}, bf16[32,1792]{1,0:T(8,128)(2,1)S(1)}, u32[]{:S(2)}, u32[]{:S(2)}) %collective-permute-start.8) | collective-permute-done | bytes 114720 | tf_op jit(solution)/shard_map/ppermute | solution.py:28
  70.4 1.5 %collective-permute-done.7.got0 = bf16[32,1792]{1,0:T(8,128)(2,1)S(1)} collective-permute-done((bf16[32,1792]{1,0:T(8,128)(2,1)S(1)}, bf16[32,1792]{1,0:T(8,128)(2,1)S(1)}, u32[]{:S(2)}, u32[]{:S(2)}) %collective-permute-start.7) | collective-permute-done | bytes 114720 | tf_op jit(solution)/shard_map/ppermute | solution.py:28
  71.9 0.6 collective-permute-start.12
  72.5 0.4 collective-permute-start.13
  72.9 3.9 %image_attention.2 = (f32[1024,256]{1,0:T(8,128)S(1)}, f32[1024,128]{1,0:T(8,128)S(1)}) custom-call(s32[5]{0:T(128)S(1)} %stack.19.place_ref, bf16[16,384,128]{2,1,0:T(8,128)(2,1)S(1)} %all-to-all-done.packed_ref), custom_call_target="tpu_custom_call" | custom-call | flops 1073741824 | bytes 2359296 | tf_op jit(solution)/shard_map/image_attention/pallas_call | solution.py:383
  76.8 1.2 collective-permute-done.12.refs_1_
  78.0 0.5 collective-permute-done.13.refs_3_
  78.6 2.4 %project.1 = (bf16[4,144,256]{2,1,0:T(8,128)(2,1)S(1)}, bf16[4,144,256]{2,1,0:T(8,128)(2,1)S(1)}, bf16[4,144,256]{2,1,0:T(8,128)(2,1)S(1)}, bf16[4,144,256]{2,1,0:T(8,128)(2,1)S(1)}) custom-call(s32[5]{0:T(128)S(1)} %stack.19.place_ref, bf16[64,1792]{1,0:T(8,128)(2,1)S(1)} %get-tuple-element.102.refs_0_, ...), custom_call_target="tpu_custom_call" | custom-call | flops 754974720 | bytes 7864320 | tf_op jit(solution)/shard_map/project/pallas_call | solution.py:216
  81.0 1.6 %collective-permute-start.14 = (bf16[4,144,256]{2,1,0:T(8,128)(2,1)S(1)}, bf16[4,144,256]{2,1,0:T(8,128)(2,1)S(1)}, u32[]{:S(2)}, u32[]{:S(2)}) collective-permute-start(bf16[4,144,256]{2,1,0:T(8,128)(2,1)S(1)} %get-tuple-element.118), channel_id=1, source_target_pairs={{0,2},{1,3},{2,0},{3,1},{4,6},{5,7},{6,4},{7,5},{8,10},{9,11},{10,... | collective-permute-start | bytes 884744 | tf_op jit(solution)/shard_map/ppermute | solution.py:28
  82.5 0.1 collective-permute-start.15
  82.6 4.1 %image_attention.3 = (f32[1024,256]{1,0:T(8,128)S(1)}, f32[1024,128]{1,0:T(8,128)S(1)}) custom-call(s32[5]{0:T(128)S(1)} %stack.19.place_ref, bf16[16,384,128]{2,1,0:T(8,128)(2,1)S(1)} %all-to-all-done.packed_ref), custom_call_target="tpu_custom_call" | custom-call | flops 1073741824 | bytes 2359296 | tf_op jit(solution)/shard_map/image_attention/pallas_call | solution.py:383
  86.7 1.0 collective-permute-done.14.refs_1_
  87.8 2.8 %collective-permute-done.15.refs_3_ = bf16[4,144,256]{2,1,0:T(8,128)(2,1)S(1)} collective-permute-done((bf16[4,144,256]{2,1,0:T(8,128)(2,1)S(1)}, bf16[4,144,256]{2,1,0:T(8,128)(2,1)S(1)}, u32[]{:S(2)}, u32[]{:S(2)}) %collective-permute-start.15) | collective-permute-done | bytes 294944 | tf_op jit(solution)/shard_map/ppermute | solution.py:28
  90.6 0.1 add_halves.6
  90.7 0.1 collective-permute-start.16
  90.8 0.6 collective-permute-start.17
  91.4 6.1 %collective-permute-done.16.refs_1_ = bf16[2,144,256]{2,1,0:T(8,128)(2,1)S(1)} collective-permute-done((bf16[2,144,256]{2,1,0:T(8,128)(2,1)S(1)}, bf16[2,144,256]{2,1,0:T(8,128)(2,1)S(1)}, u32[]{:S(2)}, u32[]{:S(2)}) %collective-permute-start.16) | collective-permute-done | bytes 147488 | tf_op jit(solution)/shard_map/ppermute | solution.py:28
  97.5 1.3 collective-permute-start.18
  98.8 6.3 %collective-permute-done.18.refs_2_ = bf16[2,1,144,256]{3,2,1,0:T(8,128)(2,1)S(1)} collective-permute-done((bf16[2,1,144,256]{3,2,1,0:T(8,128)(2,1)S(1)}, bf16[2,1,144,256]{3,2,1,0:T(8,128)(2,1)S(1)}, u32[]{:S(2)}, u32[]{:S(2)}) %collective-permute-start.18) | collective-permute-done | bytes 147488 | tf_op jit(solution)/shard_map/ppermute | solution.py:28
  105.1 0.9 combine.1
  106.1 1.2 collective-permute-done.19.got_ref
  107.4 1.2 finish.3
  108.6 1.4 %collective-permute-start.24 = (bf16[2,160,128]{2,1,0:T(8,128)(2,1)S(1)}, bf16[2,160,128]{2,1,0:T(8,128)(2,1)S(1)}, u32[]{:S(2)}, u32[]{:S(2)}) collective-permute-start(bf16[2,160,128]{2,1,0:T(8,128)(2,1)S(1)} %get-tuple-element.140), channel_id=1, source_target_pairs={{0,12},{1,13},{2,14},{3,15},{4,8},{5,9},{6,10},{7,11},{8,4},{9,5},... | collective-permute-start | bytes 245768 | tf_op jit(solution)/shard_map/ppermute | solution.py:28
  110.0 2.4 %collective-permute-start.26 = (bf16[2,160,128]{2,1,0:T(8,128)(2,1)S(1)}, bf16[2,160,128]{2,1,0:T(8,128)(2,1)S(1)}, u32[]{:S(2)}, u32[]{:S(2)}) collective-permute-start(bf16[2,160,128]{2,1,0:T(8,128)(2,1)S(1)} %get-tuple-element.142), channel_id=1, source_target_pairs={{0,14},{1,15},{2,12},{3,13},{4,10},{5,11},{6,8},{7,9},{8,6},{9,7},... | collective-permute-start | bytes 245768 | tf_op jit(solution)/shard_map/ppermute | solution.py:28
  112.4 1.2 finish.2
  113.6 2.0 %collective-permute-start.20 = (bf16[2,160,128]{2,1,0:T(8,128)(2,1)S(1)}, bf16[2,160,128]{2,1,0:T(8,128)(2,1)S(1)}, u32[]{:S(2)}, u32[]{:S(2)}) collective-permute-start(bf16[2,160,128]{2,1,0:T(8,128)(2,1)S(1)} %get-tuple-element.134), channel_id=1, source_target_pairs={{0,8},{1,9},{2,10},{3,11},{4,12},{5,13},{6,14},{7,15},{8,0},{9,1},... | collective-permute-start | bytes 245768 | tf_op jit(solution)/shard_map/ppermute | solution.py:28
  115.6 0.8 collective-permute-start.21
  116.4 1.6 %collective-permute-start.22 = (bf16[2,160,128]{2,1,0:T(8,128)(2,1)S(1)}, bf16[2,160,128]{2,1,0:T(8,128)(2,1)S(1)}, u32[]{:S(2)}, u32[]{:S(2)}) collective-permute-start(bf16[2,160,128]{2,1,0:T(8,128)(2,1)S(1)} %get-tuple-element.136), channel_id=1, source_target_pairs={{0,10},{1,11},{2,8},{3,9},{4,14},{5,15},{6,12},{7,13},{8,2},{9,3},... | collective-permute-start | bytes 245768 | tf_op jit(solution)/shard_map/ppermute | solution.py:28
  118.0 2.1 %collective-permute-start.23 = (bf16[2,160,128]{2,1,0:T(8,128)(2,1)S(1)}, bf16[2,160,128]{2,1,0:T(8,128)(2,1)S(1)}, u32[]{:S(2)}, u32[]{:S(2)}) collective-permute-start(bf16[2,160,128]{2,1,0:T(8,128)(2,1)S(1)} %get-tuple-element.137), channel_id=1, source_target_pairs={{0,4},{1,5},{2,6},{3,7},{4,0},{5,1},{6,2},{7,3},{8,12},{9,13},{10,... | collective-permute-start | bytes 245768 | tf_op jit(solution)/shard_map/ppermute | solution.py:28
  120.1 0.1 collective-permute-start.28
  120.2 4.2 %collective-permute-done.20.refs_0_ = bf16[2,160,128]{2,1,0:T(8,128)(2,1)S(1)} collective-permute-done((bf16[2,160,128]{2,1,0:T(8,128)(2,1)S(1)}, bf16[2,160,128]{2,1,0:T(8,128)(2,1)S(1)}, u32[]{:S(2)}, u32[]{:S(2)}) %collective-permute-start.20) | collective-permute-done | bytes 81952 | tf_op jit(solution)/shard_map/ppermute | solution.py:28
  124.5 1.4 %collective-permute-done.22.refs_2_ = bf16[2,160,128]{2,1,0:T(8,128)(2,1)S(1)} collective-permute-done((bf16[2,160,128]{2,1,0:T(8,128)(2,1)S(1)}, bf16[2,160,128]{2,1,0:T(8,128)(2,1)S(1)}, u32[]{:S(2)}, u32[]{:S(2)}) %collective-permute-start.22) | collective-permute-done | bytes 81952 | tf_op jit(solution)/shard_map/ppermute | solution.py:28
  125.9 0.1 collective-permute-start.27
  126.0 1.4 %collective-permute-done.27.refs_8_ = bf16[4,160,128]{2,1,0:T(8,128)(2,1)S(1)} collective-permute-done((bf16[4,160,128]{2,1,0:T(8,128)(2,1)S(1)}, bf16[4,160,128]{2,1,0:T(8,128)(2,1)S(1)}, u32[]{:S(2)}, u32[]{:S(2)}) %collective-permute-start.27) | collective-permute-done | bytes 163872 | tf_op jit(solution)/shard_map/ppermute | solution.py:28
  127.3 1.5 %unpack.1 = (bf16[128,2048]{1,0:T(8,128)(2,1)}, bf16[16,4096]{1,0:T(8,128)(2,1)}) custom-call(s32[5]{0:T(128)S(1)} %stack.19.place_ref, bf16[2,160,128]{2,1,0:T(8,128)(2,1)S(1)} %collective-permute-done.20.refs_0_, bf16[2,160,128]{2,1,0:T(8,128)(2,1)S(1)} %collective-permute-done.21.refs_1_, bf16[2,160,128]{2,1,0:T(8,128)(2,1)S(1)} %collective-permute-done.22.refs_2_, ...), custom_call_target="tpu_custom_call" | custom-call | tf_op jit(solution)/shard_map/unpack/pallas_call | solution.py:341
  (35 shorter events, 0.5 us)
Async XLA Ops:
  2.2 1.0 copy-start.4
  4.7 8.3 %copy-start.3 = (bf16[1,256,1184]{1,2,0:T(8,128)(2,1)S(1)}, bf16[1,256,1184]{1,2,0:T(8,128)(2,1)}, u32[]{:S(2)}) copy-start(bf16[1,256,1184]{1,2,0:T(8,128)(2,1)} %param.10) | copy-start | bytes 1818628
  4.7 46.4 %all-to-all-start = ((bf16[16,384,128]{2,1,0:T(8,128)(2,1)}), bf16[16,384,128]{2,1,0:T(8,128)(2,1)S(1)}, u32[]{:S(2)}, u32[]{:S(2)}) async-start(bf16[16,384,128]{2,1,0:T(8,128)(2,1)} %pack.1), calls=%async_computation | async-start | bytes 3145728 | tf_op jit(solution)/shard_map/all_to_all | solution.py:645
  13.0 3.4 %copy-start = (bf16[1184,3584]{1,0:T(8,128)(2,1)S(1)}, bf16[1184,3584]{1,0:T(8,128)(2,1)}, u32[]{:S(2)}) copy-start(bf16[1184,3584]{1,0:T(8,128)(2,1)} %weight_ref.1) | copy-start | bytes 25460740
  19.8 1.9 %collective-permute-start = (bf16[8,16,1792]{2,1,0:T(8,128)(2,1)S(1)}, bf16[8,16,1792]{2,1,0:T(8,128)(2,1)S(1)}, u32[]{:S(2)}, u32[]{:S(2)}) collective-permute-start(bf16[8,16,1792]{2,1,0:T(8,128)(2,1)S(1)} %get-tuple-element.78), channel_id=1, source_target_pairs={{0,1},{1,0},{2,3},{3,2},{4,5},{5,4},{6,7},{7,6},{8,9},{9,8},{10,11... | collective-permute-start | bytes 1376264 | tf_op jit(solution)/shard_map/ppermute | solution.py:28
  20.3 2.1 %collective-permute-start.1 = (bf16[8,16,1792]{2,1,0:T(8,128)(2,1)S(1)}, bf16[8,16,1792]{2,1,0:T(8,128)(2,1)S(1)}, u32[]{:S(2)}, u32[]{:S(2)}) collective-permute-start(bf16[8,16,1792]{2,1,0:T(8,128)(2,1)S(1)} %get-tuple-element.80), channel_id=1, source_target_pairs={{0,1},{1,0},{2,3},{3,2},{4,5},{5,4},{6,7},{7,6},{8,9},{9,8},{10,11... | collective-permute-start | bytes 1376264 | tf_op jit(solution)/shard_map/ppermute | solution.py:28
  22.6 28.5 %copy-start.1 = (bf16[192,4096]{1,0:T(8,128)(2,1)S(1)}, bf16[192,4096]{1,0:T(8,128)(2,1)}, u32[]{:S(2)}) copy-start(bf16[192,4096]{1,0:T(8,128)(2,1)} %refs_7_.1) | copy-start | bytes 4718596
  22.6 32.6 %copy-start.6 = (bf16[3584]{0:T(1024)(128)(2,1)S(1)}, bf16[3584]{0:T(1024)(128)(2,1)}, u32[]{:S(2)}) copy-start(bf16[3584]{0:T(1024)(128)(2,1)} %param.12) | copy-start | bytes 21508
  22.6 13.5 %collective-permute-start.2 = (bf16[4,16,1792]{2,1,0:T(8,128)(2,1)S(1)}, bf16[4,16,1792]{2,1,0:T(8,128)(2,1)S(1)}, u32[]{:S(2)}, u32[]{:S(2)}) collective-permute-start(bf16[4,16,1792]{2,1,0:T(8,128)(2,1)S(1)} %get-tuple-element.82), channel_id=1, source_target_pairs={{0,2},{1,3},{2,0},{3,1},{4,6},{5,7},{6,4},{7,5},{8,10},{9,11},{10,... | collective-permute-start | bytes 688136 | tf_op jit(solution)/shard_map/ppermute | solution.py:28
  24.6 19.1 %collective-permute-start.3 = (bf16[4,16,1792]{2,1,0:T(8,128)(2,1)S(1)}, bf16[4,16,1792]{2,1,0:T(8,128)(2,1)S(1)}, u32[]{:S(2)}, u32[]{:S(2)}) collective-permute-start(bf16[4,16,1792]{2,1,0:T(8,128)(2,1)S(1)} %get-tuple-element.84), channel_id=1, source_target_pairs={{0,4},{1,5},{2,6},{3,7},{4,0},{5,1},{6,2},{7,3},{8,12},{9,13},{10,... | collective-permute-start | bytes 688136 | tf_op jit(solution)/shard_map/ppermute | solution.py:28
  43.7 5.8 %collective-permute-start.4 = (bf16[2,16,1792]{2,1,0:T(8,128)(2,1)S(1)}, bf16[2,16,1792]{2,1,0:T(8,128)(2,1)S(1)}, u32[]{:S(2)}, u32[]{:S(2)}) collective-permute-start(bf16[2,16,1792]{2,1,0:T(8,128)(2,1)S(1)} %get-tuple-element.86), channel_id=1, source_target_pairs={{0,4},{1,5},{2,6},{3,7},{4,0},{5,1},{6,2},{7,3},{8,12},{9,13},{10,... | collective-permute-start | bytes 344072 | tf_op jit(solution)/shard_map/ppermute | solution.py:28
  46.3 4.8 %collective-permute-start.5 = (bf16[2,16,1792]{2,1,0:T(8,128)(2,1)S(1)}, bf16[2,16,1792]{2,1,0:T(8,128)(2,1)S(1)}, u32[]{:S(2)}, u32[]{:S(2)}) collective-permute-start(bf16[2,16,1792]{2,1,0:T(8,128)(2,1)S(1)} %get-tuple-element.88), channel_id=1, source_target_pairs={{0,2},{1,3},{2,0},{3,1},{4,6},{5,7},{6,4},{7,5},{8,10},{9,11},{10,... | collective-permute-start | bytes 344072 | tf_op jit(solution)/shard_map/ppermute | solution.py:28
  51.1 20.7 %collective-permute-start.10 = (bf16[192,4096]{1,0:T(8,128)(2,1)S(1)}, bf16[192,4096]{1,0:T(8,128)(2,1)S(1)}, u32[]{:S(2)}, u32[]{:S(2)}) collective-permute-start(bf16[192,4096]{1,0:T(8,128)(2,1)S(1)} %copy-done.1), channel_id=1, source_target_pairs={{0,1},{1,0},{2,3},{3,2},{4,5},{5,4},{6,7},{7,6},{8,9},{9,8},{10,11... | collective-permute-start | bytes 4718600 | tf_op jit(solution)/shard_map/ppermute | solution.py:28
  51.2 20.7 %collective-permute-start.9 = (bf16[192,3584]{1,0:T(8,128)(2,1)}, bf16[192,3584]{1,0:T(8,128)(2,1)S(1)}, u32[]{:S(2)}, u32[]{:S(2)}) collective-permute-start(bf16[192,3584]{1,0:T(8,128)(2,1)} %bitcast.22), channel_id=1, source_target_pairs={{0,1},{1,0},{2,3},{3,2},{4,5},{5,4},{6,7},{7,6},{8,9},{9,8},{10,11... | collective-permute-start | bytes 4128776 | tf_op jit(solution)/shard_map/ppermute | solution.py:28
  51.7 13.6 %collective-permute-start.6 = (bf16[2,2,16,1792]{3,2,1,0:T(8,128)(2,1)S(1)}, bf16[2,2,16,1792]{3,2,1,0:T(8,128)(2,1)S(1)}, u32[]{:S(2)}, u32[]{:S(2)}) collective-permute-start(bf16[2,2,16,1792]{3,2,1,0:T(8,128)(2,1)S(1)} %add_all.1.mine_ref), channel_id=1, source_target_pairs={{0,8},{1,9},{2,10},{3,11},{4,12},{5,13},{6,14},{7,15},{8,0},{9,1},... | collective-permute-start | bytes 688136 | tf_op jit(solution)/shard_map/ppermute | solution.py:28
  55.3 11.9 %collective-permute-start.11 = (bf16[2,192,256]{2,1,0:T(8,128)(2,1)}, bf16[2,192,256]{2,1,0:T(8,128)(2,1)S(1)}, u32[]{:S(2)}, u32[]{:S(2)}) collective-permute-start(bf16[2,192,256]{2,1,0:T(8,128)(2,1)} %bitcast.26), channel_id=1, source_target_pairs={{0,1},{1,0},{2,3},{3,2},{4,5},{5,4},{6,7},{7,6},{8,9},{9,8},{10,11... | collective-permute-start | bytes 589832 | tf_op jit(solution)/shard_map/ppermute | solution.py:28
  65.5 4.9 %collective-permute-start.8 = (bf16[32,1792]{1,0:T(8,128)(2,1)S(1)}, bf16[32,1792]{1,0:T(8,128)(2,1)S(1)}, u32[]{:S(2)}, u32[]{:S(2)}) collective-permute-start(bf16[32,1792]{1,0:T(8,128)(2,1)S(1)} %bitcast.30), channel_id=1, source_target_pairs={{0,2},{1,3},{2,0},{3,1},{4,6},{5,7},{6,4},{7,5},{8,10},{9,11},{10,... | collective-permute-start | bytes 344072 | tf_op jit(solution)/shard_map/ppermute | solution.py:28
  67.1 4.8 %collective-permute-start.7 = (bf16[32,1792]{1,0:T(8,128)(2,1)S(1)}, bf16[32,1792]{1,0:T(8,128)(2,1)S(1)}, u32[]{:S(2)}, u32[]{:S(2)}) collective-permute-start(bf16[32,1792]{1,0:T(8,128)(2,1)S(1)} %bitcast.28), channel_id=1, source_target_pairs={{0,4},{1,5},{2,6},{3,7},{4,0},{5,1},{6,2},{7,3},{8,12},{9,13},{10,... | collective-permute-start | bytes 344072 | tf_op jit(solution)/shard_map/ppermute | solution.py:28
  67.2 0.9 copy-start.5
  71.9 6.6 %copy-start.2 = (bf16[3584,192]{0,1:T(8,128)(2,1)S(1)}, bf16[3584,192]{0,1:T(8,128)(2,1)}, u32[]{:S(2)}) copy-start(bf16[3584,192]{0,1:T(8,128)(2,1)} %param.13) | copy-start | bytes 4128772
  71.9 6.1 %collective-permute-start.12 = (bf16[64,1792]{1,0:T(8,128)(2,1)S(1)}, bf16[64,1792]{1,0:T(8,128)(2,1)S(1)}, u32[]{:S(2)}, u32[]{:S(2)}) collective-permute-start(bf16[64,1792]{1,0:T(8,128)(2,1)S(1)} %get-tuple-element.102.refs_0_), channel_id=1, source_target_pairs={{0,2},{1,3},{2,0},{3,1},{4,6},{5,7},{6,4},{7,5},{8,10},{9,11},{10,... | collective-permute-start | bytes 688136 | tf_op jit(solution)/shard_map/ppermute | solution.py:28
  72.5 6.0 %collective-permute-start.13 = (bf16[64,1792]{1,0:T(8,128)(2,1)S(1)}, bf16[64,1792]{1,0:T(8,128)(2,1)S(1)}, u32[]{:S(2)}, u32[]{:S(2)}) collective-permute-start(bf16[64,1792]{1,0:T(8,128)(2,1)S(1)} %get-tuple-element.103.refs_2_), channel_id=1, source_target_pairs={{0,4},{1,5},{2,6},{3,7},{4,0},{5,1},{6,2},{7,3},{8,12},{9,13},{10,... | collective-permute-start | bytes 688136 | tf_op jit(solution)/shard_map/ppermute | solution.py:28
  81.0 6.8 %collective-permute-start.14 = (bf16[4,144,256]{2,1,0:T(8,128)(2,1)S(1)}, bf16[4,144,256]{2,1,0:T(8,128)(2,1)S(1)}, u32[]{:S(2)}, u32[]{:S(2)}) collective-permute-start(bf16[4,144,256]{2,1,0:T(8,128)(2,1)S(1)} %get-tuple-element.118), channel_id=1, source_target_pairs={{0,2},{1,3},{2,0},{3,1},{4,6},{5,7},{6,4},{7,5},{8,10},{9,11},{10,... | collective-permute-start | bytes 884744 | tf_op jit(solution)/shard_map/ppermute | solution.py:28
  82.5 8.0 %collective-permute-start.15 = (bf16[4,144,256]{2,1,0:T(8,128)(2,1)S(1)}, bf16[4,144,256]{2,1,0:T(8,128)(2,1)S(1)}, u32[]{:S(2)}, u32[]{:S(2)}) collective-permute-start(bf16[4,144,256]{2,1,0:T(8,128)(2,1)S(1)} %get-tuple-element.119), channel_id=1, source_target_pairs={{0,4},{1,5},{2,6},{3,7},{4,0},{5,1},{6,2},{7,3},{8,12},{9,13},{10,... | collective-permute-start | bytes 884744 | tf_op jit(solution)/shard_map/ppermute | solution.py:28
  90.7 6.8 %collective-permute-start.16 = (bf16[2,144,256]{2,1,0:T(8,128)(2,1)S(1)}, bf16[2,144,256]{2,1,0:T(8,128)(2,1)S(1)}, u32[]{:S(2)}, u32[]{:S(2)}) collective-permute-start(bf16[2,144,256]{2,1,0:T(8,128)(2,1)S(1)} %get-tuple-element.126), channel_id=1, source_target_pairs={{0,4},{1,5},{2,6},{3,7},{4,0},{5,1},{6,2},{7,3},{8,12},{9,13},{10,... | collective-permute-start | bytes 442376 | tf_op jit(solution)/shard_map/ppermute | solution.py:28
  90.8 6.7 %collective-permute-start.17 = (bf16[2,144,256]{2,1,0:T(8,128)(2,1)S(1)}, bf16[2,144,256]{2,1,0:T(8,128)(2,1)S(1)}, u32[]{:S(2)}, u32[]{:S(2)}) collective-permute-start(bf16[2,144,256]{2,1,0:T(8,128)(2,1)S(1)} %get-tuple-element.128), channel_id=1, source_target_pairs={{0,2},{1,3},{2,0},{3,1},{4,6},{5,7},{6,4},{7,5},{8,10},{9,11},{10,... | collective-permute-start | bytes 442376 | tf_op jit(solution)/shard_map/ppermute | solution.py:28
  97.5 7.6 %collective-permute-start.18 = (bf16[2,1,144,256]{3,2,1,0:T(8,128)(2,1)S(1)}, bf16[2,1,144,256]{3,2,1,0:T(8,128)(2,1)S(1)}, u32[]{:S(2)}, u32[]{:S(2)}) collective-permute-start(bf16[2,1,144,256]{3,2,1,0:T(8,128)(2,1)S(1)} %get-tuple-element.131), channel_id=1, source_target_pairs={{0,8},{1,9},{2,10},{3,11},{4,12},{5,13},{6,14},{7,15},{8,0},{9,1},... | collective-permute-start | bytes 442376 | tf_op jit(solution)/shard_map/ppermute | solution.py:28
  106.0 1.3 %collective-permute-start.19 = (bf16[128,256]{1,0:T(8,128)(2,1)S(1)}, bf16[128,256]{1,0:T(8,128)(2,1)S(1)}, u32[]{:S(2)}, u32[]{:S(2)}) collective-permute-start(bf16[128,256]{1,0:T(8,128)(2,1)S(1)} %get-tuple-element.133), channel_id=1, source_target_pairs={{0,1},{1,0},{2,3},{3,2},{4,5},{5,4},{6,7},{7,6},{8,9},{9,8},{10,11... | collective-permute-start | bytes 196616 | tf_op jit(solution)/shard_map/ppermute | solution.py:28
  108.6 7.9 %collective-permute-start.24 = (bf16[2,160,128]{2,1,0:T(8,128)(2,1)S(1)}, bf16[2,160,128]{2,1,0:T(8,128)(2,1)S(1)}, u32[]{:S(2)}, u32[]{:S(2)}) collective-permute-start(bf16[2,160,128]{2,1,0:T(8,128)(2,1)S(1)} %get-tuple-element.140), channel_id=1, source_target_pairs={{0,12},{1,13},{2,14},{3,15},{4,8},{5,9},{6,10},{7,11},{8,4},{9,5},... | collective-permute-start | bytes 245768 | tf_op jit(solution)/shard_map/ppermute | solution.py:28
  110.0 8.1 %collective-permute-start.25 = (bf16[2,160,128]{2,1,0:T(8,128)(2,1)S(1)}, bf16[2,160,128]{2,1,0:T(8,128)(2,1)S(1)}, u32[]{:S(2)}, u32[]{:S(2)}) collective-permute-start(bf16[2,160,128]{2,1,0:T(8,128)(2,1)S(1)} %get-tuple-element.141), channel_id=1, source_target_pairs={{0,6},{1,7},{2,4},{3,5},{4,2},{5,3},{6,0},{7,1},{8,14},{9,15},{10,... | collective-permute-start | bytes 245768 | tf_op jit(solution)/shard_map/ppermute | solution.py:28
  110.0 10.1 %collective-permute-start.26 = (bf16[2,160,128]{2,1,0:T(8,128)(2,1)S(1)}, bf16[2,160,128]{2,1,0:T(8,128)(2,1)S(1)}, u32[]{:S(2)}, u32[]{:S(2)}) collective-permute-start(bf16[2,160,128]{2,1,0:T(8,128)(2,1)S(1)} %get-tuple-element.142), channel_id=1, source_target_pairs={{0,14},{1,15},{2,12},{3,13},{4,10},{5,11},{6,8},{7,9},{8,6},{9,7},... | collective-permute-start | bytes 245768 | tf_op jit(solution)/shard_map/ppermute | solution.py:28
  113.6 10.9 %collective-permute-start.20 = (bf16[2,160,128]{2,1,0:T(8,128)(2,1)S(1)}, bf16[2,160,128]{2,1,0:T(8,128)(2,1)S(1)}, u32[]{:S(2)}, u32[]{:S(2)}) collective-permute-start(bf16[2,160,128]{2,1,0:T(8,128)(2,1)S(1)} %get-tuple-element.134), channel_id=1, source_target_pairs={{0,8},{1,9},{2,10},{3,11},{4,12},{5,13},{6,14},{7,15},{8,0},{9,1},... | collective-permute-start | bytes 245768 | tf_op jit(solution)/shard_map/ppermute | solution.py:28
  115.6 8.8 %collective-permute-start.21 = (bf16[2,160,128]{2,1,0:T(8,128)(2,1)S(1)}, bf16[2,160,128]{2,1,0:T(8,128)(2,1)S(1)}, u32[]{:S(2)}, u32[]{:S(2)}) collective-permute-start(bf16[2,160,128]{2,1,0:T(8,128)(2,1)S(1)} %get-tuple-element.135), channel_id=1, source_target_pairs={{0,2},{1,3},{2,0},{3,1},{4,6},{5,7},{6,4},{7,5},{8,10},{9,11},{10,... | collective-permute-start | bytes 245768 | tf_op jit(solution)/shard_map/ppermute | solution.py:28
  116.4 9.4 %collective-permute-start.22 = (bf16[2,160,128]{2,1,0:T(8,128)(2,1)S(1)}, bf16[2,160,128]{2,1,0:T(8,128)(2,1)S(1)}, u32[]{:S(2)}, u32[]{:S(2)}) collective-permute-start(bf16[2,160,128]{2,1,0:T(8,128)(2,1)S(1)} %get-tuple-element.136), channel_id=1, source_target_pairs={{0,10},{1,11},{2,8},{3,9},{4,14},{5,15},{6,12},{7,13},{8,2},{9,3},... | collective-permute-start | bytes 245768 | tf_op jit(solution)/shard_map/ppermute | solution.py:28
  118.0 7.8 %collective-permute-start.23 = (bf16[2,160,128]{2,1,0:T(8,128)(2,1)S(1)}, bf16[2,160,128]{2,1,0:T(8,128)(2,1)S(1)}, u32[]{:S(2)}, u32[]{:S(2)}) collective-permute-start(bf16[2,160,128]{2,1,0:T(8,128)(2,1)S(1)} %get-tuple-element.137), channel_id=1, source_target_pairs={{0,4},{1,5},{2,6},{3,7},{4,0},{5,1},{6,2},{7,3},{8,12},{9,13},{10,... | collective-permute-start | bytes 245768 | tf_op jit(solution)/shard_map/ppermute | solution.py:28
  120.1 5.8 %collective-permute-start.28 = (bf16[4,160,128]{2,1,0:T(8,128)(2,1)S(1)}, bf16[4,160,128]{2,1,0:T(8,128)(2,1)S(1)}, u32[]{:S(2)}, u32[]{:S(2)}) collective-permute-start(bf16[4,160,128]{2,1,0:T(8,128)(2,1)S(1)} %gather_other.3), channel_id=1, source_target_pairs={{0,1},{1,0},{2,3},{3,2},{4,5},{5,4},{6,7},{7,6},{8,9},{9,8},{10,11... | collective-permute-start | bytes 491528 | tf_op jit(solution)/shard_map/ppermute | solution.py:28
  125.9 1.5 %collective-permute-start.27 = (bf16[4,160,128]{2,1,0:T(8,128)(2,1)S(1)}, bf16[4,160,128]{2,1,0:T(8,128)(2,1)S(1)}, u32[]{:S(2)}, u32[]{:S(2)}) collective-permute-start(bf16[4,160,128]{2,1,0:T(8,128)(2,1)S(1)} %gather_other.2), channel_id=1, source_target_pairs={{0,1},{1,0},{2,3},{3,2},{4,5},{5,4},{6,7},{7,6},{8,9},{9,8},{10,11... | collective-permute-start | bytes 491528 | tf_op jit(solution)/shard_map/ppermute | solution.py:28

commit v23 on v20

--- a/solution.py
+++ b/solution.py
@@ -408,8 +408,8 @@
     return turns[:half], turns[half:]
 
 
-def finish_kernel(factor, masks, img_dev, place_ref, packed_ref, sum_ref, top_ref, mine_ref, got_ref, *refs):
-    *outs, text_ref = refs
+def finish_kernel(factor, masks, img_dev, place_ref, packed_ref, *refs):
+    images, mine_ref, got_ref, *outs, text_ref = refs[:4], *refs[4:]
     core, valid = place_ref[2], place_ref[4]
     me = 2 * place_ref[3] + core
     part_rows = packed_ref.shape[1] - 2 * img_dev
@@ -424,8 +424,10 @@
     bias = jnp.where(text_position < valid, 0.0, -jnp.inf)
     group = max(1, 512 // part_rows)
     rows = group * part_rows
-    for step in range(2 * len(outs) // group):
-        span = slice(step * rows, (step + 1) * rows)
+    each = len(outs) // group
+    for step in range(2 * each):
+        sum_ref, top_ref = images[step // each * 2 : step // each * 2 + 2]
+        span = slice(step % each * rows, (step % each + 1) * rows)
         queries = [
             packed_ref[me ^ (2 * masks[at // 2] + at % 2), 2 * img_dev :, :]
             for at in range(step * group, (step + 1) * group)
@@ -455,16 +457,16 @@
         outs[to // 2][to % 2, part_rows:, :] = block.astype(jnp.bfloat16)
 
 
-def finish(place, masks, packed, image, mine, got, img_dev, factor):
+def finish(place, masks, packed, images, mine, got, img_dev, factor):
     devices, part_rows = packed.shape[0], packed.shape[1] - 2 * img_dev
     half = mine.shape[0]
-    count = image[0].shape[0]
+    count = 2 * images[0].shape[0]
     outs = count // part_rows // 2
     out = jax.ShapeDtypeStruct((2, part_rows + 4 * half // devices, HEAD_DIM), jnp.bfloat16)
     return pl.pallas_call(
         functools.partial(finish_kernel, factor, masks, img_dev),
         out_shape=(out,) * outs,
-        in_specs=[SMEM_SPEC] + [VMEM_SPEC] * 5,
+        in_specs=[SMEM_SPEC] + [VMEM_SPEC] * 7,
         out_specs=(VMEM_SPEC,) * outs,
         scratch_shapes=[pltpu.VMEM((2 * half, 2 * HEAD_DIM), jnp.float32)],
         compiler_params=params(10),
@@ -474,7 +476,7 @@
             transcendentals=2 * count * half,
         ),
         name="finish",
-    )(place, packed, *image, mine, got)
+    )(place, packed, *images, mine, got)
 
 
 def gather_kernel(*refs):
@@ -691,14 +693,12 @@
     mine, sent = combine(place, parts, chips, text_len // 2, model_width)
     got = swap(sent, 1)
 
-    pieces, passed = [], []
-    for call, masks in enumerate(turns):
-        image = images[2 * call : 2 * call + 2]
-        blocks = finish(place, masks, packed, image, mine, got, img_dev, factor)
-        pieces += [swap(block, 2 * mask) if mask else block for mask, block in zip(masks, blocks)]
+    masks, passed = turns[0] + turns[1], []
+    blocks = finish(place, masks, packed, images, mine, got, img_dev, factor)
+    pieces = [swap(block, 2 * mask) if mask else block for mask, block in zip(masks, blocks)]
     for call in range(2):
         passed.append(swap(gather_other(pieces[call * chips // 2 : (call + 1) * chips // 2]), 1))
-    attended, text_kv = unpack(copies, part_rows, turns[0] + turns[1], place, pieces, *passed)
+    attended, text_kv = unpack(copies, part_rows, masks, place, pieces, *passed)
     return (attended[None], text_kv)
 
 

time: 128 us -> 129 us (level)
  waiting for transfers between devices: 60.8 us -> 63.4 us
  starting transfers between devices: 36.8 us -> 35.5 us
    ppermute x29, waiting for transfers between devices: 60.8 us -> 63.4 us  [swap(): return lax.ppermute(value, 'seq', [(i, i ^ mask) for i in range(devices)])]
  transfers between devices with their start and end apart: 30 -> 30, of which waited for: 20 -> 20; matrix products, arithmetic and copies ran while one was open for 0% -> 0% of each run, Pallas kernels for 10% -> 9%
where the time goes in v23:
time: 129 us
  waiting for transfers between devices  63.4 us (49%)
  starting transfers between devices  35.5 us (28%)
  Pallas kernels  20.3 us (16%)
  local copies, waits for them, and re-layouts  7.06 us (5%)
  between operations  2.25 us (2%)
    ppermute x29, waiting for transfers between devices, swap(): return lax.ppermute(value, 'seq', [(i, i ^ mask) for i in range(devices)])  63.4 us
    ppermute x29, starting transfers between devices, swap(): return lax.ppermute(value, 'seq', [(i, i ^ mask) for i in range(devices)])  28 us
    pallas_call x2, Pallas kernels, image_attention(): pl.pallas_call(functools.partial(image_kernel, factor, masks, img_dev), o...  8.03 us
    all_to_all x1, starting transfers between devices, exchange(): return lax.all_to_all(rows, 'seq', split_axis=0, concat_axis=0, tiled=True)  7.49 us
    unnamed x14, local copies, waits for them, and re-layouts  5.31 us
    pallas_call x1, Pallas kernels, encoder(): pl.pallas_call(functools.partial(encoder_kernel, lanes), out_shape=(out,)...  3.47 us
  transfers between devices with their start and end apart: 30, of which 20 were waited for; matrix products, arithmetic and copies ran while one was open for 0% of the time, Pallas kernels for 9%

profile of v23, /device:TPU:0, one launch (start us, length us, event | category | flops | bytes accessed | tf_op | source)
XLA Modules:
  0.0 128.6 jit_solution(1159823053126670520)
XLA Ops:
  0.6 1.6 %copy.12 = bf16[1,128,2,2048]{3,1,2,0:T(8,128)(2,1)S(1)} copy(bf16[1,128,2,2048]{3,2,1,0:T(2,128)(2,1)} %param.19) | data formatting | bytes 2097152 | tf_op jit(solution)/shard_map/optimization_barrier | solution.py:649
  2.3 1.0 copy-done.4
  3.3 1.4 %pack.1 = bf16[16,384,128]{2,1,0:T(8,128)(2,1)} custom-call(bf16[128,2048]{1,0:T(8,128)(2,1)S(1)} %bitcast.25, bf16[128,2048]{1,0:T(8,128)(2,1)S(1)} %get-tuple-element.147.keys_ref, bf16[128,2048]{1,0:T(8,128)(2,1)S(1)} %get-tuple-element.146.values_ref), custom_call_target="tpu_custom_call" | custom-call | bytes 3145728 | tf_op jit(solution)/shard_map/pack/pallas_call | solution.py:306
  4.7 7.5 %all-to-all-start = ((bf16[16,384,128]{2,1,0:T(8,128)(2,1)}), bf16[16,384,128]{2,1,0:T(8,128)(2,1)S(1)}, u32[]{:S(2)}, u32[]{:S(2)}) async-start(bf16[16,384,128]{2,1,0:T(8,128)(2,1)} %pack.1), calls=%async_computation | async-start | bytes 3145728 | tf_op jit(solution)/shard_map/all_to_all | solution.py:647
  12.9 0.1 stack.19.place_ref
  13.0 3.4 %copy-done = bf16[1184,3584]{1,0:T(8,128)(2,1)S(1)} copy-done((bf16[1184,3584]{1,0:T(8,128)(2,1)S(1)}, bf16[1184,3584]{1,0:T(8,128)(2,1)}, u32[]{:S(2)}) %copy-start) | copy-done | bytes 8486936
  16.4 3.5 %encoder.1 = (bf16[8,16,1792]{2,1,0:T(8,128)(2,1)S(1)}, bf16[8,16,1792]{2,1,0:T(8,128)(2,1)S(1)}, bf16[8,16,1792]{2,1,0:T(8,128)(2,1)S(1)}, bf16[8,16,1792]{2,1,0:T(8,128)(2,1)S(1)}) custom-call(s32[5]{0:T(128)S(1)} %stack.19.place_ref, bf16[1184,256]{1,0:T(8,128)(2,1)S(1)} %bitcast.24, bf16[1184,3584]{1,0:T(8,128)(2,1)S(1)} %copy-done), custom_call_target="tpu_custom_call" | custom-call | flops 2172649472 | bytes 10928128 | tf_op jit(solution)/shard_map/encoder/pallas_call | solution.py:84
  19.8 0.5 collective-permute-start
  20.3 0.1 collective-permute-start.1
  20.4 1.3 %collective-permute-done.refs_1_ = bf16[8,16,1792]{2,1,0:T(8,128)(2,1)S(1)} collective-permute-done((bf16[8,16,1792]{2,1,0:T(8,128)(2,1)S(1)}, bf16[8,16,1792]{2,1,0:T(8,128)(2,1)S(1)}, u32[]{:S(2)}, u32[]{:S(2)}) %collective-permute-start) | collective-permute-done | bytes 458784 | tf_op jit(solution)/shard_map/ppermute | solution.py:28
  21.8 0.7 collective-permute-done.1.refs_3_
  22.4 0.2 add_halves.4
  22.6 1.9 %collective-permute-start.2 = (bf16[4,16,1792]{2,1,0:T(8,128)(2,1)S(1)}, bf16[4,16,1792]{2,1,0:T(8,128)(2,1)S(1)}, u32[]{:S(2)}, u32[]{:S(2)}) collective-permute-start(bf16[4,16,1792]{2,1,0:T(8,128)(2,1)S(1)} %get-tuple-element.82), channel_id=1, source_target_pairs={{0,2},{1,3},{2,0},{3,1},{4,6},{5,7},{6,4},{7,5},{8,10},{9,11},{10,... | collective-permute-start | bytes 688136 | tf_op jit(solution)/shard_map/ppermute | solution.py:28
  24.6 1.5 %collective-permute-start.3 = (bf16[4,16,1792]{2,1,0:T(8,128)(2,1)S(1)}, bf16[4,16,1792]{2,1,0:T(8,128)(2,1)S(1)}, u32[]{:S(2)}, u32[]{:S(2)}) collective-permute-start(bf16[4,16,1792]{2,1,0:T(8,128)(2,1)S(1)} %get-tuple-element.84), channel_id=1, source_target_pairs={{0,4},{1,5},{2,6},{3,7},{4,0},{5,1},{6,2},{7,3},{8,12},{9,13},{10,... | collective-permute-start | bytes 688136 | tf_op jit(solution)/shard_map/ppermute | solution.py:28
  26.1 10.1 %collective-permute-done.2.refs_1_ = bf16[4,16,1792]{2,1,0:T(8,128)(2,1)S(1)} collective-permute-done((bf16[4,16,1792]{2,1,0:T(8,128)(2,1)S(1)}, bf16[4,16,1792]{2,1,0:T(8,128)(2,1)S(1)}, u32[]{:S(2)}, u32[]{:S(2)}) %collective-permute-start.2) | collective-permute-done | bytes 229408 | tf_op jit(solution)/shard_map/ppermute | solution.py:28
  36.1 7.6 %collective-permute-done.3.refs_3_ = bf16[4,16,1792]{2,1,0:T(8,128)(2,1)S(1)} collective-permute-done((bf16[4,16,1792]{2,1,0:T(8,128)(2,1)S(1)}, bf16[4,16,1792]{2,1,0:T(8,128)(2,1)S(1)}, u32[]{:S(2)}, u32[]{:S(2)}) %collective-permute-start.3) | collective-permute-done | bytes 229408 | tf_op jit(solution)/shard_map/ppermute | solution.py:28
  43.7 0.1 add_halves.5
  43.7 2.5 %collective-permute-start.4 = (bf16[2,16,1792]{2,1,0:T(8,128)(2,1)S(1)}, bf16[2,16,1792]{2,1,0:T(8,128)(2,1)S(1)}, u32[]{:S(2)}, u32[]{:S(2)}) collective-permute-start(bf16[2,16,1792]{2,1,0:T(8,128)(2,1)S(1)} %get-tuple-element.86), channel_id=1, source_target_pairs={{0,4},{1,5},{2,6},{3,7},{4,0},{5,1},{6,2},{7,3},{8,12},{9,13},{10,... | collective-permute-start | bytes 344072 | tf_op jit(solution)/shard_map/ppermute | solution.py:28
  46.3 1.7 %collective-permute-start.5 = (bf16[2,16,1792]{2,1,0:T(8,128)(2,1)S(1)}, bf16[2,16,1792]{2,1,0:T(8,128)(2,1)S(1)}, u32[]{:S(2)}, u32[]{:S(2)}) collective-permute-start(bf16[2,16,1792]{2,1,0:T(8,128)(2,1)S(1)} %get-tuple-element.88), channel_id=1, source_target_pairs={{0,2},{1,3},{2,0},{3,1},{4,6},{5,7},{6,4},{7,5},{8,10},{9,11},{10,... | collective-permute-start | bytes 344072 | tf_op jit(solution)/shard_map/ppermute | solution.py:28
  48.0 1.5 %collective-permute-done.4.got0 = bf16[2,16,1792]{2,1,0:T(8,128)(2,1)S(1)} collective-permute-done((bf16[2,16,1792]{2,1,0:T(8,128)(2,1)S(1)}, bf16[2,16,1792]{2,1,0:T(8,128)(2,1)S(1)}, u32[]{:S(2)}, u32[]{:S(2)}) %collective-permute-start.4) | collective-permute-done | bytes 114720 | tf_op jit(solution)/shard_map/ppermute | solution.py:28
  49.5 1.6 %collective-permute-done.5.got1 = bf16[2,16,1792]{2,1,0:T(8,128)(2,1)S(1)} collective-permute-done((bf16[2,16,1792]{2,1,0:T(8,128)(2,1)S(1)}, bf16[2,16,1792]{2,1,0:T(8,128)(2,1)S(1)}, u32[]{:S(2)}, u32[]{:S(2)}) %collective-permute-start.5) | collective-permute-done | bytes 114720 | tf_op jit(solution)/shard_map/ppermute | solution.py:28
  51.2 0.1 collective-permute-start.10
  51.2 0.5 collective-permute-start.9
  51.7 2.9 %collective-permute-start.6 = (bf16[2,2,16,1792]{3,2,1,0:T(8,128)(2,1)S(1)}, bf16[2,2,16,1792]{3,2,1,0:T(8,128)(2,1)S(1)}, u32[]{:S(2)}, u32[]{:S(2)}) collective-permute-start(bf16[2,2,16,1792]{3,2,1,0:T(8,128)(2,1)S(1)} %add_all.1.mine_ref), channel_id=1, source_target_pairs={{0,8},{1,9},{2,10},{3,11},{4,12},{5,13},{6,14},{7,15},{8,0},{9,1},... | collective-permute-start | bytes 688136 | tf_op jit(solution)/shard_map/ppermute | solution.py:28
  55.3 0.1 collective-permute-start.11
  55.3 10.0 %collective-permute-done.6.got_ref = bf16[2,2,16,1792]{3,2,1,0:T(8,128)(2,1)S(1)} collective-permute-done((bf16[2,2,16,1792]{3,2,1,0:T(8,128)(2,1)S(1)}, bf16[2,2,16,1792]{3,2,1,0:T(8,128)(2,1)S(1)}, u32[]{:S(2)}, u32[]{:S(2)}) %collective-permute-start.6) | collective-permute-done | bytes 229408 | tf_op jit(solution)/shard_map/ppermute | solution.py:28
  65.3 0.2 normalize.1
  65.5 1.6 %collective-permute-start.8 = (bf16[32,1792]{1,0:T(8,128)(2,1)S(1)}, bf16[32,1792]{1,0:T(8,128)(2,1)S(1)}, u32[]{:S(2)}, u32[]{:S(2)}) collective-permute-start(bf16[32,1792]{1,0:T(8,128)(2,1)S(1)} %bitcast.30), channel_id=1, source_target_pairs={{0,2},{1,3},{2,0},{3,1},{4,6},{5,7},{6,4},{7,5},{8,10},{9,11},{10,... | collective-permute-start | bytes 344072 | tf_op jit(solution)/shard_map/ppermute | solution.py:28
  67.2 0.9 copy-done.5
  68.1 0.2 modulation.1.refs_4_
  68.3 2.1 %collective-permute-done.8.got1 = bf16[32,1792]{1,0:T(8,128)(2,1)S(1)} collective-permute-done((bf16[32,1792]{1,0:T(8,128)(2,1)S(1)}, bf16[32,1792]{1,0:T(8,128)(2,1)S(1)}, u32[]{:S(2)}, u32[]{:S(2)}) %collective-permute-start.8) | collective-permute-done | bytes 114720 | tf_op jit(solution)/shard_map/ppermute | solution.py:28
  70.4 1.5 %collective-permute-done.7.got0 = bf16[32,1792]{1,0:T(8,128)(2,1)S(1)} collective-permute-done((bf16[32,1792]{1,0:T(8,128)(2,1)S(1)}, bf16[32,1792]{1,0:T(8,128)(2,1)S(1)}, u32[]{:S(2)}, u32[]{:S(2)}) %collective-permute-start.7) | collective-permute-done | bytes 114720 | tf_op jit(solution)/shard_map/ppermute | solution.py:28
  72.0 0.6 collective-permute-start.12
  72.5 0.4 collective-permute-start.13
  72.9 3.9 %image_attention.2 = (f32[1024,256]{1,0:T(8,128)S(1)}, f32[1024,128]{1,0:T(8,128)S(1)}) custom-call(s32[5]{0:T(128)S(1)} %stack.19.place_ref, bf16[16,384,128]{2,1,0:T(8,128)(2,1)S(1)} %all-to-all-done.packed_ref), custom_call_target="tpu_custom_call" | custom-call | flops 1073741824 | bytes 2359296 | tf_op jit(solution)/shard_map/image_attention/pallas_call | solution.py:383
  76.8 1.2 collective-permute-done.12.refs_1_
  78.0 0.5 collective-permute-done.13.refs_3_
  78.6 2.4 %project.1 = (bf16[4,144,256]{2,1,0:T(8,128)(2,1)S(1)}, bf16[4,144,256]{2,1,0:T(8,128)(2,1)S(1)}, bf16[4,144,256]{2,1,0:T(8,128)(2,1)S(1)}, bf16[4,144,256]{2,1,0:T(8,128)(2,1)S(1)}) custom-call(s32[5]{0:T(128)S(1)} %stack.19.place_ref, bf16[64,1792]{1,0:T(8,128)(2,1)S(1)} %get-tuple-element.102.refs_0_, ...), custom_call_target="tpu_custom_call" | custom-call | flops 754974720 | bytes 7864320 | tf_op jit(solution)/shard_map/project/pallas_call | solution.py:216
  81.0 1.6 %collective-permute-start.14 = (bf16[4,144,256]{2,1,0:T(8,128)(2,1)S(1)}, bf16[4,144,256]{2,1,0:T(8,128)(2,1)S(1)}, u32[]{:S(2)}, u32[]{:S(2)}) collective-permute-start(bf16[4,144,256]{2,1,0:T(8,128)(2,1)S(1)} %get-tuple-element.117), channel_id=1, source_target_pairs={{0,2},{1,3},{2,0},{3,1},{4,6},{5,7},{6,4},{7,5},{8,10},{9,11},{10,... | collective-permute-start | bytes 884744 | tf_op jit(solution)/shard_map/ppermute | solution.py:28
  82.6 4.1 %image_attention.3 = (f32[1024,256]{1,0:T(8,128)S(1)}, f32[1024,128]{1,0:T(8,128)S(1)}) custom-call(s32[5]{0:T(128)S(1)} %stack.19.place_ref, bf16[16,384,128]{2,1,0:T(8,128)(2,1)S(1)} %all-to-all-done.packed_ref), custom_call_target="tpu_custom_call" | custom-call | flops 1073741824 | bytes 2359296 | tf_op jit(solution)/shard_map/image_attention/pallas_call | solution.py:383
  86.7 1.0 collective-permute-done.14.refs_1_
  87.8 2.8 %collective-permute-done.15.refs_3_ = bf16[4,144,256]{2,1,0:T(8,128)(2,1)S(1)} collective-permute-done((bf16[4,144,256]{2,1,0:T(8,128)(2,1)S(1)}, bf16[4,144,256]{2,1,0:T(8,128)(2,1)S(1)}, u32[]{:S(2)}, u32[]{:S(2)}) %collective-permute-start.15) | collective-permute-done | bytes 294944 | tf_op jit(solution)/shard_map/ppermute | solution.py:28
  90.6 0.1 add_halves.6
  90.7 0.1 collective-permute-start.16
  90.8 0.6 collective-permute-start.17
  91.4 6.1 %collective-permute-done.16.refs_1_ = bf16[2,144,256]{2,1,0:T(8,128)(2,1)S(1)} collective-permute-done((bf16[2,144,256]{2,1,0:T(8,128)(2,1)S(1)}, bf16[2,144,256]{2,1,0:T(8,128)(2,1)S(1)}, u32[]{:S(2)}, u32[]{:S(2)}) %collective-permute-start.16) | collective-permute-done | bytes 147488 | tf_op jit(solution)/shard_map/ppermute | solution.py:28
  97.5 1.3 %collective-permute-start.18 = (bf16[2,1,144,256]{3,2,1,0:T(8,128)(2,1)S(1)}, bf16[2,1,144,256]{3,2,1,0:T(8,128)(2,1)S(1)}, u32[]{:S(2)}, u32[]{:S(2)}) collective-permute-start(bf16[2,1,144,256]{3,2,1,0:T(8,128)(2,1)S(1)} %get-tuple-element.133), channel_id=1, source_target_pairs={{0,8},{1,9},{2,10},{3,11},{4,12},{5,13},{6,14},{7,15},{8,0},{9,1},... | collective-permute-start | bytes 442376 | tf_op jit(solution)/shard_map/ppermute | solution.py:28
  98.8 6.3 %collective-permute-done.18.refs_2_ = bf16[2,1,144,256]{3,2,1,0:T(8,128)(2,1)S(1)} collective-permute-done((bf16[2,1,144,256]{3,2,1,0:T(8,128)(2,1)S(1)}, bf16[2,1,144,256]{3,2,1,0:T(8,128)(2,1)S(1)}, u32[]{:S(2)}, u32[]{:S(2)}) %collective-permute-start.18) | collective-permute-done | bytes 147488 | tf_op jit(solution)/shard_map/ppermute | solution.py:28
  105.1 0.9 combine.1
  106.1 0.1 collective-permute-start.19
  106.1 1.2 collective-permute-done.19.refs_5_
  107.4 1.5 %finish.1 = (bf16[2,160,128]{2,1,0:T(8,128)(2,1)S(1)}, bf16[2,160,128]{2,1,0:T(8,128)(2,1)S(1)}, bf16[2,160,128]{2,1,0:T(8,128)(2,1)S(1)}, bf16[2,160,128]{2,1,0...) custom-call(s32[5]{0:T(128)S(1)} %stack.19.place_ref, ...), custom_call_target="tpu_custom_call" | custom-call | flops 268435456 | bytes 3145728 | tf_op jit(solution)/shard_map/finish/pallas_call | solution.py:466
  108.9 0.1 collective-permute-start.20
  109.0 2.2 %collective-permute-start.21 = (bf16[2,160,128]{2,1,0:T(8,128)(2,1)S(1)}, bf16[2,160,128]{2,1,0:T(8,128)(2,1)S(1)}, u32[]{:S(2)}, u32[]{:S(2)}) collective-permute-start(bf16[2,160,128]{2,1,0:T(8,128)(2,1)S(1)} %get-tuple-element.137), channel_id=1, source_target_pairs={{0,6},{1,7},{2,4},{3,5},{4,2},{5,3},{6,0},{7,1},{8,14},{9,15},{10,... | collective-permute-start | bytes 245768 | tf_op jit(solution)/shard_map/ppermute | solution.py:28
  111.2 0.7 collective-permute-start.22
  111.9 2.9 %collective-permute-start.23 = (bf16[2,160,128]{2,1,0:T(8,128)(2,1)S(1)}, bf16[2,160,128]{2,1,0:T(8,128)(2,1)S(1)}, u32[]{:S(2)}, u32[]{:S(2)}) collective-permute-start(bf16[2,160,128]{2,1,0:T(8,128)(2,1)S(1)} %get-tuple-element.139), channel_id=1, source_target_pairs={{0,4},{1,5},{2,6},{3,7},{4,0},{5,1},{6,2},{7,3},{8,12},{9,13},{10,... | collective-permute-start | bytes 245768 | tf_op jit(solution)/shard_map/ppermute | solution.py:28
  114.8 1.4 %collective-permute-start.24 = (bf16[2,160,128]{2,1,0:T(8,128)(2,1)S(1)}, bf16[2,160,128]{2,1,0:T(8,128)(2,1)S(1)}, u32[]{:S(2)}, u32[]{:S(2)}) collective-permute-start(bf16[2,160,128]{2,1,0:T(8,128)(2,1)S(1)} %get-tuple-element.140), channel_id=1, source_target_pairs={{0,12},{1,13},{2,14},{3,15},{4,8},{5,9},{6,10},{7,11},{8,4},{9,5},... | collective-permute-start | bytes 245768 | tf_op jit(solution)/shard_map/ppermute | solution.py:28
  116.2 0.8 collective-permute-start.25
  117.0 1.3 %collective-permute-done.21.refs_1_ = bf16[2,160,128]{2,1,0:T(8,128)(2,1)S(1)} collective-permute-done((bf16[2,160,128]{2,1,0:T(8,128)(2,1)S(1)}, bf16[2,160,128]{2,1,0:T(8,128)(2,1)S(1)}, u32[]{:S(2)}, u32[]{:S(2)}) %collective-permute-start.21) | collective-permute-done | bytes 81952 | tf_op jit(solution)/shard_map/ppermute | solution.py:28
  118.3 1.9 %collective-permute-start.26 = (bf16[2,160,128]{2,1,0:T(8,128)(2,1)S(1)}, bf16[2,160,128]{2,1,0:T(8,128)(2,1)S(1)}, u32[]{:S(2)}, u32[]{:S(2)}) collective-permute-start(bf16[2,160,128]{2,1,0:T(8,128)(2,1)S(1)} %get-tuple-element.142), channel_id=1, source_target_pairs={{0,14},{1,15},{2,12},{3,13},{4,10},{5,11},{6,8},{7,9},{8,6},{9,7},... | collective-permute-start | bytes 245768 | tf_op jit(solution)/shard_map/ppermute | solution.py:28
  120.3 1.4 %collective-permute-done.24.refs_0_.refs_4_ = bf16[2,160,128]{2,1,0:T(8,128)(2,1)S(1)} collective-permute-done((bf16[2,160,128]{2,1,0:T(8,128)(2,1)S(1)}, bf16[2,160,128]{2,1,0:T(8,128)(2,1)S(1)}, u32[]{:S(2)}, u32[]{:S(2)}) %collective-permute-start.24) | collective-permute-done | bytes 81952 | tf_op jit(solution)/shard_map/ppermute | solution.py:28
  121.7 3.8 %collective-permute-done.26.refs_2_.refs_6_ = bf16[2,160,128]{2,1,0:T(8,128)(2,1)S(1)} collective-permute-done((bf16[2,160,128]{2,1,0:T(8,128)(2,1)S(1)}, bf16[2,160,128]{2,1,0:T(8,128)(2,1)S(1)}, u32[]{:S(2)}, u32[]{:S(2)}) %collective-permute-start.26) | collective-permute-done | bytes 81952 | tf_op jit(solution)/shard_map/ppermute | solution.py:28
  125.7 1.4 %collective-permute-done.28.refs_9_ = bf16[4,160,128]{2,1,0:T(8,128)(2,1)S(1)} collective-permute-done((bf16[4,160,128]{2,1,0:T(8,128)(2,1)S(1)}, bf16[4,160,128]{2,1,0:T(8,128)(2,1)S(1)}, u32[]{:S(2)}, u32[]{:S(2)}) %collective-permute-start.28) | collective-permute-done | bytes 163872 | tf_op jit(solution)/shard_map/ppermute | solution.py:28
  127.0 1.5 %unpack.1 = (bf16[128,2048]{1,0:T(8,128)(2,1)}, bf16[16,4096]{1,0:T(8,128)(2,1)}) custom-call(s32[5]{0:T(128)S(1)} %stack.19.place_ref, bf16[2,160,128]{2,1,0:T(8,128)(2,1)S(1)} %collective-permute-done.20.refs_0_, bf16[2,160,128]{2,1,0:T(8,128)(2,1)S(1)} %collective-permute-done.21.refs_1_, bf16[2,160,128]{2,1,0:T(8,128)(2,1)S(1)} %collective-permute-done.22.refs_2_, ...), custom_call_target="tpu_custom_call" | custom-call | tf_op jit(solution)/shard_map/unpack/pallas_call | solution.py:341
  (34 shorter events, 0.6 us)
Async XLA Ops:
  2.2 1.0 copy-start.4
  4.7 8.3 %copy-start.3 = (bf16[1,256,1184]{1,2,0:T(8,128)(2,1)S(1)}, bf16[1,256,1184]{1,2,0:T(8,128)(2,1)}, u32[]{:S(2)}) copy-start(bf16[1,256,1184]{1,2,0:T(8,128)(2,1)} %param.10) | copy-start | bytes 1818628
  4.7 46.4 %all-to-all-start = ((bf16[16,384,128]{2,1,0:T(8,128)(2,1)}), bf16[16,384,128]{2,1,0:T(8,128)(2,1)S(1)}, u32[]{:S(2)}, u32[]{:S(2)}) async-start(bf16[16,384,128]{2,1,0:T(8,128)(2,1)} %pack.1), calls=%async_computation | async-start | bytes 3145728 | tf_op jit(solution)/shard_map/all_to_all | solution.py:647
  13.0 3.4 %copy-start = (bf16[1184,3584]{1,0:T(8,128)(2,1)S(1)}, bf16[1184,3584]{1,0:T(8,128)(2,1)}, u32[]{:S(2)}) copy-start(bf16[1184,3584]{1,0:T(8,128)(2,1)} %weight_ref.1) | copy-start | bytes 25460740
  19.8 1.9 %collective-permute-start = (bf16[8,16,1792]{2,1,0:T(8,128)(2,1)S(1)}, bf16[8,16,1792]{2,1,0:T(8,128)(2,1)S(1)}, u32[]{:S(2)}, u32[]{:S(2)}) collective-permute-start(bf16[8,16,1792]{2,1,0:T(8,128)(2,1)S(1)} %get-tuple-element.78), channel_id=1, source_target_pairs={{0,1},{1,0},{2,3},{3,2},{4,5},{5,4},{6,7},{7,6},{8,9},{9,8},{10,11... | collective-permute-start | bytes 1376264 | tf_op jit(solution)/shard_map/ppermute | solution.py:28
  20.3 2.1 %collective-permute-start.1 = (bf16[8,16,1792]{2,1,0:T(8,128)(2,1)S(1)}, bf16[8,16,1792]{2,1,0:T(8,128)(2,1)S(1)}, u32[]{:S(2)}, u32[]{:S(2)}) collective-permute-start(bf16[8,16,1792]{2,1,0:T(8,128)(2,1)S(1)} %get-tuple-element.80), channel_id=1, source_target_pairs={{0,1},{1,0},{2,3},{3,2},{4,5},{5,4},{6,7},{7,6},{8,9},{9,8},{10,11... | collective-permute-start | bytes 1376264 | tf_op jit(solution)/shard_map/ppermute | solution.py:28
  22.6 28.5 %copy-start.1 = (bf16[192,4096]{1,0:T(8,128)(2,1)S(1)}, bf16[192,4096]{1,0:T(8,128)(2,1)}, u32[]{:S(2)}) copy-start(bf16[192,4096]{1,0:T(8,128)(2,1)} %refs_7_.1) | copy-start | bytes 4718596
  22.6 32.6 %copy-start.6 = (bf16[3584]{0:T(1024)(128)(2,1)S(1)}, bf16[3584]{0:T(1024)(128)(2,1)}, u32[]{:S(2)}) copy-start(bf16[3584]{0:T(1024)(128)(2,1)} %param.12) | copy-start | bytes 21508
  22.6 13.5 %collective-permute-start.2 = (bf16[4,16,1792]{2,1,0:T(8,128)(2,1)S(1)}, bf16[4,16,1792]{2,1,0:T(8,128)(2,1)S(1)}, u32[]{:S(2)}, u32[]{:S(2)}) collective-permute-start(bf16[4,16,1792]{2,1,0:T(8,128)(2,1)S(1)} %get-tuple-element.82), channel_id=1, source_target_pairs={{0,2},{1,3},{2,0},{3,1},{4,6},{5,7},{6,4},{7,5},{8,10},{9,11},{10,... | collective-permute-start | bytes 688136 | tf_op jit(solution)/shard_map/ppermute | solution.py:28
  24.6 19.1 %collective-permute-start.3 = (bf16[4,16,1792]{2,1,0:T(8,128)(2,1)S(1)}, bf16[4,16,1792]{2,1,0:T(8,128)(2,1)S(1)}, u32[]{:S(2)}, u32[]{:S(2)}) collective-permute-start(bf16[4,16,1792]{2,1,0:T(8,128)(2,1)S(1)} %get-tuple-element.84), channel_id=1, source_target_pairs={{0,4},{1,5},{2,6},{3,7},{4,0},{5,1},{6,2},{7,3},{8,12},{9,13},{10,... | collective-permute-start | bytes 688136 | tf_op jit(solution)/shard_map/ppermute | solution.py:28
  43.7 5.8 %collective-permute-start.4 = (bf16[2,16,1792]{2,1,0:T(8,128)(2,1)S(1)}, bf16[2,16,1792]{2,1,0:T(8,128)(2,1)S(1)}, u32[]{:S(2)}, u32[]{:S(2)}) collective-permute-start(bf16[2,16,1792]{2,1,0:T(8,128)(2,1)S(1)} %get-tuple-element.86), channel_id=1, source_target_pairs={{0,4},{1,5},{2,6},{3,7},{4,0},{5,1},{6,2},{7,3},{8,12},{9,13},{10,... | collective-permute-start | bytes 344072 | tf_op jit(solution)/shard_map/ppermute | solution.py:28
  46.3 4.8 %collective-permute-start.5 = (bf16[2,16,1792]{2,1,0:T(8,128)(2,1)S(1)}, bf16[2,16,1792]{2,1,0:T(8,128)(2,1)S(1)}, u32[]{:S(2)}, u32[]{:S(2)}) collective-permute-start(bf16[2,16,1792]{2,1,0:T(8,128)(2,1)S(1)} %get-tuple-element.88), channel_id=1, source_target_pairs={{0,2},{1,3},{2,0},{3,1},{4,6},{5,7},{6,4},{7,5},{8,10},{9,11},{10,... | collective-permute-start | bytes 344072 | tf_op jit(solution)/shard_map/ppermute | solution.py:28
  51.2 20.8 %collective-permute-start.10 = (bf16[192,4096]{1,0:T(8,128)(2,1)S(1)}, bf16[192,4096]{1,0:T(8,128)(2,1)S(1)}, u32[]{:S(2)}, u32[]{:S(2)}) collective-permute-start(bf16[192,4096]{1,0:T(8,128)(2,1)S(1)} %copy-done.1), channel_id=1, source_target_pairs={{0,1},{1,0},{2,3},{3,2},{4,5},{5,4},{6,7},{7,6},{8,9},{9,8},{10,11... | collective-permute-start | bytes 4718600 | tf_op jit(solution)/shard_map/ppermute | solution.py:28
  51.2 20.7 %collective-permute-start.9 = (bf16[192,3584]{1,0:T(8,128)(2,1)}, bf16[192,3584]{1,0:T(8,128)(2,1)S(1)}, u32[]{:S(2)}, u32[]{:S(2)}) collective-permute-start(bf16[192,3584]{1,0:T(8,128)(2,1)} %bitcast.22), channel_id=1, source_target_pairs={{0,1},{1,0},{2,3},{3,2},{4,5},{5,4},{6,7},{7,6},{8,9},{9,8},{10,11... | collective-permute-start | bytes 4128776 | tf_op jit(solution)/shard_map/ppermute | solution.py:28
  51.7 13.6 %collective-permute-start.6 = (bf16[2,2,16,1792]{3,2,1,0:T(8,128)(2,1)S(1)}, bf16[2,2,16,1792]{3,2,1,0:T(8,128)(2,1)S(1)}, u32[]{:S(2)}, u32[]{:S(2)}) collective-permute-start(bf16[2,2,16,1792]{3,2,1,0:T(8,128)(2,1)S(1)} %add_all.1.mine_ref), channel_id=1, source_target_pairs={{0,8},{1,9},{2,10},{3,11},{4,12},{5,13},{6,14},{7,15},{8,0},{9,1},... | collective-permute-start | bytes 688136 | tf_op jit(solution)/shard_map/ppermute | solution.py:28
  55.3 11.9 %collective-permute-start.11 = (bf16[2,192,256]{2,1,0:T(8,128)(2,1)}, bf16[2,192,256]{2,1,0:T(8,128)(2,1)S(1)}, u32[]{:S(2)}, u32[]{:S(2)}) collective-permute-start(bf16[2,192,256]{2,1,0:T(8,128)(2,1)} %bitcast.26), channel_id=1, source_target_pairs={{0,1},{1,0},{2,3},{3,2},{4,5},{5,4},{6,7},{7,6},{8,9},{9,8},{10,11... | collective-permute-start | bytes 589832 | tf_op jit(solution)/shard_map/ppermute | solution.py:28
  65.5 4.9 %collective-permute-start.8 = (bf16[32,1792]{1,0:T(8,128)(2,1)S(1)}, bf16[32,1792]{1,0:T(8,128)(2,1)S(1)}, u32[]{:S(2)}, u32[]{:S(2)}) collective-permute-start(bf16[32,1792]{1,0:T(8,128)(2,1)S(1)} %bitcast.30), channel_id=1, source_target_pairs={{0,2},{1,3},{2,0},{3,1},{4,6},{5,7},{6,4},{7,5},{8,10},{9,11},{10,... | collective-permute-start | bytes 344072 | tf_op jit(solution)/shard_map/ppermute | solution.py:28
  67.1 4.8 %collective-permute-start.7 = (bf16[32,1792]{1,0:T(8,128)(2,1)S(1)}, bf16[32,1792]{1,0:T(8,128)(2,1)S(1)}, u32[]{:S(2)}, u32[]{:S(2)}) collective-permute-start(bf16[32,1792]{1,0:T(8,128)(2,1)S(1)} %bitcast.28), channel_id=1, source_target_pairs={{0,4},{1,5},{2,6},{3,7},{4,0},{5,1},{6,2},{7,3},{8,12},{9,13},{10,... | collective-permute-start | bytes 344072 | tf_op jit(solution)/shard_map/ppermute | solution.py:28
  67.2 0.9 copy-start.5
  71.9 6.6 %copy-start.2 = (bf16[3584,192]{0,1:T(8,128)(2,1)S(1)}, bf16[3584,192]{0,1:T(8,128)(2,1)}, u32[]{:S(2)}) copy-start(bf16[3584,192]{0,1:T(8,128)(2,1)} %param.13) | copy-start | bytes 4128772
  72.0 6.1 %collective-permute-start.12 = (bf16[64,1792]{1,0:T(8,128)(2,1)S(1)}, bf16[64,1792]{1,0:T(8,128)(2,1)S(1)}, u32[]{:S(2)}, u32[]{:S(2)}) collective-permute-start(bf16[64,1792]{1,0:T(8,128)(2,1)S(1)} %get-tuple-element.102.refs_0_), channel_id=1, source_target_pairs={{0,2},{1,3},{2,0},{3,1},{4,6},{5,7},{6,4},{7,5},{8,10},{9,11},{10,... | collective-permute-start | bytes 688136 | tf_op jit(solution)/shard_map/ppermute | solution.py:28
  72.5 6.0 %collective-permute-start.13 = (bf16[64,1792]{1,0:T(8,128)(2,1)S(1)}, bf16[64,1792]{1,0:T(8,128)(2,1)S(1)}, u32[]{:S(2)}, u32[]{:S(2)}) collective-permute-start(bf16[64,1792]{1,0:T(8,128)(2,1)S(1)} %get-tuple-element.103.refs_2_), channel_id=1, source_target_pairs={{0,4},{1,5},{2,6},{3,7},{4,0},{5,1},{6,2},{7,3},{8,12},{9,13},{10,... | collective-permute-start | bytes 688136 | tf_op jit(solution)/shard_map/ppermute | solution.py:28
  81.0 6.8 %collective-permute-start.14 = (bf16[4,144,256]{2,1,0:T(8,128)(2,1)S(1)}, bf16[4,144,256]{2,1,0:T(8,128)(2,1)S(1)}, u32[]{:S(2)}, u32[]{:S(2)}) collective-permute-start(bf16[4,144,256]{2,1,0:T(8,128)(2,1)S(1)} %get-tuple-element.117), channel_id=1, source_target_pairs={{0,2},{1,3},{2,0},{3,1},{4,6},{5,7},{6,4},{7,5},{8,10},{9,11},{10,... | collective-permute-start | bytes 884744 | tf_op jit(solution)/shard_map/ppermute | solution.py:28
  82.6 8.0 %collective-permute-start.15 = (bf16[4,144,256]{2,1,0:T(8,128)(2,1)S(1)}, bf16[4,144,256]{2,1,0:T(8,128)(2,1)S(1)}, u32[]{:S(2)}, u32[]{:S(2)}) collective-permute-start(bf16[4,144,256]{2,1,0:T(8,128)(2,1)S(1)} %get-tuple-element.118), channel_id=1, source_target_pairs={{0,4},{1,5},{2,6},{3,7},{4,0},{5,1},{6,2},{7,3},{8,12},{9,13},{10,... | collective-permute-start | bytes 884744 | tf_op jit(solution)/shard_map/ppermute | solution.py:28
  90.7 6.8 %collective-permute-start.16 = (bf16[2,144,256]{2,1,0:T(8,128)(2,1)S(1)}, bf16[2,144,256]{2,1,0:T(8,128)(2,1)S(1)}, u32[]{:S(2)}, u32[]{:S(2)}) collective-permute-start(bf16[2,144,256]{2,1,0:T(8,128)(2,1)S(1)} %get-tuple-element.128), channel_id=1, source_target_pairs={{0,4},{1,5},{2,6},{3,7},{4,0},{5,1},{6,2},{7,3},{8,12},{9,13},{10,... | collective-permute-start | bytes 442376 | tf_op jit(solution)/shard_map/ppermute | solution.py:28
  90.8 6.7 %collective-permute-start.17 = (bf16[2,144,256]{2,1,0:T(8,128)(2,1)S(1)}, bf16[2,144,256]{2,1,0:T(8,128)(2,1)S(1)}, u32[]{:S(2)}, u32[]{:S(2)}) collective-permute-start(bf16[2,144,256]{2,1,0:T(8,128)(2,1)S(1)} %get-tuple-element.130), channel_id=1, source_target_pairs={{0,2},{1,3},{2,0},{3,1},{4,6},{5,7},{6,4},{7,5},{8,10},{9,11},{10,... | collective-permute-start | bytes 442376 | tf_op jit(solution)/shard_map/ppermute | solution.py:28
  97.5 7.6 %collective-permute-start.18 = (bf16[2,1,144,256]{3,2,1,0:T(8,128)(2,1)S(1)}, bf16[2,1,144,256]{3,2,1,0:T(8,128)(2,1)S(1)}, u32[]{:S(2)}, u32[]{:S(2)}) collective-permute-start(bf16[2,1,144,256]{3,2,1,0:T(8,128)(2,1)S(1)} %get-tuple-element.133), channel_id=1, source_target_pairs={{0,8},{1,9},{2,10},{3,11},{4,12},{5,13},{6,14},{7,15},{8,0},{9,1},... | collective-permute-start | bytes 442376 | tf_op jit(solution)/shard_map/ppermute | solution.py:28
  106.1 1.3 %collective-permute-start.19 = (bf16[128,256]{1,0:T(8,128)(2,1)S(1)}, bf16[128,256]{1,0:T(8,128)(2,1)S(1)}, u32[]{:S(2)}, u32[]{:S(2)}) collective-permute-start(bf16[128,256]{1,0:T(8,128)(2,1)S(1)} %get-tuple-element.135), channel_id=1, source_target_pairs={{0,1},{1,0},{2,3},{3,2},{4,5},{5,4},{6,7},{7,6},{8,9},{9,8},{10,11... | collective-permute-start | bytes 196616 | tf_op jit(solution)/shard_map/ppermute | solution.py:28
  108.9 7.3 %collective-permute-start.20 = (bf16[2,160,128]{2,1,0:T(8,128)(2,1)S(1)}, bf16[2,160,128]{2,1,0:T(8,128)(2,1)S(1)}, u32[]{:S(2)}, u32[]{:S(2)}) collective-permute-start(bf16[2,160,128]{2,1,0:T(8,128)(2,1)S(1)} %get-tuple-element.136), channel_id=1, source_target_pairs={{0,8},{1,9},{2,10},{3,11},{4,12},{5,13},{6,14},{7,15},{8,0},{9,1},... | collective-permute-start | bytes 245768 | tf_op jit(solution)/shard_map/ppermute | solution.py:28
  109.0 9.3 %collective-permute-start.21 = (bf16[2,160,128]{2,1,0:T(8,128)(2,1)S(1)}, bf16[2,160,128]{2,1,0:T(8,128)(2,1)S(1)}, u32[]{:S(2)}, u32[]{:S(2)}) collective-permute-start(bf16[2,160,128]{2,1,0:T(8,128)(2,1)S(1)} %get-tuple-element.137), channel_id=1, source_target_pairs={{0,6},{1,7},{2,4},{3,5},{4,2},{5,3},{6,0},{7,1},{8,14},{9,15},{10,... | collective-permute-start | bytes 245768 | tf_op jit(solution)/shard_map/ppermute | solution.py:28
  111.2 9.1 %collective-permute-start.22 = (bf16[2,160,128]{2,1,0:T(8,128)(2,1)S(1)}, bf16[2,160,128]{2,1,0:T(8,128)(2,1)S(1)}, u32[]{:S(2)}, u32[]{:S(2)}) collective-permute-start(bf16[2,160,128]{2,1,0:T(8,128)(2,1)S(1)} %get-tuple-element.138), channel_id=1, source_target_pairs={{0,10},{1,11},{2,8},{3,9},{4,14},{5,15},{6,12},{7,13},{8,2},{9,3},... | collective-permute-start | bytes 245768 | tf_op jit(solution)/shard_map/ppermute | solution.py:28
  111.9 8.3 %collective-permute-start.23 = (bf16[2,160,128]{2,1,0:T(8,128)(2,1)S(1)}, bf16[2,160,128]{2,1,0:T(8,128)(2,1)S(1)}, u32[]{:S(2)}, u32[]{:S(2)}) collective-permute-start(bf16[2,160,128]{2,1,0:T(8,128)(2,1)S(1)} %get-tuple-element.139), channel_id=1, source_target_pairs={{0,4},{1,5},{2,6},{3,7},{4,0},{5,1},{6,2},{7,3},{8,12},{9,13},{10,... | collective-permute-start | bytes 245768 | tf_op jit(solution)/shard_map/ppermute | solution.py:28
  114.8 6.9 %collective-permute-start.24 = (bf16[2,160,128]{2,1,0:T(8,128)(2,1)S(1)}, bf16[2,160,128]{2,1,0:T(8,128)(2,1)S(1)}, u32[]{:S(2)}, u32[]{:S(2)}) collective-permute-start(bf16[2,160,128]{2,1,0:T(8,128)(2,1)S(1)} %get-tuple-element.140), channel_id=1, source_target_pairs={{0,12},{1,13},{2,14},{3,15},{4,8},{5,9},{6,10},{7,11},{8,4},{9,5},... | collective-permute-start | bytes 245768 | tf_op jit(solution)/shard_map/ppermute | solution.py:28
  116.2 5.5 %collective-permute-start.25 = (bf16[2,160,128]{2,1,0:T(8,128)(2,1)S(1)}, bf16[2,160,128]{2,1,0:T(8,128)(2,1)S(1)}, u32[]{:S(2)}, u32[]{:S(2)}) collective-permute-start(bf16[2,160,128]{2,1,0:T(8,128)(2,1)S(1)} %get-tuple-element.141), channel_id=1, source_target_pairs={{0,2},{1,3},{2,0},{3,1},{4,6},{5,7},{6,4},{7,5},{8,10},{9,11},{10,... | collective-permute-start | bytes 245768 | tf_op jit(solution)/shard_map/ppermute | solution.py:28
  118.3 7.2 %collective-permute-start.26 = (bf16[2,160,128]{2,1,0:T(8,128)(2,1)S(1)}, bf16[2,160,128]{2,1,0:T(8,128)(2,1)S(1)}, u32[]{:S(2)}, u32[]{:S(2)}) collective-permute-start(bf16[2,160,128]{2,1,0:T(8,128)(2,1)S(1)} %get-tuple-element.142), channel_id=1, source_target_pairs={{0,14},{1,15},{2,12},{3,13},{4,10},{5,11},{6,8},{7,9},{8,6},{9,7},... | collective-permute-start | bytes 245768 | tf_op jit(solution)/shard_map/ppermute | solution.py:28
  120.2 5.4 %collective-permute-start.27 = (bf16[4,160,128]{2,1,0:T(8,128)(2,1)S(1)}, bf16[4,160,128]{2,1,0:T(8,128)(2,1)S(1)}, u32[]{:S(2)}, u32[]{:S(2)}) collective-permute-start(bf16[4,160,128]{2,1,0:T(8,128)(2,1)S(1)} %gather_other.2), channel_id=1, source_target_pairs={{0,1},{1,0},{2,3},{3,2},{4,5},{5,4},{6,7},{7,6},{8,9},{9,8},{10,11... | collective-permute-start | bytes 491528 | tf_op jit(solution)/shard_map/ppermute | solution.py:28
  125.6 1.5 %collective-permute-start.28 = (bf16[4,160,128]{2,1,0:T(8,128)(2,1)S(1)}, bf16[4,160,128]{2,1,0:T(8,128)(2,1)S(1)}, u32[]{:S(2)}, u32[]{:S(2)}) collective-permute-start(bf16[4,160,128]{2,1,0:T(8,128)(2,1)S(1)} %gather_other.3), channel_id=1, source_target_pairs={{0,1},{1,0},{2,3},{3,2},{4,5},{5,4},{6,7},{7,6},{8,9},{9,8},{10,11... | collective-permute-start | bytes 491528 | tf_op jit(solution)/shard_map/ppermute | solution.py:28

commit v24 on v22

--- a/solution.py
+++ b/solution.py
@@ -404,8 +404,9 @@
 
 def send_order(chips):
     half = chips // 2
-    turns = [mask for at in range(half) for mask in (half + at, (at + 1) % half)]
-    return turns[:half], turns[half:]
+    cut = half // 2
+    far, near = list(range(half, chips)), list(range(half))[::-1]
+    return far[:cut] + near[:cut], far[cut:] + near[cut:]
 
 
 def finish_kernel(factor, masks, img_dev, place_ref, packed_ref, sum_ref, top_ref, mine_ref, got_ref, *refs):

time: 129 us -> 130 us (level)
  transfers between devices with their start and end apart: 30 -> 30, of which waited for: 19 -> 21; matrix products, arithmetic and copies ran while one was open for 0% -> 0% of each run, Pallas kernels for 10% -> 10%
where the time goes in v24:
time: 130 us
  waiting for transfers between devices  62.5 us (48%)
  starting transfers between devices  36.8 us (28%)
  Pallas kernels  21.1 us (16%)
  local copies, waits for them, and re-layouts  7.06 us (5%)
  between operations  2.25 us (2%)
    ppermute x29, waiting for transfers between devices, swap(): return lax.ppermute(value, 'seq', [(i, i ^ mask) for i in range(devices)])  62.5 us
    ppermute x29, starting transfers between devices, swap(): return lax.ppermute(value, 'seq', [(i, i ^ mask) for i in range(devices)])  29.3 us
    pallas_call x2, Pallas kernels, image_attention(): pl.pallas_call(functools.partial(image_kernel, factor, masks, img_dev), o...  8.03 us
    all_to_all x1, starting transfers between devices, exchange(): return lax.all_to_all(rows, 'seq', split_axis=0, concat_axis=0, tiled=True)  7.49 us
    unnamed x14, local copies, waits for them, and re-layouts  5.31 us
    pallas_call x1, Pallas kernels, encoder(): pl.pallas_call(functools.partial(encoder_kernel, lanes), out_shape=(out,)...  3.47 us
  transfers between devices with their start and end apart: 30, of which 21 were waited for; matrix products, arithmetic and copies ran while one was open for 0% of the time, Pallas kernels for 10%

profile of v24, /device:TPU:0, one launch (start us, length us, event | category | flops | bytes accessed | tf_op | source)
XLA Modules:
  0.0 129.8 jit_solution(3133699689682410366)
XLA Ops:
  0.6 1.6 %copy.12 = bf16[1,128,2,2048]{3,1,2,0:T(8,128)(2,1)S(1)} copy(bf16[1,128,2,2048]{3,2,1,0:T(2,128)(2,1)} %param.19) | data formatting | bytes 2097152 | tf_op jit(solution)/shard_map/optimization_barrier | solution.py:648
  2.3 1.0 copy-done.4
  3.3 1.4 %pack.1 = bf16[16,384,128]{2,1,0:T(8,128)(2,1)} custom-call(bf16[128,2048]{1,0:T(8,128)(2,1)S(1)} %bitcast.25, bf16[128,2048]{1,0:T(8,128)(2,1)S(1)} %get-tuple-element.147.keys_ref, bf16[128,2048]{1,0:T(8,128)(2,1)S(1)} %get-tuple-element.146.values_ref), custom_call_target="tpu_custom_call" | custom-call | bytes 3145728 | tf_op jit(solution)/shard_map/pack/pallas_call | solution.py:306
  4.7 7.5 %all-to-all-start = ((bf16[16,384,128]{2,1,0:T(8,128)(2,1)}), bf16[16,384,128]{2,1,0:T(8,128)(2,1)S(1)}, u32[]{:S(2)}, u32[]{:S(2)}) async-start(bf16[16,384,128]{2,1,0:T(8,128)(2,1)} %pack.1), calls=%async_computation | async-start | bytes 3145728 | tf_op jit(solution)/shard_map/all_to_all | solution.py:646
  12.9 0.1 stack.19.place_ref
  13.0 3.4 %copy-done = bf16[1184,3584]{1,0:T(8,128)(2,1)S(1)} copy-done((bf16[1184,3584]{1,0:T(8,128)(2,1)S(1)}, bf16[1184,3584]{1,0:T(8,128)(2,1)}, u32[]{:S(2)}) %copy-start) | copy-done | bytes 8486936
  16.4 3.5 %encoder.1 = (bf16[8,16,1792]{2,1,0:T(8,128)(2,1)S(1)}, bf16[8,16,1792]{2,1,0:T(8,128)(2,1)S(1)}, bf16[8,16,1792]{2,1,0:T(8,128)(2,1)S(1)}, bf16[8,16,1792]{2,1,0:T(8,128)(2,1)S(1)}) custom-call(s32[5]{0:T(128)S(1)} %stack.19.place_ref, bf16[1184,256]{1,0:T(8,128)(2,1)S(1)} %bitcast.24, bf16[1184,3584]{1,0:T(8,128)(2,1)S(1)} %copy-done), custom_call_target="tpu_custom_call" | custom-call | flops 2172649472 | bytes 10928128 | tf_op jit(solution)/shard_map/encoder/pallas_call | solution.py:84
  19.8 0.5 collective-permute-start
  20.3 0.1 collective-permute-start.1
  20.4 1.3 %collective-permute-done.refs_1_ = bf16[8,16,1792]{2,1,0:T(8,128)(2,1)S(1)} collective-permute-done((bf16[8,16,1792]{2,1,0:T(8,128)(2,1)S(1)}, bf16[8,16,1792]{2,1,0:T(8,128)(2,1)S(1)}, u32[]{:S(2)}, u32[]{:S(2)}) %collective-permute-start) | collective-permute-done | bytes 458784 | tf_op jit(solution)/shard_map/ppermute | solution.py:28
  21.7 0.7 collective-permute-done.1.refs_3_
  22.4 0.2 add_halves.4
  22.6 2.0 %collective-permute-start.2 = (bf16[4,16,1792]{2,1,0:T(8,128)(2,1)S(1)}, bf16[4,16,1792]{2,1,0:T(8,128)(2,1)S(1)}, u32[]{:S(2)}, u32[]{:S(2)}) collective-permute-start(bf16[4,16,1792]{2,1,0:T(8,128)(2,1)S(1)} %get-tuple-element.82), channel_id=1, source_target_pairs={{0,2},{1,3},{2,0},{3,1},{4,6},{5,7},{6,4},{7,5},{8,10},{9,11},{10,... | collective-permute-start | bytes 688136 | tf_op jit(solution)/shard_map/ppermute | solution.py:28
  24.6 1.5 %collective-permute-start.3 = (bf16[4,16,1792]{2,1,0:T(8,128)(2,1)S(1)}, bf16[4,16,1792]{2,1,0:T(8,128)(2,1)S(1)}, u32[]{:S(2)}, u32[]{:S(2)}) collective-permute-start(bf16[4,16,1792]{2,1,0:T(8,128)(2,1)S(1)} %get-tuple-element.84), channel_id=1, source_target_pairs={{0,4},{1,5},{2,6},{3,7},{4,0},{5,1},{6,2},{7,3},{8,12},{9,13},{10,... | collective-permute-start | bytes 688136 | tf_op jit(solution)/shard_map/ppermute | solution.py:28
  26.0 10.1 %collective-permute-done.2.refs_1_ = bf16[4,16,1792]{2,1,0:T(8,128)(2,1)S(1)} collective-permute-done((bf16[4,16,1792]{2,1,0:T(8,128)(2,1)S(1)}, bf16[4,16,1792]{2,1,0:T(8,128)(2,1)S(1)}, u32[]{:S(2)}, u32[]{:S(2)}) %collective-permute-start.2) | collective-permute-done | bytes 229408 | tf_op jit(solution)/shard_map/ppermute | solution.py:28
  36.1 7.6 %collective-permute-done.3.refs_3_ = bf16[4,16,1792]{2,1,0:T(8,128)(2,1)S(1)} collective-permute-done((bf16[4,16,1792]{2,1,0:T(8,128)(2,1)S(1)}, bf16[4,16,1792]{2,1,0:T(8,128)(2,1)S(1)}, u32[]{:S(2)}, u32[]{:S(2)}) %collective-permute-start.3) | collective-permute-done | bytes 229408 | tf_op jit(solution)/shard_map/ppermute | solution.py:28
  43.7 0.1 add_halves.5
  43.7 2.5 %collective-permute-start.4 = (bf16[2,16,1792]{2,1,0:T(8,128)(2,1)S(1)}, bf16[2,16,1792]{2,1,0:T(8,128)(2,1)S(1)}, u32[]{:S(2)}, u32[]{:S(2)}) collective-permute-start(bf16[2,16,1792]{2,1,0:T(8,128)(2,1)S(1)} %get-tuple-element.86), channel_id=1, source_target_pairs={{0,4},{1,5},{2,6},{3,7},{4,0},{5,1},{6,2},{7,3},{8,12},{9,13},{10,... | collective-permute-start | bytes 344072 | tf_op jit(solution)/shard_map/ppermute | solution.py:28
  46.3 1.7 %collective-permute-start.5 = (bf16[2,16,1792]{2,1,0:T(8,128)(2,1)S(1)}, bf16[2,16,1792]{2,1,0:T(8,128)(2,1)S(1)}, u32[]{:S(2)}, u32[]{:S(2)}) collective-permute-start(bf16[2,16,1792]{2,1,0:T(8,128)(2,1)S(1)} %get-tuple-element.88), channel_id=1, source_target_pairs={{0,2},{1,3},{2,0},{3,1},{4,6},{5,7},{6,4},{7,5},{8,10},{9,11},{10,... | collective-permute-start | bytes 344072 | tf_op jit(solution)/shard_map/ppermute | solution.py:28
  48.0 1.5 %collective-permute-done.4.got0 = bf16[2,16,1792]{2,1,0:T(8,128)(2,1)S(1)} collective-permute-done((bf16[2,16,1792]{2,1,0:T(8,128)(2,1)S(1)}, bf16[2,16,1792]{2,1,0:T(8,128)(2,1)S(1)}, u32[]{:S(2)}, u32[]{:S(2)}) %collective-permute-start.4) | collective-permute-done | bytes 114720 | tf_op jit(solution)/shard_map/ppermute | solution.py:28
  49.5 1.6 %collective-permute-done.5.got1 = bf16[2,16,1792]{2,1,0:T(8,128)(2,1)S(1)} collective-permute-done((bf16[2,16,1792]{2,1,0:T(8,128)(2,1)S(1)}, bf16[2,16,1792]{2,1,0:T(8,128)(2,1)S(1)}, u32[]{:S(2)}, u32[]{:S(2)}) %collective-permute-start.5) | collective-permute-done | bytes 114720 | tf_op jit(solution)/shard_map/ppermute | solution.py:28
  51.1 0.1 collective-permute-start.10
  51.2 0.5 collective-permute-start.9
  51.7 2.9 %collective-permute-start.6 = (bf16[2,2,16,1792]{3,2,1,0:T(8,128)(2,1)S(1)}, bf16[2,2,16,1792]{3,2,1,0:T(8,128)(2,1)S(1)}, u32[]{:S(2)}, u32[]{:S(2)}) collective-permute-start(bf16[2,2,16,1792]{3,2,1,0:T(8,128)(2,1)S(1)} %add_all.1.mine_ref), channel_id=1, source_target_pairs={{0,8},{1,9},{2,10},{3,11},{4,12},{5,13},{6,14},{7,15},{8,0},{9,1},... | collective-permute-start | bytes 688136 | tf_op jit(solution)/shard_map/ppermute | solution.py:28
  55.3 0.1 collective-permute-start.11
  55.3 10.0 %collective-permute-done.6.got_ref = bf16[2,2,16,1792]{3,2,1,0:T(8,128)(2,1)S(1)} collective-permute-done((bf16[2,2,16,1792]{3,2,1,0:T(8,128)(2,1)S(1)}, bf16[2,2,16,1792]{3,2,1,0:T(8,128)(2,1)S(1)}, u32[]{:S(2)}, u32[]{:S(2)}) %collective-permute-start.6) | collective-permute-done | bytes 229408 | tf_op jit(solution)/shard_map/ppermute | solution.py:28
  65.3 0.2 normalize.1
  65.5 1.6 %collective-permute-start.8 = (bf16[32,1792]{1,0:T(8,128)(2,1)S(1)}, bf16[32,1792]{1,0:T(8,128)(2,1)S(1)}, u32[]{:S(2)}, u32[]{:S(2)}) collective-permute-start(bf16[32,1792]{1,0:T(8,128)(2,1)S(1)} %bitcast.30), channel_id=1, source_target_pairs={{0,2},{1,3},{2,0},{3,1},{4,6},{5,7},{6,4},{7,5},{8,10},{9,11},{10,... | collective-permute-start | bytes 344072 | tf_op jit(solution)/shard_map/ppermute | solution.py:28
  67.2 0.9 copy-done.5
  68.1 0.2 modulation.1.refs_4_
  68.3 2.1 %collective-permute-done.8.got1 = bf16[32,1792]{1,0:T(8,128)(2,1)S(1)} collective-permute-done((bf16[32,1792]{1,0:T(8,128)(2,1)S(1)}, bf16[32,1792]{1,0:T(8,128)(2,1)S(1)}, u32[]{:S(2)}, u32[]{:S(2)}) %collective-permute-start.8) | collective-permute-done | bytes 114720 | tf_op jit(solution)/shard_map/ppermute | solution.py:28
  70.4 1.5 %collective-permute-done.7.got0 = bf16[32,1792]{1,0:T(8,128)(2,1)S(1)} collective-permute-done((bf16[32,1792]{1,0:T(8,128)(2,1)S(1)}, bf16[32,1792]{1,0:T(8,128)(2,1)S(1)}, u32[]{:S(2)}, u32[]{:S(2)}) %collective-permute-start.7) | collective-permute-done | bytes 114720 | tf_op jit(solution)/shard_map/ppermute | solution.py:28
  71.9 0.6 collective-permute-start.12
  72.5 0.4 collective-permute-start.13
  72.9 3.9 %image_attention.2 = (f32[1024,256]{1,0:T(8,128)S(1)}, f32[1024,128]{1,0:T(8,128)S(1)}) custom-call(s32[5]{0:T(128)S(1)} %stack.19.place_ref, bf16[16,384,128]{2,1,0:T(8,128)(2,1)S(1)} %all-to-all-done.packed_ref), custom_call_target="tpu_custom_call" | custom-call | flops 1073741824 | bytes 2359296 | tf_op jit(solution)/shard_map/image_attention/pallas_call | solution.py:383
  76.8 1.2 collective-permute-done.12.refs_1_
  78.0 0.5 collective-permute-done.13.refs_3_
  78.6 2.4 %project.1 = (bf16[4,144,256]{2,1,0:T(8,128)(2,1)S(1)}, bf16[4,144,256]{2,1,0:T(8,128)(2,1)S(1)}, bf16[4,144,256]{2,1,0:T(8,128)(2,1)S(1)}, bf16[4,144,256]{2,1,0:T(8,128)(2,1)S(1)}) custom-call(s32[5]{0:T(128)S(1)} %stack.19.place_ref, bf16[64,1792]{1,0:T(8,128)(2,1)S(1)} %get-tuple-element.102.refs_0_, ...), custom_call_target="tpu_custom_call" | custom-call | flops 754974720 | bytes 7864320 | tf_op jit(solution)/shard_map/project/pallas_call | solution.py:216
  81.0 1.6 %collective-permute-start.14 = (bf16[4,144,256]{2,1,0:T(8,128)(2,1)S(1)}, bf16[4,144,256]{2,1,0:T(8,128)(2,1)S(1)}, u32[]{:S(2)}, u32[]{:S(2)}) collective-permute-start(bf16[4,144,256]{2,1,0:T(8,128)(2,1)S(1)} %get-tuple-element.118), channel_id=1, source_target_pairs={{0,2},{1,3},{2,0},{3,1},{4,6},{5,7},{6,4},{7,5},{8,10},{9,11},{10,... | collective-permute-start | bytes 884744 | tf_op jit(solution)/shard_map/ppermute | solution.py:28
  82.5 0.1 collective-permute-start.15
  82.6 4.1 %image_attention.3 = (f32[1024,256]{1,0:T(8,128)S(1)}, f32[1024,128]{1,0:T(8,128)S(1)}) custom-call(s32[5]{0:T(128)S(1)} %stack.19.place_ref, bf16[16,384,128]{2,1,0:T(8,128)(2,1)S(1)} %all-to-all-done.packed_ref), custom_call_target="tpu_custom_call" | custom-call | flops 1073741824 | bytes 2359296 | tf_op jit(solution)/shard_map/image_attention/pallas_call | solution.py:383
  86.7 1.0 collective-permute-done.14.refs_1_
  87.8 2.8 %collective-permute-done.15.refs_3_ = bf16[4,144,256]{2,1,0:T(8,128)(2,1)S(1)} collective-permute-done((bf16[4,144,256]{2,1,0:T(8,128)(2,1)S(1)}, bf16[4,144,256]{2,1,0:T(8,128)(2,1)S(1)}, u32[]{:S(2)}, u32[]{:S(2)}) %collective-permute-start.15) | collective-permute-done | bytes 294944 | tf_op jit(solution)/shard_map/ppermute | solution.py:28
  90.6 0.1 add_halves.6
  90.8 0.6 collective-permute-start.17
  91.4 6.1 %collective-permute-done.16.refs_1_ = bf16[2,144,256]{2,1,0:T(8,128)(2,1)S(1)} collective-permute-done((bf16[2,144,256]{2,1,0:T(8,128)(2,1)S(1)}, bf16[2,144,256]{2,1,0:T(8,128)(2,1)S(1)}, u32[]{:S(2)}, u32[]{:S(2)}) %collective-permute-start.16) | collective-permute-done | bytes 147488 | tf_op jit(solution)/shard_map/ppermute | solution.py:28
  97.5 1.3 collective-permute-start.18
  98.8 6.3 %collective-permute-done.18.refs_2_ = bf16[2,1,144,256]{3,2,1,0:T(8,128)(2,1)S(1)} collective-permute-done((bf16[2,1,144,256]{3,2,1,0:T(8,128)(2,1)S(1)}, bf16[2,1,144,256]{3,2,1,0:T(8,128)(2,1)S(1)}, u32[]{:S(2)}, u32[]{:S(2)}) %collective-permute-start.18) | collective-permute-done | bytes 147488 | tf_op jit(solution)/shard_map/ppermute | solution.py:28
  105.1 0.9 combine.1
  106.0 0.1 collective-permute-start.19
  106.1 1.2 collective-permute-done.19.got_ref
  107.4 1.2 finish.3
  108.6 1.4 %collective-permute-start.24 = (bf16[2,160,128]{2,1,0:T(8,128)(2,1)S(1)}, bf16[2,160,128]{2,1,0:T(8,128)(2,1)S(1)}, u32[]{:S(2)}, u32[]{:S(2)}) collective-permute-start(bf16[2,160,128]{2,1,0:T(8,128)(2,1)S(1)} %get-tuple-element.140), channel_id=1, source_target_pairs={{0,12},{1,13},{2,14},{3,15},{4,8},{5,9},{6,10},{7,11},{8,4},{9,5},... | collective-permute-start | bytes 245768 | tf_op jit(solution)/shard_map/ppermute | solution.py:28
  110.0 2.4 %collective-permute-start.25 = (bf16[2,160,128]{2,1,0:T(8,128)(2,1)S(1)}, bf16[2,160,128]{2,1,0:T(8,128)(2,1)S(1)}, u32[]{:S(2)}, u32[]{:S(2)}) collective-permute-start(bf16[2,160,128]{2,1,0:T(8,128)(2,1)S(1)} %get-tuple-element.141), channel_id=1, source_target_pairs={{0,14},{1,15},{2,12},{3,13},{4,10},{5,11},{6,8},{7,9},{8,6},{9,7},... | collective-permute-start | bytes 245768 | tf_op jit(solution)/shard_map/ppermute | solution.py:28
  112.4 1.5 %collective-permute-start.26 = (bf16[2,160,128]{2,1,0:T(8,128)(2,1)S(1)}, bf16[2,160,128]{2,1,0:T(8,128)(2,1)S(1)}, u32[]{:S(2)}, u32[]{:S(2)}) collective-permute-start(bf16[2,160,128]{2,1,0:T(8,128)(2,1)S(1)} %get-tuple-element.142), channel_id=1, source_target_pairs={{0,2},{1,3},{2,0},{3,1},{4,6},{5,7},{6,4},{7,5},{8,10},{9,11},{10,... | collective-permute-start | bytes 245768 | tf_op jit(solution)/shard_map/ppermute | solution.py:28
  113.9 1.2 finish.2
  115.2 2.9 %collective-permute-start.21 = (bf16[2,160,128]{2,1,0:T(8,128)(2,1)S(1)}, bf16[2,160,128]{2,1,0:T(8,128)(2,1)S(1)}, u32[]{:S(2)}, u32[]{:S(2)}) collective-permute-start(bf16[2,160,128]{2,1,0:T(8,128)(2,1)S(1)} %get-tuple-element.135), channel_id=1, source_target_pairs={{0,10},{1,11},{2,8},{3,9},{4,14},{5,15},{6,12},{7,13},{8,2},{9,3},... | collective-permute-start | bytes 245768 | tf_op jit(solution)/shard_map/ppermute | solution.py:28
  118.1 3.0 %collective-permute-start.23 = (bf16[2,160,128]{2,1,0:T(8,128)(2,1)S(1)}, bf16[2,160,128]{2,1,0:T(8,128)(2,1)S(1)}, u32[]{:S(2)}, u32[]{:S(2)}) collective-permute-start(bf16[2,160,128]{2,1,0:T(8,128)(2,1)S(1)} %get-tuple-element.137), channel_id=1, source_target_pairs={{0,4},{1,5},{2,6},{3,7},{4,0},{5,1},{6,2},{7,3},{8,12},{9,13},{10,... | collective-permute-start | bytes 245768 | tf_op jit(solution)/shard_map/ppermute | solution.py:28
  121.1 1.7 %collective-permute-done.20.refs_0_ = bf16[2,160,128]{2,1,0:T(8,128)(2,1)S(1)} collective-permute-done((bf16[2,160,128]{2,1,0:T(8,128)(2,1)S(1)}, bf16[2,160,128]{2,1,0:T(8,128)(2,1)S(1)}, u32[]{:S(2)}, u32[]{:S(2)}) %collective-permute-start.20) | collective-permute-done | bytes 81952 | tf_op jit(solution)/shard_map/ppermute | solution.py:28
  122.9 1.5 %collective-permute-done.21.refs_1_ = bf16[2,160,128]{2,1,0:T(8,128)(2,1)S(1)} collective-permute-done((bf16[2,160,128]{2,1,0:T(8,128)(2,1)S(1)}, bf16[2,160,128]{2,1,0:T(8,128)(2,1)S(1)}, u32[]{:S(2)}, u32[]{:S(2)}) %collective-permute-start.21) | collective-permute-done | bytes 81952 | tf_op jit(solution)/shard_map/ppermute | solution.py:28
  124.3 1.1 collective-permute-done.22.refs_2_
  125.4 1.3 %collective-permute-done.23.refs_3_ = bf16[2,160,128]{2,1,0:T(8,128)(2,1)S(1)} collective-permute-done((bf16[2,160,128]{2,1,0:T(8,128)(2,1)S(1)}, bf16[2,160,128]{2,1,0:T(8,128)(2,1)S(1)}, u32[]{:S(2)}, u32[]{:S(2)}) %collective-permute-start.23) | collective-permute-done | bytes 81952 | tf_op jit(solution)/shard_map/ppermute | solution.py:28
  126.9 1.4 %collective-permute-done.27.refs_8_ = bf16[4,160,128]{2,1,0:T(8,128)(2,1)S(1)} collective-permute-done((bf16[4,160,128]{2,1,0:T(8,128)(2,1)S(1)}, bf16[4,160,128]{2,1,0:T(8,128)(2,1)S(1)}, u32[]{:S(2)}, u32[]{:S(2)}) %collective-permute-start.27) | collective-permute-done | bytes 163872 | tf_op jit(solution)/shard_map/ppermute | solution.py:28
  128.2 1.5 %unpack.1 = (bf16[128,2048]{1,0:T(8,128)(2,1)}, bf16[16,4096]{1,0:T(8,128)(2,1)}) custom-call(s32[5]{0:T(128)S(1)} %stack.19.place_ref, bf16[2,160,128]{2,1,0:T(8,128)(2,1)S(1)} %collective-permute-done.20.refs_0_, bf16[2,160,128]{2,1,0:T(8,128)(2,1)S(1)} %collective-permute-done.21.refs_1_, bf16[2,160,128]{2,1,0:T(8,128)(2,1)S(1)} %collective-permute-done.22.refs_2_, ...), custom_call_target="tpu_custom_call" | custom-call | tf_op jit(solution)/shard_map/unpack/pallas_call | solution.py:341
  (35 shorter events, 0.7 us)
Async XLA Ops:
  2.2 1.0 copy-start.4
  4.7 8.3 %copy-start.3 = (bf16[1,256,1184]{1,2,0:T(8,128)(2,1)S(1)}, bf16[1,256,1184]{1,2,0:T(8,128)(2,1)}, u32[]{:S(2)}) copy-start(bf16[1,256,1184]{1,2,0:T(8,128)(2,1)} %param.10) | copy-start | bytes 1818628
  4.7 46.4 %all-to-all-start = ((bf16[16,384,128]{2,1,0:T(8,128)(2,1)}), bf16[16,384,128]{2,1,0:T(8,128)(2,1)S(1)}, u32[]{:S(2)}, u32[]{:S(2)}) async-start(bf16[16,384,128]{2,1,0:T(8,128)(2,1)} %pack.1), calls=%async_computation | async-start | bytes 3145728 | tf_op jit(solution)/shard_map/all_to_all | solution.py:646
  13.0 3.4 %copy-start = (bf16[1184,3584]{1,0:T(8,128)(2,1)S(1)}, bf16[1184,3584]{1,0:T(8,128)(2,1)}, u32[]{:S(2)}) copy-start(bf16[1184,3584]{1,0:T(8,128)(2,1)} %weight_ref.1) | copy-start | bytes 25460740
  19.8 1.9 %collective-permute-start = (bf16[8,16,1792]{2,1,0:T(8,128)(2,1)S(1)}, bf16[8,16,1792]{2,1,0:T(8,128)(2,1)S(1)}, u32[]{:S(2)}, u32[]{:S(2)}) collective-permute-start(bf16[8,16,1792]{2,1,0:T(8,128)(2,1)S(1)} %get-tuple-element.78), channel_id=1, source_target_pairs={{0,1},{1,0},{2,3},{3,2},{4,5},{5,4},{6,7},{7,6},{8,9},{9,8},{10,11... | collective-permute-start | bytes 1376264 | tf_op jit(solution)/shard_map/ppermute | solution.py:28
  20.3 2.1 %collective-permute-start.1 = (bf16[8,16,1792]{2,1,0:T(8,128)(2,1)S(1)}, bf16[8,16,1792]{2,1,0:T(8,128)(2,1)S(1)}, u32[]{:S(2)}, u32[]{:S(2)}) collective-permute-start(bf16[8,16,1792]{2,1,0:T(8,128)(2,1)S(1)} %get-tuple-element.80), channel_id=1, source_target_pairs={{0,1},{1,0},{2,3},{3,2},{4,5},{5,4},{6,7},{7,6},{8,9},{9,8},{10,11... | collective-permute-start | bytes 1376264 | tf_op jit(solution)/shard_map/ppermute | solution.py:28
  22.6 28.5 %copy-start.1 = (bf16[192,4096]{1,0:T(8,128)(2,1)S(1)}, bf16[192,4096]{1,0:T(8,128)(2,1)}, u32[]{:S(2)}) copy-start(bf16[192,4096]{1,0:T(8,128)(2,1)} %refs_7_.1) | copy-start | bytes 4718596
  22.6 32.6 %copy-start.6 = (bf16[3584]{0:T(1024)(128)(2,1)S(1)}, bf16[3584]{0:T(1024)(128)(2,1)}, u32[]{:S(2)}) copy-start(bf16[3584]{0:T(1024)(128)(2,1)} %param.12) | copy-start | bytes 21508
  22.6 13.5 %collective-permute-start.2 = (bf16[4,16,1792]{2,1,0:T(8,128)(2,1)S(1)}, bf16[4,16,1792]{2,1,0:T(8,128)(2,1)S(1)}, u32[]{:S(2)}, u32[]{:S(2)}) collective-permute-start(bf16[4,16,1792]{2,1,0:T(8,128)(2,1)S(1)} %get-tuple-element.82), channel_id=1, source_target_pairs={{0,2},{1,3},{2,0},{3,1},{4,6},{5,7},{6,4},{7,5},{8,10},{9,11},{10,... | collective-permute-start | bytes 688136 | tf_op jit(solution)/shard_map/ppermute | solution.py:28
  24.6 19.1 %collective-permute-start.3 = (bf16[4,16,1792]{2,1,0:T(8,128)(2,1)S(1)}, bf16[4,16,1792]{2,1,0:T(8,128)(2,1)S(1)}, u32[]{:S(2)}, u32[]{:S(2)}) collective-permute-start(bf16[4,16,1792]{2,1,0:T(8,128)(2,1)S(1)} %get-tuple-element.84), channel_id=1, source_target_pairs={{0,4},{1,5},{2,6},{3,7},{4,0},{5,1},{6,2},{7,3},{8,12},{9,13},{10,... | collective-permute-start | bytes 688136 | tf_op jit(solution)/shard_map/ppermute | solution.py:28
  43.7 5.8 %collective-permute-start.4 = (bf16[2,16,1792]{2,1,0:T(8,128)(2,1)S(1)}, bf16[2,16,1792]{2,1,0:T(8,128)(2,1)S(1)}, u32[]{:S(2)}, u32[]{:S(2)}) collective-permute-start(bf16[2,16,1792]{2,1,0:T(8,128)(2,1)S(1)} %get-tuple-element.86), channel_id=1, source_target_pairs={{0,4},{1,5},{2,6},{3,7},{4,0},{5,1},{6,2},{7,3},{8,12},{9,13},{10,... | collective-permute-start | bytes 344072 | tf_op jit(solution)/shard_map/ppermute | solution.py:28
  46.3 4.8 %collective-permute-start.5 = (bf16[2,16,1792]{2,1,0:T(8,128)(2,1)S(1)}, bf16[2,16,1792]{2,1,0:T(8,128)(2,1)S(1)}, u32[]{:S(2)}, u32[]{:S(2)}) collective-permute-start(bf16[2,16,1792]{2,1,0:T(8,128)(2,1)S(1)} %get-tuple-element.88), channel_id=1, source_target_pairs={{0,2},{1,3},{2,0},{3,1},{4,6},{5,7},{6,4},{7,5},{8,10},{9,11},{10,... | collective-permute-start | bytes 344072 | tf_op jit(solution)/shard_map/ppermute | solution.py:28
  51.1 20.7 %collective-permute-start.10 = (bf16[192,4096]{1,0:T(8,128)(2,1)S(1)}, bf16[192,4096]{1,0:T(8,128)(2,1)S(1)}, u32[]{:S(2)}, u32[]{:S(2)}) collective-permute-start(bf16[192,4096]{1,0:T(8,128)(2,1)S(1)} %copy-done.1), channel_id=1, source_target_pairs={{0,1},{1,0},{2,3},{3,2},{4,5},{5,4},{6,7},{7,6},{8,9},{9,8},{10,11... | collective-permute-start | bytes 4718600 | tf_op jit(solution)/shard_map/ppermute | solution.py:28
  51.2 20.7 %collective-permute-start.9 = (bf16[192,3584]{1,0:T(8,128)(2,1)}, bf16[192,3584]{1,0:T(8,128)(2,1)S(1)}, u32[]{:S(2)}, u32[]{:S(2)}) collective-permute-start(bf16[192,3584]{1,0:T(8,128)(2,1)} %bitcast.22), channel_id=1, source_target_pairs={{0,1},{1,0},{2,3},{3,2},{4,5},{5,4},{6,7},{7,6},{8,9},{9,8},{10,11... | collective-permute-start | bytes 4128776 | tf_op jit(solution)/shard_map/ppermute | solution.py:28
  51.7 13.6 %collective-permute-start.6 = (bf16[2,2,16,1792]{3,2,1,0:T(8,128)(2,1)S(1)}, bf16[2,2,16,1792]{3,2,1,0:T(8,128)(2,1)S(1)}, u32[]{:S(2)}, u32[]{:S(2)}) collective-permute-start(bf16[2,2,16,1792]{3,2,1,0:T(8,128)(2,1)S(1)} %add_all.1.mine_ref), channel_id=1, source_target_pairs={{0,8},{1,9},{2,10},{3,11},{4,12},{5,13},{6,14},{7,15},{8,0},{9,1},... | collective-permute-start | bytes 688136 | tf_op jit(solution)/shard_map/ppermute | solution.py:28
  55.3 11.9 %collective-permute-start.11 = (bf16[2,192,256]{2,1,0:T(8,128)(2,1)}, bf16[2,192,256]{2,1,0:T(8,128)(2,1)S(1)}, u32[]{:S(2)}, u32[]{:S(2)}) collective-permute-start(bf16[2,192,256]{2,1,0:T(8,128)(2,1)} %bitcast.26), channel_id=1, source_target_pairs={{0,1},{1,0},{2,3},{3,2},{4,5},{5,4},{6,7},{7,6},{8,9},{9,8},{10,11... | collective-permute-start | bytes 589832 | tf_op jit(solution)/shard_map/ppermute | solution.py:28
  65.5 4.9 %collective-permute-start.8 = (bf16[32,1792]{1,0:T(8,128)(2,1)S(1)}, bf16[32,1792]{1,0:T(8,128)(2,1)S(1)}, u32[]{:S(2)}, u32[]{:S(2)}) collective-permute-start(bf16[32,1792]{1,0:T(8,128)(2,1)S(1)} %bitcast.30), channel_id=1, source_target_pairs={{0,2},{1,3},{2,0},{3,1},{4,6},{5,7},{6,4},{7,5},{8,10},{9,11},{10,... | collective-permute-start | bytes 344072 | tf_op jit(solution)/shard_map/ppermute | solution.py:28
  67.1 4.8 %collective-permute-start.7 = (bf16[32,1792]{1,0:T(8,128)(2,1)S(1)}, bf16[32,1792]{1,0:T(8,128)(2,1)S(1)}, u32[]{:S(2)}, u32[]{:S(2)}) collective-permute-start(bf16[32,1792]{1,0:T(8,128)(2,1)S(1)} %bitcast.28), channel_id=1, source_target_pairs={{0,4},{1,5},{2,6},{3,7},{4,0},{5,1},{6,2},{7,3},{8,12},{9,13},{10,... | collective-permute-start | bytes 344072 | tf_op jit(solution)/shard_map/ppermute | solution.py:28
  67.2 0.9 copy-start.5
  71.9 6.6 %copy-start.2 = (bf16[3584,192]{0,1:T(8,128)(2,1)S(1)}, bf16[3584,192]{0,1:T(8,128)(2,1)}, u32[]{:S(2)}) copy-start(bf16[3584,192]{0,1:T(8,128)(2,1)} %param.13) | copy-start | bytes 4128772
  71.9 6.1 %collective-permute-start.12 = (bf16[64,1792]{1,0:T(8,128)(2,1)S(1)}, bf16[64,1792]{1,0:T(8,128)(2,1)S(1)}, u32[]{:S(2)}, u32[]{:S(2)}) collective-permute-start(bf16[64,1792]{1,0:T(8,128)(2,1)S(1)} %get-tuple-element.102.refs_0_), channel_id=1, source_target_pairs={{0,2},{1,3},{2,0},{3,1},{4,6},{5,7},{6,4},{7,5},{8,10},{9,11},{10,... | collective-permute-start | bytes 688136 | tf_op jit(solution)/shard_map/ppermute | solution.py:28
  72.5 6.0 %collective-permute-start.13 = (bf16[64,1792]{1,0:T(8,128)(2,1)S(1)}, bf16[64,1792]{1,0:T(8,128)(2,1)S(1)}, u32[]{:S(2)}, u32[]{:S(2)}) collective-permute-start(bf16[64,1792]{1,0:T(8,128)(2,1)S(1)} %get-tuple-element.103.refs_2_), channel_id=1, source_target_pairs={{0,4},{1,5},{2,6},{3,7},{4,0},{5,1},{6,2},{7,3},{8,12},{9,13},{10,... | collective-permute-start | bytes 688136 | tf_op jit(solution)/shard_map/ppermute | solution.py:28
  81.0 6.8 %collective-permute-start.14 = (bf16[4,144,256]{2,1,0:T(8,128)(2,1)S(1)}, bf16[4,144,256]{2,1,0:T(8,128)(2,1)S(1)}, u32[]{:S(2)}, u32[]{:S(2)}) collective-permute-start(bf16[4,144,256]{2,1,0:T(8,128)(2,1)S(1)} %get-tuple-element.118), channel_id=1, source_target_pairs={{0,2},{1,3},{2,0},{3,1},{4,6},{5,7},{6,4},{7,5},{8,10},{9,11},{10,... | collective-permute-start | bytes 884744 | tf_op jit(solution)/shard_map/ppermute | solution.py:28
  82.5 8.0 %collective-permute-start.15 = (bf16[4,144,256]{2,1,0:T(8,128)(2,1)S(1)}, bf16[4,144,256]{2,1,0:T(8,128)(2,1)S(1)}, u32[]{:S(2)}, u32[]{:S(2)}) collective-permute-start(bf16[4,144,256]{2,1,0:T(8,128)(2,1)S(1)} %get-tuple-element.119), channel_id=1, source_target_pairs={{0,4},{1,5},{2,6},{3,7},{4,0},{5,1},{6,2},{7,3},{8,12},{9,13},{10,... | collective-permute-start | bytes 884744 | tf_op jit(solution)/shard_map/ppermute | solution.py:28
  90.7 6.8 %collective-permute-start.16 = (bf16[2,144,256]{2,1,0:T(8,128)(2,1)S(1)}, bf16[2,144,256]{2,1,0:T(8,128)(2,1)S(1)}, u32[]{:S(2)}, u32[]{:S(2)}) collective-permute-start(bf16[2,144,256]{2,1,0:T(8,128)(2,1)S(1)} %get-tuple-element.126), channel_id=1, source_target_pairs={{0,4},{1,5},{2,6},{3,7},{4,0},{5,1},{6,2},{7,3},{8,12},{9,13},{10,... | collective-permute-start | bytes 442376 | tf_op jit(solution)/shard_map/ppermute | solution.py:28
  90.8 6.7 %collective-permute-start.17 = (bf16[2,144,256]{2,1,0:T(8,128)(2,1)S(1)}, bf16[2,144,256]{2,1,0:T(8,128)(2,1)S(1)}, u32[]{:S(2)}, u32[]{:S(2)}) collective-permute-start(bf16[2,144,256]{2,1,0:T(8,128)(2,1)S(1)} %get-tuple-element.128), channel_id=1, source_target_pairs={{0,2},{1,3},{2,0},{3,1},{4,6},{5,7},{6,4},{7,5},{8,10},{9,11},{10,... | collective-permute-start | bytes 442376 | tf_op jit(solution)/shard_map/ppermute | solution.py:28
  97.5 7.6 %collective-permute-start.18 = (bf16[2,1,144,256]{3,2,1,0:T(8,128)(2,1)S(1)}, bf16[2,1,144,256]{3,2,1,0:T(8,128)(2,1)S(1)}, u32[]{:S(2)}, u32[]{:S(2)}) collective-permute-start(bf16[2,1,144,256]{3,2,1,0:T(8,128)(2,1)S(1)} %get-tuple-element.131), channel_id=1, source_target_pairs={{0,8},{1,9},{2,10},{3,11},{4,12},{5,13},{6,14},{7,15},{8,0},{9,1},... | collective-permute-start | bytes 442376 | tf_op jit(solution)/shard_map/ppermute | solution.py:28
  106.0 1.3 %collective-permute-start.19 = (bf16[128,256]{1,0:T(8,128)(2,1)S(1)}, bf16[128,256]{1,0:T(8,128)(2,1)S(1)}, u32[]{:S(2)}, u32[]{:S(2)}) collective-permute-start(bf16[128,256]{1,0:T(8,128)(2,1)S(1)} %get-tuple-element.133), channel_id=1, source_target_pairs={{0,1},{1,0},{2,3},{3,2},{4,5},{5,4},{6,7},{7,6},{8,9},{9,8},{10,11... | collective-permute-start | bytes 196616 | tf_op jit(solution)/shard_map/ppermute | solution.py:28
  108.6 9.5 %collective-permute-start.24 = (bf16[2,160,128]{2,1,0:T(8,128)(2,1)S(1)}, bf16[2,160,128]{2,1,0:T(8,128)(2,1)S(1)}, u32[]{:S(2)}, u32[]{:S(2)}) collective-permute-start(bf16[2,160,128]{2,1,0:T(8,128)(2,1)S(1)} %get-tuple-element.140), channel_id=1, source_target_pairs={{0,12},{1,13},{2,14},{3,15},{4,8},{5,9},{6,10},{7,11},{8,4},{9,5},... | collective-permute-start | bytes 245768 | tf_op jit(solution)/shard_map/ppermute | solution.py:28
  110.0 8.1 %collective-permute-start.25 = (bf16[2,160,128]{2,1,0:T(8,128)(2,1)S(1)}, bf16[2,160,128]{2,1,0:T(8,128)(2,1)S(1)}, u32[]{:S(2)}, u32[]{:S(2)}) collective-permute-start(bf16[2,160,128]{2,1,0:T(8,128)(2,1)S(1)} %get-tuple-element.141), channel_id=1, source_target_pairs={{0,14},{1,15},{2,12},{3,13},{4,10},{5,11},{6,8},{7,9},{8,6},{9,7},... | collective-permute-start | bytes 245768 | tf_op jit(solution)/shard_map/ppermute | solution.py:28
  112.4 8.6 %collective-permute-start.26 = (bf16[2,160,128]{2,1,0:T(8,128)(2,1)S(1)}, bf16[2,160,128]{2,1,0:T(8,128)(2,1)S(1)}, u32[]{:S(2)}, u32[]{:S(2)}) collective-permute-start(bf16[2,160,128]{2,1,0:T(8,128)(2,1)S(1)} %get-tuple-element.142), channel_id=1, source_target_pairs={{0,2},{1,3},{2,0},{3,1},{4,6},{5,7},{6,4},{7,5},{8,10},{9,11},{10,... | collective-permute-start | bytes 245768 | tf_op jit(solution)/shard_map/ppermute | solution.py:28
  115.1 7.8 %collective-permute-start.20 = (bf16[2,160,128]{2,1,0:T(8,128)(2,1)S(1)}, bf16[2,160,128]{2,1,0:T(8,128)(2,1)S(1)}, u32[]{:S(2)}, u32[]{:S(2)}) collective-permute-start(bf16[2,160,128]{2,1,0:T(8,128)(2,1)S(1)} %get-tuple-element.134), channel_id=1, source_target_pairs={{0,8},{1,9},{2,10},{3,11},{4,12},{5,13},{6,14},{7,15},{8,0},{9,1},... | collective-permute-start | bytes 245768 | tf_op jit(solution)/shard_map/ppermute | solution.py:28
  115.2 9.2 %collective-permute-start.21 = (bf16[2,160,128]{2,1,0:T(8,128)(2,1)S(1)}, bf16[2,160,128]{2,1,0:T(8,128)(2,1)S(1)}, u32[]{:S(2)}, u32[]{:S(2)}) collective-permute-start(bf16[2,160,128]{2,1,0:T(8,128)(2,1)S(1)} %get-tuple-element.135), channel_id=1, source_target_pairs={{0,10},{1,11},{2,8},{3,9},{4,14},{5,15},{6,12},{7,13},{8,2},{9,3},... | collective-permute-start | bytes 245768 | tf_op jit(solution)/shard_map/ppermute | solution.py:28
  118.0 7.4 %collective-permute-start.22 = (bf16[2,160,128]{2,1,0:T(8,128)(2,1)S(1)}, bf16[2,160,128]{2,1,0:T(8,128)(2,1)S(1)}, u32[]{:S(2)}, u32[]{:S(2)}) collective-permute-start(bf16[2,160,128]{2,1,0:T(8,128)(2,1)S(1)} %get-tuple-element.136), channel_id=1, source_target_pairs={{0,6},{1,7},{2,4},{3,5},{4,2},{5,3},{6,0},{7,1},{8,14},{9,15},{10,... | collective-permute-start | bytes 245768 | tf_op jit(solution)/shard_map/ppermute | solution.py:28
  118.1 8.7 %collective-permute-start.23 = (bf16[2,160,128]{2,1,0:T(8,128)(2,1)S(1)}, bf16[2,160,128]{2,1,0:T(8,128)(2,1)S(1)}, u32[]{:S(2)}, u32[]{:S(2)}) collective-permute-start(bf16[2,160,128]{2,1,0:T(8,128)(2,1)S(1)} %get-tuple-element.137), channel_id=1, source_target_pairs={{0,4},{1,5},{2,6},{3,7},{4,0},{5,1},{6,2},{7,3},{8,12},{9,13},{10,... | collective-permute-start | bytes 245768 | tf_op jit(solution)/shard_map/ppermute | solution.py:28
  121.0 5.8 %collective-permute-start.28 = (bf16[4,160,128]{2,1,0:T(8,128)(2,1)S(1)}, bf16[4,160,128]{2,1,0:T(8,128)(2,1)S(1)}, u32[]{:S(2)}, u32[]{:S(2)}) collective-permute-start(bf16[4,160,128]{2,1,0:T(8,128)(2,1)S(1)} %gather_other.3), channel_id=1, source_target_pairs={{0,1},{1,0},{2,3},{3,2},{4,5},{5,4},{6,7},{7,6},{8,9},{9,8},{10,11... | collective-permute-start | bytes 491528 | tf_op jit(solution)/shard_map/ppermute | solution.py:28
  126.8 1.5 %collective-permute-start.27 = (bf16[4,160,128]{2,1,0:T(8,128)(2,1)S(1)}, bf16[4,160,128]{2,1,0:T(8,128)(2,1)S(1)}, u32[]{:S(2)}, u32[]{:S(2)}) collective-permute-start(bf16[4,160,128]{2,1,0:T(8,128)(2,1)S(1)} %gather_other.2), channel_id=1, source_target_pairs={{0,1},{1,0},{2,3},{3,2},{4,5},{5,4},{6,7},{7,6},{8,9},{9,8},{10,11... | collective-permute-start | bytes 491528 | tf_op jit(solution)/shard_map/ppermute | solution.py:28
